TPU v7x, 32 devices: a whole 2x2x4 slice. The times are simulated.
32 devices in a mesh: groups: 2 (over x), rows: 16 (over z, y, core).
Axes of the slice: x: 2, y: 2, z: 4, core: 2. Of those that a mesh axis runs over, the one named last changes fastest.
Arguments:
- queries: float32 [1024, 4096], P('groups', 'rows'), parts along dimension 0, may hold values from -6 to 6
- precond: float32 [4096, 4096], P('rows'), may hold values from -0.125 to 0.125
- train: bfloat16 [256, 32, 4096], P('rows', 'groups'), parts along dimension 1, may hold values from -0.09375 to 0.09375
- query_cluster: int32 [1024], P('groups'), parts along dimension 0, may hold values from 0 to 7
- cand_blocks: int32 [16, 12], P('groups'), parts along dimension 0, may hold values from 0 to 15, as said below
- cand_count: int32 [16], P('groups'), parts along dimension 0, may hold values from 1 to 12, 64 in all
- slot_block: int32 [32], P('groups'), parts along dimension 0, may hold values from 0 to 15, each once
Outputs:
- scores: float32 [256, 32, 512], P(None, ('groups', 'rows')), parts along dimension 1
There are 2 independent parts, one for each index of `groups`. A program takes and returns all parts, laid end to end along the dimension named above; an argument that names none is the same for every part. Nothing has to cross between parts.
Inputs may be any that keep to these rules, and one draw needn't show every extreme that they name: `cand_blocks`: each row holds 12 different block ids; the first cand_count[c] entries of row c are cluster c's candidates.
All inputs are finite; a program needn't handle non-finite values.
Results may differ from a plain program's by a relative error of at most 0.0029.
Values may be sent and summed in bfloat16 or wider, within the bound.
No kernel may reach another device: no remote copies, remote signals or barrier semaphores. Data moves between devices by JAX's collectives and lax.ppermute only.
A program may use at most 64 MiB of HBM per device.

v0:
```python
import jax
import jax.numpy as jnp
from jax import lax
from jax.sharding import PartitionSpec as P


def listed_mask(query_cluster, cand_blocks, cand_count, nblocks):
    nclusters = cand_blocks.shape[0]
    valid = jnp.arange(cand_blocks.shape[1])[None, :] < cand_count[:, None]
    hits = (cand_blocks[:, :, None] == jnp.arange(nblocks)[None, None, :]) & valid[:, :, None]
    listed = jnp.any(hits, axis=1).astype(jnp.float32)
    onehot = (query_cluster[:, None] == jnp.arange(nclusters)[None, :]).astype(jnp.float32)
    return jnp.dot(listed.T, onehot.T, preferred_element_type=jnp.float32)


def shards(queries, precond, train, query_cluster, cand_blocks, cand_count, slot_block):
    nblocks = train.shape[1]
    owned_count = nblocks // lax.axis_size("rows")
    prequery = lax.psum_scatter(
        jnp.einsum(
            "fd,qf->dq",
            precond,
            queries,
            precision=lax.Precision.HIGHEST,
            preferred_element_type=jnp.float32,
        ),
        "rows",
        scatter_dimension=0,
        tiled=True,
    ).astype(jnp.bfloat16)
    allowed = listed_mask(query_cluster, cand_blocks, cand_count, nblocks)
    ordered = jnp.take(train, slot_block, axis=1)
    owned = lax.all_to_all(ordered, "rows", split_axis=1, concat_axis=0, tiled=True)
    mine = lax.dynamic_slice_in_dim(slot_block, lax.axis_index("rows") * owned_count, owned_count)
    own_allowed = jnp.take(allowed, mine, axis=0)
    return (
        jnp.einsum(
            "rbd,dq->rbq",
            owned,
            lax.all_gather(prequery, "rows", axis=0, tiled=True),
            preferred_element_type=jnp.float32,
        )
        * own_allowed[None, :, :]
    )


def solution(mesh):
    placed = (
        P("groups", "rows"),
        P("rows", None),
        P("rows", "groups", None),
        P("groups"),
        P("groups", None),
        P("groups"),
        P("groups"),
    )
    return jax.shard_map(
        shards,
        mesh=mesh,
        in_specs=placed,
        out_specs=P(None, ("groups", "rows"), None),
        check_vma=False,
    )
```

profile of v0, /device:TPU:0, one launch (start us, length us, event | category | flops | bytes accessed | tf_op | source)
XLA Modules:
  0.0 223.1 jit_solution(15777133985286591811)
XLA Ops:
  6.5 0.0 copy-start
  6.5 0.0 reduce-scatter.2.cloned.1.call-start
  6.5 17.2 %fusion.6 = f32[4096,512]{1,0:T(8,128)} fusion(f32[256,4096]{1,0:T(8,128)} %param.8, f32[512,256]{1,0:T(8,128)} %param.7), kind=kOutput, calls=%fused_computation.16 | convolution fusion | flops 6442450944 | bytes 13107200 | tf_op jit(solution)/shard_map/fd,qf->dq/dot_general | solution.py:20
  23.7 0.0 copy-start.4
  23.7 0.0 reduce-scatter.2.cloned.1.call-update
  23.8 0.2 all-gather.2.cloned.1.call-start
  24.0 107.3 %reduce-scatter.2.cloned.1.call-done = f32[256,512]{1,0:T(8,128)} async-done(((f32[4096,512]{1,0:T(8,128)}), f32[256,512]{1,0:T(8,128)}) %reduce-scatter.2.cloned.1.call-update) | async-done | bytes 524304 | tf_op jit(solution)/shard_map/reduce_scatter | solution.py:19
  131.3 1.8 convert_element_type.2
  133.1 0.0 all-gather.2.cloned.1.call-update
  133.1 0.0 copy-done.4
  133.1 0.0 copy-done
  133.2 7.9 %gather_fusion = bf16[16,16,4096]{2,0,1:T(8,128)(2,1)} fusion(bf16[16,16,4096]{2,1,0:T(8,128)(2,1)S(1)} %copy-done, s32[1024]{0:T(1024)S(1)} %pad_clamp_fusion), kind=kCustom, calls=%fused_computation | custom fusion | bytes 4194368 | tf_op jit(solution)/shard_map/jit(_take)/gather | solution.py:32
  141.0 1.9 select_bitcast_fusion
  142.9 2.5 %copy.13 = bf16[16,16,4096]{2,0,1:T(8,128)(2,1)} copy(bf16[16,16,4096]{2,1,0:T(8,128)(2,1)S(1)} %select_bitcast_fusion) | data formatting | bytes 4194304 | tf_op jit(solution)/shard_map/jit(_take)/select_n | solution.py:32
  145.5 0.0 copy-start.1
  145.5 0.0 copy-start.2
  145.5 0.0 copy-start.3
  145.5 4.6 %all-to-all-start = ((bf16[16,16,4096]{2,0,1:T(8,128)(2,1)}), bf16[16,16,4096]{2,0,1:T(8,128)(2,1)}, u32[]{:S(2)}, u32[]{:S(2)}) async-start(bf16[16,16,4096]{2,0,1:T(8,128)(2,1)} %copy.13), calls=%async_computation | async-start | bytes 4194304 | tf_op jit(solution)/shard_map/all_to_all | solution.py:33
  150.1 0.6 dynamic_slice.3
  152.6 0.0 copy-done.1
  152.6 0.1 copy.14
  152.7 0.0 copy-done.2
  152.7 0.1 fusion.4
  152.8 0.0 copy-done.3
  152.8 0.3 fusion.1
  153.1 54.8 %all-to-all-done = bf16[16,16,4096]{2,0,1:T(8,128)(2,1)} async-done(((bf16[16,16,4096]{2,0,1:T(8,128)(2,1)}), bf16[16,16,4096]{2,0,1:T(8,128)(2,1)}, u32[]{:S(2)}, u32[]{:S(2)}) %all-to-all-start) | async-done | bytes 2097184 | tf_op jit(solution)/shard_map/all_to_all | solution.py:33
  207.9 2.9 %all-gather.2.cloned.1.call-done = bf16[4096,512]{1,0:T(8,128)(2,1)} async-done(((bf16[256,512]{1,0:T(8,128)(2,1)}), bf16[4096,512]{1,0:T(8,128)(2,1)}) %all-gather.2.cloned.1.call-update) | async-done | bytes 4194320 | tf_op jit(solution)/shard_map/all_gather | solution.py:40
  210.8 4.1 %fusion = f32[256,1,512]{2,0,1:T(8,128)S(1)} fusion(bf16[256,4096]{1,0:T(8,128)(2,1)} %bitcast.3, bf16[4096,512]{1,0:T(8,128)(2,1)} %all-gather.2.cloned.1.call-done, f32[512]{0:T(512)S(1)} %bitcast.16), kind=kOutput, calls=%fused_computation.3 | convolution fusion | flops 1073872896 | bytes 6817792 | tf_op jit(solution)/shard_map/rbd,dq->rbq/dot_general | solution.py:37
  214.9 1.3 copy.15
  (5 shorter events, 0.0 us)
Async XLA Ops:
  6.5 126.6 %copy-start = (bf16[16,16,4096]{2,1,0:T(8,128)(2,1)S(1)}, bf16[16,16,4096]{2,1,0:T(8,128)(2,1)}, u32[]{:S(2)}) copy-start(bf16[16,16,4096]{2,1,0:T(8,128)(2,1)} %param.9) | copy-start | bytes 6291460
  6.5 124.8 %reduce-scatter.2.cloned.1.call-start = ((), (), s32[]{:S(2)}) async-start(), calls=%async_computation.2 | async-start | bytes 8912896 | tf_op jit(solution)/shard_map/reduce_scatter | solution.py:19
  23.7 109.4 %copy-start.4 = (s32[16]{0:T(128)S(1)}, s32[16]{0:T(128)}, u32[]{:S(2)}) copy-start(s32[16]{0:T(128)} %param.13) | copy-start | bytes 196
  23.8 187.1 %all-gather.2.cloned.1.call-start = ((), (), s32[]{:S(2)}) async-start(), calls=%async_computation.3 | async-start | bytes 4456448 | tf_op jit(solution)/shard_map/all_gather | solution.py:40
  145.5 7.2 %copy-start.1 = (s32[8,12]{1,0:T(8,128)S(1)}, s32[8,12]{1,0:T(8,128)}, u32[]{:S(2)}) copy-start(s32[8,12]{1,0:T(8,128)} %param.11) | copy-start | bytes 1156
  145.5 7.3 %copy-start.2 = (s32[8]{0:T(128)S(1)}, s32[8]{0:T(128)}, u32[]{:S(2)}) copy-start(s32[8]{0:T(128)} %param.12) | copy-start | bytes 100
  145.5 7.4 %copy-start.3 = (s32[512]{0:T(512)S(1)}, s32[512]{0:T(512)}, u32[]{:S(2)}) copy-start(s32[512]{0:T(512)} %param.10) | copy-start | bytes 6148
  145.5 62.5 %all-to-all-start = ((bf16[16,16,4096]{2,0,1:T(8,128)(2,1)}), bf16[16,16,4096]{2,0,1:T(8,128)(2,1)}, u32[]{:S(2)}, u32[]{:S(2)}) async-start(bf16[16,16,4096]{2,0,1:T(8,128)(2,1)} %copy.13), calls=%async_computation | async-start | bytes 4194304 | tf_op jit(solution)/shard_map/all_to_all | solution.py:33
Sparse Core Ops, SparseCore 0:
  23.9 107.3 reduce-scatter.1
  133.5 77.3 all-gather.1
where the time goes:
time: 227 us; the launch traced here: 223 us
  waiting for transfers between devices  165 us (73%)
  matrix products  21.5 us (9%)
  between operations  15.4 us (7%)
  local copies, waits for them, and re-layouts  12.4 us (5%)
  starting transfers between devices  4.84 us (2%)
  other arithmetic  3.83 us (2%)
    reduce_scatter x1, waiting for transfers between devices, shards(): lax.psum_scatter(jnp.einsum('fd,qf->dq', precond, queries, precision=lax....  107 us
    all_to_all x1, waiting for transfers between devices, shards(): lax.all_to_all(ordered, 'rows', split_axis=1, concat_axis=0, tiled=True)  54.8 us
    dot_general x1, matrix products, shards(): jnp.einsum('fd,qf->dq', precond, queries, precision=lax.Precision.HIGHEST...  17.2 us
    gather x1, local copies, waits for them, and re-layouts, shards(): ordered = jnp.take(train, slot_block, axis=1)  7.85 us
    all_to_all x1, starting transfers between devices, shards(): lax.all_to_all(ordered, 'rows', split_axis=1, concat_axis=0, tiled=True)  4.62 us
  transfers between devices with their start and end apart: 3, of which 3 were waited for; matrix products, arithmetic and copies ran while one was open for 6% of the time, Pallas kernels for 0%

commit v1 on v0

v1 whole, which is shorter than its diff:
```python
import jax
import jax.numpy as jnp
from jax import lax
from jax.sharding import PartitionSpec as P

CORES = 2
CHUNKS = 4
UNIT = 4.0


def listed_mask(query_cluster, cand_blocks, cand_count, nblocks):
    nclusters = cand_blocks.shape[0]
    valid = jnp.arange(cand_blocks.shape[1])[None, :] < cand_count[:, None]
    hits = (cand_blocks[:, :, None] == jnp.arange(nblocks)[None, None, :]) & valid[:, :, None]
    listed = jnp.any(hits, axis=1).astype(jnp.float32)
    onehot = (query_cluster[:, None] == jnp.arange(nclusters)[None, :]).astype(jnp.float32)
    return jnp.dot(listed.T, onehot.T, preferred_element_type=jnp.float32)


def shards(queries, precond, train, query_cluster, cand_blocks, cand_count, slot_block):
    n = lax.axis_size("rows")
    chips = n // CORES
    ny = 1 << ((chips.bit_length() - 1) // 2)
    nz = chips // ny
    me = lax.axis_index("rows")
    core = me % CORES
    y = (me // CORES) % ny
    z = me // (CORES * ny)

    examples, nblocks, width = train.shape
    nq = queries.shape[0]
    half = nq // CORES

    def swap(value, step):
        return lax.ppermute(value, "rows", [(r, r ^ step) for r in range(n)])

    def pack(value):
        return (value * UNIT).astype(jnp.float16)

    def unpack(value):
        return value.astype(jnp.float32) * (1.0 / UNIT)

    def reduce_scatter(value, place, count, stride):
        rows = value.shape[0] // count
        got = [
            swap(pack(lax.dynamic_slice_in_dim(value, (place ^ k) * rows, rows)), k * stride)
            for k in range(1, count)
        ]
        total = lax.dynamic_slice_in_dim(value, place * rows, rows)
        for part in got:
            total = total + unpack(part)
        return total

    def gather(value, place, count, stride):
        rows = value.shape[0]
        full = jnp.zeros((rows * count,) + value.shape[1:], value.dtype)
        full = lax.dynamic_update_slice_in_dim(full, value, place * rows, 0)
        for k in range(1, count):
            full = lax.dynamic_update_slice_in_dim(full, swap(value, k * stride), (place ^ k) * rows, 0)
        return full

    both = jnp.concatenate([train, swap(train, 1)], axis=0).reshape(CORES * examples * nblocks, width)

    mine = lax.dynamic_slice_in_dim(queries, core * half, half)
    other = lax.dynamic_slice_in_dim(queries, (1 - core) * half, half)

    def product(columns, rows):
        return lax.dot_general(
            columns, rows, (((0,), (1,)), ((), ())),
            precision=lax.Precision.HIGH, preferred_element_type=jnp.float32,
        )

    depth = width // CHUNKS
    prequery = []
    for chunk in range(CHUNKS):
        columns = precond[:, chunk * depth:(chunk + 1) * depth]
        sent = swap(pack(product(columns, other)), 1)
        value = product(columns, mine) + unpack(sent)
        value = reduce_scatter(value, y, ny, CORES)
        value = reduce_scatter(value, z, nz, CORES * ny)
        value = gather(value.astype(jnp.bfloat16), z, nz, CORES * ny)
        prequery.append(gather(value, y, ny, CORES))
    prequery = jnp.concatenate(prequery, axis=0)

    raw = jnp.dot(both, prequery, preferred_element_type=jnp.float32)
    raw = raw.reshape(CORES * examples, nblocks, half)
    ordered = jnp.take(jnp.swapaxes(raw, 0, 1), slot_block, axis=0, mode="clip")
    owned_count = nblocks // n
    ordered = ordered.reshape(n, owned_count, CORES * examples, half)
    got = lax.all_to_all(ordered, "rows", split_axis=0, concat_axis=0, tiled=True)
    got = got.reshape(chips, CORES, owned_count, CORES, examples, half)
    got = jnp.stack([got[:, 0], got[:, 1, :, ::-1]], axis=4)
    got = got.transpose(0, 2, 3, 1, 4, 5).reshape(n * examples, owned_count, nq)

    allowed = listed_mask(query_cluster, cand_blocks, cand_count, nblocks)
    slots = lax.dynamic_slice_in_dim(slot_block, me * owned_count, owned_count)
    return got * jnp.take(allowed, slots, axis=0, mode="clip")[None]


def solution(mesh):
    placed = (
        P("groups", "rows"),
        P("rows", None),
        P("rows", "groups", None),
        P("groups"),
        P("groups", None),
        P("groups"),
        P("groups"),
    )
    return jax.shard_map(
        shards,
        mesh=mesh,
        in_specs=placed,
        out_specs=P(None, ("groups", "rows"), None),
        check_vma=False,
    )
```

time: 227 us -> 136 us (0.60); the launches traced: 223 us -> 135 us
  waiting for transfers between devices: 165 us -> 37.1 us
  starting transfers between devices: 4.84 us -> 61.5 us
  between operations: 15.4 us -> 0.77 us
    reduce_scatter x1 -> x0, waiting for transfers between devices: 107 us -> none  [shards(): lax.psum_scatter(jnp.einsum('fd,qf->dq', precond, queries, precision=lax....]
    ppermute x0 -> x37, starting transfers between devices: none -> 57.9 us  [swap(): return lax.ppermute(value, 'rows', [(r, r ^ step) for r in range(n)])]
    all_to_all x1, waiting for transfers between devices: 54.8 us -> 12.6 us  [shards(): lax.all_to_all(ordered, 'rows', split_axis=0, concat_axis=0, tiled=True)]
    ppermute x0 -> x37, waiting for transfers between devices: none -> 24.4 us  [swap(): return lax.ppermute(value, 'rows', [(r, r ^ step) for r in range(n)])]
    gather x1 -> x2, local copies, waits for them, and re-layouts: 7.85 us -> 2.02 us  [the longest x1 1.37 us: shards(): ordered = jnp.take(jnp.swapaxes(raw, 0, 1), slot_block, axis=0, mode='clip')]
    all_gather x1 -> x0, waiting for transfers between devices: 2.9 us -> none  [shards(): lax.all_gather(prequery, 'rows', axis=0, tiled=True)]
    select_n x1 -> x0, local copies, waits for them, and re-layouts: 2.51 us -> none  [shards(): ordered = jnp.take(train, slot_block, axis=1)]
    dot_general x2 -> x9, matrix products: 21.3 us -> 22.8 us  [the longest x8 14.4 us: product(): lax.dot_general(columns, rows, (((0,), (1,)), ((), ())), precision=lax.Pr...]
  transfers between devices with their start and end apart: 3 -> 38, of which waited for: 3 -> 14; matrix products, arithmetic and copies ran while one was open for 6% -> 14% of each run, Pallas kernels for 0% -> 0%
where the time goes in v1:
time: 136 us; the launch traced here: 135 us
  starting transfers between devices  61.5 us (45%)
  waiting for transfers between devices  37.1 us (27%)
  matrix products  23 us (17%)
  local copies, waits for them, and re-layouts  10.4 us (8%)
  other arithmetic  2.33 us (2%)
    ppermute x37, starting transfers between devices, swap(): return lax.ppermute(value, 'rows', [(r, r ^ step) for r in range(n)])  57.9 us
    ppermute x37, waiting for transfers between devices, swap(): return lax.ppermute(value, 'rows', [(r, r ^ step) for r in range(n)])  24.4 us
    dot_general x8, matrix products, product(): lax.dot_general(columns, rows, (((0,), (1,)), ((), ())), precision=lax.Pr...  14.4 us
    all_to_all x1, waiting for transfers between devices, shards(): lax.all_to_all(ordered, 'rows', split_axis=0, concat_axis=0, tiled=True)  12.6 us
    dot_general x1, matrix products, shards(): raw = jnp.dot(both, prequery, preferred_element_type=jnp.float32)  8.4 us
    all_to_all x1, starting transfers between devices, shards(): lax.all_to_all(ordered, 'rows', split_axis=0, concat_axis=0, tiled=True)  3.57 us
  transfers between devices with their start and end apart: 38, of which 14 were waited for; matrix products, arithmetic and copies ran while one was open for 14% of the time, Pallas kernels for 0%

profile of v1, /device:TPU:0, one launch (start us, length us, event | category | flops | bytes accessed | tf_op | source)
XLA Modules:
  0.0 135.1 jit_solution(11278150234380723066)
XLA Ops:
  0.0 1.0 copy-done
  1.0 2.7 %fusion.17 = f16[1024,256]{0,1:T(8,128)(2,1)} fusion(f32[256,4096]{1,0:T(8,128)} %param.8, f32[512,256]{1,0:T(8,128)S(1)} %copy-done, s32[]{:T(128)S(6)} %select_n.38), kind=kOutput, calls=%fused_computation.27 | convolution fusion | flops 403177472 | bytes 1835012 | tf_op jit(solution)/shard_map/dot_general | solution.py:68
  4.2 2.6 %fusion.16 = f16[1024,256]{0,1:T(8,128)(2,1)} fusion(f32[256,4096]{1,0:T(8,128)} %param.8, f32[512,256]{1,0:T(8,128)S(1)} %copy-done, s32[]{:T(128)S(6)} %select_n.38), kind=kOutput, calls=%fused_computation.26 | convolution fusion | flops 403177472 | bytes 1835012 | tf_op jit(solution)/shard_map/dot_general | solution.py:68
  6.9 1.9 %fusion.15 = f16[1024,256]{0,1:T(8,128)(2,1)S(1)} fusion(f32[256,4096]{1,0:T(8,128)} %param.8, f32[512,256]{1,0:T(8,128)S(1)} %copy-done, s32[]{:T(128)S(6)} %select_n.38), kind=kOutput, calls=%fused_computation.25 | convolution fusion | flops 403177472 | bytes 1835012 | tf_op jit(solution)/shard_map/dot_general | solution.py:68
  9.3 1.9 %fusion.14 = f16[1024,256]{0,1:T(8,128)(2,1)S(1)} fusion(f32[256,4096]{1,0:T(8,128)} %param.8, f32[512,256]{1,0:T(8,128)S(1)} %copy-done, s32[]{:T(128)S(6)} %select_n.38), kind=kOutput, calls=%fused_computation.24 | convolution fusion | flops 403177472 | bytes 1835012 | tf_op jit(solution)/shard_map/dot_general | solution.py:68
  11.7 2.2 %multiply_add_fusion.3 = f32[1024,256]{0,1:T(8,128)S(1)} fusion(f16[1024,256]{0,1:T(8,128)(2,1)} %collective-permute-done.1, f32[256,4096]{1,0:T(8,128)} %param.8, f32[512,256]{1,0:T(8,128)S(1)} %copy-done, s32[]{:T(128)S(6)} %select_n.37), kind=kOutput, calls=%fused_computation.32 | convolution fusion | flops 403439616 | bytes 2883588 | tf_op jit(solution)/shard_map/dot_general | solution.py:68
  14.0 2.7 %collective-permute-start.2 = (f16[512,256]{0,1:T(8,128)(2,1)S(1)}, f16[512,256]{0,1:T(8,128)(2,1)S(1)}, u32[]{:S(2)}, u32[]{:S(2)}) collective-permute-start(f16[512,256]{0,1:T(8,128)(2,1)S(1)} %multiply_convert_fusion.3), channel_id=1, source_target_pairs={{0,2},{1,3},{2,0},{3,1},{4,6},{5,7},{6,4},{7,5},{8,10},{9,11},{10,... | collective-permute-start | bytes 786440 | tf_op jit(solution)/shard_map/ppermute | solution.py:35
  16.6 1.9 %multiply_add_fusion.2 = f32[1024,256]{0,1:T(8,128)S(1)} fusion(f16[1024,256]{0,1:T(8,128)(2,1)S(1)} %collective-permute-done.10, f32[256,4096]{1,0:T(8,128)} %param.8, f32[512,256]{1,0:T(8,128)S(1)} %copy-done, s32[]{:T(128)S(6)} %select_n.37), kind=kOutput, calls=%fused_computation.31 | convolution fusion | flops 403439616 | bytes 2883588 | tf_op jit(solution)/shard_map/dot_general | solution.py:68
  19.4 2.1 %collective-permute-start.20 = (f16[512,256]{0,1:T(8,128)(2,1)S(1)}, f16[512,256]{0,1:T(8,128)(2,1)S(1)}, u32[]{:S(2)}, u32[]{:S(2)}) collective-permute-start(f16[512,256]{0,1:T(8,128)(2,1)S(1)} %multiply_convert_fusion.1), channel_id=1, source_target_pairs={{0,2},{1,3},{2,0},{3,1},{4,6},{5,7},{6,4},{7,5},{8,10},{9,11},{10,... | collective-permute-start | bytes 786440 | tf_op jit(solution)/shard_map/ppermute | solution.py:35
  22.2 1.5 %collective-permute-done.2 = f16[512,256]{0,1:T(8,128)(2,1)S(1)} collective-permute-done((f16[512,256]{0,1:T(8,128)(2,1)S(1)}, f16[512,256]{0,1:T(8,128)(2,1)S(1)}, u32[]{:S(2)}, u32[]{:S(2)}) %collective-permute-start.2) | collective-permute-done | bytes 262176 | tf_op jit(solution)/shard_map/ppermute | solution.py:35
  23.9 2.1 %collective-permute-start.3 = (f16[128,256]{0,1:T(8,128)(2,1)S(1)}, f16[128,256]{0,1:T(8,128)(2,1)S(1)}, u32[]{:S(2)}, u32[]{:S(2)}) collective-permute-start(f16[128,256]{0,1:T(8,128)(2,1)S(1)} %get-tuple-element.18), channel_id=1, source_target_pairs={{0,4},{1,5},{2,6},{3,7},{4,0},{5,1},{6,2},{7,3},{8,12},{9,13},{10,... | collective-permute-start | bytes 196616 | tf_op jit(solution)/shard_map/ppermute | solution.py:35
  26.0 3.4 %collective-permute-done.11 = f16[512,256]{0,1:T(8,128)(2,1)S(1)} collective-permute-done((f16[512,256]{0,1:T(8,128)(2,1)S(1)}, f16[512,256]{0,1:T(8,128)(2,1)S(1)}, u32[]{:S(2)}, u32[]{:S(2)}) %collective-permute-start.11) | collective-permute-done | bytes 262176 | tf_op jit(solution)/shard_map/ppermute | solution.py:35
  29.4 3.0 %collective-permute-start.4 = (f16[128,256]{0,1:T(8,128)(2,1)S(1)}, f16[128,256]{0,1:T(8,128)(2,1)S(1)}, u32[]{:S(2)}, u32[]{:S(2)}) collective-permute-start(f16[128,256]{0,1:T(8,128)(2,1)S(1)} %get-tuple-element.20), channel_id=1, source_target_pairs={{0,8},{1,9},{2,10},{3,11},{4,12},{5,13},{6,14},{7,15},{8,0},{9,1},... | collective-permute-start | bytes 196616 | tf_op jit(solution)/shard_map/ppermute | solution.py:35
  32.5 2.5 %collective-permute-done.20 = f16[512,256]{0,1:T(8,128)(2,1)S(1)} collective-permute-done((f16[512,256]{0,1:T(8,128)(2,1)S(1)}, f16[512,256]{0,1:T(8,128)(2,1)S(1)}, u32[]{:S(2)}, u32[]{:S(2)}) %collective-permute-start.20) | collective-permute-done | bytes 262176 | tf_op jit(solution)/shard_map/ppermute | solution.py:35
  35.0 4.0 %collective-permute-start.5 = (f16[128,256]{0,1:T(8,128)(2,1)S(1)}, f16[128,256]{0,1:T(8,128)(2,1)S(1)}, u32[]{:S(2)}, u32[]{:S(2)}) collective-permute-start(f16[128,256]{0,1:T(8,128)(2,1)S(1)} %get-tuple-element.19), channel_id=1, source_target_pairs={{0,12},{1,13},{2,14},{3,15},{4,8},{5,9},{6,10},{7,11},{8,4},{9,5},... | collective-permute-start | bytes 196616 | tf_op jit(solution)/shard_map/ppermute | solution.py:35
  39.3 1.1 collective-permute-done.29
  40.4 1.8 %collective-permute-start.12 = (f16[128,256]{0,1:T(8,128)(2,1)S(1)}, f16[128,256]{0,1:T(8,128)(2,1)S(1)}, u32[]{:S(2)}, u32[]{:S(2)}) collective-permute-start(f16[128,256]{0,1:T(8,128)(2,1)S(1)} %get-tuple-element.21), channel_id=1, source_target_pairs={{0,4},{1,5},{2,6},{3,7},{4,0},{5,1},{6,2},{7,3},{8,12},{9,13},{10,... | collective-permute-start | bytes 196616 | tf_op jit(solution)/shard_map/ppermute | solution.py:35
  42.6 2.8 %collective-permute-start.22 = (f16[128,256]{0,1:T(8,128)(2,1)S(1)}, f16[128,256]{0,1:T(8,128)(2,1)S(1)}, u32[]{:S(2)}, u32[]{:S(2)}) collective-permute-start(f16[128,256]{0,1:T(8,128)(2,1)S(1)} %get-tuple-element.26), channel_id=1, source_target_pairs={{0,8},{1,9},{2,10},{3,11},{4,12},{5,13},{6,14},{7,15},{8,0},{9,1},... | collective-permute-start | bytes 196616 | tf_op jit(solution)/shard_map/ppermute | solution.py:35
  45.5 1.3 collective-permute-start.23
  46.9 3.0 %collective-permute-start.13 = (f16[128,256]{0,1:T(8,128)(2,1)S(1)}, f16[128,256]{0,1:T(8,128)(2,1)S(1)}, u32[]{:S(2)}, u32[]{:S(2)}) collective-permute-start(f16[128,256]{0,1:T(8,128)(2,1)S(1)} %get-tuple-element.23), channel_id=1, source_target_pairs={{0,8},{1,9},{2,10},{3,11},{4,12},{5,13},{6,14},{7,15},{8,0},{9,1},... | collective-permute-start | bytes 196616 | tf_op jit(solution)/shard_map/ppermute | solution.py:35
  49.9 4.5 %collective-permute-start.14 = (f16[128,256]{0,1:T(8,128)(2,1)S(1)}, f16[128,256]{0,1:T(8,128)(2,1)S(1)}, u32[]{:S(2)}, u32[]{:S(2)}) collective-permute-start(f16[128,256]{0,1:T(8,128)(2,1)S(1)} %get-tuple-element.22), channel_id=1, source_target_pairs={{0,12},{1,13},{2,14},{3,15},{4,8},{5,9},{6,10},{7,11},{8,4},{9,5},... | collective-permute-start | bytes 196616 | tf_op jit(solution)/shard_map/ppermute | solution.py:35
  54.4 0.9 collective-permute-start.30
  56.5 2.5 %collective-permute-start.32 = (f16[128,256]{0,1:T(8,128)(2,1)S(1)}, f16[128,256]{0,1:T(8,128)(2,1)S(1)}, u32[]{:S(2)}, u32[]{:S(2)}) collective-permute-start(f16[128,256]{0,1:T(8,128)(2,1)S(1)} %get-tuple-element.28), channel_id=1, source_target_pairs={{0,12},{1,13},{2,14},{3,15},{4,8},{5,9},{6,10},{7,11},{8,4},{9,5},... | collective-permute-start | bytes 196616 | tf_op jit(solution)/shard_map/ppermute | solution.py:35
  59.7 1.9 %collective-permute-start.7 = (bf16[128,256]{0,1:T(8,128)(2,1)S(1)}, bf16[128,256]{0,1:T(8,128)(2,1)S(1)}, u32[]{:S(2)}, u32[]{:S(2)}) collective-permute-start(bf16[128,256]{0,1:T(8,128)(2,1)S(1)} %add_convert_fusion.3), channel_id=1, source_target_pairs={{0,8},{1,9},{2,10},{3,11},{4,12},{5,13},{6,14},{7,15},{8,0},{9,1},... | collective-permute-start | bytes 196616 | tf_op jit(solution)/shard_map/ppermute | solution.py:35
  61.6 1.0 collective-permute-done.31
  62.6 1.7 %collective-permute-start.8 = (bf16[128,256]{0,1:T(8,128)(2,1)S(1)}, bf16[128,256]{0,1:T(8,128)(2,1)S(1)}, u32[]{:S(2)}, u32[]{:S(2)}) collective-permute-start(bf16[128,256]{0,1:T(8,128)(2,1)S(1)} %add_convert_fusion.3), channel_id=1, source_target_pairs={{0,12},{1,13},{2,14},{3,15},{4,8},{5,9},{6,10},{7,11},{8,4},{9,5},... | collective-permute-start | bytes 196616 | tf_op jit(solution)/shard_map/ppermute | solution.py:35
  64.3 2.7 %collective-permute-start.15 = (bf16[128,256]{0,1:T(8,128)(2,1)S(1)}, bf16[128,256]{0,1:T(8,128)(2,1)S(1)}, u32[]{:S(2)}, u32[]{:S(2)}) collective-permute-start(bf16[128,256]{0,1:T(8,128)(2,1)S(1)} %add_convert_fusion.2), channel_id=1, source_target_pairs={{0,4},{1,5},{2,6},{3,7},{4,0},{5,1},{6,2},{7,3},{8,12},{9,13},{10,... | collective-permute-start | bytes 196616 | tf_op jit(solution)/shard_map/ppermute | solution.py:35
  67.7 3.7 %collective-permute-start.17 = (bf16[128,256]{0,1:T(8,128)(2,1)S(1)}, bf16[128,256]{0,1:T(8,128)(2,1)S(1)}, u32[]{:S(2)}, u32[]{:S(2)}) collective-permute-start(bf16[128,256]{0,1:T(8,128)(2,1)S(1)} %add_convert_fusion.2), channel_id=1, source_target_pairs={{0,12},{1,13},{2,14},{3,15},{4,8},{5,9},{6,10},{7,11},{8,4},{9,5},... | collective-permute-start | bytes 196616 | tf_op jit(solution)/shard_map/ppermute | solution.py:35
  72.5 1.5 %collective-permute-done.16 = bf16[128,256]{0,1:T(8,128)(2,1)S(1)} collective-permute-done((bf16[128,256]{0,1:T(8,128)(2,1)S(1)}, bf16[128,256]{0,1:T(8,128)(2,1)S(1)}, u32[]{:S(2)}, u32[]{:S(2)}) %collective-permute-start.16) | collective-permute-done | bytes 65568 | tf_op jit(solution)/shard_map/ppermute | solution.py:35
  74.0 3.5 %collective-permute-start.26 = (bf16[128,256]{0,1:T(8,128)(2,1)S(1)}, bf16[128,256]{0,1:T(8,128)(2,1)S(1)}, u32[]{:S(2)}, u32[]{:S(2)}) collective-permute-start(bf16[128,256]{0,1:T(8,128)(2,1)S(1)} %add_convert_fusion.1), channel_id=1, source_target_pairs={{0,12},{1,13},{2,14},{3,15},{4,8},{5,9},{6,10},{7,11},{8,4},{9,5},... | collective-permute-start | bytes 196616 | tf_op jit(solution)/shard_map/ppermute | solution.py:35
  77.8 1.8 %collective-permute-start.34 = (bf16[128,256]{0,1:T(8,128)(2,1)S(1)}, bf16[128,256]{0,1:T(8,128)(2,1)S(1)}, u32[]{:S(2)}, u32[]{:S(2)}) collective-permute-start(bf16[128,256]{0,1:T(8,128)(2,1)S(1)} %add_convert_fusion), channel_id=1, source_target_pairs={{0,8},{1,9},{2,10},{3,11},{4,12},{5,13},{6,14},{7,15},{8,0},{9,1},... | collective-permute-start | bytes 196616 | tf_op jit(solution)/shard_map/ppermute | solution.py:35
  79.7 1.5 %collective-permute-done.25 = bf16[128,256]{0,1:T(8,128)(2,1)S(1)} collective-permute-done((bf16[128,256]{0,1:T(8,128)(2,1)S(1)}, bf16[128,256]{0,1:T(8,128)(2,1)S(1)}, u32[]{:S(2)}, u32[]{:S(2)}) %collective-permute-start.25) | collective-permute-done | bytes 65568 | tf_op jit(solution)/shard_map/ppermute | solution.py:35
  81.2 1.2 collective-permute-start.35
  82.6 3.4 %collective-permute-start.9 = (bf16[512,256]{1,0:T(8,128)(2,1)S(1)}, bf16[512,256]{1,0:T(8,128)(2,1)S(1)}, u32[]{:S(2)}, u32[]{:S(2)}) collective-permute-start(bf16[512,256]{1,0:T(8,128)(2,1)S(1)} %constant_dynamic-update-slice_fusion.20), channel_id=1, source_target_pairs={{0,2},{1,3},{2,0},{3,1},{4,6},{5,7},{6,4},{7,5},{8,10},{9,11},{10,... | collective-permute-start | bytes 786440 | tf_op jit(solution)/shard_map/ppermute | solution.py:35
  86.4 2.1 %collective-permute-start.27 = (bf16[512,256]{1,0:T(8,128)(2,1)S(1)}, bf16[512,256]{1,0:T(8,128)(2,1)}, u32[]{:S(2)}, u32[]{:S(2)}) collective-permute-start(bf16[512,256]{1,0:T(8,128)(2,1)S(1)} %constant_dynamic-update-slice_fusion.8), channel_id=1, source_target_pairs={{0,2},{1,3},{2,0},{3,1},{4,6},{5,7},{6,4},{7,5},{8,10},{9,11},{10,... | collective-permute-start | bytes 786440 | tf_op jit(solution)/shard_map/ppermute | solution.py:35
  88.9 0.9 copy.80
  89.9 1.3 collective-permute-start.36
  91.3 1.9 %collective-permute-done.9 = bf16[512,256]{1,0:T(8,128)(2,1)S(1)} collective-permute-done((bf16[512,256]{1,0:T(8,128)(2,1)S(1)}, bf16[512,256]{1,0:T(8,128)(2,1)S(1)}, u32[]{:S(2)}, u32[]{:S(2)}) %collective-permute-start.9) | collective-permute-done | bytes 262176 | tf_op jit(solution)/shard_map/ppermute | solution.py:35
  93.2 5.7 %collective-permute-done.18 = bf16[512,256]{1,0:T(8,128)(2,1)} collective-permute-done((bf16[512,256]{1,0:T(8,128)(2,1)S(1)}, bf16[512,256]{1,0:T(8,128)(2,1)}, u32[]{:S(2)}, u32[]{:S(2)}) %collective-permute-start.18) | collective-permute-done | bytes 262176 | tf_op jit(solution)/shard_map/ppermute | solution.py:35
  98.9 1.0 constant_dynamic-update-slice_fusion.12
  99.9 1.9 %collective-permute-done.27 = bf16[512,256]{1,0:T(8,128)(2,1)} collective-permute-done((bf16[512,256]{1,0:T(8,128)(2,1)S(1)}, bf16[512,256]{1,0:T(8,128)(2,1)}, u32[]{:S(2)}, u32[]{:S(2)}) %collective-permute-start.27) | collective-permute-done | bytes 262176 | tf_op jit(solution)/shard_map/ppermute | solution.py:35
  101.8 1.0 constant_dynamic-update-slice_fusion.6
  102.7 1.7 %collective-permute-done.36 = bf16[512,256]{1,0:T(8,128)(2,1)S(1)} collective-permute-done((bf16[512,256]{1,0:T(8,128)(2,1)S(1)}, bf16[512,256]{1,0:T(8,128)(2,1)S(1)}, u32[]{:S(2)}, u32[]{:S(2)}) %collective-permute-start.36) | collective-permute-done | bytes 262176 | tf_op jit(solution)/shard_map/ppermute | solution.py:35
  104.5 8.4 %fusion.18 = f32[16,32,256]{2,0,1:T(8,128)S(1)} fusion(bf16[1024,256]{1,0:T(8,128)(2,1)S(1)} %constant_dynamic-update-slice_fusion, bf16[1024,256]{1,0:T(8,128)(2,1)S(1)} %constant_dynamic-update-slice_fusion.6, bf16[1024,256]{1,0:T(8,128)(2,1)S(1)} %constant_dynamic-update-slice_fusion.12, bf16[1024,256]{1,0:T(8,128)(2,1)S(1)} %constant_dynamic-update-slice_fusion.18, ...), kind=kOutput, calls=%fused_computation.28 | convolution fusion | flops 1084227584 | bytes 6815744 | tf_op jit(solution)/shard_map/dot_general | solution.py:85
  113.3 1.4 %gather_fusion = f32[16,32,256]{2,1,0:T(8,128)} fusion(f32[16,32,256]{2,1,0:T(8,128)S(1)} %copy.81, s32[1024]{0:T(1024)S(1)} %pad_clamp_fusion), kind=kCustom, calls=%fused_computation | custom fusion | bytes 1048640 | tf_op jit(solution)/shard_map/jit(_take)/gather | solution.py:87
  114.6 3.6 %all-to-all-start = ((f32[16,1,32,256]{3,2,1,0:T(8,128)}), f32[16,1,32,256]{3,2,1,0:T(8,128)S(1)}, u32[]{:S(2)}, u32[]{:S(2)}) async-start(f32[16,1,32,256]{3,2,1,0:T(8,128)} %bitcast.11), calls=%async_computation | async-start | bytes 1048576 | tf_op jit(solution)/shard_map/all_to_all | solution.py:90
  120.0 12.6 %all-to-all-done = f32[16,1,32,256]{3,2,1,0:T(8,128)S(1)} async-done(((f32[16,1,32,256]{3,2,1,0:T(8,128)}), f32[16,1,32,256]{3,2,1,0:T(8,128)S(1)}, u32[]{:S(2)}, u32[]{:S(2)}) %all-to-all-start) | async-done | bytes 524320 | tf_op jit(solution)/shard_map/all_to_all | solution.py:90
  134.0 1.2 broadcast_multiply_fusion
  (128 shorter events, 12.4 us)
Async XLA Ops:
  0.0 1.0 copy-start
  0.0 11.7 %copy-start.3 = (s32[16]{0:T(128)S(1)}, s32[16]{0:T(128)}, u32[]{:S(2)}) copy-start(s32[16]{0:T(128)} %param.13) | copy-start | bytes 196
  3.7 8.0 %collective-permute-start.1 = (f16[1024,256]{0,1:T(8,128)(2,1)}, f16[1024,256]{0,1:T(8,128)(2,1)}, u32[]{:S(2)}, u32[]{:S(2)}) collective-permute-start(f16[1024,256]{0,1:T(8,128)(2,1)} %fusion.17), channel_id=1, source_target_pairs={{0,1},{1,0},{2,3},{3,2},{4,5},{5,4},{6,7},{7,6},{8,9},{9,8},{10,11... | collective-permute-start | bytes 1572872 | tf_op jit(solution)/shard_map/ppermute | solution.py:35
  6.8 9.8 %collective-permute-start.10 = (f16[1024,256]{0,1:T(8,128)(2,1)}, f16[1024,256]{0,1:T(8,128)(2,1)S(1)}, u32[]{:S(2)}, u32[]{:S(2)}) collective-permute-start(f16[1024,256]{0,1:T(8,128)(2,1)} %fusion.16), channel_id=1, source_target_pairs={{0,1},{1,0},{2,3},{3,2},{4,5},{5,4},{6,7},{7,6},{8,9},{9,8},{10,11... | collective-permute-start | bytes 1572872 | tf_op jit(solution)/shard_map/ppermute | solution.py:35
  8.7 9.9 %collective-permute-start.19 = (f16[1024,256]{0,1:T(8,128)(2,1)S(1)}, f16[1024,256]{0,1:T(8,128)(2,1)S(1)}, u32[]{:S(2)}, u32[]{:S(2)}) collective-permute-start(f16[1024,256]{0,1:T(8,128)(2,1)S(1)} %fusion.15), channel_id=1, source_target_pairs={{0,1},{1,0},{2,3},{3,2},{4,5},{5,4},{6,7},{7,6},{8,9},{9,8},{10,11... | collective-permute-start | bytes 1572872 | tf_op jit(solution)/shard_map/ppermute | solution.py:35
  11.1 10.3 %collective-permute-start.28 = (f16[1024,256]{0,1:T(8,128)(2,1)S(1)}, f16[1024,256]{0,1:T(8,128)(2,1)S(1)}, u32[]{:S(2)}, u32[]{:S(2)}) collective-permute-start(f16[1024,256]{0,1:T(8,128)(2,1)S(1)} %fusion.14), channel_id=1, source_target_pairs={{0,1},{1,0},{2,3},{3,2},{4,5},{5,4},{6,7},{7,6},{8,9},{9,8},{10,11... | collective-permute-start | bytes 1572872 | tf_op jit(solution)/shard_map/ppermute | solution.py:35
  11.2 93.3 %collective-permute-start = (bf16[16,16,4096]{2,1,0:T(8,128)(2,1)}, bf16[16,16,4096]{2,1,0:T(8,128)(2,1)}, u32[]{:S(2)}, u32[]{:S(2)}) collective-permute-start(bf16[16,16,4096]{2,1,0:T(8,128)(2,1)} %param.9), channel_id=1, source_target_pairs={{0,1},{1,0},{2,3},{3,2},{4,5},{5,4},{6,7},{7,6},{8,9},{9,8},{10,11... | collective-permute-start | bytes 6291464 | tf_op jit(solution)/shard_map/ppermute | solution.py:35
  11.7 7.0 %copy-start.1 = (f32[256,4096]{1,0:T(8,128)S(1)}, f32[256,4096]{1,0:T(8,128)}, u32[]{:S(2)}) copy-start(f32[256,4096]{1,0:T(8,128)} %param.8) | copy-start | bytes 12582916
  14.0 9.8 %collective-permute-start.2 = (f16[512,256]{0,1:T(8,128)(2,1)S(1)}, f16[512,256]{0,1:T(8,128)(2,1)S(1)}, u32[]{:S(2)}, u32[]{:S(2)}) collective-permute-start(f16[512,256]{0,1:T(8,128)(2,1)S(1)} %multiply_convert_fusion.3), channel_id=1, source_target_pairs={{0,2},{1,3},{2,0},{3,1},{4,6},{5,7},{6,4},{7,5},{8,10},{9,11},{10,... | collective-permute-start | bytes 786440 | tf_op jit(solution)/shard_map/ppermute | solution.py:35
  18.6 10.8 %collective-permute-start.11 = (f16[512,256]{0,1:T(8,128)(2,1)S(1)}, f16[512,256]{0,1:T(8,128)(2,1)S(1)}, u32[]{:S(2)}, u32[]{:S(2)}) collective-permute-start(f16[512,256]{0,1:T(8,128)(2,1)S(1)} %multiply_convert_fusion.2), channel_id=1, source_target_pairs={{0,2},{1,3},{2,0},{3,1},{4,6},{5,7},{6,4},{7,5},{8,10},{9,11},{10,... | collective-permute-start | bytes 786440 | tf_op jit(solution)/shard_map/ppermute | solution.py:35
  19.4 15.6 %collective-permute-start.20 = (f16[512,256]{0,1:T(8,128)(2,1)S(1)}, f16[512,256]{0,1:T(8,128)(2,1)S(1)}, u32[]{:S(2)}, u32[]{:S(2)}) collective-permute-start(f16[512,256]{0,1:T(8,128)(2,1)S(1)} %multiply_convert_fusion.1), channel_id=1, source_target_pairs={{0,2},{1,3},{2,0},{3,1},{4,6},{5,7},{6,4},{7,5},{8,10},{9,11},{10,... | collective-permute-start | bytes 786440 | tf_op jit(solution)/shard_map/ppermute | solution.py:35
  22.2 18.2 %collective-permute-start.29 = (f16[512,256]{0,1:T(8,128)(2,1)S(1)}, f16[512,256]{0,1:T(8,128)(2,1)S(1)}, u32[]{:S(2)}, u32[]{:S(2)}) collective-permute-start(f16[512,256]{0,1:T(8,128)(2,1)S(1)} %multiply_convert_fusion), channel_id=1, source_target_pairs={{0,2},{1,3},{2,0},{3,1},{4,6},{5,7},{6,4},{7,5},{8,10},{9,11},{10,... | collective-permute-start | bytes 786440 | tf_op jit(solution)/shard_map/ppermute | solution.py:35
  23.9 18.4 %collective-permute-start.3 = (f16[128,256]{0,1:T(8,128)(2,1)S(1)}, f16[128,256]{0,1:T(8,128)(2,1)S(1)}, u32[]{:S(2)}, u32[]{:S(2)}) collective-permute-start(f16[128,256]{0,1:T(8,128)(2,1)S(1)} %get-tuple-element.18), channel_id=1, source_target_pairs={{0,4},{1,5},{2,6},{3,7},{4,0},{5,1},{6,2},{7,3},{8,12},{9,13},{10,... | collective-permute-start | bytes 196616 | tf_op jit(solution)/shard_map/ppermute | solution.py:35
  29.4 13.3 %collective-permute-start.4 = (f16[128,256]{0,1:T(8,128)(2,1)S(1)}, f16[128,256]{0,1:T(8,128)(2,1)S(1)}, u32[]{:S(2)}, u32[]{:S(2)}) collective-permute-start(f16[128,256]{0,1:T(8,128)(2,1)S(1)} %get-tuple-element.20), channel_id=1, source_target_pairs={{0,8},{1,9},{2,10},{3,11},{4,12},{5,13},{6,14},{7,15},{8,0},{9,1},... | collective-permute-start | bytes 196616 | tf_op jit(solution)/shard_map/ppermute | solution.py:35
  35.0 10.5 %collective-permute-start.5 = (f16[128,256]{0,1:T(8,128)(2,1)S(1)}, f16[128,256]{0,1:T(8,128)(2,1)S(1)}, u32[]{:S(2)}, u32[]{:S(2)}) collective-permute-start(f16[128,256]{0,1:T(8,128)(2,1)S(1)} %get-tuple-element.19), channel_id=1, source_target_pairs={{0,12},{1,13},{2,14},{3,15},{4,8},{5,9},{6,10},{7,11},{8,4},{9,5},... | collective-permute-start | bytes 196616 | tf_op jit(solution)/shard_map/ppermute | solution.py:35
  40.4 15.1 %collective-permute-start.12 = (f16[128,256]{0,1:T(8,128)(2,1)S(1)}, f16[128,256]{0,1:T(8,128)(2,1)S(1)}, u32[]{:S(2)}, u32[]{:S(2)}) collective-permute-start(f16[128,256]{0,1:T(8,128)(2,1)S(1)} %get-tuple-element.21), channel_id=1, source_target_pairs={{0,4},{1,5},{2,6},{3,7},{4,0},{5,1},{6,2},{7,3},{8,12},{9,13},{10,... | collective-permute-start | bytes 196616 | tf_op jit(solution)/shard_map/ppermute | solution.py:35
  42.4 4.5 %collective-permute-start.21 = (f16[128,256]{0,1:T(8,128)(2,1)S(1)}, f16[128,256]{0,1:T(8,128)(2,1)S(1)}, u32[]{:S(2)}, u32[]{:S(2)}) collective-permute-start(f16[128,256]{0,1:T(8,128)(2,1)S(1)} %get-tuple-element.24), channel_id=1, source_target_pairs={{0,4},{1,5},{2,6},{3,7},{4,0},{5,1},{6,2},{7,3},{8,12},{9,13},{10,... | collective-permute-start | bytes 196616 | tf_op jit(solution)/shard_map/ppermute | solution.py:35
  42.6 7.3 %collective-permute-start.22 = (f16[128,256]{0,1:T(8,128)(2,1)S(1)}, f16[128,256]{0,1:T(8,128)(2,1)S(1)}, u32[]{:S(2)}, u32[]{:S(2)}) collective-permute-start(f16[128,256]{0,1:T(8,128)(2,1)S(1)} %get-tuple-element.26), channel_id=1, source_target_pairs={{0,8},{1,9},{2,10},{3,11},{4,12},{5,13},{6,14},{7,15},{8,0},{9,1},... | collective-permute-start | bytes 196616 | tf_op jit(solution)/shard_map/ppermute | solution.py:35
  45.5 8.9 %collective-permute-start.23 = (f16[128,256]{0,1:T(8,128)(2,1)S(1)}, f16[128,256]{0,1:T(8,128)(2,1)S(1)}, u32[]{:S(2)}, u32[]{:S(2)}) collective-permute-start(f16[128,256]{0,1:T(8,128)(2,1)S(1)} %get-tuple-element.25), channel_id=1, source_target_pairs={{0,12},{1,13},{2,14},{3,15},{4,8},{5,9},{6,10},{7,11},{8,4},{9,5},... | collective-permute-start | bytes 196616 | tf_op jit(solution)/shard_map/ppermute | solution.py:35
  46.9 9.6 %collective-permute-start.13 = (f16[128,256]{0,1:T(8,128)(2,1)S(1)}, f16[128,256]{0,1:T(8,128)(2,1)S(1)}, u32[]{:S(2)}, u32[]{:S(2)}) collective-permute-start(f16[128,256]{0,1:T(8,128)(2,1)S(1)} %get-tuple-element.23), channel_id=1, source_target_pairs={{0,8},{1,9},{2,10},{3,11},{4,12},{5,13},{6,14},{7,15},{8,0},{9,1},... | collective-permute-start | bytes 196616 | tf_op jit(solution)/shard_map/ppermute | solution.py:35
  49.9 9.1 %collective-permute-start.14 = (f16[128,256]{0,1:T(8,128)(2,1)S(1)}, f16[128,256]{0,1:T(8,128)(2,1)S(1)}, u32[]{:S(2)}, u32[]{:S(2)}) collective-permute-start(f16[128,256]{0,1:T(8,128)(2,1)S(1)} %get-tuple-element.22), channel_id=1, source_target_pairs={{0,12},{1,13},{2,14},{3,15},{4,8},{5,9},{6,10},{7,11},{8,4},{9,5},... | collective-permute-start | bytes 196616 | tf_op jit(solution)/shard_map/ppermute | solution.py:35
  54.4 5.3 %collective-permute-start.30 = (f16[128,256]{0,1:T(8,128)(2,1)S(1)}, f16[128,256]{0,1:T(8,128)(2,1)S(1)}, u32[]{:S(2)}, u32[]{:S(2)}) collective-permute-start(f16[128,256]{0,1:T(8,128)(2,1)S(1)} %get-tuple-element.27), channel_id=1, source_target_pairs={{0,4},{1,5},{2,6},{3,7},{4,0},{5,1},{6,2},{7,3},{8,12},{9,13},{10,... | collective-permute-start | bytes 196616 | tf_op jit(solution)/shard_map/ppermute | solution.py:35
  55.5 7.1 %collective-permute-start.31 = (f16[128,256]{0,1:T(8,128)(2,1)S(1)}, f16[128,256]{0,1:T(8,128)(2,1)S(1)}, u32[]{:S(2)}, u32[]{:S(2)}) collective-permute-start(f16[128,256]{0,1:T(8,128)(2,1)S(1)} %get-tuple-element.29), channel_id=1, source_target_pairs={{0,8},{1,9},{2,10},{3,11},{4,12},{5,13},{6,14},{7,15},{8,0},{9,1},... | collective-permute-start | bytes 196616 | tf_op jit(solution)/shard_map/ppermute | solution.py:35
  56.5 7.8 %collective-permute-start.32 = (f16[128,256]{0,1:T(8,128)(2,1)S(1)}, f16[128,256]{0,1:T(8,128)(2,1)S(1)}, u32[]{:S(2)}, u32[]{:S(2)}) collective-permute-start(f16[128,256]{0,1:T(8,128)(2,1)S(1)} %get-tuple-element.28), channel_id=1, source_target_pairs={{0,12},{1,13},{2,14},{3,15},{4,8},{5,9},{6,10},{7,11},{8,4},{9,5},... | collective-permute-start | bytes 196616 | tf_op jit(solution)/shard_map/ppermute | solution.py:35
  59.0 8.3 %collective-permute-start.6 = (bf16[128,256]{0,1:T(8,128)(2,1)S(1)}, bf16[128,256]{0,1:T(8,128)(2,1)S(1)}, u32[]{:S(2)}, u32[]{:S(2)}) collective-permute-start(bf16[128,256]{0,1:T(8,128)(2,1)S(1)} %add_convert_fusion.3), channel_id=1, source_target_pairs={{0,4},{1,5},{2,6},{3,7},{4,0},{5,1},{6,2},{7,3},{8,12},{9,13},{10,... | collective-permute-start | bytes 196616 | tf_op jit(solution)/shard_map/ppermute | solution.py:35
  59.7 8.0 %collective-permute-start.7 = (bf16[128,256]{0,1:T(8,128)(2,1)S(1)}, bf16[128,256]{0,1:T(8,128)(2,1)S(1)}, u32[]{:S(2)}, u32[]{:S(2)}) collective-permute-start(bf16[128,256]{0,1:T(8,128)(2,1)S(1)} %add_convert_fusion.3), channel_id=1, source_target_pairs={{0,8},{1,9},{2,10},{3,11},{4,12},{5,13},{6,14},{7,15},{8,0},{9,1},... | collective-permute-start | bytes 196616 | tf_op jit(solution)/shard_map/ppermute | solution.py:35
  62.6 8.9 %collective-permute-start.8 = (bf16[128,256]{0,1:T(8,128)(2,1)S(1)}, bf16[128,256]{0,1:T(8,128)(2,1)S(1)}, u32[]{:S(2)}, u32[]{:S(2)}) collective-permute-start(bf16[128,256]{0,1:T(8,128)(2,1)S(1)} %add_convert_fusion.3), channel_id=1, source_target_pairs={{0,12},{1,13},{2,14},{3,15},{4,8},{5,9},{6,10},{7,11},{8,4},{9,5},... | collective-permute-start | bytes 196616 | tf_op jit(solution)/shard_map/ppermute | solution.py:35
  64.3 7.3 %collective-permute-start.15 = (bf16[128,256]{0,1:T(8,128)(2,1)S(1)}, bf16[128,256]{0,1:T(8,128)(2,1)S(1)}, u32[]{:S(2)}, u32[]{:S(2)}) collective-permute-start(bf16[128,256]{0,1:T(8,128)(2,1)S(1)} %add_convert_fusion.2), channel_id=1, source_target_pairs={{0,4},{1,5},{2,6},{3,7},{4,0},{5,1},{6,2},{7,3},{8,12},{9,13},{10,... | collective-permute-start | bytes 196616 | tf_op jit(solution)/shard_map/ppermute | solution.py:35
  67.4 6.6 %collective-permute-start.16 = (bf16[128,256]{0,1:T(8,128)(2,1)S(1)}, bf16[128,256]{0,1:T(8,128)(2,1)S(1)}, u32[]{:S(2)}, u32[]{:S(2)}) collective-permute-start(bf16[128,256]{0,1:T(8,128)(2,1)S(1)} %add_convert_fusion.2), channel_id=1, source_target_pairs={{0,8},{1,9},{2,10},{3,11},{4,12},{5,13},{6,14},{7,15},{8,0},{9,1},... | collective-permute-start | bytes 196616 | tf_op jit(solution)/shard_map/ppermute | solution.py:35
  67.7 9.9 %collective-permute-start.17 = (bf16[128,256]{0,1:T(8,128)(2,1)S(1)}, bf16[128,256]{0,1:T(8,128)(2,1)S(1)}, u32[]{:S(2)}, u32[]{:S(2)}) collective-permute-start(bf16[128,256]{0,1:T(8,128)(2,1)S(1)} %add_convert_fusion.2), channel_id=1, source_target_pairs={{0,12},{1,13},{2,14},{3,15},{4,8},{5,9},{6,10},{7,11},{8,4},{9,5},... | collective-permute-start | bytes 196616 | tf_op jit(solution)/shard_map/ppermute | solution.py:35
  71.5 6.2 %collective-permute-start.24 = (bf16[128,256]{0,1:T(8,128)(2,1)S(1)}, bf16[128,256]{0,1:T(8,128)(2,1)S(1)}, u32[]{:S(2)}, u32[]{:S(2)}) collective-permute-start(bf16[128,256]{0,1:T(8,128)(2,1)S(1)} %add_convert_fusion.1), channel_id=1, source_target_pairs={{0,4},{1,5},{2,6},{3,7},{4,0},{5,1},{6,2},{7,3},{8,12},{9,13},{10,... | collective-permute-start | bytes 196616 | tf_op jit(solution)/shard_map/ppermute | solution.py:35
  71.6 9.6 %collective-permute-start.25 = (bf16[128,256]{0,1:T(8,128)(2,1)S(1)}, bf16[128,256]{0,1:T(8,128)(2,1)S(1)}, u32[]{:S(2)}, u32[]{:S(2)}) collective-permute-start(bf16[128,256]{0,1:T(8,128)(2,1)S(1)} %add_convert_fusion.1), channel_id=1, source_target_pairs={{0,8},{1,9},{2,10},{3,11},{4,12},{5,13},{6,14},{7,15},{8,0},{9,1},... | collective-permute-start | bytes 196616 | tf_op jit(solution)/shard_map/ppermute | solution.py:35
  74.0 8.5 %collective-permute-start.26 = (bf16[128,256]{0,1:T(8,128)(2,1)S(1)}, bf16[128,256]{0,1:T(8,128)(2,1)S(1)}, u32[]{:S(2)}, u32[]{:S(2)}) collective-permute-start(bf16[128,256]{0,1:T(8,128)(2,1)S(1)} %add_convert_fusion.1), channel_id=1, source_target_pairs={{0,12},{1,13},{2,14},{3,15},{4,8},{5,9},{6,10},{7,11},{8,4},{9,5},... | collective-permute-start | bytes 196616 | tf_op jit(solution)/shard_map/ppermute | solution.py:35
  77.6 8.6 %collective-permute-start.33 = (bf16[128,256]{0,1:T(8,128)(2,1)S(1)}, bf16[128,256]{0,1:T(8,128)(2,1)S(1)}, u32[]{:S(2)}, u32[]{:S(2)}) collective-permute-start(bf16[128,256]{0,1:T(8,128)(2,1)S(1)} %add_convert_fusion), channel_id=1, source_target_pairs={{0,4},{1,5},{2,6},{3,7},{4,0},{5,1},{6,2},{7,3},{8,12},{9,13},{10,... | collective-permute-start | bytes 196616 | tf_op jit(solution)/shard_map/ppermute | solution.py:35
  77.8 8.6 %collective-permute-start.34 = (bf16[128,256]{0,1:T(8,128)(2,1)S(1)}, bf16[128,256]{0,1:T(8,128)(2,1)S(1)}, u32[]{:S(2)}, u32[]{:S(2)}) collective-permute-start(bf16[128,256]{0,1:T(8,128)(2,1)S(1)} %add_convert_fusion), channel_id=1, source_target_pairs={{0,8},{1,9},{2,10},{3,11},{4,12},{5,13},{6,14},{7,15},{8,0},{9,1},... | collective-permute-start | bytes 196616 | tf_op jit(solution)/shard_map/ppermute | solution.py:35
  81.2 7.7 %collective-permute-start.35 = (bf16[128,256]{0,1:T(8,128)(2,1)S(1)}, bf16[128,256]{0,1:T(8,128)(2,1)}, u32[]{:S(2)}, u32[]{:S(2)}) collective-permute-start(bf16[128,256]{0,1:T(8,128)(2,1)S(1)} %add_convert_fusion), channel_id=1, source_target_pairs={{0,12},{1,13},{2,14},{3,15},{4,8},{5,9},{6,10},{7,11},{8,4},{9,5},... | collective-permute-start | bytes 196616 | tf_op jit(solution)/shard_map/ppermute | solution.py:35
  82.6 10.6 %collective-permute-start.9 = (bf16[512,256]{1,0:T(8,128)(2,1)S(1)}, bf16[512,256]{1,0:T(8,128)(2,1)S(1)}, u32[]{:S(2)}, u32[]{:S(2)}) collective-permute-start(bf16[512,256]{1,0:T(8,128)(2,1)S(1)} %constant_dynamic-update-slice_fusion.20), channel_id=1, source_target_pairs={{0,2},{1,3},{2,0},{3,1},{4,6},{5,7},{6,4},{7,5},{8,10},{9,11},{10,... | collective-permute-start | bytes 786440 | tf_op jit(solution)/shard_map/ppermute | solution.py:35
  86.2 12.8 %collective-permute-start.18 = (bf16[512,256]{1,0:T(8,128)(2,1)S(1)}, bf16[512,256]{1,0:T(8,128)(2,1)}, u32[]{:S(2)}, u32[]{:S(2)}) collective-permute-start(bf16[512,256]{1,0:T(8,128)(2,1)S(1)} %constant_dynamic-update-slice_fusion.14), channel_id=1, source_target_pairs={{0,2},{1,3},{2,0},{3,1},{4,6},{5,7},{6,4},{7,5},{8,10},{9,11},{10,... | collective-permute-start | bytes 786440 | tf_op jit(solution)/shard_map/ppermute | solution.py:35
  86.4 15.3 %collective-permute-start.27 = (bf16[512,256]{1,0:T(8,128)(2,1)S(1)}, bf16[512,256]{1,0:T(8,128)(2,1)}, u32[]{:S(2)}, u32[]{:S(2)}) collective-permute-start(bf16[512,256]{1,0:T(8,128)(2,1)S(1)} %constant_dynamic-update-slice_fusion.8), channel_id=1, source_target_pairs={{0,2},{1,3},{2,0},{3,1},{4,6},{5,7},{6,4},{7,5},{8,10},{9,11},{10,... | collective-permute-start | bytes 786440 | tf_op jit(solution)/shard_map/ppermute | solution.py:35
  89.9 14.6 %collective-permute-start.36 = (bf16[512,256]{1,0:T(8,128)(2,1)S(1)}, bf16[512,256]{1,0:T(8,128)(2,1)S(1)}, u32[]{:S(2)}, u32[]{:S(2)}) collective-permute-start(bf16[512,256]{1,0:T(8,128)(2,1)S(1)} %constant_dynamic-update-slice_fusion.2), channel_id=1, source_target_pairs={{0,2},{1,3},{2,0},{3,1},{4,6},{5,7},{6,4},{7,5},{8,10},{9,11},{10,... | collective-permute-start | bytes 786440 | tf_op jit(solution)/shard_map/ppermute | solution.py:35
  104.5 14.4 %copy-start.2 = (s32[8,12]{1,0:T(8,128)S(1)}, s32[8,12]{1,0:T(8,128)}, u32[]{:S(2)}) copy-start(s32[8,12]{1,0:T(8,128)} %param.11) | copy-start | bytes 1156
  104.5 14.5 %copy-start.4 = (s32[8]{0:T(128)S(1)}, s32[8]{0:T(128)}, u32[]{:S(2)}) copy-start(s32[8]{0:T(128)} %param.12) | copy-start | bytes 100
  104.5 14.6 %copy-start.5 = (s32[512]{0:T(512)S(1)}, s32[512]{0:T(512)}, u32[]{:S(2)}) copy-start(s32[512]{0:T(512)} %param.10) | copy-start | bytes 6148
  114.6 18.0 %all-to-all-start = ((f32[16,1,32,256]{3,2,1,0:T(8,128)}), f32[16,1,32,256]{3,2,1,0:T(8,128)S(1)}, u32[]{:S(2)}, u32[]{:S(2)}) async-start(f32[16,1,32,256]{3,2,1,0:T(8,128)} %bitcast.11), calls=%async_computation | async-start | bytes 1048576 | tf_op jit(solution)/shard_map/all_to_all | solution.py:90

commit v2 on v1

v2 whole, which is shorter than its diff:
```python
import jax
import jax.numpy as jnp
from jax import lax
from jax.sharding import PartitionSpec as P

CORES = 2
UNIT = 4.0


def listed_mask(query_cluster, cand_blocks, cand_count, nblocks):
    nclusters = cand_blocks.shape[0]
    valid = jnp.arange(cand_blocks.shape[1])[None, :] < cand_count[:, None]
    hits = (cand_blocks[:, :, None] == jnp.arange(nblocks)[None, None, :]) & valid[:, :, None]
    listed = jnp.any(hits, axis=1).astype(jnp.float32)
    onehot = (query_cluster[:, None] == jnp.arange(nclusters)[None, :]).astype(jnp.float32)
    return jnp.dot(listed.T, onehot.T, preferred_element_type=jnp.float32)


def shards(queries, precond, train, query_cluster, cand_blocks, cand_count, slot_block):
    n = lax.axis_size("rows")
    chips = n // CORES
    bits = chips.bit_length() - 1
    ybits = [1 + b for b in range(bits // 2)]
    zbits = [1 + b for b in range(bits // 2, bits)]
    orders = (ybits + zbits, zbits[:1] + ybits + zbits[1:])
    me = lax.axis_index("rows")
    core = me & 1

    examples, nblocks, width = train.shape
    nq = queries.shape[0]
    half = nq // CORES

    def swap(value, bit):
        return lax.ppermute(value, "rows", [(r, r ^ (1 << bit)) for r in range(n)])

    def side(bit):
        return (me >> bit) & 1

    def pack(value):
        return (value * UNIT).astype(jnp.float16)

    def unpack(value):
        return value.astype(jnp.float32) * (1.0 / UNIT)

    def split(value, bit):
        rows = value.shape[0] // 2
        keep = lax.dynamic_slice_in_dim(value, side(bit) * rows, rows)
        give = lax.dynamic_slice_in_dim(value, (1 - side(bit)) * rows, rows)
        return keep, pack(give)

    def join(own, got, bit):
        rows = own.shape[0]
        full = jnp.zeros((2 * rows,) + own.shape[1:], own.dtype)
        full = lax.dynamic_update_slice_in_dim(full, own, side(bit) * rows, 0)
        return lax.dynamic_update_slice_in_dim(full, got, (1 - side(bit)) * rows, 0)

    def product(rows):
        return jnp.dot(rows, precond, precision=lax.Precision.HIGH, preferred_element_type=jnp.float32)

    part = half // 2
    mine = lax.dynamic_slice_in_dim(queries, core * half, half)
    other = lax.dynamic_slice_in_dim(queries, (1 - core) * half, half)
    sent = [swap(pack(product(other[i * part:(i + 1) * part])), 0) for i in range(2)]
    other_train = swap(train, 0)
    values = [product(mine[i * part:(i + 1) * part]) + unpack(sent[i]) for i in range(2)]

    for step in range(bits - 1):
        pieces = [split(values[i], orders[i][step]) for i in range(2)]
        got = [swap(pieces[i][1], orders[i][step]) for i in range(2)]
        values = [pieces[i][0] + unpack(got[i]) for i in range(2)]
    last = orders[0][-1]
    pieces = [split(value, last) for value in values]
    got = swap(jnp.concatenate([give for _, give in pieces]), last)
    kept = jnp.concatenate([keep for keep, _ in pieces])
    own = (kept + unpack(got)).astype(jnp.bfloat16)
    got = swap(own, last)
    rows = own.shape[0] // 2
    values = [join(own[i * rows:(i + 1) * rows], got[i * rows:(i + 1) * rows], last) for i in range(2)]
    for step in reversed(range(bits - 1)):
        got = [swap(values[i], orders[i][step]) for i in range(2)]
        values = [join(values[i], got[i], orders[i][step]) for i in range(2)]
    prequery = jnp.concatenate(values, axis=0)

    both = jnp.concatenate([train, other_train], axis=0).reshape(CORES * examples * nblocks, width)
    raw = lax.dot_general(both, prequery, (((1,), (1,)), ((), ())), preferred_element_type=jnp.float32)
    raw = raw.astype(jnp.bfloat16).reshape(CORES * examples, nblocks, half)
    ordered = jnp.take(jnp.swapaxes(raw, 0, 1), slot_block, axis=0, mode="clip")
    owned_count = nblocks // n
    ordered = ordered.reshape(n, owned_count, CORES * examples, half)
    got = lax.all_to_all(ordered, "rows", split_axis=0, concat_axis=0, tiled=True)
    got = got.reshape(chips, CORES, owned_count, CORES, examples, half)
    got = jnp.stack([got[:, 0], got[:, 1, :, ::-1]], axis=4)
    got = got.transpose(0, 2, 3, 1, 4, 5).reshape(n * examples, owned_count, nq)

    allowed = listed_mask(query_cluster, cand_blocks, cand_count, nblocks)
    slots = lax.dynamic_slice_in_dim(slot_block, me * owned_count, owned_count)
    return got.astype(jnp.float32) * jnp.take(allowed, slots, axis=0, mode="clip")[None]


def solution(mesh):
    placed = (
        P("groups", "rows"),
        P("rows", None),
        P("rows", "groups", None),
        P("groups"),
        P("groups", None),
        P("groups"),
        P("groups"),
    )
    return jax.shard_map(
        shards,
        mesh=mesh,
        in_specs=placed,
        out_specs=P(None, ("groups", "rows"), None),
        check_vma=False,
    )
```

time: 136 us -> 107 us (0.79)
  starting transfers between devices: 61.5 us -> 17.2 us
  waiting for transfers between devices: 37.1 us -> 65.7 us
  matrix products: 23 us -> 15.7 us
  local copies, waits for them, and re-layouts: 10.4 us -> 6.61 us
    ppermute x37 -> x13, starting transfers between devices: 57.9 us -> 13.6 us  [swap(): return lax.ppermute(value, 'rows', [(r, r ^ 1 << bit) for r in range(n)])]
    ppermute x37 -> x13, waiting for transfers between devices: 24.4 us -> 57.5 us  [swap(): return lax.ppermute(value, 'rows', [(r, r ^ 1 << bit) for r in range(n)])]
    dot_general x9 -> x5, matrix products: 22.8 us -> 15.4 us  [the longest x4 14.1 us: product(): jnp.dot(rows, precond, precision=lax.Precision.HIGH, preferred_element_ty...]
    all_to_all x1, waiting for transfers between devices: 12.6 us -> 8.23 us  [shards(): lax.all_to_all(ordered, 'rows', split_axis=0, concat_axis=0, tiled=True)]
    ppermute x12 -> x0, local copies, waits for them, and re-layouts: 2.1 us -> none  [swap(): return lax.ppermute(value, 'rows', [(r, r ^ step) for r in range(n)])]
    dynamic_update_slice x24 -> x11, local copies, waits for them, and re-layouts: 2.27 us -> 0.31 us  [the longest x6 0.17 us: join(): full = lax.dynamic_update_slice_in_dim(full, own, side(bit) * rows, 0)]
  transfers between devices with their start and end apart: 38 -> 14, of which waited for: 14 -> 10; matrix products, arithmetic and copies ran while one was open for 14% -> 13% of each run, Pallas kernels for 0% -> 0%
where the time goes in v2:
time: 107 us
  waiting for transfers between devices  65.7 us (61%)
  starting transfers between devices  17.2 us (16%)
  matrix products  15.7 us (15%)
  local copies, waits for them, and re-layouts  6.61 us (6%)
  other arithmetic  1.5 us (1%)
    ppermute x13, waiting for transfers between devices, swap(): return lax.ppermute(value, 'rows', [(r, r ^ 1 << bit) for r in range(n)])  57.5 us
    dot_general x4, matrix products, product(): jnp.dot(rows, precond, precision=lax.Precision.HIGH, preferred_element_ty...  14.1 us
    ppermute x13, starting transfers between devices, swap(): return lax.ppermute(value, 'rows', [(r, r ^ 1 << bit) for r in range(n)])  13.6 us
    all_to_all x1, waiting for transfers between devices, shards(): lax.all_to_all(ordered, 'rows', split_axis=0, concat_axis=0, tiled=True)  8.23 us
    all_to_all x1, starting transfers between devices, shards(): lax.all_to_all(ordered, 'rows', split_axis=0, concat_axis=0, tiled=True)  3.53 us
  transfers between devices with their start and end apart: 14, of which 10 were waited for; matrix products, arithmetic and copies ran while one was open for 13% of the time, Pallas kernels for 0%

profile of v2, /device:TPU:0, one launch (start us, length us, event | category | flops | bytes accessed | tf_op | source)
XLA Modules:
  0.0 107.1 jit_solution(12573164114649465462)
XLA Ops:
  0.0 1.0 copy-done
  1.0 3.6 %fusion = f16[128,4096]{1,0:T(8,128)(2,1)S(1)} fusion(f32[256,4096]{1,0:T(8,128)} %param.8, f32[512,256]{1,0:T(8,128)S(1)} %copy-done, s32[]{:T(128)S(6)} %select_n.54), kind=kOutput, calls=%fused_computation.3 | convolution fusion | flops 806354944 | bytes 5373956 | tf_op jit(solution)/shard_map/dot_general | solution.py:58
  4.6 0.5 collective-permute-start.1
  5.1 3.6 %fusion.1 = f16[128,4096]{1,0:T(8,128)(2,1)S(1)} fusion(f32[256,4096]{1,0:T(8,128)} %param.8, f32[512,256]{1,0:T(8,128)S(1)} %copy-done, s32[]{:T(128)S(6)} %add.97), kind=kOutput, calls=%fused_computation.4 | convolution fusion | flops 806354944 | bytes 5373956 | tf_op jit(solution)/shard_map/dot_general | solution.py:58
  8.7 0.1 collective-permute-start.4
  8.8 4.1 %multiply_add_fusion.1 = f32[128,4096]{1,0:T(8,128)S(1)} fusion(f16[128,4096]{1,0:T(8,128)(2,1)} %collective-permute-done.1, f32[256,4096]{1,0:T(8,128)} %param.8, f32[512,256]{1,0:T(8,128)S(1)} %copy-done, s32[]{:T(128)S(6)} %select_n.26), kind=kOutput, calls=%fused_computation.11 | convolution fusion | flops 806879232 | bytes 7471108 | tf_op jit(solution)/shard_map/dot_general | solution.py:58
  13.0 0.1 multiply_convert_fusion.1
  13.1 3.0 %collective-permute-start.2 = (f16[64,4096]{1,0:T(8,128)(2,1)S(1)}, f16[64,4096]{1,0:T(8,128)(2,1)S(1)}, u32[]{:S(2)}, u32[]{:S(2)}) collective-permute-start(f16[64,4096]{1,0:T(8,128)(2,1)S(1)} %multiply_convert_fusion.1), channel_id=1, source_target_pairs={{0,2},{1,3},{2,0},{3,1},{4,6},{5,7},{6,4},{7,5},{8,10},{9,11},{10,... | collective-permute-start | bytes 1572872 | tf_op jit(solution)/shard_map/ppermute | solution.py:34
  16.1 2.9 %multiply_add_fusion = f32[128,4096]{1,0:T(8,128)S(1)} fusion(f16[128,4096]{1,0:T(8,128)(2,1)} %collective-permute-done.4, f32[256,4096]{1,0:T(8,128)S(1)} %copy-done.1, f32[512,256]{1,0:T(8,128)S(1)} %copy-done, s32[]{:T(128)S(6)} %add.96), kind=kOutput, calls=%fused_computation.10 | convolution fusion | flops 806879232 | bytes 7471108 | tf_op jit(solution)/shard_map/dot_general | solution.py:58
  19.0 0.1 multiply_convert_fusion
  19.1 1.6 %collective-permute-start.5 = (f16[64,4096]{1,0:T(8,128)(2,1)S(1)}, f16[64,4096]{1,0:T(8,128)(2,1)S(1)}, u32[]{:S(2)}, u32[]{:S(2)}) collective-permute-start(f16[64,4096]{1,0:T(8,128)(2,1)S(1)} %multiply_convert_fusion), channel_id=1, source_target_pairs={{0,4},{1,5},{2,6},{3,7},{4,0},{5,1},{6,2},{7,3},{8,12},{9,13},{10,... | collective-permute-start | bytes 1572872 | tf_op jit(solution)/shard_map/ppermute | solution.py:34
  20.8 7.5 %collective-permute-done.2 = f16[64,4096]{1,0:T(8,128)(2,1)S(1)} collective-permute-done((f16[64,4096]{1,0:T(8,128)(2,1)S(1)}, f16[64,4096]{1,0:T(8,128)(2,1)S(1)}, u32[]{:S(2)}, u32[]{:S(2)}) %collective-permute-start.2) | collective-permute-done | bytes 524320 | tf_op jit(solution)/shard_map/ppermute | solution.py:34
  28.2 0.1 multiply_add_fusion.3
  28.4 1.9 %collective-permute-start.3 = (f16[32,4096]{1,0:T(8,128)(2,1)S(1)}, f16[32,4096]{1,0:T(8,128)(2,1)S(1)}, u32[]{:S(2)}, u32[]{:S(2)}) collective-permute-start(f16[32,4096]{1,0:T(8,128)(2,1)S(1)} %multiply_convert_fusion.3), channel_id=1, source_target_pairs={{0,4},{1,5},{2,6},{3,7},{4,0},{5,1},{6,2},{7,3},{8,12},{9,13},{10,... | collective-permute-start | bytes 786440 | tf_op jit(solution)/shard_map/ppermute | solution.py:34
  30.3 3.7 %collective-permute-done.5 = f16[64,4096]{1,0:T(8,128)(2,1)S(1)} collective-permute-done((f16[64,4096]{1,0:T(8,128)(2,1)S(1)}, f16[64,4096]{1,0:T(8,128)(2,1)S(1)}, u32[]{:S(2)}, u32[]{:S(2)}) %collective-permute-start.5) | collective-permute-done | bytes 524320 | tf_op jit(solution)/shard_map/ppermute | solution.py:34
  34.0 0.2 multiply_add_fusion.2
  34.2 0.1 collective-permute-start.6
  34.3 4.1 %collective-permute-done.3 = f16[32,4096]{1,0:T(8,128)(2,1)S(1)} collective-permute-done((f16[32,4096]{1,0:T(8,128)(2,1)S(1)}, f16[32,4096]{1,0:T(8,128)(2,1)S(1)}, u32[]{:S(2)}, u32[]{:S(2)}) %collective-permute-start.3) | collective-permute-done | bytes 262176 | tf_op jit(solution)/shard_map/ppermute | solution.py:34
  38.5 2.1 %collective-permute-done.6 = f16[32,4096]{1,0:T(8,128)(2,1)S(1)} collective-permute-done((f16[32,4096]{1,0:T(8,128)(2,1)S(1)}, f16[32,4096]{1,0:T(8,128)(2,1)S(1)}, u32[]{:S(2)}, u32[]{:S(2)}) %collective-permute-start.6) | collective-permute-done | bytes 262176 | tf_op jit(solution)/shard_map/ppermute | solution.py:34
  40.8 0.1 pad_maximum_fusion.1
  40.9 2.7 %collective-permute-start.7 = (f16[32,4096]{1,0:T(8,128)(2,1)S(1)}, f16[32,4096]{1,0:T(8,128)(2,1)S(1)}, u32[]{:S(2)}, u32[]{:S(2)}) collective-permute-start(f16[32,4096]{1,0:T(8,128)(2,1)S(1)} %pad_maximum_fusion.1), channel_id=1, source_target_pairs={{0,8},{1,9},{2,10},{3,11},{4,12},{5,13},{6,14},{7,15},{8,0},{9,1},... | collective-permute-start | bytes 786440 | tf_op jit(solution)/shard_map/ppermute | solution.py:34
  43.5 8.9 %collective-permute-done.7 = f16[32,4096]{1,0:T(8,128)(2,1)S(1)} collective-permute-done((f16[32,4096]{1,0:T(8,128)(2,1)S(1)}, f16[32,4096]{1,0:T(8,128)(2,1)S(1)}, u32[]{:S(2)}, u32[]{:S(2)}) %collective-permute-start.7) | collective-permute-done | bytes 262176 | tf_op jit(solution)/shard_map/ppermute | solution.py:34
  52.5 0.1 fusion.9
  52.5 0.1 collective-permute-start.8
  52.7 0.4 pad_maximum_fusion
  53.1 12.9 %collective-permute-done.8 = bf16[32,4096]{1,0:T(8,128)(2,1)S(1)} collective-permute-done((bf16[32,4096]{1,0:T(8,128)(2,1)S(1)}, bf16[32,4096]{1,0:T(8,128)(2,1)S(1)}, u32[]{:S(2)}, u32[]{:S(2)}) %collective-permute-start.8) | collective-permute-done | bytes 262176 | tf_op jit(solution)/shard_map/ppermute | solution.py:34
  66.1 0.1 collective-permute-start.9
  66.2 1.3 %collective-permute-start.11 = (bf16[32,4096]{1,0:T(8,128)(2,1)S(1)}, bf16[32,4096]{1,0:T(8,128)(2,1)S(1)}, u32[]{:S(2)}, u32[]{:S(2)}) collective-permute-start(bf16[32,4096]{1,0:T(8,128)(2,1)S(1)} %get-tuple-element.23), channel_id=1, source_target_pairs={{0,2},{1,3},{2,0},{3,1},{4,6},{5,7},{6,4},{7,5},{8,10},{9,11},{10,... | collective-permute-start | bytes 786440 | tf_op jit(solution)/shard_map/ppermute | solution.py:34
  67.5 6.0 %collective-permute-done.9 = bf16[32,4096]{1,0:T(8,128)(2,1)S(1)} collective-permute-done((bf16[32,4096]{1,0:T(8,128)(2,1)S(1)}, bf16[32,4096]{1,0:T(8,128)(2,1)S(1)}, u32[]{:S(2)}, u32[]{:S(2)}) %collective-permute-start.9) | collective-permute-done | bytes 262176 | tf_op jit(solution)/shard_map/ppermute | solution.py:34
  73.6 2.0 %collective-permute-start.10 = (bf16[64,4096]{1,0:T(8,128)(2,1)S(1)}, bf16[64,4096]{1,0:T(8,128)(2,1)S(1)}, u32[]{:S(2)}, u32[]{:S(2)}) collective-permute-start(bf16[64,4096]{1,0:T(8,128)(2,1)S(1)} %constant_dynamic-update-slice_fusion.6), channel_id=1, source_target_pairs={{0,2},{1,3},{2,0},{3,1},{4,6},{5,7},{6,4},{7,5},{8,10},{9,11},{10,... | collective-permute-start | bytes 1572872 | tf_op jit(solution)/shard_map/ppermute | solution.py:34
  75.6 0.1 broadcast.67.clone.1
  75.8 0.4 collective-permute-start.12
  76.1 0.1 broadcast.67.clone
  76.3 10.5 %collective-permute-done.10 = bf16[64,4096]{1,0:T(8,128)(2,1)S(1)} collective-permute-done((bf16[64,4096]{1,0:T(8,128)(2,1)S(1)}, bf16[64,4096]{1,0:T(8,128)(2,1)S(1)}, u32[]{:S(2)}, u32[]{:S(2)}) %collective-permute-start.10) | collective-permute-done | bytes 524320 | tf_op jit(solution)/shard_map/ppermute | solution.py:34
  86.8 1.7 %collective-permute-done.12 = bf16[64,4096]{1,0:T(8,128)(2,1)S(1)} collective-permute-done((bf16[64,4096]{1,0:T(8,128)(2,1)S(1)}, bf16[64,4096]{1,0:T(8,128)(2,1)S(1)}, u32[]{:S(2)}, u32[]{:S(2)}) %collective-permute-start.12) | collective-permute-done | bytes 524320 | tf_op jit(solution)/shard_map/ppermute | solution.py:34
  88.6 1.3 %fusion.6 = bf16[512,256]{1,0:T(8,128)(2,1)S(1)} fusion(bf16[512,4096]{1,0:T(8,128)(2,1)S(1)} %bitcast.22, bf16[128,4096]{1,0:T(8,128)(2,1)S(1)} %constant_dynamic-update-slice_fusion, bf16[128,4096]{1,0:T(8,128)(2,1)S(1)} %constant_dynamic-update-slice_fusion.4), kind=kOutput, calls=%fused_computation.12 | convolution fusion | flops 1078067200 | bytes 6553600 | tf_op jit(solution)/shard_map/dot_general | solution.py:85
  89.9 0.1 copy.32
  89.9 1.3 %gather_fusion = bf16[16,32,256]{2,1,0:T(8,128)(2,1)} fusion(bf16[16,32,256]{2,1,0:T(8,128)(2,1)S(1)} %bitcast.23, s32[1024]{0:T(1024)S(1)} %pad_clamp_fusion), kind=kCustom, calls=%fused_computation | custom fusion | bytes 524352 | tf_op jit(solution)/shard_map/jit(_take)/gather | solution.py:87
  91.2 3.5 %all-to-all-start = ((bf16[16,1,32,256]{3,2,1,0:T(8,128)(2,1)}), bf16[16,1,32,256]{3,2,1,0:T(8,128)(2,1)S(1)}, u32[]{:S(2)}, u32[]{:S(2)}) async-start(bf16[16,1,32,256]{3,2,1,0:T(8,128)(2,1)} %bitcast.4), calls=%async_computation | async-start | bytes 524288 | tf_op jit(solution)/shard_map/all_to_all | solution.py:90
  94.8 0.7 dynamic_slice.59
  95.4 0.1 copy.29
  95.5 0.1 fusion.23
  95.6 0.3 fusion.10
  95.9 0.6 constant_dynamic-slice_fusion
  96.5 8.2 %all-to-all-done = bf16[16,1,32,256]{3,2,1,0:T(8,128)(2,1)S(1)} async-done(((bf16[16,1,32,256]{3,2,1,0:T(8,128)(2,1)}), bf16[16,1,32,256]{3,2,1,0:T(8,128)(2,1)S(1)}, u32[]{:S(2)}, u32[]{:S(2)}) %all-to-all-start) | async-done | bytes 262176 | tf_op jit(solution)/shard_map/all_to_all | solution.py:90
  104.8 0.4 copy.28
  105.3 0.4 reshape.103
  105.8 1.3 %copy.30 = f32[256,1,512]{2,1,0:T(1,128)} copy(f32[256,1,512]{2,0,1:T(8,128)S(1)} %broadcast_multiply_fusion) | data formatting | bytes 1048576 | tf_op jit(solution)/shard_map/mul | solution.py:97
  (45 shorter events, 0.9 us)
Async XLA Ops:
  0.0 1.0 copy-start
  4.6 4.2 %collective-permute-start.1 = (f16[128,4096]{1,0:T(8,128)(2,1)S(1)}, f16[128,4096]{1,0:T(8,128)(2,1)}, u32[]{:S(2)}, u32[]{:S(2)}) collective-permute-start(f16[128,4096]{1,0:T(8,128)(2,1)S(1)} %fusion), channel_id=1, source_target_pairs={{0,1},{1,0},{2,3},{3,2},{4,5},{5,4},{6,7},{7,6},{8,9},{9,8},{10,11... | collective-permute-start | bytes 3145736 | tf_op jit(solution)/shard_map/ppermute | solution.py:34
  8.7 7.4 %collective-permute-start.4 = (f16[128,4096]{1,0:T(8,128)(2,1)S(1)}, f16[128,4096]{1,0:T(8,128)(2,1)}, u32[]{:S(2)}, u32[]{:S(2)}) collective-permute-start(f16[128,4096]{1,0:T(8,128)(2,1)S(1)} %fusion.1), channel_id=1, source_target_pairs={{0,1},{1,0},{2,3},{3,2},{4,5},{5,4},{6,7},{7,6},{8,9},{9,8},{10,11... | collective-permute-start | bytes 3145736 | tf_op jit(solution)/shard_map/ppermute | solution.py:34
  8.8 7.3 %copy-start.1 = (f32[256,4096]{1,0:T(8,128)S(1)}, f32[256,4096]{1,0:T(8,128)}, u32[]{:S(2)}) copy-start(f32[256,4096]{1,0:T(8,128)} %param.8) | copy-start | bytes 12582916
  13.1 15.2 %collective-permute-start.2 = (f16[64,4096]{1,0:T(8,128)(2,1)S(1)}, f16[64,4096]{1,0:T(8,128)(2,1)S(1)}, u32[]{:S(2)}, u32[]{:S(2)}) collective-permute-start(f16[64,4096]{1,0:T(8,128)(2,1)S(1)} %multiply_convert_fusion.1), channel_id=1, source_target_pairs={{0,2},{1,3},{2,0},{3,1},{4,6},{5,7},{6,4},{7,5},{8,10},{9,11},{10,... | collective-permute-start | bytes 1572872 | tf_op jit(solution)/shard_map/ppermute | solution.py:34
  19.1 14.9 %collective-permute-start.5 = (f16[64,4096]{1,0:T(8,128)(2,1)S(1)}, f16[64,4096]{1,0:T(8,128)(2,1)S(1)}, u32[]{:S(2)}, u32[]{:S(2)}) collective-permute-start(f16[64,4096]{1,0:T(8,128)(2,1)S(1)} %multiply_convert_fusion), channel_id=1, source_target_pairs={{0,4},{1,5},{2,6},{3,7},{4,0},{5,1},{6,2},{7,3},{8,12},{9,13},{10,... | collective-permute-start | bytes 1572872 | tf_op jit(solution)/shard_map/ppermute | solution.py:34
  28.4 10.0 %collective-permute-start.3 = (f16[32,4096]{1,0:T(8,128)(2,1)S(1)}, f16[32,4096]{1,0:T(8,128)(2,1)S(1)}, u32[]{:S(2)}, u32[]{:S(2)}) collective-permute-start(f16[32,4096]{1,0:T(8,128)(2,1)S(1)} %multiply_convert_fusion.3), channel_id=1, source_target_pairs={{0,4},{1,5},{2,6},{3,7},{4,0},{5,1},{6,2},{7,3},{8,12},{9,13},{10,... | collective-permute-start | bytes 786440 | tf_op jit(solution)/shard_map/ppermute | solution.py:34
  34.2 6.4 %collective-permute-start.6 = (f16[32,4096]{1,0:T(8,128)(2,1)S(1)}, f16[32,4096]{1,0:T(8,128)(2,1)S(1)}, u32[]{:S(2)}, u32[]{:S(2)}) collective-permute-start(f16[32,4096]{1,0:T(8,128)(2,1)S(1)} %multiply_convert_fusion.2), channel_id=1, source_target_pairs={{0,2},{1,3},{2,0},{3,1},{4,6},{5,7},{6,4},{7,5},{8,10},{9,11},{10,... | collective-permute-start | bytes 786440 | tf_op jit(solution)/shard_map/ppermute | solution.py:34
  38.5 5.1 %copy-start.2 = (bf16[16,16,4096]{2,1,0:T(8,128)(2,1)S(1)}, bf16[16,16,4096]{2,1,0:T(8,128)(2,1)}, u32[]{:S(2)}) copy-start(bf16[16,16,4096]{2,1,0:T(8,128)(2,1)} %param.9) | copy-start | bytes 6291460
  38.5 5.0 %copy-start.5 = (s32[16]{0:T(128)S(1)}, s32[16]{0:T(128)}, u32[]{:S(2)}) copy-start(s32[16]{0:T(128)} %param.13) | copy-start | bytes 196
  40.9 11.6 %collective-permute-start.7 = (f16[32,4096]{1,0:T(8,128)(2,1)S(1)}, f16[32,4096]{1,0:T(8,128)(2,1)S(1)}, u32[]{:S(2)}, u32[]{:S(2)}) collective-permute-start(f16[32,4096]{1,0:T(8,128)(2,1)S(1)} %pad_maximum_fusion.1), channel_id=1, source_target_pairs={{0,8},{1,9},{2,10},{3,11},{4,12},{5,13},{6,14},{7,15},{8,0},{9,1},... | collective-permute-start | bytes 786440 | tf_op jit(solution)/shard_map/ppermute | solution.py:34
  43.5 9.2 %collective-permute-start = (bf16[16,16,4096]{2,1,0:T(8,128)(2,1)S(1)}, bf16[16,16,4096]{2,1,0:T(8,128)(2,1)S(1)}, u32[]{:S(2)}, u32[]{:S(2)}) collective-permute-start(bf16[16,16,4096]{2,1,0:T(8,128)(2,1)S(1)} %copy-done.2), channel_id=1, source_target_pairs={{0,1},{1,0},{2,3},{3,2},{4,5},{5,4},{6,7},{7,6},{8,9},{9,8},{10,11... | collective-permute-start | bytes 6291464 | tf_op jit(solution)/shard_map/ppermute | solution.py:34
  52.5 13.5 %collective-permute-start.8 = (bf16[32,4096]{1,0:T(8,128)(2,1)S(1)}, bf16[32,4096]{1,0:T(8,128)(2,1)S(1)}, u32[]{:S(2)}, u32[]{:S(2)}) collective-permute-start(bf16[32,4096]{1,0:T(8,128)(2,1)S(1)} %fusion.9), channel_id=1, source_target_pairs={{0,8},{1,9},{2,10},{3,11},{4,12},{5,13},{6,14},{7,15},{8,0},{9,1},... | collective-permute-start | bytes 786440 | tf_op jit(solution)/shard_map/ppermute | solution.py:34
  66.1 7.5 %collective-permute-start.9 = (bf16[32,4096]{1,0:T(8,128)(2,1)S(1)}, bf16[32,4096]{1,0:T(8,128)(2,1)S(1)}, u32[]{:S(2)}, u32[]{:S(2)}) collective-permute-start(bf16[32,4096]{1,0:T(8,128)(2,1)S(1)} %get-tuple-element.22), channel_id=1, source_target_pairs={{0,4},{1,5},{2,6},{3,7},{4,0},{5,1},{6,2},{7,3},{8,12},{9,13},{10,... | collective-permute-start | bytes 786440 | tf_op jit(solution)/shard_map/ppermute | solution.py:34
  66.2 9.5 %collective-permute-start.11 = (bf16[32,4096]{1,0:T(8,128)(2,1)S(1)}, bf16[32,4096]{1,0:T(8,128)(2,1)S(1)}, u32[]{:S(2)}, u32[]{:S(2)}) collective-permute-start(bf16[32,4096]{1,0:T(8,128)(2,1)S(1)} %get-tuple-element.23), channel_id=1, source_target_pairs={{0,2},{1,3},{2,0},{3,1},{4,6},{5,7},{6,4},{7,5},{8,10},{9,11},{10,... | collective-permute-start | bytes 786440 | tf_op jit(solution)/shard_map/ppermute | solution.py:34
  73.6 13.2 %collective-permute-start.10 = (bf16[64,4096]{1,0:T(8,128)(2,1)S(1)}, bf16[64,4096]{1,0:T(8,128)(2,1)S(1)}, u32[]{:S(2)}, u32[]{:S(2)}) collective-permute-start(bf16[64,4096]{1,0:T(8,128)(2,1)S(1)} %constant_dynamic-update-slice_fusion.6), channel_id=1, source_target_pairs={{0,2},{1,3},{2,0},{3,1},{4,6},{5,7},{6,4},{7,5},{8,10},{9,11},{10,... | collective-permute-start | bytes 1572872 | tf_op jit(solution)/shard_map/ppermute | solution.py:34
  75.8 12.7 %collective-permute-start.12 = (bf16[64,4096]{1,0:T(8,128)(2,1)S(1)}, bf16[64,4096]{1,0:T(8,128)(2,1)S(1)}, u32[]{:S(2)}, u32[]{:S(2)}) collective-permute-start(bf16[64,4096]{1,0:T(8,128)(2,1)S(1)} %constant_dynamic-update-slice_fusion.2), channel_id=1, source_target_pairs={{0,4},{1,5},{2,6},{3,7},{4,0},{5,1},{6,2},{7,3},{8,12},{9,13},{10,... | collective-permute-start | bytes 1572872 | tf_op jit(solution)/shard_map/ppermute | solution.py:34
  88.5 6.2 %copy-start.4 = (s32[8]{0:T(128)S(1)}, s32[8]{0:T(128)}, u32[]{:S(2)}) copy-start(s32[8]{0:T(128)} %param.12) | copy-start | bytes 100
  88.5 6.9 %copy-start.3 = (s32[8,12]{1,0:T(8,128)S(1)}, s32[8,12]{1,0:T(8,128)}, u32[]{:S(2)}) copy-start(s32[8,12]{1,0:T(8,128)} %param.11) | copy-start | bytes 1156
  88.6 7.1 %copy-start.6 = (s32[512]{0:T(512)S(1)}, s32[512]{0:T(512)}, u32[]{:S(2)}) copy-start(s32[512]{0:T(512)} %param.10) | copy-start | bytes 6148
  91.2 13.5 %all-to-all-start = ((bf16[16,1,32,256]{3,2,1,0:T(8,128)(2,1)}), bf16[16,1,32,256]{3,2,1,0:T(8,128)(2,1)S(1)}, u32[]{:S(2)}, u32[]{:S(2)}) async-start(bf16[16,1,32,256]{3,2,1,0:T(8,128)(2,1)} %bitcast.4), calls=%async_computation | async-start | bytes 524288 | tf_op jit(solution)/shard_map/all_to_all | solution.py:90

commit v3 on v2

v3 whole, which is shorter than its diff:
```python
import jax
import jax.numpy as jnp
from jax import lax
from jax.experimental import pallas as pl
from jax.experimental.pallas import tpu as pltpu
from jax.sharding import PartitionSpec as P

CORES = 2
CHUNKS = 2
PATHS = 2
UNIT = 4.0


def listed_mask(query_cluster, cand_blocks, cand_count, nblocks):
    nclusters = cand_blocks.shape[0]
    valid = jnp.arange(cand_blocks.shape[1])[None, :] < cand_count[:, None]
    hits = (cand_blocks[:, :, None] == jnp.arange(nblocks)[None, None, :]) & valid[:, :, None]
    listed = jnp.any(hits, axis=1).astype(jnp.float32)
    onehot = (query_cluster[:, None] == jnp.arange(nclusters)[None, :]).astype(jnp.float32)
    return jnp.dot(listed.T, onehot.T, preferred_element_type=jnp.float32)


def product_kernel(rows_ref, columns_ref, out_ref, split_ref):
    nrows = rows_ref.shape[0]

    @pl.when(pl.program_id(0) == 0)
    def _():
        rows = rows_ref[...]
        high = rows.astype(jnp.bfloat16)
        split_ref[:nrows] = high
        split_ref[nrows:] = (rows - high.astype(jnp.float32)).astype(jnp.bfloat16)

    columns = columns_ref[...]
    high = columns.astype(jnp.bfloat16)
    low = (columns - high.astype(jnp.float32)).astype(jnp.bfloat16)
    both = jnp.dot(split_ref[...], high, preferred_element_type=jnp.float32)
    out_ref[...] = (
        both[:nrows] + both[nrows:] + jnp.dot(split_ref[:nrows], low, preferred_element_type=jnp.float32)
    )


def product(rows, columns):
    nrows, depth = rows.shape
    width = columns.shape[1]
    block = min(512, width)
    return pl.pallas_call(
        product_kernel,
        grid=(width // block,),
        in_specs=[
            pl.BlockSpec((nrows, depth), lambda i: (0, 0)),
            pl.BlockSpec((depth, block), lambda i: (0, i)),
        ],
        out_specs=pl.BlockSpec((nrows, block), lambda i: (0, i)),
        out_shape=jax.ShapeDtypeStruct((nrows, width), jnp.float32),
        scratch_shapes=[pltpu.VMEM((2 * nrows, depth), jnp.bfloat16)],
        compiler_params=pltpu.CompilerParams(vmem_limit_bytes=16 * 1024 * 1024),
        cost_estimate=pl.CostEstimate(
            flops=6 * nrows * depth * width, bytes_accessed=4 * width * (nrows + depth), transcendentals=0
        ),
    )(rows, columns)


def shards(queries, precond, train, query_cluster, cand_blocks, cand_count, slot_block):
    n = lax.axis_size("rows")
    chips = n // CORES
    bits = chips.bit_length() - 1
    ybits = [1 + b for b in range(bits // 2)]
    zbits = [1 + b for b in range(bits // 2, bits)]
    orders = (ybits + zbits, zbits[:1] + ybits + zbits[1:])
    me = lax.axis_index("rows")
    core = me & 1

    examples, nblocks, width = train.shape
    nq = queries.shape[0]
    half = nq // CORES

    def swap(value, bit):
        return lax.ppermute(value, "rows", [(r, r ^ (1 << bit)) for r in range(n)])

    def side(bit):
        return (me >> bit) & 1

    def pack(value):
        return (value * UNIT).astype(jnp.float16)

    def unpack(value):
        return value.astype(jnp.float32) * (1.0 / UNIT)

    def part(value, index, count):
        rows = value.shape[0] // count
        return lax.dynamic_slice_in_dim(value, index * rows, rows)

    def join(own, got, bit):
        rows = own.shape[0]
        full = jnp.zeros((2 * rows,) + own.shape[1:], own.dtype)
        full = lax.dynamic_update_slice_in_dim(full, own, side(bit) * rows, 0)
        return lax.dynamic_update_slice_in_dim(full, got, (1 - side(bit)) * rows, 0)

    def after(values, first):
        return list(lax.optimization_barrier((tuple(values), tuple(first)))[0])

    def messages(values, step):
        return [pack(part(values[i], 1 - side(orders[i][step]), 2)) for i in range(PATHS)]

    def exchange(values, sent, step):
        got = [swap(sent[i], orders[i][step]) for i in range(PATHS)]
        return [part(values[i], side(orders[i][step]), 2) + unpack(got[i]) for i in range(PATHS)]

    def gather(values, step):
        got = [swap(values[i], orders[i][step]) for i in range(PATHS)]
        return [join(values[i], got[i], orders[i][step]) for i in range(PATHS)]

    def whole(values):
        return pack(jnp.concatenate(values))

    def total(values, sent):
        got = swap(sent, orders[0][-1])
        rows = values[0].shape[0]
        return [
            (values[i] + unpack(got[i * rows:(i + 1) * rows])).astype(jnp.bfloat16) for i in range(PATHS)
        ]

    other_train = swap(train, 0)

    chunked = queries.reshape(CORES, CHUNKS, half // CHUNKS, queries.shape[1])
    values = []
    for chunk in range(CHUNKS):
        full = product(chunked[:, chunk].reshape(nq // CHUNKS, queries.shape[1]), precond)
        got = swap(pack(part(full, 1 - core, CORES)), 0)
        mixed = part(full, core, CORES) + unpack(got)
        rows = mixed.shape[0] // PATHS
        values.append([mixed[i * rows:(i + 1) * rows] for i in range(PATHS)])
    one, two = values

    steps = bits - 1
    sent = messages(one, 0)
    one = exchange(one, sent, 0)
    sent_two = after(messages(two, 0), one)
    two = exchange(two, sent_two, 0)
    for step in range(1, steps):
        one = exchange(one, messages(one, step), step)
        two = exchange(two, messages(two, step), step)
    one = total(one, whole(one))
    sent_two = whole(two)
    one = after(one, [sent_two])
    two = total(two, sent_two)
    for step in reversed(range(steps)):
        one = gather(one, step)
        if step:
            two = after(two, one)
        two = gather(two, step)
    prequery = jnp.concatenate(one + two, axis=0)

    both = jnp.concatenate([train, other_train], axis=0)
    both, _ = lax.optimization_barrier((both, sent))
    both = jnp.take(jnp.swapaxes(both, 0, 1), slot_block, axis=0, mode="clip")
    both = both.reshape(nblocks * CORES * examples, width)
    raw = lax.dot_general(both, prequery, (((1,), (1,)), ((), ())), preferred_element_type=jnp.float32)
    owned_count = nblocks // n
    ordered = raw.astype(jnp.bfloat16).reshape(n, owned_count, CORES * examples, half)
    got = lax.all_to_all(ordered, "rows", split_axis=0, concat_axis=0, tiled=True)
    got = got.reshape(chips, CORES, owned_count, CORES, examples, half)
    got = jnp.stack([got[:, 0], got[:, 1, :, ::-1]], axis=4)
    got = got.transpose(0, 2, 3, 1, 4, 5).reshape(n * examples, owned_count, nq)

    allowed = listed_mask(query_cluster, cand_blocks, cand_count, nblocks)
    slots = lax.dynamic_slice_in_dim(slot_block, me * owned_count, owned_count)
    return got.astype(jnp.float32) * jnp.take(allowed, slots, axis=0, mode="clip")[None]


def solution(mesh):
    placed = (
        P("groups", "rows"),
        P("rows", None),
        P("rows", "groups", None),
        P("groups"),
        P("groups", None),
        P("groups"),
        P("groups"),
    )
    return jax.shard_map(
        shards,
        mesh=mesh,
        in_specs=placed,
        out_specs=P(None, ("groups", "rows"), None),
        check_vma=False,
    )
```

time: 107 us -> 112 us (1.047)
  waiting for transfers between devices: 65.7 us -> 25.5 us
  starting transfers between devices: 17.2 us -> 42.2 us
  local copies, waits for them, and re-layouts: 6.61 us -> 20.9 us
  matrix products: 15.7 us -> 4.45 us
  other arithmetic: 1.5 us -> 10.7 us
  Pallas kernels: 0 us -> 7.53 us
    ppermute x13 -> x21, waiting for transfers between devices: 57.5 us -> 17.2 us  [swap(): return lax.ppermute(value, 'rows', [(r, r ^ 1 << bit) for r in range(n)])]
    ppermute x13 -> x21, starting transfers between devices: 13.6 us -> 33.5 us  [swap(): return lax.ppermute(value, 'rows', [(r, r ^ 1 << bit) for r in range(n)])]
    dot_general x4 -> x0, matrix products: 14.1 us -> none  [product(): jnp.dot(rows, precond, precision=lax.Precision.HIGH, preferred_element_ty...]
    pallas_call x0 -> x2, Pallas kernels: none -> 7.53 us  [product(): pl.pallas_call(product_kernel, grid=(width // block,), in_specs=[pl.Block...]
    unnamed x15 -> x34, local copies, waits for them, and re-layouts: 1.16 us -> 7.54 us
    all_to_all x1, starting transfers between devices: 3.53 us -> 8.7 us  [shards(): lax.all_to_all(ordered, 'rows', split_axis=0, concat_axis=0, tiled=True)]
    gather x1, local copies, waits for them, and re-layouts: 1.27 us -> 5.07 us  [shards(): both = jnp.take(jnp.swapaxes(both, 0, 1), slot_block, axis=0, mode='clip')]
    add x4 -> x10, other arithmetic: 0.41 us -> 4.21 us  [the longest x2 3.79 us: shards(): mixed = part(full, core, CORES) + unpack(got)]
  transfers between devices with their start and end apart: 14 -> 22, of which waited for: 10 -> 9; matrix products, arithmetic and copies ran while one was open for 13% -> 18% of each run, Pallas kernels for 0% -> 3%
where the time goes in v3:
time: 112 us
  starting transfers between devices  42.2 us (38%)
  waiting for transfers between devices  25.5 us (23%)
  local copies, waits for them, and re-layouts  20.9 us (19%)
  other arithmetic  10.7 us (10%)
  Pallas kernels  7.53 us (7%)
  matrix products  4.45 us (4%)
    ppermute x21, starting transfers between devices, swap(): return lax.ppermute(value, 'rows', [(r, r ^ 1 << bit) for r in range(n)])  33.5 us
    ppermute x21, waiting for transfers between devices, swap(): return lax.ppermute(value, 'rows', [(r, r ^ 1 << bit) for r in range(n)])  17.2 us
    all_to_all x1, starting transfers between devices, shards(): lax.all_to_all(ordered, 'rows', split_axis=0, concat_axis=0, tiled=True)  8.7 us
    all_to_all x1, waiting for transfers between devices, shards(): lax.all_to_all(ordered, 'rows', split_axis=0, concat_axis=0, tiled=True)  8.29 us
    unnamed x34, local copies, waits for them, and re-layouts  7.54 us
    pallas_call x2, Pallas kernels, product(): pl.pallas_call(product_kernel, grid=(width // block,), in_specs=[pl.Block...  7.53 us
    gather x1, local copies, waits for them, and re-layouts, shards(): both = jnp.take(jnp.swapaxes(both, 0, 1), slot_block, axis=0, mode='clip')  5.07 us
    dot_general x1, matrix products, shards(): lax.dot_general(both, prequery, (((1,), (1,)), ((), ())), preferred_eleme...  4.19 us
  transfers between devices with their start and end apart: 22, of which 9 were waited for; matrix products, arithmetic and copies ran while one was open for 18% of the time, Pallas kernels for 3%

profile of v3, /device:TPU:0, one launch (start us, length us, event | category | flops | bytes accessed | tf_op | source)
XLA Modules:
  0.0 111.8 jit_solution(9032668687110352150)
XLA Ops:
  0.0 1.1 fusion.21
  1.1 2.2 %copy-done = f32[256,4096]{1,0:T(8,128)S(1)} copy-done((f32[256,4096]{1,0:T(8,128)S(1)}, f32[256,4096]{1,0:T(8,128)}, u32[]{:S(2)}) %copy-start) | copy-done | bytes 4194328
  3.3 3.8 %shard_map.73 = f32[256,4096]{1,0:T(8,128)S(1)} custom-call(f32[256,256]{1,0:T(8,128)S(1)} %bitcast.23, f32[256,4096]{1,0:T(8,128)S(1)} %copy-done), custom_call_target="tpu_custom_call" | custom-call | flops 1610612736 | bytes 8388608 | tf_op jit(solution)/shard_map/pallas_call | solution.py:46
  7.0 1.4 %multiply_convert_fusion.1 = f16[128,4096]{1,0:T(8,128)(2,1)} fusion(f32[256,4096]{1,0:T(8,128)S(1)} %shard_map.73, s32[]{:T(128)S(6)} %select_n.23), kind=kLoop, calls=%fused_computation.13 | loop fusion | flops 1048576 | bytes 3145732 | tf_op jit(solution)/shard_map/convert_element_type | solution.py:84
  8.4 0.5 collective-permute-start.1
  8.9 3.8 %shard_map.74 = f32[256,4096]{1,0:T(8,128)S(1)} custom-call(f32[256,256]{1,0:T(8,128)S(1)} %bitcast.22, f32[256,4096]{1,0:T(8,128)S(1)} %copy-done.1), custom_call_target="tpu_custom_call" | custom-call | flops 1610612736 | bytes 8388608 | tf_op jit(solution)/shard_map/pallas_call | solution.py:46
  12.7 2.0 %copy-done.2 = f32[256,4096]{1,0:T(8,128)} copy-done((f32[256,4096]{1,0:T(8,128)}, f32[256,4096]{1,0:T(8,128)S(1)}, u32[]{:S(2)}) %copy-start.2) | copy-done | bytes 4194328
  15.0 1.3 %copy-done.5 = bf16[16,16,4096]{2,1,0:T(8,128)(2,1)S(1)} copy-done((bf16[16,16,4096]{2,1,0:T(8,128)(2,1)S(1)}, bf16[16,16,4096]{2,1,0:T(8,128)(2,1)}, u32[]{:S(2)}) %copy-start.5) | copy-done | bytes 2097176
  16.3 1.2 %copy.30 = bf16[16,16,4096]{2,0,1:T(8,128)(2,1)S(1)} copy(bf16[16,16,4096]{2,1,0:T(8,128)(2,1)S(1)} %copy-done.5) | data formatting | bytes 4194304 | tf_op args[2]
  17.6 2.2 %multiply_add_fusion.1 = f32[128,4096]{1,0:T(8,128)S(1)} fusion(f16[128,4096]{1,0:T(8,128)(2,1)} %collective-permute-done.1, f32[256,4096]{1,0:T(8,128)} %copy-done.4, s32[]{:T(128)S(6)} %select_n.22), kind=kLoop, calls=%fused_computation.12 | loop fusion | flops 1572864 | bytes 5242884 | tf_op jit(solution)/shard_map/add | solution.py:130
  20.1 3.0 %collective-permute-start.2 = (f16[32,4096]{1,0:T(8,128)(2,1)S(1)}, f16[32,4096]{1,0:T(8,128)(2,1)S(1)}, u32[]{:S(2)}, u32[]{:S(2)}) collective-permute-start(f16[32,4096]{1,0:T(8,128)(2,1)S(1)} %multiply_convert_fusion.5), channel_id=1, source_target_pairs={{0,2},{1,3},{2,0},{3,1},{4,6},{5,7},{6,4},{7,5},{8,10},{9,11},{10,... | collective-permute-start | bytes 786440 | tf_op jit(solution)/shard_map/ppermute | solution.py:78
  23.1 1.6 %collective-permute-start.4 = (f16[32,4096]{1,0:T(8,128)(2,1)S(1)}, f16[32,4096]{1,0:T(8,128)(2,1)S(1)}, u32[]{:S(2)}, u32[]{:S(2)}) collective-permute-start(f16[32,4096]{1,0:T(8,128)(2,1)S(1)} %multiply_convert_fusion.4), channel_id=1, source_target_pairs={{0,4},{1,5},{2,6},{3,7},{4,0},{5,1},{6,2},{7,3},{8,12},{9,13},{10,... | collective-permute-start | bytes 786440 | tf_op jit(solution)/shard_map/ppermute | solution.py:78
  24.8 1.6 %multiply_add_fusion = f32[128,4096]{1,0:T(8,128)S(1)} fusion(f16[128,4096]{1,0:T(8,128)(2,1)} %collective-permute-done.7, f32[256,4096]{1,0:T(8,128)S(1)} %copy-done.3, s32[]{:T(128)S(6)} %select_n.22), kind=kLoop, calls=%fused_computation.10 | loop fusion | flops 1572864 | bytes 5242884 | tf_op jit(solution)/shard_map/add | solution.py:130
  26.6 3.0 %collective-permute-done.2 = f16[32,4096]{1,0:T(8,128)(2,1)S(1)} collective-permute-done((f16[32,4096]{1,0:T(8,128)(2,1)S(1)}, f16[32,4096]{1,0:T(8,128)(2,1)S(1)}, u32[]{:S(2)}, u32[]{:S(2)}) %collective-permute-start.2) | collective-permute-done | bytes 262176 | tf_op jit(solution)/shard_map/ppermute | solution.py:78
  29.7 1.9 %collective-permute-start.3 = (f16[16,4096]{1,0:T(8,128)(2,1)S(1)}, f16[16,4096]{1,0:T(8,128)(2,1)S(1)}, u32[]{:S(2)}, u32[]{:S(2)}) collective-permute-start(f16[16,4096]{1,0:T(8,128)(2,1)S(1)} %multiply_convert_fusion.9), channel_id=1, source_target_pairs={{0,4},{1,5},{2,6},{3,7},{4,0},{5,1},{6,2},{7,3},{8,12},{9,13},{10,... | collective-permute-start | bytes 393224 | tf_op jit(solution)/shard_map/ppermute | solution.py:78
  31.7 1.6 %collective-permute-start.5 = (f16[16,4096]{1,0:T(8,128)(2,1)S(1)}, f16[16,4096]{1,0:T(8,128)(2,1)S(1)}, u32[]{:S(2)}, u32[]{:S(2)}) collective-permute-start(f16[16,4096]{1,0:T(8,128)(2,1)S(1)} %multiply_convert_fusion.8), channel_id=1, source_target_pairs={{0,2},{1,3},{2,0},{3,1},{4,6},{5,7},{6,4},{7,5},{8,10},{9,11},{10,... | collective-permute-start | bytes 393224 | tf_op jit(solution)/shard_map/ppermute | solution.py:78
  33.3 0.5 collective-permute-start.8
  33.8 1.2 %collective-permute-start.10 = (f16[32,4096]{1,0:T(8,128)(2,1)S(1)}, f16[32,4096]{1,0:T(8,128)(2,1)S(1)}, u32[]{:S(2)}, u32[]{:S(2)}) collective-permute-start(f16[32,4096]{1,0:T(8,128)(2,1)S(1)} %get-tuple-element.14), channel_id=1, source_target_pairs={{0,4},{1,5},{2,6},{3,7},{4,0},{5,1},{6,2},{7,3},{8,12},{9,13},{10,... | collective-permute-start | bytes 786440 | tf_op jit(solution)/shard_map/ppermute | solution.py:78
  35.0 3.2 %collective-permute-done.5 = f16[16,4096]{1,0:T(8,128)(2,1)S(1)} collective-permute-done((f16[16,4096]{1,0:T(8,128)(2,1)S(1)}, f16[16,4096]{1,0:T(8,128)(2,1)S(1)}, u32[]{:S(2)}, u32[]{:S(2)}) %collective-permute-start.5) | collective-permute-done | bytes 131104 | tf_op jit(solution)/shard_map/ppermute | solution.py:78
  38.3 2.7 %collective-permute-start.6 = (f16[32,4096]{1,0:T(8,128)(2,1)S(1)}, f16[32,4096]{1,0:T(8,128)(2,1)S(1)}, u32[]{:S(2)}, u32[]{:S(2)}) collective-permute-start(f16[32,4096]{1,0:T(8,128)(2,1)S(1)} %fusion.11), channel_id=1, source_target_pairs={{0,8},{1,9},{2,10},{3,11},{4,12},{5,13},{6,14},{7,15},{8,0},{9,1},... | collective-permute-start | bytes 786440 | tf_op jit(solution)/shard_map/ppermute | solution.py:78
  41.0 0.8 collective-permute-done.8
  41.8 1.2 %collective-permute-start.9 = (f16[16,4096]{1,0:T(8,128)(2,1)S(1)}, f16[16,4096]{1,0:T(8,128)(2,1)S(1)}, u32[]{:S(2)}, u32[]{:S(2)}) collective-permute-start(f16[16,4096]{1,0:T(8,128)(2,1)S(1)} %multiply_convert_fusion.7), channel_id=1, source_target_pairs={{0,4},{1,5},{2,6},{3,7},{4,0},{5,1},{6,2},{7,3},{8,12},{9,13},{10,... | collective-permute-start | bytes 393224 | tf_op jit(solution)/shard_map/ppermute | solution.py:78
  43.0 1.8 %collective-permute-done.10 = f16[32,4096]{1,0:T(8,128)(2,1)S(1)} collective-permute-done((f16[32,4096]{1,0:T(8,128)(2,1)S(1)}, f16[32,4096]{1,0:T(8,128)(2,1)S(1)}, u32[]{:S(2)}, u32[]{:S(2)}) %collective-permute-start.10) | collective-permute-done | bytes 262176 | tf_op jit(solution)/shard_map/ppermute | solution.py:78
  44.9 2.3 %collective-permute-start.11 = (f16[16,4096]{1,0:T(8,128)(2,1)S(1)}, f16[16,4096]{1,0:T(8,128)(2,1)S(1)}, u32[]{:S(2)}, u32[]{:S(2)}) collective-permute-start(f16[16,4096]{1,0:T(8,128)(2,1)S(1)} %multiply_convert_fusion.6), channel_id=1, source_target_pairs={{0,2},{1,3},{2,0},{3,1},{4,6},{5,7},{6,4},{7,5},{8,10},{9,11},{10,... | collective-permute-start | bytes 393224 | tf_op jit(solution)/shard_map/ppermute | solution.py:78
  47.2 1.2 %collective-permute-done.9 = f16[16,4096]{1,0:T(8,128)(2,1)S(1)} collective-permute-done((f16[16,4096]{1,0:T(8,128)(2,1)S(1)}, f16[16,4096]{1,0:T(8,128)(2,1)S(1)}, u32[]{:S(2)}, u32[]{:S(2)}) %collective-permute-start.9) | collective-permute-done | bytes 131104 | tf_op jit(solution)/shard_map/ppermute | solution.py:78
  48.5 1.7 %collective-permute-done.11 = f16[16,4096]{1,0:T(8,128)(2,1)S(1)} collective-permute-done((f16[16,4096]{1,0:T(8,128)(2,1)S(1)}, f16[16,4096]{1,0:T(8,128)(2,1)S(1)}, u32[]{:S(2)}, u32[]{:S(2)}) %collective-permute-start.11) | collective-permute-done | bytes 131104 | tf_op jit(solution)/shard_map/ppermute | solution.py:78
  50.2 1.7 %collective-permute-start.16 = (f16[32,4096]{1,0:T(8,128)(2,1)S(1)}, f16[32,4096]{1,0:T(8,128)(2,1)S(1)}, u32[]{:S(2)}, u32[]{:S(2)}) collective-permute-start(f16[32,4096]{1,0:T(8,128)(2,1)S(1)} %fusion.12), channel_id=1, source_target_pairs={{0,8},{1,9},{2,10},{3,11},{4,12},{5,13},{6,14},{7,15},{8,0},{9,1},... | collective-permute-start | bytes 786440 | tf_op jit(solution)/shard_map/ppermute | solution.py:78
  52.0 3.4 %collective-permute-start.12 = (bf16[16,4096]{1,0:T(8,128)(2,1)S(1)}, bf16[16,4096]{1,0:T(8,128)(2,1)S(1)}, u32[]{:S(2)}, u32[]{:S(2)}) collective-permute-start(bf16[16,4096]{1,0:T(8,128)(2,1)S(1)} %get-tuple-element.15), channel_id=1, source_target_pairs={{0,4},{1,5},{2,6},{3,7},{4,0},{5,1},{6,2},{7,3},{8,12},{9,13},{10,... | collective-permute-start | bytes 393224 | tf_op jit(solution)/shard_map/ppermute | solution.py:78
  55.4 2.4 %collective-permute-start.14 = (bf16[16,4096]{1,0:T(8,128)(2,1)S(1)}, bf16[16,4096]{1,0:T(8,128)(2,1)S(1)}, u32[]{:S(2)}, u32[]{:S(2)}) collective-permute-start(bf16[16,4096]{1,0:T(8,128)(2,1)S(1)} %get-tuple-element.16), channel_id=1, source_target_pairs={{0,2},{1,3},{2,0},{3,1},{4,6},{5,7},{6,4},{7,5},{8,10},{9,11},{10,... | collective-permute-start | bytes 393224 | tf_op jit(solution)/shard_map/ppermute | solution.py:78
  57.9 0.4 collective-permute-done.12
  58.4 4.1 %collective-permute-start.13 = (bf16[32,4096]{1,0:T(8,128)(2,1)S(1)}, bf16[32,4096]{1,0:T(8,128)(2,1)S(1)}, u32[]{:S(2)}, u32[]{:S(2)}) collective-permute-start(bf16[32,4096]{1,0:T(8,128)(2,1)S(1)} %constant_dynamic-update-slice_fusion.14), channel_id=1, source_target_pairs={{0,2},{1,3},{2,0},{3,1},{4,6},{5,7},{6,4},{7,5},{8,10},{9,11},{10,... | collective-permute-start | bytes 786440 | tf_op jit(solution)/shard_map/ppermute | solution.py:78
  62.5 1.4 %collective-permute-start.15 = (bf16[32,4096]{1,0:T(8,128)(2,1)S(1)}, bf16[32,4096]{1,0:T(8,128)(2,1)}, u32[]{:S(2)}, u32[]{:S(2)}) collective-permute-start(bf16[32,4096]{1,0:T(8,128)(2,1)S(1)} %constant_dynamic-update-slice_fusion.10), channel_id=1, source_target_pairs={{0,4},{1,5},{2,6},{3,7},{4,0},{5,1},{6,2},{7,3},{8,12},{9,13},{10,... | collective-permute-start | bytes 786440 | tf_op jit(solution)/shard_map/ppermute | solution.py:78
  64.1 0.7 collective-permute-start.17
  65.3 5.1 %collective-permute-done.17 = bf16[16,4096]{1,0:T(8,128)(2,1)S(1)} collective-permute-done((bf16[16,4096]{1,0:T(8,128)(2,1)S(1)}, bf16[16,4096]{1,0:T(8,128)(2,1)S(1)}, u32[]{:S(2)}, u32[]{:S(2)}) %collective-permute-start.17) | collective-permute-done | bytes 131104 | tf_op jit(solution)/shard_map/ppermute | solution.py:78
  70.4 1.6 %collective-permute-start.18 = (bf16[32,4096]{1,0:T(8,128)(2,1)S(1)}, bf16[32,4096]{1,0:T(8,128)(2,1)}, u32[]{:S(2)}, u32[]{:S(2)}) collective-permute-start(bf16[32,4096]{1,0:T(8,128)(2,1)S(1)} %constant_dynamic-update-slice_fusion.6), channel_id=1, source_target_pairs={{0,2},{1,3},{2,0},{3,1},{4,6},{5,7},{6,4},{7,5},{8,10},{9,11},{10,... | collective-permute-start | bytes 786440 | tf_op jit(solution)/shard_map/ppermute | solution.py:78
  72.0 1.3 %collective-permute-start.20 = (bf16[32,4096]{1,0:T(8,128)(2,1)S(1)}, bf16[32,4096]{1,0:T(8,128)(2,1)}, u32[]{:S(2)}, u32[]{:S(2)}) collective-permute-start(bf16[32,4096]{1,0:T(8,128)(2,1)S(1)} %constant_dynamic-update-slice_fusion.2), channel_id=1, source_target_pairs={{0,4},{1,5},{2,6},{3,7},{4,0},{5,1},{6,2},{7,3},{8,12},{9,13},{10,... | collective-permute-start | bytes 786440 | tf_op jit(solution)/shard_map/ppermute | solution.py:78
  73.4 0.8 copy-done.6
  74.2 4.1 %pad_maximum_fusion = bf16[32,16,4096]{2,0,1:T(8,128)(2,1)} fusion(bf16[16,16,4096]{2,0,1:T(8,128)(2,1)} %collective-permute-done, bf16[16,16,4096]{2,0,1:T(8,128)(2,1)S(1)} %copy.30), kind=kLoop, calls=%fused_computation.1 | loop fusion | flops 8388608 | bytes 8388608 | tf_op jit(solution)/shard_map/concatenate | solution.py:154
  78.3 5.1 %gather_fusion = bf16[16,32,4096]{2,1,0:T(8,128)(2,1)} fusion(bf16[16,32,4096]{2,1,0:T(8,128)(2,1)} %bitcast.24, s32[1024]{0:T(1024)S(1)} %pad_clamp_fusion), kind=kCustom, calls=%fused_computation | custom fusion | bytes 8388672 | tf_op jit(solution)/shard_map/jit(_take)/gather | solution.py:156
  83.5 1.0 constant_dynamic-update-slice_fusion.8
  84.5 1.0 constant_dynamic-update-slice_fusion.4
  85.5 1.0 constant_dynamic-update-slice_fusion
  86.5 4.2 %fusion.8 = bf16[512,256]{1,0:T(8,128)(2,1)} fusion(bf16[512,4096]{1,0:T(8,128)(2,1)} %bitcast.25, bf16[64,4096]{1,0:T(8,128)(2,1)S(1)} %constant_dynamic-update-slice_fusion, bf16[64,4096]{1,0:T(8,128)(2,1)S(1)} %constant_dynamic-update-slice_fusion.4, bf16[64,4096]{1,0:T(8,128)(2,1)S(1)} %constant_dynamic-update-slice_fusion.8, ...), kind=kOutput, calls=%fused_computation.14 | convolution fusion | flops 1082261504 | bytes 6553600 | tf_op jit(solution)/shard_map/dot_general | solution.py:158
  90.7 8.7 %all-to-all-start = ((bf16[16,1,32,256]{3,2,1,0:T(8,128)(2,1)}), bf16[16,1,32,256]{3,2,1,0:T(8,128)(2,1)S(1)}, u32[]{:S(2)}, u32[]{:S(2)}) async-start(bf16[16,1,32,256]{3,2,1,0:T(8,128)(2,1)} %bitcast.6), calls=%async_computation | async-start | bytes 524288 | tf_op jit(solution)/shard_map/all_to_all | solution.py:161
  99.4 0.6 dynamic_slice.83
  100.5 0.6 constant_dynamic-slice_fusion
  101.2 8.3 %all-to-all-done = bf16[16,1,32,256]{3,2,1,0:T(8,128)(2,1)S(1)} async-done(((bf16[16,1,32,256]{3,2,1,0:T(8,128)(2,1)}), bf16[16,1,32,256]{3,2,1,0:T(8,128)(2,1)S(1)}, u32[]{:S(2)}, u32[]{:S(2)}) %all-to-all-start) | async-done | bytes 262176 | tf_op jit(solution)/shard_map/all_to_all | solution.py:161
  110.5 1.3 %copy.36 = f32[256,1,512]{2,1,0:T(1,128)} copy(f32[256,1,512]{2,0,1:T(8,128)S(1)} %broadcast_multiply_fusion) | data formatting | bytes 1048576 | tf_op jit(solution)/shard_map/mul | solution.py:168
  (98 shorter events, 4.0 us)
Async XLA Ops:
  1.1 2.2 %copy-start = (f32[256,4096]{1,0:T(8,128)S(1)}, f32[256,4096]{1,0:T(8,128)}, u32[]{:S(2)}) copy-start(f32[256,4096]{1,0:T(8,128)} %columns_ref.3) | copy-start | bytes 12582916
  3.3 5.6 %copy-start.1 = (f32[256,4096]{1,0:T(8,128)S(1)}, f32[256,4096]{1,0:T(8,128)}, u32[]{:S(2)}) copy-start(f32[256,4096]{1,0:T(8,128)} %columns_ref.3) | copy-start | bytes 12582916
  7.0 7.9 %copy-start.4 = (f32[256,4096]{1,0:T(8,128)}, f32[256,4096]{1,0:T(8,128)S(1)}, u32[]{:S(2)}) copy-start(f32[256,4096]{1,0:T(8,128)S(1)} %shard_map.73) | copy-start | bytes 12582916
  8.4 9.1 %collective-permute-start.1 = (f16[128,4096]{1,0:T(8,128)(2,1)}, f16[128,4096]{1,0:T(8,128)(2,1)}, u32[]{:S(2)}, u32[]{:S(2)}) collective-permute-start(f16[128,4096]{1,0:T(8,128)(2,1)} %multiply_convert_fusion.1), channel_id=1, source_target_pairs={{0,1},{1,0},{2,3},{3,2},{4,5},{5,4},{6,7},{7,6},{8,9},{9,8},{10,11... | collective-permute-start | bytes 3145736 | tf_op jit(solution)/shard_map/ppermute | solution.py:78
  12.7 2.0 %copy-start.2 = (f32[256,4096]{1,0:T(8,128)}, f32[256,4096]{1,0:T(8,128)S(1)}, u32[]{:S(2)}) copy-start(f32[256,4096]{1,0:T(8,128)S(1)} %shard_map.74) | copy-start | bytes 12582916
  14.7 1.6 %copy-start.5 = (bf16[16,16,4096]{2,1,0:T(8,128)(2,1)S(1)}, bf16[16,16,4096]{2,1,0:T(8,128)(2,1)}, u32[]{:S(2)}) copy-start(bf16[16,16,4096]{2,1,0:T(8,128)(2,1)} %param.9) | copy-start | bytes 6291460
  14.9 2.7 %copy-start.14 = (s32[16]{0:T(128)S(1)}, s32[16]{0:T(128)}, u32[]{:S(2)}) copy-start(s32[16]{0:T(128)} %param.13) | copy-start | bytes 196
  14.9 9.9 %collective-permute-start.7 = (f16[128,4096]{1,0:T(8,128)(2,1)S(1)}, f16[128,4096]{1,0:T(8,128)(2,1)}, u32[]{:S(2)}, u32[]{:S(2)}) collective-permute-start(f16[128,4096]{1,0:T(8,128)(2,1)S(1)} %multiply_convert_fusion), channel_id=1, source_target_pairs={{0,1},{1,0},{2,3},{3,2},{4,5},{5,4},{6,7},{7,6},{8,9},{9,8},{10,11... | collective-permute-start | bytes 3145736 | tf_op jit(solution)/shard_map/ppermute | solution.py:78
  17.4 56.7 %collective-permute-start = (bf16[16,16,4096]{2,0,1:T(8,128)(2,1)S(1)}, bf16[16,16,4096]{2,0,1:T(8,128)(2,1)}, u32[]{:S(2)}, u32[]{:S(2)}) collective-permute-start(bf16[16,16,4096]{2,0,1:T(8,128)(2,1)S(1)} %copy.30), channel_id=1, source_target_pairs={{0,1},{1,0},{2,3},{3,2},{4,5},{5,4},{6,7},{7,6},{8,9},{9,8},{10,11... | collective-permute-start | bytes 6291464 | tf_op jit(solution)/shard_map/ppermute | solution.py:78
  19.8 5.0 %copy-start.3 = (f32[256,4096]{1,0:T(8,128)S(1)}, f32[256,4096]{1,0:T(8,128)}, u32[]{:S(2)}) copy-start(f32[256,4096]{1,0:T(8,128)} %copy-done.2) | copy-start | bytes 12582916
  20.1 9.5 %collective-permute-start.2 = (f16[32,4096]{1,0:T(8,128)(2,1)S(1)}, f16[32,4096]{1,0:T(8,128)(2,1)S(1)}, u32[]{:S(2)}, u32[]{:S(2)}) collective-permute-start(f16[32,4096]{1,0:T(8,128)(2,1)S(1)} %multiply_convert_fusion.5), channel_id=1, source_target_pairs={{0,2},{1,3},{2,0},{3,1},{4,6},{5,7},{6,4},{7,5},{8,10},{9,11},{10,... | collective-permute-start | bytes 786440 | tf_op jit(solution)/shard_map/ppermute | solution.py:78
  23.1 8.4 %collective-permute-start.4 = (f16[32,4096]{1,0:T(8,128)(2,1)S(1)}, f16[32,4096]{1,0:T(8,128)(2,1)S(1)}, u32[]{:S(2)}, u32[]{:S(2)}) collective-permute-start(f16[32,4096]{1,0:T(8,128)(2,1)S(1)} %multiply_convert_fusion.4), channel_id=1, source_target_pairs={{0,4},{1,5},{2,6},{3,7},{4,0},{5,1},{6,2},{7,3},{8,12},{9,13},{10,... | collective-permute-start | bytes 786440 | tf_op jit(solution)/shard_map/ppermute | solution.py:78
  29.7 5.2 %collective-permute-start.3 = (f16[16,4096]{1,0:T(8,128)(2,1)S(1)}, f16[16,4096]{1,0:T(8,128)(2,1)S(1)}, u32[]{:S(2)}, u32[]{:S(2)}) collective-permute-start(f16[16,4096]{1,0:T(8,128)(2,1)S(1)} %multiply_convert_fusion.9), channel_id=1, source_target_pairs={{0,4},{1,5},{2,6},{3,7},{4,0},{5,1},{6,2},{7,3},{8,12},{9,13},{10,... | collective-permute-start | bytes 393224 | tf_op jit(solution)/shard_map/ppermute | solution.py:78
  31.7 6.5 %collective-permute-start.5 = (f16[16,4096]{1,0:T(8,128)(2,1)S(1)}, f16[16,4096]{1,0:T(8,128)(2,1)S(1)}, u32[]{:S(2)}, u32[]{:S(2)}) collective-permute-start(f16[16,4096]{1,0:T(8,128)(2,1)S(1)} %multiply_convert_fusion.8), channel_id=1, source_target_pairs={{0,2},{1,3},{2,0},{3,1},{4,6},{5,7},{6,4},{7,5},{8,10},{9,11},{10,... | collective-permute-start | bytes 393224 | tf_op jit(solution)/shard_map/ppermute | solution.py:78
  33.3 8.4 %collective-permute-start.8 = (f16[32,4096]{1,0:T(8,128)(2,1)S(1)}, f16[32,4096]{1,0:T(8,128)(2,1)S(1)}, u32[]{:S(2)}, u32[]{:S(2)}) collective-permute-start(f16[32,4096]{1,0:T(8,128)(2,1)S(1)} %get-tuple-element.13), channel_id=1, source_target_pairs={{0,2},{1,3},{2,0},{3,1},{4,6},{5,7},{6,4},{7,5},{8,10},{9,11},{10,... | collective-permute-start | bytes 786440 | tf_op jit(solution)/shard_map/ppermute | solution.py:78
  33.8 11.0 %collective-permute-start.10 = (f16[32,4096]{1,0:T(8,128)(2,1)S(1)}, f16[32,4096]{1,0:T(8,128)(2,1)S(1)}, u32[]{:S(2)}, u32[]{:S(2)}) collective-permute-start(f16[32,4096]{1,0:T(8,128)(2,1)S(1)} %get-tuple-element.14), channel_id=1, source_target_pairs={{0,4},{1,5},{2,6},{3,7},{4,0},{5,1},{6,2},{7,3},{8,12},{9,13},{10,... | collective-permute-start | bytes 786440 | tf_op jit(solution)/shard_map/ppermute | solution.py:78
  38.3 13.7 %collective-permute-start.6 = (f16[32,4096]{1,0:T(8,128)(2,1)S(1)}, f16[32,4096]{1,0:T(8,128)(2,1)S(1)}, u32[]{:S(2)}, u32[]{:S(2)}) collective-permute-start(f16[32,4096]{1,0:T(8,128)(2,1)S(1)} %fusion.11), channel_id=1, source_target_pairs={{0,8},{1,9},{2,10},{3,11},{4,12},{5,13},{6,14},{7,15},{8,0},{9,1},... | collective-permute-start | bytes 786440 | tf_op jit(solution)/shard_map/ppermute | solution.py:78
  41.8 6.6 %collective-permute-start.9 = (f16[16,4096]{1,0:T(8,128)(2,1)S(1)}, f16[16,4096]{1,0:T(8,128)(2,1)S(1)}, u32[]{:S(2)}, u32[]{:S(2)}) collective-permute-start(f16[16,4096]{1,0:T(8,128)(2,1)S(1)} %multiply_convert_fusion.7), channel_id=1, source_target_pairs={{0,4},{1,5},{2,6},{3,7},{4,0},{5,1},{6,2},{7,3},{8,12},{9,13},{10,... | collective-permute-start | bytes 393224 | tf_op jit(solution)/shard_map/ppermute | solution.py:78
  44.9 5.2 %collective-permute-start.11 = (f16[16,4096]{1,0:T(8,128)(2,1)S(1)}, f16[16,4096]{1,0:T(8,128)(2,1)S(1)}, u32[]{:S(2)}, u32[]{:S(2)}) collective-permute-start(f16[16,4096]{1,0:T(8,128)(2,1)S(1)} %multiply_convert_fusion.6), channel_id=1, source_target_pairs={{0,2},{1,3},{2,0},{3,1},{4,6},{5,7},{6,4},{7,5},{8,10},{9,11},{10,... | collective-permute-start | bytes 393224 | tf_op jit(solution)/shard_map/ppermute | solution.py:78
  50.2 13.8 %collective-permute-start.16 = (f16[32,4096]{1,0:T(8,128)(2,1)S(1)}, f16[32,4096]{1,0:T(8,128)(2,1)S(1)}, u32[]{:S(2)}, u32[]{:S(2)}) collective-permute-start(f16[32,4096]{1,0:T(8,128)(2,1)S(1)} %fusion.12), channel_id=1, source_target_pairs={{0,8},{1,9},{2,10},{3,11},{4,12},{5,13},{6,14},{7,15},{8,0},{9,1},... | collective-permute-start | bytes 786440 | tf_op jit(solution)/shard_map/ppermute | solution.py:78
  52.0 6.3 %collective-permute-start.12 = (bf16[16,4096]{1,0:T(8,128)(2,1)S(1)}, bf16[16,4096]{1,0:T(8,128)(2,1)S(1)}, u32[]{:S(2)}, u32[]{:S(2)}) collective-permute-start(bf16[16,4096]{1,0:T(8,128)(2,1)S(1)} %get-tuple-element.15), channel_id=1, source_target_pairs={{0,4},{1,5},{2,6},{3,7},{4,0},{5,1},{6,2},{7,3},{8,12},{9,13},{10,... | collective-permute-start | bytes 393224 | tf_op jit(solution)/shard_map/ppermute | solution.py:78
  55.4 7.1 %collective-permute-start.14 = (bf16[16,4096]{1,0:T(8,128)(2,1)S(1)}, bf16[16,4096]{1,0:T(8,128)(2,1)S(1)}, u32[]{:S(2)}, u32[]{:S(2)}) collective-permute-start(bf16[16,4096]{1,0:T(8,128)(2,1)S(1)} %get-tuple-element.16), channel_id=1, source_target_pairs={{0,2},{1,3},{2,0},{3,1},{4,6},{5,7},{6,4},{7,5},{8,10},{9,11},{10,... | collective-permute-start | bytes 393224 | tf_op jit(solution)/shard_map/ppermute | solution.py:78
  58.4 25.1 %collective-permute-start.13 = (bf16[32,4096]{1,0:T(8,128)(2,1)S(1)}, bf16[32,4096]{1,0:T(8,128)(2,1)S(1)}, u32[]{:S(2)}, u32[]{:S(2)}) collective-permute-start(bf16[32,4096]{1,0:T(8,128)(2,1)S(1)} %constant_dynamic-update-slice_fusion.14), channel_id=1, source_target_pairs={{0,2},{1,3},{2,0},{3,1},{4,6},{5,7},{6,4},{7,5},{8,10},{9,11},{10,... | collective-permute-start | bytes 786440 | tf_op jit(solution)/shard_map/ppermute | solution.py:78
  62.5 10.8 %copy-start.8 = (bf16[64,4096]{1,0:T(8,128)(2,1)}, bf16[64,4096]{1,0:T(8,128)(2,1)S(1)}, u32[]{:S(2)}) copy-start(bf16[64,4096]{1,0:T(8,128)(2,1)S(1)} %constant_dynamic-update-slice_fusion.13) | copy-start | bytes 1572868
  62.5 21.0 %collective-permute-start.15 = (bf16[32,4096]{1,0:T(8,128)(2,1)S(1)}, bf16[32,4096]{1,0:T(8,128)(2,1)}, u32[]{:S(2)}, u32[]{:S(2)}) collective-permute-start(bf16[32,4096]{1,0:T(8,128)(2,1)S(1)} %constant_dynamic-update-slice_fusion.10), channel_id=1, source_target_pairs={{0,4},{1,5},{2,6},{3,7},{4,0},{5,1},{6,2},{7,3},{8,12},{9,13},{10,... | collective-permute-start | bytes 786440 | tf_op jit(solution)/shard_map/ppermute | solution.py:78
  64.0 9.3 %copy-start.10 = (bf16[64,4096]{1,0:T(8,128)(2,1)}, bf16[64,4096]{1,0:T(8,128)(2,1)S(1)}, u32[]{:S(2)}) copy-start(bf16[64,4096]{1,0:T(8,128)(2,1)S(1)} %constant_dynamic-update-slice_fusion.9) | copy-start | bytes 1572868
  64.1 6.2 %collective-permute-start.17 = (bf16[16,4096]{1,0:T(8,128)(2,1)S(1)}, bf16[16,4096]{1,0:T(8,128)(2,1)S(1)}, u32[]{:S(2)}, u32[]{:S(2)}) collective-permute-start(bf16[16,4096]{1,0:T(8,128)(2,1)S(1)} %get-tuple-element.17), channel_id=1, source_target_pairs={{0,4},{1,5},{2,6},{3,7},{4,0},{5,1},{6,2},{7,3},{8,12},{9,13},{10,... | collective-permute-start | bytes 393224 | tf_op jit(solution)/shard_map/ppermute | solution.py:78
  64.9 7.1 %collective-permute-start.19 = (bf16[16,4096]{1,0:T(8,128)(2,1)S(1)}, bf16[16,4096]{1,0:T(8,128)(2,1)S(1)}, u32[]{:S(2)}, u32[]{:S(2)}) collective-permute-start(bf16[16,4096]{1,0:T(8,128)(2,1)S(1)} %get-tuple-element.18), channel_id=1, source_target_pairs={{0,2},{1,3},{2,0},{3,1},{4,6},{5,7},{6,4},{7,5},{8,10},{9,11},{10,... | collective-permute-start | bytes 393224 | tf_op jit(solution)/shard_map/ppermute | solution.py:78
  70.4 14.1 %collective-permute-start.18 = (bf16[32,4096]{1,0:T(8,128)(2,1)S(1)}, bf16[32,4096]{1,0:T(8,128)(2,1)}, u32[]{:S(2)}, u32[]{:S(2)}) collective-permute-start(bf16[32,4096]{1,0:T(8,128)(2,1)S(1)} %constant_dynamic-update-slice_fusion.6), channel_id=1, source_target_pairs={{0,2},{1,3},{2,0},{3,1},{4,6},{5,7},{6,4},{7,5},{8,10},{9,11},{10,... | collective-permute-start | bytes 786440 | tf_op jit(solution)/shard_map/ppermute | solution.py:78
  72.0 13.5 %collective-permute-start.20 = (bf16[32,4096]{1,0:T(8,128)(2,1)S(1)}, bf16[32,4096]{1,0:T(8,128)(2,1)}, u32[]{:S(2)}, u32[]{:S(2)}) collective-permute-start(bf16[32,4096]{1,0:T(8,128)(2,1)S(1)} %constant_dynamic-update-slice_fusion.2), channel_id=1, source_target_pairs={{0,4},{1,5},{2,6},{3,7},{4,0},{5,1},{6,2},{7,3},{8,12},{9,13},{10,... | collective-permute-start | bytes 786440 | tf_op jit(solution)/shard_map/ppermute | solution.py:78
  73.4 0.8 copy-start.6
  78.3 5.2 %copy-start.9 = (bf16[64,4096]{1,0:T(8,128)(2,1)S(1)}, bf16[64,4096]{1,0:T(8,128)(2,1)}, u32[]{:S(2)}) copy-start(bf16[64,4096]{1,0:T(8,128)(2,1)} %copy-done.8) | copy-start | bytes 1572868
  78.3 5.2 %copy-start.11 = (bf16[64,4096]{1,0:T(8,128)(2,1)S(1)}, bf16[64,4096]{1,0:T(8,128)(2,1)}, u32[]{:S(2)}) copy-start(bf16[64,4096]{1,0:T(8,128)(2,1)} %copy-done.10) | copy-start | bytes 1572868
  83.4 1.2 %copy-start.7 = (bf16[64,4096]{1,0:T(8,128)(2,1)S(1)}, bf16[64,4096]{1,0:T(8,128)(2,1)}, u32[]{:S(2)}) copy-start(bf16[64,4096]{1,0:T(8,128)(2,1)} %copy-done.6) | copy-start | bytes 1572868
  86.5 12.9 %copy-start.13 = (s32[8]{0:T(128)S(1)}, s32[8]{0:T(128)}, u32[]{:S(2)}) copy-start(s32[8]{0:T(128)} %param.12) | copy-start | bytes 100
  86.5 13.6 %copy-start.12 = (s32[8,12]{1,0:T(8,128)S(1)}, s32[8,12]{1,0:T(8,128)}, u32[]{:S(2)}) copy-start(s32[8,12]{1,0:T(8,128)} %param.11) | copy-start | bytes 1156
  86.5 13.7 %copy-start.15 = (s32[512]{0:T(512)S(1)}, s32[512]{0:T(512)}, u32[]{:S(2)}) copy-start(s32[512]{0:T(512)} %param.10) | copy-start | bytes 6148
  90.7 18.8 %all-to-all-start = ((bf16[16,1,32,256]{3,2,1,0:T(8,128)(2,1)}), bf16[16,1,32,256]{3,2,1,0:T(8,128)(2,1)S(1)}, u32[]{:S(2)}, u32[]{:S(2)}) async-start(bf16[16,1,32,256]{3,2,1,0:T(8,128)(2,1)} %bitcast.6), calls=%async_computation | async-start | bytes 524288 | tf_op jit(solution)/shard_map/all_to_all | solution.py:161

commit v4 on v3

--- a/solution.py
+++ b/solution.py
@@ -9,6 +9,8 @@
 CHUNKS = 2
 PATHS = 2
 UNIT = 4.0
+LANES = 128
+PRODUCT_VMEM = 43
 
 
 def listed_mask(query_cluster, cand_blocks, cand_count, nblocks):
@@ -20,44 +22,117 @@
     return jnp.dot(listed.T, onehot.T, preferred_element_type=jnp.float32)
 
 
-def product_kernel(rows_ref, columns_ref, out_ref, split_ref):
-    nrows = rows_ref.shape[0]
-
-    @pl.when(pl.program_id(0) == 0)
+def product_kernel(rows_ref, columns_hbm, *refs):
+    outs, (columns_ref, left_ref, right_ref, sems) = refs[:-4], refs[-4:]
+    depth = rows_ref.shape[-1]
+    nrows = rows_ref.size // depth
+    steps, _, block = columns_ref.shape
+    step = pl.program_id(0)
+
+    def load(i):
+        return pltpu.make_async_copy(
+            columns_hbm.at[:, pl.ds(pl.multiple_of(i * block, block), block)], columns_ref.at[i], sems.at[i]
+        )
+
+    @pl.when(step == 0)
     def _():
-        rows = rows_ref[...]
+        for i in range(steps):
+            load(i).start()
+        rows = rows_ref[...].reshape(nrows, depth)
         high = rows.astype(jnp.bfloat16)
-        split_ref[:nrows] = high
-        split_ref[nrows:] = (rows - high.astype(jnp.float32)).astype(jnp.bfloat16)
-
-    columns = columns_ref[...]
+        left_ref[:, :depth] = high
+        left_ref[:, depth:2 * depth] = (rows - high.astype(jnp.float32)).astype(jnp.bfloat16)
+        left_ref[:, 2 * depth:] = high
+
+    load(step).wait()
+    columns = columns_ref[step]
     high = columns.astype(jnp.bfloat16)
-    low = (columns - high.astype(jnp.float32)).astype(jnp.bfloat16)
-    both = jnp.dot(split_ref[...], high, preferred_element_type=jnp.float32)
-    out_ref[...] = (
-        both[:nrows] + both[nrows:] + jnp.dot(split_ref[:nrows], low, preferred_element_type=jnp.float32)
-    )
+    right_ref[:depth] = high
+    right_ref[depth:2 * depth] = high
+    right_ref[2 * depth:] = (columns - high.astype(jnp.float32)).astype(jnp.bfloat16)
+    result = jnp.dot(left_ref[...], right_ref[...], preferred_element_type=jnp.float32)
+    result = result.reshape(CORES, CHUNKS, nrows // CORES // CHUNKS, block)
+    for chunk, out_ref in enumerate(outs):
+        out_ref[...] = result[:, chunk]
 
 
 def product(rows, columns):
     nrows, depth = rows.shape
     width = columns.shape[1]
     block = min(512, width)
+    part = nrows // CORES // CHUNKS
     return pl.pallas_call(
         product_kernel,
         grid=(width // block,),
         in_specs=[
             pl.BlockSpec((nrows, depth), lambda i: (0, 0)),
-            pl.BlockSpec((depth, block), lambda i: (0, i)),
+            pl.BlockSpec(memory_space=pltpu.HBM),
         ],
-        out_specs=pl.BlockSpec((nrows, block), lambda i: (0, i)),
-        out_shape=jax.ShapeDtypeStruct((nrows, width), jnp.float32),
-        scratch_shapes=[pltpu.VMEM((2 * nrows, depth), jnp.bfloat16)],
-        compiler_params=pltpu.CompilerParams(vmem_limit_bytes=16 * 1024 * 1024),
+        out_specs=[pl.BlockSpec((CORES, part, block), lambda i: (0, 0, i))] * CHUNKS,
+        out_shape=[jax.ShapeDtypeStruct((CORES, part, width), jnp.float32)] * CHUNKS,
+        scratch_shapes=[
+            pltpu.VMEM((width // block, depth, block), jnp.float32),
+            pltpu.VMEM((nrows, 3 * depth), jnp.bfloat16),
+            pltpu.VMEM((3 * depth, block), jnp.bfloat16),
+            pltpu.SemaphoreType.DMA((width // block,)),
+        ],
+        compiler_params=pltpu.CompilerParams(vmem_limit_bytes=PRODUCT_VMEM * 1024 * 1024),
         cost_estimate=pl.CostEstimate(
             flops=6 * nrows * depth * width, bytes_accessed=4 * width * (nrows + depth), transcendentals=0
         ),
     )(rows, columns)
+
+
+def order_kernel(slots_ref, raw_ref, out_ref, lanes_ref):
+    nblocks, examples, _ = out_ref.shape
+    parts = lanes_ref.shape[0]
+    for i in range(parts):
+        lanes_ref[i] = raw_ref[:, i * LANES:(i + 1) * LANES]
+    for slot in range(nblocks):
+        rows = pl.ds(slots_ref[slot], examples, stride=nblocks)
+        for i in range(parts):
+            out_ref[slot, :, i * LANES:(i + 1) * LANES] = lanes_ref[i, rows, :].astype(out_ref.dtype)
+
+
+def in_slot_order(raw, slots):
+    nblocks = slots.shape[0]
+    examples = raw.shape[0] // nblocks
+    return pl.pallas_call(
+        order_kernel,
+        in_specs=[pl.BlockSpec(memory_space=pltpu.SMEM), pl.BlockSpec(memory_space=pltpu.VMEM)],
+        out_specs=pl.BlockSpec(memory_space=pltpu.VMEM),
+        out_shape=jax.ShapeDtypeStruct((nblocks, examples, raw.shape[1]), jnp.bfloat16),
+        scratch_shapes=[pltpu.VMEM((raw.shape[1] // LANES, raw.shape[0], LANES), jnp.float32)],
+        compiler_params=pltpu.CompilerParams(vmem_limit_bytes=4 * 1024 * 1024),
+        cost_estimate=pl.CostEstimate(flops=raw.size, bytes_accessed=6 * raw.size, transcendentals=0),
+    )(slots, raw)
+
+
+def finish_kernel(got_ref, allowed_ref, out_ref):
+    chips, cores, owned, rows, half = got_ref.shape
+    parts = half // LANES
+    per_row = owned * cores * parts
+    for chip in range(chips):
+        for core in range(cores):
+            for slot in range(owned):
+                scores = got_ref[chip, core, slot].astype(jnp.float32)
+                if core:
+                    scores = jnp.concatenate([scores[rows // 2:], scores[:rows // 2]], axis=0)
+                scores = scores * allowed_ref[slot:slot + 1, core * half:(core + 1) * half]
+                for i in range(parts):
+                    first = chip * rows * per_row + slot * cores * parts + core * parts + i
+                    out_ref[pl.ds(first, rows, stride=per_row), :] = scores[:, i * LANES:(i + 1) * LANES]
+
+
+def finish(got, allowed):
+    chips, cores, owned, rows, half = got.shape
+    flat = pl.pallas_call(
+        finish_kernel,
+        out_shape=jax.ShapeDtypeStruct((chips * rows * owned * cores * half // LANES, LANES), jnp.float32),
+        compiler_params=pltpu.CompilerParams(vmem_limit_bytes=4 * 1024 * 1024),
+        cost_estimate=pl.CostEstimate(flops=got.size, bytes_accessed=6 * got.size, transcendentals=0),
+    )(got, allowed)
+    return flat.reshape(chips * rows, owned, cores * half)
 
 
 def shards(queries, precond, train, query_cluster, cand_blocks, cand_count, slot_block):
@@ -120,20 +195,19 @@
             (values[i] + unpack(got[i * rows:(i + 1) * rows])).astype(jnp.bfloat16) for i in range(PATHS)
         ]
 
-    other_train = swap(train, 0)
-
-    chunked = queries.reshape(CORES, CHUNKS, half // CHUNKS, queries.shape[1])
+    products = product(queries, precond)
+    sent = [swap(pack(lax.dynamic_index_in_dim(full, 1 - core, 0, False)), 0) for full in products]
     values = []
     for chunk in range(CHUNKS):
-        full = product(chunked[:, chunk].reshape(nq // CHUNKS, queries.shape[1]), precond)
-        got = swap(pack(part(full, 1 - core, CORES)), 0)
-        mixed = part(full, core, CORES) + unpack(got)
+        mixed = lax.dynamic_index_in_dim(products[chunk], core, 0, False) + unpack(sent[chunk])
         rows = mixed.shape[0] // PATHS
         values.append([mixed[i * rows:(i + 1) * rows] for i in range(PATHS)])
     one, two = values
 
     steps = bits - 1
     sent = messages(one, 0)
+    train = after([train], sent)[0]
+    other_train = swap(train, 0)
     one = exchange(one, sent, 0)
     sent_two = after(messages(two, 0), one)
     two = exchange(two, sent_two, 0)
@@ -151,21 +225,16 @@
         two = gather(two, step)
     prequery = jnp.concatenate(one + two, axis=0)
 
-    both = jnp.concatenate([train, other_train], axis=0)
-    both, _ = lax.optimization_barrier((both, sent))
-    both = jnp.take(jnp.swapaxes(both, 0, 1), slot_block, axis=0, mode="clip")
-    both = both.reshape(nblocks * CORES * examples, width)
+    both = jnp.concatenate([train, other_train], axis=0).reshape(CORES * examples * nblocks, width)
     raw = lax.dot_general(both, prequery, (((1,), (1,)), ((), ())), preferred_element_type=jnp.float32)
-    owned_count = nblocks // n
-    ordered = raw.astype(jnp.bfloat16).reshape(n, owned_count, CORES * examples, half)
+    owned = nblocks // n
+    ordered = in_slot_order(raw, slot_block).reshape(n, owned, CORES * examples, half)
     got = lax.all_to_all(ordered, "rows", split_axis=0, concat_axis=0, tiled=True)
-    got = got.reshape(chips, CORES, owned_count, CORES, examples, half)
-    got = jnp.stack([got[:, 0], got[:, 1, :, ::-1]], axis=4)
-    got = got.transpose(0, 2, 3, 1, 4, 5).reshape(n * examples, owned_count, nq)
 
     allowed = listed_mask(query_cluster, cand_blocks, cand_count, nblocks)
-    slots = lax.dynamic_slice_in_dim(slot_block, me * owned_count, owned_count)
-    return got.astype(jnp.float32) * jnp.take(allowed, slots, axis=0, mode="clip")[None]
+    slots = lax.dynamic_slice_in_dim(slot_block, me * owned, owned)
+    own_allowed = jnp.take(allowed, slots, axis=0, mode="clip")
+    return finish(got.reshape(chips, CORES, owned, CORES * examples, half), own_allowed)
 
 
 def solution(mesh):

time: 112 us -> 97.4 us (0.87)
  local copies, waits for them, and re-layouts: 20.9 us -> 6.97 us
  waiting for transfers between devices: 25.5 us -> 33.3 us
  other arithmetic: 10.7 us -> 4.4 us
  matrix products: 4.45 us -> 1.54 us
    ppermute x21, waiting for transfers between devices: 17.2 us -> 24.9 us  [swap(): return lax.ppermute(value, 'rows', [(r, r ^ 1 << bit) for r in range(n)])]
    gather x2 -> x1, local copies, waits for them, and re-layouts: 5.71 us -> 0.57 us  [shards(): own_allowed = jnp.take(allowed, slots, axis=0, mode='clip')]
    concatenate x1, other arithmetic: 4.12 us -> 0.36 us  [shards(): jnp.concatenate([train, other_train], axis=0)]
    dot_general x1, matrix products: 4.19 us -> 1.28 us  [shards(): lax.dot_general(both, prequery, (((1,), (1,)), ((), ())), preferred_eleme...]
    dynamic_update_slice x8, local copies, waits for them, and re-layouts: 3.03 us -> 0.15 us  [join(): return lax.dynamic_update_slice_in_dim(full, got, (1 - side(bit)) * rows, 0)]
    unnamed x34 -> x19, local copies, waits for them, and re-layouts: 7.54 us -> 4.95 us
    pallas_call x0 -> x2, Pallas kernels: none -> 2.38 us  [the longest x1 1.55 us: in_slot_order(): pl.pallas_call(order_kernel, in_specs=[pl.BlockSpec(memory_space=pltpu.SM...]
    mul x1 -> x0, local copies, waits for them, and re-layouts: 1.34 us -> none  [shards(): got.astype(jnp.float32)]
  transfers between devices with their start and end apart: 22 -> 22, of which waited for: 9 -> 12; matrix products, arithmetic and copies ran while one was open for 18% -> 6% of each run, Pallas kernels for 3% -> 0%
where the time goes in v4:
time: 97.4 us; the launch traced here: 97.1 us
  starting transfers between devices  41.7 us (43%)
  waiting for transfers between devices  33.3 us (34%)
  Pallas kernels  8.64 us (9%)
  local copies, waits for them, and re-layouts  6.97 us (7%)
  other arithmetic  4.4 us (5%)
  matrix products  1.54 us (2%)
    ppermute x21, starting transfers between devices, swap(): return lax.ppermute(value, 'rows', [(r, r ^ 1 << bit) for r in range(n)])  33.1 us
    ppermute x21, waiting for transfers between devices, swap(): return lax.ppermute(value, 'rows', [(r, r ^ 1 << bit) for r in range(n)])  24.9 us
    all_to_all x1, starting transfers between devices, shards(): lax.all_to_all(ordered, 'rows', split_axis=0, concat_axis=0, tiled=True)  8.6 us
    all_to_all x1, waiting for transfers between devices, shards(): lax.all_to_all(ordered, 'rows', split_axis=0, concat_axis=0, tiled=True)  8.4 us
    pallas_call x1, Pallas kernels, product(): pl.pallas_call(product_kernel, grid=(width // block,), in_specs=[pl.Block...  6.26 us
    unnamed x19, local copies, waits for them, and re-layouts  4.95 us
    add x2, other arithmetic, shards(): lax.dynamic_index_in_dim(products[chunk], core, 0, False)  2.56 us
  transfers between devices with their start and end apart: 22, of which 12 were waited for; matrix products, arithmetic and copies ran while one was open for 6% of the time, Pallas kernels for 0%

profile of v4, /device:TPU:0, one launch (start us, length us, event | category | flops | bytes accessed | tf_op | source)
XLA Modules:
  0.0 97.1 jit_solution(17341777216003760156)
XLA Ops:
  0.0 1.0 %copy-done.4 = f32[512,256]{1,0:T(8,128)S(1)} copy-done((f32[512,256]{1,0:T(8,128)S(1)}, f32[512,256]{1,0:T(8,128)}, u32[]{:S(2)}) %copy-start.4) | copy-done | bytes 524312
  1.0 6.3 %shard_map.73 = (f32[2,128,4096]{2,1,0:T(8,128)S(1)}, f32[2,128,4096]{2,1,0:T(8,128)S(1)}) custom-call(f32[512,256]{1,0:T(8,128)S(1)} %copy-done.4, f32[256,4096]{1,0:T(8,128)} %columns_hbm.1), custom_call_target="tpu_custom_call" | custom-call | flops 3221225472 | bytes 12582912 | tf_op jit(solution)/shard_map/pallas_call | solution.py:64
  7.3 2.0 %copy-done.2 = f32[2,128,4096]{2,1,0:T(8,128)} copy-done((f32[2,128,4096]{2,1,0:T(8,128)}, f32[2,128,4096]{2,1,0:T(8,128)S(1)}, u32[]{:S(2)}) %copy-start.2) | copy-done | bytes 4194328
  9.3 0.2 fusion.8
  9.5 0.5 collective-permute-start
  10.0 0.2 fusion.9
  10.2 0.4 copy-done
  10.6 0.5 collective-permute-start.7
  11.1 1.4 %collective-permute-done = f16[128,4096]{1,0:T(8,128)(2,1)} collective-permute-done((f16[128,4096]{1,0:T(8,128)(2,1)S(1)}, f16[128,4096]{1,0:T(8,128)(2,1)}, u32[]{:S(2)}, u32[]{:S(2)}) %collective-permute-start) | collective-permute-done | bytes 1048608 | tf_op jit(solution)/shard_map/ppermute | solution.py:153
  12.5 2.2 %bitcast_add_fusion.1 = f32[128,4096]{1,0:T(8,128)S(1)} fusion(f16[128,4096]{1,0:T(8,128)(2,1)} %collective-permute-done, f32[2,128,4096]{2,1,0:T(8,128)} %copy-done.2, s32[]{:T(128)S(6)} %select_n.27), kind=kLoop, calls=%fused_computation.10 | loop fusion | flops 1572864 | bytes 5242884 | tf_op jit(solution)/shard_map/add | solution.py:202
  14.7 0.2 fusion.19
  14.9 3.0 %collective-permute-start.2 = (f16[32,4096]{1,0:T(8,128)(2,1)S(1)}, f16[32,4096]{1,0:T(8,128)(2,1)S(1)}, u32[]{:S(2)}, u32[]{:S(2)}) collective-permute-start(f16[32,4096]{1,0:T(8,128)(2,1)S(1)} %multiply_convert_fusion.5), channel_id=1, source_target_pairs={{0,2},{1,3},{2,0},{3,1},{4,6},{5,7},{6,4},{7,5},{8,10},{9,11},{10,... | collective-permute-start | bytes 786440 | tf_op jit(solution)/shard_map/ppermute | solution.py:153
  17.9 1.6 %collective-permute-start.4 = (f16[32,4096]{1,0:T(8,128)(2,1)S(1)}, f16[32,4096]{1,0:T(8,128)(2,1)S(1)}, u32[]{:S(2)}, u32[]{:S(2)}) collective-permute-start(f16[32,4096]{1,0:T(8,128)(2,1)S(1)} %multiply_convert_fusion.4), channel_id=1, source_target_pairs={{0,4},{1,5},{2,6},{3,7},{4,0},{5,1},{6,2},{7,3},{8,12},{9,13},{10,... | collective-permute-start | bytes 786440 | tf_op jit(solution)/shard_map/ppermute | solution.py:153
  19.6 0.4 bitcast_add_fusion
  20.1 1.4 %copy-done.5 = bf16[16,16,4096]{2,1,0:T(8,128)(2,1)S(1)} copy-done((bf16[16,16,4096]{2,1,0:T(8,128)(2,1)S(1)}, bf16[16,16,4096]{2,1,0:T(8,128)(2,1)}, u32[]{:S(2)}) %copy-start.5) | copy-done | bytes 2097176
  21.6 2.9 %collective-permute-done.2 = f16[32,4096]{1,0:T(8,128)(2,1)S(1)} collective-permute-done((f16[32,4096]{1,0:T(8,128)(2,1)S(1)}, f16[32,4096]{1,0:T(8,128)(2,1)S(1)}, u32[]{:S(2)}, u32[]{:S(2)}) %collective-permute-start.2) | collective-permute-done | bytes 262176 | tf_op jit(solution)/shard_map/ppermute | solution.py:153
  24.6 1.9 %collective-permute-start.3 = (f16[16,4096]{1,0:T(8,128)(2,1)S(1)}, f16[16,4096]{1,0:T(8,128)(2,1)S(1)}, u32[]{:S(2)}, u32[]{:S(2)}) collective-permute-start(f16[16,4096]{1,0:T(8,128)(2,1)S(1)} %multiply_convert_fusion.9), channel_id=1, source_target_pairs={{0,4},{1,5},{2,6},{3,7},{4,0},{5,1},{6,2},{7,3},{8,12},{9,13},{10,... | collective-permute-start | bytes 393224 | tf_op jit(solution)/shard_map/ppermute | solution.py:153
  26.6 1.6 %collective-permute-start.5 = (f16[16,4096]{1,0:T(8,128)(2,1)S(1)}, f16[16,4096]{1,0:T(8,128)(2,1)S(1)}, u32[]{:S(2)}, u32[]{:S(2)}) collective-permute-start(f16[16,4096]{1,0:T(8,128)(2,1)S(1)} %multiply_convert_fusion.8), channel_id=1, source_target_pairs={{0,2},{1,3},{2,0},{3,1},{4,6},{5,7},{6,4},{7,5},{8,10},{9,11},{10,... | collective-permute-start | bytes 393224 | tf_op jit(solution)/shard_map/ppermute | solution.py:153
  28.2 0.5 collective-permute-start.8
  28.7 1.2 %collective-permute-start.10 = (f16[32,4096]{1,0:T(8,128)(2,1)S(1)}, f16[32,4096]{1,0:T(8,128)(2,1)S(1)}, u32[]{:S(2)}, u32[]{:S(2)}) collective-permute-start(f16[32,4096]{1,0:T(8,128)(2,1)S(1)} %get-tuple-element.18), channel_id=1, source_target_pairs={{0,4},{1,5},{2,6},{3,7},{4,0},{5,1},{6,2},{7,3},{8,12},{9,13},{10,... | collective-permute-start | bytes 786440 | tf_op jit(solution)/shard_map/ppermute | solution.py:153
  29.9 3.2 %collective-permute-done.5 = f16[16,4096]{1,0:T(8,128)(2,1)S(1)} collective-permute-done((f16[16,4096]{1,0:T(8,128)(2,1)S(1)}, f16[16,4096]{1,0:T(8,128)(2,1)S(1)}, u32[]{:S(2)}, u32[]{:S(2)}) %collective-permute-start.5) | collective-permute-done | bytes 131104 | tf_op jit(solution)/shard_map/ppermute | solution.py:153
  33.2 2.7 %collective-permute-start.6 = (f16[32,4096]{1,0:T(8,128)(2,1)S(1)}, f16[32,4096]{1,0:T(8,128)(2,1)S(1)}, u32[]{:S(2)}, u32[]{:S(2)}) collective-permute-start(f16[32,4096]{1,0:T(8,128)(2,1)S(1)} %fusion.10), channel_id=1, source_target_pairs={{0,8},{1,9},{2,10},{3,11},{4,12},{5,13},{6,14},{7,15},{8,0},{9,1},... | collective-permute-start | bytes 786440 | tf_op jit(solution)/shard_map/ppermute | solution.py:153
  35.9 0.9 collective-permute-done.8
  36.8 1.2 %collective-permute-start.9 = (f16[16,4096]{1,0:T(8,128)(2,1)S(1)}, f16[16,4096]{1,0:T(8,128)(2,1)S(1)}, u32[]{:S(2)}, u32[]{:S(2)}) collective-permute-start(f16[16,4096]{1,0:T(8,128)(2,1)S(1)} %multiply_convert_fusion.7), channel_id=1, source_target_pairs={{0,4},{1,5},{2,6},{3,7},{4,0},{5,1},{6,2},{7,3},{8,12},{9,13},{10,... | collective-permute-start | bytes 393224 | tf_op jit(solution)/shard_map/ppermute | solution.py:153
  38.0 1.6 %collective-permute-done.10 = f16[32,4096]{1,0:T(8,128)(2,1)S(1)} collective-permute-done((f16[32,4096]{1,0:T(8,128)(2,1)S(1)}, f16[32,4096]{1,0:T(8,128)(2,1)S(1)}, u32[]{:S(2)}, u32[]{:S(2)}) %collective-permute-start.10) | collective-permute-done | bytes 262176 | tf_op jit(solution)/shard_map/ppermute | solution.py:153
  39.8 2.1 %collective-permute-start.11 = (f16[16,4096]{1,0:T(8,128)(2,1)S(1)}, f16[16,4096]{1,0:T(8,128)(2,1)S(1)}, u32[]{:S(2)}, u32[]{:S(2)}) collective-permute-start(f16[16,4096]{1,0:T(8,128)(2,1)S(1)} %multiply_convert_fusion.6), channel_id=1, source_target_pairs={{0,2},{1,3},{2,0},{3,1},{4,6},{5,7},{6,4},{7,5},{8,10},{9,11},{10,... | collective-permute-start | bytes 393224 | tf_op jit(solution)/shard_map/ppermute | solution.py:153
  41.9 1.7 %collective-permute-done.9 = f16[16,4096]{1,0:T(8,128)(2,1)S(1)} collective-permute-done((f16[16,4096]{1,0:T(8,128)(2,1)S(1)}, f16[16,4096]{1,0:T(8,128)(2,1)S(1)}, u32[]{:S(2)}, u32[]{:S(2)}) %collective-permute-start.9) | collective-permute-done | bytes 131104 | tf_op jit(solution)/shard_map/ppermute | solution.py:153
  43.6 1.3 %collective-permute-done.11 = f16[16,4096]{1,0:T(8,128)(2,1)S(1)} collective-permute-done((f16[16,4096]{1,0:T(8,128)(2,1)S(1)}, f16[16,4096]{1,0:T(8,128)(2,1)S(1)}, u32[]{:S(2)}, u32[]{:S(2)}) %collective-permute-start.11) | collective-permute-done | bytes 131104 | tf_op jit(solution)/shard_map/ppermute | solution.py:153
  44.9 1.9 %collective-permute-start.16 = (f16[32,4096]{1,0:T(8,128)(2,1)S(1)}, f16[32,4096]{1,0:T(8,128)(2,1)S(1)}, u32[]{:S(2)}, u32[]{:S(2)}) collective-permute-start(f16[32,4096]{1,0:T(8,128)(2,1)S(1)} %fusion.11), channel_id=1, source_target_pairs={{0,8},{1,9},{2,10},{3,11},{4,12},{5,13},{6,14},{7,15},{8,0},{9,1},... | collective-permute-start | bytes 786440 | tf_op jit(solution)/shard_map/ppermute | solution.py:153
  46.9 3.6 %collective-permute-start.12 = (bf16[16,4096]{1,0:T(8,128)(2,1)S(1)}, bf16[16,4096]{1,0:T(8,128)(2,1)S(1)}, u32[]{:S(2)}, u32[]{:S(2)}) collective-permute-start(bf16[16,4096]{1,0:T(8,128)(2,1)S(1)} %get-tuple-element.19), channel_id=1, source_target_pairs={{0,4},{1,5},{2,6},{3,7},{4,0},{5,1},{6,2},{7,3},{8,12},{9,13},{10,... | collective-permute-start | bytes 393224 | tf_op jit(solution)/shard_map/ppermute | solution.py:153
  50.5 2.4 %collective-permute-start.14 = (bf16[16,4096]{1,0:T(8,128)(2,1)S(1)}, bf16[16,4096]{1,0:T(8,128)(2,1)S(1)}, u32[]{:S(2)}, u32[]{:S(2)}) collective-permute-start(bf16[16,4096]{1,0:T(8,128)(2,1)S(1)} %get-tuple-element.20), channel_id=1, source_target_pairs={{0,2},{1,3},{2,0},{3,1},{4,6},{5,7},{6,4},{7,5},{8,10},{9,11},{10,... | collective-permute-start | bytes 393224 | tf_op jit(solution)/shard_map/ppermute | solution.py:153
  53.0 0.4 collective-permute-done.12
  53.5 4.7 %collective-permute-start.13 = (bf16[32,4096]{1,0:T(8,128)(2,1)S(1)}, bf16[32,4096]{1,0:T(8,128)(2,1)S(1)}, u32[]{:S(2)}, u32[]{:S(2)}) collective-permute-start(bf16[32,4096]{1,0:T(8,128)(2,1)S(1)} %constant_dynamic-update-slice_fusion.14), channel_id=1, source_target_pairs={{0,2},{1,3},{2,0},{3,1},{4,6},{5,7},{6,4},{7,5},{8,10},{9,11},{10,... | collective-permute-start | bytes 786440 | tf_op jit(solution)/shard_map/ppermute | solution.py:153
  58.2 0.9 collective-permute-start.15
  59.3 1.2 %collective-permute-start.17 = (bf16[16,4096]{1,0:T(8,128)(2,1)S(1)}, bf16[16,4096]{1,0:T(8,128)(2,1)S(1)}, u32[]{:S(2)}, u32[]{:S(2)}) collective-permute-start(bf16[16,4096]{1,0:T(8,128)(2,1)S(1)} %get-tuple-element.21), channel_id=1, source_target_pairs={{0,4},{1,5},{2,6},{3,7},{4,0},{5,1},{6,2},{7,3},{8,12},{9,13},{10,... | collective-permute-start | bytes 393224 | tf_op jit(solution)/shard_map/ppermute | solution.py:153
  60.7 6.9 %collective-permute-done.17 = bf16[16,4096]{1,0:T(8,128)(2,1)S(1)} collective-permute-done((bf16[16,4096]{1,0:T(8,128)(2,1)S(1)}, bf16[16,4096]{1,0:T(8,128)(2,1)S(1)}, u32[]{:S(2)}, u32[]{:S(2)}) %collective-permute-start.17) | collective-permute-done | bytes 131104 | tf_op jit(solution)/shard_map/ppermute | solution.py:153
  67.9 1.6 %collective-permute-start.20 = (bf16[32,4096]{1,0:T(8,128)(2,1)S(1)}, bf16[32,4096]{1,0:T(8,128)(2,1)S(1)}, u32[]{:S(2)}, u32[]{:S(2)}) collective-permute-start(bf16[32,4096]{1,0:T(8,128)(2,1)S(1)} %constant_dynamic-update-slice_fusion.2), channel_id=1, source_target_pairs={{0,4},{1,5},{2,6},{3,7},{4,0},{5,1},{6,2},{7,3},{8,12},{9,13},{10,... | collective-permute-start | bytes 786440 | tf_op jit(solution)/shard_map/ppermute | solution.py:153
  69.6 4.5 %collective-permute-done.18 = bf16[32,4096]{1,0:T(8,128)(2,1)S(1)} collective-permute-done((bf16[32,4096]{1,0:T(8,128)(2,1)S(1)}, bf16[32,4096]{1,0:T(8,128)(2,1)S(1)}, u32[]{:S(2)}, u32[]{:S(2)}) %collective-permute-start.18) | collective-permute-done | bytes 262176 | tf_op jit(solution)/shard_map/ppermute | solution.py:153
  74.1 0.2 collective-permute-done.20
  74.3 0.4 pad_maximum_fusion
  74.8 1.3 %fusion.raw_ref = f32[512,256]{1,0:T(8,128)S(1)} fusion(bf16[512,4096]{1,0:T(8,128)(2,1)S(1)} %bitcast.17, bf16[64,4096]{1,0:T(8,128)(2,1)S(1)} %constant_dynamic-update-slice_fusion, bf16[64,4096]{1,0:T(8,128)(2,1)S(1)} %constant_dynamic-update-slice_fusion.4, bf16[64,4096]{1,0:T(8,128)(2,1)S(1)} %constant_dynamic-update-slice_fusion.8, ...), kind=kOutput, calls=%fused_computation.1 | convolution fusion | flops 1082130432 | bytes 6815744 | tf_op jit(solution)/shard_map/dot_general | solution.py:229
  76.1 1.6 %shard_map.74 = bf16[16,32,256]{2,1,0:T(8,128)(2,1)} custom-call(s32[16]{0:T(128)S(1)} %copy-done.3, f32[512,256]{1,0:T(8,128)S(1)} %fusion.raw_ref), custom_call_target="tpu_custom_call" | custom-call | flops 131072 | bytes 786432 | tf_op jit(solution)/shard_map/pallas_call | solution.py:100
  77.6 8.6 %all-to-all-start = ((bf16[16,1,32,256]{3,2,1,0:T(8,128)(2,1)}), bf16[16,1,32,256]{3,2,1,0:T(8,128)(2,1)S(1)}, u32[]{:S(2)}, u32[]{:S(2)}) async-start(bf16[16,1,32,256]{3,2,1,0:T(8,128)(2,1)} %bitcast.6), calls=%async_computation | async-start | bytes 524288 | tf_op jit(solution)/shard_map/all_to_all | solution.py:232
  86.2 0.6 dynamic_slice.84
  87.0 0.3 fusion.12
  87.3 0.6 constant_dynamic-slice_fusion.allowed_ref
  87.9 8.4 %all-to-all-done = bf16[16,1,32,256]{3,2,1,0:T(8,128)(2,1)S(1)} async-done(((bf16[16,1,32,256]{3,2,1,0:T(8,128)(2,1)}), bf16[16,1,32,256]{3,2,1,0:T(8,128)(2,1)S(1)}, u32[]{:S(2)}, u32[]{:S(2)}) %all-to-all-start) | async-done | bytes 262176 | tf_op jit(solution)/shard_map/all_to_all | solution.py:232
  96.3 0.8 shard_map.75
  (74 shorter events, 2.1 us)
Async XLA Ops:
  0.0 1.0 %copy-start.4 = (f32[512,256]{1,0:T(8,128)S(1)}, f32[512,256]{1,0:T(8,128)}, u32[]{:S(2)}) copy-start(f32[512,256]{1,0:T(8,128)} %rows_ref.1) | copy-start | bytes 1572868
  7.3 2.0 %copy-start.2 = (f32[2,128,4096]{2,1,0:T(8,128)}, f32[2,128,4096]{2,1,0:T(8,128)S(1)}, u32[]{:S(2)}) copy-start(f32[2,128,4096]{2,1,0:T(8,128)S(1)} %get-tuple-element.14) | copy-start | bytes 12582916
  7.3 3.3 %copy-start = (f32[2,128,4096]{2,1,0:T(8,128)}, f32[2,128,4096]{2,1,0:T(8,128)S(1)}, u32[]{:S(2)}) copy-start(f32[2,128,4096]{2,1,0:T(8,128)S(1)} %get-tuple-element.16) | copy-start | bytes 12582916
  9.5 2.9 %collective-permute-start = (f16[128,4096]{1,0:T(8,128)(2,1)S(1)}, f16[128,4096]{1,0:T(8,128)(2,1)}, u32[]{:S(2)}, u32[]{:S(2)}) collective-permute-start(f16[128,4096]{1,0:T(8,128)(2,1)S(1)} %fusion.8), channel_id=1, source_target_pairs={{0,1},{1,0},{2,3},{3,2},{4,5},{5,4},{6,7},{7,6},{8,9},{9,8},{10,11... | collective-permute-start | bytes 3145736 | tf_op jit(solution)/shard_map/ppermute | solution.py:153
  10.6 9.0 %collective-permute-start.7 = (f16[128,4096]{1,0:T(8,128)(2,1)S(1)}, f16[128,4096]{1,0:T(8,128)(2,1)S(1)}, u32[]{:S(2)}, u32[]{:S(2)}) collective-permute-start(f16[128,4096]{1,0:T(8,128)(2,1)S(1)} %fusion.9), channel_id=1, source_target_pairs={{0,1},{1,0},{2,3},{3,2},{4,5},{5,4},{6,7},{7,6},{8,9},{9,8},{10,11... | collective-permute-start | bytes 3145736 | tf_op jit(solution)/shard_map/ppermute | solution.py:153
  14.7 4.9 %copy-start.1 = (f32[2,128,4096]{2,1,0:T(8,128)S(1)}, f32[2,128,4096]{2,1,0:T(8,128)}, u32[]{:S(2)}) copy-start(f32[2,128,4096]{2,1,0:T(8,128)} %copy-done) | copy-start | bytes 12582916
  14.9 9.6 %collective-permute-start.2 = (f16[32,4096]{1,0:T(8,128)(2,1)S(1)}, f16[32,4096]{1,0:T(8,128)(2,1)S(1)}, u32[]{:S(2)}, u32[]{:S(2)}) collective-permute-start(f16[32,4096]{1,0:T(8,128)(2,1)S(1)} %multiply_convert_fusion.5), channel_id=1, source_target_pairs={{0,2},{1,3},{2,0},{3,1},{4,6},{5,7},{6,4},{7,5},{8,10},{9,11},{10,... | collective-permute-start | bytes 786440 | tf_op jit(solution)/shard_map/ppermute | solution.py:153
  17.9 8.5 %collective-permute-start.4 = (f16[32,4096]{1,0:T(8,128)(2,1)S(1)}, f16[32,4096]{1,0:T(8,128)(2,1)S(1)}, u32[]{:S(2)}, u32[]{:S(2)}) collective-permute-start(f16[32,4096]{1,0:T(8,128)(2,1)S(1)} %multiply_convert_fusion.4), channel_id=1, source_target_pairs={{0,4},{1,5},{2,6},{3,7},{4,0},{5,1},{6,2},{7,3},{8,12},{9,13},{10,... | collective-permute-start | bytes 786440 | tf_op jit(solution)/shard_map/ppermute | solution.py:153
  20.0 1.6 %copy-start.5 = (bf16[16,16,4096]{2,1,0:T(8,128)(2,1)S(1)}, bf16[16,16,4096]{2,1,0:T(8,128)(2,1)}, u32[]{:S(2)}) copy-start(bf16[16,16,4096]{2,1,0:T(8,128)(2,1)} %param.9) | copy-start | bytes 6291460
  21.6 52.8 %collective-permute-start.1 = (bf16[16,16,4096]{2,1,0:T(8,128)(2,1)S(1)}, bf16[16,16,4096]{2,1,0:T(8,128)(2,1)S(1)}, u32[]{:S(2)}, u32[]{:S(2)}) collective-permute-start(bf16[16,16,4096]{2,1,0:T(8,128)(2,1)S(1)} %copy-done.5), channel_id=1, source_target_pairs={{0,1},{1,0},{2,3},{3,2},{4,5},{5,4},{6,7},{7,6},{8,9},{9,8},{10,11... | collective-permute-start | bytes 6291464 | tf_op jit(solution)/shard_map/ppermute | solution.py:153
  24.6 5.2 %collective-permute-start.3 = (f16[16,4096]{1,0:T(8,128)(2,1)S(1)}, f16[16,4096]{1,0:T(8,128)(2,1)S(1)}, u32[]{:S(2)}, u32[]{:S(2)}) collective-permute-start(f16[16,4096]{1,0:T(8,128)(2,1)S(1)} %multiply_convert_fusion.9), channel_id=1, source_target_pairs={{0,4},{1,5},{2,6},{3,7},{4,0},{5,1},{6,2},{7,3},{8,12},{9,13},{10,... | collective-permute-start | bytes 393224 | tf_op jit(solution)/shard_map/ppermute | solution.py:153
  26.6 6.5 %collective-permute-start.5 = (f16[16,4096]{1,0:T(8,128)(2,1)S(1)}, f16[16,4096]{1,0:T(8,128)(2,1)S(1)}, u32[]{:S(2)}, u32[]{:S(2)}) collective-permute-start(f16[16,4096]{1,0:T(8,128)(2,1)S(1)} %multiply_convert_fusion.8), channel_id=1, source_target_pairs={{0,2},{1,3},{2,0},{3,1},{4,6},{5,7},{6,4},{7,5},{8,10},{9,11},{10,... | collective-permute-start | bytes 393224 | tf_op jit(solution)/shard_map/ppermute | solution.py:153
  28.2 8.5 %collective-permute-start.8 = (f16[32,4096]{1,0:T(8,128)(2,1)S(1)}, f16[32,4096]{1,0:T(8,128)(2,1)S(1)}, u32[]{:S(2)}, u32[]{:S(2)}) collective-permute-start(f16[32,4096]{1,0:T(8,128)(2,1)S(1)} %get-tuple-element.17), channel_id=1, source_target_pairs={{0,2},{1,3},{2,0},{3,1},{4,6},{5,7},{6,4},{7,5},{8,10},{9,11},{10,... | collective-permute-start | bytes 786440 | tf_op jit(solution)/shard_map/ppermute | solution.py:153
  28.7 11.0 %collective-permute-start.10 = (f16[32,4096]{1,0:T(8,128)(2,1)S(1)}, f16[32,4096]{1,0:T(8,128)(2,1)S(1)}, u32[]{:S(2)}, u32[]{:S(2)}) collective-permute-start(f16[32,4096]{1,0:T(8,128)(2,1)S(1)} %get-tuple-element.18), channel_id=1, source_target_pairs={{0,4},{1,5},{2,6},{3,7},{4,0},{5,1},{6,2},{7,3},{8,12},{9,13},{10,... | collective-permute-start | bytes 786440 | tf_op jit(solution)/shard_map/ppermute | solution.py:153
  33.2 13.6 %collective-permute-start.6 = (f16[32,4096]{1,0:T(8,128)(2,1)S(1)}, f16[32,4096]{1,0:T(8,128)(2,1)S(1)}, u32[]{:S(2)}, u32[]{:S(2)}) collective-permute-start(f16[32,4096]{1,0:T(8,128)(2,1)S(1)} %fusion.10), channel_id=1, source_target_pairs={{0,8},{1,9},{2,10},{3,11},{4,12},{5,13},{6,14},{7,15},{8,0},{9,1},... | collective-permute-start | bytes 786440 | tf_op jit(solution)/shard_map/ppermute | solution.py:153
  36.8 6.7 %collective-permute-start.9 = (f16[16,4096]{1,0:T(8,128)(2,1)S(1)}, f16[16,4096]{1,0:T(8,128)(2,1)S(1)}, u32[]{:S(2)}, u32[]{:S(2)}) collective-permute-start(f16[16,4096]{1,0:T(8,128)(2,1)S(1)} %multiply_convert_fusion.7), channel_id=1, source_target_pairs={{0,4},{1,5},{2,6},{3,7},{4,0},{5,1},{6,2},{7,3},{8,12},{9,13},{10,... | collective-permute-start | bytes 393224 | tf_op jit(solution)/shard_map/ppermute | solution.py:153
  39.8 5.0 %collective-permute-start.11 = (f16[16,4096]{1,0:T(8,128)(2,1)S(1)}, f16[16,4096]{1,0:T(8,128)(2,1)S(1)}, u32[]{:S(2)}, u32[]{:S(2)}) collective-permute-start(f16[16,4096]{1,0:T(8,128)(2,1)S(1)} %multiply_convert_fusion.6), channel_id=1, source_target_pairs={{0,2},{1,3},{2,0},{3,1},{4,6},{5,7},{6,4},{7,5},{8,10},{9,11},{10,... | collective-permute-start | bytes 393224 | tf_op jit(solution)/shard_map/ppermute | solution.py:153
  44.9 14.3 %collective-permute-start.16 = (f16[32,4096]{1,0:T(8,128)(2,1)S(1)}, f16[32,4096]{1,0:T(8,128)(2,1)S(1)}, u32[]{:S(2)}, u32[]{:S(2)}) collective-permute-start(f16[32,4096]{1,0:T(8,128)(2,1)S(1)} %fusion.11), channel_id=1, source_target_pairs={{0,8},{1,9},{2,10},{3,11},{4,12},{5,13},{6,14},{7,15},{8,0},{9,1},... | collective-permute-start | bytes 786440 | tf_op jit(solution)/shard_map/ppermute | solution.py:153
  46.9 6.6 %collective-permute-start.12 = (bf16[16,4096]{1,0:T(8,128)(2,1)S(1)}, bf16[16,4096]{1,0:T(8,128)(2,1)S(1)}, u32[]{:S(2)}, u32[]{:S(2)}) collective-permute-start(bf16[16,4096]{1,0:T(8,128)(2,1)S(1)} %get-tuple-element.19), channel_id=1, source_target_pairs={{0,4},{1,5},{2,6},{3,7},{4,0},{5,1},{6,2},{7,3},{8,12},{9,13},{10,... | collective-permute-start | bytes 393224 | tf_op jit(solution)/shard_map/ppermute | solution.py:153
  50.5 7.7 %collective-permute-start.14 = (bf16[16,4096]{1,0:T(8,128)(2,1)S(1)}, bf16[16,4096]{1,0:T(8,128)(2,1)S(1)}, u32[]{:S(2)}, u32[]{:S(2)}) collective-permute-start(bf16[16,4096]{1,0:T(8,128)(2,1)S(1)} %get-tuple-element.20), channel_id=1, source_target_pairs={{0,2},{1,3},{2,0},{3,1},{4,6},{5,7},{6,4},{7,5},{8,10},{9,11},{10,... | collective-permute-start | bytes 393224 | tf_op jit(solution)/shard_map/ppermute | solution.py:153
  53.5 16.1 %collective-permute-start.13 = (bf16[32,4096]{1,0:T(8,128)(2,1)S(1)}, bf16[32,4096]{1,0:T(8,128)(2,1)S(1)}, u32[]{:S(2)}, u32[]{:S(2)}) collective-permute-start(bf16[32,4096]{1,0:T(8,128)(2,1)S(1)} %constant_dynamic-update-slice_fusion.14), channel_id=1, source_target_pairs={{0,2},{1,3},{2,0},{3,1},{4,6},{5,7},{6,4},{7,5},{8,10},{9,11},{10,... | collective-permute-start | bytes 786440 | tf_op jit(solution)/shard_map/ppermute | solution.py:153
  58.2 11.4 %collective-permute-start.15 = (bf16[32,4096]{1,0:T(8,128)(2,1)S(1)}, bf16[32,4096]{1,0:T(8,128)(2,1)S(1)}, u32[]{:S(2)}, u32[]{:S(2)}) collective-permute-start(bf16[32,4096]{1,0:T(8,128)(2,1)S(1)} %constant_dynamic-update-slice_fusion.10), channel_id=1, source_target_pairs={{0,4},{1,5},{2,6},{3,7},{4,0},{5,1},{6,2},{7,3},{8,12},{9,13},{10,... | collective-permute-start | bytes 786440 | tf_op jit(solution)/shard_map/ppermute | solution.py:153
  59.3 8.3 %collective-permute-start.17 = (bf16[16,4096]{1,0:T(8,128)(2,1)S(1)}, bf16[16,4096]{1,0:T(8,128)(2,1)S(1)}, u32[]{:S(2)}, u32[]{:S(2)}) collective-permute-start(bf16[16,4096]{1,0:T(8,128)(2,1)S(1)} %get-tuple-element.21), channel_id=1, source_target_pairs={{0,4},{1,5},{2,6},{3,7},{4,0},{5,1},{6,2},{7,3},{8,12},{9,13},{10,... | collective-permute-start | bytes 393224 | tf_op jit(solution)/shard_map/ppermute | solution.py:153
  60.6 7.2 %collective-permute-start.19 = (bf16[16,4096]{1,0:T(8,128)(2,1)S(1)}, bf16[16,4096]{1,0:T(8,128)(2,1)S(1)}, u32[]{:S(2)}, u32[]{:S(2)}) collective-permute-start(bf16[16,4096]{1,0:T(8,128)(2,1)S(1)} %get-tuple-element.22), channel_id=1, source_target_pairs={{0,2},{1,3},{2,0},{3,1},{4,6},{5,7},{6,4},{7,5},{8,10},{9,11},{10,... | collective-permute-start | bytes 393224 | tf_op jit(solution)/shard_map/ppermute | solution.py:153
  67.7 6.4 %collective-permute-start.18 = (bf16[32,4096]{1,0:T(8,128)(2,1)S(1)}, bf16[32,4096]{1,0:T(8,128)(2,1)S(1)}, u32[]{:S(2)}, u32[]{:S(2)}) collective-permute-start(bf16[32,4096]{1,0:T(8,128)(2,1)S(1)} %constant_dynamic-update-slice_fusion.6), channel_id=1, source_target_pairs={{0,2},{1,3},{2,0},{3,1},{4,6},{5,7},{6,4},{7,5},{8,10},{9,11},{10,... | collective-permute-start | bytes 786440 | tf_op jit(solution)/shard_map/ppermute | solution.py:153
  67.9 6.4 %collective-permute-start.20 = (bf16[32,4096]{1,0:T(8,128)(2,1)S(1)}, bf16[32,4096]{1,0:T(8,128)(2,1)S(1)}, u32[]{:S(2)}, u32[]{:S(2)}) collective-permute-start(bf16[32,4096]{1,0:T(8,128)(2,1)S(1)} %constant_dynamic-update-slice_fusion.2), channel_id=1, source_target_pairs={{0,4},{1,5},{2,6},{3,7},{4,0},{5,1},{6,2},{7,3},{8,12},{9,13},{10,... | collective-permute-start | bytes 786440 | tf_op jit(solution)/shard_map/ppermute | solution.py:153
  74.7 1.3 %copy-start.3 = (s32[16]{0:T(128)S(1)}, s32[16]{0:T(128)}, u32[]{:S(2)}) copy-start(s32[16]{0:T(128)} %slots_ref.1) | copy-start | bytes 196
  74.7 11.5 %copy-start.7 = (s32[8]{0:T(128)S(1)}, s32[8]{0:T(128)}, u32[]{:S(2)}) copy-start(s32[8]{0:T(128)} %param.12) | copy-start | bytes 100
  74.7 12.1 %copy-start.6 = (s32[8,12]{1,0:T(8,128)S(1)}, s32[8,12]{1,0:T(8,128)}, u32[]{:S(2)}) copy-start(s32[8,12]{1,0:T(8,128)} %param.11) | copy-start | bytes 1156
  74.7 12.3 %copy-start.8 = (s32[512]{0:T(512)S(1)}, s32[512]{0:T(512)}, u32[]{:S(2)}) copy-start(s32[512]{0:T(512)} %param.10) | copy-start | bytes 6148
  77.6 18.7 %all-to-all-start = ((bf16[16,1,32,256]{3,2,1,0:T(8,128)(2,1)}), bf16[16,1,32,256]{3,2,1,0:T(8,128)(2,1)S(1)}, u32[]{:S(2)}, u32[]{:S(2)}) async-start(bf16[16,1,32,256]{3,2,1,0:T(8,128)(2,1)} %bitcast.6), calls=%async_computation | async-start | bytes 524288 | tf_op jit(solution)/shard_map/all_to_all | solution.py:232

commit v5 on v2

v5 whole, which is shorter than its diff:
```python
import jax
import jax.numpy as jnp
from jax import lax
from jax.experimental import pallas as pl
from jax.experimental.pallas import tpu as pltpu
from jax.sharding import PartitionSpec as P

CORES = 2
CHUNKS = 2
UNIT = 4.0
LANES = 128
OTHER_VMEM = 47
MINE_VMEM = 43


def listed_mask(query_cluster, cand_blocks, cand_count, nblocks):
    nclusters = cand_blocks.shape[0]
    valid = jnp.arange(cand_blocks.shape[1])[None, :] < cand_count[:, None]
    hits = (cand_blocks[:, :, None] == jnp.arange(nblocks)[None, None, :]) & valid[:, :, None]
    listed = jnp.any(hits, axis=1).astype(jnp.float32)
    onehot = (query_cluster[:, None] == jnp.arange(nclusters)[None, :]).astype(jnp.float32)
    return jnp.dot(listed.T, onehot.T, preferred_element_type=jnp.float32)


def product_kernel(core_ref, rows_ref, columns_hbm, *refs):
    outs, (columns_ref, sems) = refs[:-2], refs[-2:]
    steps, _, block = columns_ref.shape

    def load(i):
        return pltpu.make_async_copy(
            columns_hbm.at[:, i * block:(i + 1) * block], columns_ref.at[i], sems.at[i]
        )

    for i in range(steps):
        load(i).start()
    half = rows_ref.shape[0] // CORES
    rows = rows_ref[pl.ds(pl.multiple_of(core_ref[0] * half, half), half), :]
    high = rows.astype(jnp.bfloat16)
    low = (rows - high.astype(jnp.float32)).astype(jnp.bfloat16)
    left = jnp.concatenate([high, low, high], axis=1)
    part = half // len(outs)
    for i in range(steps):
        load(i).wait()
        columns = columns_ref[i]
        high = columns.astype(jnp.bfloat16)
        low = (columns - high.astype(jnp.float32)).astype(jnp.bfloat16)
        right = jnp.concatenate([high, high, low], axis=0)
        result = jnp.dot(left, right, preferred_element_type=jnp.float32)
        for chunk, out_ref in enumerate(outs):
            out_ref[:, i * block:(i + 1) * block] = result[chunk * part:(chunk + 1) * part]


def product(core, rows, columns, vmem):
    nrows, depth = rows.shape
    width = columns.shape[1]
    block = min(512, width)
    part = nrows // CORES // CHUNKS
    return pl.pallas_call(
        product_kernel,
        in_specs=[
            pl.BlockSpec(memory_space=pltpu.SMEM),
            pl.BlockSpec(memory_space=pltpu.VMEM),
            pl.BlockSpec(memory_space=pltpu.HBM),
        ],
        out_specs=[pl.BlockSpec(memory_space=pltpu.VMEM)] * CHUNKS,
        out_shape=[jax.ShapeDtypeStruct((part, width), jnp.float32)] * CHUNKS,
        scratch_shapes=[
            pltpu.VMEM((width // block, depth, block), jnp.float32),
            pltpu.SemaphoreType.DMA((width // block,)),
        ],
        compiler_params=pltpu.CompilerParams(vmem_limit_bytes=vmem * 1024 * 1024),
        cost_estimate=pl.CostEstimate(
            flops=3 * nrows * depth * width,
            bytes_accessed=4 * width * depth + 2 * width * nrows,
            transcendentals=0,
        ),
    )(core.reshape(1), rows, columns)


def pieces_kernel(order_ref, *refs):
    raws, outs = refs[:CHUNKS], refs[CHUNKS:]
    nblocks = order_ref.shape[0]
    owned = nblocks // len(outs)
    for k, out_ref in enumerate(outs):
        for slot in range(owned):
            examples = out_ref.shape[1]
            rows = pl.ds(order_ref[k * owned + slot], examples, stride=nblocks)
            for i in range(CHUNKS):
                width = raws[i].shape[1]
                out_ref[slot, :, i * width:(i + 1) * width] = raws[i][rows, :].astype(out_ref.dtype)


def pieces(raws, order, n):
    nblocks = order.shape[0]
    rows, width = raws[0].shape
    shape = jax.ShapeDtypeStruct((nblocks // n, rows // nblocks, CHUNKS * width), jnp.bfloat16)
    return pl.pallas_call(
        pieces_kernel,
        in_specs=[pl.BlockSpec(memory_space=pltpu.SMEM)] + [pl.BlockSpec(memory_space=pltpu.VMEM)] * CHUNKS,
        out_specs=[pl.BlockSpec(memory_space=pltpu.VMEM)] * n,
        out_shape=[shape] * n,
        compiler_params=pltpu.CompilerParams(vmem_limit_bytes=4 * 1024 * 1024),
        cost_estimate=pl.CostEstimate(flops=rows * width, bytes_accessed=12 * rows * width, transcendentals=0),
    )(order, *raws)


def finish_kernel(me_ref, allowed_ref, *refs):
    got, out_ref = refs[:-1], refs[-1]
    owned, rows, half = got[0].shape
    parts = half // LANES
    per_row = owned * CORES * parts
    examples = rows // CORES
    for k, got_ref in enumerate(got):
        source = me_ref[0] ^ k
        core = source & 1
        for slot in range(owned):
            scores = got_ref[slot].astype(jnp.float32)
            for i in range(parts):
                allowed = allowed_ref[pl.ds(slot * CORES * parts + core * parts + i, 1), :]
                lanes = scores[:, i * LANES:(i + 1) * LANES] * allowed
                for j in range(CORES):
                    first = ((source >> 1) * CORES + (core ^ j)) * examples * per_row
                    first = first + (slot * CORES + core) * parts + i
                    out_ref[pl.ds(first, examples, stride=per_row), :] = lanes[j * examples:(j + 1) * examples]


def finish(me, allowed, got):
    owned, rows, half = got[0].shape
    total = len(got) * rows * half
    flat = pl.pallas_call(
        finish_kernel,
        in_specs=[pl.BlockSpec(memory_space=pltpu.SMEM)]
        + [pl.BlockSpec(memory_space=pltpu.VMEM)] * (1 + len(got)),
        out_specs=pl.BlockSpec(memory_space=pltpu.VMEM),
        out_shape=jax.ShapeDtypeStruct((owned * total // LANES, LANES), jnp.float32),
        compiler_params=pltpu.CompilerParams(vmem_limit_bytes=4 * 1024 * 1024),
        cost_estimate=pl.CostEstimate(flops=total, bytes_accessed=6 * total, transcendentals=0),
    )(me.reshape(1), allowed.reshape(-1, LANES), *got)
    return flat.reshape(len(got) * rows // CORES, owned, CORES * half)


def shards(queries, precond, train, query_cluster, cand_blocks, cand_count, slot_block):
    n = lax.axis_size("rows")
    chips = n // CORES
    bits = chips.bit_length() - 1
    ybits = [1 + b for b in range(bits // 2)]
    zbits = [1 + b for b in range(bits // 2, bits)]
    orders = (ybits + zbits, zbits[:1] + ybits + zbits[1:])
    me = lax.axis_index("rows")
    core = me & 1

    examples, nblocks, width = train.shape
    nq = queries.shape[0]

    def swap(value, step):
        return lax.ppermute(value, "rows", [(r, r ^ step) for r in range(n)])

    def swap_level(value, step):
        return lax.ppermute(value, "rows", [(r, r ^ (1 << orders[r & 1][step])) for r in range(n)])

    def side(step):
        return jnp.where(core == 0, (me >> orders[0][step]) & 1, (me >> orders[1][step]) & 1)

    def pack(value):
        return (value * UNIT).astype(jnp.float16)

    def unpack(value):
        return value.astype(jnp.float32) * (1.0 / UNIT)

    def part(value, index):
        rows = value.shape[0] // 2
        return lax.dynamic_slice_in_dim(value, index * rows, rows)

    def join(own, got, index):
        rows = own.shape[0]
        full = jnp.zeros((2 * rows,) + own.shape[1:], own.dtype)
        full = lax.dynamic_update_slice_in_dim(full, own, index * rows, 0)
        return lax.dynamic_update_slice_in_dim(full, got, (1 - index) * rows, 0)

    def after(value, first):
        return lax.optimization_barrier((value, first))[0]

    def message(value, step):
        return pack(part(value, 1 - side(step)))

    def exchange(value, sent, step):
        return part(value, side(step)) + unpack(swap_level(sent, step))

    def total(value, sent):
        return (value + unpack(swap_level(sent, bits - 1))).astype(jnp.bfloat16)

    def gather(value, step):
        return join(value, swap_level(value, step), side(step))

    sent = [pack(value) for value in product(1 - core, queries, precond, OTHER_VMEM)]
    got = [swap(value, 1) for value in sent]
    mine = product(core, after(queries, sent[0]), precond, MINE_VMEM)
    one, two = [value + unpack(other) for value, other in zip(mine, got)]

    steps = bits - 1
    sent = message(one, 0)
    train = after(train, sent)
    other_train = swap(train, 1)
    one = exchange(one, sent, 0)
    two = exchange(two, after(message(two, 0), one), 0)
    for step in range(1, steps):
        one = exchange(one, message(one, step), step)
        two = exchange(two, message(two, step), step)
    one = total(one, pack(one))
    sent = pack(two)
    one = after(one, sent)
    two = total(two, sent)
    for step in reversed(range(steps)):
        one = gather(one, step)
        if step:
            two = after(two, one)
        two = gather(two, step)

    both = jnp.concatenate([train, other_train], axis=0).reshape(CORES * examples * nblocks, width)
    raws = [
        lax.dot_general(both, value, (((1,), (1,)), ((), ())), preferred_element_type=jnp.float32)
        for value in (one, two)
    ]
    owned = nblocks // n
    order = jnp.take(slot_block.reshape(n, owned), me ^ jnp.arange(n), axis=0, mode="clip").reshape(nblocks)
    parts = pieces(raws, order, n)
    got = [None] * n
    got[0] = parts[0]
    for k in reversed(range(1, n)):
        got[k] = swap(parts[k], k)

    allowed = listed_mask(query_cluster, cand_blocks, cand_count, nblocks)
    slots = lax.dynamic_slice_in_dim(slot_block, me * owned, owned)
    own_allowed = jnp.take(allowed, slots, axis=0, mode="clip")
    return finish(me, own_allowed, got)


def solution(mesh):
    placed = (
        P("groups", "rows"),
        P("rows", None),
        P("rows", "groups", None),
        P("groups"),
        P("groups", None),
        P("groups"),
        P("groups"),
    )
    return jax.shard_map(
        shards,
        mesh=mesh,
        in_specs=placed,
        out_specs=P(None, ("groups", "rows"), None),
        check_vma=False,
    )
```

time: 107 us -> 109 us (1.019)
  starting transfers between devices: 17.2 us -> 43.8 us
  waiting for transfers between devices: 65.7 us -> 41.6 us
  matrix products: 15.7 us -> 2.78 us
  Pallas kernels: 0 us -> 9.35 us
  other arithmetic: 1.5 us -> 4.96 us
    ppermute x13 -> x28, starting transfers between devices: 13.6 us -> 43.8 us  [the longest x10 22.3 us: swap_level(): lax.ppermute(value, 'rows', [(r, r ^ 1 << orders[r & 1][step]) for r in r...]
    ppermute x13 -> x28, waiting for transfers between devices: 57.5 us -> 41.6 us  [the longest x10 38.4 us: swap_level(): lax.ppermute(value, 'rows', [(r, r ^ 1 << orders[r & 1][step]) for r in r...]
    dot_general x5 -> x2, matrix products: 15.4 us -> 2.52 us  [shards(): lax.dot_general(both, value, (((1,), (1,)), ((), ())), preferred_element_...]
    pallas_call x0 -> x4, Pallas kernels: none -> 9.35 us  [the longest x2 7.67 us: product(): pl.pallas_call(product_kernel, in_specs=[pl.BlockSpec(memory_space=pltpu....]
    all_to_all x1 -> x0, waiting for transfers between devices: 8.23 us -> none  [shards(): lax.all_to_all(ordered, 'rows', split_axis=0, concat_axis=0, tiled=True)]
    all_to_all x1 -> x0, starting transfers between devices: 3.53 us -> none  [shards(): lax.all_to_all(ordered, 'rows', split_axis=0, concat_axis=0, tiled=True)]
    unnamed x15 -> x17, local copies, waits for them, and re-layouts: 1.16 us -> 3.34 us
    add x4, other arithmetic: 0.41 us -> 2.38 us  [the longest x2 2.06 us: shards(): one, two = [value + unpack(other) for value, other in zip(mine, got)]]
  transfers between devices with their start and end apart: 14 -> 28, of which waited for: 10 -> 9; matrix products, arithmetic and copies ran while one was open for 13% -> 7% of each run, Pallas kernels for 0% -> 3%
where the time goes in v5:
time: 109 us
  starting transfers between devices  43.8 us (40%)
  waiting for transfers between devices  41.6 us (38%)
  Pallas kernels  9.35 us (9%)
  local copies, waits for them, and re-layouts  5.76 us (5%)
  other arithmetic  4.96 us (5%)
  matrix products  2.78 us (3%)
    ppermute x10, waiting for transfers between devices, swap_level(): lax.ppermute(value, 'rows', [(r, r ^ 1 << orders[r & 1][step]) for r in r...  38.4 us
    ppermute x10, starting transfers between devices, swap_level(): lax.ppermute(value, 'rows', [(r, r ^ 1 << orders[r & 1][step]) for r in r...  22.3 us
    ppermute x18, starting transfers between devices, swap(): return lax.ppermute(value, 'rows', [(r, r ^ step) for r in range(n)])  21.4 us
    pallas_call x2, Pallas kernels, product(): pl.pallas_call(product_kernel, in_specs=[pl.BlockSpec(memory_space=pltpu....  7.67 us
    unnamed x17, local copies, waits for them, and re-layouts  3.34 us
    ppermute x18, waiting for transfers between devices, swap(): return lax.ppermute(value, 'rows', [(r, r ^ step) for r in range(n)])  3.19 us
    dot_general x2, matrix products, shards(): lax.dot_general(both, value, (((1,), (1,)), ((), ())), preferred_element_...  2.52 us
  transfers between devices with their start and end apart: 28, of which 9 were waited for; matrix products, arithmetic and copies ran while one was open for 7% of the time, Pallas kernels for 3%

profile of v5, /device:TPU:0, one launch (start us, length us, event | category | flops | bytes accessed | tf_op | source)
XLA Modules:
  0.0 108.6 jit_solution(14748712982125570301)
XLA Ops:
  0.0 1.0 copy-done.1
  1.0 4.1 %shard_map.73 = (f32[128,4096]{1,0:T(8,128)S(1)}, f32[128,4096]{1,0:T(8,128)S(1)}) custom-call(s32[1]{0:T(128)} %bitcast.5.core_ref, f32[512,256]{1,0:T(8,128)S(1)} %copy-done.1, f32[256,4096]{1,0:T(8,128)} %columns_hbm.3), custom_call_target="tpu_custom_call" | custom-call | flops 1610612736 | bytes 8388608 | tf_op jit(solution)/shard_map/pallas_call | solution.py:58
  5.2 1.2 %multiply_convert_fusion.1 = f16[128,4096]{1,0:T(8,128)(2,1)} fusion(f32[128,4096]{1,0:T(8,128)S(1)} %get-tuple-element.30), kind=kLoop, calls=%fused_computation.5 | loop fusion | flops 1048576 | bytes 3145728 | tf_op jit(solution)/shard_map/convert_element_type | solution.py:165
  6.4 0.5 collective-permute-start
  6.8 0.2 multiply_convert_fusion
  7.2 0.7 gather_fusion
  7.8 2.2 %copy-done = f32[256,4096]{1,0:T(8,128)S(1)} copy-done((f32[256,4096]{1,0:T(8,128)S(1)}, f32[256,4096]{1,0:T(8,128)}, u32[]{:S(2)}) %copy-start) | copy-done | bytes 4194328
  10.0 3.5 %shard_map.74 = (f32[128,4096]{1,0:T(8,128)S(1)}, f32[128,4096]{1,0:T(8,128)S(1)}) custom-call(s32[1]{0:T(128)} %bitcast.4.core_ref, f32[512,256]{1,0:T(8,128)S(1)} %copy-done.2, f32[256,4096]{1,0:T(8,128)S(1)} %copy-done), custom_call_target="tpu_custom_call" | custom-call | flops 1610612736 | bytes 8388608 | tf_op jit(solution)/shard_map/pallas_call | solution.py:58
  13.6 1.7 %multiply_add_fusion.1 = f32[128,4096]{1,0:T(8,128)S(1)} fusion(f32[128,4096]{1,0:T(8,128)S(1)} %get-tuple-element.32, f16[128,4096]{1,0:T(8,128)(2,1)} %collective-permute-done), kind=kLoop, calls=%fused_computation.4 | loop fusion | flops 1572864 | bytes 5242880 | tf_op jit(solution)/shard_map/add | solution.py:198
  15.4 3.0 %collective-permute-start.2 = (f16[64,4096]{1,0:T(8,128)(2,1)S(1)}, f16[64,4096]{1,0:T(8,128)(2,1)S(1)}, u32[]{:S(2)}, u32[]{:S(2)}) collective-permute-start(f16[64,4096]{1,0:T(8,128)(2,1)S(1)} %multiply_convert_fusion.3), channel_id=1, source_target_pairs={{0,2},{1,5},{2,0},{3,7},{4,6},{5,1},{6,4},{7,3},{8,10},{9,13},{10,... | collective-permute-start | bytes 1572872 | tf_op jit(solution)/shard_map/ppermute | solution.py:159
  18.5 0.3 multiply_add_fusion
  18.8 6.8 %collective-permute-done.2 = f16[64,4096]{1,0:T(8,128)(2,1)S(1)} collective-permute-done((f16[64,4096]{1,0:T(8,128)(2,1)S(1)}, f16[64,4096]{1,0:T(8,128)(2,1)S(1)}, u32[]{:S(2)}, u32[]{:S(2)}) %collective-permute-start.2) | collective-permute-done | bytes 524320 | tf_op jit(solution)/shard_map/ppermute | solution.py:159
  25.9 2.1 %collective-permute-start.3 = (f16[32,4096]{1,0:T(8,128)(2,1)S(1)}, f16[32,4096]{1,0:T(8,128)(2,1)S(1)}, u32[]{:S(2)}, u32[]{:S(2)}) collective-permute-start(f16[32,4096]{1,0:T(8,128)(2,1)S(1)} %multiply_convert_fusion.7), channel_id=1, source_target_pairs={{0,4},{1,3},{2,6},{3,1},{4,0},{5,7},{6,2},{7,5},{8,12},{9,11},{10,... | collective-permute-start | bytes 786440 | tf_op jit(solution)/shard_map/ppermute | solution.py:159
  28.1 1.6 %collective-permute-start.6 = (f16[64,4096]{1,0:T(8,128)(2,1)S(1)}, f16[64,4096]{1,0:T(8,128)(2,1)S(1)}, u32[]{:S(2)}, u32[]{:S(2)}) collective-permute-start(f16[64,4096]{1,0:T(8,128)(2,1)S(1)} %multiply_convert_fusion.2), channel_id=1, source_target_pairs={{0,2},{1,5},{2,0},{3,7},{4,6},{5,1},{6,4},{7,3},{8,10},{9,13},{10,... | collective-permute-start | bytes 1572872 | tf_op jit(solution)/shard_map/ppermute | solution.py:159
  29.7 8.2 %collective-permute-done.3 = f16[32,4096]{1,0:T(8,128)(2,1)S(1)} collective-permute-done((f16[32,4096]{1,0:T(8,128)(2,1)S(1)}, f16[32,4096]{1,0:T(8,128)(2,1)S(1)}, u32[]{:S(2)}, u32[]{:S(2)}) %collective-permute-start.3) | collective-permute-done | bytes 262176 | tf_op jit(solution)/shard_map/ppermute | solution.py:159
  38.0 0.3 collective-permute-start.4
  38.5 4.3 %collective-permute-start.7 = (f16[32,4096]{1,0:T(8,128)(2,1)S(1)}, f16[32,4096]{1,0:T(8,128)(2,1)S(1)}, u32[]{:S(2)}, u32[]{:S(2)}) collective-permute-start(f16[32,4096]{1,0:T(8,128)(2,1)S(1)} %multiply_convert_fusion.5), channel_id=1, source_target_pairs={{0,4},{1,3},{2,6},{3,1},{4,0},{5,7},{6,2},{7,5},{8,12},{9,11},{10,... | collective-permute-start | bytes 786440 | tf_op jit(solution)/shard_map/ppermute | solution.py:159
  42.8 5.7 %collective-permute-done.4 = f16[32,4096]{1,0:T(8,128)(2,1)S(1)} collective-permute-done((f16[32,4096]{1,0:T(8,128)(2,1)S(1)}, f16[32,4096]{1,0:T(8,128)(2,1)S(1)}, u32[]{:S(2)}, u32[]{:S(2)}) %collective-permute-start.4) | collective-permute-done | bytes 262176 | tf_op jit(solution)/shard_map/ppermute | solution.py:159
  48.7 0.5 collective-permute-done.7
  49.3 0.6 collective-permute-start.10
  49.9 2.4 %collective-permute-start.8 = (bf16[32,4096]{1,0:T(8,128)(2,1)S(1)}, bf16[32,4096]{1,0:T(8,128)(2,1)S(1)}, u32[]{:S(2)}, u32[]{:S(2)}) collective-permute-start(bf16[32,4096]{1,0:T(8,128)(2,1)S(1)} %add_convert_fusion.1), channel_id=1, source_target_pairs={{0,4},{1,3},{2,6},{3,1},{4,0},{5,7},{6,2},{7,5},{8,12},{9,11},{10,... | collective-permute-start | bytes 786440 | tf_op jit(solution)/shard_map/ppermute | solution.py:159
  52.4 5.6 %collective-permute-done.8 = bf16[32,4096]{1,0:T(8,128)(2,1)S(1)} collective-permute-done((bf16[32,4096]{1,0:T(8,128)(2,1)S(1)}, bf16[32,4096]{1,0:T(8,128)(2,1)S(1)}, u32[]{:S(2)}, u32[]{:S(2)}) %collective-permute-start.8) | collective-permute-done | bytes 262176 | tf_op jit(solution)/shard_map/ppermute | solution.py:159
  58.0 5.8 %collective-permute-start.9 = (bf16[64,4096]{1,0:T(8,128)(2,1)S(1)}, bf16[64,4096]{1,0:T(8,128)(2,1)S(1)}, u32[]{:S(2)}, u32[]{:S(2)}) collective-permute-start(bf16[64,4096]{1,0:T(8,128)(2,1)S(1)} %constant_dynamic-update-slice_fusion.6), channel_id=1, source_target_pairs={{0,2},{1,5},{2,0},{3,7},{4,6},{5,1},{6,4},{7,3},{8,10},{9,13},{10,... | collective-permute-start | bytes 1572872 | tf_op jit(solution)/shard_map/ppermute | solution.py:159
  64.2 6.2 %collective-permute-done.11 = bf16[32,4096]{1,0:T(8,128)(2,1)S(1)} collective-permute-done((bf16[32,4096]{1,0:T(8,128)(2,1)S(1)}, bf16[32,4096]{1,0:T(8,128)(2,1)S(1)}, u32[]{:S(2)}, u32[]{:S(2)}) %collective-permute-start.11) | collective-permute-done | bytes 262176 | tf_op jit(solution)/shard_map/ppermute | solution.py:159
  70.5 2.1 %collective-permute-start.12 = (bf16[64,4096]{1,0:T(8,128)(2,1)S(1)}, bf16[64,4096]{1,0:T(8,128)(2,1)S(1)}, u32[]{:S(2)}, u32[]{:S(2)}) collective-permute-start(bf16[64,4096]{1,0:T(8,128)(2,1)S(1)} %constant_dynamic-update-slice_fusion.2), channel_id=1, source_target_pairs={{0,2},{1,5},{2,0},{3,7},{4,6},{5,1},{6,4},{7,3},{8,10},{9,13},{10,... | collective-permute-start | bytes 1572872 | tf_op jit(solution)/shard_map/ppermute | solution.py:159
  72.8 0.4 pad_maximum_fusion
  73.2 1.3 %fusion.5.refs_0_ = f32[512,128]{1,0:T(8,128)S(1)} fusion(bf16[512,4096]{1,0:T(8,128)(2,1)S(1)} %bitcast.14, bf16[128,4096]{1,0:T(8,128)(2,1)S(1)} %constant_dynamic-update-slice_fusion.4), kind=kOutput, calls=%fused_computation.37 | convolution fusion | flops 536870912 | bytes 5505024 | tf_op jit(solution)/shard_map/dot_general | solution.py:221
  74.5 5.3 %collective-permute-done.12 = bf16[64,4096]{1,0:T(8,128)(2,1)S(1)} collective-permute-done((bf16[64,4096]{1,0:T(8,128)(2,1)S(1)}, bf16[64,4096]{1,0:T(8,128)(2,1)S(1)}, u32[]{:S(2)}, u32[]{:S(2)}) %collective-permute-start.12) | collective-permute-done | bytes 524320 | tf_op jit(solution)/shard_map/ppermute | solution.py:159
  79.8 1.3 %fusion.6.refs_1_ = f32[512,128]{1,0:T(8,128)S(1)} fusion(bf16[512,4096]{1,0:T(8,128)(2,1)S(1)} %bitcast.15, bf16[128,4096]{1,0:T(8,128)(2,1)S(1)} %constant_dynamic-update-slice_fusion), kind=kOutput, calls=%fused_computation.38 | convolution fusion | flops 536870912 | bytes 5505024 | tf_op jit(solution)/shard_map/dot_general | solution.py:221
  81.2 0.8 shard_map.75
  82.1 2.1 %collective-permute-start.14 = (bf16[1,32,256]{2,1,0:T(8,128)(2,1)S(1)}, bf16[1,32,256]{2,1,0:T(8,128)(2,1)S(1)}, u32[]{:S(2)}, u32[]{:S(2)}) collective-permute-start(bf16[1,32,256]{2,1,0:T(8,128)(2,1)S(1)} %get-tuple-element.41), channel_id=1, source_target_pairs={{0,2},{1,3},{2,0},{3,1},{4,6},{5,7},{6,4},{7,5},{8,10},{9,11},{10,... | collective-permute-start | bytes 49160 | tf_op jit(solution)/shard_map/ppermute | solution.py:156
  84.2 1.5 %collective-permute-start.17 = (bf16[1,32,256]{2,1,0:T(8,128)(2,1)S(1)}, bf16[1,32,256]{2,1,0:T(8,128)(2,1)S(1)}, u32[]{:S(2)}, u32[]{:S(2)}) collective-permute-start(bf16[1,32,256]{2,1,0:T(8,128)(2,1)S(1)} %get-tuple-element.44), channel_id=1, source_target_pairs={{0,5},{1,4},{2,7},{3,6},{4,1},{5,0},{6,3},{7,2},{8,13},{9,12},{10,... | collective-permute-start | bytes 49160 | tf_op jit(solution)/shard_map/ppermute | solution.py:156
  85.8 1.8 %collective-permute-start.18 = (bf16[1,32,256]{2,1,0:T(8,128)(2,1)S(1)}, bf16[1,32,256]{2,1,0:T(8,128)(2,1)S(1)}, u32[]{:S(2)}, u32[]{:S(2)}) collective-permute-start(bf16[1,32,256]{2,1,0:T(8,128)(2,1)S(1)} %get-tuple-element.45), channel_id=1, source_target_pairs={{0,6},{1,7},{2,4},{3,5},{4,2},{5,3},{6,0},{7,1},{8,14},{9,15},{10,... | collective-permute-start | bytes 49160 | tf_op jit(solution)/shard_map/ppermute | solution.py:156
  87.6 1.2 %collective-permute-start.19 = (bf16[1,32,256]{2,1,0:T(8,128)(2,1)S(1)}, bf16[1,32,256]{2,1,0:T(8,128)(2,1)S(1)}, u32[]{:S(2)}, u32[]{:S(2)}) collective-permute-start(bf16[1,32,256]{2,1,0:T(8,128)(2,1)S(1)} %get-tuple-element.46), channel_id=1, source_target_pairs={{0,7},{1,6},{2,5},{3,4},{4,3},{5,2},{6,1},{7,0},{8,15},{9,14},{10,... | collective-permute-start | bytes 49160 | tf_op jit(solution)/shard_map/ppermute | solution.py:156
  88.8 1.4 %collective-permute-start.20 = (bf16[1,32,256]{2,1,0:T(8,128)(2,1)S(1)}, bf16[1,32,256]{2,1,0:T(8,128)(2,1)S(1)}, u32[]{:S(2)}, u32[]{:S(2)}) collective-permute-start(bf16[1,32,256]{2,1,0:T(8,128)(2,1)S(1)} %get-tuple-element.47), channel_id=1, source_target_pairs={{0,8},{1,9},{2,10},{3,11},{4,12},{5,13},{6,14},{7,15},{8,0},{9,1},... | collective-permute-start | bytes 49160 | tf_op jit(solution)/shard_map/ppermute | solution.py:156
  90.2 1.0 collective-permute-start.21
  91.2 1.8 %collective-permute-start.22 = (bf16[1,32,256]{2,1,0:T(8,128)(2,1)S(1)}, bf16[1,32,256]{2,1,0:T(8,128)(2,1)S(1)}, u32[]{:S(2)}, u32[]{:S(2)}) collective-permute-start(bf16[1,32,256]{2,1,0:T(8,128)(2,1)S(1)} %get-tuple-element.49), channel_id=1, source_target_pairs={{0,10},{1,11},{2,8},{3,9},{4,14},{5,15},{6,12},{7,13},{8,2},{9,3},... | collective-permute-start | bytes 49160 | tf_op jit(solution)/shard_map/ppermute | solution.py:156
  93.0 0.3 fusion
  93.3 0.6 dynamic_slice.27
  93.8 2.0 %collective-permute-start.23 = (bf16[1,32,256]{2,1,0:T(8,128)(2,1)S(1)}, bf16[1,32,256]{2,1,0:T(8,128)(2,1)S(1)}, u32[]{:S(2)}, u32[]{:S(2)}) collective-permute-start(bf16[1,32,256]{2,1,0:T(8,128)(2,1)S(1)} %get-tuple-element.50), channel_id=1, source_target_pairs={{0,11},{1,10},{2,9},{3,8},{4,15},{5,14},{6,13},{7,12},{8,3},{9,2},... | collective-permute-start | bytes 49160 | tf_op jit(solution)/shard_map/ppermute | solution.py:156
  95.9 2.8 %collective-permute-start.24 = (bf16[1,32,256]{2,1,0:T(8,128)(2,1)S(1)}, bf16[1,32,256]{2,1,0:T(8,128)(2,1)S(1)}, u32[]{:S(2)}, u32[]{:S(2)}) collective-permute-start(bf16[1,32,256]{2,1,0:T(8,128)(2,1)S(1)} %get-tuple-element.51), channel_id=1, source_target_pairs={{0,12},{1,13},{2,14},{3,15},{4,8},{5,9},{6,10},{7,11},{8,4},{9,5},... | collective-permute-start | bytes 49160 | tf_op jit(solution)/shard_map/ppermute | solution.py:156
  98.7 0.5 collective-permute-start.25
  99.2 2.7 %collective-permute-start.26 = (bf16[1,32,256]{2,1,0:T(8,128)(2,1)S(1)}, bf16[1,32,256]{2,1,0:T(8,128)(2,1)S(1)}, u32[]{:S(2)}, u32[]{:S(2)}) collective-permute-start(bf16[1,32,256]{2,1,0:T(8,128)(2,1)S(1)} %get-tuple-element.53), channel_id=1, source_target_pairs={{0,14},{1,15},{2,12},{3,13},{4,10},{5,11},{6,8},{7,9},{8,6},{9,7},... | collective-permute-start | bytes 49160 | tf_op jit(solution)/shard_map/ppermute | solution.py:156
  101.8 2.0 %collective-permute-start.27 = (bf16[1,32,256]{2,1,0:T(8,128)(2,1)S(1)}, bf16[1,32,256]{2,1,0:T(8,128)(2,1)S(1)}, u32[]{:S(2)}, u32[]{:S(2)}) collective-permute-start(bf16[1,32,256]{2,1,0:T(8,128)(2,1)S(1)} %get-tuple-element.54), channel_id=1, source_target_pairs={{0,15},{1,14},{2,13},{3,12},{4,11},{5,10},{6,9},{7,8},{8,7},{9,6},... | collective-permute-start | bytes 49160 | tf_op jit(solution)/shard_map/ppermute | solution.py:156
  103.9 0.7 constant_dynamic-slice_fusion
  104.6 1.1 collective-permute-done.26.refs_14_
  105.6 2.1 %collective-permute-done.27.refs_15_ = bf16[1,32,256]{2,1,0:T(8,128)(2,1)S(1)} collective-permute-done((bf16[1,32,256]{2,1,0:T(8,128)(2,1)S(1)}, bf16[1,32,256]{2,1,0:T(8,128)(2,1)S(1)}, u32[]{:S(2)}, u32[]{:S(2)}) %collective-permute-start.27) | collective-permute-done | bytes 16416 | tf_op jit(solution)/shard_map/ppermute | solution.py:156
  107.7 0.9 shard_map.76
  (66 shorter events, 2.2 us)
Async XLA Ops:
  0.0 1.0 copy-start.1
  6.4 0.8 copy-start.3
  6.4 1.5 %copy-start.2 = (f32[512,256]{1,0:T(8,128)S(1)}, f32[512,256]{1,0:T(8,128)}, u32[]{:S(2)}) copy-start(f32[512,256]{1,0:T(8,128)} %rows_ref.2) | copy-start | bytes 1572868
  6.4 7.2 %collective-permute-start = (f16[128,4096]{1,0:T(8,128)(2,1)}, f16[128,4096]{1,0:T(8,128)(2,1)}, u32[]{:S(2)}, u32[]{:S(2)}) collective-permute-start(f16[128,4096]{1,0:T(8,128)(2,1)} %multiply_convert_fusion.1), channel_id=1, source_target_pairs={{0,1},{1,0},{2,3},{3,2},{4,5},{5,4},{6,7},{7,6},{8,9},{9,8},{10,11... | collective-permute-start | bytes 3145736 | tf_op jit(solution)/shard_map/ppermute | solution.py:156
  7.0 11.5 %collective-permute-start.5 = (f16[128,4096]{1,0:T(8,128)(2,1)S(1)}, f16[128,4096]{1,0:T(8,128)(2,1)S(1)}, u32[]{:S(2)}, u32[]{:S(2)}) collective-permute-start(f16[128,4096]{1,0:T(8,128)(2,1)S(1)} %multiply_convert_fusion), channel_id=1, source_target_pairs={{0,1},{1,0},{2,3},{3,2},{4,5},{5,4},{6,7},{7,6},{8,9},{9,8},{10,11... | collective-permute-start | bytes 3145736 | tf_op jit(solution)/shard_map/ppermute | solution.py:156
  7.8 2.2 %copy-start = (f32[256,4096]{1,0:T(8,128)S(1)}, f32[256,4096]{1,0:T(8,128)}, u32[]{:S(2)}) copy-start(f32[256,4096]{1,0:T(8,128)} %columns_hbm.3) | copy-start | bytes 12582916
  10.0 3.5 %copy-start.6 = (s32[8]{0:T(128)S(1)}, s32[8]{0:T(128)}, u32[]{:S(2)}) copy-start(s32[8]{0:T(128)} %param.12) | copy-start | bytes 100
  13.6 4.9 %copy-start.4 = (bf16[16,16,4096]{2,1,0:T(8,128)(2,1)S(1)}, bf16[16,16,4096]{2,1,0:T(8,128)(2,1)}, u32[]{:S(2)}) copy-start(bf16[16,16,4096]{2,1,0:T(8,128)(2,1)} %param.9) | copy-start | bytes 6291460
  15.4 10.2 %collective-permute-start.2 = (f16[64,4096]{1,0:T(8,128)(2,1)S(1)}, f16[64,4096]{1,0:T(8,128)(2,1)S(1)}, u32[]{:S(2)}, u32[]{:S(2)}) collective-permute-start(f16[64,4096]{1,0:T(8,128)(2,1)S(1)} %multiply_convert_fusion.3), channel_id=1, source_target_pairs={{0,2},{1,5},{2,0},{3,7},{4,6},{5,1},{6,4},{7,3},{8,10},{9,13},{10,... | collective-permute-start | bytes 1572872 | tf_op jit(solution)/shard_map/ppermute | solution.py:159
  18.5 54.3 %collective-permute-start.1 = (bf16[16,16,4096]{2,1,0:T(8,128)(2,1)S(1)}, bf16[16,16,4096]{2,1,0:T(8,128)(2,1)S(1)}, u32[]{:S(2)}, u32[]{:S(2)}) collective-permute-start(bf16[16,16,4096]{2,1,0:T(8,128)(2,1)S(1)} %copy-done.4), channel_id=1, source_target_pairs={{0,1},{1,0},{2,3},{3,2},{4,5},{5,4},{6,7},{7,6},{8,9},{9,8},{10,11... | collective-permute-start | bytes 6291464 | tf_op jit(solution)/shard_map/ppermute | solution.py:156
  25.9 12.1 %collective-permute-start.3 = (f16[32,4096]{1,0:T(8,128)(2,1)S(1)}, f16[32,4096]{1,0:T(8,128)(2,1)S(1)}, u32[]{:S(2)}, u32[]{:S(2)}) collective-permute-start(f16[32,4096]{1,0:T(8,128)(2,1)S(1)} %multiply_convert_fusion.7), channel_id=1, source_target_pairs={{0,4},{1,3},{2,6},{3,1},{4,0},{5,7},{6,2},{7,5},{8,12},{9,11},{10,... | collective-permute-start | bytes 786440 | tf_op jit(solution)/shard_map/ppermute | solution.py:159
  28.1 10.2 %collective-permute-start.6 = (f16[64,4096]{1,0:T(8,128)(2,1)S(1)}, f16[64,4096]{1,0:T(8,128)(2,1)S(1)}, u32[]{:S(2)}, u32[]{:S(2)}) collective-permute-start(f16[64,4096]{1,0:T(8,128)(2,1)S(1)} %multiply_convert_fusion.2), channel_id=1, source_target_pairs={{0,2},{1,5},{2,0},{3,7},{4,6},{5,1},{6,4},{7,3},{8,10},{9,13},{10,... | collective-permute-start | bytes 1572872 | tf_op jit(solution)/shard_map/ppermute | solution.py:159
  38.0 10.6 %collective-permute-start.4 = (f16[32,4096]{1,0:T(8,128)(2,1)S(1)}, f16[32,4096]{1,0:T(8,128)(2,1)S(1)}, u32[]{:S(2)}, u32[]{:S(2)}) collective-permute-start(f16[32,4096]{1,0:T(8,128)(2,1)S(1)} %multiply_convert_fusion.6), channel_id=1, source_target_pairs={{0,8},{1,9},{2,10},{3,11},{4,12},{5,13},{6,14},{7,15},{8,0},{9,1},... | collective-permute-start | bytes 786440 | tf_op jit(solution)/shard_map/ppermute | solution.py:159
  38.5 10.7 %collective-permute-start.7 = (f16[32,4096]{1,0:T(8,128)(2,1)S(1)}, f16[32,4096]{1,0:T(8,128)(2,1)S(1)}, u32[]{:S(2)}, u32[]{:S(2)}) collective-permute-start(f16[32,4096]{1,0:T(8,128)(2,1)S(1)} %multiply_convert_fusion.5), channel_id=1, source_target_pairs={{0,4},{1,3},{2,6},{3,1},{4,0},{5,7},{6,2},{7,5},{8,12},{9,11},{10,... | collective-permute-start | bytes 786440 | tf_op jit(solution)/shard_map/ppermute | solution.py:159
  49.3 14.4 %collective-permute-start.10 = (f16[32,4096]{1,0:T(8,128)(2,1)S(1)}, f16[32,4096]{1,0:T(8,128)(2,1)S(1)}, u32[]{:S(2)}, u32[]{:S(2)}) collective-permute-start(f16[32,4096]{1,0:T(8,128)(2,1)S(1)} %multiply_convert_fusion.4), channel_id=1, source_target_pairs={{0,8},{1,9},{2,10},{3,11},{4,12},{5,13},{6,14},{7,15},{8,0},{9,1},... | collective-permute-start | bytes 786440 | tf_op jit(solution)/shard_map/ppermute | solution.py:159
  49.9 8.1 %collective-permute-start.8 = (bf16[32,4096]{1,0:T(8,128)(2,1)S(1)}, bf16[32,4096]{1,0:T(8,128)(2,1)S(1)}, u32[]{:S(2)}, u32[]{:S(2)}) collective-permute-start(bf16[32,4096]{1,0:T(8,128)(2,1)S(1)} %add_convert_fusion.1), channel_id=1, source_target_pairs={{0,4},{1,3},{2,6},{3,1},{4,0},{5,7},{6,2},{7,5},{8,12},{9,11},{10,... | collective-permute-start | bytes 786440 | tf_op jit(solution)/shard_map/ppermute | solution.py:159
  58.0 15.1 %collective-permute-start.9 = (bf16[64,4096]{1,0:T(8,128)(2,1)S(1)}, bf16[64,4096]{1,0:T(8,128)(2,1)S(1)}, u32[]{:S(2)}, u32[]{:S(2)}) collective-permute-start(bf16[64,4096]{1,0:T(8,128)(2,1)S(1)} %constant_dynamic-update-slice_fusion.6), channel_id=1, source_target_pairs={{0,2},{1,5},{2,0},{3,7},{4,6},{5,1},{6,4},{7,3},{8,10},{9,13},{10,... | collective-permute-start | bytes 1572872 | tf_op jit(solution)/shard_map/ppermute | solution.py:159
  63.9 6.5 %collective-permute-start.11 = (bf16[32,4096]{1,0:T(8,128)(2,1)S(1)}, bf16[32,4096]{1,0:T(8,128)(2,1)S(1)}, u32[]{:S(2)}, u32[]{:S(2)}) collective-permute-start(bf16[32,4096]{1,0:T(8,128)(2,1)S(1)} %add_convert_fusion), channel_id=1, source_target_pairs={{0,4},{1,3},{2,6},{3,1},{4,0},{5,7},{6,2},{7,5},{8,12},{9,11},{10,... | collective-permute-start | bytes 786440 | tf_op jit(solution)/shard_map/ppermute | solution.py:159
  70.5 9.3 %collective-permute-start.12 = (bf16[64,4096]{1,0:T(8,128)(2,1)S(1)}, bf16[64,4096]{1,0:T(8,128)(2,1)S(1)}, u32[]{:S(2)}, u32[]{:S(2)}) collective-permute-start(bf16[64,4096]{1,0:T(8,128)(2,1)S(1)} %constant_dynamic-update-slice_fusion.2), channel_id=1, source_target_pairs={{0,2},{1,5},{2,0},{3,7},{4,6},{5,1},{6,4},{7,3},{8,10},{9,13},{10,... | collective-permute-start | bytes 1572872 | tf_op jit(solution)/shard_map/ppermute | solution.py:159
  79.8 1.3 %copy-start.5 = (s32[8,12]{1,0:T(8,128)S(1)}, s32[8,12]{1,0:T(8,128)}, u32[]{:S(2)}) copy-start(s32[8,12]{1,0:T(8,128)} %param.11) | copy-start | bytes 1156
  79.8 13.2 %copy-start.7 = (s32[512]{0:T(512)S(1)}, s32[512]{0:T(512)}, u32[]{:S(2)}) copy-start(s32[512]{0:T(512)} %param.10) | copy-start | bytes 6148
  82.0 3.8 %collective-permute-start.13 = (bf16[1,32,256]{2,1,0:T(8,128)(2,1)S(1)}, bf16[1,32,256]{2,1,0:T(8,128)(2,1)S(1)}, u32[]{:S(2)}, u32[]{:S(2)}) collective-permute-start(bf16[1,32,256]{2,1,0:T(8,128)(2,1)S(1)} %get-tuple-element.40), channel_id=1, source_target_pairs={{0,1},{1,0},{2,3},{3,2},{4,5},{5,4},{6,7},{7,6},{8,9},{9,8},{10,11... | collective-permute-start | bytes 49160 | tf_op jit(solution)/shard_map/ppermute | solution.py:156
  82.1 5.5 %collective-permute-start.14 = (bf16[1,32,256]{2,1,0:T(8,128)(2,1)S(1)}, bf16[1,32,256]{2,1,0:T(8,128)(2,1)S(1)}, u32[]{:S(2)}, u32[]{:S(2)}) collective-permute-start(bf16[1,32,256]{2,1,0:T(8,128)(2,1)S(1)} %get-tuple-element.41), channel_id=1, source_target_pairs={{0,2},{1,3},{2,0},{3,1},{4,6},{5,7},{6,4},{7,5},{8,10},{9,11},{10,... | collective-permute-start | bytes 49160 | tf_op jit(solution)/shard_map/ppermute | solution.py:156
  84.2 4.6 %collective-permute-start.15 = (bf16[1,32,256]{2,1,0:T(8,128)(2,1)S(1)}, bf16[1,32,256]{2,1,0:T(8,128)(2,1)S(1)}, u32[]{:S(2)}, u32[]{:S(2)}) collective-permute-start(bf16[1,32,256]{2,1,0:T(8,128)(2,1)S(1)} %get-tuple-element.42), channel_id=1, source_target_pairs={{0,3},{1,2},{2,1},{3,0},{4,7},{5,6},{6,5},{7,4},{8,11},{9,10},{10,... | collective-permute-start | bytes 49160 | tf_op jit(solution)/shard_map/ppermute | solution.py:156
  84.2 6.0 %collective-permute-start.16 = (bf16[1,32,256]{2,1,0:T(8,128)(2,1)S(1)}, bf16[1,32,256]{2,1,0:T(8,128)(2,1)S(1)}, u32[]{:S(2)}, u32[]{:S(2)}) collective-permute-start(bf16[1,32,256]{2,1,0:T(8,128)(2,1)S(1)} %get-tuple-element.43), channel_id=1, source_target_pairs={{0,4},{1,5},{2,6},{3,7},{4,0},{5,1},{6,2},{7,3},{8,12},{9,13},{10,... | collective-permute-start | bytes 49160 | tf_op jit(solution)/shard_map/ppermute | solution.py:156
  84.2 7.0 %collective-permute-start.17 = (bf16[1,32,256]{2,1,0:T(8,128)(2,1)S(1)}, bf16[1,32,256]{2,1,0:T(8,128)(2,1)S(1)}, u32[]{:S(2)}, u32[]{:S(2)}) collective-permute-start(bf16[1,32,256]{2,1,0:T(8,128)(2,1)S(1)} %get-tuple-element.44), channel_id=1, source_target_pairs={{0,5},{1,4},{2,7},{3,6},{4,1},{5,0},{6,3},{7,2},{8,13},{9,12},{10,... | collective-permute-start | bytes 49160 | tf_op jit(solution)/shard_map/ppermute | solution.py:156
  85.8 8.0 %collective-permute-start.18 = (bf16[1,32,256]{2,1,0:T(8,128)(2,1)S(1)}, bf16[1,32,256]{2,1,0:T(8,128)(2,1)S(1)}, u32[]{:S(2)}, u32[]{:S(2)}) collective-permute-start(bf16[1,32,256]{2,1,0:T(8,128)(2,1)S(1)} %get-tuple-element.45), channel_id=1, source_target_pairs={{0,6},{1,7},{2,4},{3,5},{4,2},{5,3},{6,0},{7,1},{8,14},{9,15},{10,... | collective-permute-start | bytes 49160 | tf_op jit(solution)/shard_map/ppermute | solution.py:156
  87.6 8.2 %collective-permute-start.19 = (bf16[1,32,256]{2,1,0:T(8,128)(2,1)S(1)}, bf16[1,32,256]{2,1,0:T(8,128)(2,1)S(1)}, u32[]{:S(2)}, u32[]{:S(2)}) collective-permute-start(bf16[1,32,256]{2,1,0:T(8,128)(2,1)S(1)} %get-tuple-element.46), channel_id=1, source_target_pairs={{0,7},{1,6},{2,5},{3,4},{4,3},{5,2},{6,1},{7,0},{8,15},{9,14},{10,... | collective-permute-start | bytes 49160 | tf_op jit(solution)/shard_map/ppermute | solution.py:156
  88.8 9.9 %collective-permute-start.20 = (bf16[1,32,256]{2,1,0:T(8,128)(2,1)S(1)}, bf16[1,32,256]{2,1,0:T(8,128)(2,1)S(1)}, u32[]{:S(2)}, u32[]{:S(2)}) collective-permute-start(bf16[1,32,256]{2,1,0:T(8,128)(2,1)S(1)} %get-tuple-element.47), channel_id=1, source_target_pairs={{0,8},{1,9},{2,10},{3,11},{4,12},{5,13},{6,14},{7,15},{8,0},{9,1},... | collective-permute-start | bytes 49160 | tf_op jit(solution)/shard_map/ppermute | solution.py:156
  90.2 9.0 %collective-permute-start.21 = (bf16[1,32,256]{2,1,0:T(8,128)(2,1)S(1)}, bf16[1,32,256]{2,1,0:T(8,128)(2,1)S(1)}, u32[]{:S(2)}, u32[]{:S(2)}) collective-permute-start(bf16[1,32,256]{2,1,0:T(8,128)(2,1)S(1)} %get-tuple-element.48), channel_id=1, source_target_pairs={{0,9},{1,8},{2,11},{3,10},{4,13},{5,12},{6,15},{7,14},{8,1},{9,0},... | collective-permute-start | bytes 49160 | tf_op jit(solution)/shard_map/ppermute | solution.py:156
  91.2 10.6 %collective-permute-start.22 = (bf16[1,32,256]{2,1,0:T(8,128)(2,1)S(1)}, bf16[1,32,256]{2,1,0:T(8,128)(2,1)S(1)}, u32[]{:S(2)}, u32[]{:S(2)}) collective-permute-start(bf16[1,32,256]{2,1,0:T(8,128)(2,1)S(1)} %get-tuple-element.49), channel_id=1, source_target_pairs={{0,10},{1,11},{2,8},{3,9},{4,14},{5,15},{6,12},{7,13},{8,2},{9,3},... | collective-permute-start | bytes 49160 | tf_op jit(solution)/shard_map/ppermute | solution.py:156
  93.8 10.7 %collective-permute-start.23 = (bf16[1,32,256]{2,1,0:T(8,128)(2,1)S(1)}, bf16[1,32,256]{2,1,0:T(8,128)(2,1)S(1)}, u32[]{:S(2)}, u32[]{:S(2)}) collective-permute-start(bf16[1,32,256]{2,1,0:T(8,128)(2,1)S(1)} %get-tuple-element.50), channel_id=1, source_target_pairs={{0,11},{1,10},{2,9},{3,8},{4,15},{5,14},{6,13},{7,12},{8,3},{9,2},... | collective-permute-start | bytes 49160 | tf_op jit(solution)/shard_map/ppermute | solution.py:156
  95.9 8.7 %collective-permute-start.24 = (bf16[1,32,256]{2,1,0:T(8,128)(2,1)S(1)}, bf16[1,32,256]{2,1,0:T(8,128)(2,1)S(1)}, u32[]{:S(2)}, u32[]{:S(2)}) collective-permute-start(bf16[1,32,256]{2,1,0:T(8,128)(2,1)S(1)} %get-tuple-element.51), channel_id=1, source_target_pairs={{0,12},{1,13},{2,14},{3,15},{4,8},{5,9},{6,10},{7,11},{8,4},{9,5},... | collective-permute-start | bytes 49160 | tf_op jit(solution)/shard_map/ppermute | solution.py:156
  98.7 5.9 %collective-permute-start.25 = (bf16[1,32,256]{2,1,0:T(8,128)(2,1)S(1)}, bf16[1,32,256]{2,1,0:T(8,128)(2,1)S(1)}, u32[]{:S(2)}, u32[]{:S(2)}) collective-permute-start(bf16[1,32,256]{2,1,0:T(8,128)(2,1)S(1)} %get-tuple-element.52), channel_id=1, source_target_pairs={{0,13},{1,12},{2,15},{3,14},{4,9},{5,8},{6,11},{7,10},{8,5},{9,4},... | collective-permute-start | bytes 49160 | tf_op jit(solution)/shard_map/ppermute | solution.py:156
  99.2 6.4 %collective-permute-start.26 = (bf16[1,32,256]{2,1,0:T(8,128)(2,1)S(1)}, bf16[1,32,256]{2,1,0:T(8,128)(2,1)S(1)}, u32[]{:S(2)}, u32[]{:S(2)}) collective-permute-start(bf16[1,32,256]{2,1,0:T(8,128)(2,1)S(1)} %get-tuple-element.53), channel_id=1, source_target_pairs={{0,14},{1,15},{2,12},{3,13},{4,10},{5,11},{6,8},{7,9},{8,6},{9,7},... | collective-permute-start | bytes 49160 | tf_op jit(solution)/shard_map/ppermute | solution.py:156
  101.8 5.9 %collective-permute-start.27 = (bf16[1,32,256]{2,1,0:T(8,128)(2,1)S(1)}, bf16[1,32,256]{2,1,0:T(8,128)(2,1)S(1)}, u32[]{:S(2)}, u32[]{:S(2)}) collective-permute-start(bf16[1,32,256]{2,1,0:T(8,128)(2,1)S(1)} %get-tuple-element.54), channel_id=1, source_target_pairs={{0,15},{1,14},{2,13},{3,12},{4,11},{5,10},{6,9},{7,8},{8,7},{9,6},... | collective-permute-start | bytes 49160 | tf_op jit(solution)/shard_map/ppermute | solution.py:156

commit v6 on v5

v6 whole, which is shorter than its diff:
```python
import jax
import jax.numpy as jnp
from jax import lax
from jax.experimental import pallas as pl
from jax.experimental.pallas import tpu as pltpu
from jax.sharding import PartitionSpec as P

CORES = 2
CHUNKS = 2
PATHS = 2
UNIT = 4.0
LANES = 128
OTHER_VMEM = 48
MINE_VMEM = 47


def listed_mask(query_cluster, cand_blocks, cand_count, nblocks):
    nclusters = cand_blocks.shape[0]
    valid = jnp.arange(cand_blocks.shape[1])[None, :] < cand_count[:, None]
    hits = (cand_blocks[:, :, None] == jnp.arange(nblocks)[None, None, :]) & valid[:, :, None]
    listed = jnp.any(hits, axis=1).astype(jnp.float32)
    onehot = (query_cluster[:, None] == jnp.arange(nclusters)[None, :]).astype(jnp.float32)
    return jnp.dot(listed.T, onehot.T, preferred_element_type=jnp.float32)


def product_kernel(core_ref, rows_ref, columns_hbm, *refs):
    outs, (columns_ref, sems) = refs[:-2], refs[-2:]
    steps, _, block = columns_ref.shape

    def load(i):
        return pltpu.make_async_copy(
            columns_hbm.at[:, i * block:(i + 1) * block], columns_ref.at[i], sems.at[i]
        )

    for i in range(steps):
        load(i).start()
    half = rows_ref.shape[0] // CORES
    rows = rows_ref[pl.ds(pl.multiple_of(core_ref[0] * half, half), half), :]
    high = rows.astype(jnp.bfloat16)
    low = (rows - high.astype(jnp.float32)).astype(jnp.bfloat16)
    left = jnp.concatenate([high, low, high], axis=1)
    part = half // len(outs)
    for i in range(steps):
        load(i).wait()
        columns = columns_ref[i]
        high = columns.astype(jnp.bfloat16)
        low = (columns - high.astype(jnp.float32)).astype(jnp.bfloat16)
        right = jnp.concatenate([high, high, low], axis=0)
        result = jnp.dot(left, right, preferred_element_type=jnp.float32)
        for chunk, out_ref in enumerate(outs):
            out_ref[:, i * block:(i + 1) * block] = result[chunk * part:(chunk + 1) * part]


def product(core, rows, columns, vmem):
    nrows, depth = rows.shape
    width = columns.shape[1]
    block = min(512, width)
    part = nrows // CORES // CHUNKS
    return pl.pallas_call(
        product_kernel,
        in_specs=[
            pl.BlockSpec(memory_space=pltpu.SMEM),
            pl.BlockSpec(memory_space=pltpu.VMEM),
            pl.BlockSpec(memory_space=pltpu.HBM),
        ],
        out_specs=[pl.BlockSpec(memory_space=pltpu.VMEM)] * CHUNKS,
        out_shape=[jax.ShapeDtypeStruct((part, width), jnp.float32)] * CHUNKS,
        scratch_shapes=[
            pltpu.VMEM((width // block, depth, block), jnp.float32),
            pltpu.SemaphoreType.DMA((width // block,)),
        ],
        compiler_params=pltpu.CompilerParams(vmem_limit_bytes=vmem * 1024 * 1024),
        cost_estimate=pl.CostEstimate(
            flops=3 * nrows * depth * width,
            bytes_accessed=4 * width * depth + 2 * width * nrows,
            transcendentals=0,
        ),
    )(core.reshape(1), rows, columns)


def order_kernel(slots_ref, *refs):
    raws, out_ref = refs[:-1], refs[-1]
    nblocks, examples, _ = out_ref.shape
    for slot in range(nblocks):
        rows = pl.ds(slots_ref[slot], examples, stride=nblocks)
        for i, raw_ref in enumerate(raws):
            width = raw_ref.shape[1]
            out_ref[slot, :, i * width:(i + 1) * width] = raw_ref[rows, :].astype(out_ref.dtype)


def in_slot_order(raws, slots):
    nblocks = slots.shape[0]
    rows, width = raws[0].shape
    return pl.pallas_call(
        order_kernel,
        in_specs=[pl.BlockSpec(memory_space=pltpu.SMEM)] + [pl.BlockSpec(memory_space=pltpu.VMEM)] * CHUNKS,
        out_specs=pl.BlockSpec(memory_space=pltpu.VMEM),
        out_shape=jax.ShapeDtypeStruct((nblocks, rows // nblocks, CHUNKS * width), jnp.bfloat16),
        compiler_params=pltpu.CompilerParams(vmem_limit_bytes=4 * 1024 * 1024),
        cost_estimate=pl.CostEstimate(flops=rows * width, bytes_accessed=12 * rows * width, transcendentals=0),
    )(slots, *raws)


def finish_kernel(got_ref, allowed_ref, out_ref):
    chips, cores, owned, rows, half = got_ref.shape
    parts = half // LANES
    per_row = owned * cores * parts
    for chip in range(chips):
        for core in range(cores):
            for slot in range(owned):
                scores = got_ref[chip, core, slot].astype(jnp.float32)
                if core:
                    scores = jnp.concatenate([scores[rows // 2:], scores[:rows // 2]], axis=0)
                scores = scores * allowed_ref[slot:slot + 1, core * half:(core + 1) * half]
                for i in range(parts):
                    first = chip * rows * per_row + slot * cores * parts + core * parts + i
                    out_ref[pl.ds(first, rows, stride=per_row), :] = scores[:, i * LANES:(i + 1) * LANES]


def finish(got, allowed):
    chips, cores, owned, rows, half = got.shape
    flat = pl.pallas_call(
        finish_kernel,
        out_shape=jax.ShapeDtypeStruct((chips * rows * owned * cores * half // LANES, LANES), jnp.float32),
        compiler_params=pltpu.CompilerParams(vmem_limit_bytes=4 * 1024 * 1024),
        cost_estimate=pl.CostEstimate(flops=got.size, bytes_accessed=6 * got.size, transcendentals=0),
    )(got, allowed)
    return flat.reshape(chips * rows, owned, cores * half)


def shards(queries, precond, train, query_cluster, cand_blocks, cand_count, slot_block):
    n = lax.axis_size("rows")
    chips = n // CORES
    bits = chips.bit_length() - 1
    ybits = [1 + b for b in range(bits // 2)]
    zbits = [1 + b for b in range(bits // 2, bits)]
    orders = (ybits + zbits, zbits[:1] + ybits + zbits[1:])
    me = lax.axis_index("rows")
    core = me & 1

    examples, nblocks, width = train.shape
    nq = queries.shape[0]

    def swap(value, bit):
        return lax.ppermute(value, "rows", [(r, r ^ (1 << bit)) for r in range(n)])

    def side(bit):
        return (me >> bit) & 1

    def pack(value):
        return (value * UNIT).astype(jnp.float16)

    def unpack(value):
        return value.astype(jnp.float32) * (1.0 / UNIT)

    def part(value, index):
        rows = value.shape[0] // 2
        return lax.dynamic_slice_in_dim(value, index * rows, rows)

    def join(own, got, index):
        rows = own.shape[0]
        full = jnp.zeros((2 * rows,) + own.shape[1:], own.dtype)
        full = lax.dynamic_update_slice_in_dim(full, own, index * rows, 0)
        return lax.dynamic_update_slice_in_dim(full, got, (1 - index) * rows, 0)

    def after(value, first):
        return lax.optimization_barrier((value, first))[0]

    def messages(values, step):
        return [pack(part(value, 1 - side(order[step]))) for value, order in zip(values, orders)]

    def exchange(values, sent, step):
        got = [swap(message, order[step]) for message, order in zip(sent, orders)]
        return [
            part(value, side(order[step])) + unpack(message)
            for value, message, order in zip(values, got, orders)
        ]

    def gather(values, step):
        got = [swap(value, order[step]) for value, order in zip(values, orders)]
        return [join(value, message, side(order[step])) for value, message, order in zip(values, got, orders)]

    def whole(values):
        return pack(jnp.concatenate(values))

    def total(values, got):
        rows = values[0].shape[0]
        return [
            (value + unpack(got[i * rows:(i + 1) * rows])).astype(jnp.bfloat16)
            for i, value in enumerate(values)
        ]

    sent = [pack(value) for value in product(1 - core, queries, precond, OTHER_VMEM)]
    got = [swap(value, 0) for value in sent]
    mine = product(core, after(queries, sent[0]), precond, MINE_VMEM)
    rows = mine[0].shape[0] // PATHS

    def paths(value, other):
        value = value + unpack(other)
        return [value[i * rows:(i + 1) * rows] for i in range(PATHS)]

    steps = bits - 1
    last = orders[0][-1]
    one = paths(mine[0], got[0])
    sent = messages(one, 0)
    two = paths(mine[1], after(got[1], sent))
    one = exchange(one, sent, 0)
    for step in range(1, steps):
        one = exchange(one, messages(one, step), step)
    sent = whole(one)
    train, two = after((train, two), sent)
    got_one = swap(sent, last)
    for step in range(steps):
        two = exchange(two, messages(two, step), step)
    other_train = swap(train, 0)
    sent = whole(two)
    one = after(total(one, got_one), sent)
    two = total(two, swap(sent, last))
    both = jnp.concatenate([train, other_train], axis=0).reshape(CORES * examples * nblocks, width)
    two = after(two, both)
    for step in reversed(range(steps)):
        one = gather(one, step)
        if step:
            two = after(two, one)
        two = gather(two, step)

    raws = [
        lax.dot_general(
            both, jnp.concatenate(values), (((1,), (1,)), ((), ())), preferred_element_type=jnp.float32
        )
        for values in (one, two)
    ]
    owned = nblocks // n
    ordered = in_slot_order(raws, slot_block).reshape(n, owned, CORES * examples, nq // CORES)
    got = lax.all_to_all(ordered, "rows", split_axis=0, concat_axis=0, tiled=True)

    allowed = listed_mask(query_cluster, cand_blocks, cand_count, nblocks)
    slots = lax.dynamic_slice_in_dim(slot_block, me * owned, owned)
    own_allowed = jnp.take(allowed, slots, axis=0, mode="clip")
    return finish(got.reshape(chips, CORES, owned, CORES * examples, nq // CORES), own_allowed)


def solution(mesh):
    placed = (
        P("groups", "rows"),
        P("rows", None),
        P("rows", "groups", None),
        P("groups"),
        P("groups", None),
        P("groups"),
        P("groups"),
    )
    return jax.shard_map(
        shards,
        mesh=mesh,
        in_specs=placed,
        out_specs=P(None, ("groups", "rows"), None),
        check_vma=False,
    )
```

time: 109 us -> 105 us (0.963)
  starting transfers between devices: 43.8 us -> 32.6 us
  waiting for transfers between devices: 41.6 us -> 50.1 us
  local copies, waits for them, and re-layouts: 5.76 us -> 3.6 us
  Pallas kernels: 9.35 us -> 10.7 us
    ppermute x28 -> x21, starting transfers between devices: 43.8 us -> 26 us  [swap(): return lax.ppermute(value, 'rows', [(r, r ^ 1 << bit) for r in range(n)])]
    all_to_all x0 -> x1, waiting for transfers between devices: none -> 8.25 us  [shards(): lax.all_to_all(ordered, 'rows', split_axis=0, concat_axis=0, tiled=True)]
    all_to_all x0 -> x1, starting transfers between devices: none -> 6.59 us  [shards(): lax.all_to_all(ordered, 'rows', split_axis=0, concat_axis=0, tiled=True)]
    unnamed x17 -> x15, local copies, waits for them, and re-layouts: 3.34 us -> 1.42 us
    ppermute x28 -> x21, waiting for transfers between devices: 41.6 us -> 41.9 us  [swap(): return lax.ppermute(value, 'rows', [(r, r ^ 1 << bit) for r in range(n)])]
    add x4 -> x10, other arithmetic: 2.38 us -> 2.35 us  [the longest x2 1.89 us: paths(): value = value + unpack(other)]
  transfers between devices with their start and end apart: 28 -> 22, of which waited for: 9 -> 15; matrix products, arithmetic and copies ran while one was open for 7% -> 7% of each run, Pallas kernels for 3% -> 4%
where the time goes in v6:
time: 105 us
  waiting for transfers between devices  50.1 us (48%)
  starting transfers between devices  32.6 us (31%)
  Pallas kernels  10.7 us (10%)
  other arithmetic  4.73 us (5%)
  local copies, waits for them, and re-layouts  3.6 us (3%)
  matrix products  2.84 us (3%)
    ppermute x21, waiting for transfers between devices, swap(): return lax.ppermute(value, 'rows', [(r, r ^ 1 << bit) for r in range(n)])  41.9 us
    ppermute x21, starting transfers between devices, swap(): return lax.ppermute(value, 'rows', [(r, r ^ 1 << bit) for r in range(n)])  26 us
    pallas_call x2, Pallas kernels, product(): pl.pallas_call(product_kernel, in_specs=[pl.BlockSpec(memory_space=pltpu....  8.3 us
    all_to_all x1, waiting for transfers between devices, shards(): lax.all_to_all(ordered, 'rows', split_axis=0, concat_axis=0, tiled=True)  8.25 us
    all_to_all x1, starting transfers between devices, shards(): lax.all_to_all(ordered, 'rows', split_axis=0, concat_axis=0, tiled=True)  6.59 us
    dot_general x2, matrix products, shards(): lax.dot_general(both, jnp.concatenate(values), (((1,), (1,)), ((), ())),...  2.57 us
  transfers between devices with their start and end apart: 22, of which 15 were waited for; matrix products, arithmetic and copies ran while one was open for 7% of the time, Pallas kernels for 4%

profile of v6, /device:TPU:0, one launch (start us, length us, event | category | flops | bytes accessed | tf_op | source)
XLA Modules:
  0.0 105.0 jit_solution(9225897117339627667)
XLA Ops:
  0.0 1.0 copy-done.1
  1.0 4.2 %shard_map.73 = (f32[128,4096]{1,0:T(8,128)S(1)}, f32[128,4096]{1,0:T(8,128)S(1)}) custom-call(s32[1]{0:T(128)} %bitcast.1.core_ref, f32[512,256]{1,0:T(8,128)S(1)} %copy-done.1, f32[256,4096]{1,0:T(8,128)} %columns_hbm.3), custom_call_target="tpu_custom_call" | custom-call | flops 1610612736 | bytes 8388608 | tf_op jit(solution)/shard_map/pallas_call | solution.py:59
  5.2 1.2 %multiply_convert_fusion.1 = f16[128,4096]{1,0:T(8,128)(2,1)} fusion(f32[128,4096]{1,0:T(8,128)S(1)} %get-tuple-element.20), kind=kLoop, calls=%fused_computation.4 | loop fusion | flops 1048576 | bytes 3145728 | tf_op jit(solution)/shard_map/convert_element_type | solution.py:151
  6.4 0.4 collective-permute-start.1
  7.2 0.3 copy-done.2
  7.4 4.1 %shard_map.74 = (f32[128,4096]{1,0:T(8,128)S(1)}, f32[128,4096]{1,0:T(8,128)S(1)}) custom-call(s32[1]{0:T(128)} %bitcast.core_ref, f32[512,256]{1,0:T(8,128)S(1)} %copy-done.2, f32[256,4096]{1,0:T(8,128)} %columns_hbm.3), custom_call_target="tpu_custom_call" | custom-call | flops 1610612736 | bytes 8388608 | tf_op jit(solution)/shard_map/pallas_call | solution.py:59
  11.6 1.6 %multiply_add_fusion.1 = f32[128,4096]{1,0:T(8,128)S(1)} fusion(f32[128,4096]{1,0:T(8,128)S(1)} %get-tuple-element.24, f16[128,4096]{1,0:T(8,128)(2,1)} %collective-permute-done.1), kind=kLoop, calls=%fused_computation.2 | loop fusion | flops 1572864 | bytes 5242880 | tf_op jit(solution)/shard_map/add | solution.py:199
  13.4 3.1 %collective-permute-start.4 = (f16[32,4096]{1,0:T(8,128)(2,1)S(1)}, f16[32,4096]{1,0:T(8,128)(2,1)S(1)}, u32[]{:S(2)}, u32[]{:S(2)}) collective-permute-start(f16[32,4096]{1,0:T(8,128)(2,1)S(1)} %multiply_convert_fusion.4), channel_id=1, source_target_pairs={{0,4},{1,5},{2,6},{3,7},{4,0},{5,1},{6,2},{7,3},{8,12},{9,13},{10,... | collective-permute-start | bytes 786440 | tf_op jit(solution)/shard_map/ppermute | solution.py:145
  16.5 1.6 %collective-permute-start.2 = (f16[32,4096]{1,0:T(8,128)(2,1)S(1)}, f16[32,4096]{1,0:T(8,128)(2,1)S(1)}, u32[]{:S(2)}, u32[]{:S(2)}) collective-permute-start(f16[32,4096]{1,0:T(8,128)(2,1)S(1)} %multiply_convert_fusion.5), channel_id=1, source_target_pairs={{0,2},{1,3},{2,0},{3,1},{4,6},{5,7},{6,4},{7,5},{8,10},{9,11},{10,... | collective-permute-start | bytes 786440 | tf_op jit(solution)/shard_map/ppermute | solution.py:145
  18.1 0.3 multiply_add_fusion
  18.6 4.2 %collective-permute-done.4 = f16[32,4096]{1,0:T(8,128)(2,1)S(1)} collective-permute-done((f16[32,4096]{1,0:T(8,128)(2,1)S(1)}, f16[32,4096]{1,0:T(8,128)(2,1)S(1)}, u32[]{:S(2)}, u32[]{:S(2)}) %collective-permute-start.4) | collective-permute-done | bytes 262176 | tf_op jit(solution)/shard_map/ppermute | solution.py:145
  22.9 1.7 %collective-permute-start.5 = (f16[16,4096]{1,0:T(8,128)(2,1)S(1)}, f16[16,4096]{1,0:T(8,128)(2,1)S(1)}, u32[]{:S(2)}, u32[]{:S(2)}) collective-permute-start(f16[16,4096]{1,0:T(8,128)(2,1)S(1)} %multiply_convert_fusion.8), channel_id=1, source_target_pairs={{0,2},{1,3},{2,0},{3,1},{4,6},{5,7},{6,4},{7,5},{8,10},{9,11},{10,... | collective-permute-start | bytes 393224 | tf_op jit(solution)/shard_map/ppermute | solution.py:145
  24.8 1.6 %collective-permute-start.3 = (f16[16,4096]{1,0:T(8,128)(2,1)S(1)}, f16[16,4096]{1,0:T(8,128)(2,1)S(1)}, u32[]{:S(2)}, u32[]{:S(2)}) collective-permute-start(f16[16,4096]{1,0:T(8,128)(2,1)S(1)} %multiply_convert_fusion.9), channel_id=1, source_target_pairs={{0,4},{1,5},{2,6},{3,7},{4,0},{5,1},{6,2},{7,3},{8,12},{9,13},{10,... | collective-permute-start | bytes 393224 | tf_op jit(solution)/shard_map/ppermute | solution.py:145
  26.4 1.5 %collective-permute-done.5 = f16[16,4096]{1,0:T(8,128)(2,1)S(1)} collective-permute-done((f16[16,4096]{1,0:T(8,128)(2,1)S(1)}, f16[16,4096]{1,0:T(8,128)(2,1)S(1)}, u32[]{:S(2)}, u32[]{:S(2)}) %collective-permute-start.5) | collective-permute-done | bytes 131104 | tf_op jit(solution)/shard_map/ppermute | solution.py:145
  28.0 1.8 %collective-permute-done.3 = f16[16,4096]{1,0:T(8,128)(2,1)S(1)} collective-permute-done((f16[16,4096]{1,0:T(8,128)(2,1)S(1)}, f16[16,4096]{1,0:T(8,128)(2,1)S(1)}, u32[]{:S(2)}, u32[]{:S(2)}) %collective-permute-start.3) | collective-permute-done | bytes 131104 | tf_op jit(solution)/shard_map/ppermute | solution.py:145
  29.9 2.7 %collective-permute-start.7 = (f16[32,4096]{1,0:T(8,128)(2,1)S(1)}, f16[32,4096]{1,0:T(8,128)(2,1)S(1)}, u32[]{:S(2)}, u32[]{:S(2)}) collective-permute-start(f16[32,4096]{1,0:T(8,128)(2,1)S(1)} %fusion.8), channel_id=1, source_target_pairs={{0,8},{1,9},{2,10},{3,11},{4,12},{5,13},{6,14},{7,15},{8,0},{9,1},... | collective-permute-start | bytes 786440 | tf_op jit(solution)/shard_map/ppermute | solution.py:145
  32.6 1.6 %collective-permute-start.10 = (f16[32,4096]{1,0:T(8,128)(2,1)S(1)}, f16[32,4096]{1,0:T(8,128)(2,1)S(1)}, u32[]{:S(2)}, u32[]{:S(2)}) collective-permute-start(f16[32,4096]{1,0:T(8,128)(2,1)S(1)} %multiply_convert_fusion.2), channel_id=1, source_target_pairs={{0,4},{1,5},{2,6},{3,7},{4,0},{5,1},{6,2},{7,3},{8,12},{9,13},{10,... | collective-permute-start | bytes 786440 | tf_op jit(solution)/shard_map/ppermute | solution.py:145
  34.3 0.6 collective-permute-start.8
  34.9 10.7 %collective-permute-done.10 = f16[32,4096]{1,0:T(8,128)(2,1)S(1)} collective-permute-done((f16[32,4096]{1,0:T(8,128)(2,1)S(1)}, f16[32,4096]{1,0:T(8,128)(2,1)S(1)}, u32[]{:S(2)}, u32[]{:S(2)}) %collective-permute-start.10) | collective-permute-done | bytes 262176 | tf_op jit(solution)/shard_map/ppermute | solution.py:145
  45.7 2.4 %collective-permute-start.11 = (f16[16,4096]{1,0:T(8,128)(2,1)S(1)}, f16[16,4096]{1,0:T(8,128)(2,1)S(1)}, u32[]{:S(2)}, u32[]{:S(2)}) collective-permute-start(f16[16,4096]{1,0:T(8,128)(2,1)S(1)} %multiply_convert_fusion.6), channel_id=1, source_target_pairs={{0,2},{1,3},{2,0},{3,1},{4,6},{5,7},{6,4},{7,5},{8,10},{9,11},{10,... | collective-permute-start | bytes 393224 | tf_op jit(solution)/shard_map/ppermute | solution.py:145
  48.3 3.3 %collective-permute-done.11 = f16[16,4096]{1,0:T(8,128)(2,1)S(1)} collective-permute-done((f16[16,4096]{1,0:T(8,128)(2,1)S(1)}, f16[16,4096]{1,0:T(8,128)(2,1)S(1)}, u32[]{:S(2)}, u32[]{:S(2)}) %collective-permute-start.11) | collective-permute-done | bytes 131104 | tf_op jit(solution)/shard_map/ppermute | solution.py:145
  51.6 1.6 %collective-permute-done.9 = f16[16,4096]{1,0:T(8,128)(2,1)S(1)} collective-permute-done((f16[16,4096]{1,0:T(8,128)(2,1)S(1)}, f16[16,4096]{1,0:T(8,128)(2,1)S(1)}, u32[]{:S(2)}, u32[]{:S(2)}) %collective-permute-start.9) | collective-permute-done | bytes 131104 | tf_op jit(solution)/shard_map/ppermute | solution.py:145
  53.4 1.1 %collective-permute-start.14 = (bf16[16,4096]{1,0:T(8,128)(2,1)S(1)}, bf16[16,4096]{1,0:T(8,128)(2,1)S(1)}, u32[]{:S(2)}, u32[]{:S(2)}) collective-permute-start(bf16[16,4096]{1,0:T(8,128)(2,1)S(1)} %get-tuple-element.30), channel_id=1, source_target_pairs={{0,2},{1,3},{2,0},{3,1},{4,6},{5,7},{6,4},{7,5},{8,10},{9,11},{10,... | collective-permute-start | bytes 393224 | tf_op jit(solution)/shard_map/ppermute | solution.py:145
  54.6 1.9 %collective-permute-start.12 = (bf16[16,4096]{1,0:T(8,128)(2,1)S(1)}, bf16[16,4096]{1,0:T(8,128)(2,1)S(1)}, u32[]{:S(2)}, u32[]{:S(2)}) collective-permute-start(bf16[16,4096]{1,0:T(8,128)(2,1)S(1)} %get-tuple-element.29), channel_id=1, source_target_pairs={{0,4},{1,5},{2,6},{3,7},{4,0},{5,1},{6,2},{7,3},{8,12},{9,13},{10,... | collective-permute-start | bytes 393224 | tf_op jit(solution)/shard_map/ppermute | solution.py:145
  56.5 1.9 %collective-permute-done.14 = bf16[16,4096]{1,0:T(8,128)(2,1)S(1)} collective-permute-done((bf16[16,4096]{1,0:T(8,128)(2,1)S(1)}, bf16[16,4096]{1,0:T(8,128)(2,1)S(1)}, u32[]{:S(2)}, u32[]{:S(2)}) %collective-permute-start.14) | collective-permute-done | bytes 131104 | tf_op jit(solution)/shard_map/ppermute | solution.py:145
  58.5 1.1 %collective-permute-start.15 = (bf16[32,4096]{1,0:T(8,128)(2,1)S(1)}, bf16[32,4096]{1,0:T(8,128)(2,1)S(1)}, u32[]{:S(2)}, u32[]{:S(2)}) collective-permute-start(bf16[32,4096]{1,0:T(8,128)(2,1)S(1)} %constant_dynamic-update-slice_fusion.10), channel_id=1, source_target_pairs={{0,4},{1,5},{2,6},{3,7},{4,0},{5,1},{6,2},{7,3},{8,12},{9,13},{10,... | collective-permute-start | bytes 786440 | tf_op jit(solution)/shard_map/ppermute | solution.py:145
  59.7 3.3 %collective-permute-done.12 = bf16[16,4096]{1,0:T(8,128)(2,1)S(1)} collective-permute-done((bf16[16,4096]{1,0:T(8,128)(2,1)S(1)}, bf16[16,4096]{1,0:T(8,128)(2,1)S(1)}, u32[]{:S(2)}, u32[]{:S(2)}) %collective-permute-start.12) | collective-permute-done | bytes 131104 | tf_op jit(solution)/shard_map/ppermute | solution.py:145
  63.0 1.2 %collective-permute-start.13 = (bf16[32,4096]{1,0:T(8,128)(2,1)S(1)}, bf16[32,4096]{1,0:T(8,128)(2,1)S(1)}, u32[]{:S(2)}, u32[]{:S(2)}) collective-permute-start(bf16[32,4096]{1,0:T(8,128)(2,1)S(1)} %constant_dynamic-update-slice_fusion.14), channel_id=1, source_target_pairs={{0,2},{1,3},{2,0},{3,1},{4,6},{5,7},{6,4},{7,5},{8,10},{9,11},{10,... | collective-permute-start | bytes 786440 | tf_op jit(solution)/shard_map/ppermute | solution.py:145
  64.2 2.4 %collective-permute-done.16 = f16[32,4096]{1,0:T(8,128)(2,1)S(1)} collective-permute-done((f16[32,4096]{1,0:T(8,128)(2,1)S(1)}, f16[32,4096]{1,0:T(8,128)(2,1)S(1)}, u32[]{:S(2)}, u32[]{:S(2)}) %collective-permute-start.16) | collective-permute-done | bytes 262176 | tf_op jit(solution)/shard_map/ppermute | solution.py:145
  66.8 3.7 %collective-permute-done.15 = bf16[32,4096]{1,0:T(8,128)(2,1)S(1)} collective-permute-done((bf16[32,4096]{1,0:T(8,128)(2,1)S(1)}, bf16[32,4096]{1,0:T(8,128)(2,1)S(1)}, u32[]{:S(2)}, u32[]{:S(2)}) %collective-permute-start.15) | collective-permute-done | bytes 262176 | tf_op jit(solution)/shard_map/ppermute | solution.py:145
  70.5 0.4 pad_maximum_fusion
  70.9 1.3 %collective-permute-start.19 = (bf16[16,4096]{1,0:T(8,128)(2,1)S(1)}, bf16[16,4096]{1,0:T(8,128)(2,1)S(1)}, u32[]{:S(2)}, u32[]{:S(2)}) collective-permute-start(bf16[16,4096]{1,0:T(8,128)(2,1)S(1)} %get-tuple-element.34), channel_id=1, source_target_pairs={{0,2},{1,3},{2,0},{3,1},{4,6},{5,7},{6,4},{7,5},{8,10},{9,11},{10,... | collective-permute-start | bytes 393224 | tf_op jit(solution)/shard_map/ppermute | solution.py:145
  72.2 1.4 %collective-permute-start.17 = (bf16[16,4096]{1,0:T(8,128)(2,1)S(1)}, bf16[16,4096]{1,0:T(8,128)(2,1)S(1)}, u32[]{:S(2)}, u32[]{:S(2)}) collective-permute-start(bf16[16,4096]{1,0:T(8,128)(2,1)S(1)} %get-tuple-element.33), channel_id=1, source_target_pairs={{0,4},{1,5},{2,6},{3,7},{4,0},{5,1},{6,2},{7,3},{8,12},{9,13},{10,... | collective-permute-start | bytes 393224 | tf_op jit(solution)/shard_map/ppermute | solution.py:145
  73.7 1.3 %fusion.refs_0_ = f32[512,128]{1,0:T(8,128)S(1)} fusion(bf16[512,4096]{1,0:T(8,128)(2,1)S(1)} %bitcast.12, bf16[64,4096]{1,0:T(8,128)(2,1)S(1)} %constant_dynamic-update-slice_fusion.8, bf16[64,4096]{1,0:T(8,128)(2,1)S(1)} %constant_dynamic-update-slice_fusion.12), kind=kOutput, calls=%fused_computation.5 | convolution fusion | flops 538968064 | bytes 5505024 | tf_op jit(solution)/shard_map/dot_general | solution.py:228
  74.9 1.0 collective-permute-done.19
  76.0 1.5 %collective-permute-start.20 = (bf16[32,4096]{1,0:T(8,128)(2,1)S(1)}, bf16[32,4096]{1,0:T(8,128)(2,1)S(1)}, u32[]{:S(2)}, u32[]{:S(2)}) collective-permute-start(bf16[32,4096]{1,0:T(8,128)(2,1)S(1)} %constant_dynamic-update-slice_fusion.2), channel_id=1, source_target_pairs={{0,4},{1,5},{2,6},{3,7},{4,0},{5,1},{6,2},{7,3},{8,12},{9,13},{10,... | collective-permute-start | bytes 786440 | tf_op jit(solution)/shard_map/ppermute | solution.py:145
  77.5 0.7 collective-permute-done.17
  78.2 0.5 collective-permute-start.18
  78.8 4.1 %collective-permute-done.20 = bf16[32,4096]{1,0:T(8,128)(2,1)S(1)} collective-permute-done((bf16[32,4096]{1,0:T(8,128)(2,1)S(1)}, bf16[32,4096]{1,0:T(8,128)(2,1)S(1)}, u32[]{:S(2)}, u32[]{:S(2)}) %collective-permute-start.20) | collective-permute-done | bytes 262176 | tf_op jit(solution)/shard_map/ppermute | solution.py:145
  82.9 1.7 %collective-permute-done.18 = bf16[32,4096]{1,0:T(8,128)(2,1)S(1)} collective-permute-done((bf16[32,4096]{1,0:T(8,128)(2,1)S(1)}, bf16[32,4096]{1,0:T(8,128)(2,1)S(1)}, u32[]{:S(2)}, u32[]{:S(2)}) %collective-permute-start.18) | collective-permute-done | bytes 262176 | tf_op jit(solution)/shard_map/ppermute | solution.py:145
  84.7 1.3 %fusion.4.refs_1_ = f32[512,128]{1,0:T(8,128)S(1)} fusion(bf16[512,4096]{1,0:T(8,128)(2,1)S(1)} %bitcast.13, bf16[64,4096]{1,0:T(8,128)(2,1)S(1)} %constant_dynamic-update-slice_fusion, bf16[64,4096]{1,0:T(8,128)(2,1)S(1)} %constant_dynamic-update-slice_fusion.4), kind=kOutput, calls=%fused_computation.9 | convolution fusion | flops 538968064 | bytes 5505024 | tf_op jit(solution)/shard_map/dot_general | solution.py:228
  86.0 1.5 %shard_map.75 = bf16[16,32,256]{2,1,0:T(8,128)(2,1)} custom-call(s32[16]{0:T(128)S(1)} %copy-done, f32[512,128]{1,0:T(8,128)S(1)} %fusion.refs_0_, f32[512,128]{1,0:T(8,128)S(1)} %fusion.4.refs_1_), custom_call_target="tpu_custom_call" | custom-call | flops 65536 | bytes 786432 | tf_op jit(solution)/shard_map/pallas_call | solution.py:94
  87.6 6.6 %all-to-all-start = ((bf16[16,1,32,256]{3,2,1,0:T(8,128)(2,1)}), bf16[16,1,32,256]{3,2,1,0:T(8,128)(2,1)S(1)}, u32[]{:S(2)}, u32[]{:S(2)}) async-start(bf16[16,1,32,256]{3,2,1,0:T(8,128)(2,1)} %bitcast.4), calls=%async_computation | async-start | bytes 524288 | tf_op jit(solution)/shard_map/all_to_all | solution.py:235
  94.3 0.7 dynamic_slice.67
  95.0 0.3 fusion.10
  95.3 0.6 constant_dynamic-slice_fusion.allowed_ref
  96.0 8.2 %all-to-all-done = bf16[16,1,32,256]{3,2,1,0:T(8,128)(2,1)S(1)} async-done(((bf16[16,1,32,256]{3,2,1,0:T(8,128)(2,1)}), bf16[16,1,32,256]{3,2,1,0:T(8,128)(2,1)S(1)}, u32[]{:S(2)}, u32[]{:S(2)}) %all-to-all-start) | async-done | bytes 262176 | tf_op jit(solution)/shard_map/all_to_all | solution.py:235
  104.2 0.8 shard_map.76
  (73 shorter events, 2.6 us)
Async XLA Ops:
  0.0 1.0 copy-start.1
  6.4 1.0 copy-start.2
  6.4 5.2 %collective-permute-start.1 = (f16[128,4096]{1,0:T(8,128)(2,1)}, f16[128,4096]{1,0:T(8,128)(2,1)}, u32[]{:S(2)}, u32[]{:S(2)}) collective-permute-start(f16[128,4096]{1,0:T(8,128)(2,1)} %multiply_convert_fusion.1), channel_id=1, source_target_pairs={{0,1},{1,0},{2,3},{3,2},{4,5},{5,4},{6,7},{7,6},{8,9},{9,8},{10,11... | collective-permute-start | bytes 3145736 | tf_op jit(solution)/shard_map/ppermute | solution.py:145
  7.0 11.1 %collective-permute-start = (f16[128,4096]{1,0:T(8,128)(2,1)S(1)}, f16[128,4096]{1,0:T(8,128)(2,1)S(1)}, u32[]{:S(2)}, u32[]{:S(2)}) collective-permute-start(f16[128,4096]{1,0:T(8,128)(2,1)S(1)} %multiply_convert_fusion), channel_id=1, source_target_pairs={{0,1},{1,0},{2,3},{3,2},{4,5},{5,4},{6,7},{7,6},{8,9},{9,8},{10,11... | collective-permute-start | bytes 3145736 | tf_op jit(solution)/shard_map/ppermute | solution.py:145
  13.4 9.4 %collective-permute-start.4 = (f16[32,4096]{1,0:T(8,128)(2,1)S(1)}, f16[32,4096]{1,0:T(8,128)(2,1)S(1)}, u32[]{:S(2)}, u32[]{:S(2)}) collective-permute-start(f16[32,4096]{1,0:T(8,128)(2,1)S(1)} %multiply_convert_fusion.4), channel_id=1, source_target_pairs={{0,4},{1,5},{2,6},{3,7},{4,0},{5,1},{6,2},{7,3},{8,12},{9,13},{10,... | collective-permute-start | bytes 786440 | tf_op jit(solution)/shard_map/ppermute | solution.py:145
  16.5 8.1 %collective-permute-start.2 = (f16[32,4096]{1,0:T(8,128)(2,1)S(1)}, f16[32,4096]{1,0:T(8,128)(2,1)S(1)}, u32[]{:S(2)}, u32[]{:S(2)}) collective-permute-start(f16[32,4096]{1,0:T(8,128)(2,1)S(1)} %multiply_convert_fusion.5), channel_id=1, source_target_pairs={{0,2},{1,3},{2,0},{3,1},{4,6},{5,7},{6,4},{7,5},{8,10},{9,11},{10,... | collective-permute-start | bytes 786440 | tf_op jit(solution)/shard_map/ppermute | solution.py:145
  22.9 9.7 %copy-start.3 = (bf16[16,16,4096]{2,1,0:T(8,128)(2,1)S(1)}, bf16[16,16,4096]{2,1,0:T(8,128)(2,1)}, u32[]{:S(2)}) copy-start(bf16[16,16,4096]{2,1,0:T(8,128)(2,1)} %param.9) | copy-start | bytes 6291460
  22.9 5.0 %collective-permute-start.5 = (f16[16,4096]{1,0:T(8,128)(2,1)S(1)}, f16[16,4096]{1,0:T(8,128)(2,1)S(1)}, u32[]{:S(2)}, u32[]{:S(2)}) collective-permute-start(f16[16,4096]{1,0:T(8,128)(2,1)S(1)} %multiply_convert_fusion.8), channel_id=1, source_target_pairs={{0,2},{1,3},{2,0},{3,1},{4,6},{5,7},{6,4},{7,5},{8,10},{9,11},{10,... | collective-permute-start | bytes 393224 | tf_op jit(solution)/shard_map/ppermute | solution.py:145
  24.8 5.0 %collective-permute-start.3 = (f16[16,4096]{1,0:T(8,128)(2,1)S(1)}, f16[16,4096]{1,0:T(8,128)(2,1)S(1)}, u32[]{:S(2)}, u32[]{:S(2)}) collective-permute-start(f16[16,4096]{1,0:T(8,128)(2,1)S(1)} %multiply_convert_fusion.9), channel_id=1, source_target_pairs={{0,4},{1,5},{2,6},{3,7},{4,0},{5,1},{6,2},{7,3},{8,12},{9,13},{10,... | collective-permute-start | bytes 393224 | tf_op jit(solution)/shard_map/ppermute | solution.py:145
  29.9 18.3 %collective-permute-start.7 = (f16[32,4096]{1,0:T(8,128)(2,1)S(1)}, f16[32,4096]{1,0:T(8,128)(2,1)S(1)}, u32[]{:S(2)}, u32[]{:S(2)}) collective-permute-start(f16[32,4096]{1,0:T(8,128)(2,1)S(1)} %fusion.8), channel_id=1, source_target_pairs={{0,8},{1,9},{2,10},{3,11},{4,12},{5,13},{6,14},{7,15},{8,0},{9,1},... | collective-permute-start | bytes 786440 | tf_op jit(solution)/shard_map/ppermute | solution.py:145
  32.6 37.9 %collective-permute-start.6 = (bf16[16,16,4096]{2,1,0:T(8,128)(2,1)S(1)}, bf16[16,16,4096]{2,1,0:T(8,128)(2,1)S(1)}, u32[]{:S(2)}, u32[]{:S(2)}) collective-permute-start(bf16[16,16,4096]{2,1,0:T(8,128)(2,1)S(1)} %copy-done.3), channel_id=1, source_target_pairs={{0,1},{1,0},{2,3},{3,2},{4,5},{5,4},{6,7},{7,6},{8,9},{9,8},{10,11... | collective-permute-start | bytes 6291464 | tf_op jit(solution)/shard_map/ppermute | solution.py:145
  32.6 12.9 %collective-permute-start.10 = (f16[32,4096]{1,0:T(8,128)(2,1)S(1)}, f16[32,4096]{1,0:T(8,128)(2,1)S(1)}, u32[]{:S(2)}, u32[]{:S(2)}) collective-permute-start(f16[32,4096]{1,0:T(8,128)(2,1)S(1)} %multiply_convert_fusion.2), channel_id=1, source_target_pairs={{0,4},{1,5},{2,6},{3,7},{4,0},{5,1},{6,2},{7,3},{8,12},{9,13},{10,... | collective-permute-start | bytes 786440 | tf_op jit(solution)/shard_map/ppermute | solution.py:145
  34.3 13.7 %collective-permute-start.8 = (f16[32,4096]{1,0:T(8,128)(2,1)S(1)}, f16[32,4096]{1,0:T(8,128)(2,1)S(1)}, u32[]{:S(2)}, u32[]{:S(2)}) collective-permute-start(f16[32,4096]{1,0:T(8,128)(2,1)S(1)} %multiply_convert_fusion.3), channel_id=1, source_target_pairs={{0,2},{1,3},{2,0},{3,1},{4,6},{5,7},{6,4},{7,5},{8,10},{9,11},{10,... | collective-permute-start | bytes 786440 | tf_op jit(solution)/shard_map/ppermute | solution.py:145
  45.7 5.9 %collective-permute-start.11 = (f16[16,4096]{1,0:T(8,128)(2,1)S(1)}, f16[16,4096]{1,0:T(8,128)(2,1)S(1)}, u32[]{:S(2)}, u32[]{:S(2)}) collective-permute-start(f16[16,4096]{1,0:T(8,128)(2,1)S(1)} %multiply_convert_fusion.6), channel_id=1, source_target_pairs={{0,2},{1,3},{2,0},{3,1},{4,6},{5,7},{6,4},{7,5},{8,10},{9,11},{10,... | collective-permute-start | bytes 393224 | tf_op jit(solution)/shard_map/ppermute | solution.py:145
  48.2 5.1 %collective-permute-start.9 = (f16[16,4096]{1,0:T(8,128)(2,1)S(1)}, f16[16,4096]{1,0:T(8,128)(2,1)S(1)}, u32[]{:S(2)}, u32[]{:S(2)}) collective-permute-start(f16[16,4096]{1,0:T(8,128)(2,1)S(1)} %multiply_convert_fusion.7), channel_id=1, source_target_pairs={{0,4},{1,5},{2,6},{3,7},{4,0},{5,1},{6,2},{7,3},{8,12},{9,13},{10,... | collective-permute-start | bytes 393224 | tf_op jit(solution)/shard_map/ppermute | solution.py:145
  53.3 13.4 %collective-permute-start.16 = (f16[32,4096]{1,0:T(8,128)(2,1)S(1)}, f16[32,4096]{1,0:T(8,128)(2,1)S(1)}, u32[]{:S(2)}, u32[]{:S(2)}) collective-permute-start(f16[32,4096]{1,0:T(8,128)(2,1)S(1)} %fusion.9), channel_id=1, source_target_pairs={{0,8},{1,9},{2,10},{3,11},{4,12},{5,13},{6,14},{7,15},{8,0},{9,1},... | collective-permute-start | bytes 786440 | tf_op jit(solution)/shard_map/ppermute | solution.py:145
  53.4 5.0 %collective-permute-start.14 = (bf16[16,4096]{1,0:T(8,128)(2,1)S(1)}, bf16[16,4096]{1,0:T(8,128)(2,1)S(1)}, u32[]{:S(2)}, u32[]{:S(2)}) collective-permute-start(bf16[16,4096]{1,0:T(8,128)(2,1)S(1)} %get-tuple-element.30), channel_id=1, source_target_pairs={{0,2},{1,3},{2,0},{3,1},{4,6},{5,7},{6,4},{7,5},{8,10},{9,11},{10,... | collective-permute-start | bytes 393224 | tf_op jit(solution)/shard_map/ppermute | solution.py:145
  54.6 8.4 %collective-permute-start.12 = (bf16[16,4096]{1,0:T(8,128)(2,1)S(1)}, bf16[16,4096]{1,0:T(8,128)(2,1)S(1)}, u32[]{:S(2)}, u32[]{:S(2)}) collective-permute-start(bf16[16,4096]{1,0:T(8,128)(2,1)S(1)} %get-tuple-element.29), channel_id=1, source_target_pairs={{0,4},{1,5},{2,6},{3,7},{4,0},{5,1},{6,2},{7,3},{8,12},{9,13},{10,... | collective-permute-start | bytes 393224 | tf_op jit(solution)/shard_map/ppermute | solution.py:145
  58.5 12.0 %collective-permute-start.15 = (bf16[32,4096]{1,0:T(8,128)(2,1)S(1)}, bf16[32,4096]{1,0:T(8,128)(2,1)S(1)}, u32[]{:S(2)}, u32[]{:S(2)}) collective-permute-start(bf16[32,4096]{1,0:T(8,128)(2,1)S(1)} %constant_dynamic-update-slice_fusion.10), channel_id=1, source_target_pairs={{0,4},{1,5},{2,6},{3,7},{4,0},{5,1},{6,2},{7,3},{8,12},{9,13},{10,... | collective-permute-start | bytes 786440 | tf_op jit(solution)/shard_map/ppermute | solution.py:145
  63.0 7.5 %collective-permute-start.13 = (bf16[32,4096]{1,0:T(8,128)(2,1)S(1)}, bf16[32,4096]{1,0:T(8,128)(2,1)S(1)}, u32[]{:S(2)}, u32[]{:S(2)}) collective-permute-start(bf16[32,4096]{1,0:T(8,128)(2,1)S(1)} %constant_dynamic-update-slice_fusion.14), channel_id=1, source_target_pairs={{0,2},{1,3},{2,0},{3,1},{4,6},{5,7},{6,4},{7,5},{8,10},{9,11},{10,... | collective-permute-start | bytes 786440 | tf_op jit(solution)/shard_map/ppermute | solution.py:145
  70.9 5.0 %collective-permute-start.19 = (bf16[16,4096]{1,0:T(8,128)(2,1)S(1)}, bf16[16,4096]{1,0:T(8,128)(2,1)S(1)}, u32[]{:S(2)}, u32[]{:S(2)}) collective-permute-start(bf16[16,4096]{1,0:T(8,128)(2,1)S(1)} %get-tuple-element.34), channel_id=1, source_target_pairs={{0,2},{1,3},{2,0},{3,1},{4,6},{5,7},{6,4},{7,5},{8,10},{9,11},{10,... | collective-permute-start | bytes 393224 | tf_op jit(solution)/shard_map/ppermute | solution.py:145
  72.2 5.9 %collective-permute-start.17 = (bf16[16,4096]{1,0:T(8,128)(2,1)S(1)}, bf16[16,4096]{1,0:T(8,128)(2,1)S(1)}, u32[]{:S(2)}, u32[]{:S(2)}) collective-permute-start(bf16[16,4096]{1,0:T(8,128)(2,1)S(1)} %get-tuple-element.33), channel_id=1, source_target_pairs={{0,4},{1,5},{2,6},{3,7},{4,0},{5,1},{6,2},{7,3},{8,12},{9,13},{10,... | collective-permute-start | bytes 393224 | tf_op jit(solution)/shard_map/ppermute | solution.py:145
  76.0 6.9 %collective-permute-start.20 = (bf16[32,4096]{1,0:T(8,128)(2,1)S(1)}, bf16[32,4096]{1,0:T(8,128)(2,1)S(1)}, u32[]{:S(2)}, u32[]{:S(2)}) collective-permute-start(bf16[32,4096]{1,0:T(8,128)(2,1)S(1)} %constant_dynamic-update-slice_fusion.2), channel_id=1, source_target_pairs={{0,4},{1,5},{2,6},{3,7},{4,0},{5,1},{6,2},{7,3},{8,12},{9,13},{10,... | collective-permute-start | bytes 786440 | tf_op jit(solution)/shard_map/ppermute | solution.py:145
  78.2 6.4 %collective-permute-start.18 = (bf16[32,4096]{1,0:T(8,128)(2,1)S(1)}, bf16[32,4096]{1,0:T(8,128)(2,1)S(1)}, u32[]{:S(2)}, u32[]{:S(2)}) collective-permute-start(bf16[32,4096]{1,0:T(8,128)(2,1)S(1)} %constant_dynamic-update-slice_fusion.6), channel_id=1, source_target_pairs={{0,2},{1,3},{2,0},{3,1},{4,6},{5,7},{6,4},{7,5},{8,10},{9,11},{10,... | collective-permute-start | bytes 786440 | tf_op jit(solution)/shard_map/ppermute | solution.py:145
  84.7 1.4 %copy-start = (s32[16]{0:T(128)S(1)}, s32[16]{0:T(128)}, u32[]{:S(2)}) copy-start(s32[16]{0:T(128)} %slots_ref.1) | copy-start | bytes 196
  84.7 9.5 %copy-start.5 = (s32[8]{0:T(128)S(1)}, s32[8]{0:T(128)}, u32[]{:S(2)}) copy-start(s32[8]{0:T(128)} %param.12) | copy-start | bytes 100
  84.7 9.5 %copy-start.4 = (s32[8,12]{1,0:T(8,128)S(1)}, s32[8,12]{1,0:T(8,128)}, u32[]{:S(2)}) copy-start(s32[8,12]{1,0:T(8,128)} %param.11) | copy-start | bytes 1156
  84.7 10.3 %copy-start.6 = (s32[512]{0:T(512)S(1)}, s32[512]{0:T(512)}, u32[]{:S(2)}) copy-start(s32[512]{0:T(512)} %param.10) | copy-start | bytes 6148
  87.6 16.6 %all-to-all-start = ((bf16[16,1,32,256]{3,2,1,0:T(8,128)(2,1)}), bf16[16,1,32,256]{3,2,1,0:T(8,128)(2,1)S(1)}, u32[]{:S(2)}, u32[]{:S(2)}) async-start(bf16[16,1,32,256]{3,2,1,0:T(8,128)(2,1)} %bitcast.4), calls=%async_computation | async-start | bytes 524288 | tf_op jit(solution)/shard_map/all_to_all | solution.py:235

commit v7 on v6

--- a/solution.py
+++ b/solution.py
@@ -11,7 +11,7 @@
 UNIT = 4.0
 LANES = 128
 OTHER_VMEM = 48
-MINE_VMEM = 47
+MINE_VMEM = 44
 
 
 def listed_mask(query_cluster, cand_blocks, cand_count, nblocks):
@@ -102,39 +102,37 @@
 
 
 def finish_kernel(got_ref, allowed_ref, out_ref):
-    chips, cores, owned, rows, half = got_ref.shape
+    n, owned, quad, examples, half = got_ref.shape
     parts = half // LANES
-    per_row = owned * cores * parts
-    for chip in range(chips):
-        for core in range(cores):
+    per_row = owned * CORES * parts
+    for device in range(n):
+        for core in range(CORES):
+            sources = [(device & ~3) | (y << 1) | core for y in range(quad // CORES)]
             for slot in range(owned):
-                scores = got_ref[chip, core, slot].astype(jnp.float32)
-                if core:
-                    scores = jnp.concatenate([scores[rows // 2:], scores[:rows // 2]], axis=0)
+                scores = sum(got_ref[s, slot, s ^ device].astype(jnp.float32) for s in sources)
                 scores = scores * allowed_ref[slot:slot + 1, core * half:(core + 1) * half]
                 for i in range(parts):
-                    first = chip * rows * per_row + slot * cores * parts + core * parts + i
-                    out_ref[pl.ds(first, rows, stride=per_row), :] = scores[:, i * LANES:(i + 1) * LANES]
+                    first = device * examples * per_row + (slot * CORES + core) * parts + i
+                    out_ref[pl.ds(first, examples, stride=per_row), :] = scores[:, i * LANES:(i + 1) * LANES]
 
 
 def finish(got, allowed):
-    chips, cores, owned, rows, half = got.shape
+    n, owned, _, examples, half = got.shape
     flat = pl.pallas_call(
         finish_kernel,
-        out_shape=jax.ShapeDtypeStruct((chips * rows * owned * cores * half // LANES, LANES), jnp.float32),
+        out_shape=jax.ShapeDtypeStruct((n * examples * owned * CORES * half // LANES, LANES), jnp.float32),
         compiler_params=pltpu.CompilerParams(vmem_limit_bytes=4 * 1024 * 1024),
-        cost_estimate=pl.CostEstimate(flops=got.size, bytes_accessed=6 * got.size, transcendentals=0),
+        cost_estimate=pl.CostEstimate(flops=got.size, bytes_accessed=4 * got.size, transcendentals=0),
     )(got, allowed)
-    return flat.reshape(chips * rows, owned, cores * half)
+    return flat.reshape(n * examples, owned, CORES * half)
 
 
 def shards(queries, precond, train, query_cluster, cand_blocks, cand_count, slot_block):
     n = lax.axis_size("rows")
     chips = n // CORES
     bits = chips.bit_length() - 1
-    ybits = [1 + b for b in range(bits // 2)]
-    zbits = [1 + b for b in range(bits // 2, bits)]
-    orders = (ybits + zbits, zbits[:1] + ybits + zbits[1:])
+    ybit, zbit = 1, 1 + bits // 2
+    rest = [bit for bit in range(1, 1 + bits) if bit not in (ybit, zbit)]
     me = lax.axis_index("rows")
     core = me & 1
 
@@ -153,91 +151,94 @@
     def unpack(value):
         return value.astype(jnp.float32) * (1.0 / UNIT)
 
-    def part(value, index):
-        rows = value.shape[0] // 2
-        return lax.dynamic_slice_in_dim(value, index * rows, rows)
-
-    def join(own, got, index):
-        rows = own.shape[0]
-        full = jnp.zeros((2 * rows,) + own.shape[1:], own.dtype)
-        full = lax.dynamic_update_slice_in_dim(full, own, index * rows, 0)
-        return lax.dynamic_update_slice_in_dim(full, got, (1 - index) * rows, 0)
+    def part(value, index, axis):
+        size = value.shape[axis] // 2
+        return lax.dynamic_slice_in_dim(value, index * size, size, axis)
+
+    def give(value, bit, axis):
+        return pack(part(value, 1 - side(bit), axis))
+
+    def keep(value, got, bit, axis):
+        return part(value, side(bit), axis) + unpack(got)
+
+    def join(own, got, bit):
+        size = own.shape[1]
+        full = jnp.zeros((own.shape[0], 2 * size) + own.shape[2:], own.dtype)
+        full = lax.dynamic_update_slice_in_dim(full, own, side(bit) * size, 1)
+        return lax.dynamic_update_slice_in_dim(full, got, (1 - side(bit)) * size, 1)
 
     def after(value, first):
         return lax.optimization_barrier((value, first))[0]
 
+    def paths(value, other):
+        value = value + unpack(other)
+        rows = value.shape[0] // PATHS
+        return [value[i * rows:(i + 1) * rows] for i in range(PATHS)]
+
+    levels = ((ybit, 1), (zbit, 0)), ((zbit, 0), (ybit, 1))
+
     def messages(values, step):
-        return [pack(part(value, 1 - side(order[step]))) for value, order in zip(values, orders)]
+        return [give(value, *level[step]) for value, level in zip(values, levels)]
 
     def exchange(values, sent, step):
-        got = [swap(message, order[step]) for message, order in zip(sent, orders)]
-        return [
-            part(value, side(order[step])) + unpack(message)
-            for value, message, order in zip(values, got, orders)
-        ]
-
-    def gather(values, step):
-        got = [swap(value, order[step]) for value, order in zip(values, orders)]
-        return [join(value, message, side(order[step])) for value, message, order in zip(values, got, orders)]
-
-    def whole(values):
-        return pack(jnp.concatenate(values))
-
-    def total(values, got):
-        rows = values[0].shape[0]
-        return [
-            (value + unpack(got[i * rows:(i + 1) * rows])).astype(jnp.bfloat16)
-            for i, value in enumerate(values)
-        ]
-
+        got = [swap(message, level[step][0]) for message, level in zip(sent, levels)]
+        return [keep(value, message, *level[step]) for value, message, level in zip(values, got, levels)]
+
+    def halve(values):
+        value = jnp.stack(values)
+        for bit in rest[:-1]:
+            value = keep(value, swap(give(value, bit, 1), bit), bit, 1)
+        return value
+
+    def gather(value):
+        for bit in reversed([zbit] + rest[:-1]):
+            value = join(value, swap(value, bit), bit)
+        return value.reshape(-1, value.shape[-1])
+
+    rows = train.reshape(examples * nblocks, width)
+    near = part(rows, side(ybit), 1)
+    far = part(rows, 1 - side(ybit), 1)
+    far = [part(far, i, 0) for i in range(2)]
+
+    early = swap(far[0], ybit)
+    queries = after(queries, far[0])
     sent = [pack(value) for value in product(1 - core, queries, precond, OTHER_VMEM)]
     got = [swap(value, 0) for value in sent]
     mine = product(core, after(queries, sent[0]), precond, MINE_VMEM)
-    rows = mine[0].shape[0] // PATHS
-
-    def paths(value, other):
-        value = value + unpack(other)
-        return [value[i * rows:(i + 1) * rows] for i in range(PATHS)]
-
-    steps = bits - 1
-    last = orders[0][-1]
     one = paths(mine[0], got[0])
     sent = messages(one, 0)
     two = paths(mine[1], after(got[1], sent))
     one = exchange(one, sent, 0)
-    for step in range(1, steps):
-        one = exchange(one, messages(one, step), step)
-    sent = whole(one)
-    train, two = after((train, two), sent)
-    got_one = swap(sent, last)
-    for step in range(steps):
-        two = exchange(two, messages(two, step), step)
-    other_train = swap(train, 0)
-    sent = whole(two)
-    one = after(total(one, got_one), sent)
-    two = total(two, swap(sent, last))
-    both = jnp.concatenate([train, other_train], axis=0).reshape(CORES * examples * nblocks, width)
-    two = after(two, both)
-    for step in reversed(range(steps)):
-        one = gather(one, step)
-        if step:
-            two = after(two, one)
-        two = gather(two, step)
+    sent = messages(one, 1)
+    two = exchange(two, after(messages(two, 0), sent), 0)
+    one = halve(exchange(one, sent, 1))
+    sent = pack(one)
+    far[1], near, early = after((far[1], near, early), sent)
+    got_one = swap(sent, rest[-1])
+    two = halve(exchange(two, messages(two, 1), 1))
+    late = swap(far[1], ybit)
+    moved = [near, swap(near, 0), early, late, swap(early, 0)]
+    sent = pack(two)
+    one = (after(one, sent) + unpack(got_one)).astype(jnp.bfloat16)
+    got_two = swap(sent, rest[-1])
+    one, late = after((one, late), sent)
+    both = jnp.concatenate(moved + [swap(late, 0)], axis=0)
+    one = gather(one)
+    two, both = lax.optimization_barrier(((two + unpack(got_two)).astype(jnp.bfloat16), both))
+    two = gather(two)
 
     raws = [
-        lax.dot_general(
-            both, jnp.concatenate(values), (((1,), (1,)), ((), ())), preferred_element_type=jnp.float32
-        )
-        for values in (one, two)
+        lax.dot_general(both, value, (((1,), (1,)), ((), ())), preferred_element_type=jnp.float32)
+        for value in (one, two)
     ]
     owned = nblocks // n
-    ordered = in_slot_order(raws, slot_block).reshape(n, owned, CORES * examples, nq // CORES)
+    ordered = in_slot_order(raws, slot_block).reshape(n, owned, 2 * CORES * examples, nq // CORES)
     got = lax.all_to_all(ordered, "rows", split_axis=0, concat_axis=0, tiled=True)
 
     allowed = listed_mask(query_cluster, cand_blocks, cand_count, nblocks)
     slots = lax.dynamic_slice_in_dim(slot_block, me * owned, owned)
     own_allowed = jnp.take(allowed, slots, axis=0, mode="clip")
-    return finish(got.reshape(chips, CORES, owned, CORES * examples, nq // CORES), own_allowed)
+    return finish(got.reshape(n, owned, 2 * CORES, examples, nq // CORES), own_allowed)
 
 
 def solution(mesh):

time: 105 us -> 109 us (1.038)
  waiting for transfers between devices: 50.1 us -> 58.2 us
  starting transfers between devices: 32.6 us -> 25.9 us
  local copies, waits for them, and re-layouts: 3.6 us -> 6.77 us
    ppermute x21 -> x19, starting transfers between devices: 26 us -> 18 us  [swap(): return lax.ppermute(value, 'rows', [(r, r ^ 1 << bit) for r in range(n)])]
    all_to_all x1, waiting for transfers between devices: 8.25 us -> 12.8 us  [shards(): lax.all_to_all(ordered, 'rows', split_axis=0, concat_axis=0, tiled=True)]
    ppermute x21 -> x19, waiting for transfers between devices: 41.9 us -> 45.4 us  [swap(): return lax.ppermute(value, 'rows', [(r, r ^ 1 << bit) for r in range(n)])]
    dynamic_slice x0 -> x2, local copies, waits for them, and re-layouts: none -> 2.42 us  [part(): return lax.dynamic_slice_in_dim(value, index * size, size, axis)]
    all_to_all x1, starting transfers between devices: 6.59 us -> 7.96 us  [shards(): lax.all_to_all(ordered, 'rows', split_axis=0, concat_axis=0, tiled=True)]
    unnamed x15 -> x22, local copies, waits for them, and re-layouts: 1.42 us -> 2.6 us
  transfers between devices with their start and end apart: 22 -> 20, of which waited for: 15 -> 9; matrix products, arithmetic and copies ran while one was open for 7% -> 7% of each run, Pallas kernels for 4% -> 7%
where the time goes in v7:
time: 109 us
  waiting for transfers between devices  58.2 us (53%)
  starting transfers between devices  25.9 us (24%)
  Pallas kernels  10.4 us (10%)
  local copies, waits for them, and re-layouts  6.77 us (6%)
  other arithmetic  4.44 us (4%)
  matrix products  2.76 us (3%)
    ppermute x19, waiting for transfers between devices, swap(): return lax.ppermute(value, 'rows', [(r, r ^ 1 << bit) for r in range(n)])  45.4 us
    ppermute x19, starting transfers between devices, swap(): return lax.ppermute(value, 'rows', [(r, r ^ 1 << bit) for r in range(n)])  18 us
    all_to_all x1, waiting for transfers between devices, shards(): lax.all_to_all(ordered, 'rows', split_axis=0, concat_axis=0, tiled=True)  12.8 us
    all_to_all x1, starting transfers between devices, shards(): lax.all_to_all(ordered, 'rows', split_axis=0, concat_axis=0, tiled=True)  7.96 us
    pallas_call x2, Pallas kernels, product(): pl.pallas_call(product_kernel, in_specs=[pl.BlockSpec(memory_space=pltpu....  7.68 us
    unnamed x22, local copies, waits for them, and re-layouts  2.6 us
    dot_general x2, matrix products, shards(): lax.dot_general(both, value, (((1,), (1,)), ((), ())), preferred_element_...  2.5 us
    dynamic_slice x2, local copies, waits for them, and re-layouts, part(): return lax.dynamic_slice_in_dim(value, index * size, size, axis)  2.42 us
  transfers between devices with their start and end apart: 20, of which 9 were waited for; matrix products, arithmetic and copies ran while one was open for 7% of the time, Pallas kernels for 7%

profile of v7, /device:TPU:0, one launch (start us, length us, event | category | flops | bytes accessed | tf_op | source)
XLA Modules:
  0.0 109.0 jit_solution(14718466940026999148)
XLA Ops:
  0.0 2.3 %fusion.5 = (bf16[128,2048]{1,0:T(8,128)(2,1)}, bf16[128,2048]{1,0:T(8,128)(2,1)}) fusion(bf16[256,4096]{1,0:T(8,128)(2,1)} %bitcast.26, s32[]{:T(128)S(6)} %add.88, s32[]{:T(128)S(6)} %select_n.10), kind=kLoop, calls=%fused_computation.47 | loop fusion | bytes 2097160 | tf_op jit(solution)/shard_map/dynamic_slice | solution.py:156
  2.4 3.0 %collective-permute-start.9 = (bf16[128,2048]{1,0:T(8,128)(2,1)}, bf16[128,2048]{1,0:T(8,128)(2,1)S(1)}, u32[]{:S(2)}, u32[]{:S(2)}) collective-permute-start(bf16[128,2048]{1,0:T(8,128)(2,1)} %get-tuple-element.51), channel_id=1, source_target_pairs={{0,2},{1,3},{2,0},{3,1},{4,6},{5,7},{6,4},{7,5},{8,10},{9,11},{10,... | collective-permute-start | bytes 1572872 | tf_op jit(solution)/shard_map/ppermute | solution.py:143
  5.3 4.1 %shard_map.73 = (f32[128,4096]{1,0:T(8,128)S(1)}, f32[128,4096]{1,0:T(8,128)S(1)}) custom-call(s32[1]{0:T(128)} %bitcast.2.core_ref, f32[512,256]{1,0:T(8,128)S(1)} %copy-done.2, f32[256,4096]{1,0:T(8,128)} %columns_hbm.3), custom_call_target="tpu_custom_call" | custom-call | flops 1610612736 | bytes 8388608 | tf_op jit(solution)/shard_map/pallas_call | solution.py:59
  9.5 1.2 %multiply_convert_fusion.1 = f16[128,4096]{1,0:T(8,128)(2,1)} fusion(f32[128,4096]{1,0:T(8,128)S(1)} %get-tuple-element.23), kind=kLoop, calls=%fused_computation.3 | loop fusion | flops 1048576 | bytes 3145728 | tf_op jit(solution)/shard_map/convert_element_type | solution.py:149
  10.6 0.2 multiply_convert_fusion
  10.8 0.6 collective-permute-start
  11.4 2.2 %copy-done.1 = f32[256,4096]{1,0:T(8,128)S(1)} copy-done((f32[256,4096]{1,0:T(8,128)S(1)}, f32[256,4096]{1,0:T(8,128)}, u32[]{:S(2)}) %copy-start.1) | copy-done | bytes 4194328
  13.6 3.5 %shard_map.74 = (f32[128,4096]{1,0:T(8,128)S(1)}, f32[128,4096]{1,0:T(8,128)S(1)}) custom-call(s32[1]{0:T(128)} %bitcast.core_ref, f32[512,256]{1,0:T(8,128)S(1)} %copy-done.2, f32[256,4096]{1,0:T(8,128)S(1)} %copy-done.1), custom_call_target="tpu_custom_call" | custom-call | flops 1610612736 | bytes 8388608 | tf_op jit(solution)/shard_map/pallas_call | solution.py:59
  17.2 0.1 constant_dynamic-slice_fusion.2
  17.3 1.6 %multiply_add_fusion.1 = f32[128,4096]{1,0:T(8,128)S(1)} fusion(f32[128,4096]{1,0:T(8,128)S(1)} %get-tuple-element.27, f16[128,4096]{1,0:T(8,128)(2,1)} %collective-permute-done.1), kind=kLoop, calls=%fused_computation.1 | loop fusion | flops 1572864 | bytes 5242880 | tf_op jit(solution)/shard_map/add | solution.py:174
  18.8 0.2 fusion.7
  19.2 2.1 %collective-permute-start.3 = (f16[32,4096]{1,0:T(8,128)(2,1)S(1)}, f16[32,4096]{1,0:T(8,128)(2,1)S(1)}, u32[]{:S(2)}, u32[]{:S(2)}) collective-permute-start(f16[32,4096]{1,0:T(8,128)(2,1)S(1)} %multiply_convert_fusion.6), channel_id=1, source_target_pairs={{0,4},{1,5},{2,6},{3,7},{4,0},{5,1},{6,2},{7,3},{8,12},{9,13},{10,... | collective-permute-start | bytes 786440 | tf_op jit(solution)/shard_map/ppermute | solution.py:143
  21.4 0.3 multiply_add_fusion
  21.7 0.2 fusion.6
  22.0 5.6 %collective-permute-done.3 = f16[32,4096]{1,0:T(8,128)(2,1)S(1)} collective-permute-done((f16[32,4096]{1,0:T(8,128)(2,1)S(1)}, f16[32,4096]{1,0:T(8,128)(2,1)S(1)}, u32[]{:S(2)}, u32[]{:S(2)}) %collective-permute-start.3) | collective-permute-done | bytes 262176 | tf_op jit(solution)/shard_map/ppermute | solution.py:143
  27.6 0.1 multiply_add_fusion.4
  27.7 1.7 %collective-permute-start.11 = (f16[32,2048]{1,0:T(8,128)(2,1)S(1)}, f16[32,2048]{1,0:T(8,128)(2,1)S(1)}, u32[]{:S(2)}, u32[]{:S(2)}) collective-permute-start(f16[32,2048]{1,0:T(8,128)(2,1)S(1)} %multiply_convert_fusion.10), channel_id=1, source_target_pairs={{0,2},{1,3},{2,0},{3,1},{4,6},{5,7},{6,4},{7,5},{8,10},{9,11},{10,... | collective-permute-start | bytes 393224 | tf_op jit(solution)/shard_map/ppermute | solution.py:143
  29.4 0.1 multiply_add_fusion.5
  29.6 1.7 %collective-permute-start.10 = (f16[32,2048]{1,0:T(8,128)(2,1)S(1)}, f16[32,2048]{1,0:T(8,128)(2,1)S(1)}, u32[]{:S(2)}, u32[]{:S(2)}) collective-permute-start(f16[32,2048]{1,0:T(8,128)(2,1)S(1)} %multiply_convert_fusion.11), channel_id=1, source_target_pairs={{0,4},{1,5},{2,6},{3,7},{4,0},{5,1},{6,2},{7,3},{8,12},{9,13},{10,... | collective-permute-start | bytes 393224 | tf_op jit(solution)/shard_map/ppermute | solution.py:143
  31.2 0.4 collective-permute-start.6
  31.7 0.4 collective-permute-start.4
  32.0 1.3 %collective-permute-done.11 = f16[32,2048]{1,0:T(8,128)(2,1)S(1)} collective-permute-done((f16[32,2048]{1,0:T(8,128)(2,1)S(1)}, f16[32,2048]{1,0:T(8,128)(2,1)S(1)}, u32[]{:S(2)}, u32[]{:S(2)}) %collective-permute-start.11) | collective-permute-done | bytes 131104 | tf_op jit(solution)/shard_map/ppermute | solution.py:143
  33.4 2.7 %collective-permute-done.10 = f16[32,2048]{1,0:T(8,128)(2,1)S(1)} collective-permute-done((f16[32,2048]{1,0:T(8,128)(2,1)S(1)}, f16[32,2048]{1,0:T(8,128)(2,1)S(1)}, u32[]{:S(2)}, u32[]{:S(2)}) %collective-permute-start.10) | collective-permute-done | bytes 131104 | tf_op jit(solution)/shard_map/ppermute | solution.py:143
  36.2 2.7 %collective-permute-start.15 = (f16[2,32,2048]{2,1,0:T(8,128)(2,1)S(1)}, f16[2,32,2048]{2,1,0:T(8,128)(2,1)S(1)}, u32[]{:S(2)}, u32[]{:S(2)}) collective-permute-start(f16[2,32,2048]{2,1,0:T(8,128)(2,1)S(1)} %get-tuple-element.57), channel_id=1, source_target_pairs={{0,8},{1,9},{2,10},{3,11},{4,12},{5,13},{6,14},{7,15},{8,0},{9,1},... | collective-permute-start | bytes 786440 | tf_op jit(solution)/shard_map/ppermute | solution.py:143
  38.9 0.6 collective-permute-start.13
  39.4 0.1 constant_dynamic-update-slice_fusion.5
  39.5 3.8 %collective-permute-done.6 = f16[32,4096]{1,0:T(8,128)(2,1)S(1)} collective-permute-done((f16[32,4096]{1,0:T(8,128)(2,1)S(1)}, f16[32,4096]{1,0:T(8,128)(2,1)S(1)}, u32[]{:S(2)}, u32[]{:S(2)}) %collective-permute-start.6) | collective-permute-done | bytes 262176 | tf_op jit(solution)/shard_map/ppermute | solution.py:143
  43.5 1.0 collective-permute-start.7
  44.5 0.1 multiply_add_fusion.3
  44.6 11.4 %collective-permute-done.7 = f16[32,2048]{1,0:T(8,128)(2,1)S(1)} collective-permute-done((f16[32,2048]{1,0:T(8,128)(2,1)S(1)}, f16[32,2048]{1,0:T(8,128)(2,1)S(1)}, u32[]{:S(2)}, u32[]{:S(2)}) %collective-permute-start.7) | collective-permute-done | bytes 131104 | tf_op jit(solution)/shard_map/ppermute | solution.py:143
  56.0 1.6 %collective-permute-start.5 = (f16[32,2048]{1,0:T(8,128)(2,1)S(1)}, f16[32,2048]{1,0:T(8,128)(2,1)S(1)}, u32[]{:S(2)}, u32[]{:S(2)}) collective-permute-start(f16[32,2048]{1,0:T(8,128)(2,1)S(1)} %multiply_convert_fusion.9), channel_id=1, source_target_pairs={{0,4},{1,5},{2,6},{3,7},{4,0},{5,1},{6,2},{7,3},{8,12},{9,13},{10,... | collective-permute-start | bytes 393224 | tf_op jit(solution)/shard_map/ppermute | solution.py:143
  57.6 3.4 %collective-permute-done.5 = f16[32,2048]{1,0:T(8,128)(2,1)S(1)} collective-permute-done((f16[32,2048]{1,0:T(8,128)(2,1)S(1)}, f16[32,2048]{1,0:T(8,128)(2,1)S(1)}, u32[]{:S(2)}, u32[]{:S(2)}) %collective-permute-start.5) | collective-permute-done | bytes 131104 | tf_op jit(solution)/shard_map/ppermute | solution.py:143
  61.2 0.4 collective-permute-start.8
  61.6 0.1 add_convert_fusion
  61.7 1.6 %collective-permute-start.17 = (bf16[2,32,2048]{2,1,0:T(8,128)(2,1)S(1)}, bf16[2,32,2048]{2,1,0:T(8,128)(2,1)S(1)}, u32[]{:S(2)}, u32[]{:S(2)}) collective-permute-start(bf16[2,32,2048]{2,1,0:T(8,128)(2,1)S(1)} %add_convert_fusion), channel_id=1, source_target_pairs={{0,4},{1,5},{2,6},{3,7},{4,0},{5,1},{6,2},{7,3},{8,12},{9,13},{10,... | collective-permute-start | bytes 786440 | tf_op jit(solution)/shard_map/ppermute | solution.py:143
  63.4 11.4 %collective-permute-done.8 = f16[2,32,2048]{2,1,0:T(8,128)(2,1)S(1)} collective-permute-done((f16[2,32,2048]{2,1,0:T(8,128)(2,1)S(1)}, f16[2,32,2048]{2,1,0:T(8,128)(2,1)S(1)}, u32[]{:S(2)}, u32[]{:S(2)}) %collective-permute-start.8) | collective-permute-done | bytes 262176 | tf_op jit(solution)/shard_map/ppermute | solution.py:143
  75.4 1.3 %fusion.8.refs_0_ = f32[1024,128]{1,0:T(8,128)S(1)} fusion(bf16[1024,2048]{1,0:T(8,128)(2,1)S(1)} %constant_dynamic-update-slice_fusion, bf16[128,2048]{1,0:T(8,128)(2,1)S(1)} %bitcast.25), kind=kOutput, calls=%fused_computation.50 | convolution fusion | flops 536870912 | bytes 5242880 | tf_op jit(solution)/shard_map/dot_general | solution.py:231
  76.7 5.7 %collective-permute-done.18 = bf16[2,32,2048]{2,1,0:T(8,128)(2,1)S(1)} collective-permute-done((bf16[2,32,2048]{2,1,0:T(8,128)(2,1)S(1)}, bf16[2,32,2048]{2,1,0:T(8,128)(2,1)S(1)}, u32[]{:S(2)}, u32[]{:S(2)}) %collective-permute-start.18) | collective-permute-done | bytes 262176 | tf_op jit(solution)/shard_map/ppermute | solution.py:143
  82.5 1.2 %fusion.9.refs_1_ = f32[1024,128]{1,0:T(8,128)S(1)} fusion(bf16[1024,2048]{1,0:T(8,128)(2,1)S(1)} %constant_dynamic-update-slice_fusion, bf16[128,2048]{1,0:T(8,128)(2,1)S(1)} %bitcast.24), kind=kOutput, calls=%fused_computation.51 | convolution fusion | flops 536870912 | bytes 5242880 | tf_op jit(solution)/shard_map/dot_general | solution.py:231
  83.8 1.9 %shard_map.75 = bf16[16,64,256]{2,1,0:T(8,128)(2,1)} custom-call(s32[16]{0:T(128)S(1)} %copy-done, f32[1024,128]{1,0:T(8,128)S(1)} %fusion.8.refs_0_, f32[1024,128]{1,0:T(8,128)S(1)} %fusion.9.refs_1_), custom_call_target="tpu_custom_call" | custom-call | flops 131072 | bytes 1572864 | tf_op jit(solution)/shard_map/pallas_call | solution.py:94
  85.7 8.0 %all-to-all-start = ((bf16[16,1,64,256]{3,2,1,0:T(8,128)(2,1)}), bf16[16,1,64,256]{3,2,1,0:T(8,128)(2,1)S(1)}, u32[]{:S(2)}, u32[]{:S(2)}) async-start(bf16[16,1,64,256]{3,2,1,0:T(8,128)(2,1)} %bitcast.10), calls=%async_computation | async-start | bytes 1048576 | tf_op jit(solution)/shard_map/all_to_all | solution.py:236
  93.6 0.1 copy.12
  93.7 0.6 dynamic_slice.83
  94.3 0.1 fusion.3
  94.4 0.3 fusion
  94.7 0.6 constant_dynamic-slice_fusion.1.allowed_ref
  95.3 12.8 %all-to-all-done = bf16[16,1,64,256]{3,2,1,0:T(8,128)(2,1)S(1)} async-done(((bf16[16,1,64,256]{3,2,1,0:T(8,128)(2,1)}), bf16[16,1,64,256]{3,2,1,0:T(8,128)(2,1)S(1)}, u32[]{:S(2)}, u32[]{:S(2)}) %all-to-all-start) | async-done | bytes 524320 | tf_op jit(solution)/shard_map/all_to_all | solution.py:236
  108.1 0.9 shard_map.76
  (60 shorter events, 1.5 us)
Async XLA Ops:
  0.0 5.3 %copy-start.2 = (f32[512,256]{1,0:T(8,128)S(1)}, f32[512,256]{1,0:T(8,128)}, u32[]{:S(2)}) copy-start(f32[512,256]{1,0:T(8,128)} %rows_ref.1) | copy-start | bytes 1572868
  2.4 36.5 %collective-permute-start.9 = (bf16[128,2048]{1,0:T(8,128)(2,1)}, bf16[128,2048]{1,0:T(8,128)(2,1)S(1)}, u32[]{:S(2)}, u32[]{:S(2)}) collective-permute-start(bf16[128,2048]{1,0:T(8,128)(2,1)} %get-tuple-element.51), channel_id=1, source_target_pairs={{0,2},{1,3},{2,0},{3,1},{4,6},{5,7},{6,4},{7,5},{8,10},{9,11},{10,... | collective-permute-start | bytes 1572872 | tf_op jit(solution)/shard_map/ppermute | solution.py:143
  10.6 6.6 %collective-permute-start.1 = (f16[128,4096]{1,0:T(8,128)(2,1)}, f16[128,4096]{1,0:T(8,128)(2,1)}, u32[]{:S(2)}, u32[]{:S(2)}) collective-permute-start(f16[128,4096]{1,0:T(8,128)(2,1)} %multiply_convert_fusion.1), channel_id=1, source_target_pairs={{0,1},{1,0},{2,3},{3,2},{4,5},{5,4},{6,7},{7,6},{8,9},{9,8},{10,11... | collective-permute-start | bytes 3145736 | tf_op jit(solution)/shard_map/ppermute | solution.py:143
  10.8 10.5 %collective-permute-start = (f16[128,4096]{1,0:T(8,128)(2,1)S(1)}, f16[128,4096]{1,0:T(8,128)(2,1)S(1)}, u32[]{:S(2)}, u32[]{:S(2)}) collective-permute-start(f16[128,4096]{1,0:T(8,128)(2,1)S(1)} %multiply_convert_fusion), channel_id=1, source_target_pairs={{0,1},{1,0},{2,3},{3,2},{4,5},{5,4},{6,7},{7,6},{8,9},{9,8},{10,11... | collective-permute-start | bytes 3145736 | tf_op jit(solution)/shard_map/ppermute | solution.py:143
  11.4 2.2 %copy-start.1 = (f32[256,4096]{1,0:T(8,128)S(1)}, f32[256,4096]{1,0:T(8,128)}, u32[]{:S(2)}) copy-start(f32[256,4096]{1,0:T(8,128)} %columns_hbm.3) | copy-start | bytes 12582916
  13.6 3.5 %copy-start.3 = (bf16[16,16,4096]{2,1,0:T(8,128)(2,1)S(1)}, bf16[16,16,4096]{2,1,0:T(8,128)(2,1)}, u32[]{:S(2)}) copy-start(bf16[16,16,4096]{2,1,0:T(8,128)(2,1)} %param.9) | copy-start | bytes 6291460
  19.1 10.4 %collective-permute-start.2 = (f16[64,2048]{1,0:T(8,128)(2,1)S(1)}, f16[64,2048]{1,0:T(8,128)(2,1)S(1)}, u32[]{:S(2)}, u32[]{:S(2)}) collective-permute-start(f16[64,2048]{1,0:T(8,128)(2,1)S(1)} %multiply_convert_fusion.7), channel_id=1, source_target_pairs={{0,2},{1,3},{2,0},{3,1},{4,6},{5,7},{6,4},{7,5},{8,10},{9,11},{10,... | collective-permute-start | bytes 786440 | tf_op jit(solution)/shard_map/ppermute | solution.py:143
  19.2 8.3 %collective-permute-start.3 = (f16[32,4096]{1,0:T(8,128)(2,1)S(1)}, f16[32,4096]{1,0:T(8,128)(2,1)S(1)}, u32[]{:S(2)}, u32[]{:S(2)}) collective-permute-start(f16[32,4096]{1,0:T(8,128)(2,1)S(1)} %multiply_convert_fusion.6), channel_id=1, source_target_pairs={{0,4},{1,5},{2,6},{3,7},{4,0},{5,1},{6,2},{7,3},{8,12},{9,13},{10,... | collective-permute-start | bytes 786440 | tf_op jit(solution)/shard_map/ppermute | solution.py:143
  27.7 11.2 %copy-start.4 = (bf16[128,2048]{1,0:T(8,128)(2,1)S(1)}, bf16[128,2048]{1,0:T(8,128)(2,1)}, u32[]{:S(2)}) copy-start(bf16[128,2048]{1,0:T(8,128)(2,1)} %get-tuple-element.33) | copy-start | bytes 1572868
  27.7 5.6 %collective-permute-start.11 = (f16[32,2048]{1,0:T(8,128)(2,1)S(1)}, f16[32,2048]{1,0:T(8,128)(2,1)S(1)}, u32[]{:S(2)}, u32[]{:S(2)}) collective-permute-start(f16[32,2048]{1,0:T(8,128)(2,1)S(1)} %multiply_convert_fusion.10), channel_id=1, source_target_pairs={{0,2},{1,3},{2,0},{3,1},{4,6},{5,7},{6,4},{7,5},{8,10},{9,11},{10,... | collective-permute-start | bytes 393224 | tf_op jit(solution)/shard_map/ppermute | solution.py:143
  29.6 6.5 %collective-permute-start.10 = (f16[32,2048]{1,0:T(8,128)(2,1)S(1)}, f16[32,2048]{1,0:T(8,128)(2,1)S(1)}, u32[]{:S(2)}, u32[]{:S(2)}) collective-permute-start(f16[32,2048]{1,0:T(8,128)(2,1)S(1)} %multiply_convert_fusion.11), channel_id=1, source_target_pairs={{0,4},{1,5},{2,6},{3,7},{4,0},{5,1},{6,2},{7,3},{8,12},{9,13},{10,... | collective-permute-start | bytes 393224 | tf_op jit(solution)/shard_map/ppermute | solution.py:143
  31.2 12.1 %collective-permute-start.6 = (f16[32,4096]{1,0:T(8,128)(2,1)S(1)}, f16[32,4096]{1,0:T(8,128)(2,1)S(1)}, u32[]{:S(2)}, u32[]{:S(2)}) collective-permute-start(f16[32,4096]{1,0:T(8,128)(2,1)S(1)} %multiply_convert_fusion.4), channel_id=1, source_target_pairs={{0,4},{1,5},{2,6},{3,7},{4,0},{5,1},{6,2},{7,3},{8,12},{9,13},{10,... | collective-permute-start | bytes 786440 | tf_op jit(solution)/shard_map/ppermute | solution.py:143
  31.7 11.8 %collective-permute-start.4 = (f16[64,2048]{1,0:T(8,128)(2,1)S(1)}, f16[64,2048]{1,0:T(8,128)(2,1)S(1)}, u32[]{:S(2)}, u32[]{:S(2)}) collective-permute-start(f16[64,2048]{1,0:T(8,128)(2,1)S(1)} %multiply_convert_fusion.5), channel_id=1, source_target_pairs={{0,2},{1,3},{2,0},{3,1},{4,6},{5,7},{6,4},{7,5},{8,10},{9,11},{10,... | collective-permute-start | bytes 786440 | tf_op jit(solution)/shard_map/ppermute | solution.py:143
  36.2 25.4 %collective-permute-start.15 = (f16[2,32,2048]{2,1,0:T(8,128)(2,1)S(1)}, f16[2,32,2048]{2,1,0:T(8,128)(2,1)S(1)}, u32[]{:S(2)}, u32[]{:S(2)}) collective-permute-start(f16[2,32,2048]{2,1,0:T(8,128)(2,1)S(1)} %get-tuple-element.57), channel_id=1, source_target_pairs={{0,8},{1,9},{2,10},{3,11},{4,12},{5,13},{6,14},{7,15},{8,0},{9,1},... | collective-permute-start | bytes 786440 | tf_op jit(solution)/shard_map/ppermute | solution.py:143
  38.9 36.2 %collective-permute-start.12 = (bf16[256,2048]{1,0:T(8,128)(2,1)S(1)}, bf16[256,2048]{1,0:T(8,128)(2,1)S(1)}, u32[]{:S(2)}, u32[]{:S(2)}) collective-permute-start(bf16[256,2048]{1,0:T(8,128)(2,1)S(1)} %constant_dynamic-slice_fusion.2), channel_id=1, source_target_pairs={{0,1},{1,0},{2,3},{3,2},{4,5},{5,4},{6,7},{7,6},{8,9},{9,8},{10,11... | collective-permute-start | bytes 3145736 | tf_op jit(solution)/shard_map/ppermute | solution.py:143
  38.9 22.8 %collective-permute-start.13 = (bf16[128,2048]{1,0:T(8,128)(2,1)S(1)}, bf16[128,2048]{1,0:T(8,128)(2,1)S(1)}, u32[]{:S(2)}, u32[]{:S(2)}) collective-permute-start(bf16[128,2048]{1,0:T(8,128)(2,1)S(1)} %copy-done.4), channel_id=1, source_target_pairs={{0,2},{1,3},{2,0},{3,1},{4,6},{5,7},{6,4},{7,5},{8,10},{9,11},{10,... | collective-permute-start | bytes 1572872 | tf_op jit(solution)/shard_map/ppermute | solution.py:143
  43.4 31.8 %collective-permute-start.14 = (bf16[128,2048]{1,0:T(8,128)(2,1)S(1)}, bf16[128,2048]{1,0:T(8,128)(2,1)S(1)}, u32[]{:S(2)}, u32[]{:S(2)}) collective-permute-start(bf16[128,2048]{1,0:T(8,128)(2,1)S(1)} %collective-permute-done.9), channel_id=1, source_target_pairs={{0,1},{1,0},{2,3},{3,2},{4,5},{5,4},{6,7},{7,6},{8,9},{9,8},{10,11... | collective-permute-start | bytes 1572872 | tf_op jit(solution)/shard_map/ppermute | solution.py:143
  43.5 12.5 %collective-permute-start.7 = (f16[32,2048]{1,0:T(8,128)(2,1)S(1)}, f16[32,2048]{1,0:T(8,128)(2,1)S(1)}, u32[]{:S(2)}, u32[]{:S(2)}) collective-permute-start(f16[32,2048]{1,0:T(8,128)(2,1)S(1)} %multiply_convert_fusion.8), channel_id=1, source_target_pairs={{0,2},{1,3},{2,0},{3,1},{4,6},{5,7},{6,4},{7,5},{8,10},{9,11},{10,... | collective-permute-start | bytes 393224 | tf_op jit(solution)/shard_map/ppermute | solution.py:143
  56.0 5.1 %collective-permute-start.5 = (f16[32,2048]{1,0:T(8,128)(2,1)S(1)}, f16[32,2048]{1,0:T(8,128)(2,1)S(1)}, u32[]{:S(2)}, u32[]{:S(2)}) collective-permute-start(f16[32,2048]{1,0:T(8,128)(2,1)S(1)} %multiply_convert_fusion.9), channel_id=1, source_target_pairs={{0,4},{1,5},{2,6},{3,7},{4,0},{5,1},{6,2},{7,3},{8,12},{9,13},{10,... | collective-permute-start | bytes 393224 | tf_op jit(solution)/shard_map/ppermute | solution.py:143
  61.2 13.6 %collective-permute-start.8 = (f16[2,32,2048]{2,1,0:T(8,128)(2,1)S(1)}, f16[2,32,2048]{2,1,0:T(8,128)(2,1)S(1)}, u32[]{:S(2)}, u32[]{:S(2)}) collective-permute-start(f16[2,32,2048]{2,1,0:T(8,128)(2,1)S(1)} %multiply_convert_fusion.3), channel_id=1, source_target_pairs={{0,8},{1,9},{2,10},{3,11},{4,12},{5,13},{6,14},{7,15},{8,0},{9,1},... | collective-permute-start | bytes 786440 | tf_op jit(solution)/shard_map/ppermute | solution.py:143
  61.7 13.6 %collective-permute-start.16 = (bf16[128,2048]{1,0:T(8,128)(2,1)S(1)}, bf16[128,2048]{1,0:T(8,128)(2,1)S(1)}, u32[]{:S(2)}, u32[]{:S(2)}) collective-permute-start(bf16[128,2048]{1,0:T(8,128)(2,1)S(1)} %collective-permute-done.13), channel_id=1, source_target_pairs={{0,1},{1,0},{2,3},{3,2},{4,5},{5,4},{6,7},{7,6},{8,9},{9,8},{10,11... | collective-permute-start | bytes 1572872 | tf_op jit(solution)/shard_map/ppermute | solution.py:143
  61.7 13.2 %collective-permute-start.17 = (bf16[2,32,2048]{2,1,0:T(8,128)(2,1)S(1)}, bf16[2,32,2048]{2,1,0:T(8,128)(2,1)S(1)}, u32[]{:S(2)}, u32[]{:S(2)}) collective-permute-start(bf16[2,32,2048]{2,1,0:T(8,128)(2,1)S(1)} %add_convert_fusion), channel_id=1, source_target_pairs={{0,4},{1,5},{2,6},{3,7},{4,0},{5,1},{6,2},{7,3},{8,12},{9,13},{10,... | collective-permute-start | bytes 786440 | tf_op jit(solution)/shard_map/ppermute | solution.py:143
  75.3 7.1 %collective-permute-start.18 = (bf16[2,32,2048]{2,1,0:T(8,128)(2,1)S(1)}, bf16[2,32,2048]{2,1,0:T(8,128)(2,1)S(1)}, u32[]{:S(2)}, u32[]{:S(2)}) collective-permute-start(bf16[2,32,2048]{2,1,0:T(8,128)(2,1)S(1)} %add_convert_fusion.1), channel_id=1, source_target_pairs={{0,4},{1,5},{2,6},{3,7},{4,0},{5,1},{6,2},{7,3},{8,12},{9,13},{10,... | collective-permute-start | bytes 786440 | tf_op jit(solution)/shard_map/ppermute | solution.py:143
  82.5 1.3 %copy-start = (s32[16]{0:T(128)S(1)}, s32[16]{0:T(128)}, u32[]{:S(2)}) copy-start(s32[16]{0:T(128)} %slots_ref.1) | copy-start | bytes 196
  83.8 9.9 %copy-start.5 = (s32[8,12]{1,0:T(8,128)S(1)}, s32[8,12]{1,0:T(8,128)}, u32[]{:S(2)}) copy-start(s32[8,12]{1,0:T(8,128)} %param.11) | copy-start | bytes 1156
  83.8 10.5 %copy-start.6 = (s32[8]{0:T(128)S(1)}, s32[8]{0:T(128)}, u32[]{:S(2)}) copy-start(s32[8]{0:T(128)} %param.12) | copy-start | bytes 100
  83.8 10.6 %copy-start.7 = (s32[512]{0:T(512)S(1)}, s32[512]{0:T(512)}, u32[]{:S(2)}) copy-start(s32[512]{0:T(512)} %param.10) | copy-start | bytes 6148
  85.7 22.4 %all-to-all-start = ((bf16[16,1,64,256]{3,2,1,0:T(8,128)(2,1)}), bf16[16,1,64,256]{3,2,1,0:T(8,128)(2,1)S(1)}, u32[]{:S(2)}, u32[]{:S(2)}) async-start(bf16[16,1,64,256]{3,2,1,0:T(8,128)(2,1)} %bitcast.10), calls=%async_computation | async-start | bytes 1048576 | tf_op jit(solution)/shard_map/all_to_all | solution.py:236

commit v8 on v7

--- a/solution.py
+++ b/solution.py
@@ -10,8 +10,8 @@
 PATHS = 2
 UNIT = 4.0
 LANES = 128
-OTHER_VMEM = 48
-MINE_VMEM = 44
+OTHER_VMEM = 43
+MINE_VMEM = 16
 
 
 def listed_mask(query_cluster, cand_blocks, cand_count, nblocks):
@@ -23,8 +23,27 @@
     return jnp.dot(listed.T, onehot.T, preferred_element_type=jnp.float32)
 
 
-def product_kernel(core_ref, rows_ref, columns_hbm, *refs):
-    outs, (columns_ref, sems) = refs[:-2], refs[-2:]
+def split(value):
+    high = value.astype(jnp.bfloat16)
+    return high, (value - high.astype(jnp.float32)).astype(jnp.bfloat16)
+
+
+def rows_of(core_ref, rows_ref):
+    half = rows_ref.shape[0] // CORES
+    high, low = split(rows_ref[pl.ds(pl.multiple_of(core_ref[0] * half, half), half), :])
+    return jnp.concatenate([high, low, high], axis=1)
+
+
+def multiply(left, high, low, outs, columns):
+    right = jnp.concatenate([high, high, low], axis=0)
+    result = jnp.dot(left, right, preferred_element_type=jnp.float32)
+    part = result.shape[0] // len(outs)
+    for chunk, out_ref in enumerate(outs):
+        out_ref[:, columns] = result[chunk * part:(chunk + 1) * part]
+
+
+def other_kernel(core_ref, rows_ref, columns_hbm, *refs):
+    outs, (high_ref, low_ref, columns_ref, sems) = refs[:-4], refs[-4:]
     steps, _, block = columns_ref.shape
 
     def load(i):
@@ -34,70 +53,81 @@
 
     for i in range(steps):
         load(i).start()
-    half = rows_ref.shape[0] // CORES
-    rows = rows_ref[pl.ds(pl.multiple_of(core_ref[0] * half, half), half), :]
-    high = rows.astype(jnp.bfloat16)
-    low = (rows - high.astype(jnp.float32)).astype(jnp.bfloat16)
-    left = jnp.concatenate([high, low, high], axis=1)
-    part = half // len(outs)
+    left = rows_of(core_ref, rows_ref)
     for i in range(steps):
         load(i).wait()
-        columns = columns_ref[i]
-        high = columns.astype(jnp.bfloat16)
-        low = (columns - high.astype(jnp.float32)).astype(jnp.bfloat16)
-        right = jnp.concatenate([high, high, low], axis=0)
-        result = jnp.dot(left, right, preferred_element_type=jnp.float32)
-        for chunk, out_ref in enumerate(outs):
-            out_ref[:, i * block:(i + 1) * block] = result[chunk * part:(chunk + 1) * part]
-
-
-def product(core, rows, columns, vmem):
+        columns = slice(i * block, (i + 1) * block)
+        high, low = split(columns_ref[i])
+        high_ref[:, columns] = high
+        low_ref[:, columns] = low
+        multiply(left, high, low, outs, columns)
+
+
+def mine_kernel(core_ref, rows_ref, high_ref, low_ref, *outs):
+    left = rows_of(core_ref, rows_ref)
+    width = high_ref.shape[1]
+    block = min(512, width)
+    for i in range(width // block):
+        columns = slice(i * block, (i + 1) * block)
+        multiply(left, high_ref[:, columns], low_ref[:, columns], outs, columns)
+
+
+def product(core, rows, columns, kernel, vmem):
+    first = kernel is other_kernel
     nrows, depth = rows.shape
-    width = columns.shape[1]
+    width = columns[0].shape[1]
     block = min(512, width)
     part = nrows // CORES // CHUNKS
+    out = [jax.ShapeDtypeStruct((part, width), jnp.float32)] * CHUNKS
+    if first:
+        out = out + [jax.ShapeDtypeStruct((depth, width), jnp.bfloat16)] * 2
+    vmem_spec = pl.BlockSpec(memory_space=pltpu.VMEM)
     return pl.pallas_call(
-        product_kernel,
-        in_specs=[
-            pl.BlockSpec(memory_space=pltpu.SMEM),
-            pl.BlockSpec(memory_space=pltpu.VMEM),
-            pl.BlockSpec(memory_space=pltpu.HBM),
-        ],
-        out_specs=[pl.BlockSpec(memory_space=pltpu.VMEM)] * CHUNKS,
-        out_shape=[jax.ShapeDtypeStruct((part, width), jnp.float32)] * CHUNKS,
+        kernel,
+        in_specs=[pl.BlockSpec(memory_space=pltpu.SMEM), vmem_spec]
+        + [pl.BlockSpec(memory_space=pltpu.HBM) if first else vmem_spec] * len(columns),
+        out_specs=[vmem_spec] * len(out),
+        out_shape=out,
         scratch_shapes=[
             pltpu.VMEM((width // block, depth, block), jnp.float32),
             pltpu.SemaphoreType.DMA((width // block,)),
-        ],
+        ] if first else [],
         compiler_params=pltpu.CompilerParams(vmem_limit_bytes=vmem * 1024 * 1024),
         cost_estimate=pl.CostEstimate(
             flops=3 * nrows * depth * width,
             bytes_accessed=4 * width * depth + 2 * width * nrows,
             transcendentals=0,
         ),
-    )(core.reshape(1), rows, columns)
+    )(core.reshape(1), rows, *columns)
 
 
 def order_kernel(slots_ref, *refs):
     raws, out_ref = refs[:-1], refs[-1]
-    nblocks, examples, _ = out_ref.shape
+    nblocks = slots_ref.shape[0]
+    groups = len(raws) // CHUNKS
     for slot in range(nblocks):
-        rows = pl.ds(slots_ref[slot], examples, stride=nblocks)
         for i, raw_ref in enumerate(raws):
-            width = raw_ref.shape[1]
-            out_ref[slot, :, i * width:(i + 1) * width] = raw_ref[rows, :].astype(out_ref.dtype)
+            examples, width = raw_ref.shape[0] // nblocks, raw_ref.shape[1]
+            chunk, group = divmod(i, groups)
+            rows = pl.ds(slots_ref[slot], examples, stride=nblocks)
+            out_ref[
+                slot, group * examples:(group + 1) * examples, chunk * width:(chunk + 1) * width
+            ] = raw_ref[rows, :].astype(out_ref.dtype)
 
 
 def in_slot_order(raws, slots):
     nblocks = slots.shape[0]
     rows, width = raws[0].shape
+    groups = len(raws) // CHUNKS
     return pl.pallas_call(
         order_kernel,
-        in_specs=[pl.BlockSpec(memory_space=pltpu.SMEM)] + [pl.BlockSpec(memory_space=pltpu.VMEM)] * CHUNKS,
+        in_specs=[pl.BlockSpec(memory_space=pltpu.SMEM)] + [pl.BlockSpec(memory_space=pltpu.VMEM)] * len(raws),
         out_specs=pl.BlockSpec(memory_space=pltpu.VMEM),
-        out_shape=jax.ShapeDtypeStruct((nblocks, rows // nblocks, CHUNKS * width), jnp.bfloat16),
+        out_shape=jax.ShapeDtypeStruct((nblocks, groups * rows // nblocks, CHUNKS * width), jnp.bfloat16),
         compiler_params=pltpu.CompilerParams(vmem_limit_bytes=4 * 1024 * 1024),
-        cost_estimate=pl.CostEstimate(flops=rows * width, bytes_accessed=12 * rows * width, transcendentals=0),
+        cost_estimate=pl.CostEstimate(
+            flops=rows * width, bytes_accessed=6 * len(raws) * rows * width, transcendentals=0
+        ),
     )(slots, *raws)
 
 
@@ -196,15 +226,18 @@
         return value.reshape(-1, value.shape[-1])
 
     rows = train.reshape(examples * nblocks, width)
-    near = part(rows, side(ybit), 1)
     far = part(rows, 1 - side(ybit), 1)
     far = [part(far, i, 0) for i in range(2)]
-
     early = swap(far[0], ybit)
     queries = after(queries, far[0])
-    sent = [pack(value) for value in product(1 - core, queries, precond, OTHER_VMEM)]
+
+    *full, high, low = product(1 - core, queries, [precond], other_kernel, OTHER_VMEM)
+    sent = [pack(value) for value in full]
     got = [swap(value, 0) for value in sent]
-    mine = product(core, after(queries, sent[0]), precond, MINE_VMEM)
+    rows = after(rows, sent)
+    near = part(rows, side(ybit), 1)
+    sibling = swap(near, 0)
+    mine = product(after(core, sent), queries, [high, low], mine_kernel, MINE_VMEM)
     one = paths(mine[0], got[0])
     sent = messages(one, 0)
     two = paths(mine[1], after(got[1], sent))
@@ -212,24 +245,21 @@
     sent = messages(one, 1)
     two = exchange(two, after(messages(two, 0), sent), 0)
     one = halve(exchange(one, sent, 1))
-    sent = pack(one)
-    far[1], near, early = after((far[1], near, early), sent)
-    got_one = swap(sent, rest[-1])
+    got_one = swap(pack(one), rest[-1])
     two = halve(exchange(two, messages(two, 1), 1))
-    late = swap(far[1], ybit)
-    moved = [near, swap(near, 0), early, late, swap(early, 0)]
     sent = pack(two)
     one = (after(one, sent) + unpack(got_one)).astype(jnp.bfloat16)
     got_two = swap(sent, rest[-1])
-    one, late = after((one, late), sent)
-    both = jnp.concatenate(moved + [swap(late, 0)], axis=0)
+    late = swap(after(far[1], one), ybit)
     one = gather(one)
-    two, both = lax.optimization_barrier(((two + unpack(got_two)).astype(jnp.bfloat16), both))
-    two = gather(two)
+    far = jnp.concatenate([early, late], axis=0)
+    groups = [jnp.concatenate([near, sibling], axis=0), jnp.concatenate([far, swap(far, 0)], axis=0)]
+    two = gather((two + unpack(got_two)).astype(jnp.bfloat16))
 
     raws = [
-        lax.dot_general(both, value, (((1,), (1,)), ((), ())), preferred_element_type=jnp.float32)
+        lax.dot_general(group, value, (((1,), (1,)), ((), ())), preferred_element_type=jnp.float32)
         for value in (one, two)
+        for group in groups
     ]
     owned = nblocks // n
     ordered = in_slot_order(raws, slot_block).reshape(n, owned, 2 * CORES * examples, nq // CORES)

time: 109 us -> 97.7 us (0.90)
  waiting for transfers between devices: 58.2 us -> 37.8 us
  matrix products: 2.76 us -> 6.24 us
  starting transfers between devices: 25.9 us -> 28.8 us
  other arithmetic: 4.44 us -> 6.86 us
  local copies, waits for them, and re-layouts: 6.77 us -> 8.4 us
  Pallas kernels: 10.4 us -> 8.78 us
    ppermute x19 -> x18, waiting for transfers between devices: 45.4 us -> 25.1 us  [swap(): return lax.ppermute(value, 'rows', [(r, r ^ 1 << bit) for r in range(n)])]
    ppermute x19 -> x18, starting transfers between devices: 18 us -> 22.9 us  [swap(): return lax.ppermute(value, 'rows', [(r, r ^ 1 << bit) for r in range(n)])]
    dot_general x2 -> x4, matrix products: 2.5 us -> 5.98 us  [shards(): lax.dot_general(group, value, (((1,), (1,)), ((), ())), preferred_element...]
    dynamic_slice x2, local copies, waits for them, and re-layouts: 2.42 us -> 4.7 us  [part(): return lax.dynamic_slice_in_dim(value, index * size, size, axis)]
    all_to_all x1, starting transfers between devices: 7.96 us -> 5.89 us  [shards(): lax.all_to_all(ordered, 'rows', split_axis=0, concat_axis=0, tiled=True)]
    pallas_call x2, Pallas kernels: 7.68 us -> 6.04 us  [product(): pl.pallas_call(kernel, in_specs=[pl.BlockSpec(memory_space=pltpu.SMEM), v...]
    add x2, other arithmetic: 1.89 us -> 3.13 us  [paths(): value = value + unpack(other)]
    convert_element_type x11 -> x12, other arithmetic: 1.77 us -> 2.95 us  [pack(): return (value * UNIT).astype(jnp.float16)]
  transfers between devices with their start and end apart: 20 -> 19, of which waited for: 9 -> 12; matrix products, arithmetic and copies ran while one was open for 7% -> 16% of each run, Pallas kernels for 7% -> 6%
where the time goes in v8:
time: 97.7 us; the launch traced here: 97.3 us
  waiting for transfers between devices  37.8 us (39%)
  starting transfers between devices  28.8 us (29%)
  Pallas kernels  8.78 us (9%)
  local copies, waits for them, and re-layouts  8.4 us (9%)
  other arithmetic  6.86 us (7%)
  matrix products  6.24 us (6%)
    ppermute x18, waiting for transfers between devices, swap(): return lax.ppermute(value, 'rows', [(r, r ^ 1 << bit) for r in range(n)])  25.1 us
    ppermute x18, starting transfers between devices, swap(): return lax.ppermute(value, 'rows', [(r, r ^ 1 << bit) for r in range(n)])  22.9 us
    all_to_all x1, waiting for transfers between devices, shards(): lax.all_to_all(ordered, 'rows', split_axis=0, concat_axis=0, tiled=True)  12.7 us
    pallas_call x2, Pallas kernels, product(): pl.pallas_call(kernel, in_specs=[pl.BlockSpec(memory_space=pltpu.SMEM), v...  6.04 us
    dot_general x4, matrix products, shards(): lax.dot_general(group, value, (((1,), (1,)), ((), ())), preferred_element...  5.98 us
    all_to_all x1, starting transfers between devices, shards(): lax.all_to_all(ordered, 'rows', split_axis=0, concat_axis=0, tiled=True)  5.89 us
    dynamic_slice x2, local copies, waits for them, and re-layouts, part(): return lax.dynamic_slice_in_dim(value, index * size, size, axis)  4.7 us
    add x2, other arithmetic, paths(): value = value + unpack(other)  3.13 us
  transfers between devices with their start and end apart: 19, of which 12 were waited for; matrix products, arithmetic and copies ran while one was open for 16% of the time, Pallas kernels for 6%

profile of v8, /device:TPU:0, one launch (start us, length us, event | category | flops | bytes accessed | tf_op | source)
XLA Modules:
  0.0 97.3 jit_solution(9188491815315058105)
XLA Ops:
  0.0 2.4 %fusion.9 = (bf16[128,2048]{1,0:T(8,128)(2,1)}, bf16[128,2048]{1,0:T(8,128)(2,1)}) fusion(bf16[256,4096]{1,0:T(8,128)(2,1)} %bitcast.26, s32[]{:T(128)S(6)} %add.88, s32[]{:T(128)S(6)} %select_n.10), kind=kLoop, calls=%fused_computation.50 | loop fusion | bytes 2097160 | tf_op jit(solution)/shard_map/dynamic_slice | solution.py:186
  2.4 3.0 %collective-permute-start.13 = (bf16[128,2048]{1,0:T(8,128)(2,1)}, bf16[128,2048]{1,0:T(8,128)(2,1)S(1)}, u32[]{:S(2)}, u32[]{:S(2)}) collective-permute-start(bf16[128,2048]{1,0:T(8,128)(2,1)} %get-tuple-element.49), channel_id=1, source_target_pairs={{0,2},{1,3},{2,0},{3,1},{4,6},{5,7},{6,4},{7,5},{8,10},{9,11},{10,... | collective-permute-start | bytes 1572872 | tf_op jit(solution)/shard_map/ppermute | solution.py:173
  5.4 4.2 %shard_map.73 = (f32[128,4096]{1,0:T(8,128)S(1)}, f32[128,4096]{1,0:T(8,128)S(1)}, bf16[256,4096]{1,0:T(8,128)(2,1)S(1)}, bf16[256,4096]{1,0:T(8,128)(2,1)S(1)}) custom-call(s32[1]{0:T(128)} %bitcast.1.core_ref, f32[512,256]{1,0:T(8,128)S(1)} %copy-done.1, f32[256,4096]{1,0:T(8,128)} %columns_hbm.1), custom_call_target="tpu_custom_call" | custom-call | flops 1610612736 | bytes 8388608 | tf_op jit(solution)/shard_map/pallas_call | solution.py:85
  9.6 1.3 %multiply_convert_fusion.1 = f16[128,4096]{1,0:T(8,128)(2,1)} fusion(f32[128,4096]{1,0:T(8,128)S(1)} %get-tuple-element.20), kind=kLoop, calls=%fused_computation.4 | loop fusion | flops 1048576 | bytes 3145728 | tf_op jit(solution)/shard_map/convert_element_type | solution.py:179
  11.0 1.2 %multiply_convert_fusion = f16[128,4096]{1,0:T(8,128)(2,1)} fusion(f32[128,4096]{1,0:T(8,128)S(1)} %get-tuple-element.21), kind=kLoop, calls=%fused_computation.3 | loop fusion | flops 1048576 | bytes 3145728 | tf_op jit(solution)/shard_map/convert_element_type | solution.py:179
  12.1 0.5 collective-permute-start.6
  12.6 2.3 %constant_dynamic-slice_fusion.2 = bf16[256,2048]{1,0:T(8,128)(2,1)} fusion(bf16[256,4096]{1,0:T(8,128)(2,1)} %bitcast.27, s32[]{:T(128)S(6)} %select_n.11), kind=kLoop, calls=%fused_computation.46 | loop fusion | bytes 2097156 | tf_op jit(solution)/shard_map/dynamic_slice | solution.py:186
  15.0 1.6 %copy-done.3 = bf16[256,4096]{1,0:T(8,128)(2,1)S(1)} copy-done((bf16[256,4096]{1,0:T(8,128)(2,1)S(1)}, bf16[256,4096]{1,0:T(8,128)(2,1)}, u32[]{:S(2)}) %copy-start.3) | copy-done | bytes 2097176
  16.6 1.8 %shard_map.74 = (f32[128,4096]{1,0:T(8,128)S(1)}, f32[128,4096]{1,0:T(8,128)S(1)}) custom-call(s32[1]{0:T(128)} %bitcast.2.core_ref, f32[512,256]{1,0:T(8,128)S(1)} %copy-done.1, bf16[256,4096]{1,0:T(8,128)(2,1)S(1)} %get-tuple-element.24.high_ref, bf16[256,4096]{1,0:T(8,128)(2,1)S(1)} %copy-done.3), custom_call_target="tpu_custom_call" | custom-call | flops 1610612736 | bytes 8388608 | tf_op jit(solution)/shard_map/pallas_call | solution.py:85
  18.4 1.6 %multiply_add_fusion.1 = f32[128,4096]{1,0:T(8,128)S(1)} fusion(f32[128,4096]{1,0:T(8,128)S(1)} %get-tuple-element.26, f16[128,4096]{1,0:T(8,128)(2,1)} %collective-permute-done.1), kind=kLoop, calls=%fused_computation.2 | loop fusion | flops 1572864 | bytes 5242880 | tf_op jit(solution)/shard_map/add | solution.py:204
  19.9 0.2 fusion.11
  20.3 2.1 %collective-permute-start.4 = (f16[32,4096]{1,0:T(8,128)(2,1)S(1)}, f16[32,4096]{1,0:T(8,128)(2,1)S(1)}, u32[]{:S(2)}, u32[]{:S(2)}) collective-permute-start(f16[32,4096]{1,0:T(8,128)(2,1)S(1)} %multiply_convert_fusion.6), channel_id=1, source_target_pairs={{0,4},{1,5},{2,6},{3,7},{4,0},{5,1},{6,2},{7,3},{8,12},{9,13},{10,... | collective-permute-start | bytes 786440 | tf_op jit(solution)/shard_map/ppermute | solution.py:173
  22.4 1.6 %multiply_add_fusion = f32[128,4096]{1,0:T(8,128)S(1)} fusion(f32[128,4096]{1,0:T(8,128)S(1)} %get-tuple-element.27, f16[128,4096]{1,0:T(8,128)(2,1)} %collective-permute-done.6), kind=kLoop, calls=%fused_computation.1 | loop fusion | flops 1572864 | bytes 5242880 | tf_op jit(solution)/shard_map/add | solution.py:204
  24.0 0.2 fusion.10
  24.3 4.7 %collective-permute-done.2 = f16[64,2048]{1,0:T(8,128)(2,1)S(1)} collective-permute-done((f16[64,2048]{1,0:T(8,128)(2,1)S(1)}, f16[64,2048]{1,0:T(8,128)(2,1)S(1)}, u32[]{:S(2)}, u32[]{:S(2)}) %collective-permute-start.2) | collective-permute-done | bytes 262176 | tf_op jit(solution)/shard_map/ppermute | solution.py:173
  29.1 1.6 %collective-permute-start.3 = (f16[32,2048]{1,0:T(8,128)(2,1)S(1)}, f16[32,2048]{1,0:T(8,128)(2,1)S(1)}, u32[]{:S(2)}, u32[]{:S(2)}) collective-permute-start(f16[32,2048]{1,0:T(8,128)(2,1)S(1)} %multiply_convert_fusion.11), channel_id=1, source_target_pairs={{0,4},{1,5},{2,6},{3,7},{4,0},{5,1},{6,2},{7,3},{8,12},{9,13},{10,... | collective-permute-start | bytes 393224 | tf_op jit(solution)/shard_map/ppermute | solution.py:173
  30.8 0.6 collective-permute-start.5
  31.4 1.5 %collective-permute-start.7 = (f16[64,2048]{1,0:T(8,128)(2,1)S(1)}, f16[64,2048]{1,0:T(8,128)(2,1)S(1)}, u32[]{:S(2)}, u32[]{:S(2)}) collective-permute-start(f16[64,2048]{1,0:T(8,128)(2,1)S(1)} %multiply_convert_fusion.5), channel_id=1, source_target_pairs={{0,2},{1,3},{2,0},{3,1},{4,6},{5,7},{6,4},{7,5},{8,10},{9,11},{10,... | collective-permute-start | bytes 786440 | tf_op jit(solution)/shard_map/ppermute | solution.py:173
  32.9 1.4 %collective-permute-done.3 = f16[32,2048]{1,0:T(8,128)(2,1)S(1)} collective-permute-done((f16[32,2048]{1,0:T(8,128)(2,1)S(1)}, f16[32,2048]{1,0:T(8,128)(2,1)S(1)}, u32[]{:S(2)}, u32[]{:S(2)}) %collective-permute-start.3) | collective-permute-done | bytes 131104 | tf_op jit(solution)/shard_map/ppermute | solution.py:173
  34.3 1.6 %collective-permute-start.9 = (f16[32,4096]{1,0:T(8,128)(2,1)S(1)}, f16[32,4096]{1,0:T(8,128)(2,1)S(1)}, u32[]{:S(2)}, u32[]{:S(2)}) collective-permute-start(f16[32,4096]{1,0:T(8,128)(2,1)S(1)} %multiply_convert_fusion.4), channel_id=1, source_target_pairs={{0,4},{1,5},{2,6},{3,7},{4,0},{5,1},{6,2},{7,3},{8,12},{9,13},{10,... | collective-permute-start | bytes 786440 | tf_op jit(solution)/shard_map/ppermute | solution.py:173
  35.9 1.4 %collective-permute-done.5 = f16[32,2048]{1,0:T(8,128)(2,1)S(1)} collective-permute-done((f16[32,2048]{1,0:T(8,128)(2,1)S(1)}, f16[32,2048]{1,0:T(8,128)(2,1)S(1)}, u32[]{:S(2)}, u32[]{:S(2)}) %collective-permute-start.5) | collective-permute-done | bytes 131104 | tf_op jit(solution)/shard_map/ppermute | solution.py:173
  37.4 2.7 %collective-permute-start.11 = (f16[2,32,2048]{2,1,0:T(8,128)(2,1)S(1)}, f16[2,32,2048]{2,1,0:T(8,128)(2,1)S(1)}, u32[]{:S(2)}, u32[]{:S(2)}) collective-permute-start(f16[2,32,2048]{2,1,0:T(8,128)(2,1)S(1)} %get-tuple-element.54), channel_id=1, source_target_pairs={{0,8},{1,9},{2,10},{3,11},{4,12},{5,13},{6,14},{7,15},{8,0},{9,1},... | collective-permute-start | bytes 786440 | tf_op jit(solution)/shard_map/ppermute | solution.py:173
  40.1 1.3 %collective-permute-done.7 = f16[64,2048]{1,0:T(8,128)(2,1)S(1)} collective-permute-done((f16[64,2048]{1,0:T(8,128)(2,1)S(1)}, f16[64,2048]{1,0:T(8,128)(2,1)S(1)}, u32[]{:S(2)}, u32[]{:S(2)}) %collective-permute-start.7) | collective-permute-done | bytes 262176 | tf_op jit(solution)/shard_map/ppermute | solution.py:173
  41.5 0.5 collective-permute-start.8
  42.0 5.9 %collective-permute-done.9 = f16[32,4096]{1,0:T(8,128)(2,1)S(1)} collective-permute-done((f16[32,4096]{1,0:T(8,128)(2,1)S(1)}, f16[32,4096]{1,0:T(8,128)(2,1)S(1)}, u32[]{:S(2)}, u32[]{:S(2)}) %collective-permute-start.9) | collective-permute-done | bytes 262176 | tf_op jit(solution)/shard_map/ppermute | solution.py:173
  48.1 0.9 collective-permute-start.10
  49.0 0.7 collective-permute-done.8
  49.8 3.3 %collective-permute-done.10 = f16[32,2048]{1,0:T(8,128)(2,1)S(1)} collective-permute-done((f16[32,2048]{1,0:T(8,128)(2,1)S(1)}, f16[32,2048]{1,0:T(8,128)(2,1)S(1)}, u32[]{:S(2)}, u32[]{:S(2)}) %collective-permute-start.10) | collective-permute-done | bytes 131104 | tf_op jit(solution)/shard_map/ppermute | solution.py:173
  53.2 3.5 %collective-permute-start.16 = (f16[2,32,2048]{2,1,0:T(8,128)(2,1)S(1)}, f16[2,32,2048]{2,1,0:T(8,128)(2,1)S(1)}, u32[]{:S(2)}, u32[]{:S(2)}) collective-permute-start(f16[2,32,2048]{2,1,0:T(8,128)(2,1)S(1)} %multiply_convert_fusion.3), channel_id=1, source_target_pairs={{0,8},{1,9},{2,10},{3,11},{4,12},{5,13},{6,14},{7,15},{8,0},{9,1},... | collective-permute-start | bytes 786440 | tf_op jit(solution)/shard_map/ppermute | solution.py:173
  56.9 0.1 collective-permute-start.14
  57.0 2.4 %collective-permute-start.12 = (bf16[2,32,2048]{2,1,0:T(8,128)(2,1)S(1)}, bf16[2,32,2048]{2,1,0:T(8,128)(2,1)S(1)}, u32[]{:S(2)}, u32[]{:S(2)}) collective-permute-start(bf16[2,32,2048]{2,1,0:T(8,128)(2,1)S(1)} %get-tuple-element.47), channel_id=1, source_target_pairs={{0,4},{1,5},{2,6},{3,7},{4,0},{5,1},{6,2},{7,3},{8,12},{9,13},{10,... | collective-permute-start | bytes 786440 | tf_op jit(solution)/shard_map/ppermute | solution.py:173
  59.5 4.1 %collective-permute-done.16 = f16[2,32,2048]{2,1,0:T(8,128)(2,1)S(1)} collective-permute-done((f16[2,32,2048]{2,1,0:T(8,128)(2,1)S(1)}, f16[2,32,2048]{2,1,0:T(8,128)(2,1)S(1)}, u32[]{:S(2)}, u32[]{:S(2)}) %collective-permute-start.16) | collective-permute-done | bytes 262176 | tf_op jit(solution)/shard_map/ppermute | solution.py:173
  63.7 1.7 %collective-permute-start.17 = (bf16[2,32,2048]{2,1,0:T(8,128)(2,1)S(1)}, bf16[2,32,2048]{2,1,0:T(8,128)(2,1)S(1)}, u32[]{:S(2)}, u32[]{:S(2)}) collective-permute-start(bf16[2,32,2048]{2,1,0:T(8,128)(2,1)S(1)} %get-tuple-element.45), channel_id=1, source_target_pairs={{0,4},{1,5},{2,6},{3,7},{4,0},{5,1},{6,2},{7,3},{8,12},{9,13},{10,... | collective-permute-start | bytes 786440 | tf_op jit(solution)/shard_map/ppermute | solution.py:173
  65.4 0.7 collective-permute-done.14
  66.3 0.4 collective-permute-done.12
  66.7 2.3 %fusion.1.refs_0_ = f32[512,128]{1,0:T(8,128)S(1)} fusion(bf16[128,2048]{1,0:T(8,128)(2,1)S(1)} %bitcast.30, bf16[256,2048]{1,0:T(8,128)(2,1)} %collective-permute-done, bf16[256,2048]{1,0:T(8,128)(2,1)} %constant_dynamic-slice_fusion.2), kind=kOutput, calls=%fused_computation.6 | convolution fusion | flops 272629760 | bytes 2883584 | tf_op jit(solution)/shard_map/dot_general | solution.py:260
  69.0 1.2 %collective-permute-done.17 = bf16[2,32,2048]{2,1,0:T(8,128)(2,1)S(1)} collective-permute-done((bf16[2,32,2048]{2,1,0:T(8,128)(2,1)S(1)}, bf16[2,32,2048]{2,1,0:T(8,128)(2,1)S(1)}, u32[]{:S(2)}, u32[]{:S(2)}) %collective-permute-start.17) | collective-permute-done | bytes 262176 | tf_op jit(solution)/shard_map/ppermute | solution.py:173
  70.2 2.3 %fusion.refs_2_ = f32[512,128]{1,0:T(8,128)S(1)} fusion(bf16[128,2048]{1,0:T(8,128)(2,1)S(1)} %bitcast.28, bf16[256,2048]{1,0:T(8,128)(2,1)} %collective-permute-done, bf16[256,2048]{1,0:T(8,128)(2,1)} %constant_dynamic-slice_fusion.2), kind=kOutput, calls=%fused_computation.5 | convolution fusion | flops 272629760 | bytes 2883584 | tf_op jit(solution)/shard_map/dot_general | solution.py:260
  72.5 0.1 constant_dynamic-update-slice_fusion
  72.7 0.7 fusion.13.refs_3_
  73.4 0.7 fusion.12.refs_1_
  74.2 1.9 %shard_map.75 = bf16[16,64,256]{2,1,0:T(8,128)(2,1)} custom-call(s32[16]{0:T(128)S(1)} %copy-done, f32[512,128]{1,0:T(8,128)S(1)} %fusion.1.refs_0_, f32[512,128]{1,0:T(8,128)S(1)} %fusion.12.refs_1_, f32[512,128]{1,0:T(8,128)S(1)} %fusion.refs_2_, f32[512,128]{1,0:T(8,128)S(1)} %fusion.13.refs_3_), custom_call_target="tpu_custom_call" | custom-call | flops 65536 | bytes 1572864 | tf_op jit(solution)/shard_map/pallas_call | solution.py:122
  76.0 5.9 %all-to-all-start = ((bf16[16,1,64,256]{3,2,1,0:T(8,128)(2,1)}), bf16[16,1,64,256]{3,2,1,0:T(8,128)(2,1)S(1)}, u32[]{:S(2)}, u32[]{:S(2)}) async-start(bf16[16,1,64,256]{3,2,1,0:T(8,128)(2,1)} %bitcast.10), calls=%async_computation | async-start | bytes 1048576 | tf_op jit(solution)/shard_map/all_to_all | solution.py:266
  81.9 0.7 dynamic_slice.83
  82.8 0.3 fusion.2
  83.1 0.6 constant_dynamic-slice_fusion.1.allowed_ref
  83.7 12.7 %all-to-all-done = bf16[16,1,64,256]{3,2,1,0:T(8,128)(2,1)S(1)} async-done(((bf16[16,1,64,256]{3,2,1,0:T(8,128)(2,1)}), bf16[16,1,64,256]{3,2,1,0:T(8,128)(2,1)S(1)}, u32[]{:S(2)}, u32[]{:S(2)}) %all-to-all-start) | async-done | bytes 524320 | tf_op jit(solution)/shard_map/all_to_all | solution.py:266
  96.4 0.9 shard_map.76
  (56 shorter events, 1.8 us)
Async XLA Ops:
  0.0 5.4 %copy-start.1 = (f32[512,256]{1,0:T(8,128)S(1)}, f32[512,256]{1,0:T(8,128)}, u32[]{:S(2)}) copy-start(f32[512,256]{1,0:T(8,128)} %rows_ref.1) | copy-start | bytes 1572868
  2.4 54.6 %collective-permute-start.13 = (bf16[128,2048]{1,0:T(8,128)(2,1)}, bf16[128,2048]{1,0:T(8,128)(2,1)S(1)}, u32[]{:S(2)}, u32[]{:S(2)}) collective-permute-start(bf16[128,2048]{1,0:T(8,128)(2,1)} %get-tuple-element.49), channel_id=1, source_target_pairs={{0,2},{1,3},{2,0},{3,1},{4,6},{5,7},{6,4},{7,5},{8,10},{9,11},{10,... | collective-permute-start | bytes 1572872 | tf_op jit(solution)/shard_map/ppermute | solution.py:173
  9.6 2.5 %copy-start.2 = (bf16[256,4096]{1,0:T(8,128)(2,1)}, bf16[256,4096]{1,0:T(8,128)(2,1)S(1)}, u32[]{:S(2)}) copy-start(bf16[256,4096]{1,0:T(8,128)(2,1)S(1)} %get-tuple-element.25.low_ref) | copy-start | bytes 6291460
  11.0 7.4 %collective-permute-start.1 = (f16[128,4096]{1,0:T(8,128)(2,1)}, f16[128,4096]{1,0:T(8,128)(2,1)}, u32[]{:S(2)}, u32[]{:S(2)}) collective-permute-start(f16[128,4096]{1,0:T(8,128)(2,1)} %multiply_convert_fusion.1), channel_id=1, source_target_pairs={{0,1},{1,0},{2,3},{3,2},{4,5},{5,4},{6,7},{7,6},{8,9},{9,8},{10,11... | collective-permute-start | bytes 3145736 | tf_op jit(solution)/shard_map/ppermute | solution.py:173
  12.1 10.3 %collective-permute-start.6 = (f16[128,4096]{1,0:T(8,128)(2,1)}, f16[128,4096]{1,0:T(8,128)(2,1)}, u32[]{:S(2)}, u32[]{:S(2)}) collective-permute-start(f16[128,4096]{1,0:T(8,128)(2,1)} %multiply_convert_fusion), channel_id=1, source_target_pairs={{0,1},{1,0},{2,3},{3,2},{4,5},{5,4},{6,7},{7,6},{8,9},{9,8},{10,11... | collective-permute-start | bytes 3145736 | tf_op jit(solution)/shard_map/ppermute | solution.py:173
  15.0 51.8 %collective-permute-start = (bf16[256,2048]{1,0:T(8,128)(2,1)}, bf16[256,2048]{1,0:T(8,128)(2,1)}, u32[]{:S(2)}, u32[]{:S(2)}) collective-permute-start(bf16[256,2048]{1,0:T(8,128)(2,1)} %constant_dynamic-slice_fusion.2), channel_id=1, source_target_pairs={{0,1},{1,0},{2,3},{3,2},{4,5},{5,4},{6,7},{7,6},{8,9},{9,8},{10,11... | collective-permute-start | bytes 3145736 | tf_op jit(solution)/shard_map/ppermute | solution.py:173
  15.0 1.6 %copy-start.3 = (bf16[256,4096]{1,0:T(8,128)(2,1)S(1)}, bf16[256,4096]{1,0:T(8,128)(2,1)}, u32[]{:S(2)}) copy-start(bf16[256,4096]{1,0:T(8,128)(2,1)} %copy-done.2) | copy-start | bytes 6291460
  20.2 8.8 %collective-permute-start.2 = (f16[64,2048]{1,0:T(8,128)(2,1)S(1)}, f16[64,2048]{1,0:T(8,128)(2,1)S(1)}, u32[]{:S(2)}, u32[]{:S(2)}) collective-permute-start(f16[64,2048]{1,0:T(8,128)(2,1)S(1)} %multiply_convert_fusion.7), channel_id=1, source_target_pairs={{0,2},{1,3},{2,0},{3,1},{4,6},{5,7},{6,4},{7,5},{8,10},{9,11},{10,... | collective-permute-start | bytes 786440 | tf_op jit(solution)/shard_map/ppermute | solution.py:173
  20.3 10.4 %collective-permute-start.4 = (f16[32,4096]{1,0:T(8,128)(2,1)S(1)}, f16[32,4096]{1,0:T(8,128)(2,1)S(1)}, u32[]{:S(2)}, u32[]{:S(2)}) collective-permute-start(f16[32,4096]{1,0:T(8,128)(2,1)S(1)} %multiply_convert_fusion.6), channel_id=1, source_target_pairs={{0,4},{1,5},{2,6},{3,7},{4,0},{5,1},{6,2},{7,3},{8,12},{9,13},{10,... | collective-permute-start | bytes 786440 | tf_op jit(solution)/shard_map/ppermute | solution.py:173
  29.1 5.2 %collective-permute-start.3 = (f16[32,2048]{1,0:T(8,128)(2,1)S(1)}, f16[32,2048]{1,0:T(8,128)(2,1)S(1)}, u32[]{:S(2)}, u32[]{:S(2)}) collective-permute-start(f16[32,2048]{1,0:T(8,128)(2,1)S(1)} %multiply_convert_fusion.11), channel_id=1, source_target_pairs={{0,4},{1,5},{2,6},{3,7},{4,0},{5,1},{6,2},{7,3},{8,12},{9,13},{10,... | collective-permute-start | bytes 393224 | tf_op jit(solution)/shard_map/ppermute | solution.py:173
  30.8 6.5 %collective-permute-start.5 = (f16[32,2048]{1,0:T(8,128)(2,1)S(1)}, f16[32,2048]{1,0:T(8,128)(2,1)S(1)}, u32[]{:S(2)}, u32[]{:S(2)}) collective-permute-start(f16[32,2048]{1,0:T(8,128)(2,1)S(1)} %multiply_convert_fusion.10), channel_id=1, source_target_pairs={{0,2},{1,3},{2,0},{3,1},{4,6},{5,7},{6,4},{7,5},{8,10},{9,11},{10,... | collective-permute-start | bytes 393224 | tf_op jit(solution)/shard_map/ppermute | solution.py:173
  31.4 10.0 %collective-permute-start.7 = (f16[64,2048]{1,0:T(8,128)(2,1)S(1)}, f16[64,2048]{1,0:T(8,128)(2,1)S(1)}, u32[]{:S(2)}, u32[]{:S(2)}) collective-permute-start(f16[64,2048]{1,0:T(8,128)(2,1)S(1)} %multiply_convert_fusion.5), channel_id=1, source_target_pairs={{0,2},{1,3},{2,0},{3,1},{4,6},{5,7},{6,4},{7,5},{8,10},{9,11},{10,... | collective-permute-start | bytes 786440 | tf_op jit(solution)/shard_map/ppermute | solution.py:173
  34.3 13.7 %collective-permute-start.9 = (f16[32,4096]{1,0:T(8,128)(2,1)S(1)}, f16[32,4096]{1,0:T(8,128)(2,1)S(1)}, u32[]{:S(2)}, u32[]{:S(2)}) collective-permute-start(f16[32,4096]{1,0:T(8,128)(2,1)S(1)} %multiply_convert_fusion.4), channel_id=1, source_target_pairs={{0,4},{1,5},{2,6},{3,7},{4,0},{5,1},{6,2},{7,3},{8,12},{9,13},{10,... | collective-permute-start | bytes 786440 | tf_op jit(solution)/shard_map/ppermute | solution.py:173
  37.4 19.3 %collective-permute-start.11 = (f16[2,32,2048]{2,1,0:T(8,128)(2,1)S(1)}, f16[2,32,2048]{2,1,0:T(8,128)(2,1)S(1)}, u32[]{:S(2)}, u32[]{:S(2)}) collective-permute-start(f16[2,32,2048]{2,1,0:T(8,128)(2,1)S(1)} %get-tuple-element.54), channel_id=1, source_target_pairs={{0,8},{1,9},{2,10},{3,11},{4,12},{5,13},{6,14},{7,15},{8,0},{9,1},... | collective-permute-start | bytes 786440 | tf_op jit(solution)/shard_map/ppermute | solution.py:173
  41.5 8.3 %collective-permute-start.8 = (f16[32,2048]{1,0:T(8,128)(2,1)S(1)}, f16[32,2048]{1,0:T(8,128)(2,1)S(1)}, u32[]{:S(2)}, u32[]{:S(2)}) collective-permute-start(f16[32,2048]{1,0:T(8,128)(2,1)S(1)} %multiply_convert_fusion.9), channel_id=1, source_target_pairs={{0,4},{1,5},{2,6},{3,7},{4,0},{5,1},{6,2},{7,3},{8,12},{9,13},{10,... | collective-permute-start | bytes 393224 | tf_op jit(solution)/shard_map/ppermute | solution.py:173
  48.0 8.8 %copy-start.4 = (bf16[128,2048]{1,0:T(8,128)(2,1)S(1)}, bf16[128,2048]{1,0:T(8,128)(2,1)}, u32[]{:S(2)}) copy-start(bf16[128,2048]{1,0:T(8,128)(2,1)} %get-tuple-element.32) | copy-start | bytes 1572868
  48.1 5.0 %collective-permute-start.10 = (f16[32,2048]{1,0:T(8,128)(2,1)S(1)}, f16[32,2048]{1,0:T(8,128)(2,1)S(1)}, u32[]{:S(2)}, u32[]{:S(2)}) collective-permute-start(f16[32,2048]{1,0:T(8,128)(2,1)S(1)} %multiply_convert_fusion.8), channel_id=1, source_target_pairs={{0,2},{1,3},{2,0},{3,1},{4,6},{5,7},{6,4},{7,5},{8,10},{9,11},{10,... | collective-permute-start | bytes 393224 | tf_op jit(solution)/shard_map/ppermute | solution.py:173
  53.2 10.4 %collective-permute-start.16 = (f16[2,32,2048]{2,1,0:T(8,128)(2,1)S(1)}, f16[2,32,2048]{2,1,0:T(8,128)(2,1)S(1)}, u32[]{:S(2)}, u32[]{:S(2)}) collective-permute-start(f16[2,32,2048]{2,1,0:T(8,128)(2,1)S(1)} %multiply_convert_fusion.3), channel_id=1, source_target_pairs={{0,8},{1,9},{2,10},{3,11},{4,12},{5,13},{6,14},{7,15},{8,0},{9,1},... | collective-permute-start | bytes 786440 | tf_op jit(solution)/shard_map/ppermute | solution.py:173
  56.9 9.2 %collective-permute-start.14 = (bf16[128,2048]{1,0:T(8,128)(2,1)S(1)}, bf16[128,2048]{1,0:T(8,128)(2,1)S(1)}, u32[]{:S(2)}, u32[]{:S(2)}) collective-permute-start(bf16[128,2048]{1,0:T(8,128)(2,1)S(1)} %copy-done.4), channel_id=1, source_target_pairs={{0,2},{1,3},{2,0},{3,1},{4,6},{5,7},{6,4},{7,5},{8,10},{9,11},{10,... | collective-permute-start | bytes 1572872 | tf_op jit(solution)/shard_map/ppermute | solution.py:173
  57.0 9.7 %collective-permute-start.12 = (bf16[2,32,2048]{2,1,0:T(8,128)(2,1)S(1)}, bf16[2,32,2048]{2,1,0:T(8,128)(2,1)S(1)}, u32[]{:S(2)}, u32[]{:S(2)}) collective-permute-start(bf16[2,32,2048]{2,1,0:T(8,128)(2,1)S(1)} %get-tuple-element.47), channel_id=1, source_target_pairs={{0,4},{1,5},{2,6},{3,7},{4,0},{5,1},{6,2},{7,3},{8,12},{9,13},{10,... | collective-permute-start | bytes 786440 | tf_op jit(solution)/shard_map/ppermute | solution.py:173
  63.7 6.4 %collective-permute-start.17 = (bf16[2,32,2048]{2,1,0:T(8,128)(2,1)S(1)}, bf16[2,32,2048]{2,1,0:T(8,128)(2,1)S(1)}, u32[]{:S(2)}, u32[]{:S(2)}) collective-permute-start(bf16[2,32,2048]{2,1,0:T(8,128)(2,1)S(1)} %get-tuple-element.45), channel_id=1, source_target_pairs={{0,4},{1,5},{2,6},{3,7},{4,0},{5,1},{6,2},{7,3},{8,12},{9,13},{10,... | collective-permute-start | bytes 786440 | tf_op jit(solution)/shard_map/ppermute | solution.py:173
  66.2 6.3 %collective-permute-start.15 = (bf16[256,2048]{1,0:T(8,128)(2,1)S(1)}, bf16[256,2048]{1,0:T(8,128)(2,1)S(1)}, u32[]{:S(2)}, u32[]{:S(2)}) collective-permute-start(bf16[256,2048]{1,0:T(8,128)(2,1)S(1)} %pad_maximum_fusion.3), channel_id=1, source_target_pairs={{0,1},{1,0},{2,3},{3,2},{4,5},{5,4},{6,7},{7,6},{8,9},{9,8},{10,11... | collective-permute-start | bytes 3145736 | tf_op jit(solution)/shard_map/ppermute | solution.py:173
  73.4 0.8 copy-start
  73.4 9.2 %copy-start.5 = (s32[8,12]{1,0:T(8,128)S(1)}, s32[8,12]{1,0:T(8,128)}, u32[]{:S(2)}) copy-start(s32[8,12]{1,0:T(8,128)} %param.11) | copy-start | bytes 1156
  73.4 9.3 %copy-start.6 = (s32[8]{0:T(128)S(1)}, s32[8]{0:T(128)}, u32[]{:S(2)}) copy-start(s32[8]{0:T(128)} %param.12) | copy-start | bytes 100
  73.4 9.4 %copy-start.7 = (s32[512]{0:T(512)S(1)}, s32[512]{0:T(512)}, u32[]{:S(2)}) copy-start(s32[512]{0:T(512)} %param.10) | copy-start | bytes 6148
  76.0 20.4 %all-to-all-start = ((bf16[16,1,64,256]{3,2,1,0:T(8,128)(2,1)}), bf16[16,1,64,256]{3,2,1,0:T(8,128)(2,1)S(1)}, u32[]{:S(2)}, u32[]{:S(2)}) async-start(bf16[16,1,64,256]{3,2,1,0:T(8,128)(2,1)} %bitcast.10), calls=%async_computation | async-start | bytes 1048576 | tf_op jit(solution)/shard_map/all_to_all | solution.py:266

commit v9 on v8

--- a/solution.py
+++ b/solution.py
@@ -172,8 +172,19 @@
     def swap(value, bit):
         return lax.ppermute(value, "rows", [(r, r ^ (1 << bit)) for r in range(n)])
 
-    def side(bit):
-        return (me >> bit) & 1
+    rows = nq // CORES // CHUNKS // PATHS
+    sizes = {(ybit, width // 2), (zbit, rows // 2)} | {(bit, rows >> (i + 2)) for i, bit in enumerate(rest[:-1])}
+    offsets = {}
+    first_half = {}
+    for bit, size in sorted(sizes):
+        side = (me >> bit) & 1
+        offsets[bit, size] = (side * size, (1 - side) * size)
+        first_half[bit] = side == 0
+    owned = nblocks // n
+    first_slot = me * owned
+    scalars = (core, 1 - core, first_slot, offsets, first_half)
+    scalars, queries, train = lax.optimization_barrier((scalars, queries, train))
+    core, other_core, first_slot, offsets, first_half = scalars
 
     def pack(value):
         return (value * UNIT).astype(jnp.float16)
@@ -181,28 +192,28 @@
     def unpack(value):
         return value.astype(jnp.float32) * (1.0 / UNIT)
 
-    def part(value, index, axis):
-        size = value.shape[axis] // 2
-        return lax.dynamic_slice_in_dim(value, index * size, size, axis)
+    def part(value, bit, axis, other=0):
+        shape = list(value.shape)
+        shape[axis] //= 2
+        starts = [0] * value.ndim
+        starts[axis] = offsets[bit, shape[axis]][other]
+        return lax.dynamic_slice(value, starts, shape, allow_negative_indices=False)
 
     def give(value, bit, axis):
-        return pack(part(value, 1 - side(bit), axis))
+        return pack(part(value, bit, axis, 1))
 
     def keep(value, got, bit, axis):
-        return part(value, side(bit), axis) + unpack(got)
+        return part(value, bit, axis) + unpack(got)
 
     def join(own, got, bit):
-        size = own.shape[1]
-        full = jnp.zeros((own.shape[0], 2 * size) + own.shape[2:], own.dtype)
-        full = lax.dynamic_update_slice_in_dim(full, own, side(bit) * size, 1)
-        return lax.dynamic_update_slice_in_dim(full, got, (1 - side(bit)) * size, 1)
+        mine_first = jnp.concatenate([own, got], axis=1)
+        return jnp.where(first_half[bit], mine_first, jnp.concatenate([got, own], axis=1))
 
     def after(value, first):
         return lax.optimization_barrier((value, first))[0]
 
     def paths(value, other):
         value = value + unpack(other)
-        rows = value.shape[0] // PATHS
         return [value[i * rows:(i + 1) * rows] for i in range(PATHS)]
 
     levels = ((ybit, 1), (zbit, 0)), ((zbit, 0), (ybit, 1))
@@ -220,22 +231,34 @@
             value = keep(value, swap(give(value, bit, 1), bit), bit, 1)
         return value
 
-    def gather(value):
+    def gather(value, first=None):
         for bit in reversed([zbit] + rest[:-1]):
-            value = join(value, swap(value, bit), bit)
+            got = swap(value, bit)
+            if first is not None and bit == zbit:
+                got = after(got, first)
+            value = join(value, got, bit)
         return value.reshape(-1, value.shape[-1])
 
-    rows = train.reshape(examples * nblocks, width)
-    far = part(rows, 1 - side(ybit), 1)
-    far = [part(far, i, 0) for i in range(2)]
-    early = swap(far[0], ybit)
-    queries = after(queries, far[0])
-
-    *full, high, low = product(1 - core, queries, [precond], other_kernel, OTHER_VMEM)
+    def scores(group, value):
+        return lax.dot_general(group, value, (((1,), (1,)), ((), ())), preferred_element_type=jnp.float32)
+
+    blocks = train.reshape(examples * nblocks, width)
+    middle = examples // 2 * nblocks
+
+    def features(blocks, first, count, other):
+        start = offsets[ybit, width // 2][other]
+        return lax.dynamic_slice(blocks, (first, start), (count, width // 2), allow_negative_indices=False)
+
+    early = features(blocks, 0, middle, 1)
+    queries, blocks = after((queries, blocks), early)
+    early = swap(early, ybit)
+
+    *full, high, low = product(other_core, queries, [precond], other_kernel, OTHER_VMEM)
     sent = [pack(value) for value in full]
     got = [swap(value, 0) for value in sent]
-    rows = after(rows, sent)
-    near = part(rows, side(ybit), 1)
+    blocks = after(blocks, sent)
+    near = features(blocks, 0, 2 * middle, 0)
+    late = features(blocks, middle, middle, 1)
     sibling = swap(near, 0)
     mine = product(after(core, sent), queries, [high, low], mine_kernel, MINE_VMEM)
     one = paths(mine[0], got[0])
@@ -250,23 +273,21 @@
     sent = pack(two)
     one = (after(one, sent) + unpack(got_one)).astype(jnp.bfloat16)
     got_two = swap(sent, rest[-1])
-    late = swap(after(far[1], one), ybit)
+    late = swap(after(late, one), ybit)
     one = gather(one)
     far = jnp.concatenate([early, late], axis=0)
     groups = [jnp.concatenate([near, sibling], axis=0), jnp.concatenate([far, swap(far, 0)], axis=0)]
-    two = gather((two + unpack(got_two)).astype(jnp.bfloat16))
-
-    raws = [
-        lax.dot_general(group, value, (((1,), (1,)), ((), ())), preferred_element_type=jnp.float32)
-        for value in (one, two)
-        for group in groups
-    ]
-    owned = nblocks // n
+    raws = [scores(group, one) for group in groups]
+    two = gather((two + unpack(got_two)).astype(jnp.bfloat16), raws)
+    raws = raws + [scores(group, two) for group in groups]
+
     ordered = in_slot_order(raws, slot_block).reshape(n, owned, 2 * CORES * examples, nq // CORES)
     got = lax.all_to_all(ordered, "rows", split_axis=0, concat_axis=0, tiled=True)
 
+    lists = (query_cluster, cand_blocks, cand_count, slot_block, first_slot)
+    query_cluster, cand_blocks, cand_count, slot_block, first_slot = after(lists, ordered)
     allowed = listed_mask(query_cluster, cand_blocks, cand_count, nblocks)
-    slots = lax.dynamic_slice_in_dim(slot_block, me * owned, owned)
+    slots = lax.dynamic_slice(slot_block, (first_slot,), (owned,), allow_negative_indices=False)
     own_allowed = jnp.take(allowed, slots, axis=0, mode="clip")
     return finish(got.reshape(n, owned, 2 * CORES, examples, nq // CORES), own_allowed)
 

time: 97.7 us -> 94.1 us (0.963)
  waiting for transfers between devices: 37.8 us -> 44 us
  other arithmetic: 6.86 us -> 3.57 us
  matrix products: 6.24 us -> 3.16 us
  local copies, waits for them, and re-layouts: 8.4 us -> 5.42 us
    ppermute x18, waiting for transfers between devices: 25.1 us -> 31.4 us  [swap(): return lax.ppermute(value, 'rows', [(r, r ^ 1 << bit) for r in range(n)])]
    dynamic_slice x3 -> x4, local copies, waits for them, and re-layouts: 5.36 us -> 1.51 us  [the longest x3 0.84 us: features(): lax.dynamic_slice(blocks, (first, start), (count, width // 2), allow_nega...]
    dot_general x4, matrix products: 5.98 us -> 2.9 us  [scores(): lax.dot_general(group, value, (((1,), (1,)), ((), ())), preferred_element...]
    add x2, other arithmetic: 3.13 us -> 0.56 us  [paths(): value = value + unpack(other)]
    convert_element_type x12, other arithmetic: 2.95 us -> 1.48 us  [pack(): return (value * UNIT).astype(jnp.float16)]
    all_to_all x1, starting transfers between devices: 5.89 us -> 4.81 us  [shards(): lax.all_to_all(ordered, 'rows', split_axis=0, concat_axis=0, tiled=True)]
    unnamed x19 -> x14, local copies, waits for them, and re-layouts: 1.79 us -> 2.73 us
  transfers between devices with their start and end apart: 19 -> 19, of which waited for: 12 -> 11; matrix products, arithmetic and copies ran while one was open for 16% -> 8% of each run, Pallas kernels for 6% -> 6%
where the time goes in v9:
time: 94.1 us; the launch traced here: 93.8 us
  waiting for transfers between devices  44 us (47%)
  starting transfers between devices  28.4 us (30%)
  Pallas kernels  8.79 us (9%)
  local copies, waits for them, and re-layouts  5.42 us (6%)
  other arithmetic  3.57 us (4%)
  matrix products  3.16 us (3%)
    ppermute x18, waiting for transfers between devices, swap(): return lax.ppermute(value, 'rows', [(r, r ^ 1 << bit) for r in range(n)])  31.4 us
    ppermute x18, starting transfers between devices, swap(): return lax.ppermute(value, 'rows', [(r, r ^ 1 << bit) for r in range(n)])  23.6 us
    all_to_all x1, waiting for transfers between devices, shards(): lax.all_to_all(ordered, 'rows', split_axis=0, concat_axis=0, tiled=True)  12.6 us
    pallas_call x2, Pallas kernels, product(): pl.pallas_call(kernel, in_specs=[pl.BlockSpec(memory_space=pltpu.SMEM), v...  6.05 us
    all_to_all x1, starting transfers between devices, shards(): lax.all_to_all(ordered, 'rows', split_axis=0, concat_axis=0, tiled=True)  4.81 us
    dot_general x4, matrix products, scores(): lax.dot_general(group, value, (((1,), (1,)), ((), ())), preferred_element...  2.9 us
    unnamed x14, local copies, waits for them, and re-layouts  2.73 us
  transfers between devices with their start and end apart: 19, of which 11 were waited for; matrix products, arithmetic and copies ran while one was open for 8% of the time, Pallas kernels for 6%

profile of v9, /device:TPU:0, one launch (start us, length us, event | category | flops | bytes accessed | tf_op | source)
XLA Modules:
  0.0 93.8 jit_solution(16383978426965087739)
XLA Ops:
  0.0 1.6 %copy-done = bf16[16,16,4096]{2,1,0:T(8,128)(2,1)S(1)} copy-done((bf16[16,16,4096]{2,1,0:T(8,128)(2,1)S(1)}, bf16[16,16,4096]{2,1,0:T(8,128)(2,1)}, u32[]{:S(2)}) %copy-start) | copy-done | bytes 2097176
  1.6 0.2 constant_dynamic-slice_fusion.2
  1.8 3.0 %collective-permute-start.13 = (bf16[128,2048]{1,0:T(8,128)(2,1)S(1)}, bf16[128,2048]{1,0:T(8,128)(2,1)S(1)}, u32[]{:S(2)}, u32[]{:S(2)}) collective-permute-start(bf16[128,2048]{1,0:T(8,128)(2,1)S(1)} %constant_dynamic-slice_fusion.2), channel_id=1, source_target_pairs={{0,2},{1,3},{2,0},{3,1},{4,6},{5,7},{6,4},{7,5},{8,10},{9,11},{10,... | collective-permute-start | bytes 1572872 | tf_op jit(solution)/shard_map/ppermute | solution.py:173
  4.8 1.0 %copy-done.2 = f32[512,256]{1,0:T(8,128)S(1)} copy-done((f32[512,256]{1,0:T(8,128)S(1)}, f32[512,256]{1,0:T(8,128)}, u32[]{:S(2)}) %copy-start.2) | copy-done | bytes 524312
  5.9 4.2 %shard_map.73 = (f32[128,4096]{1,0:T(8,128)S(1)}, f32[128,4096]{1,0:T(8,128)S(1)}, bf16[256,4096]{1,0:T(8,128)(2,1)S(1)}, bf16[256,4096]{1,0:T(8,128)(2,1)S(1)}) custom-call(s32[1]{0:T(128)} %bitcast.1.core_ref, f32[512,256]{1,0:T(8,128)S(1)} %copy-done.2, f32[256,4096]{1,0:T(8,128)} %columns_hbm.1), custom_call_target="tpu_custom_call" | custom-call | flops 1610612736 | bytes 8388608 | tf_op jit(solution)/shard_map/pallas_call | solution.py:85
  10.6 0.6 collective-permute-start.6
  11.2 1.8 %shard_map.74 = (f32[128,4096]{1,0:T(8,128)S(1)}, f32[128,4096]{1,0:T(8,128)S(1)}) custom-call(s32[1]{0:T(128)} %bitcast.2.core_ref, f32[512,256]{1,0:T(8,128)S(1)} %copy-done.2, bf16[256,4096]{1,0:T(8,128)(2,1)S(1)} %get-tuple-element.49.high_ref, bf16[256,4096]{1,0:T(8,128)(2,1)S(1)} %get-tuple-element.50.low_ref), custom_call_target="tpu_custom_call" | custom-call | flops 1610612736 | bytes 8388608 | tf_op jit(solution)/shard_map/pallas_call | solution.py:85
  13.0 0.2 constant_dynamic-slice_fusion.3
  13.2 0.3 multiply_add_fusion.1
  13.7 0.2 multiply_convert_fusion.7
  14.1 2.1 %collective-permute-start.4 = (f16[32,4096]{1,0:T(8,128)(2,1)S(1)}, f16[32,4096]{1,0:T(8,128)(2,1)S(1)}, u32[]{:S(2)}, u32[]{:S(2)}) collective-permute-start(f16[32,4096]{1,0:T(8,128)(2,1)S(1)} %multiply_convert_fusion.6), channel_id=1, source_target_pairs={{0,4},{1,5},{2,6},{3,7},{4,0},{5,1},{6,2},{7,3},{8,12},{9,13},{10,... | collective-permute-start | bytes 786440 | tf_op jit(solution)/shard_map/ppermute | solution.py:173
  16.2 0.3 multiply_add_fusion
  16.8 0.2 multiply_convert_fusion.5
  17.0 5.4 %collective-permute-done.2 = f16[64,2048]{1,0:T(8,128)(2,1)S(1)} collective-permute-done((f16[64,2048]{1,0:T(8,128)(2,1)S(1)}, f16[64,2048]{1,0:T(8,128)(2,1)S(1)}, u32[]{:S(2)}, u32[]{:S(2)}) %collective-permute-start.2) | collective-permute-done | bytes 262176 | tf_op jit(solution)/shard_map/ppermute | solution.py:173
  22.4 0.2 multiply_add_fusion.5
  22.7 1.9 %collective-permute-start.3 = (f16[32,2048]{1,0:T(8,128)(2,1)S(1)}, f16[32,2048]{1,0:T(8,128)(2,1)S(1)}, u32[]{:S(2)}, u32[]{:S(2)}) collective-permute-start(f16[32,2048]{1,0:T(8,128)(2,1)S(1)} %multiply_convert_fusion.11), channel_id=1, source_target_pairs={{0,4},{1,5},{2,6},{3,7},{4,0},{5,1},{6,2},{7,3},{8,12},{9,13},{10,... | collective-permute-start | bytes 393224 | tf_op jit(solution)/shard_map/ppermute | solution.py:173
  24.8 1.6 %collective-permute-start.5 = (f16[32,2048]{1,0:T(8,128)(2,1)S(1)}, f16[32,2048]{1,0:T(8,128)(2,1)S(1)}, u32[]{:S(2)}, u32[]{:S(2)}) collective-permute-start(f16[32,2048]{1,0:T(8,128)(2,1)S(1)} %multiply_convert_fusion.10), channel_id=1, source_target_pairs={{0,2},{1,3},{2,0},{3,1},{4,6},{5,7},{6,4},{7,5},{8,10},{9,11},{10,... | collective-permute-start | bytes 393224 | tf_op jit(solution)/shard_map/ppermute | solution.py:173
  26.4 0.5 collective-permute-start.7
  26.9 0.2 collective-permute-start.9
  27.1 1.0 %collective-permute-done.3 = f16[32,2048]{1,0:T(8,128)(2,1)S(1)} collective-permute-done((f16[32,2048]{1,0:T(8,128)(2,1)S(1)}, f16[32,2048]{1,0:T(8,128)(2,1)S(1)}, u32[]{:S(2)}, u32[]{:S(2)}) %collective-permute-start.3) | collective-permute-done | bytes 131104 | tf_op jit(solution)/shard_map/ppermute | solution.py:173
  28.2 3.1 %collective-permute-done.5 = f16[32,2048]{1,0:T(8,128)(2,1)S(1)} collective-permute-done((f16[32,2048]{1,0:T(8,128)(2,1)S(1)}, f16[32,2048]{1,0:T(8,128)(2,1)S(1)}, u32[]{:S(2)}, u32[]{:S(2)}) %collective-permute-start.5) | collective-permute-done | bytes 131104 | tf_op jit(solution)/shard_map/ppermute | solution.py:173
  31.5 2.7 %collective-permute-start.11 = (f16[2,32,2048]{2,1,0:T(8,128)(2,1)S(1)}, f16[2,32,2048]{2,1,0:T(8,128)(2,1)S(1)}, u32[]{:S(2)}, u32[]{:S(2)}) collective-permute-start(f16[2,32,2048]{2,1,0:T(8,128)(2,1)S(1)} %get-tuple-element.82), channel_id=1, source_target_pairs={{0,8},{1,9},{2,10},{3,11},{4,12},{5,13},{6,14},{7,15},{8,0},{9,1},... | collective-permute-start | bytes 786440 | tf_op jit(solution)/shard_map/ppermute | solution.py:173
  34.1 1.0 %collective-permute-done.7 = f16[64,2048]{1,0:T(8,128)(2,1)S(1)} collective-permute-done((f16[64,2048]{1,0:T(8,128)(2,1)S(1)}, f16[64,2048]{1,0:T(8,128)(2,1)S(1)}, u32[]{:S(2)}, u32[]{:S(2)}) %collective-permute-start.7) | collective-permute-done | bytes 262176 | tf_op jit(solution)/shard_map/ppermute | solution.py:173
  35.1 0.2 multiply_add_fusion.3
  35.4 0.4 collective-permute-start.8
  35.8 2.0 %collective-permute-done.9 = f16[32,4096]{1,0:T(8,128)(2,1)S(1)} collective-permute-done((f16[32,4096]{1,0:T(8,128)(2,1)S(1)}, f16[32,4096]{1,0:T(8,128)(2,1)S(1)}, u32[]{:S(2)}, u32[]{:S(2)}) %collective-permute-start.9) | collective-permute-done | bytes 262176 | tf_op jit(solution)/shard_map/ppermute | solution.py:173
  38.0 2.2 %collective-permute-start.10 = (f16[32,2048]{1,0:T(8,128)(2,1)S(1)}, f16[32,2048]{1,0:T(8,128)(2,1)S(1)}, u32[]{:S(2)}, u32[]{:S(2)}) collective-permute-start(f16[32,2048]{1,0:T(8,128)(2,1)S(1)} %multiply_convert_fusion.8), channel_id=1, source_target_pairs={{0,2},{1,3},{2,0},{3,1},{4,6},{5,7},{6,4},{7,5},{8,10},{9,11},{10,... | collective-permute-start | bytes 393224 | tf_op jit(solution)/shard_map/ppermute | solution.py:173
  40.2 1.6 %collective-permute-done.8 = f16[32,2048]{1,0:T(8,128)(2,1)S(1)} collective-permute-done((f16[32,2048]{1,0:T(8,128)(2,1)S(1)}, f16[32,2048]{1,0:T(8,128)(2,1)S(1)}, u32[]{:S(2)}, u32[]{:S(2)}) %collective-permute-start.8) | collective-permute-done | bytes 131104 | tf_op jit(solution)/shard_map/ppermute | solution.py:173
  41.9 1.7 %collective-permute-done.10 = f16[32,2048]{1,0:T(8,128)(2,1)S(1)} collective-permute-done((f16[32,2048]{1,0:T(8,128)(2,1)S(1)}, f16[32,2048]{1,0:T(8,128)(2,1)S(1)}, u32[]{:S(2)}, u32[]{:S(2)}) %collective-permute-start.10) | collective-permute-done | bytes 131104 | tf_op jit(solution)/shard_map/ppermute | solution.py:173
  43.9 2.4 %collective-permute-start.14 = (bf16[128,2048]{1,0:T(8,128)(2,1)S(1)}, bf16[128,2048]{1,0:T(8,128)(2,1)S(1)}, u32[]{:S(2)}, u32[]{:S(2)}) collective-permute-start(bf16[128,2048]{1,0:T(8,128)(2,1)S(1)} %constant_dynamic-slice_fusion.3), channel_id=1, source_target_pairs={{0,2},{1,3},{2,0},{3,1},{4,6},{5,7},{6,4},{7,5},{8,10},{9,11},{10,... | collective-permute-start | bytes 1572872 | tf_op jit(solution)/shard_map/ppermute | solution.py:173
  46.3 0.4 constant_dynamic-slice_fusion.1
  46.8 2.2 %collective-permute-start.16 = (f16[2,32,2048]{2,1,0:T(8,128)(2,1)S(1)}, f16[2,32,2048]{2,1,0:T(8,128)(2,1)S(1)}, u32[]{:S(2)}, u32[]{:S(2)}) collective-permute-start(f16[2,32,2048]{2,1,0:T(8,128)(2,1)S(1)} %multiply_convert_fusion.3), channel_id=1, source_target_pairs={{0,8},{1,9},{2,10},{3,11},{4,12},{5,13},{6,14},{7,15},{8,0},{9,1},... | collective-permute-start | bytes 786440 | tf_op jit(solution)/shard_map/ppermute | solution.py:173
  49.0 3.4 %collective-permute-start.12 = (bf16[2,32,2048]{2,1,0:T(8,128)(2,1)S(1)}, bf16[2,32,2048]{2,1,0:T(8,128)(2,1)S(1)}, u32[]{:S(2)}, u32[]{:S(2)}) collective-permute-start(bf16[2,32,2048]{2,1,0:T(8,128)(2,1)S(1)} %add_convert_fusion.1), channel_id=1, source_target_pairs={{0,4},{1,5},{2,6},{3,7},{4,0},{5,1},{6,2},{7,3},{8,12},{9,13},{10,... | collective-permute-start | bytes 786440 | tf_op jit(solution)/shard_map/ppermute | solution.py:173
  52.4 2.0 %collective-permute-done.14 = bf16[128,2048]{1,0:T(8,128)(2,1)S(1)} collective-permute-done((bf16[128,2048]{1,0:T(8,128)(2,1)S(1)}, bf16[128,2048]{1,0:T(8,128)(2,1)S(1)}, u32[]{:S(2)}, u32[]{:S(2)}) %collective-permute-start.14) | collective-permute-done | bytes 524320 | tf_op jit(solution)/shard_map/ppermute | solution.py:173
  54.6 7.6 %collective-permute-done.16 = f16[2,32,2048]{2,1,0:T(8,128)(2,1)S(1)} collective-permute-done((f16[2,32,2048]{2,1,0:T(8,128)(2,1)S(1)}, f16[2,32,2048]{2,1,0:T(8,128)(2,1)S(1)}, u32[]{:S(2)}, u32[]{:S(2)}) %collective-permute-start.16) | collective-permute-done | bytes 262176 | tf_op jit(solution)/shard_map/ppermute | solution.py:173
  62.2 0.2 collective-permute-start.17
  62.6 0.7 fusion.1.refs_0_
  63.4 0.7 fusion.11.refs_1_
  64.2 5.9 %collective-permute-done.17 = bf16[2,32,2048]{2,1,0:T(8,128)(2,1)S(1)} collective-permute-done((bf16[2,32,2048]{2,1,0:T(8,128)(2,1)S(1)}, bf16[2,32,2048]{2,1,0:T(8,128)(2,1)S(1)}, u32[]{:S(2)}, u32[]{:S(2)}) %collective-permute-start.17) | collective-permute-done | bytes 262176 | tf_op jit(solution)/shard_map/ppermute | solution.py:173
  70.2 0.7 fusion.12.refs_3_
  71.0 0.7 fusion.refs_2_
  71.8 1.9 %shard_map.75 = bf16[16,64,256]{2,1,0:T(8,128)(2,1)} custom-call(s32[16]{0:T(128)S(1)} %copy-done.1, f32[512,128]{1,0:T(8,128)S(1)} %fusion.1.refs_0_, f32[512,128]{1,0:T(8,128)S(1)} %fusion.11.refs_1_, f32[512,128]{1,0:T(8,128)S(1)} %fusion.refs_2_, f32[512,128]{1,0:T(8,128)S(1)} %fusion.12.refs_3_), custom_call_target="tpu_custom_call" | custom-call | flops 65536 | bytes 1572864 | tf_op jit(solution)/shard_map/pallas_call | solution.py:122
  73.6 4.8 %all-to-all-start = ((bf16[16,1,64,256]{3,2,1,0:T(8,128)(2,1)}), bf16[16,1,64,256]{3,2,1,0:T(8,128)(2,1)S(1)}, u32[]{:S(2)}, u32[]{:S(2)}) async-start(bf16[16,1,64,256]{3,2,1,0:T(8,128)(2,1)} %bitcast.10), calls=%async_computation | async-start | bytes 1048576 | tf_op jit(solution)/shard_map/all_to_all | solution.py:285
  78.5 0.7 dynamic_slice.79
  79.3 0.3 fusion.2
  79.6 0.7 constant_dynamic-slice_fusion.allowed_ref
  80.3 12.6 %all-to-all-done = bf16[16,1,64,256]{3,2,1,0:T(8,128)(2,1)S(1)} async-done(((bf16[16,1,64,256]{3,2,1,0:T(8,128)(2,1)}), bf16[16,1,64,256]{3,2,1,0:T(8,128)(2,1)S(1)}, u32[]{:S(2)}, u32[]{:S(2)}) %all-to-all-start) | async-done | bytes 524320 | tf_op jit(solution)/shard_map/all_to_all | solution.py:285
  92.9 0.9 shard_map.76
  (51 shorter events, 3.1 us)
Async XLA Ops:
  0.0 1.6 %copy-start = (bf16[16,16,4096]{2,1,0:T(8,128)(2,1)S(1)}, bf16[16,16,4096]{2,1,0:T(8,128)(2,1)}, u32[]{:S(2)}) copy-start(bf16[16,16,4096]{2,1,0:T(8,128)(2,1)} %param.9) | copy-start | bytes 6291460
  1.8 47.2 %collective-permute-start.13 = (bf16[128,2048]{1,0:T(8,128)(2,1)S(1)}, bf16[128,2048]{1,0:T(8,128)(2,1)S(1)}, u32[]{:S(2)}, u32[]{:S(2)}) collective-permute-start(bf16[128,2048]{1,0:T(8,128)(2,1)S(1)} %constant_dynamic-slice_fusion.2), channel_id=1, source_target_pairs={{0,2},{1,3},{2,0},{3,1},{4,6},{5,7},{6,4},{7,5},{8,10},{9,11},{10,... | collective-permute-start | bytes 1572872 | tf_op jit(solution)/shard_map/ppermute | solution.py:173
  4.8 1.0 %copy-start.2 = (f32[512,256]{1,0:T(8,128)S(1)}, f32[512,256]{1,0:T(8,128)}, u32[]{:S(2)}) copy-start(f32[512,256]{1,0:T(8,128)} %rows_ref.1) | copy-start | bytes 1572868
  10.3 2.9 %collective-permute-start.1 = (f16[128,4096]{1,0:T(8,128)(2,1)S(1)}, f16[128,4096]{1,0:T(8,128)(2,1)S(1)}, u32[]{:S(2)}, u32[]{:S(2)}) collective-permute-start(f16[128,4096]{1,0:T(8,128)(2,1)S(1)} %multiply_convert_fusion.1), channel_id=1, source_target_pairs={{0,1},{1,0},{2,3},{3,2},{4,5},{5,4},{6,7},{7,6},{8,9},{9,8},{10,11... | collective-permute-start | bytes 3145736 | tf_op jit(solution)/shard_map/ppermute | solution.py:173
  10.6 5.6 %collective-permute-start.6 = (f16[128,4096]{1,0:T(8,128)(2,1)S(1)}, f16[128,4096]{1,0:T(8,128)(2,1)S(1)}, u32[]{:S(2)}, u32[]{:S(2)}) collective-permute-start(f16[128,4096]{1,0:T(8,128)(2,1)S(1)} %multiply_convert_fusion), channel_id=1, source_target_pairs={{0,1},{1,0},{2,3},{3,2},{4,5},{5,4},{6,7},{7,6},{8,9},{9,8},{10,11... | collective-permute-start | bytes 3145736 | tf_op jit(solution)/shard_map/ppermute | solution.py:173
  13.9 8.4 %collective-permute-start.2 = (f16[64,2048]{1,0:T(8,128)(2,1)S(1)}, f16[64,2048]{1,0:T(8,128)(2,1)S(1)}, u32[]{:S(2)}, u32[]{:S(2)}) collective-permute-start(f16[64,2048]{1,0:T(8,128)(2,1)S(1)} %multiply_convert_fusion.7), channel_id=1, source_target_pairs={{0,2},{1,3},{2,0},{3,1},{4,6},{5,7},{6,4},{7,5},{8,10},{9,11},{10,... | collective-permute-start | bytes 786440 | tf_op jit(solution)/shard_map/ppermute | solution.py:173
  14.1 10.4 %collective-permute-start.4 = (f16[32,4096]{1,0:T(8,128)(2,1)S(1)}, f16[32,4096]{1,0:T(8,128)(2,1)S(1)}, u32[]{:S(2)}, u32[]{:S(2)}) collective-permute-start(f16[32,4096]{1,0:T(8,128)(2,1)S(1)} %multiply_convert_fusion.6), channel_id=1, source_target_pairs={{0,4},{1,5},{2,6},{3,7},{4,0},{5,1},{6,2},{7,3},{8,12},{9,13},{10,... | collective-permute-start | bytes 786440 | tf_op jit(solution)/shard_map/ppermute | solution.py:173
  22.7 5.5 %collective-permute-start.3 = (f16[32,2048]{1,0:T(8,128)(2,1)S(1)}, f16[32,2048]{1,0:T(8,128)(2,1)S(1)}, u32[]{:S(2)}, u32[]{:S(2)}) collective-permute-start(f16[32,2048]{1,0:T(8,128)(2,1)S(1)} %multiply_convert_fusion.11), channel_id=1, source_target_pairs={{0,4},{1,5},{2,6},{3,7},{4,0},{5,1},{6,2},{7,3},{8,12},{9,13},{10,... | collective-permute-start | bytes 393224 | tf_op jit(solution)/shard_map/ppermute | solution.py:173
  24.8 6.5 %collective-permute-start.5 = (f16[32,2048]{1,0:T(8,128)(2,1)S(1)}, f16[32,2048]{1,0:T(8,128)(2,1)S(1)}, u32[]{:S(2)}, u32[]{:S(2)}) collective-permute-start(f16[32,2048]{1,0:T(8,128)(2,1)S(1)} %multiply_convert_fusion.10), channel_id=1, source_target_pairs={{0,2},{1,3},{2,0},{3,1},{4,6},{5,7},{6,4},{7,5},{8,10},{9,11},{10,... | collective-permute-start | bytes 393224 | tf_op jit(solution)/shard_map/ppermute | solution.py:173
  26.4 8.8 %collective-permute-start.7 = (f16[64,2048]{1,0:T(8,128)(2,1)S(1)}, f16[64,2048]{1,0:T(8,128)(2,1)S(1)}, u32[]{:S(2)}, u32[]{:S(2)}) collective-permute-start(f16[64,2048]{1,0:T(8,128)(2,1)S(1)} %multiply_convert_fusion.5), channel_id=1, source_target_pairs={{0,2},{1,3},{2,0},{3,1},{4,6},{5,7},{6,4},{7,5},{8,10},{9,11},{10,... | collective-permute-start | bytes 786440 | tf_op jit(solution)/shard_map/ppermute | solution.py:173
  26.9 10.9 %collective-permute-start.9 = (f16[32,4096]{1,0:T(8,128)(2,1)S(1)}, f16[32,4096]{1,0:T(8,128)(2,1)S(1)}, u32[]{:S(2)}, u32[]{:S(2)}) collective-permute-start(f16[32,4096]{1,0:T(8,128)(2,1)S(1)} %multiply_convert_fusion.4), channel_id=1, source_target_pairs={{0,4},{1,5},{2,6},{3,7},{4,0},{5,1},{6,2},{7,3},{8,12},{9,13},{10,... | collective-permute-start | bytes 786440 | tf_op jit(solution)/shard_map/ppermute | solution.py:173
  31.5 12.3 %collective-permute-start.11 = (f16[2,32,2048]{2,1,0:T(8,128)(2,1)S(1)}, f16[2,32,2048]{2,1,0:T(8,128)(2,1)S(1)}, u32[]{:S(2)}, u32[]{:S(2)}) collective-permute-start(f16[2,32,2048]{2,1,0:T(8,128)(2,1)S(1)} %get-tuple-element.82), channel_id=1, source_target_pairs={{0,8},{1,9},{2,10},{3,11},{4,12},{5,13},{6,14},{7,15},{8,0},{9,1},... | collective-permute-start | bytes 786440 | tf_op jit(solution)/shard_map/ppermute | solution.py:173
  35.4 6.5 %collective-permute-start.8 = (f16[32,2048]{1,0:T(8,128)(2,1)S(1)}, f16[32,2048]{1,0:T(8,128)(2,1)S(1)}, u32[]{:S(2)}, u32[]{:S(2)}) collective-permute-start(f16[32,2048]{1,0:T(8,128)(2,1)S(1)} %multiply_convert_fusion.9), channel_id=1, source_target_pairs={{0,4},{1,5},{2,6},{3,7},{4,0},{5,1},{6,2},{7,3},{8,12},{9,13},{10,... | collective-permute-start | bytes 393224 | tf_op jit(solution)/shard_map/ppermute | solution.py:173
  38.0 5.6 %collective-permute-start.10 = (f16[32,2048]{1,0:T(8,128)(2,1)S(1)}, f16[32,2048]{1,0:T(8,128)(2,1)S(1)}, u32[]{:S(2)}, u32[]{:S(2)}) collective-permute-start(f16[32,2048]{1,0:T(8,128)(2,1)S(1)} %multiply_convert_fusion.8), channel_id=1, source_target_pairs={{0,2},{1,3},{2,0},{3,1},{4,6},{5,7},{6,4},{7,5},{8,10},{9,11},{10,... | collective-permute-start | bytes 393224 | tf_op jit(solution)/shard_map/ppermute | solution.py:173
  43.9 10.5 %collective-permute-start.14 = (bf16[128,2048]{1,0:T(8,128)(2,1)S(1)}, bf16[128,2048]{1,0:T(8,128)(2,1)S(1)}, u32[]{:S(2)}, u32[]{:S(2)}) collective-permute-start(bf16[128,2048]{1,0:T(8,128)(2,1)S(1)} %constant_dynamic-slice_fusion.3), channel_id=1, source_target_pairs={{0,2},{1,3},{2,0},{3,1},{4,6},{5,7},{6,4},{7,5},{8,10},{9,11},{10,... | collective-permute-start | bytes 1572872 | tf_op jit(solution)/shard_map/ppermute | solution.py:173
  46.7 15.9 %collective-permute-start = (bf16[256,2048]{1,0:T(8,128)(2,1)S(1)}, bf16[256,2048]{1,0:T(8,128)(2,1)S(1)}, u32[]{:S(2)}, u32[]{:S(2)}) collective-permute-start(bf16[256,2048]{1,0:T(8,128)(2,1)S(1)} %constant_dynamic-slice_fusion.1), channel_id=1, source_target_pairs={{0,1},{1,0},{2,3},{3,2},{4,5},{5,4},{6,7},{7,6},{8,9},{9,8},{10,11... | collective-permute-start | bytes 3145736 | tf_op jit(solution)/shard_map/ppermute | solution.py:173
  46.8 15.3 %collective-permute-start.16 = (f16[2,32,2048]{2,1,0:T(8,128)(2,1)S(1)}, f16[2,32,2048]{2,1,0:T(8,128)(2,1)S(1)}, u32[]{:S(2)}, u32[]{:S(2)}) collective-permute-start(f16[2,32,2048]{2,1,0:T(8,128)(2,1)S(1)} %multiply_convert_fusion.3), channel_id=1, source_target_pairs={{0,8},{1,9},{2,10},{3,11},{4,12},{5,13},{6,14},{7,15},{8,0},{9,1},... | collective-permute-start | bytes 786440 | tf_op jit(solution)/shard_map/ppermute | solution.py:173
  49.0 13.4 %collective-permute-start.12 = (bf16[2,32,2048]{2,1,0:T(8,128)(2,1)S(1)}, bf16[2,32,2048]{2,1,0:T(8,128)(2,1)S(1)}, u32[]{:S(2)}, u32[]{:S(2)}) collective-permute-start(bf16[2,32,2048]{2,1,0:T(8,128)(2,1)S(1)} %add_convert_fusion.1), channel_id=1, source_target_pairs={{0,4},{1,5},{2,6},{3,7},{4,0},{5,1},{6,2},{7,3},{8,12},{9,13},{10,... | collective-permute-start | bytes 786440 | tf_op jit(solution)/shard_map/ppermute | solution.py:173
  54.5 8.8 %collective-permute-start.15 = (bf16[256,2048]{1,0:T(8,128)(2,1)S(1)}, bf16[256,2048]{1,0:T(8,128)(2,1)S(1)}, u32[]{:S(2)}, u32[]{:S(2)}) collective-permute-start(bf16[256,2048]{1,0:T(8,128)(2,1)S(1)} %pad_maximum_fusion.3), channel_id=1, source_target_pairs={{0,1},{1,0},{2,3},{3,2},{4,5},{5,4},{6,7},{7,6},{8,9},{9,8},{10,11... | collective-permute-start | bytes 3145736 | tf_op jit(solution)/shard_map/ppermute | solution.py:173
  62.2 7.9 %collective-permute-start.17 = (bf16[2,32,2048]{2,1,0:T(8,128)(2,1)S(1)}, bf16[2,32,2048]{2,1,0:T(8,128)(2,1)S(1)}, u32[]{:S(2)}, u32[]{:S(2)}) collective-permute-start(bf16[2,32,2048]{2,1,0:T(8,128)(2,1)S(1)} %add_convert_fusion), channel_id=1, source_target_pairs={{0,4},{1,5},{2,6},{3,7},{4,0},{5,1},{6,2},{7,3},{8,12},{9,13},{10,... | collective-permute-start | bytes 786440 | tf_op jit(solution)/shard_map/ppermute | solution.py:173
  70.9 0.8 copy-start.1
  71.7 6.7 %copy-start.3 = (s32[8,12]{1,0:T(8,128)S(1)}, s32[8,12]{1,0:T(8,128)}, u32[]{:S(2)}) copy-start(s32[8,12]{1,0:T(8,128)} %param.11) | copy-start | bytes 1156
  71.7 7.5 %copy-start.4 = (s32[8]{0:T(128)S(1)}, s32[8]{0:T(128)}, u32[]{:S(2)}) copy-start(s32[8]{0:T(128)} %param.12) | copy-start | bytes 100
  71.7 7.6 %copy-start.5 = (s32[512]{0:T(512)S(1)}, s32[512]{0:T(512)}, u32[]{:S(2)}) copy-start(s32[512]{0:T(512)} %param.10) | copy-start | bytes 6148
  73.6 19.3 %all-to-all-start = ((bf16[16,1,64,256]{3,2,1,0:T(8,128)(2,1)}), bf16[16,1,64,256]{3,2,1,0:T(8,128)(2,1)S(1)}, u32[]{:S(2)}, u32[]{:S(2)}) async-start(bf16[16,1,64,256]{3,2,1,0:T(8,128)(2,1)} %bitcast.10), calls=%async_computation | async-start | bytes 1048576 | tf_op jit(solution)/shard_map/all_to_all | solution.py:285

commit v10 on v9

--- a/solution.py
+++ b/solution.py
@@ -10,7 +10,7 @@
 PATHS = 2
 UNIT = 4.0
 LANES = 128
-OTHER_VMEM = 43
+OTHER_VMEM = 44
 MINE_VMEM = 16
 
 
@@ -42,8 +42,8 @@
         out_ref[:, columns] = result[chunk * part:(chunk + 1) * part]
 
 
-def other_kernel(core_ref, rows_ref, columns_hbm, *refs):
-    outs, (high_ref, low_ref, columns_ref, sems) = refs[:-4], refs[-4:]
+def other_kernel(core_ref, rows_hbm, columns_hbm, *refs):
+    outs, (high_ref, low_ref, rows_ref, columns_ref, sems) = refs[:-5], refs[-5:]
     steps, _, block = columns_ref.shape
 
     def load(i):
@@ -51,8 +51,11 @@
             columns_hbm.at[:, i * block:(i + 1) * block], columns_ref.at[i], sems.at[i]
         )
 
+    load_rows = pltpu.make_async_copy(rows_hbm, rows_ref, sems.at[steps])
+    load_rows.start()
     for i in range(steps):
         load(i).start()
+    load_rows.wait()
     left = rows_of(core_ref, rows_ref)
     for i in range(steps):
         load(i).wait()
@@ -73,25 +76,27 @@
 
 
 def product(core, rows, columns, kernel, vmem):
-    first = kernel is other_kernel
     nrows, depth = rows.shape
     width = columns[0].shape[1]
     block = min(512, width)
     part = nrows // CORES // CHUNKS
     out = [jax.ShapeDtypeStruct((part, width), jnp.float32)] * CHUNKS
-    if first:
+    in_vmem = pl.BlockSpec(memory_space=pltpu.VMEM)
+    operand, scratch = in_vmem, []
+    if kernel is other_kernel:
         out = out + [jax.ShapeDtypeStruct((depth, width), jnp.bfloat16)] * 2
-    vmem_spec = pl.BlockSpec(memory_space=pltpu.VMEM)
+        operand = pl.BlockSpec(memory_space=pltpu.HBM)
+        scratch = [
+            pltpu.VMEM((nrows, depth), jnp.float32),
+            pltpu.VMEM((width // block, depth, block), jnp.float32),
+            pltpu.SemaphoreType.DMA((1 + width // block,)),
+        ]
     return pl.pallas_call(
         kernel,
-        in_specs=[pl.BlockSpec(memory_space=pltpu.SMEM), vmem_spec]
-        + [pl.BlockSpec(memory_space=pltpu.HBM) if first else vmem_spec] * len(columns),
-        out_specs=[vmem_spec] * len(out),
+        in_specs=[pl.BlockSpec(memory_space=pltpu.SMEM)] + [operand] * (1 + len(columns)),
+        out_specs=[in_vmem] * len(out),
         out_shape=out,
-        scratch_shapes=[
-            pltpu.VMEM((width // block, depth, block), jnp.float32),
-            pltpu.SemaphoreType.DMA((width // block,)),
-        ] if first else [],
+        scratch_shapes=scratch,
         compiler_params=pltpu.CompilerParams(vmem_limit_bytes=vmem * 1024 * 1024),
         cost_estimate=pl.CostEstimate(
             flops=3 * nrows * depth * width,
@@ -249,16 +254,12 @@
         start = offsets[ybit, width // 2][other]
         return lax.dynamic_slice(blocks, (first, start), (count, width // 2), allow_negative_indices=False)
 
-    early = features(blocks, 0, middle, 1)
-    queries, blocks = after((queries, blocks), early)
-    early = swap(early, ybit)
-
     *full, high, low = product(other_core, queries, [precond], other_kernel, OTHER_VMEM)
     sent = [pack(value) for value in full]
     got = [swap(value, 0) for value in sent]
     blocks = after(blocks, sent)
     near = features(blocks, 0, 2 * middle, 0)
-    late = features(blocks, middle, middle, 1)
+    far = [features(blocks, i * middle, middle, 1) for i in range(2)]
     sibling = swap(near, 0)
     mine = product(after(core, sent), queries, [high, low], mine_kernel, MINE_VMEM)
     one = paths(mine[0], got[0])
@@ -266,17 +267,21 @@
     two = paths(mine[1], after(got[1], sent))
     one = exchange(one, sent, 0)
     sent = messages(one, 1)
-    two = exchange(two, after(messages(two, 0), sent), 0)
+    two = exchange(two, after(messages(two, 0), (sent, sibling)), 0)
     one = halve(exchange(one, sent, 1))
     got_one = swap(pack(one), rest[-1])
-    two = halve(exchange(two, messages(two, 1), 1))
+    two = exchange(two, messages(two, 1), 1)
+    far[0] = swap(after(far[0], two[0]), ybit)
+    two = halve(two)
     sent = pack(two)
     one = (after(one, sent) + unpack(got_one)).astype(jnp.bfloat16)
     got_two = swap(sent, rest[-1])
-    late = swap(after(late, one), ybit)
+    far[1] = swap(after(far[1], one), ybit)
     one = gather(one)
-    far = jnp.concatenate([early, late], axis=0)
-    groups = [jnp.concatenate([near, sibling], axis=0), jnp.concatenate([far, swap(far, 0)], axis=0)]
+    groups = [
+        jnp.concatenate([near, sibling], axis=0),
+        jnp.concatenate(far + [swap(value, 0) for value in far], axis=0),
+    ]
     raws = [scores(group, one) for group in groups]
     two = gather((two + unpack(got_two)).astype(jnp.bfloat16), raws)
     raws = raws + [scores(group, two) for group in groups]

time: 94.1 us -> 93.2 us (level)
  waiting for transfers between devices: 44 us -> 47.7 us
  starting transfers between devices: 28.4 us -> 25 us
  local copies, waits for them, and re-layouts: 5.42 us -> 4.47 us
    ppermute x18 -> x19, waiting for transfers between devices: 31.4 us -> 34.9 us  [swap(): return lax.ppermute(value, 'rows', [(r, r ^ 1 << bit) for r in range(n)])]
    ppermute x18 -> x19, starting transfers between devices: 23.6 us -> 20.9 us  [swap(): return lax.ppermute(value, 'rows', [(r, r ^ 1 << bit) for r in range(n)])]
    unnamed x14 -> x15, local copies, waits for them, and re-layouts: 2.73 us -> 1.94 us
  transfers between devices with their start and end apart: 19 -> 20, of which waited for: 11 -> 13; matrix products, arithmetic and copies ran while one was open for 8% -> 8% of each run, Pallas kernels for 6% -> 2%
where the time goes in v10:
time: 93.2 us; the launch traced here: 92.9 us
  waiting for transfers between devices  47.7 us (51%)
  starting transfers between devices  25 us (27%)
  Pallas kernels  8.82 us (9%)
  local copies, waits for them, and re-layouts  4.47 us (5%)
  other arithmetic  3.46 us (4%)
  matrix products  3.11 us (3%)
    ppermute x19, waiting for transfers between devices, swap(): return lax.ppermute(value, 'rows', [(r, r ^ 1 << bit) for r in range(n)])  34.9 us
    ppermute x19, starting transfers between devices, swap(): return lax.ppermute(value, 'rows', [(r, r ^ 1 << bit) for r in range(n)])  20.9 us
    all_to_all x1, waiting for transfers between devices, shards(): lax.all_to_all(ordered, 'rows', split_axis=0, concat_axis=0, tiled=True)  12.7 us
    pallas_call x2, Pallas kernels, product(): pl.pallas_call(kernel, in_specs=[pl.BlockSpec(memory_space=pltpu.SMEM)] +...  6.08 us
    all_to_all x1, starting transfers between devices, shards(): lax.all_to_all(ordered, 'rows', split_axis=0, concat_axis=0, tiled=True)  4.04 us
    dot_general x4, matrix products, scores(): lax.dot_general(group, value, (((1,), (1,)), ((), ())), preferred_element...  2.85 us
    unnamed x15, local copies, waits for them, and re-layouts  1.94 us
    pallas_call x1, Pallas kernels, in_slot_order(): pl.pallas_call(order_kernel, in_specs=[pl.BlockSpec(memory_space=pltpu.SM...  1.88 us
  transfers between devices with their start and end apart: 20, of which 13 were waited for; matrix products, arithmetic and copies ran while one was open for 8% of the time, Pallas kernels for 2%

profile of v10, /device:TPU:0, one launch (start us, length us, event | category | flops | bytes accessed | tf_op | source)
XLA Modules:
  0.0 92.9 jit_solution(13696663984694957124)
XLA Ops:
  0.0 1.0 %copy-done.1 = f32[512,256]{1,0:T(8,128)S(1)} copy-done((f32[512,256]{1,0:T(8,128)S(1)}, f32[512,256]{1,0:T(8,128)}, u32[]{:S(2)}) %copy-start.1) | copy-done | bytes 524312
  1.0 4.3 %shard_map.73 = (f32[128,4096]{1,0:T(8,128)S(1)}, f32[128,4096]{1,0:T(8,128)S(1)}, bf16[256,4096]{1,0:T(8,128)(2,1)S(1)}, bf16[256,4096]{1,0:T(8,128)(2,1)S(1)}) custom-call(s32[1]{0:T(128)} %bitcast.1.core_ref, f32[512,256]{1,0:T(8,128)S(1)} %copy-done.1, f32[256,4096]{1,0:T(8,128)} %columns_hbm.1), custom_call_target="tpu_custom_call" | custom-call | flops 1610612736 | bytes 8388608 | tf_op jit(solution)/shard_map/pallas_call | solution.py:94
  5.5 0.5 collective-permute-start.1
  6.4 0.7 copy-done.2
  7.1 0.4 constant_dynamic-slice_fusion.2
  7.5 0.5 collective-permute-start
  8.1 1.8 %shard_map.74 = (f32[128,4096]{1,0:T(8,128)S(1)}, f32[128,4096]{1,0:T(8,128)S(1)}) custom-call(s32[1]{0:T(128)} %bitcast.2.core_ref, f32[512,256]{1,0:T(8,128)S(1)} %copy-done.1, bf16[256,4096]{1,0:T(8,128)(2,1)S(1)} %get-tuple-element.45.high_ref, bf16[256,4096]{1,0:T(8,128)(2,1)S(1)} %get-tuple-element.46.low_ref), custom_call_target="tpu_custom_call" | custom-call | flops 1610612736 | bytes 8388608 | tf_op jit(solution)/shard_map/pallas_call | solution.py:94
  9.9 0.4 constant_dynamic-slice_fusion.3
  10.3 0.3 multiply_add_fusion.1
  10.8 0.2 multiply_convert_fusion.7
  11.0 2.6 %collective-permute-start.2 = (f16[64,2048]{1,0:T(8,128)(2,1)S(1)}, f16[64,2048]{1,0:T(8,128)(2,1)S(1)}, u32[]{:S(2)}, u32[]{:S(2)}) collective-permute-start(f16[64,2048]{1,0:T(8,128)(2,1)S(1)} %multiply_convert_fusion.7), channel_id=1, source_target_pairs={{0,2},{1,3},{2,0},{3,1},{4,6},{5,7},{6,4},{7,5},{8,10},{9,11},{10,... | collective-permute-start | bytes 786440 | tf_op jit(solution)/shard_map/ppermute | solution.py:178
  13.7 1.7 %collective-permute-start.4 = (f16[32,4096]{1,0:T(8,128)(2,1)S(1)}, f16[32,4096]{1,0:T(8,128)(2,1)S(1)}, u32[]{:S(2)}, u32[]{:S(2)}) collective-permute-start(f16[32,4096]{1,0:T(8,128)(2,1)S(1)} %multiply_convert_fusion.6), channel_id=1, source_target_pairs={{0,4},{1,5},{2,6},{3,7},{4,0},{5,1},{6,2},{7,3},{8,12},{9,13},{10,... | collective-permute-start | bytes 786440 | tf_op jit(solution)/shard_map/ppermute | solution.py:178
  15.4 0.3 multiply_add_fusion
  15.9 0.2 multiply_convert_fusion.5
  16.1 4.5 %collective-permute-done.2 = f16[64,2048]{1,0:T(8,128)(2,1)S(1)} collective-permute-done((f16[64,2048]{1,0:T(8,128)(2,1)S(1)}, f16[64,2048]{1,0:T(8,128)(2,1)S(1)}, u32[]{:S(2)}, u32[]{:S(2)}) %collective-permute-start.2) | collective-permute-done | bytes 262176 | tf_op jit(solution)/shard_map/ppermute | solution.py:178
  20.8 1.8 %collective-permute-start.3 = (f16[32,2048]{1,0:T(8,128)(2,1)S(1)}, f16[32,2048]{1,0:T(8,128)(2,1)S(1)}, u32[]{:S(2)}, u32[]{:S(2)}) collective-permute-start(f16[32,2048]{1,0:T(8,128)(2,1)S(1)} %multiply_convert_fusion.11), channel_id=1, source_target_pairs={{0,4},{1,5},{2,6},{3,7},{4,0},{5,1},{6,2},{7,3},{8,12},{9,13},{10,... | collective-permute-start | bytes 393224 | tf_op jit(solution)/shard_map/ppermute | solution.py:178
  22.9 1.6 %collective-permute-start.5 = (f16[32,2048]{1,0:T(8,128)(2,1)S(1)}, f16[32,2048]{1,0:T(8,128)(2,1)S(1)}, u32[]{:S(2)}, u32[]{:S(2)}) collective-permute-start(f16[32,2048]{1,0:T(8,128)(2,1)S(1)} %multiply_convert_fusion.10), channel_id=1, source_target_pairs={{0,2},{1,3},{2,0},{3,1},{4,6},{5,7},{6,4},{7,5},{8,10},{9,11},{10,... | collective-permute-start | bytes 393224 | tf_op jit(solution)/shard_map/ppermute | solution.py:178
  24.6 0.5 collective-permute-start.7
  25.0 1.1 %collective-permute-start.9 = (f16[32,4096]{1,0:T(8,128)(2,1)S(1)}, f16[32,4096]{1,0:T(8,128)(2,1)S(1)}, u32[]{:S(2)}, u32[]{:S(2)}) collective-permute-start(f16[32,4096]{1,0:T(8,128)(2,1)S(1)} %multiply_convert_fusion.4), channel_id=1, source_target_pairs={{0,4},{1,5},{2,6},{3,7},{4,0},{5,1},{6,2},{7,3},{8,12},{9,13},{10,... | collective-permute-start | bytes 786440 | tf_op jit(solution)/shard_map/ppermute | solution.py:178
  26.3 3.2 %collective-permute-done.5 = f16[32,2048]{1,0:T(8,128)(2,1)S(1)} collective-permute-done((f16[32,2048]{1,0:T(8,128)(2,1)S(1)}, f16[32,2048]{1,0:T(8,128)(2,1)S(1)}, u32[]{:S(2)}, u32[]{:S(2)}) %collective-permute-start.5) | collective-permute-done | bytes 131104 | tf_op jit(solution)/shard_map/ppermute | solution.py:178
  29.7 2.7 %collective-permute-start.11 = (f16[2,32,2048]{2,1,0:T(8,128)(2,1)S(1)}, f16[2,32,2048]{2,1,0:T(8,128)(2,1)S(1)}, u32[]{:S(2)}, u32[]{:S(2)}) collective-permute-start(f16[2,32,2048]{2,1,0:T(8,128)(2,1)S(1)} %get-tuple-element.82), channel_id=1, source_target_pairs={{0,8},{1,9},{2,10},{3,11},{4,12},{5,13},{6,14},{7,15},{8,0},{9,1},... | collective-permute-start | bytes 786440 | tf_op jit(solution)/shard_map/ppermute | solution.py:178
  32.3 1.1 %collective-permute-done.7 = f16[64,2048]{1,0:T(8,128)(2,1)S(1)} collective-permute-done((f16[64,2048]{1,0:T(8,128)(2,1)S(1)}, f16[64,2048]{1,0:T(8,128)(2,1)S(1)}, u32[]{:S(2)}, u32[]{:S(2)}) %collective-permute-start.7) | collective-permute-done | bytes 262176 | tf_op jit(solution)/shard_map/ppermute | solution.py:178
  33.5 0.2 multiply_add_fusion.3
  33.7 1.1 %collective-permute-start.8 = (f16[32,2048]{1,0:T(8,128)(2,1)S(1)}, f16[32,2048]{1,0:T(8,128)(2,1)S(1)}, u32[]{:S(2)}, u32[]{:S(2)}) collective-permute-start(f16[32,2048]{1,0:T(8,128)(2,1)S(1)} %multiply_convert_fusion.9), channel_id=1, source_target_pairs={{0,4},{1,5},{2,6},{3,7},{4,0},{5,1},{6,2},{7,3},{8,12},{9,13},{10,... | collective-permute-start | bytes 393224 | tf_op jit(solution)/shard_map/ppermute | solution.py:178
  34.8 1.5 %collective-permute-done.9 = f16[32,4096]{1,0:T(8,128)(2,1)S(1)} collective-permute-done((f16[32,4096]{1,0:T(8,128)(2,1)S(1)}, f16[32,4096]{1,0:T(8,128)(2,1)S(1)}, u32[]{:S(2)}, u32[]{:S(2)}) %collective-permute-start.9) | collective-permute-done | bytes 262176 | tf_op jit(solution)/shard_map/ppermute | solution.py:178
  36.6 1.7 %collective-permute-start.10 = (f16[32,2048]{1,0:T(8,128)(2,1)S(1)}, f16[32,2048]{1,0:T(8,128)(2,1)S(1)}, u32[]{:S(2)}, u32[]{:S(2)}) collective-permute-start(f16[32,2048]{1,0:T(8,128)(2,1)S(1)} %multiply_convert_fusion.8), channel_id=1, source_target_pairs={{0,2},{1,3},{2,0},{3,1},{4,6},{5,7},{6,4},{7,5},{8,10},{9,11},{10,... | collective-permute-start | bytes 393224 | tf_op jit(solution)/shard_map/ppermute | solution.py:178
  38.2 1.8 %collective-permute-done.8 = f16[32,2048]{1,0:T(8,128)(2,1)S(1)} collective-permute-done((f16[32,2048]{1,0:T(8,128)(2,1)S(1)}, f16[32,2048]{1,0:T(8,128)(2,1)S(1)}, u32[]{:S(2)}, u32[]{:S(2)}) %collective-permute-start.8) | collective-permute-done | bytes 131104 | tf_op jit(solution)/shard_map/ppermute | solution.py:178
  40.1 1.5 %collective-permute-done.10 = f16[32,2048]{1,0:T(8,128)(2,1)S(1)} collective-permute-done((f16[32,2048]{1,0:T(8,128)(2,1)S(1)}, f16[32,2048]{1,0:T(8,128)(2,1)S(1)}, u32[]{:S(2)}, u32[]{:S(2)}) %collective-permute-start.10) | collective-permute-done | bytes 131104 | tf_op jit(solution)/shard_map/ppermute | solution.py:178
  41.8 1.7 %collective-permute-start.17 = (f16[2,32,2048]{2,1,0:T(8,128)(2,1)S(1)}, f16[2,32,2048]{2,1,0:T(8,128)(2,1)S(1)}, u32[]{:S(2)}, u32[]{:S(2)}) collective-permute-start(f16[2,32,2048]{2,1,0:T(8,128)(2,1)S(1)} %multiply_convert_fusion.3), channel_id=1, source_target_pairs={{0,8},{1,9},{2,10},{3,11},{4,12},{5,13},{6,14},{7,15},{8,0},{9,1},... | collective-permute-start | bytes 786440 | tf_op jit(solution)/shard_map/ppermute | solution.py:178
  43.6 0.7 collective-permute-start.12
  44.2 2.0 %collective-permute-start.14 = (bf16[128,2048]{1,0:T(8,128)(2,1)S(1)}, bf16[128,2048]{1,0:T(8,128)(2,1)S(1)}, u32[]{:S(2)}, u32[]{:S(2)}) collective-permute-start(bf16[128,2048]{1,0:T(8,128)(2,1)S(1)} %get-tuple-element.57), channel_id=1, source_target_pairs={{0,2},{1,3},{2,0},{3,1},{4,6},{5,7},{6,4},{7,5},{8,10},{9,11},{10,... | collective-permute-start | bytes 1572872 | tf_op jit(solution)/shard_map/ppermute | solution.py:178
  46.3 7.3 %collective-permute-done.17 = f16[2,32,2048]{2,1,0:T(8,128)(2,1)S(1)} collective-permute-done((f16[2,32,2048]{2,1,0:T(8,128)(2,1)S(1)}, f16[2,32,2048]{2,1,0:T(8,128)(2,1)S(1)}, u32[]{:S(2)}, u32[]{:S(2)}) %collective-permute-start.17) | collective-permute-done | bytes 262176 | tf_op jit(solution)/shard_map/ppermute | solution.py:178
  53.8 0.8 collective-permute-done.12
  54.7 11.7 %collective-permute-done.13 = bf16[128,2048]{1,0:T(8,128)(2,1)S(1)} collective-permute-done((bf16[128,2048]{1,0:T(8,128)(2,1)S(1)}, bf16[128,2048]{1,0:T(8,128)(2,1)S(1)}, u32[]{:S(2)}, u32[]{:S(2)}) %collective-permute-start.13) | collective-permute-done | bytes 524320 | tf_op jit(solution)/shard_map/ppermute | solution.py:178
  66.4 0.7 fusion.1.refs_0_
  67.2 0.6 collective-permute-start.16
  67.9 0.5 collective-permute-done.15
  68.4 0.9 collective-permute-done.16
  69.3 0.7 fusion.11.refs_1_
  70.2 0.7 fusion.12.refs_3_
  70.9 0.7 fusion.refs_2_
  71.7 1.9 %shard_map.75 = bf16[16,64,256]{2,1,0:T(8,128)(2,1)} custom-call(s32[16]{0:T(128)S(1)} %copy-done, f32[512,128]{1,0:T(8,128)S(1)} %fusion.1.refs_0_, f32[512,128]{1,0:T(8,128)S(1)} %fusion.11.refs_1_, f32[512,128]{1,0:T(8,128)S(1)} %fusion.refs_2_, f32[512,128]{1,0:T(8,128)S(1)} %fusion.12.refs_3_), custom_call_target="tpu_custom_call" | custom-call | flops 65536 | bytes 1572864 | tf_op jit(solution)/shard_map/pallas_call | solution.py:127
  73.6 4.0 %all-to-all-start = ((bf16[16,1,64,256]{3,2,1,0:T(8,128)(2,1)}), bf16[16,1,64,256]{3,2,1,0:T(8,128)(2,1)S(1)}, u32[]{:S(2)}, u32[]{:S(2)}) async-start(bf16[16,1,64,256]{3,2,1,0:T(8,128)(2,1)} %bitcast.10), calls=%async_computation | async-start | bytes 1048576 | tf_op jit(solution)/shard_map/all_to_all | solution.py:290
  77.7 0.6 dynamic_slice.79
  78.4 0.3 fusion.2
  78.7 0.6 constant_dynamic-slice_fusion.allowed_ref
  79.3 12.7 %all-to-all-done = bf16[16,1,64,256]{3,2,1,0:T(8,128)(2,1)S(1)} async-done(((bf16[16,1,64,256]{3,2,1,0:T(8,128)(2,1)}), bf16[16,1,64,256]{3,2,1,0:T(8,128)(2,1)S(1)}, u32[]{:S(2)}, u32[]{:S(2)}) %all-to-all-start) | async-done | bytes 524320 | tf_op jit(solution)/shard_map/all_to_all | solution.py:290
  92.1 0.9 shard_map.76
  (52 shorter events, 3.2 us)
Async XLA Ops:
  0.0 1.0 %copy-start.1 = (f32[512,256]{1,0:T(8,128)S(1)}, f32[512,256]{1,0:T(8,128)}, u32[]{:S(2)}) copy-start(f32[512,256]{1,0:T(8,128)} %rows_ref) | copy-start | bytes 1572868
  5.5 1.6 %copy-start.2 = (bf16[16,16,4096]{2,1,0:T(8,128)(2,1)S(1)}, bf16[16,16,4096]{2,1,0:T(8,128)(2,1)}, u32[]{:S(2)}) copy-start(bf16[16,16,4096]{2,1,0:T(8,128)(2,1)} %param.9) | copy-start | bytes 6291460
  5.5 4.8 %collective-permute-start.1 = (f16[128,4096]{1,0:T(8,128)(2,1)S(1)}, f16[128,4096]{1,0:T(8,128)(2,1)S(1)}, u32[]{:S(2)}, u32[]{:S(2)}) collective-permute-start(f16[128,4096]{1,0:T(8,128)(2,1)S(1)} %multiply_convert_fusion.1), channel_id=1, source_target_pairs={{0,1},{1,0},{2,3},{3,2},{4,5},{5,4},{6,7},{7,6},{8,9},{9,8},{10,11... | collective-permute-start | bytes 3145736 | tf_op jit(solution)/shard_map/ppermute | solution.py:178
  6.3 9.1 %collective-permute-start.6 = (f16[128,4096]{1,0:T(8,128)(2,1)S(1)}, f16[128,4096]{1,0:T(8,128)(2,1)S(1)}, u32[]{:S(2)}, u32[]{:S(2)}) collective-permute-start(f16[128,4096]{1,0:T(8,128)(2,1)S(1)} %multiply_convert_fusion), channel_id=1, source_target_pairs={{0,1},{1,0},{2,3},{3,2},{4,5},{5,4},{6,7},{7,6},{8,9},{9,8},{10,11... | collective-permute-start | bytes 3145736 | tf_op jit(solution)/shard_map/ppermute | solution.py:178
  7.5 17.0 %collective-permute-start = (bf16[256,2048]{1,0:T(8,128)(2,1)S(1)}, bf16[256,2048]{1,0:T(8,128)(2,1)S(1)}, u32[]{:S(2)}, u32[]{:S(2)}) collective-permute-start(bf16[256,2048]{1,0:T(8,128)(2,1)S(1)} %constant_dynamic-slice_fusion.2), channel_id=1, source_target_pairs={{0,1},{1,0},{2,3},{3,2},{4,5},{5,4},{6,7},{7,6},{8,9},{9,8},{10,11... | collective-permute-start | bytes 3145736 | tf_op jit(solution)/shard_map/ppermute | solution.py:178
  11.0 9.6 %collective-permute-start.2 = (f16[64,2048]{1,0:T(8,128)(2,1)S(1)}, f16[64,2048]{1,0:T(8,128)(2,1)S(1)}, u32[]{:S(2)}, u32[]{:S(2)}) collective-permute-start(f16[64,2048]{1,0:T(8,128)(2,1)S(1)} %multiply_convert_fusion.7), channel_id=1, source_target_pairs={{0,2},{1,3},{2,0},{3,1},{4,6},{5,7},{6,4},{7,5},{8,10},{9,11},{10,... | collective-permute-start | bytes 786440 | tf_op jit(solution)/shard_map/ppermute | solution.py:178
  13.7 9.0 %collective-permute-start.4 = (f16[32,4096]{1,0:T(8,128)(2,1)S(1)}, f16[32,4096]{1,0:T(8,128)(2,1)S(1)}, u32[]{:S(2)}, u32[]{:S(2)}) collective-permute-start(f16[32,4096]{1,0:T(8,128)(2,1)S(1)} %multiply_convert_fusion.6), channel_id=1, source_target_pairs={{0,4},{1,5},{2,6},{3,7},{4,0},{5,1},{6,2},{7,3},{8,12},{9,13},{10,... | collective-permute-start | bytes 786440 | tf_op jit(solution)/shard_map/ppermute | solution.py:178
  20.8 5.4 %collective-permute-start.3 = (f16[32,2048]{1,0:T(8,128)(2,1)S(1)}, f16[32,2048]{1,0:T(8,128)(2,1)S(1)}, u32[]{:S(2)}, u32[]{:S(2)}) collective-permute-start(f16[32,2048]{1,0:T(8,128)(2,1)S(1)} %multiply_convert_fusion.11), channel_id=1, source_target_pairs={{0,4},{1,5},{2,6},{3,7},{4,0},{5,1},{6,2},{7,3},{8,12},{9,13},{10,... | collective-permute-start | bytes 393224 | tf_op jit(solution)/shard_map/ppermute | solution.py:178
  22.9 6.5 %collective-permute-start.5 = (f16[32,2048]{1,0:T(8,128)(2,1)S(1)}, f16[32,2048]{1,0:T(8,128)(2,1)S(1)}, u32[]{:S(2)}, u32[]{:S(2)}) collective-permute-start(f16[32,2048]{1,0:T(8,128)(2,1)S(1)} %multiply_convert_fusion.10), channel_id=1, source_target_pairs={{0,2},{1,3},{2,0},{3,1},{4,6},{5,7},{6,4},{7,5},{8,10},{9,11},{10,... | collective-permute-start | bytes 393224 | tf_op jit(solution)/shard_map/ppermute | solution.py:178
  24.6 8.9 %collective-permute-start.7 = (f16[64,2048]{1,0:T(8,128)(2,1)S(1)}, f16[64,2048]{1,0:T(8,128)(2,1)S(1)}, u32[]{:S(2)}, u32[]{:S(2)}) collective-permute-start(f16[64,2048]{1,0:T(8,128)(2,1)S(1)} %multiply_convert_fusion.5), channel_id=1, source_target_pairs={{0,2},{1,3},{2,0},{3,1},{4,6},{5,7},{6,4},{7,5},{8,10},{9,11},{10,... | collective-permute-start | bytes 786440 | tf_op jit(solution)/shard_map/ppermute | solution.py:178
  25.0 11.3 %collective-permute-start.9 = (f16[32,4096]{1,0:T(8,128)(2,1)S(1)}, f16[32,4096]{1,0:T(8,128)(2,1)S(1)}, u32[]{:S(2)}, u32[]{:S(2)}) collective-permute-start(f16[32,4096]{1,0:T(8,128)(2,1)S(1)} %multiply_convert_fusion.4), channel_id=1, source_target_pairs={{0,4},{1,5},{2,6},{3,7},{4,0},{5,1},{6,2},{7,3},{8,12},{9,13},{10,... | collective-permute-start | bytes 786440 | tf_op jit(solution)/shard_map/ppermute | solution.py:178
  29.7 13.9 %collective-permute-start.11 = (f16[2,32,2048]{2,1,0:T(8,128)(2,1)S(1)}, f16[2,32,2048]{2,1,0:T(8,128)(2,1)S(1)}, u32[]{:S(2)}, u32[]{:S(2)}) collective-permute-start(f16[2,32,2048]{2,1,0:T(8,128)(2,1)S(1)} %get-tuple-element.82), channel_id=1, source_target_pairs={{0,8},{1,9},{2,10},{3,11},{4,12},{5,13},{6,14},{7,15},{8,0},{9,1},... | collective-permute-start | bytes 786440 | tf_op jit(solution)/shard_map/ppermute | solution.py:178
  33.7 6.3 %collective-permute-start.8 = (f16[32,2048]{1,0:T(8,128)(2,1)S(1)}, f16[32,2048]{1,0:T(8,128)(2,1)S(1)}, u32[]{:S(2)}, u32[]{:S(2)}) collective-permute-start(f16[32,2048]{1,0:T(8,128)(2,1)S(1)} %multiply_convert_fusion.9), channel_id=1, source_target_pairs={{0,4},{1,5},{2,6},{3,7},{4,0},{5,1},{6,2},{7,3},{8,12},{9,13},{10,... | collective-permute-start | bytes 393224 | tf_op jit(solution)/shard_map/ppermute | solution.py:178
  36.6 5.0 %collective-permute-start.10 = (f16[32,2048]{1,0:T(8,128)(2,1)S(1)}, f16[32,2048]{1,0:T(8,128)(2,1)S(1)}, u32[]{:S(2)}, u32[]{:S(2)}) collective-permute-start(f16[32,2048]{1,0:T(8,128)(2,1)S(1)} %multiply_convert_fusion.8), channel_id=1, source_target_pairs={{0,2},{1,3},{2,0},{3,1},{4,6},{5,7},{6,4},{7,5},{8,10},{9,11},{10,... | collective-permute-start | bytes 393224 | tf_op jit(solution)/shard_map/ppermute | solution.py:178
  41.8 11.8 %collective-permute-start.17 = (f16[2,32,2048]{2,1,0:T(8,128)(2,1)S(1)}, f16[2,32,2048]{2,1,0:T(8,128)(2,1)S(1)}, u32[]{:S(2)}, u32[]{:S(2)}) collective-permute-start(f16[2,32,2048]{2,1,0:T(8,128)(2,1)S(1)} %multiply_convert_fusion.3), channel_id=1, source_target_pairs={{0,8},{1,9},{2,10},{3,11},{4,12},{5,13},{6,14},{7,15},{8,0},{9,1},... | collective-permute-start | bytes 786440 | tf_op jit(solution)/shard_map/ppermute | solution.py:178
  43.6 11.0 %collective-permute-start.12 = (bf16[2,32,2048]{2,1,0:T(8,128)(2,1)S(1)}, bf16[2,32,2048]{2,1,0:T(8,128)(2,1)S(1)}, u32[]{:S(2)}, u32[]{:S(2)}) collective-permute-start(bf16[2,32,2048]{2,1,0:T(8,128)(2,1)S(1)} %add_convert_fusion.1), channel_id=1, source_target_pairs={{0,4},{1,5},{2,6},{3,7},{4,0},{5,1},{6,2},{7,3},{8,12},{9,13},{10,... | collective-permute-start | bytes 786440 | tf_op jit(solution)/shard_map/ppermute | solution.py:178
  44.2 22.9 %collective-permute-start.14 = (bf16[128,2048]{1,0:T(8,128)(2,1)S(1)}, bf16[128,2048]{1,0:T(8,128)(2,1)S(1)}, u32[]{:S(2)}, u32[]{:S(2)}) collective-permute-start(bf16[128,2048]{1,0:T(8,128)(2,1)S(1)} %get-tuple-element.57), channel_id=1, source_target_pairs={{0,2},{1,3},{2,0},{3,1},{4,6},{5,7},{6,4},{7,5},{8,10},{9,11},{10,... | collective-permute-start | bytes 1572872 | tf_op jit(solution)/shard_map/ppermute | solution.py:178
  46.3 20.2 %collective-permute-start.13 = (bf16[128,2048]{1,0:T(8,128)(2,1)S(1)}, bf16[128,2048]{1,0:T(8,128)(2,1)S(1)}, u32[]{:S(2)}, u32[]{:S(2)}) collective-permute-start(bf16[128,2048]{1,0:T(8,128)(2,1)S(1)} %get-tuple-element.56), channel_id=1, source_target_pairs={{0,2},{1,3},{2,0},{3,1},{4,6},{5,7},{6,4},{7,5},{8,10},{9,11},{10,... | collective-permute-start | bytes 1572872 | tf_op jit(solution)/shard_map/ppermute | solution.py:178
  53.7 16.3 %collective-permute-start.18 = (bf16[2,32,2048]{2,1,0:T(8,128)(2,1)S(1)}, bf16[2,32,2048]{2,1,0:T(8,128)(2,1)S(1)}, u32[]{:S(2)}, u32[]{:S(2)}) collective-permute-start(bf16[2,32,2048]{2,1,0:T(8,128)(2,1)S(1)} %add_convert_fusion), channel_id=1, source_target_pairs={{0,4},{1,5},{2,6},{3,7},{4,0},{5,1},{6,2},{7,3},{8,12},{9,13},{10,... | collective-permute-start | bytes 786440 | tf_op jit(solution)/shard_map/ppermute | solution.py:178
  66.4 1.9 %collective-permute-start.15 = (bf16[128,2048]{1,0:T(8,128)(2,1)S(1)}, bf16[128,2048]{1,0:T(8,128)(2,1)S(1)}, u32[]{:S(2)}, u32[]{:S(2)}) collective-permute-start(bf16[128,2048]{1,0:T(8,128)(2,1)S(1)} %collective-permute-done.13), channel_id=1, source_target_pairs={{0,1},{1,0},{2,3},{3,2},{4,5},{5,4},{6,7},{7,6},{8,9},{9,8},{10,11... | collective-permute-start | bytes 1572872 | tf_op jit(solution)/shard_map/ppermute | solution.py:178
  67.2 2.1 %collective-permute-start.16 = (bf16[128,2048]{1,0:T(8,128)(2,1)S(1)}, bf16[128,2048]{1,0:T(8,128)(2,1)S(1)}, u32[]{:S(2)}, u32[]{:S(2)}) collective-permute-start(bf16[128,2048]{1,0:T(8,128)(2,1)S(1)} %collective-permute-done.14), channel_id=1, source_target_pairs={{0,1},{1,0},{2,3},{3,2},{4,5},{5,4},{6,7},{7,6},{8,9},{9,8},{10,11... | collective-permute-start | bytes 1572872 | tf_op jit(solution)/shard_map/ppermute | solution.py:178
  70.9 0.7 copy-start
  71.6 6.0 %copy-start.3 = (s32[8,12]{1,0:T(8,128)S(1)}, s32[8,12]{1,0:T(8,128)}, u32[]{:S(2)}) copy-start(s32[8,12]{1,0:T(8,128)} %param.11) | copy-start | bytes 1156
  71.6 6.7 %copy-start.4 = (s32[8]{0:T(128)S(1)}, s32[8]{0:T(128)}, u32[]{:S(2)}) copy-start(s32[8]{0:T(128)} %param.12) | copy-start | bytes 100
  71.7 6.8 %copy-start.5 = (s32[512]{0:T(512)S(1)}, s32[512]{0:T(512)}, u32[]{:S(2)}) copy-start(s32[512]{0:T(512)} %param.10) | copy-start | bytes 6148
  73.6 18.5 %all-to-all-start = ((bf16[16,1,64,256]{3,2,1,0:T(8,128)(2,1)}), bf16[16,1,64,256]{3,2,1,0:T(8,128)(2,1)S(1)}, u32[]{:S(2)}, u32[]{:S(2)}) async-start(bf16[16,1,64,256]{3,2,1,0:T(8,128)(2,1)} %bitcast.10), calls=%async_computation | async-start | bytes 1048576 | tf_op jit(solution)/shard_map/all_to_all | solution.py:290

commit v11 on v10

--- a/solution.py
+++ b/solution.py
@@ -254,12 +254,16 @@
         start = offsets[ybit, width // 2][other]
         return lax.dynamic_slice(blocks, (first, start), (count, width // 2), allow_negative_indices=False)
 
+    early = features(blocks, 0, middle, 1)
+    other_core, blocks = after((other_core, blocks), early)
+    early = swap(early, ybit)
+
     *full, high, low = product(other_core, queries, [precond], other_kernel, OTHER_VMEM)
     sent = [pack(value) for value in full]
     got = [swap(value, 0) for value in sent]
     blocks = after(blocks, sent)
     near = features(blocks, 0, 2 * middle, 0)
-    far = [features(blocks, i * middle, middle, 1) for i in range(2)]
+    late = features(blocks, middle, middle, 1)
     sibling = swap(near, 0)
     mine = product(after(core, sent), queries, [high, low], mine_kernel, MINE_VMEM)
     one = paths(mine[0], got[0])
@@ -271,16 +275,16 @@
     one = halve(exchange(one, sent, 1))
     got_one = swap(pack(one), rest[-1])
     two = exchange(two, messages(two, 1), 1)
-    far[0] = swap(after(far[0], two[0]), ybit)
     two = halve(two)
     sent = pack(two)
     one = (after(one, sent) + unpack(got_one)).astype(jnp.bfloat16)
     got_two = swap(sent, rest[-1])
-    far[1] = swap(after(far[1], one), ybit)
+    late, early = after((late, early), one)
+    late = swap(late, ybit)
     one = gather(one)
     groups = [
         jnp.concatenate([near, sibling], axis=0),
-        jnp.concatenate(far + [swap(value, 0) for value in far], axis=0),
+        jnp.concatenate([early, late, swap(early, 0), swap(late, 0)], axis=0),
     ]
     raws = [scores(group, one) for group in groups]
     two = gather((two + unpack(got_two)).astype(jnp.bfloat16), raws)

time: 93.2 us -> 86.1 us (0.924)
  waiting for transfers between devices: 47.7 us -> 42.7 us
  starting transfers between devices: 25 us -> 21.9 us
    ppermute x19, waiting for transfers between devices: 34.9 us -> 30 us  [swap(): return lax.ppermute(value, 'rows', [(r, r ^ 1 << bit) for r in range(n)])]
    ppermute x19, starting transfers between devices: 20.9 us -> 18.2 us  [swap(): return lax.ppermute(value, 'rows', [(r, r ^ 1 << bit) for r in range(n)])]
  transfers between devices with their start and end apart: 20 -> 20, of which waited for: 13 -> 13; matrix products, arithmetic and copies ran while one was open for 8% -> 9% of each run, Pallas kernels for 2% -> 7%
where the time goes in v11:
time: 86.1 us; the launch traced here: 85.8 us
  waiting for transfers between devices  42.7 us (50%)
  starting transfers between devices  21.9 us (25%)
  Pallas kernels  8.85 us (10%)
  local copies, waits for them, and re-layouts  5.31 us (6%)
  other arithmetic  3.45 us (4%)
  matrix products  3.15 us (4%)
    ppermute x19, waiting for transfers between devices, swap(): return lax.ppermute(value, 'rows', [(r, r ^ 1 << bit) for r in range(n)])  30 us
    ppermute x19, starting transfers between devices, swap(): return lax.ppermute(value, 'rows', [(r, r ^ 1 << bit) for r in range(n)])  18.2 us
    all_to_all x1, waiting for transfers between devices, shards(): lax.all_to_all(ordered, 'rows', split_axis=0, concat_axis=0, tiled=True)  12.7 us
    pallas_call x2, Pallas kernels, product(): pl.pallas_call(kernel, in_specs=[pl.BlockSpec(memory_space=pltpu.SMEM)] +...  6.1 us
    all_to_all x1, starting transfers between devices, shards(): lax.all_to_all(ordered, 'rows', split_axis=0, concat_axis=0, tiled=True)  3.76 us
    dot_general x4, matrix products, scores(): lax.dot_general(group, value, (((1,), (1,)), ((), ())), preferred_element...  2.88 us
    unnamed x15, local copies, waits for them, and re-layouts  2.76 us
    pallas_call x1, Pallas kernels, in_slot_order(): pl.pallas_call(order_kernel, in_specs=[pl.BlockSpec(memory_space=pltpu.SM...  1.88 us
  transfers between devices with their start and end apart: 20, of which 13 were waited for; matrix products, arithmetic and copies ran while one was open for 9% of the time, Pallas kernels for 7%

profile of v11, /device:TPU:0, one launch (start us, length us, event | category | flops | bytes accessed | tf_op | source)
XLA Modules:
  0.0 85.8 jit_solution(6313155223544342345)
XLA Ops:
  0.0 1.6 %copy-done = bf16[16,16,4096]{2,1,0:T(8,128)(2,1)S(1)} copy-done((bf16[16,16,4096]{2,1,0:T(8,128)(2,1)S(1)}, bf16[16,16,4096]{2,1,0:T(8,128)(2,1)}, u32[]{:S(2)}) %copy-start) | copy-done | bytes 2097176
  1.6 0.2 constant_dynamic-slice_fusion.2
  1.8 3.0 %collective-permute-start.13 = (bf16[128,2048]{1,0:T(8,128)(2,1)S(1)}, bf16[128,2048]{1,0:T(8,128)(2,1)S(1)}, u32[]{:S(2)}, u32[]{:S(2)}) collective-permute-start(bf16[128,2048]{1,0:T(8,128)(2,1)S(1)} %constant_dynamic-slice_fusion.2), channel_id=1, source_target_pairs={{0,2},{1,3},{2,0},{3,1},{4,6},{5,7},{6,4},{7,5},{8,10},{9,11},{10,... | collective-permute-start | bytes 1572872 | tf_op jit(solution)/shard_map/ppermute | solution.py:178
  4.8 1.0 %copy-done.2 = f32[512,256]{1,0:T(8,128)S(1)} copy-done((f32[512,256]{1,0:T(8,128)S(1)}, f32[512,256]{1,0:T(8,128)}, u32[]{:S(2)}) %copy-start.2) | copy-done | bytes 524312
  5.9 4.3 %shard_map.73 = (f32[128,4096]{1,0:T(8,128)S(1)}, f32[128,4096]{1,0:T(8,128)S(1)}, bf16[256,4096]{1,0:T(8,128)(2,1)S(1)}, bf16[256,4096]{1,0:T(8,128)(2,1)S(1)}) custom-call(s32[1]{0:T(128)} %bitcast.1.core_ref, f32[512,256]{1,0:T(8,128)S(1)} %copy-done.2, f32[256,4096]{1,0:T(8,128)} %columns_hbm.1), custom_call_target="tpu_custom_call" | custom-call | flops 1610612736 | bytes 8388608 | tf_op jit(solution)/shard_map/pallas_call | solution.py:94
  10.7 0.6 collective-permute-start.6
  11.2 0.4 constant_dynamic-slice_fusion.1
  11.7 1.8 %shard_map.74 = (f32[128,4096]{1,0:T(8,128)S(1)}, f32[128,4096]{1,0:T(8,128)S(1)}) custom-call(s32[1]{0:T(128)} %bitcast.2.core_ref, f32[512,256]{1,0:T(8,128)S(1)} %copy-done.2, bf16[256,4096]{1,0:T(8,128)(2,1)S(1)} %get-tuple-element.50.high_ref, bf16[256,4096]{1,0:T(8,128)(2,1)S(1)} %get-tuple-element.51.low_ref), custom_call_target="tpu_custom_call" | custom-call | flops 1610612736 | bytes 8388608 | tf_op jit(solution)/shard_map/pallas_call | solution.py:94
  13.5 0.2 constant_dynamic-slice_fusion.3
  13.8 0.3 multiply_add_fusion.1
  14.3 0.2 multiply_convert_fusion.7
  14.7 2.1 %collective-permute-start.4 = (f16[32,4096]{1,0:T(8,128)(2,1)S(1)}, f16[32,4096]{1,0:T(8,128)(2,1)S(1)}, u32[]{:S(2)}, u32[]{:S(2)}) collective-permute-start(f16[32,4096]{1,0:T(8,128)(2,1)S(1)} %multiply_convert_fusion.6), channel_id=1, source_target_pairs={{0,4},{1,5},{2,6},{3,7},{4,0},{5,1},{6,2},{7,3},{8,12},{9,13},{10,... | collective-permute-start | bytes 786440 | tf_op jit(solution)/shard_map/ppermute | solution.py:178
  16.8 0.3 multiply_add_fusion
  17.3 0.2 multiply_convert_fusion.5
  17.5 5.7 %collective-permute-done.2 = f16[64,2048]{1,0:T(8,128)(2,1)S(1)} collective-permute-done((f16[64,2048]{1,0:T(8,128)(2,1)S(1)}, f16[64,2048]{1,0:T(8,128)(2,1)S(1)}, u32[]{:S(2)}, u32[]{:S(2)}) %collective-permute-start.2) | collective-permute-done | bytes 262176 | tf_op jit(solution)/shard_map/ppermute | solution.py:178
  23.5 1.6 %collective-permute-start.3 = (f16[32,2048]{1,0:T(8,128)(2,1)S(1)}, f16[32,2048]{1,0:T(8,128)(2,1)S(1)}, u32[]{:S(2)}, u32[]{:S(2)}) collective-permute-start(f16[32,2048]{1,0:T(8,128)(2,1)S(1)} %multiply_convert_fusion.11), channel_id=1, source_target_pairs={{0,4},{1,5},{2,6},{3,7},{4,0},{5,1},{6,2},{7,3},{8,12},{9,13},{10,... | collective-permute-start | bytes 393224 | tf_op jit(solution)/shard_map/ppermute | solution.py:178
  25.4 1.0 %collective-permute-start.5 = (f16[32,2048]{1,0:T(8,128)(2,1)S(1)}, f16[32,2048]{1,0:T(8,128)(2,1)S(1)}, u32[]{:S(2)}, u32[]{:S(2)}) collective-permute-start(f16[32,2048]{1,0:T(8,128)(2,1)S(1)} %multiply_convert_fusion.10), channel_id=1, source_target_pairs={{0,2},{1,3},{2,0},{3,1},{4,6},{5,7},{6,4},{7,5},{8,10},{9,11},{10,... | collective-permute-start | bytes 393224 | tf_op jit(solution)/shard_map/ppermute | solution.py:178
  26.4 1.1 %collective-permute-start.7 = (f16[64,2048]{1,0:T(8,128)(2,1)S(1)}, f16[64,2048]{1,0:T(8,128)(2,1)S(1)}, u32[]{:S(2)}, u32[]{:S(2)}) collective-permute-start(f16[64,2048]{1,0:T(8,128)(2,1)S(1)} %multiply_convert_fusion.5), channel_id=1, source_target_pairs={{0,2},{1,3},{2,0},{3,1},{4,6},{5,7},{6,4},{7,5},{8,10},{9,11},{10,... | collective-permute-start | bytes 786440 | tf_op jit(solution)/shard_map/ppermute | solution.py:178
  27.5 0.5 collective-permute-start.9
  28.0 0.7 collective-permute-done.3
  28.7 3.2 %collective-permute-done.5 = f16[32,2048]{1,0:T(8,128)(2,1)S(1)} collective-permute-done((f16[32,2048]{1,0:T(8,128)(2,1)S(1)}, f16[32,2048]{1,0:T(8,128)(2,1)S(1)}, u32[]{:S(2)}, u32[]{:S(2)}) %collective-permute-start.5) | collective-permute-done | bytes 131104 | tf_op jit(solution)/shard_map/ppermute | solution.py:178
  32.1 2.6 %collective-permute-start.11 = (f16[2,32,2048]{2,1,0:T(8,128)(2,1)S(1)}, f16[2,32,2048]{2,1,0:T(8,128)(2,1)S(1)}, u32[]{:S(2)}, u32[]{:S(2)}) collective-permute-start(f16[2,32,2048]{2,1,0:T(8,128)(2,1)S(1)} %get-tuple-element.84), channel_id=1, source_target_pairs={{0,8},{1,9},{2,10},{3,11},{4,12},{5,13},{6,14},{7,15},{8,0},{9,1},... | collective-permute-start | bytes 786440 | tf_op jit(solution)/shard_map/ppermute | solution.py:178
  34.8 1.1 %collective-permute-done.7 = f16[64,2048]{1,0:T(8,128)(2,1)S(1)} collective-permute-done((f16[64,2048]{1,0:T(8,128)(2,1)S(1)}, f16[64,2048]{1,0:T(8,128)(2,1)S(1)}, u32[]{:S(2)}, u32[]{:S(2)}) %collective-permute-start.7) | collective-permute-done | bytes 262176 | tf_op jit(solution)/shard_map/ppermute | solution.py:178
  35.9 0.2 multiply_add_fusion.3
  36.2 0.5 collective-permute-start.8
  36.7 2.0 %collective-permute-done.9 = f16[32,4096]{1,0:T(8,128)(2,1)S(1)} collective-permute-done((f16[32,4096]{1,0:T(8,128)(2,1)S(1)}, f16[32,4096]{1,0:T(8,128)(2,1)S(1)}, u32[]{:S(2)}, u32[]{:S(2)}) %collective-permute-start.9) | collective-permute-done | bytes 262176 | tf_op jit(solution)/shard_map/ppermute | solution.py:178
  39.0 1.2 %collective-permute-start.10 = (f16[32,2048]{1,0:T(8,128)(2,1)S(1)}, f16[32,2048]{1,0:T(8,128)(2,1)S(1)}, u32[]{:S(2)}, u32[]{:S(2)}) collective-permute-start(f16[32,2048]{1,0:T(8,128)(2,1)S(1)} %multiply_convert_fusion.8), channel_id=1, source_target_pairs={{0,2},{1,3},{2,0},{3,1},{4,6},{5,7},{6,4},{7,5},{8,10},{9,11},{10,... | collective-permute-start | bytes 393224 | tf_op jit(solution)/shard_map/ppermute | solution.py:178
  40.2 2.3 %collective-permute-done.8 = f16[32,2048]{1,0:T(8,128)(2,1)S(1)} collective-permute-done((f16[32,2048]{1,0:T(8,128)(2,1)S(1)}, f16[32,2048]{1,0:T(8,128)(2,1)S(1)}, u32[]{:S(2)}, u32[]{:S(2)}) %collective-permute-start.8) | collective-permute-done | bytes 131104 | tf_op jit(solution)/shard_map/ppermute | solution.py:178
  42.5 1.5 %collective-permute-done.10 = f16[32,2048]{1,0:T(8,128)(2,1)S(1)} collective-permute-done((f16[32,2048]{1,0:T(8,128)(2,1)S(1)}, f16[32,2048]{1,0:T(8,128)(2,1)S(1)}, u32[]{:S(2)}, u32[]{:S(2)}) %collective-permute-start.10) | collective-permute-done | bytes 131104 | tf_op jit(solution)/shard_map/ppermute | solution.py:178
  44.2 1.7 %collective-permute-start.17 = (f16[2,32,2048]{2,1,0:T(8,128)(2,1)S(1)}, f16[2,32,2048]{2,1,0:T(8,128)(2,1)S(1)}, u32[]{:S(2)}, u32[]{:S(2)}) collective-permute-start(f16[2,32,2048]{2,1,0:T(8,128)(2,1)S(1)} %multiply_convert_fusion.3), channel_id=1, source_target_pairs={{0,8},{1,9},{2,10},{3,11},{4,12},{5,13},{6,14},{7,15},{8,0},{9,1},... | collective-permute-start | bytes 786440 | tf_op jit(solution)/shard_map/ppermute | solution.py:178
  46.0 1.1 %collective-permute-start.12 = (bf16[2,32,2048]{2,1,0:T(8,128)(2,1)S(1)}, bf16[2,32,2048]{2,1,0:T(8,128)(2,1)S(1)}, u32[]{:S(2)}, u32[]{:S(2)}) collective-permute-start(bf16[2,32,2048]{2,1,0:T(8,128)(2,1)S(1)} %add_convert_fusion.1), channel_id=1, source_target_pairs={{0,4},{1,5},{2,6},{3,7},{4,0},{5,1},{6,2},{7,3},{8,12},{9,13},{10,... | collective-permute-start | bytes 786440 | tf_op jit(solution)/shard_map/ppermute | solution.py:178
  47.1 0.8 collective-permute-start.14
  47.9 8.2 %collective-permute-done.17 = f16[2,32,2048]{2,1,0:T(8,128)(2,1)S(1)} collective-permute-done((f16[2,32,2048]{2,1,0:T(8,128)(2,1)S(1)}, f16[2,32,2048]{2,1,0:T(8,128)(2,1)S(1)}, u32[]{:S(2)}, u32[]{:S(2)}) %collective-permute-start.17) | collective-permute-done | bytes 262176 | tf_op jit(solution)/shard_map/ppermute | solution.py:178
  56.2 0.7 collective-permute-done.12
  57.1 0.6 collective-permute-done.14
  57.6 0.7 fusion.1.refs_0_
  58.5 1.1 %collective-permute-done.16 = bf16[128,2048]{1,0:T(8,128)(2,1)S(1)} collective-permute-done((bf16[128,2048]{1,0:T(8,128)(2,1)S(1)}, bf16[128,2048]{1,0:T(8,128)(2,1)S(1)}, u32[]{:S(2)}, u32[]{:S(2)}) %collective-permute-start.16) | collective-permute-done | bytes 524320 | tf_op jit(solution)/shard_map/ppermute | solution.py:178
  59.6 0.7 fusion.11.refs_1_
  60.3 2.9 %collective-permute-done.18 = bf16[2,32,2048]{2,1,0:T(8,128)(2,1)S(1)} collective-permute-done((bf16[2,32,2048]{2,1,0:T(8,128)(2,1)S(1)}, bf16[2,32,2048]{2,1,0:T(8,128)(2,1)S(1)}, u32[]{:S(2)}, u32[]{:S(2)}) %collective-permute-start.18) | collective-permute-done | bytes 262176 | tf_op jit(solution)/shard_map/ppermute | solution.py:178
  63.3 0.7 fusion.12.refs_3_
  64.0 0.7 fusion.refs_2_
  64.8 1.9 %shard_map.75 = bf16[16,64,256]{2,1,0:T(8,128)(2,1)} custom-call(s32[16]{0:T(128)S(1)} %copy-done.1, f32[512,128]{1,0:T(8,128)S(1)} %fusion.1.refs_0_, f32[512,128]{1,0:T(8,128)S(1)} %fusion.11.refs_1_, f32[512,128]{1,0:T(8,128)S(1)} %fusion.refs_2_, f32[512,128]{1,0:T(8,128)S(1)} %fusion.12.refs_3_), custom_call_target="tpu_custom_call" | custom-call | flops 65536 | bytes 1572864 | tf_op jit(solution)/shard_map/pallas_call | solution.py:127
  66.7 3.8 %all-to-all-start = ((bf16[16,1,64,256]{3,2,1,0:T(8,128)(2,1)}), bf16[16,1,64,256]{3,2,1,0:T(8,128)(2,1)S(1)}, u32[]{:S(2)}, u32[]{:S(2)}) async-start(bf16[16,1,64,256]{3,2,1,0:T(8,128)(2,1)} %bitcast.10), calls=%async_computation | async-start | bytes 1048576 | tf_op jit(solution)/shard_map/all_to_all | solution.py:294
  70.6 0.6 dynamic_slice.79
  71.3 0.3 fusion.2
  71.6 0.6 constant_dynamic-slice_fusion.allowed_ref
  72.2 12.7 %all-to-all-done = bf16[16,1,64,256]{3,2,1,0:T(8,128)(2,1)S(1)} async-done(((bf16[16,1,64,256]{3,2,1,0:T(8,128)(2,1)}), bf16[16,1,64,256]{3,2,1,0:T(8,128)(2,1)S(1)}, u32[]{:S(2)}, u32[]{:S(2)}) %all-to-all-start) | async-done | bytes 524320 | tf_op jit(solution)/shard_map/all_to_all | solution.py:294
  84.9 0.9 %shard_map.76 = f32[1024,128]{1,0:T(8,128)} custom-call(bf16[16,1,4,16,256]{4,3,2,1,0:T(8,128)(2,1)S(1)} %bitcast.28, f32[1,512]{1,0:T(1,128)S(1)} %constant_dynamic-slice_fusion.allowed_ref), custom_call_target="tpu_custom_call" | custom-call | flops 262144 | bytes 1048576 | tf_op jit(solution)/shard_map/pallas_call | solution.py:156
  (53 shorter events, 3.2 us)
Async XLA Ops:
  0.0 1.6 %copy-start = (bf16[16,16,4096]{2,1,0:T(8,128)(2,1)S(1)}, bf16[16,16,4096]{2,1,0:T(8,128)(2,1)}, u32[]{:S(2)}) copy-start(bf16[16,16,4096]{2,1,0:T(8,128)(2,1)} %param.9) | copy-start | bytes 6291460
  1.8 45.3 %collective-permute-start.13 = (bf16[128,2048]{1,0:T(8,128)(2,1)S(1)}, bf16[128,2048]{1,0:T(8,128)(2,1)S(1)}, u32[]{:S(2)}, u32[]{:S(2)}) collective-permute-start(bf16[128,2048]{1,0:T(8,128)(2,1)S(1)} %constant_dynamic-slice_fusion.2), channel_id=1, source_target_pairs={{0,2},{1,3},{2,0},{3,1},{4,6},{5,7},{6,4},{7,5},{8,10},{9,11},{10,... | collective-permute-start | bytes 1572872 | tf_op jit(solution)/shard_map/ppermute | solution.py:178
  4.8 1.0 %copy-start.2 = (f32[512,256]{1,0:T(8,128)S(1)}, f32[512,256]{1,0:T(8,128)}, u32[]{:S(2)}) copy-start(f32[512,256]{1,0:T(8,128)} %rows_ref) | copy-start | bytes 1572868
  10.4 3.4 %collective-permute-start.1 = (f16[128,4096]{1,0:T(8,128)(2,1)S(1)}, f16[128,4096]{1,0:T(8,128)(2,1)S(1)}, u32[]{:S(2)}, u32[]{:S(2)}) collective-permute-start(f16[128,4096]{1,0:T(8,128)(2,1)S(1)} %multiply_convert_fusion.1), channel_id=1, source_target_pairs={{0,1},{1,0},{2,3},{3,2},{4,5},{5,4},{6,7},{7,6},{8,9},{9,8},{10,11... | collective-permute-start | bytes 3145736 | tf_op jit(solution)/shard_map/ppermute | solution.py:178
  10.7 6.1 %collective-permute-start.6 = (f16[128,4096]{1,0:T(8,128)(2,1)S(1)}, f16[128,4096]{1,0:T(8,128)(2,1)S(1)}, u32[]{:S(2)}, u32[]{:S(2)}) collective-permute-start(f16[128,4096]{1,0:T(8,128)(2,1)S(1)} %multiply_convert_fusion), channel_id=1, source_target_pairs={{0,1},{1,0},{2,3},{3,2},{4,5},{5,4},{6,7},{7,6},{8,9},{9,8},{10,11... | collective-permute-start | bytes 3145736 | tf_op jit(solution)/shard_map/ppermute | solution.py:178
  11.6 14.7 %collective-permute-start = (bf16[256,2048]{1,0:T(8,128)(2,1)S(1)}, bf16[256,2048]{1,0:T(8,128)(2,1)S(1)}, u32[]{:S(2)}, u32[]{:S(2)}) collective-permute-start(bf16[256,2048]{1,0:T(8,128)(2,1)S(1)} %constant_dynamic-slice_fusion.1), channel_id=1, source_target_pairs={{0,1},{1,0},{2,3},{3,2},{4,5},{5,4},{6,7},{7,6},{8,9},{9,8},{10,11... | collective-permute-start | bytes 3145736 | tf_op jit(solution)/shard_map/ppermute | solution.py:178
  14.5 8.7 %collective-permute-start.2 = (f16[64,2048]{1,0:T(8,128)(2,1)S(1)}, f16[64,2048]{1,0:T(8,128)(2,1)S(1)}, u32[]{:S(2)}, u32[]{:S(2)}) collective-permute-start(f16[64,2048]{1,0:T(8,128)(2,1)S(1)} %multiply_convert_fusion.7), channel_id=1, source_target_pairs={{0,2},{1,3},{2,0},{3,1},{4,6},{5,7},{6,4},{7,5},{8,10},{9,11},{10,... | collective-permute-start | bytes 786440 | tf_op jit(solution)/shard_map/ppermute | solution.py:178
  14.7 10.5 %collective-permute-start.4 = (f16[32,4096]{1,0:T(8,128)(2,1)S(1)}, f16[32,4096]{1,0:T(8,128)(2,1)S(1)}, u32[]{:S(2)}, u32[]{:S(2)}) collective-permute-start(f16[32,4096]{1,0:T(8,128)(2,1)S(1)} %multiply_convert_fusion.6), channel_id=1, source_target_pairs={{0,4},{1,5},{2,6},{3,7},{4,0},{5,1},{6,2},{7,3},{8,12},{9,13},{10,... | collective-permute-start | bytes 786440 | tf_op jit(solution)/shard_map/ppermute | solution.py:178
  23.5 5.2 %collective-permute-start.3 = (f16[32,2048]{1,0:T(8,128)(2,1)S(1)}, f16[32,2048]{1,0:T(8,128)(2,1)S(1)}, u32[]{:S(2)}, u32[]{:S(2)}) collective-permute-start(f16[32,2048]{1,0:T(8,128)(2,1)S(1)} %multiply_convert_fusion.11), channel_id=1, source_target_pairs={{0,4},{1,5},{2,6},{3,7},{4,0},{5,1},{6,2},{7,3},{8,12},{9,13},{10,... | collective-permute-start | bytes 393224 | tf_op jit(solution)/shard_map/ppermute | solution.py:178
  25.4 6.5 %collective-permute-start.5 = (f16[32,2048]{1,0:T(8,128)(2,1)S(1)}, f16[32,2048]{1,0:T(8,128)(2,1)S(1)}, u32[]{:S(2)}, u32[]{:S(2)}) collective-permute-start(f16[32,2048]{1,0:T(8,128)(2,1)S(1)} %multiply_convert_fusion.10), channel_id=1, source_target_pairs={{0,2},{1,3},{2,0},{3,1},{4,6},{5,7},{6,4},{7,5},{8,10},{9,11},{10,... | collective-permute-start | bytes 393224 | tf_op jit(solution)/shard_map/ppermute | solution.py:178
  26.4 9.5 %collective-permute-start.7 = (f16[64,2048]{1,0:T(8,128)(2,1)S(1)}, f16[64,2048]{1,0:T(8,128)(2,1)S(1)}, u32[]{:S(2)}, u32[]{:S(2)}) collective-permute-start(f16[64,2048]{1,0:T(8,128)(2,1)S(1)} %multiply_convert_fusion.5), channel_id=1, source_target_pairs={{0,2},{1,3},{2,0},{3,1},{4,6},{5,7},{6,4},{7,5},{8,10},{9,11},{10,... | collective-permute-start | bytes 786440 | tf_op jit(solution)/shard_map/ppermute | solution.py:178
  27.5 11.2 %collective-permute-start.9 = (f16[32,4096]{1,0:T(8,128)(2,1)S(1)}, f16[32,4096]{1,0:T(8,128)(2,1)S(1)}, u32[]{:S(2)}, u32[]{:S(2)}) collective-permute-start(f16[32,4096]{1,0:T(8,128)(2,1)S(1)} %multiply_convert_fusion.4), channel_id=1, source_target_pairs={{0,4},{1,5},{2,6},{3,7},{4,0},{5,1},{6,2},{7,3},{8,12},{9,13},{10,... | collective-permute-start | bytes 786440 | tf_op jit(solution)/shard_map/ppermute | solution.py:178
  32.1 13.8 %collective-permute-start.11 = (f16[2,32,2048]{2,1,0:T(8,128)(2,1)S(1)}, f16[2,32,2048]{2,1,0:T(8,128)(2,1)S(1)}, u32[]{:S(2)}, u32[]{:S(2)}) collective-permute-start(f16[2,32,2048]{2,1,0:T(8,128)(2,1)S(1)} %get-tuple-element.84), channel_id=1, source_target_pairs={{0,8},{1,9},{2,10},{3,11},{4,12},{5,13},{6,14},{7,15},{8,0},{9,1},... | collective-permute-start | bytes 786440 | tf_op jit(solution)/shard_map/ppermute | solution.py:178
  36.2 6.3 %collective-permute-start.8 = (f16[32,2048]{1,0:T(8,128)(2,1)S(1)}, f16[32,2048]{1,0:T(8,128)(2,1)S(1)}, u32[]{:S(2)}, u32[]{:S(2)}) collective-permute-start(f16[32,2048]{1,0:T(8,128)(2,1)S(1)} %multiply_convert_fusion.9), channel_id=1, source_target_pairs={{0,4},{1,5},{2,6},{3,7},{4,0},{5,1},{6,2},{7,3},{8,12},{9,13},{10,... | collective-permute-start | bytes 393224 | tf_op jit(solution)/shard_map/ppermute | solution.py:178
  39.0 5.0 %collective-permute-start.10 = (f16[32,2048]{1,0:T(8,128)(2,1)S(1)}, f16[32,2048]{1,0:T(8,128)(2,1)S(1)}, u32[]{:S(2)}, u32[]{:S(2)}) collective-permute-start(f16[32,2048]{1,0:T(8,128)(2,1)S(1)} %multiply_convert_fusion.8), channel_id=1, source_target_pairs={{0,2},{1,3},{2,0},{3,1},{4,6},{5,7},{6,4},{7,5},{8,10},{9,11},{10,... | collective-permute-start | bytes 393224 | tf_op jit(solution)/shard_map/ppermute | solution.py:178
  44.2 11.9 %collective-permute-start.17 = (f16[2,32,2048]{2,1,0:T(8,128)(2,1)S(1)}, f16[2,32,2048]{2,1,0:T(8,128)(2,1)S(1)}, u32[]{:S(2)}, u32[]{:S(2)}) collective-permute-start(f16[2,32,2048]{2,1,0:T(8,128)(2,1)S(1)} %multiply_convert_fusion.3), channel_id=1, source_target_pairs={{0,8},{1,9},{2,10},{3,11},{4,12},{5,13},{6,14},{7,15},{8,0},{9,1},... | collective-permute-start | bytes 786440 | tf_op jit(solution)/shard_map/ppermute | solution.py:178
  46.0 10.9 %collective-permute-start.12 = (bf16[2,32,2048]{2,1,0:T(8,128)(2,1)S(1)}, bf16[2,32,2048]{2,1,0:T(8,128)(2,1)S(1)}, u32[]{:S(2)}, u32[]{:S(2)}) collective-permute-start(bf16[2,32,2048]{2,1,0:T(8,128)(2,1)S(1)} %add_convert_fusion.1), channel_id=1, source_target_pairs={{0,4},{1,5},{2,6},{3,7},{4,0},{5,1},{6,2},{7,3},{8,12},{9,13},{10,... | collective-permute-start | bytes 786440 | tf_op jit(solution)/shard_map/ppermute | solution.py:178
  47.1 10.5 %collective-permute-start.14 = (bf16[128,2048]{1,0:T(8,128)(2,1)S(1)}, bf16[128,2048]{1,0:T(8,128)(2,1)S(1)}, u32[]{:S(2)}, u32[]{:S(2)}) collective-permute-start(bf16[128,2048]{1,0:T(8,128)(2,1)S(1)} %constant_dynamic-slice_fusion.3), channel_id=1, source_target_pairs={{0,2},{1,3},{2,0},{3,1},{4,6},{5,7},{6,4},{7,5},{8,10},{9,11},{10,... | collective-permute-start | bytes 1572872 | tf_op jit(solution)/shard_map/ppermute | solution.py:178
  47.9 10.6 %collective-permute-start.15 = (bf16[128,2048]{1,0:T(8,128)(2,1)S(1)}, bf16[128,2048]{1,0:T(8,128)(2,1)S(1)}, u32[]{:S(2)}, u32[]{:S(2)}) collective-permute-start(bf16[128,2048]{1,0:T(8,128)(2,1)S(1)} %collective-permute-done.13), channel_id=1, source_target_pairs={{0,1},{1,0},{2,3},{3,2},{4,5},{5,4},{6,7},{7,6},{8,9},{9,8},{10,11... | collective-permute-start | bytes 1572872 | tf_op jit(solution)/shard_map/ppermute | solution.py:178
  56.1 7.1 %collective-permute-start.18 = (bf16[2,32,2048]{2,1,0:T(8,128)(2,1)S(1)}, bf16[2,32,2048]{2,1,0:T(8,128)(2,1)S(1)}, u32[]{:S(2)}, u32[]{:S(2)}) collective-permute-start(bf16[2,32,2048]{2,1,0:T(8,128)(2,1)S(1)} %add_convert_fusion), channel_id=1, source_target_pairs={{0,4},{1,5},{2,6},{3,7},{4,0},{5,1},{6,2},{7,3},{8,12},{9,13},{10,... | collective-permute-start | bytes 786440 | tf_op jit(solution)/shard_map/ppermute | solution.py:178
  57.6 1.9 %collective-permute-start.16 = (bf16[128,2048]{1,0:T(8,128)(2,1)S(1)}, bf16[128,2048]{1,0:T(8,128)(2,1)S(1)}, u32[]{:S(2)}, u32[]{:S(2)}) collective-permute-start(bf16[128,2048]{1,0:T(8,128)(2,1)S(1)} %collective-permute-done.14), channel_id=1, source_target_pairs={{0,1},{1,0},{2,3},{3,2},{4,5},{5,4},{6,7},{7,6},{8,9},{9,8},{10,11... | collective-permute-start | bytes 1572872 | tf_op jit(solution)/shard_map/ppermute | solution.py:178
  64.0 0.8 copy-start.1
  64.8 5.7 %copy-start.3 = (s32[8,12]{1,0:T(8,128)S(1)}, s32[8,12]{1,0:T(8,128)}, u32[]{:S(2)}) copy-start(s32[8,12]{1,0:T(8,128)} %param.11) | copy-start | bytes 1156
  64.8 6.4 %copy-start.4 = (s32[8]{0:T(128)S(1)}, s32[8]{0:T(128)}, u32[]{:S(2)}) copy-start(s32[8]{0:T(128)} %param.12) | copy-start | bytes 100
  64.8 6.5 %copy-start.5 = (s32[512]{0:T(512)S(1)}, s32[512]{0:T(512)}, u32[]{:S(2)}) copy-start(s32[512]{0:T(512)} %param.10) | copy-start | bytes 6148
  66.7 18.2 %all-to-all-start = ((bf16[16,1,64,256]{3,2,1,0:T(8,128)(2,1)}), bf16[16,1,64,256]{3,2,1,0:T(8,128)(2,1)S(1)}, u32[]{:S(2)}, u32[]{:S(2)}) async-start(bf16[16,1,64,256]{3,2,1,0:T(8,128)(2,1)} %bitcast.10), calls=%async_computation | async-start | bytes 1048576 | tf_op jit(solution)/shard_map/all_to_all | solution.py:294

commit v12 on v11

--- a/solution.py
+++ b/solution.py
@@ -30,8 +30,7 @@
 
 def rows_of(core_ref, rows_ref):
     half = rows_ref.shape[0] // CORES
-    high, low = split(rows_ref[pl.ds(pl.multiple_of(core_ref[0] * half, half), half), :])
-    return jnp.concatenate([high, low, high], axis=1)
+    return rows_ref[pl.ds(pl.multiple_of(core_ref[0] * half, half), half), :]
 
 
 def multiply(left, high, low, outs, columns):
@@ -42,8 +41,8 @@
         out_ref[:, columns] = result[chunk * part:(chunk + 1) * part]
 
 
-def other_kernel(core_ref, rows_hbm, columns_hbm, *refs):
-    outs, (high_ref, low_ref, rows_ref, columns_ref, sems) = refs[:-5], refs[-5:]
+def other_kernel(core_ref, rows_ref, columns_hbm, *refs):
+    outs, (high_ref, low_ref, columns_ref, sems) = refs[:-4], refs[-4:]
     steps, _, block = columns_ref.shape
 
     def load(i):
@@ -51,11 +50,8 @@
             columns_hbm.at[:, i * block:(i + 1) * block], columns_ref.at[i], sems.at[i]
         )
 
-    load_rows = pltpu.make_async_copy(rows_hbm, rows_ref, sems.at[steps])
-    load_rows.start()
     for i in range(steps):
         load(i).start()
-    load_rows.wait()
     left = rows_of(core_ref, rows_ref)
     for i in range(steps):
         load(i).wait()
@@ -76,8 +72,8 @@
 
 
 def product(core, rows, columns, kernel, vmem):
-    nrows, depth = rows.shape
-    width = columns[0].shape[1]
+    nrows = rows.shape[0]
+    depth, width = columns[0].shape
     block = min(512, width)
     part = nrows // CORES // CHUNKS
     out = [jax.ShapeDtypeStruct((part, width), jnp.float32)] * CHUNKS
@@ -87,13 +83,12 @@
         out = out + [jax.ShapeDtypeStruct((depth, width), jnp.bfloat16)] * 2
         operand = pl.BlockSpec(memory_space=pltpu.HBM)
         scratch = [
-            pltpu.VMEM((nrows, depth), jnp.float32),
             pltpu.VMEM((width // block, depth, block), jnp.float32),
-            pltpu.SemaphoreType.DMA((1 + width // block,)),
+            pltpu.SemaphoreType.DMA((width // block,)),
         ]
     return pl.pallas_call(
         kernel,
-        in_specs=[pl.BlockSpec(memory_space=pltpu.SMEM)] + [operand] * (1 + len(columns)),
+        in_specs=[pl.BlockSpec(memory_space=pltpu.SMEM), in_vmem] + [operand] * len(columns),
         out_specs=[in_vmem] * len(out),
         out_shape=out,
         scratch_shapes=scratch,
@@ -110,11 +105,12 @@
     raws, out_ref = refs[:-1], refs[-1]
     nblocks = slots_ref.shape[0]
     groups = len(raws) // CHUNKS
-    for slot in range(nblocks):
+    first = pl.program_id(0) * out_ref.shape[0]
+    for slot in range(out_ref.shape[0]):
         for i, raw_ref in enumerate(raws):
             examples, width = raw_ref.shape[0] // nblocks, raw_ref.shape[1]
             chunk, group = divmod(i, groups)
-            rows = pl.ds(slots_ref[slot], examples, stride=nblocks)
+            rows = pl.ds(slots_ref[first + slot], examples, stride=nblocks)
             out_ref[
                 slot, group * examples:(group + 1) * examples, chunk * width:(chunk + 1) * width
             ] = raw_ref[rows, :].astype(out_ref.dtype)
@@ -124,12 +120,14 @@
     nblocks = slots.shape[0]
     rows, width = raws[0].shape
     groups = len(raws) // CHUNKS
+    shape = (nblocks, groups * rows // nblocks, CHUNKS * width)
     return pl.pallas_call(
         order_kernel,
+        grid=(4,),
         in_specs=[pl.BlockSpec(memory_space=pltpu.SMEM)] + [pl.BlockSpec(memory_space=pltpu.VMEM)] * len(raws),
-        out_specs=pl.BlockSpec(memory_space=pltpu.VMEM),
-        out_shape=jax.ShapeDtypeStruct((nblocks, groups * rows // nblocks, CHUNKS * width), jnp.bfloat16),
-        compiler_params=pltpu.CompilerParams(vmem_limit_bytes=4 * 1024 * 1024),
+        out_specs=pl.BlockSpec((nblocks // 4,) + shape[1:], lambda i: (i, 0, 0)),
+        out_shape=jax.ShapeDtypeStruct(shape, jnp.bfloat16),
+        compiler_params=pltpu.CompilerParams(vmem_limit_bytes=8 * 1024 * 1024),
         cost_estimate=pl.CostEstimate(
             flops=rows * width, bytes_accessed=6 * len(raws) * rows * width, transcendentals=0
         ),
@@ -254,27 +252,32 @@
         start = offsets[ybit, width // 2][other]
         return lax.dynamic_slice(blocks, (first, start), (count, width // 2), allow_negative_indices=False)
 
+    high = lax.reduce_precision(queries, 8, 7)
+    low = (queries - high).astype(jnp.bfloat16)
+    high = high.astype(jnp.bfloat16)
+    left = jnp.concatenate([high, low, high], axis=1)
+    blocks = after(blocks, left)
     early = features(blocks, 0, middle, 1)
     other_core, blocks = after((other_core, blocks), early)
     early = swap(early, ybit)
 
-    *full, high, low = product(other_core, queries, [precond], other_kernel, OTHER_VMEM)
+    *full, high, low = product(other_core, left, [precond], other_kernel, OTHER_VMEM)
     sent = [pack(value) for value in full]
     got = [swap(value, 0) for value in sent]
+    mine = product(after(core, sent), left, [high, low], mine_kernel, MINE_VMEM)
+    one = paths(mine[0], got[0])
+    sent = messages(one, 0)
+    two = paths(mine[1], after(got[1], sent))
     blocks = after(blocks, sent)
     near = features(blocks, 0, 2 * middle, 0)
     late = features(blocks, middle, middle, 1)
     sibling = swap(near, 0)
-    mine = product(after(core, sent), queries, [high, low], mine_kernel, MINE_VMEM)
-    one = paths(mine[0], got[0])
-    sent = messages(one, 0)
-    two = paths(mine[1], after(got[1], sent))
     one = exchange(one, sent, 0)
     sent = messages(one, 1)
-    two = exchange(two, after(messages(two, 0), (sent, sibling)), 0)
+    two = exchange(two, after(messages(two, 0), sent), 0)
     one = halve(exchange(one, sent, 1))
     got_one = swap(pack(one), rest[-1])
-    two = exchange(two, messages(two, 1), 1)
+    two = exchange(two, after(messages(two, 1), sibling), 1)
     two = halve(two)
     sent = pack(two)
     one = (after(one, sent) + unpack(got_one)).astype(jnp.bfloat16)

time: 86.1 us -> 96.2 us (1.12)
  waiting for transfers between devices: 42.7 us -> 49 us
  starting transfers between devices: 21.9 us -> 26.1 us
  local copies, waits for them, and re-layouts: 5.31 us -> 3.13 us
  other arithmetic: 3.45 us -> 4.85 us
    ppermute x19, waiting for transfers between devices: 30 us -> 36.3 us  [swap(): return lax.ppermute(value, 'rows', [(r, r ^ 1 << bit) for r in range(n)])]
    ppermute x19, starting transfers between devices: 18.2 us -> 20.6 us  [swap(): return lax.ppermute(value, 'rows', [(r, r ^ 1 << bit) for r in range(n)])]
    unnamed x15 -> x13, local copies, waits for them, and re-layouts: 2.76 us -> 0.57 us
    all_to_all x1, starting transfers between devices: 3.76 us -> 5.52 us  [shards(): lax.all_to_all(ordered, 'rows', split_axis=0, concat_axis=0, tiled=True)]
    convert_element_type x0 -> x1, other arithmetic: none -> 1.26 us  [shards(): low = (queries - high).astype(jnp.bfloat16)]
  transfers between devices with their start and end apart: 20 -> 20, of which waited for: 13 -> 14; matrix products, arithmetic and copies ran while one was open for 9% -> 8% of each run, Pallas kernels for 7% -> 6%
where the time goes in v12:
time: 96.2 us; the launch traced here: 95.9 us
  waiting for transfers between devices  49 us (51%)
  starting transfers between devices  26.1 us (27%)
  Pallas kernels  9.23 us (10%)
  other arithmetic  4.85 us (5%)
  matrix products  3.14 us (3%)
  local copies, waits for them, and re-layouts  3.13 us (3%)
    ppermute x19, waiting for transfers between devices, swap(): return lax.ppermute(value, 'rows', [(r, r ^ 1 << bit) for r in range(n)])  36.3 us
    ppermute x19, starting transfers between devices, swap(): return lax.ppermute(value, 'rows', [(r, r ^ 1 << bit) for r in range(n)])  20.6 us
    all_to_all x1, waiting for transfers between devices, shards(): lax.all_to_all(ordered, 'rows', split_axis=0, concat_axis=0, tiled=True)  12.7 us
    pallas_call x2, Pallas kernels, product(): pl.pallas_call(kernel, in_specs=[pl.BlockSpec(memory_space=pltpu.SMEM), i...  6.03 us
    all_to_all x1, starting transfers between devices, shards(): lax.all_to_all(ordered, 'rows', split_axis=0, concat_axis=0, tiled=True)  5.52 us
    dot_general x4, matrix products, scores(): lax.dot_general(group, value, (((1,), (1,)), ((), ())), preferred_element...  2.88 us
    pallas_call x1, Pallas kernels, in_slot_order(): pl.pallas_call(order_kernel, grid=(4,), in_specs=[pl.BlockSpec(memory_spa...  2.33 us
  transfers between devices with their start and end apart: 20, of which 14 were waited for; matrix products, arithmetic and copies ran while one was open for 8% of the time, Pallas kernels for 6%

profile of v12, /device:TPU:0, one launch (start us, length us, event | category | flops | bytes accessed | tf_op | source)
XLA Modules:
  0.0 95.9 jit_solution(6150593456444341358)
XLA Ops:
  0.0 1.3 %fusion.2 = (bf16[512,256]{1,0:T(8,128)(2,1)S(1)}, bf16[512,256]{1,0:T(8,128)(2,1)S(1)}) fusion(f32[512,256]{1,0:T(8,128)} %param.7), kind=kLoop, calls=%fused_computation.10 | loop fusion | flops 524288 | bytes 1048576 | tf_op jit(solution)/shard_map/convert_element_type | solution.py:256
  1.3 0.4 copy-done
  1.8 0.2 constant_dynamic-slice_fusion.2
  2.0 3.0 %collective-permute-start.13 = (bf16[128,2048]{1,0:T(8,128)(2,1)S(1)}, bf16[128,2048]{1,0:T(8,128)(2,1)S(1)}, u32[]{:S(2)}, u32[]{:S(2)}) collective-permute-start(bf16[128,2048]{1,0:T(8,128)(2,1)S(1)} %constant_dynamic-slice_fusion.2), channel_id=1, source_target_pairs={{0,2},{1,3},{2,0},{3,1},{4,6},{5,7},{6,4},{7,5},{8,10},{9,11},{10,... | collective-permute-start | bytes 1572872 | tf_op jit(solution)/shard_map/ppermute | solution.py:176
  5.0 4.2 %shard_map.73 = (f32[128,4096]{1,0:T(8,128)S(1)}, f32[128,4096]{1,0:T(8,128)S(1)}, bf16[256,4096]{1,0:T(8,128)(2,1)S(1)}, bf16[256,4096]{1,0:T(8,128)(2,1)S(1)}) custom-call(s32[1]{0:T(128)} %bitcast.1.core_ref, bf16[512,768]{1,0:T(8,128)(2,1)S(1)} %pad_maximum_fusion.3.rows_ref, f32[256,4096]{1,0:T(8,128)} %columns_hbm.1), custom_call_target="tpu_custom_call" | custom-call | flops 1610612736 | bytes 8388608 | tf_op jit(solution)/shard_map/pallas_call | solution.py:89
  9.7 0.6 collective-permute-start.6
  10.3 1.8 %shard_map.74 = (f32[128,4096]{1,0:T(8,128)S(1)}, f32[128,4096]{1,0:T(8,128)S(1)}) custom-call(s32[1]{0:T(128)} %bitcast.2.core_ref, bf16[512,768]{1,0:T(8,128)(2,1)S(1)} %pad_maximum_fusion.3.rows_ref, bf16[256,4096]{1,0:T(8,128)(2,1)S(1)} %get-tuple-element.51.high_ref, bf16[256,4096]{1,0:T(8,128)(2,1)S(1)} %get-tuple-element.52.low_ref), custom_call_target="tpu_custom_call" | custom-call | flops 1610612736 | bytes 8388608 | tf_op jit(solution)/shard_map/pallas_call | solution.py:89
  12.2 0.3 multiply_add_fusion.1
  12.7 0.2 multiply_convert_fusion.7
  13.1 2.1 %collective-permute-start.4 = (f16[32,4096]{1,0:T(8,128)(2,1)S(1)}, f16[32,4096]{1,0:T(8,128)(2,1)S(1)}, u32[]{:S(2)}, u32[]{:S(2)}) collective-permute-start(f16[32,4096]{1,0:T(8,128)(2,1)S(1)} %multiply_convert_fusion.6), channel_id=1, source_target_pairs={{0,4},{1,5},{2,6},{3,7},{4,0},{5,1},{6,2},{7,3},{8,12},{9,13},{10,... | collective-permute-start | bytes 786440 | tf_op jit(solution)/shard_map/ppermute | solution.py:176
  15.2 0.4 constant_dynamic-slice_fusion.1
  15.8 0.3 multiply_add_fusion
  16.3 0.2 multiply_convert_fusion.5
  16.5 0.2 constant_dynamic-slice_fusion.3
  16.7 5.8 %collective-permute-done.2 = f16[64,2048]{1,0:T(8,128)(2,1)S(1)} collective-permute-done((f16[64,2048]{1,0:T(8,128)(2,1)S(1)}, f16[64,2048]{1,0:T(8,128)(2,1)S(1)}, u32[]{:S(2)}, u32[]{:S(2)}) %collective-permute-start.2) | collective-permute-done | bytes 262176 | tf_op jit(solution)/shard_map/ppermute | solution.py:176
  22.5 0.2 multiply_add_fusion.5
  22.8 1.9 %collective-permute-start.3 = (f16[32,2048]{1,0:T(8,128)(2,1)S(1)}, f16[32,2048]{1,0:T(8,128)(2,1)S(1)}, u32[]{:S(2)}, u32[]{:S(2)}) collective-permute-start(f16[32,2048]{1,0:T(8,128)(2,1)S(1)} %multiply_convert_fusion.11), channel_id=1, source_target_pairs={{0,4},{1,5},{2,6},{3,7},{4,0},{5,1},{6,2},{7,3},{8,12},{9,13},{10,... | collective-permute-start | bytes 393224 | tf_op jit(solution)/shard_map/ppermute | solution.py:176
  24.9 1.6 %collective-permute-start.5 = (f16[32,2048]{1,0:T(8,128)(2,1)S(1)}, f16[32,2048]{1,0:T(8,128)(2,1)S(1)}, u32[]{:S(2)}, u32[]{:S(2)}) collective-permute-start(f16[32,2048]{1,0:T(8,128)(2,1)S(1)} %multiply_convert_fusion.10), channel_id=1, source_target_pairs={{0,2},{1,3},{2,0},{3,1},{4,6},{5,7},{6,4},{7,5},{8,10},{9,11},{10,... | collective-permute-start | bytes 393224 | tf_op jit(solution)/shard_map/ppermute | solution.py:176
  26.5 0.4 collective-permute-start.8
  27.0 1.6 %collective-permute-done.3 = f16[32,2048]{1,0:T(8,128)(2,1)S(1)} collective-permute-done((f16[32,2048]{1,0:T(8,128)(2,1)S(1)}, f16[32,2048]{1,0:T(8,128)(2,1)S(1)}, u32[]{:S(2)}, u32[]{:S(2)}) %collective-permute-start.3) | collective-permute-done | bytes 131104 | tf_op jit(solution)/shard_map/ppermute | solution.py:176
  28.6 2.4 %collective-permute-start.7 = (f16[64,2048]{1,0:T(8,128)(2,1)S(1)}, f16[64,2048]{1,0:T(8,128)(2,1)S(1)}, u32[]{:S(2)}, u32[]{:S(2)}) collective-permute-start(f16[64,2048]{1,0:T(8,128)(2,1)S(1)} %multiply_convert_fusion.5), channel_id=1, source_target_pairs={{0,2},{1,3},{2,0},{3,1},{4,6},{5,7},{6,4},{7,5},{8,10},{9,11},{10,... | collective-permute-start | bytes 786440 | tf_op jit(solution)/shard_map/ppermute | solution.py:176
  31.0 0.3 collective-permute-done.5
  31.5 2.0 %collective-permute-done.8 = f16[32,4096]{1,0:T(8,128)(2,1)S(1)} collective-permute-done((f16[32,4096]{1,0:T(8,128)(2,1)S(1)}, f16[32,4096]{1,0:T(8,128)(2,1)S(1)}, u32[]{:S(2)}, u32[]{:S(2)}) %collective-permute-start.8) | collective-permute-done | bytes 262176 | tf_op jit(solution)/shard_map/ppermute | solution.py:176
  33.7 1.9 %collective-permute-done.7 = f16[64,2048]{1,0:T(8,128)(2,1)S(1)} collective-permute-done((f16[64,2048]{1,0:T(8,128)(2,1)S(1)}, f16[64,2048]{1,0:T(8,128)(2,1)S(1)}, u32[]{:S(2)}, u32[]{:S(2)}) %collective-permute-start.7) | collective-permute-done | bytes 262176 | tf_op jit(solution)/shard_map/ppermute | solution.py:176
  35.9 1.9 %collective-permute-start.9 = (f16[32,2048]{1,0:T(8,128)(2,1)S(1)}, f16[32,2048]{1,0:T(8,128)(2,1)S(1)}, u32[]{:S(2)}, u32[]{:S(2)}) collective-permute-start(f16[32,2048]{1,0:T(8,128)(2,1)S(1)} %multiply_convert_fusion.9), channel_id=1, source_target_pairs={{0,4},{1,5},{2,6},{3,7},{4,0},{5,1},{6,2},{7,3},{8,12},{9,13},{10,... | collective-permute-start | bytes 393224 | tf_op jit(solution)/shard_map/ppermute | solution.py:176
  37.8 2.7 %collective-permute-start.11 = (f16[2,32,2048]{2,1,0:T(8,128)(2,1)S(1)}, f16[2,32,2048]{2,1,0:T(8,128)(2,1)S(1)}, u32[]{:S(2)}, u32[]{:S(2)}) collective-permute-start(f16[2,32,2048]{2,1,0:T(8,128)(2,1)S(1)} %get-tuple-element.90), channel_id=1, source_target_pairs={{0,8},{1,9},{2,10},{3,11},{4,12},{5,13},{6,14},{7,15},{8,0},{9,1},... | collective-permute-start | bytes 786440 | tf_op jit(solution)/shard_map/ppermute | solution.py:176
  40.5 1.6 %collective-permute-start.10 = (f16[32,2048]{1,0:T(8,128)(2,1)S(1)}, f16[32,2048]{1,0:T(8,128)(2,1)S(1)}, u32[]{:S(2)}, u32[]{:S(2)}) collective-permute-start(f16[32,2048]{1,0:T(8,128)(2,1)S(1)} %multiply_convert_fusion.8), channel_id=1, source_target_pairs={{0,2},{1,3},{2,0},{3,1},{4,6},{5,7},{6,4},{7,5},{8,10},{9,11},{10,... | collective-permute-start | bytes 393224 | tf_op jit(solution)/shard_map/ppermute | solution.py:176
  42.1 3.3 %collective-permute-done.10 = f16[32,2048]{1,0:T(8,128)(2,1)S(1)} collective-permute-done((f16[32,2048]{1,0:T(8,128)(2,1)S(1)}, f16[32,2048]{1,0:T(8,128)(2,1)S(1)}, u32[]{:S(2)}, u32[]{:S(2)}) %collective-permute-start.10) | collective-permute-done | bytes 131104 | tf_op jit(solution)/shard_map/ppermute | solution.py:176
  45.7 0.4 collective-permute-start.17
  46.1 10.4 %collective-permute-done.11 = f16[2,32,2048]{2,1,0:T(8,128)(2,1)S(1)} collective-permute-done((f16[2,32,2048]{2,1,0:T(8,128)(2,1)S(1)}, f16[2,32,2048]{2,1,0:T(8,128)(2,1)S(1)}, u32[]{:S(2)}, u32[]{:S(2)}) %collective-permute-start.11) | collective-permute-done | bytes 262176 | tf_op jit(solution)/shard_map/ppermute | solution.py:176
  56.6 1.2 %collective-permute-start.14 = (bf16[128,2048]{1,0:T(8,128)(2,1)S(1)}, bf16[128,2048]{1,0:T(8,128)(2,1)S(1)}, u32[]{:S(2)}, u32[]{:S(2)}) collective-permute-start(bf16[128,2048]{1,0:T(8,128)(2,1)S(1)} %constant_dynamic-slice_fusion.3), channel_id=1, source_target_pairs={{0,2},{1,3},{2,0},{3,1},{4,6},{5,7},{6,4},{7,5},{8,10},{9,11},{10,... | collective-permute-start | bytes 1572872 | tf_op jit(solution)/shard_map/ppermute | solution.py:176
  57.8 2.1 %collective-permute-done.17 = f16[2,32,2048]{2,1,0:T(8,128)(2,1)S(1)} collective-permute-done((f16[2,32,2048]{2,1,0:T(8,128)(2,1)S(1)}, f16[2,32,2048]{2,1,0:T(8,128)(2,1)S(1)}, u32[]{:S(2)}, u32[]{:S(2)}) %collective-permute-start.17) | collective-permute-done | bytes 262176 | tf_op jit(solution)/shard_map/ppermute | solution.py:176
  60.0 0.5 collective-permute-start.18
  60.5 5.2 %collective-permute-done.12 = bf16[2,32,2048]{2,1,0:T(8,128)(2,1)S(1)} collective-permute-done((bf16[2,32,2048]{2,1,0:T(8,128)(2,1)S(1)}, bf16[2,32,2048]{2,1,0:T(8,128)(2,1)S(1)}, u32[]{:S(2)}, u32[]{:S(2)}) %collective-permute-start.12) | collective-permute-done | bytes 262176 | tf_op jit(solution)/shard_map/ppermute | solution.py:176
  65.9 1.6 %collective-permute-done.14 = bf16[128,2048]{1,0:T(8,128)(2,1)S(1)} collective-permute-done((bf16[128,2048]{1,0:T(8,128)(2,1)S(1)}, bf16[128,2048]{1,0:T(8,128)(2,1)S(1)}, u32[]{:S(2)}, u32[]{:S(2)}) %collective-permute-start.14) | collective-permute-done | bytes 524320 | tf_op jit(solution)/shard_map/ppermute | solution.py:176
  67.4 0.7 fusion.1.refs_0_
  68.3 1.1 %collective-permute-done.16 = bf16[128,2048]{1,0:T(8,128)(2,1)S(1)} collective-permute-done((bf16[128,2048]{1,0:T(8,128)(2,1)S(1)}, bf16[128,2048]{1,0:T(8,128)(2,1)S(1)}, u32[]{:S(2)}, u32[]{:S(2)}) %collective-permute-start.16) | collective-permute-done | bytes 524320 | tf_op jit(solution)/shard_map/ppermute | solution.py:176
  69.4 0.7 fusion.12.refs_1_
  70.1 1.0 %collective-permute-done.18 = bf16[2,32,2048]{2,1,0:T(8,128)(2,1)S(1)} collective-permute-done((bf16[2,32,2048]{2,1,0:T(8,128)(2,1)S(1)}, bf16[2,32,2048]{2,1,0:T(8,128)(2,1)S(1)}, u32[]{:S(2)}, u32[]{:S(2)}) %collective-permute-start.18) | collective-permute-done | bytes 262176 | tf_op jit(solution)/shard_map/ppermute | solution.py:176
  71.2 0.7 fusion.13.refs_3_
  71.9 0.7 fusion.refs_2_
  72.7 2.3 %shard_map.75 = bf16[16,64,256]{2,1,0:T(8,128)(2,1)} custom-call(s32[16]{0:T(128)S(1)} %copy-done.1, f32[512,128]{1,0:T(8,128)S(1)} %fusion.1.refs_0_, f32[512,128]{1,0:T(8,128)S(1)} %fusion.12.refs_1_, f32[512,128]{1,0:T(8,128)S(1)} %fusion.refs_2_, f32[512,128]{1,0:T(8,128)S(1)} %fusion.13.refs_3_), custom_call_target="tpu_custom_call" | custom-call | flops 65536 | bytes 1572864 | tf_op jit(solution)/shard_map/pallas_call | solution.py:124
  75.0 5.5 %all-to-all-start = ((bf16[16,1,64,256]{3,2,1,0:T(8,128)(2,1)}), bf16[16,1,64,256]{3,2,1,0:T(8,128)(2,1)S(1)}, u32[]{:S(2)}, u32[]{:S(2)}) async-start(bf16[16,1,64,256]{3,2,1,0:T(8,128)(2,1)} %bitcast.10), calls=%async_computation | async-start | bytes 1048576 | tf_op jit(solution)/shard_map/all_to_all | solution.py:297
  80.7 0.6 dynamic_slice.79
  81.4 0.3 fusion.3
  81.7 0.6 constant_dynamic-slice_fusion.allowed_ref
  82.3 12.7 %all-to-all-done = bf16[16,1,64,256]{3,2,1,0:T(8,128)(2,1)S(1)} async-done(((bf16[16,1,64,256]{3,2,1,0:T(8,128)(2,1)}), bf16[16,1,64,256]{3,2,1,0:T(8,128)(2,1)S(1)}, u32[]{:S(2)}, u32[]{:S(2)}) %all-to-all-start) | async-done | bytes 524320 | tf_op jit(solution)/shard_map/all_to_all | solution.py:297
  95.0 0.9 shard_map.76
  (53 shorter events, 3.4 us)
Async XLA Ops:
  0.0 1.7 %copy-start = (bf16[16,16,4096]{2,1,0:T(8,128)(2,1)S(1)}, bf16[16,16,4096]{2,1,0:T(8,128)(2,1)}, u32[]{:S(2)}) copy-start(bf16[16,16,4096]{2,1,0:T(8,128)(2,1)} %param.9) | copy-start | bytes 6291460
  2.0 54.6 %collective-permute-start.13 = (bf16[128,2048]{1,0:T(8,128)(2,1)S(1)}, bf16[128,2048]{1,0:T(8,128)(2,1)S(1)}, u32[]{:S(2)}, u32[]{:S(2)}) collective-permute-start(bf16[128,2048]{1,0:T(8,128)(2,1)S(1)} %constant_dynamic-slice_fusion.2), channel_id=1, source_target_pairs={{0,2},{1,3},{2,0},{3,1},{4,6},{5,7},{6,4},{7,5},{8,10},{9,11},{10,... | collective-permute-start | bytes 1572872 | tf_op jit(solution)/shard_map/ppermute | solution.py:176
  9.4 2.7 %collective-permute-start = (f16[128,4096]{1,0:T(8,128)(2,1)S(1)}, f16[128,4096]{1,0:T(8,128)(2,1)S(1)}, u32[]{:S(2)}, u32[]{:S(2)}) collective-permute-start(f16[128,4096]{1,0:T(8,128)(2,1)S(1)} %multiply_convert_fusion.1), channel_id=1, source_target_pairs={{0,1},{1,0},{2,3},{3,2},{4,5},{5,4},{6,7},{7,6},{8,9},{9,8},{10,11... | collective-permute-start | bytes 3145736 | tf_op jit(solution)/shard_map/ppermute | solution.py:176
  9.7 6.0 %collective-permute-start.6 = (f16[128,4096]{1,0:T(8,128)(2,1)S(1)}, f16[128,4096]{1,0:T(8,128)(2,1)S(1)}, u32[]{:S(2)}, u32[]{:S(2)}) collective-permute-start(f16[128,4096]{1,0:T(8,128)(2,1)S(1)} %multiply_convert_fusion), channel_id=1, source_target_pairs={{0,1},{1,0},{2,3},{3,2},{4,5},{5,4},{6,7},{7,6},{8,9},{9,8},{10,11... | collective-permute-start | bytes 3145736 | tf_op jit(solution)/shard_map/ppermute | solution.py:176
  12.9 9.6 %collective-permute-start.2 = (f16[64,2048]{1,0:T(8,128)(2,1)S(1)}, f16[64,2048]{1,0:T(8,128)(2,1)S(1)}, u32[]{:S(2)}, u32[]{:S(2)}) collective-permute-start(f16[64,2048]{1,0:T(8,128)(2,1)S(1)} %multiply_convert_fusion.7), channel_id=1, source_target_pairs={{0,2},{1,3},{2,0},{3,1},{4,6},{5,7},{6,4},{7,5},{8,10},{9,11},{10,... | collective-permute-start | bytes 786440 | tf_op jit(solution)/shard_map/ppermute | solution.py:176
  13.1 11.6 %collective-permute-start.4 = (f16[32,4096]{1,0:T(8,128)(2,1)S(1)}, f16[32,4096]{1,0:T(8,128)(2,1)S(1)}, u32[]{:S(2)}, u32[]{:S(2)}) collective-permute-start(f16[32,4096]{1,0:T(8,128)(2,1)S(1)} %multiply_convert_fusion.6), channel_id=1, source_target_pairs={{0,4},{1,5},{2,6},{3,7},{4,0},{5,1},{6,2},{7,3},{8,12},{9,13},{10,... | collective-permute-start | bytes 786440 | tf_op jit(solution)/shard_map/ppermute | solution.py:176
  15.7 20.2 %collective-permute-start.1 = (bf16[256,2048]{1,0:T(8,128)(2,1)S(1)}, bf16[256,2048]{1,0:T(8,128)(2,1)S(1)}, u32[]{:S(2)}, u32[]{:S(2)}) collective-permute-start(bf16[256,2048]{1,0:T(8,128)(2,1)S(1)} %constant_dynamic-slice_fusion.1), channel_id=1, source_target_pairs={{0,1},{1,0},{2,3},{3,2},{4,5},{5,4},{6,7},{7,6},{8,9},{9,8},{10,11... | collective-permute-start | bytes 3145736 | tf_op jit(solution)/shard_map/ppermute | solution.py:176
  22.8 5.8 %collective-permute-start.3 = (f16[32,2048]{1,0:T(8,128)(2,1)S(1)}, f16[32,2048]{1,0:T(8,128)(2,1)S(1)}, u32[]{:S(2)}, u32[]{:S(2)}) collective-permute-start(f16[32,2048]{1,0:T(8,128)(2,1)S(1)} %multiply_convert_fusion.11), channel_id=1, source_target_pairs={{0,4},{1,5},{2,6},{3,7},{4,0},{5,1},{6,2},{7,3},{8,12},{9,13},{10,... | collective-permute-start | bytes 393224 | tf_op jit(solution)/shard_map/ppermute | solution.py:176
  24.9 6.4 %collective-permute-start.5 = (f16[32,2048]{1,0:T(8,128)(2,1)S(1)}, f16[32,2048]{1,0:T(8,128)(2,1)S(1)}, u32[]{:S(2)}, u32[]{:S(2)}) collective-permute-start(f16[32,2048]{1,0:T(8,128)(2,1)S(1)} %multiply_convert_fusion.10), channel_id=1, source_target_pairs={{0,2},{1,3},{2,0},{3,1},{4,6},{5,7},{6,4},{7,5},{8,10},{9,11},{10,... | collective-permute-start | bytes 393224 | tf_op jit(solution)/shard_map/ppermute | solution.py:176
  26.5 7.0 %collective-permute-start.8 = (f16[32,4096]{1,0:T(8,128)(2,1)S(1)}, f16[32,4096]{1,0:T(8,128)(2,1)S(1)}, u32[]{:S(2)}, u32[]{:S(2)}) collective-permute-start(f16[32,4096]{1,0:T(8,128)(2,1)S(1)} %multiply_convert_fusion.4), channel_id=1, source_target_pairs={{0,4},{1,5},{2,6},{3,7},{4,0},{5,1},{6,2},{7,3},{8,12},{9,13},{10,... | collective-permute-start | bytes 786440 | tf_op jit(solution)/shard_map/ppermute | solution.py:176
  28.6 7.0 %collective-permute-start.7 = (f16[64,2048]{1,0:T(8,128)(2,1)S(1)}, f16[64,2048]{1,0:T(8,128)(2,1)S(1)}, u32[]{:S(2)}, u32[]{:S(2)}) collective-permute-start(f16[64,2048]{1,0:T(8,128)(2,1)S(1)} %multiply_convert_fusion.5), channel_id=1, source_target_pairs={{0,2},{1,3},{2,0},{3,1},{4,6},{5,7},{6,4},{7,5},{8,10},{9,11},{10,... | collective-permute-start | bytes 786440 | tf_op jit(solution)/shard_map/ppermute | solution.py:176
  35.9 6.2 %collective-permute-start.9 = (f16[32,2048]{1,0:T(8,128)(2,1)S(1)}, f16[32,2048]{1,0:T(8,128)(2,1)S(1)}, u32[]{:S(2)}, u32[]{:S(2)}) collective-permute-start(f16[32,2048]{1,0:T(8,128)(2,1)S(1)} %multiply_convert_fusion.9), channel_id=1, source_target_pairs={{0,4},{1,5},{2,6},{3,7},{4,0},{5,1},{6,2},{7,3},{8,12},{9,13},{10,... | collective-permute-start | bytes 393224 | tf_op jit(solution)/shard_map/ppermute | solution.py:176
  37.8 18.6 %collective-permute-start.11 = (f16[2,32,2048]{2,1,0:T(8,128)(2,1)S(1)}, f16[2,32,2048]{2,1,0:T(8,128)(2,1)S(1)}, u32[]{:S(2)}, u32[]{:S(2)}) collective-permute-start(f16[2,32,2048]{2,1,0:T(8,128)(2,1)S(1)} %get-tuple-element.90), channel_id=1, source_target_pairs={{0,8},{1,9},{2,10},{3,11},{4,12},{5,13},{6,14},{7,15},{8,0},{9,1},... | collective-permute-start | bytes 786440 | tf_op jit(solution)/shard_map/ppermute | solution.py:176
  40.5 5.0 %collective-permute-start.10 = (f16[32,2048]{1,0:T(8,128)(2,1)S(1)}, f16[32,2048]{1,0:T(8,128)(2,1)S(1)}, u32[]{:S(2)}, u32[]{:S(2)}) collective-permute-start(f16[32,2048]{1,0:T(8,128)(2,1)S(1)} %multiply_convert_fusion.8), channel_id=1, source_target_pairs={{0,2},{1,3},{2,0},{3,1},{4,6},{5,7},{6,4},{7,5},{8,10},{9,11},{10,... | collective-permute-start | bytes 393224 | tf_op jit(solution)/shard_map/ppermute | solution.py:176
  45.7 14.3 %collective-permute-start.17 = (f16[2,32,2048]{2,1,0:T(8,128)(2,1)S(1)}, f16[2,32,2048]{2,1,0:T(8,128)(2,1)S(1)}, u32[]{:S(2)}, u32[]{:S(2)}) collective-permute-start(f16[2,32,2048]{2,1,0:T(8,128)(2,1)S(1)} %multiply_convert_fusion.3), channel_id=1, source_target_pairs={{0,8},{1,9},{2,10},{3,11},{4,12},{5,13},{6,14},{7,15},{8,0},{9,1},... | collective-permute-start | bytes 786440 | tf_op jit(solution)/shard_map/ppermute | solution.py:176
  56.5 9.2 %collective-permute-start.12 = (bf16[2,32,2048]{2,1,0:T(8,128)(2,1)S(1)}, bf16[2,32,2048]{2,1,0:T(8,128)(2,1)S(1)}, u32[]{:S(2)}, u32[]{:S(2)}) collective-permute-start(bf16[2,32,2048]{2,1,0:T(8,128)(2,1)S(1)} %add_convert_fusion.1), channel_id=1, source_target_pairs={{0,4},{1,5},{2,6},{3,7},{4,0},{5,1},{6,2},{7,3},{8,12},{9,13},{10,... | collective-permute-start | bytes 786440 | tf_op jit(solution)/shard_map/ppermute | solution.py:176
  56.6 10.8 %collective-permute-start.14 = (bf16[128,2048]{1,0:T(8,128)(2,1)S(1)}, bf16[128,2048]{1,0:T(8,128)(2,1)S(1)}, u32[]{:S(2)}, u32[]{:S(2)}) collective-permute-start(bf16[128,2048]{1,0:T(8,128)(2,1)S(1)} %constant_dynamic-slice_fusion.3), channel_id=1, source_target_pairs={{0,2},{1,3},{2,0},{3,1},{4,6},{5,7},{6,4},{7,5},{8,10},{9,11},{10,... | collective-permute-start | bytes 1572872 | tf_op jit(solution)/shard_map/ppermute | solution.py:176
  57.8 10.4 %collective-permute-start.15 = (bf16[128,2048]{1,0:T(8,128)(2,1)S(1)}, bf16[128,2048]{1,0:T(8,128)(2,1)S(1)}, u32[]{:S(2)}, u32[]{:S(2)}) collective-permute-start(bf16[128,2048]{1,0:T(8,128)(2,1)S(1)} %collective-permute-done.13), channel_id=1, source_target_pairs={{0,1},{1,0},{2,3},{3,2},{4,5},{5,4},{6,7},{7,6},{8,9},{9,8},{10,11... | collective-permute-start | bytes 1572872 | tf_op jit(solution)/shard_map/ppermute | solution.py:176
  60.0 11.0 %collective-permute-start.18 = (bf16[2,32,2048]{2,1,0:T(8,128)(2,1)S(1)}, bf16[2,32,2048]{2,1,0:T(8,128)(2,1)S(1)}, u32[]{:S(2)}, u32[]{:S(2)}) collective-permute-start(bf16[2,32,2048]{2,1,0:T(8,128)(2,1)S(1)} %add_convert_fusion), channel_id=1, source_target_pairs={{0,4},{1,5},{2,6},{3,7},{4,0},{5,1},{6,2},{7,3},{8,12},{9,13},{10,... | collective-permute-start | bytes 786440 | tf_op jit(solution)/shard_map/ppermute | solution.py:176
  67.4 1.9 %collective-permute-start.16 = (bf16[128,2048]{1,0:T(8,128)(2,1)S(1)}, bf16[128,2048]{1,0:T(8,128)(2,1)S(1)}, u32[]{:S(2)}, u32[]{:S(2)}) collective-permute-start(bf16[128,2048]{1,0:T(8,128)(2,1)S(1)} %collective-permute-done.14), channel_id=1, source_target_pairs={{0,1},{1,0},{2,3},{3,2},{4,5},{5,4},{6,7},{7,6},{8,9},{9,8},{10,11... | collective-permute-start | bytes 1572872 | tf_op jit(solution)/shard_map/ppermute | solution.py:176
  71.9 0.8 copy-start.1
  72.7 7.9 %copy-start.2 = (s32[8,12]{1,0:T(8,128)S(1)}, s32[8,12]{1,0:T(8,128)}, u32[]{:S(2)}) copy-start(s32[8,12]{1,0:T(8,128)} %param.11) | copy-start | bytes 1156
  72.7 8.6 %copy-start.3 = (s32[8]{0:T(128)S(1)}, s32[8]{0:T(128)}, u32[]{:S(2)}) copy-start(s32[8]{0:T(128)} %param.12) | copy-start | bytes 100
  72.7 8.7 %copy-start.4 = (s32[512]{0:T(512)S(1)}, s32[512]{0:T(512)}, u32[]{:S(2)}) copy-start(s32[512]{0:T(512)} %param.10) | copy-start | bytes 6148
  75.0 20.0 %all-to-all-start = ((bf16[16,1,64,256]{3,2,1,0:T(8,128)(2,1)}), bf16[16,1,64,256]{3,2,1,0:T(8,128)(2,1)S(1)}, u32[]{:S(2)}, u32[]{:S(2)}) async-start(bf16[16,1,64,256]{3,2,1,0:T(8,128)(2,1)} %bitcast.10), calls=%async_computation | async-start | bytes 1048576 | tf_op jit(solution)/shard_map/all_to_all | solution.py:297

commit v13 on v12

--- a/solution.py
+++ b/solution.py
@@ -105,12 +105,11 @@
     raws, out_ref = refs[:-1], refs[-1]
     nblocks = slots_ref.shape[0]
     groups = len(raws) // CHUNKS
-    first = pl.program_id(0) * out_ref.shape[0]
-    for slot in range(out_ref.shape[0]):
+    for slot in range(nblocks):
         for i, raw_ref in enumerate(raws):
             examples, width = raw_ref.shape[0] // nblocks, raw_ref.shape[1]
             chunk, group = divmod(i, groups)
-            rows = pl.ds(slots_ref[first + slot], examples, stride=nblocks)
+            rows = pl.ds(slots_ref[slot], examples, stride=nblocks)
             out_ref[
                 slot, group * examples:(group + 1) * examples, chunk * width:(chunk + 1) * width
             ] = raw_ref[rows, :].astype(out_ref.dtype)
@@ -120,14 +119,12 @@
     nblocks = slots.shape[0]
     rows, width = raws[0].shape
     groups = len(raws) // CHUNKS
-    shape = (nblocks, groups * rows // nblocks, CHUNKS * width)
     return pl.pallas_call(
         order_kernel,
-        grid=(4,),
         in_specs=[pl.BlockSpec(memory_space=pltpu.SMEM)] + [pl.BlockSpec(memory_space=pltpu.VMEM)] * len(raws),
-        out_specs=pl.BlockSpec((nblocks // 4,) + shape[1:], lambda i: (i, 0, 0)),
-        out_shape=jax.ShapeDtypeStruct(shape, jnp.bfloat16),
-        compiler_params=pltpu.CompilerParams(vmem_limit_bytes=8 * 1024 * 1024),
+        out_specs=pl.BlockSpec(memory_space=pltpu.VMEM),
+        out_shape=jax.ShapeDtypeStruct((nblocks, groups * rows // nblocks, CHUNKS * width), jnp.bfloat16),
+        compiler_params=pltpu.CompilerParams(vmem_limit_bytes=4 * 1024 * 1024),
         cost_estimate=pl.CostEstimate(
             flops=rows * width, bytes_accessed=6 * len(raws) * rows * width, transcendentals=0
         ),
@@ -264,26 +261,27 @@
     *full, high, low = product(other_core, left, [precond], other_kernel, OTHER_VMEM)
     sent = [pack(value) for value in full]
     got = [swap(value, 0) for value in sent]
+    blocks = after(blocks, sent)
+    near = features(blocks, 0, 2 * middle, 0)
+    sibling = swap(near, 0)
     mine = product(after(core, sent), left, [high, low], mine_kernel, MINE_VMEM)
     one = paths(mine[0], got[0])
     sent = messages(one, 0)
     two = paths(mine[1], after(got[1], sent))
-    blocks = after(blocks, sent)
-    near = features(blocks, 0, 2 * middle, 0)
-    late = features(blocks, middle, middle, 1)
-    sibling = swap(near, 0)
     one = exchange(one, sent, 0)
     sent = messages(one, 1)
-    two = exchange(two, after(messages(two, 0), sent), 0)
+    sent_two = after(messages(two, 0), (sent, sibling))
     one = halve(exchange(one, sent, 1))
-    got_one = swap(pack(one), rest[-1])
-    two = exchange(two, after(messages(two, 1), sibling), 1)
+    sent = pack(one)
+    got_one = swap(sent, rest[-1])
+    two = exchange(two, sent_two, 0)
+    two = exchange(two, messages(two, 1), 1)
     two = halve(two)
     sent = pack(two)
     one = (after(one, sent) + unpack(got_one)).astype(jnp.bfloat16)
     got_two = swap(sent, rest[-1])
-    late, early = after((late, early), one)
-    late = swap(late, ybit)
+    blocks, early = after((blocks, early), one)
+    late = swap(features(blocks, middle, middle, 1), ybit)
     one = gather(one)
     groups = [
         jnp.concatenate([near, sibling], axis=0),

time: 96.2 us -> 86.3 us (0.90)
  waiting for transfers between devices: 49 us -> 37.5 us
  starting transfers between devices: 26.1 us -> 28.2 us
    ppermute x19, waiting for transfers between devices: 36.3 us -> 24.8 us  [swap(): return lax.ppermute(value, 'rows', [(r, r ^ 1 << bit) for r in range(n)])]
    ppermute x19, starting transfers between devices: 20.6 us -> 23.5 us  [swap(): return lax.ppermute(value, 'rows', [(r, r ^ 1 << bit) for r in range(n)])]
  transfers between devices with their start and end apart: 20 -> 20, of which waited for: 14 -> 13; matrix products, arithmetic and copies ran while one was open for 8% -> 9% of each run, Pallas kernels for 6% -> 7%
where the time goes in v13:
time: 86.3 us; the launch traced here: 86.1 us
  waiting for transfers between devices  37.5 us (43%)
  starting transfers between devices  28.2 us (33%)
  Pallas kernels  8.77 us (10%)
  other arithmetic  4.83 us (6%)
  matrix products  3.15 us (4%)
  local copies, waits for them, and re-layouts  3.09 us (4%)
    ppermute x19, waiting for transfers between devices, swap(): return lax.ppermute(value, 'rows', [(r, r ^ 1 << bit) for r in range(n)])  24.8 us
    ppermute x19, starting transfers between devices, swap(): return lax.ppermute(value, 'rows', [(r, r ^ 1 << bit) for r in range(n)])  23.5 us
    all_to_all x1, waiting for transfers between devices, shards(): lax.all_to_all(ordered, 'rows', split_axis=0, concat_axis=0, tiled=True)  12.7 us
    pallas_call x2, Pallas kernels, product(): pl.pallas_call(kernel, in_specs=[pl.BlockSpec(memory_space=pltpu.SMEM), i...  6.03 us
    all_to_all x1, starting transfers between devices, shards(): lax.all_to_all(ordered, 'rows', split_axis=0, concat_axis=0, tiled=True)  4.73 us
    dot_general x4, matrix products, scores(): lax.dot_general(group, value, (((1,), (1,)), ((), ())), preferred_element...  2.89 us
    pallas_call x1, Pallas kernels, in_slot_order(): pl.pallas_call(order_kernel, in_specs=[pl.BlockSpec(memory_space=pltpu.SM...  1.88 us
  transfers between devices with their start and end apart: 20, of which 13 were waited for; matrix products, arithmetic and copies ran while one was open for 9% of the time, Pallas kernels for 7%

profile of v13, /device:TPU:0, one launch (start us, length us, event | category | flops | bytes accessed | tf_op | source)
XLA Modules:
  0.0 86.1 jit_solution(8613897923168543600)
XLA Ops:
  0.0 1.3 %fusion.2 = (bf16[512,256]{1,0:T(8,128)(2,1)S(1)}, bf16[512,256]{1,0:T(8,128)(2,1)S(1)}) fusion(f32[512,256]{1,0:T(8,128)} %param.7), kind=kLoop, calls=%fused_computation.10 | loop fusion | flops 524288 | bytes 1048576 | tf_op jit(solution)/shard_map/convert_element_type | solution.py:253
  1.3 0.4 copy-done
  1.8 0.2 constant_dynamic-slice_fusion.2
  2.0 3.0 %collective-permute-start.13 = (bf16[128,2048]{1,0:T(8,128)(2,1)S(1)}, bf16[128,2048]{1,0:T(8,128)(2,1)S(1)}, u32[]{:S(2)}, u32[]{:S(2)}) collective-permute-start(bf16[128,2048]{1,0:T(8,128)(2,1)S(1)} %constant_dynamic-slice_fusion.2), channel_id=1, source_target_pairs={{0,2},{1,3},{2,0},{3,1},{4,6},{5,7},{6,4},{7,5},{8,10},{9,11},{10,... | collective-permute-start | bytes 1572872 | tf_op jit(solution)/shard_map/ppermute | solution.py:173
  5.0 4.2 %shard_map.73 = (f32[128,4096]{1,0:T(8,128)S(1)}, f32[128,4096]{1,0:T(8,128)S(1)}, bf16[256,4096]{1,0:T(8,128)(2,1)S(1)}, bf16[256,4096]{1,0:T(8,128)(2,1)S(1)}) custom-call(s32[1]{0:T(128)} %bitcast.1.core_ref, bf16[512,768]{1,0:T(8,128)(2,1)S(1)} %pad_maximum_fusion.3.rows_ref, f32[256,4096]{1,0:T(8,128)} %columns_hbm.1), custom_call_target="tpu_custom_call" | custom-call | flops 1610612736 | bytes 8388608 | tf_op jit(solution)/shard_map/pallas_call | solution.py:89
  9.7 0.6 collective-permute-start.6
  10.3 0.4 constant_dynamic-slice_fusion.1
  10.8 1.8 %shard_map.74 = (f32[128,4096]{1,0:T(8,128)S(1)}, f32[128,4096]{1,0:T(8,128)S(1)}) custom-call(s32[1]{0:T(128)} %bitcast.2.core_ref, bf16[512,768]{1,0:T(8,128)(2,1)S(1)} %pad_maximum_fusion.3.rows_ref, bf16[256,4096]{1,0:T(8,128)(2,1)S(1)} %get-tuple-element.52.high_ref, bf16[256,4096]{1,0:T(8,128)(2,1)S(1)} %get-tuple-element.53.low_ref), custom_call_target="tpu_custom_call" | custom-call | flops 1610612736 | bytes 8388608 | tf_op jit(solution)/shard_map/pallas_call | solution.py:89
  12.6 0.3 multiply_add_fusion.1
  13.2 0.2 multiply_convert_fusion.7
  13.5 2.1 %collective-permute-start.4 = (f16[32,4096]{1,0:T(8,128)(2,1)S(1)}, f16[32,4096]{1,0:T(8,128)(2,1)S(1)}, u32[]{:S(2)}, u32[]{:S(2)}) collective-permute-start(f16[32,4096]{1,0:T(8,128)(2,1)S(1)} %multiply_convert_fusion.6), channel_id=1, source_target_pairs={{0,4},{1,5},{2,6},{3,7},{4,0},{5,1},{6,2},{7,3},{8,12},{9,13},{10,... | collective-permute-start | bytes 786440 | tf_op jit(solution)/shard_map/ppermute | solution.py:173
  15.7 0.3 multiply_add_fusion
  16.2 0.2 multiply_convert_fusion.5
  16.4 6.1 %collective-permute-done.2 = f16[64,2048]{1,0:T(8,128)(2,1)S(1)} collective-permute-done((f16[64,2048]{1,0:T(8,128)(2,1)S(1)}, f16[64,2048]{1,0:T(8,128)(2,1)S(1)}, u32[]{:S(2)}, u32[]{:S(2)}) %collective-permute-start.2) | collective-permute-done | bytes 262176 | tf_op jit(solution)/shard_map/ppermute | solution.py:173
  22.8 1.9 %collective-permute-start.3 = (f16[32,2048]{1,0:T(8,128)(2,1)S(1)}, f16[32,2048]{1,0:T(8,128)(2,1)S(1)}, u32[]{:S(2)}, u32[]{:S(2)}) collective-permute-start(f16[32,2048]{1,0:T(8,128)(2,1)S(1)} %multiply_convert_fusion.11), channel_id=1, source_target_pairs={{0,4},{1,5},{2,6},{3,7},{4,0},{5,1},{6,2},{7,3},{8,12},{9,13},{10,... | collective-permute-start | bytes 393224 | tf_op jit(solution)/shard_map/ppermute | solution.py:173
  24.9 1.6 %collective-permute-start.5 = (f16[32,2048]{1,0:T(8,128)(2,1)S(1)}, f16[32,2048]{1,0:T(8,128)(2,1)S(1)}, u32[]{:S(2)}, u32[]{:S(2)}) collective-permute-start(f16[32,2048]{1,0:T(8,128)(2,1)S(1)} %multiply_convert_fusion.10), channel_id=1, source_target_pairs={{0,2},{1,3},{2,0},{3,1},{4,6},{5,7},{6,4},{7,5},{8,10},{9,11},{10,... | collective-permute-start | bytes 393224 | tf_op jit(solution)/shard_map/ppermute | solution.py:173
  26.5 0.5 collective-permute-start.7
  27.0 0.2 collective-permute-start.9
  27.2 0.8 collective-permute-done.3
  28.1 3.3 %collective-permute-done.5 = f16[32,2048]{1,0:T(8,128)(2,1)S(1)} collective-permute-done((f16[32,2048]{1,0:T(8,128)(2,1)S(1)}, f16[32,2048]{1,0:T(8,128)(2,1)S(1)}, u32[]{:S(2)}, u32[]{:S(2)}) %collective-permute-start.5) | collective-permute-done | bytes 131104 | tf_op jit(solution)/shard_map/ppermute | solution.py:173
  31.6 2.7 %collective-permute-start.11 = (f16[2,32,2048]{2,1,0:T(8,128)(2,1)S(1)}, f16[2,32,2048]{2,1,0:T(8,128)(2,1)S(1)}, u32[]{:S(2)}, u32[]{:S(2)}) collective-permute-start(f16[2,32,2048]{2,1,0:T(8,128)(2,1)S(1)} %get-tuple-element.86), channel_id=1, source_target_pairs={{0,8},{1,9},{2,10},{3,11},{4,12},{5,13},{6,14},{7,15},{8,0},{9,1},... | collective-permute-start | bytes 786440 | tf_op jit(solution)/shard_map/ppermute | solution.py:173
  34.3 1.0 %collective-permute-done.7 = f16[64,2048]{1,0:T(8,128)(2,1)S(1)} collective-permute-done((f16[64,2048]{1,0:T(8,128)(2,1)S(1)}, f16[64,2048]{1,0:T(8,128)(2,1)S(1)}, u32[]{:S(2)}, u32[]{:S(2)}) %collective-permute-start.7) | collective-permute-done | bytes 262176 | tf_op jit(solution)/shard_map/ppermute | solution.py:173
  35.3 0.2 multiply_add_fusion.3
  35.6 0.5 collective-permute-start.8
  36.1 1.9 %collective-permute-done.9 = f16[32,4096]{1,0:T(8,128)(2,1)S(1)} collective-permute-done((f16[32,4096]{1,0:T(8,128)(2,1)S(1)}, f16[32,4096]{1,0:T(8,128)(2,1)S(1)}, u32[]{:S(2)}, u32[]{:S(2)}) %collective-permute-start.9) | collective-permute-done | bytes 262176 | tf_op jit(solution)/shard_map/ppermute | solution.py:173
  38.2 2.1 %collective-permute-start.10 = (f16[32,2048]{1,0:T(8,128)(2,1)S(1)}, f16[32,2048]{1,0:T(8,128)(2,1)S(1)}, u32[]{:S(2)}, u32[]{:S(2)}) collective-permute-start(f16[32,2048]{1,0:T(8,128)(2,1)S(1)} %multiply_convert_fusion.8), channel_id=1, source_target_pairs={{0,2},{1,3},{2,0},{3,1},{4,6},{5,7},{6,4},{7,5},{8,10},{9,11},{10,... | collective-permute-start | bytes 393224 | tf_op jit(solution)/shard_map/ppermute | solution.py:173
  40.4 1.6 %collective-permute-done.8 = f16[32,2048]{1,0:T(8,128)(2,1)S(1)} collective-permute-done((f16[32,2048]{1,0:T(8,128)(2,1)S(1)}, f16[32,2048]{1,0:T(8,128)(2,1)S(1)}, u32[]{:S(2)}, u32[]{:S(2)}) %collective-permute-start.8) | collective-permute-done | bytes 131104 | tf_op jit(solution)/shard_map/ppermute | solution.py:173
  42.1 1.2 %collective-permute-done.10 = f16[32,2048]{1,0:T(8,128)(2,1)S(1)} collective-permute-done((f16[32,2048]{1,0:T(8,128)(2,1)S(1)}, f16[32,2048]{1,0:T(8,128)(2,1)S(1)}, u32[]{:S(2)}, u32[]{:S(2)}) %collective-permute-start.10) | collective-permute-done | bytes 131104 | tf_op jit(solution)/shard_map/ppermute | solution.py:173
  43.5 2.2 %collective-permute-start.17 = (f16[2,32,2048]{2,1,0:T(8,128)(2,1)S(1)}, f16[2,32,2048]{2,1,0:T(8,128)(2,1)S(1)}, u32[]{:S(2)}, u32[]{:S(2)}) collective-permute-start(f16[2,32,2048]{2,1,0:T(8,128)(2,1)S(1)} %multiply_convert_fusion.3), channel_id=1, source_target_pairs={{0,8},{1,9},{2,10},{3,11},{4,12},{5,13},{6,14},{7,15},{8,0},{9,1},... | collective-permute-start | bytes 786440 | tf_op jit(solution)/shard_map/ppermute | solution.py:173
  45.8 3.3 %collective-permute-start.12 = (bf16[2,32,2048]{2,1,0:T(8,128)(2,1)S(1)}, bf16[2,32,2048]{2,1,0:T(8,128)(2,1)S(1)}, u32[]{:S(2)}, u32[]{:S(2)}) collective-permute-start(bf16[2,32,2048]{2,1,0:T(8,128)(2,1)S(1)} %add_convert_fusion.1), channel_id=1, source_target_pairs={{0,4},{1,5},{2,6},{3,7},{4,0},{5,1},{6,2},{7,3},{8,12},{9,13},{10,... | collective-permute-start | bytes 786440 | tf_op jit(solution)/shard_map/ppermute | solution.py:173
  49.1 0.2 constant_dynamic-slice_fusion.3
  49.3 2.5 %collective-permute-start.14 = (bf16[128,2048]{1,0:T(8,128)(2,1)S(1)}, bf16[128,2048]{1,0:T(8,128)(2,1)S(1)}, u32[]{:S(2)}, u32[]{:S(2)}) collective-permute-start(bf16[128,2048]{1,0:T(8,128)(2,1)S(1)} %constant_dynamic-slice_fusion.3), channel_id=1, source_target_pairs={{0,2},{1,3},{2,0},{3,1},{4,6},{5,7},{6,4},{7,5},{8,10},{9,11},{10,... | collective-permute-start | bytes 1572872 | tf_op jit(solution)/shard_map/ppermute | solution.py:173
  51.9 3.5 %collective-permute-done.17 = f16[2,32,2048]{2,1,0:T(8,128)(2,1)S(1)} collective-permute-done((f16[2,32,2048]{2,1,0:T(8,128)(2,1)S(1)}, f16[2,32,2048]{2,1,0:T(8,128)(2,1)S(1)}, u32[]{:S(2)}, u32[]{:S(2)}) %collective-permute-start.17) | collective-permute-done | bytes 262176 | tf_op jit(solution)/shard_map/ppermute | solution.py:173
  55.5 0.7 collective-permute-done.12
  56.4 2.6 %collective-permute-done.14 = bf16[128,2048]{1,0:T(8,128)(2,1)S(1)} collective-permute-done((bf16[128,2048]{1,0:T(8,128)(2,1)S(1)}, bf16[128,2048]{1,0:T(8,128)(2,1)S(1)}, u32[]{:S(2)}, u32[]{:S(2)}) %collective-permute-start.14) | collective-permute-done | bytes 524320 | tf_op jit(solution)/shard_map/ppermute | solution.py:173
  59.0 0.7 fusion.1.refs_0_
  59.8 1.1 %collective-permute-done.16 = bf16[128,2048]{1,0:T(8,128)(2,1)S(1)} collective-permute-done((bf16[128,2048]{1,0:T(8,128)(2,1)S(1)}, bf16[128,2048]{1,0:T(8,128)(2,1)S(1)}, u32[]{:S(2)}, u32[]{:S(2)}) %collective-permute-start.16) | collective-permute-done | bytes 524320 | tf_op jit(solution)/shard_map/ppermute | solution.py:173
  60.9 0.7 fusion.12.refs_1_
  61.7 0.8 collective-permute-done.18
  62.6 0.7 fusion.13.refs_3_
  63.3 0.7 fusion.refs_2_
  64.1 1.9 %shard_map.75 = bf16[16,64,256]{2,1,0:T(8,128)(2,1)} custom-call(s32[16]{0:T(128)S(1)} %copy-done.1, f32[512,128]{1,0:T(8,128)S(1)} %fusion.1.refs_0_, f32[512,128]{1,0:T(8,128)S(1)} %fusion.12.refs_1_, f32[512,128]{1,0:T(8,128)S(1)} %fusion.refs_2_, f32[512,128]{1,0:T(8,128)S(1)} %fusion.13.refs_3_), custom_call_target="tpu_custom_call" | custom-call | flops 65536 | bytes 1572864 | tf_op jit(solution)/shard_map/pallas_call | solution.py:122
  66.0 4.7 %all-to-all-start = ((bf16[16,1,64,256]{3,2,1,0:T(8,128)(2,1)}), bf16[16,1,64,256]{3,2,1,0:T(8,128)(2,1)S(1)}, u32[]{:S(2)}, u32[]{:S(2)}) async-start(bf16[16,1,64,256]{3,2,1,0:T(8,128)(2,1)} %bitcast.10), calls=%async_computation | async-start | bytes 1048576 | tf_op jit(solution)/shard_map/all_to_all | solution.py:295
  70.8 0.6 dynamic_slice.79
  71.5 0.3 fusion.3
  71.8 0.6 constant_dynamic-slice_fusion.allowed_ref
  72.5 12.7 %all-to-all-done = bf16[16,1,64,256]{3,2,1,0:T(8,128)(2,1)S(1)} async-done(((bf16[16,1,64,256]{3,2,1,0:T(8,128)(2,1)}), bf16[16,1,64,256]{3,2,1,0:T(8,128)(2,1)S(1)}, u32[]{:S(2)}, u32[]{:S(2)}) %all-to-all-start) | async-done | bytes 524320 | tf_op jit(solution)/shard_map/all_to_all | solution.py:295
  85.2 0.9 %shard_map.76 = f32[1024,128]{1,0:T(8,128)} custom-call(bf16[16,1,4,16,256]{4,3,2,1,0:T(8,128)(2,1)S(1)} %bitcast.28, f32[1,512]{1,0:T(1,128)S(1)} %constant_dynamic-slice_fusion.allowed_ref), custom_call_target="tpu_custom_call" | custom-call | flops 262144 | bytes 1048576 | tf_op jit(solution)/shard_map/pallas_call | solution.py:151
  (53 shorter events, 3.3 us)
Async XLA Ops:
  0.0 1.7 %copy-start = (bf16[16,16,4096]{2,1,0:T(8,128)(2,1)S(1)}, bf16[16,16,4096]{2,1,0:T(8,128)(2,1)}, u32[]{:S(2)}) copy-start(bf16[16,16,4096]{2,1,0:T(8,128)(2,1)} %param.9) | copy-start | bytes 6291460
  2.0 47.1 %collective-permute-start.13 = (bf16[128,2048]{1,0:T(8,128)(2,1)S(1)}, bf16[128,2048]{1,0:T(8,128)(2,1)S(1)}, u32[]{:S(2)}, u32[]{:S(2)}) collective-permute-start(bf16[128,2048]{1,0:T(8,128)(2,1)S(1)} %constant_dynamic-slice_fusion.2), channel_id=1, source_target_pairs={{0,2},{1,3},{2,0},{3,1},{4,6},{5,7},{6,4},{7,5},{8,10},{9,11},{10,... | collective-permute-start | bytes 1572872 | tf_op jit(solution)/shard_map/ppermute | solution.py:173
  9.4 3.1 %collective-permute-start.1 = (f16[128,4096]{1,0:T(8,128)(2,1)S(1)}, f16[128,4096]{1,0:T(8,128)(2,1)S(1)}, u32[]{:S(2)}, u32[]{:S(2)}) collective-permute-start(f16[128,4096]{1,0:T(8,128)(2,1)S(1)} %multiply_convert_fusion.1), channel_id=1, source_target_pairs={{0,1},{1,0},{2,3},{3,2},{4,5},{5,4},{6,7},{7,6},{8,9},{9,8},{10,11... | collective-permute-start | bytes 3145736 | tf_op jit(solution)/shard_map/ppermute | solution.py:173
  9.7 5.9 %collective-permute-start.6 = (f16[128,4096]{1,0:T(8,128)(2,1)S(1)}, f16[128,4096]{1,0:T(8,128)(2,1)S(1)}, u32[]{:S(2)}, u32[]{:S(2)}) collective-permute-start(f16[128,4096]{1,0:T(8,128)(2,1)S(1)} %multiply_convert_fusion), channel_id=1, source_target_pairs={{0,1},{1,0},{2,3},{3,2},{4,5},{5,4},{6,7},{7,6},{8,9},{9,8},{10,11... | collective-permute-start | bytes 3145736 | tf_op jit(solution)/shard_map/ppermute | solution.py:173
  10.7 15.8 %collective-permute-start = (bf16[256,2048]{1,0:T(8,128)(2,1)S(1)}, bf16[256,2048]{1,0:T(8,128)(2,1)S(1)}, u32[]{:S(2)}, u32[]{:S(2)}) collective-permute-start(bf16[256,2048]{1,0:T(8,128)(2,1)S(1)} %constant_dynamic-slice_fusion.1), channel_id=1, source_target_pairs={{0,1},{1,0},{2,3},{3,2},{4,5},{5,4},{6,7},{7,6},{8,9},{9,8},{10,11... | collective-permute-start | bytes 3145736 | tf_op jit(solution)/shard_map/ppermute | solution.py:173
  13.4 9.2 %collective-permute-start.2 = (f16[64,2048]{1,0:T(8,128)(2,1)S(1)}, f16[64,2048]{1,0:T(8,128)(2,1)S(1)}, u32[]{:S(2)}, u32[]{:S(2)}) collective-permute-start(f16[64,2048]{1,0:T(8,128)(2,1)S(1)} %multiply_convert_fusion.7), channel_id=1, source_target_pairs={{0,2},{1,3},{2,0},{3,1},{4,6},{5,7},{6,4},{7,5},{8,10},{9,11},{10,... | collective-permute-start | bytes 786440 | tf_op jit(solution)/shard_map/ppermute | solution.py:173
  13.5 11.1 %collective-permute-start.4 = (f16[32,4096]{1,0:T(8,128)(2,1)S(1)}, f16[32,4096]{1,0:T(8,128)(2,1)S(1)}, u32[]{:S(2)}, u32[]{:S(2)}) collective-permute-start(f16[32,4096]{1,0:T(8,128)(2,1)S(1)} %multiply_convert_fusion.6), channel_id=1, source_target_pairs={{0,4},{1,5},{2,6},{3,7},{4,0},{5,1},{6,2},{7,3},{8,12},{9,13},{10,... | collective-permute-start | bytes 786440 | tf_op jit(solution)/shard_map/ppermute | solution.py:173
  22.8 5.3 %collective-permute-start.3 = (f16[32,2048]{1,0:T(8,128)(2,1)S(1)}, f16[32,2048]{1,0:T(8,128)(2,1)S(1)}, u32[]{:S(2)}, u32[]{:S(2)}) collective-permute-start(f16[32,2048]{1,0:T(8,128)(2,1)S(1)} %multiply_convert_fusion.11), channel_id=1, source_target_pairs={{0,4},{1,5},{2,6},{3,7},{4,0},{5,1},{6,2},{7,3},{8,12},{9,13},{10,... | collective-permute-start | bytes 393224 | tf_op jit(solution)/shard_map/ppermute | solution.py:173
  24.9 6.5 %collective-permute-start.5 = (f16[32,2048]{1,0:T(8,128)(2,1)S(1)}, f16[32,2048]{1,0:T(8,128)(2,1)S(1)}, u32[]{:S(2)}, u32[]{:S(2)}) collective-permute-start(f16[32,2048]{1,0:T(8,128)(2,1)S(1)} %multiply_convert_fusion.10), channel_id=1, source_target_pairs={{0,2},{1,3},{2,0},{3,1},{4,6},{5,7},{6,4},{7,5},{8,10},{9,11},{10,... | collective-permute-start | bytes 393224 | tf_op jit(solution)/shard_map/ppermute | solution.py:173
  26.5 8.8 %collective-permute-start.7 = (f16[64,2048]{1,0:T(8,128)(2,1)S(1)}, f16[64,2048]{1,0:T(8,128)(2,1)S(1)}, u32[]{:S(2)}, u32[]{:S(2)}) collective-permute-start(f16[64,2048]{1,0:T(8,128)(2,1)S(1)} %multiply_convert_fusion.5), channel_id=1, source_target_pairs={{0,2},{1,3},{2,0},{3,1},{4,6},{5,7},{6,4},{7,5},{8,10},{9,11},{10,... | collective-permute-start | bytes 786440 | tf_op jit(solution)/shard_map/ppermute | solution.py:173
  27.0 11.0 %collective-permute-start.9 = (f16[32,4096]{1,0:T(8,128)(2,1)S(1)}, f16[32,4096]{1,0:T(8,128)(2,1)S(1)}, u32[]{:S(2)}, u32[]{:S(2)}) collective-permute-start(f16[32,4096]{1,0:T(8,128)(2,1)S(1)} %multiply_convert_fusion.4), channel_id=1, source_target_pairs={{0,4},{1,5},{2,6},{3,7},{4,0},{5,1},{6,2},{7,3},{8,12},{9,13},{10,... | collective-permute-start | bytes 786440 | tf_op jit(solution)/shard_map/ppermute | solution.py:173
  31.6 14.1 %collective-permute-start.11 = (f16[2,32,2048]{2,1,0:T(8,128)(2,1)S(1)}, f16[2,32,2048]{2,1,0:T(8,128)(2,1)S(1)}, u32[]{:S(2)}, u32[]{:S(2)}) collective-permute-start(f16[2,32,2048]{2,1,0:T(8,128)(2,1)S(1)} %get-tuple-element.86), channel_id=1, source_target_pairs={{0,8},{1,9},{2,10},{3,11},{4,12},{5,13},{6,14},{7,15},{8,0},{9,1},... | collective-permute-start | bytes 786440 | tf_op jit(solution)/shard_map/ppermute | solution.py:173
  35.6 6.4 %collective-permute-start.8 = (f16[32,2048]{1,0:T(8,128)(2,1)S(1)}, f16[32,2048]{1,0:T(8,128)(2,1)S(1)}, u32[]{:S(2)}, u32[]{:S(2)}) collective-permute-start(f16[32,2048]{1,0:T(8,128)(2,1)S(1)} %multiply_convert_fusion.9), channel_id=1, source_target_pairs={{0,4},{1,5},{2,6},{3,7},{4,0},{5,1},{6,2},{7,3},{8,12},{9,13},{10,... | collective-permute-start | bytes 393224 | tf_op jit(solution)/shard_map/ppermute | solution.py:173
  38.2 5.1 %collective-permute-start.10 = (f16[32,2048]{1,0:T(8,128)(2,1)S(1)}, f16[32,2048]{1,0:T(8,128)(2,1)S(1)}, u32[]{:S(2)}, u32[]{:S(2)}) collective-permute-start(f16[32,2048]{1,0:T(8,128)(2,1)S(1)} %multiply_convert_fusion.8), channel_id=1, source_target_pairs={{0,2},{1,3},{2,0},{3,1},{4,6},{5,7},{6,4},{7,5},{8,10},{9,11},{10,... | collective-permute-start | bytes 393224 | tf_op jit(solution)/shard_map/ppermute | solution.py:173
  43.5 11.9 %collective-permute-start.17 = (f16[2,32,2048]{2,1,0:T(8,128)(2,1)S(1)}, f16[2,32,2048]{2,1,0:T(8,128)(2,1)S(1)}, u32[]{:S(2)}, u32[]{:S(2)}) collective-permute-start(f16[2,32,2048]{2,1,0:T(8,128)(2,1)S(1)} %multiply_convert_fusion.3), channel_id=1, source_target_pairs={{0,8},{1,9},{2,10},{3,11},{4,12},{5,13},{6,14},{7,15},{8,0},{9,1},... | collective-permute-start | bytes 786440 | tf_op jit(solution)/shard_map/ppermute | solution.py:173
  45.8 10.5 %collective-permute-start.12 = (bf16[2,32,2048]{2,1,0:T(8,128)(2,1)S(1)}, bf16[2,32,2048]{2,1,0:T(8,128)(2,1)S(1)}, u32[]{:S(2)}, u32[]{:S(2)}) collective-permute-start(bf16[2,32,2048]{2,1,0:T(8,128)(2,1)S(1)} %add_convert_fusion.1), channel_id=1, source_target_pairs={{0,4},{1,5},{2,6},{3,7},{4,0},{5,1},{6,2},{7,3},{8,12},{9,13},{10,... | collective-permute-start | bytes 786440 | tf_op jit(solution)/shard_map/ppermute | solution.py:173
  49.3 9.7 %collective-permute-start.14 = (bf16[128,2048]{1,0:T(8,128)(2,1)S(1)}, bf16[128,2048]{1,0:T(8,128)(2,1)S(1)}, u32[]{:S(2)}, u32[]{:S(2)}) collective-permute-start(bf16[128,2048]{1,0:T(8,128)(2,1)S(1)} %constant_dynamic-slice_fusion.3), channel_id=1, source_target_pairs={{0,2},{1,3},{2,0},{3,1},{4,6},{5,7},{6,4},{7,5},{8,10},{9,11},{10,... | collective-permute-start | bytes 1572872 | tf_op jit(solution)/shard_map/ppermute | solution.py:173
  51.8 7.9 %collective-permute-start.15 = (bf16[128,2048]{1,0:T(8,128)(2,1)S(1)}, bf16[128,2048]{1,0:T(8,128)(2,1)S(1)}, u32[]{:S(2)}, u32[]{:S(2)}) collective-permute-start(bf16[128,2048]{1,0:T(8,128)(2,1)S(1)} %collective-permute-done.13), channel_id=1, source_target_pairs={{0,1},{1,0},{2,3},{3,2},{4,5},{5,4},{6,7},{7,6},{8,9},{9,8},{10,11... | collective-permute-start | bytes 1572872 | tf_op jit(solution)/shard_map/ppermute | solution.py:173
  55.5 7.0 %collective-permute-start.18 = (bf16[2,32,2048]{2,1,0:T(8,128)(2,1)S(1)}, bf16[2,32,2048]{2,1,0:T(8,128)(2,1)S(1)}, u32[]{:S(2)}, u32[]{:S(2)}) collective-permute-start(bf16[2,32,2048]{2,1,0:T(8,128)(2,1)S(1)} %add_convert_fusion), channel_id=1, source_target_pairs={{0,4},{1,5},{2,6},{3,7},{4,0},{5,1},{6,2},{7,3},{8,12},{9,13},{10,... | collective-permute-start | bytes 786440 | tf_op jit(solution)/shard_map/ppermute | solution.py:173
  59.0 1.9 %collective-permute-start.16 = (bf16[128,2048]{1,0:T(8,128)(2,1)S(1)}, bf16[128,2048]{1,0:T(8,128)(2,1)S(1)}, u32[]{:S(2)}, u32[]{:S(2)}) collective-permute-start(bf16[128,2048]{1,0:T(8,128)(2,1)S(1)} %collective-permute-done.14), channel_id=1, source_target_pairs={{0,1},{1,0},{2,3},{3,2},{4,5},{5,4},{6,7},{7,6},{8,9},{9,8},{10,11... | collective-permute-start | bytes 1572872 | tf_op jit(solution)/shard_map/ppermute | solution.py:173
  63.3 0.8 copy-start.1
  64.1 6.7 %copy-start.2 = (s32[8,12]{1,0:T(8,128)S(1)}, s32[8,12]{1,0:T(8,128)}, u32[]{:S(2)}) copy-start(s32[8,12]{1,0:T(8,128)} %param.11) | copy-start | bytes 1156
  64.1 7.3 %copy-start.3 = (s32[8]{0:T(128)S(1)}, s32[8]{0:T(128)}, u32[]{:S(2)}) copy-start(s32[8]{0:T(128)} %param.12) | copy-start | bytes 100
  64.1 7.4 %copy-start.4 = (s32[512]{0:T(512)S(1)}, s32[512]{0:T(512)}, u32[]{:S(2)}) copy-start(s32[512]{0:T(512)} %param.10) | copy-start | bytes 6148
  66.0 19.2 %all-to-all-start = ((bf16[16,1,64,256]{3,2,1,0:T(8,128)(2,1)}), bf16[16,1,64,256]{3,2,1,0:T(8,128)(2,1)S(1)}, u32[]{:S(2)}, u32[]{:S(2)}) async-start(bf16[16,1,64,256]{3,2,1,0:T(8,128)(2,1)} %bitcast.10), calls=%async_computation | async-start | bytes 1048576 | tf_op jit(solution)/shard_map/all_to_all | solution.py:295

commit v14 on v13

--- a/solution.py
+++ b/solution.py
@@ -243,7 +243,8 @@
         return lax.dot_general(group, value, (((1,), (1,)), ((), ())), preferred_element_type=jnp.float32)
 
     blocks = train.reshape(examples * nblocks, width)
-    middle = examples // 2 * nblocks
+    total = examples * nblocks
+    middle = max(1, examples * 3 // 8) * nblocks
 
     def features(blocks, first, count, other):
         start = offsets[ybit, width // 2][other]
@@ -262,7 +263,7 @@
     sent = [pack(value) for value in full]
     got = [swap(value, 0) for value in sent]
     blocks = after(blocks, sent)
-    near = features(blocks, 0, 2 * middle, 0)
+    near = features(blocks, 0, total, 0)
     sibling = swap(near, 0)
     mine = product(after(core, sent), left, [high, low], mine_kernel, MINE_VMEM)
     one = paths(mine[0], got[0])
@@ -281,7 +282,7 @@
     one = (after(one, sent) + unpack(got_one)).astype(jnp.bfloat16)
     got_two = swap(sent, rest[-1])
     blocks, early = after((blocks, early), one)
-    late = swap(features(blocks, middle, middle, 1), ybit)
+    late = swap(features(blocks, middle, total - middle, 1), ybit)
     one = gather(one)
     groups = [
         jnp.concatenate([near, sibling], axis=0),

time: 86.3 us -> 85.2 us (0.987)
  starting transfers between devices: 28.2 us -> 20.4 us
  waiting for transfers between devices: 37.5 us -> 44.1 us
    ppermute x19, waiting for transfers between devices: 24.8 us -> 31.5 us  [swap(): return lax.ppermute(value, 'rows', [(r, r ^ 1 << bit) for r in range(n)])]
    ppermute x19, starting transfers between devices: 23.5 us -> 16.9 us  [swap(): return lax.ppermute(value, 'rows', [(r, r ^ 1 << bit) for r in range(n)])]
    all_to_all x1, starting transfers between devices: 4.73 us -> 3.57 us  [shards(): lax.all_to_all(ordered, 'rows', split_axis=0, concat_axis=0, tiled=True)]
  transfers between devices with their start and end apart: 20 -> 20, of which waited for: 13 -> 12; matrix products, arithmetic and copies ran while one was open for 9% -> 9% of each run, Pallas kernels for 7% -> 7%
where the time goes in v14:
time: 85.2 us; the launch traced here: 84.9 us
  waiting for transfers between devices  44.1 us (52%)
  starting transfers between devices  20.4 us (24%)
  Pallas kernels  8.77 us (10%)
  other arithmetic  4.85 us (6%)
  matrix products  3.15 us (4%)
  local copies, waits for them, and re-layouts  3.11 us (4%)
    ppermute x19, waiting for transfers between devices, swap(): return lax.ppermute(value, 'rows', [(r, r ^ 1 << bit) for r in range(n)])  31.5 us
    ppermute x19, starting transfers between devices, swap(): return lax.ppermute(value, 'rows', [(r, r ^ 1 << bit) for r in range(n)])  16.9 us
    all_to_all x1, waiting for transfers between devices, shards(): lax.all_to_all(ordered, 'rows', split_axis=0, concat_axis=0, tiled=True)  12.7 us
    pallas_call x2, Pallas kernels, product(): pl.pallas_call(kernel, in_specs=[pl.BlockSpec(memory_space=pltpu.SMEM), i...  6.03 us
    all_to_all x1, starting transfers between devices, shards(): lax.all_to_all(ordered, 'rows', split_axis=0, concat_axis=0, tiled=True)  3.57 us
    dot_general x4, matrix products, scores(): lax.dot_general(group, value, (((1,), (1,)), ((), ())), preferred_element...  2.89 us
    pallas_call x1, Pallas kernels, in_slot_order(): pl.pallas_call(order_kernel, in_specs=[pl.BlockSpec(memory_space=pltpu.SM...  1.88 us
  transfers between devices with their start and end apart: 20, of which 12 were waited for; matrix products, arithmetic and copies ran while one was open for 9% of the time, Pallas kernels for 7%

profile of v14, /device:TPU:0, one launch (start us, length us, event | category | flops | bytes accessed | tf_op | source)
XLA Modules:
  0.0 84.9 jit_solution(7419626170786791373)
XLA Ops:
  0.0 1.3 %fusion.2 = (bf16[512,256]{1,0:T(8,128)(2,1)S(1)}, bf16[512,256]{1,0:T(8,128)(2,1)S(1)}) fusion(f32[512,256]{1,0:T(8,128)} %param.7), kind=kLoop, calls=%fused_computation.10 | loop fusion | flops 524288 | bytes 1048576 | tf_op jit(solution)/shard_map/convert_element_type | solution.py:254
  1.3 0.4 copy-done
  1.9 3.0 %collective-permute-start.13 = (bf16[96,2048]{1,0:T(8,128)(2,1)S(1)}, bf16[96,2048]{1,0:T(8,128)(2,1)S(1)}, u32[]{:S(2)}, u32[]{:S(2)}) collective-permute-start(bf16[96,2048]{1,0:T(8,128)(2,1)S(1)} %constant_dynamic-slice_fusion.2), channel_id=1, source_target_pairs={{0,2},{1,3},{2,0},{3,1},{4,6},{5,7},{6,4},{7,5},{8,10},{9,11},{10,... | collective-permute-start | bytes 1179656 | tf_op jit(solution)/shard_map/ppermute | solution.py:173
  5.0 4.2 %shard_map.73 = (f32[128,4096]{1,0:T(8,128)S(1)}, f32[128,4096]{1,0:T(8,128)S(1)}, bf16[256,4096]{1,0:T(8,128)(2,1)S(1)}, bf16[256,4096]{1,0:T(8,128)(2,1)S(1)}) custom-call(s32[1]{0:T(128)} %bitcast.1.core_ref, bf16[512,768]{1,0:T(8,128)(2,1)S(1)} %pad_maximum_fusion.3.rows_ref, f32[256,4096]{1,0:T(8,128)} %columns_hbm.1), custom_call_target="tpu_custom_call" | custom-call | flops 1610612736 | bytes 8388608 | tf_op jit(solution)/shard_map/pallas_call | solution.py:89
  9.2 0.2 multiply_convert_fusion.1
  9.5 0.2 multiply_convert_fusion
  9.7 0.6 collective-permute-start.6
  10.3 0.4 constant_dynamic-slice_fusion.1
  10.8 1.8 %shard_map.74 = (f32[128,4096]{1,0:T(8,128)S(1)}, f32[128,4096]{1,0:T(8,128)S(1)}) custom-call(s32[1]{0:T(128)} %bitcast.2.core_ref, bf16[512,768]{1,0:T(8,128)(2,1)S(1)} %pad_maximum_fusion.3.rows_ref, bf16[256,4096]{1,0:T(8,128)(2,1)S(1)} %get-tuple-element.52.high_ref, bf16[256,4096]{1,0:T(8,128)(2,1)S(1)} %get-tuple-element.53.low_ref), custom_call_target="tpu_custom_call" | custom-call | flops 1610612736 | bytes 8388608 | tf_op jit(solution)/shard_map/pallas_call | solution.py:89
  12.6 0.3 multiply_add_fusion.1
  13.1 0.2 multiply_convert_fusion.7
  13.5 2.1 %collective-permute-start.4 = (f16[32,4096]{1,0:T(8,128)(2,1)S(1)}, f16[32,4096]{1,0:T(8,128)(2,1)S(1)}, u32[]{:S(2)}, u32[]{:S(2)}) collective-permute-start(f16[32,4096]{1,0:T(8,128)(2,1)S(1)} %multiply_convert_fusion.6), channel_id=1, source_target_pairs={{0,4},{1,5},{2,6},{3,7},{4,0},{5,1},{6,2},{7,3},{8,12},{9,13},{10,... | collective-permute-start | bytes 786440 | tf_op jit(solution)/shard_map/ppermute | solution.py:173
  15.6 0.3 multiply_add_fusion
  16.2 0.2 multiply_convert_fusion.5
  16.4 5.7 %collective-permute-done.2 = f16[64,2048]{1,0:T(8,128)(2,1)S(1)} collective-permute-done((f16[64,2048]{1,0:T(8,128)(2,1)S(1)}, f16[64,2048]{1,0:T(8,128)(2,1)S(1)}, u32[]{:S(2)}, u32[]{:S(2)}) %collective-permute-start.2) | collective-permute-done | bytes 262176 | tf_op jit(solution)/shard_map/ppermute | solution.py:173
  22.1 0.2 multiply_add_fusion.5
  22.4 1.6 %collective-permute-start.3 = (f16[32,2048]{1,0:T(8,128)(2,1)S(1)}, f16[32,2048]{1,0:T(8,128)(2,1)S(1)}, u32[]{:S(2)}, u32[]{:S(2)}) collective-permute-start(f16[32,2048]{1,0:T(8,128)(2,1)S(1)} %multiply_convert_fusion.11), channel_id=1, source_target_pairs={{0,4},{1,5},{2,6},{3,7},{4,0},{5,1},{6,2},{7,3},{8,12},{9,13},{10,... | collective-permute-start | bytes 393224 | tf_op jit(solution)/shard_map/ppermute | solution.py:173
  24.2 0.6 collective-permute-start.5
  24.8 1.5 %collective-permute-start.7 = (f16[64,2048]{1,0:T(8,128)(2,1)S(1)}, f16[64,2048]{1,0:T(8,128)(2,1)S(1)}, u32[]{:S(2)}, u32[]{:S(2)}) collective-permute-start(f16[64,2048]{1,0:T(8,128)(2,1)S(1)} %multiply_convert_fusion.5), channel_id=1, source_target_pairs={{0,2},{1,3},{2,0},{3,1},{4,6},{5,7},{6,4},{7,5},{8,10},{9,11},{10,... | collective-permute-start | bytes 786440 | tf_op jit(solution)/shard_map/ppermute | solution.py:173
  26.3 0.5 collective-permute-start.9
  26.8 0.7 collective-permute-done.3
  27.6 3.1 %collective-permute-done.5 = f16[32,2048]{1,0:T(8,128)(2,1)S(1)} collective-permute-done((f16[32,2048]{1,0:T(8,128)(2,1)S(1)}, f16[32,2048]{1,0:T(8,128)(2,1)S(1)}, u32[]{:S(2)}, u32[]{:S(2)}) %collective-permute-start.5) | collective-permute-done | bytes 131104 | tf_op jit(solution)/shard_map/ppermute | solution.py:173
  31.0 2.7 %collective-permute-start.11 = (f16[2,32,2048]{2,1,0:T(8,128)(2,1)S(1)}, f16[2,32,2048]{2,1,0:T(8,128)(2,1)S(1)}, u32[]{:S(2)}, u32[]{:S(2)}) collective-permute-start(f16[2,32,2048]{2,1,0:T(8,128)(2,1)S(1)} %get-tuple-element.86), channel_id=1, source_target_pairs={{0,8},{1,9},{2,10},{3,11},{4,12},{5,13},{6,14},{7,15},{8,0},{9,1},... | collective-permute-start | bytes 786440 | tf_op jit(solution)/shard_map/ppermute | solution.py:173
  33.6 1.1 %collective-permute-done.7 = f16[64,2048]{1,0:T(8,128)(2,1)S(1)} collective-permute-done((f16[64,2048]{1,0:T(8,128)(2,1)S(1)}, f16[64,2048]{1,0:T(8,128)(2,1)S(1)}, u32[]{:S(2)}, u32[]{:S(2)}) %collective-permute-start.7) | collective-permute-done | bytes 262176 | tf_op jit(solution)/shard_map/ppermute | solution.py:173
  34.8 0.2 multiply_add_fusion.3
  35.0 0.5 collective-permute-start.8
  35.6 2.0 %collective-permute-done.9 = f16[32,4096]{1,0:T(8,128)(2,1)S(1)} collective-permute-done((f16[32,4096]{1,0:T(8,128)(2,1)S(1)}, f16[32,4096]{1,0:T(8,128)(2,1)S(1)}, u32[]{:S(2)}, u32[]{:S(2)}) %collective-permute-start.9) | collective-permute-done | bytes 262176 | tf_op jit(solution)/shard_map/ppermute | solution.py:173
  37.9 0.6 collective-permute-start.10
  38.4 2.9 %collective-permute-done.8 = f16[32,2048]{1,0:T(8,128)(2,1)S(1)} collective-permute-done((f16[32,2048]{1,0:T(8,128)(2,1)S(1)}, f16[32,2048]{1,0:T(8,128)(2,1)S(1)}, u32[]{:S(2)}, u32[]{:S(2)}) %collective-permute-start.8) | collective-permute-done | bytes 131104 | tf_op jit(solution)/shard_map/ppermute | solution.py:173
  41.4 1.5 %collective-permute-done.10 = f16[32,2048]{1,0:T(8,128)(2,1)S(1)} collective-permute-done((f16[32,2048]{1,0:T(8,128)(2,1)S(1)}, f16[32,2048]{1,0:T(8,128)(2,1)S(1)}, u32[]{:S(2)}, u32[]{:S(2)}) %collective-permute-start.10) | collective-permute-done | bytes 131104 | tf_op jit(solution)/shard_map/ppermute | solution.py:173
  43.1 1.7 %collective-permute-start.17 = (f16[2,32,2048]{2,1,0:T(8,128)(2,1)S(1)}, f16[2,32,2048]{2,1,0:T(8,128)(2,1)S(1)}, u32[]{:S(2)}, u32[]{:S(2)}) collective-permute-start(f16[2,32,2048]{2,1,0:T(8,128)(2,1)S(1)} %multiply_convert_fusion.3), channel_id=1, source_target_pairs={{0,8},{1,9},{2,10},{3,11},{4,12},{5,13},{6,14},{7,15},{8,0},{9,1},... | collective-permute-start | bytes 786440 | tf_op jit(solution)/shard_map/ppermute | solution.py:173
  44.9 1.0 %collective-permute-start.12 = (bf16[2,32,2048]{2,1,0:T(8,128)(2,1)S(1)}, bf16[2,32,2048]{2,1,0:T(8,128)(2,1)S(1)}, u32[]{:S(2)}, u32[]{:S(2)}) collective-permute-start(bf16[2,32,2048]{2,1,0:T(8,128)(2,1)S(1)} %add_convert_fusion.1), channel_id=1, source_target_pairs={{0,4},{1,5},{2,6},{3,7},{4,0},{5,1},{6,2},{7,3},{8,12},{9,13},{10,... | collective-permute-start | bytes 786440 | tf_op jit(solution)/shard_map/ppermute | solution.py:173
  45.9 0.3 constant_dynamic-slice_fusion.3
  46.4 8.6 %collective-permute-done.17 = f16[2,32,2048]{2,1,0:T(8,128)(2,1)S(1)} collective-permute-done((f16[2,32,2048]{2,1,0:T(8,128)(2,1)S(1)}, f16[2,32,2048]{2,1,0:T(8,128)(2,1)S(1)}, u32[]{:S(2)}, u32[]{:S(2)}) %collective-permute-start.17) | collective-permute-done | bytes 262176 | tf_op jit(solution)/shard_map/ppermute | solution.py:173
  55.1 0.8 collective-permute-done.12
  56.0 3.7 %collective-permute-done.14 = bf16[160,2048]{1,0:T(8,128)(2,1)S(1)} collective-permute-done((bf16[160,2048]{1,0:T(8,128)(2,1)S(1)}, bf16[160,2048]{1,0:T(8,128)(2,1)S(1)}, u32[]{:S(2)}, u32[]{:S(2)}) %collective-permute-start.14) | collective-permute-done | bytes 655392 | tf_op jit(solution)/shard_map/ppermute | solution.py:173
  59.7 0.7 fusion.1.refs_0_
  60.5 1.3 %collective-permute-done.16 = bf16[160,2048]{1,0:T(8,128)(2,1)S(1)} collective-permute-done((bf16[160,2048]{1,0:T(8,128)(2,1)S(1)}, bf16[160,2048]{1,0:T(8,128)(2,1)S(1)}, u32[]{:S(2)}, u32[]{:S(2)}) %collective-permute-start.16) | collective-permute-done | bytes 655392 | tf_op jit(solution)/shard_map/ppermute | solution.py:173
  61.8 0.7 fusion.12.refs_1_
  62.6 0.7 fusion.13.refs_3_
  63.4 0.7 fusion.refs_2_
  64.2 1.9 %shard_map.75 = bf16[16,64,256]{2,1,0:T(8,128)(2,1)} custom-call(s32[16]{0:T(128)S(1)} %copy-done.1, f32[512,128]{1,0:T(8,128)S(1)} %fusion.1.refs_0_, f32[512,128]{1,0:T(8,128)S(1)} %fusion.12.refs_1_, f32[512,128]{1,0:T(8,128)S(1)} %fusion.refs_2_, f32[512,128]{1,0:T(8,128)S(1)} %fusion.13.refs_3_), custom_call_target="tpu_custom_call" | custom-call | flops 65536 | bytes 1572864 | tf_op jit(solution)/shard_map/pallas_call | solution.py:122
  66.1 3.6 %all-to-all-start = ((bf16[16,1,64,256]{3,2,1,0:T(8,128)(2,1)}), bf16[16,1,64,256]{3,2,1,0:T(8,128)(2,1)S(1)}, u32[]{:S(2)}, u32[]{:S(2)}) async-start(bf16[16,1,64,256]{3,2,1,0:T(8,128)(2,1)} %bitcast.10), calls=%async_computation | async-start | bytes 1048576 | tf_op jit(solution)/shard_map/all_to_all | solution.py:296
  69.7 0.6 dynamic_slice.79
  70.5 0.3 fusion.3
  70.7 0.6 constant_dynamic-slice_fusion.allowed_ref
  71.4 12.7 %all-to-all-done = bf16[16,1,64,256]{3,2,1,0:T(8,128)(2,1)S(1)} async-done(((bf16[16,1,64,256]{3,2,1,0:T(8,128)(2,1)}), bf16[16,1,64,256]{3,2,1,0:T(8,128)(2,1)S(1)}, u32[]{:S(2)}, u32[]{:S(2)}) %all-to-all-start) | async-done | bytes 524320 | tf_op jit(solution)/shard_map/all_to_all | solution.py:296
  84.1 0.9 %shard_map.76 = f32[1024,128]{1,0:T(8,128)} custom-call(bf16[16,1,4,16,256]{4,3,2,1,0:T(8,128)(2,1)S(1)} %bitcast.28, f32[1,512]{1,0:T(1,128)S(1)} %constant_dynamic-slice_fusion.allowed_ref), custom_call_target="tpu_custom_call" | custom-call | flops 262144 | bytes 1048576 | tf_op jit(solution)/shard_map/pallas_call | solution.py:151
  (53 shorter events, 3.0 us)
Async XLA Ops:
  0.0 1.7 %copy-start = (bf16[16,16,4096]{2,1,0:T(8,128)(2,1)S(1)}, bf16[16,16,4096]{2,1,0:T(8,128)(2,1)}, u32[]{:S(2)}) copy-start(bf16[16,16,4096]{2,1,0:T(8,128)(2,1)} %param.9) | copy-start | bytes 6291460
  1.9 44.0 %collective-permute-start.13 = (bf16[96,2048]{1,0:T(8,128)(2,1)S(1)}, bf16[96,2048]{1,0:T(8,128)(2,1)S(1)}, u32[]{:S(2)}, u32[]{:S(2)}) collective-permute-start(bf16[96,2048]{1,0:T(8,128)(2,1)S(1)} %constant_dynamic-slice_fusion.2), channel_id=1, source_target_pairs={{0,2},{1,3},{2,0},{3,1},{4,6},{5,7},{6,4},{7,5},{8,10},{9,11},{10,... | collective-permute-start | bytes 1179656 | tf_op jit(solution)/shard_map/ppermute | solution.py:173
  9.4 3.1 %collective-permute-start.1 = (f16[128,4096]{1,0:T(8,128)(2,1)S(1)}, f16[128,4096]{1,0:T(8,128)(2,1)S(1)}, u32[]{:S(2)}, u32[]{:S(2)}) collective-permute-start(f16[128,4096]{1,0:T(8,128)(2,1)S(1)} %multiply_convert_fusion.1), channel_id=1, source_target_pairs={{0,1},{1,0},{2,3},{3,2},{4,5},{5,4},{6,7},{7,6},{8,9},{9,8},{10,11... | collective-permute-start | bytes 3145736 | tf_op jit(solution)/shard_map/ppermute | solution.py:173
  9.7 5.9 %collective-permute-start.6 = (f16[128,4096]{1,0:T(8,128)(2,1)S(1)}, f16[128,4096]{1,0:T(8,128)(2,1)S(1)}, u32[]{:S(2)}, u32[]{:S(2)}) collective-permute-start(f16[128,4096]{1,0:T(8,128)(2,1)S(1)} %multiply_convert_fusion), channel_id=1, source_target_pairs={{0,1},{1,0},{2,3},{3,2},{4,5},{5,4},{6,7},{7,6},{8,9},{9,8},{10,11... | collective-permute-start | bytes 3145736 | tf_op jit(solution)/shard_map/ppermute | solution.py:173
  10.7 14.2 %collective-permute-start = (bf16[256,2048]{1,0:T(8,128)(2,1)S(1)}, bf16[256,2048]{1,0:T(8,128)(2,1)S(1)}, u32[]{:S(2)}, u32[]{:S(2)}) collective-permute-start(bf16[256,2048]{1,0:T(8,128)(2,1)S(1)} %constant_dynamic-slice_fusion.1), channel_id=1, source_target_pairs={{0,1},{1,0},{2,3},{3,2},{4,5},{5,4},{6,7},{7,6},{8,9},{9,8},{10,11... | collective-permute-start | bytes 3145736 | tf_op jit(solution)/shard_map/ppermute | solution.py:173
  13.3 8.8 %collective-permute-start.2 = (f16[64,2048]{1,0:T(8,128)(2,1)S(1)}, f16[64,2048]{1,0:T(8,128)(2,1)S(1)}, u32[]{:S(2)}, u32[]{:S(2)}) collective-permute-start(f16[64,2048]{1,0:T(8,128)(2,1)S(1)} %multiply_convert_fusion.7), channel_id=1, source_target_pairs={{0,2},{1,3},{2,0},{3,1},{4,6},{5,7},{6,4},{7,5},{8,10},{9,11},{10,... | collective-permute-start | bytes 786440 | tf_op jit(solution)/shard_map/ppermute | solution.py:173
  13.5 10.5 %collective-permute-start.4 = (f16[32,4096]{1,0:T(8,128)(2,1)S(1)}, f16[32,4096]{1,0:T(8,128)(2,1)S(1)}, u32[]{:S(2)}, u32[]{:S(2)}) collective-permute-start(f16[32,4096]{1,0:T(8,128)(2,1)S(1)} %multiply_convert_fusion.6), channel_id=1, source_target_pairs={{0,4},{1,5},{2,6},{3,7},{4,0},{5,1},{6,2},{7,3},{8,12},{9,13},{10,... | collective-permute-start | bytes 786440 | tf_op jit(solution)/shard_map/ppermute | solution.py:173
  22.4 5.2 %collective-permute-start.3 = (f16[32,2048]{1,0:T(8,128)(2,1)S(1)}, f16[32,2048]{1,0:T(8,128)(2,1)S(1)}, u32[]{:S(2)}, u32[]{:S(2)}) collective-permute-start(f16[32,2048]{1,0:T(8,128)(2,1)S(1)} %multiply_convert_fusion.11), channel_id=1, source_target_pairs={{0,4},{1,5},{2,6},{3,7},{4,0},{5,1},{6,2},{7,3},{8,12},{9,13},{10,... | collective-permute-start | bytes 393224 | tf_op jit(solution)/shard_map/ppermute | solution.py:173
  24.2 6.5 %collective-permute-start.5 = (f16[32,2048]{1,0:T(8,128)(2,1)S(1)}, f16[32,2048]{1,0:T(8,128)(2,1)S(1)}, u32[]{:S(2)}, u32[]{:S(2)}) collective-permute-start(f16[32,2048]{1,0:T(8,128)(2,1)S(1)} %multiply_convert_fusion.10), channel_id=1, source_target_pairs={{0,2},{1,3},{2,0},{3,1},{4,6},{5,7},{6,4},{7,5},{8,10},{9,11},{10,... | collective-permute-start | bytes 393224 | tf_op jit(solution)/shard_map/ppermute | solution.py:173
  24.8 9.9 %collective-permute-start.7 = (f16[64,2048]{1,0:T(8,128)(2,1)S(1)}, f16[64,2048]{1,0:T(8,128)(2,1)S(1)}, u32[]{:S(2)}, u32[]{:S(2)}) collective-permute-start(f16[64,2048]{1,0:T(8,128)(2,1)S(1)} %multiply_convert_fusion.5), channel_id=1, source_target_pairs={{0,2},{1,3},{2,0},{3,1},{4,6},{5,7},{6,4},{7,5},{8,10},{9,11},{10,... | collective-permute-start | bytes 786440 | tf_op jit(solution)/shard_map/ppermute | solution.py:173
  26.3 11.3 %collective-permute-start.9 = (f16[32,4096]{1,0:T(8,128)(2,1)S(1)}, f16[32,4096]{1,0:T(8,128)(2,1)S(1)}, u32[]{:S(2)}, u32[]{:S(2)}) collective-permute-start(f16[32,4096]{1,0:T(8,128)(2,1)S(1)} %multiply_convert_fusion.4), channel_id=1, source_target_pairs={{0,4},{1,5},{2,6},{3,7},{4,0},{5,1},{6,2},{7,3},{8,12},{9,13},{10,... | collective-permute-start | bytes 786440 | tf_op jit(solution)/shard_map/ppermute | solution.py:173
  31.0 13.9 %collective-permute-start.11 = (f16[2,32,2048]{2,1,0:T(8,128)(2,1)S(1)}, f16[2,32,2048]{2,1,0:T(8,128)(2,1)S(1)}, u32[]{:S(2)}, u32[]{:S(2)}) collective-permute-start(f16[2,32,2048]{2,1,0:T(8,128)(2,1)S(1)} %get-tuple-element.86), channel_id=1, source_target_pairs={{0,8},{1,9},{2,10},{3,11},{4,12},{5,13},{6,14},{7,15},{8,0},{9,1},... | collective-permute-start | bytes 786440 | tf_op jit(solution)/shard_map/ppermute | solution.py:173
  35.0 6.3 %collective-permute-start.8 = (f16[32,2048]{1,0:T(8,128)(2,1)S(1)}, f16[32,2048]{1,0:T(8,128)(2,1)S(1)}, u32[]{:S(2)}, u32[]{:S(2)}) collective-permute-start(f16[32,2048]{1,0:T(8,128)(2,1)S(1)} %multiply_convert_fusion.9), channel_id=1, source_target_pairs={{0,4},{1,5},{2,6},{3,7},{4,0},{5,1},{6,2},{7,3},{8,12},{9,13},{10,... | collective-permute-start | bytes 393224 | tf_op jit(solution)/shard_map/ppermute | solution.py:173
  37.9 5.0 %collective-permute-start.10 = (f16[32,2048]{1,0:T(8,128)(2,1)S(1)}, f16[32,2048]{1,0:T(8,128)(2,1)S(1)}, u32[]{:S(2)}, u32[]{:S(2)}) collective-permute-start(f16[32,2048]{1,0:T(8,128)(2,1)S(1)} %multiply_convert_fusion.8), channel_id=1, source_target_pairs={{0,2},{1,3},{2,0},{3,1},{4,6},{5,7},{6,4},{7,5},{8,10},{9,11},{10,... | collective-permute-start | bytes 393224 | tf_op jit(solution)/shard_map/ppermute | solution.py:173
  43.1 11.9 %collective-permute-start.17 = (f16[2,32,2048]{2,1,0:T(8,128)(2,1)S(1)}, f16[2,32,2048]{2,1,0:T(8,128)(2,1)S(1)}, u32[]{:S(2)}, u32[]{:S(2)}) collective-permute-start(f16[2,32,2048]{2,1,0:T(8,128)(2,1)S(1)} %multiply_convert_fusion.3), channel_id=1, source_target_pairs={{0,8},{1,9},{2,10},{3,11},{4,12},{5,13},{6,14},{7,15},{8,0},{9,1},... | collective-permute-start | bytes 786440 | tf_op jit(solution)/shard_map/ppermute | solution.py:173
  44.9 11.0 %collective-permute-start.12 = (bf16[2,32,2048]{2,1,0:T(8,128)(2,1)S(1)}, bf16[2,32,2048]{2,1,0:T(8,128)(2,1)S(1)}, u32[]{:S(2)}, u32[]{:S(2)}) collective-permute-start(bf16[2,32,2048]{2,1,0:T(8,128)(2,1)S(1)} %add_convert_fusion.1), channel_id=1, source_target_pairs={{0,4},{1,5},{2,6},{3,7},{4,0},{5,1},{6,2},{7,3},{8,12},{9,13},{10,... | collective-permute-start | bytes 786440 | tf_op jit(solution)/shard_map/ppermute | solution.py:173
  46.2 13.5 %collective-permute-start.14 = (bf16[160,2048]{1,0:T(8,128)(2,1)S(1)}, bf16[160,2048]{1,0:T(8,128)(2,1)S(1)}, u32[]{:S(2)}, u32[]{:S(2)}) collective-permute-start(bf16[160,2048]{1,0:T(8,128)(2,1)S(1)} %constant_dynamic-slice_fusion.3), channel_id=1, source_target_pairs={{0,2},{1,3},{2,0},{3,1},{4,6},{5,7},{6,4},{7,5},{8,10},{9,11},{10,... | collective-permute-start | bytes 1966088 | tf_op jit(solution)/shard_map/ppermute | solution.py:173
  46.3 14.1 %collective-permute-start.15 = (bf16[96,2048]{1,0:T(8,128)(2,1)S(1)}, bf16[96,2048]{1,0:T(8,128)(2,1)S(1)}, u32[]{:S(2)}, u32[]{:S(2)}) collective-permute-start(bf16[96,2048]{1,0:T(8,128)(2,1)S(1)} %collective-permute-done.13), channel_id=1, source_target_pairs={{0,1},{1,0},{2,3},{3,2},{4,5},{5,4},{6,7},{7,6},{8,9},{9,8},{10,11... | collective-permute-start | bytes 1179656 | tf_op jit(solution)/shard_map/ppermute | solution.py:173
  55.0 7.5 %collective-permute-start.18 = (bf16[2,32,2048]{2,1,0:T(8,128)(2,1)S(1)}, bf16[2,32,2048]{2,1,0:T(8,128)(2,1)S(1)}, u32[]{:S(2)}, u32[]{:S(2)}) collective-permute-start(bf16[2,32,2048]{2,1,0:T(8,128)(2,1)S(1)} %add_convert_fusion), channel_id=1, source_target_pairs={{0,4},{1,5},{2,6},{3,7},{4,0},{5,1},{6,2},{7,3},{8,12},{9,13},{10,... | collective-permute-start | bytes 786440 | tf_op jit(solution)/shard_map/ppermute | solution.py:173
  59.7 2.1 %collective-permute-start.16 = (bf16[160,2048]{1,0:T(8,128)(2,1)S(1)}, bf16[160,2048]{1,0:T(8,128)(2,1)S(1)}, u32[]{:S(2)}, u32[]{:S(2)}) collective-permute-start(bf16[160,2048]{1,0:T(8,128)(2,1)S(1)} %collective-permute-done.14), channel_id=1, source_target_pairs={{0,1},{1,0},{2,3},{3,2},{4,5},{5,4},{6,7},{7,6},{8,9},{9,8},{10,11... | collective-permute-start | bytes 1966088 | tf_op jit(solution)/shard_map/ppermute | solution.py:173
  63.4 0.8 copy-start.1
  64.1 5.5 %copy-start.2 = (s32[8,12]{1,0:T(8,128)S(1)}, s32[8,12]{1,0:T(8,128)}, u32[]{:S(2)}) copy-start(s32[8,12]{1,0:T(8,128)} %param.11) | copy-start | bytes 1156
  64.2 6.2 %copy-start.3 = (s32[8]{0:T(128)S(1)}, s32[8]{0:T(128)}, u32[]{:S(2)}) copy-start(s32[8]{0:T(128)} %param.12) | copy-start | bytes 100
  64.2 6.3 %copy-start.4 = (s32[512]{0:T(512)S(1)}, s32[512]{0:T(512)}, u32[]{:S(2)}) copy-start(s32[512]{0:T(512)} %param.10) | copy-start | bytes 6148
  66.1 18.0 %all-to-all-start = ((bf16[16,1,64,256]{3,2,1,0:T(8,128)(2,1)}), bf16[16,1,64,256]{3,2,1,0:T(8,128)(2,1)S(1)}, u32[]{:S(2)}, u32[]{:S(2)}) async-start(bf16[16,1,64,256]{3,2,1,0:T(8,128)(2,1)} %bitcast.10), calls=%async_computation | async-start | bytes 1048576 | tf_op jit(solution)/shard_map/all_to_all | solution.py:296

commit v15 on v14

--- a/solution.py
+++ b/solution.py
@@ -8,10 +8,11 @@
 CORES = 2
 CHUNKS = 2
 PATHS = 2
-UNIT = 4.0
+TOP = 15.0
+LEAST = -100.0
 LANES = 128
-OTHER_VMEM = 44
-MINE_VMEM = 16
+LOAD_VMEM = 48
+PRODUCT_VMEM = 16
 
 
 def listed_mask(query_cluster, cand_blocks, cand_count, nblocks):
@@ -41,9 +42,8 @@
         out_ref[:, columns] = result[chunk * part:(chunk + 1) * part]
 
 
-def other_kernel(core_ref, rows_ref, columns_hbm, *refs):
-    outs, (high_ref, low_ref, columns_ref, sems) = refs[:-4], refs[-4:]
-    steps, _, block = columns_ref.shape
+def load_kernel(rows_ref, columns_hbm, high_ref, low_ref, power_ref, columns_ref, sems):
+    steps, depth, block = columns_ref.shape
 
     def load(i):
         return pltpu.make_async_copy(
@@ -52,17 +52,42 @@
 
     for i in range(steps):
         load(i).start()
-    left = rows_of(core_ref, rows_ref)
+    rows_peak = jnp.max(jnp.abs(rows_ref[:, :depth].astype(jnp.float32)), axis=0, keepdims=True)
+    peak = jnp.zeros((1, block), jnp.float32)
     for i in range(steps):
         load(i).wait()
-        columns = slice(i * block, (i + 1) * block)
-        high, low = split(columns_ref[i])
-        high_ref[:, columns] = high
-        low_ref[:, columns] = low
-        multiply(left, high, low, outs, columns)
-
-
-def mine_kernel(core_ref, rows_ref, high_ref, low_ref, *outs):
+        columns = columns_ref[i]
+        peak = jnp.maximum(peak, jnp.max(jnp.abs(columns), axis=0, keepdims=True))
+        high, low = split(columns)
+        high_ref[:, i * block:(i + 1) * block] = high
+        low_ref[:, i * block:(i + 1) * block] = low
+    bound = 1.02 * depth * jnp.max(rows_peak, axis=1, keepdims=True) * jnp.max(peak, axis=1, keepdims=True)
+    power = jnp.maximum(jnp.ceil(jnp.log2(bound)), LEAST)
+    power_ref[...] = jnp.broadcast_to(power, power_ref.shape)
+
+
+def load_columns(rows, columns):
+    depth, width = columns.shape
+    block = min(512, width)
+    in_vmem = pl.BlockSpec(memory_space=pltpu.VMEM)
+    return pl.pallas_call(
+        load_kernel,
+        in_specs=[in_vmem, pl.BlockSpec(memory_space=pltpu.HBM)],
+        out_specs=[in_vmem] * 3,
+        out_shape=[jax.ShapeDtypeStruct((depth, width), jnp.bfloat16)] * 2
+        + [jax.ShapeDtypeStruct((1, width), jnp.float32)],
+        scratch_shapes=[
+            pltpu.VMEM((width // block, depth, block), jnp.float32),
+            pltpu.SemaphoreType.DMA((width // block,)),
+        ],
+        compiler_params=pltpu.CompilerParams(vmem_limit_bytes=LOAD_VMEM * 1024 * 1024),
+        cost_estimate=pl.CostEstimate(
+            flops=4 * depth * width, bytes_accessed=4 * depth * width, transcendentals=0
+        ),
+    )(rows, columns)
+
+
+def product_kernel(core_ref, rows_ref, high_ref, low_ref, *outs):
     left = rows_of(core_ref, rows_ref)
     width = high_ref.shape[1]
     block = min(512, width)
@@ -71,34 +96,23 @@
         multiply(left, high_ref[:, columns], low_ref[:, columns], outs, columns)
 
 
-def product(core, rows, columns, kernel, vmem):
+def product(core, rows, high, low):
     nrows = rows.shape[0]
-    depth, width = columns[0].shape
-    block = min(512, width)
+    depth, width = high.shape
     part = nrows // CORES // CHUNKS
-    out = [jax.ShapeDtypeStruct((part, width), jnp.float32)] * CHUNKS
     in_vmem = pl.BlockSpec(memory_space=pltpu.VMEM)
-    operand, scratch = in_vmem, []
-    if kernel is other_kernel:
-        out = out + [jax.ShapeDtypeStruct((depth, width), jnp.bfloat16)] * 2
-        operand = pl.BlockSpec(memory_space=pltpu.HBM)
-        scratch = [
-            pltpu.VMEM((width // block, depth, block), jnp.float32),
-            pltpu.SemaphoreType.DMA((width // block,)),
-        ]
     return pl.pallas_call(
-        kernel,
-        in_specs=[pl.BlockSpec(memory_space=pltpu.SMEM), in_vmem] + [operand] * len(columns),
-        out_specs=[in_vmem] * len(out),
-        out_shape=out,
-        scratch_shapes=scratch,
-        compiler_params=pltpu.CompilerParams(vmem_limit_bytes=vmem * 1024 * 1024),
+        product_kernel,
+        in_specs=[pl.BlockSpec(memory_space=pltpu.SMEM)] + [in_vmem] * 3,
+        out_specs=[in_vmem] * CHUNKS,
+        out_shape=[jax.ShapeDtypeStruct((part, width), jnp.float32)] * CHUNKS,
+        compiler_params=pltpu.CompilerParams(vmem_limit_bytes=PRODUCT_VMEM * 1024 * 1024),
         cost_estimate=pl.CostEstimate(
             flops=3 * nrows * depth * width,
             bytes_accessed=4 * width * depth + 2 * width * nrows,
             transcendentals=0,
         ),
-    )(core.reshape(1), rows, *columns)
+    )(core.reshape(1), rows, high, low)
 
 
 def order_kernel(slots_ref, *refs):
@@ -186,11 +200,14 @@
     scalars, queries, train = lax.optimization_barrier((scalars, queries, train))
     core, other_core, first_slot, offsets, first_half = scalars
 
-    def pack(value):
-        return (value * UNIT).astype(jnp.float16)
-
-    def unpack(value):
-        return value.astype(jnp.float32) * (1.0 / UNIT)
+    def pack(value, power):
+        return (value * jnp.exp2(TOP - power[:, :value.shape[-1]])).astype(jnp.float16)
+
+    def unpack(got, power):
+        return got.astype(jnp.float32) * jnp.exp2(power[:, :got.shape[-1]] - TOP)
+
+    def agree(power, bit, added):
+        return jnp.maximum(power, swap(power, bit)) + added
 
     def part(value, bit, axis, other=0):
         shape = list(value.shape)
@@ -199,11 +216,11 @@
         starts[axis] = offsets[bit, shape[axis]][other]
         return lax.dynamic_slice(value, starts, shape, allow_negative_indices=False)
 
-    def give(value, bit, axis):
-        return pack(part(value, bit, axis, 1))
-
-    def keep(value, got, bit, axis):
-        return part(value, bit, axis) + unpack(got)
+    def give(value, power, bit, axis):
+        return pack(part(value, bit, axis, 1), power)
+
+    def keep(value, got, power, bit, axis):
+        return part(value, bit, axis) + unpack(got, power)
 
     def join(own, got, bit):
         mine_first = jnp.concatenate([own, got], axis=1)
@@ -212,24 +229,30 @@
     def after(value, first):
         return lax.optimization_barrier((value, first))[0]
 
-    def paths(value, other):
-        value = value + unpack(other)
+    def paths(value, got, power):
+        value = value + unpack(got, power)
         return [value[i * rows:(i + 1) * rows] for i in range(PATHS)]
 
     levels = ((ybit, 1), (zbit, 0)), ((zbit, 0), (ybit, 1))
 
-    def messages(values, step):
-        return [give(value, *level[step]) for value, level in zip(values, levels)]
-
-    def exchange(values, sent, step):
+    def messages(values, powers, step):
+        return [give(value, power, *level[step]) for value, power, level in zip(values, powers, levels)]
+
+    def exchange(values, sent, powers, step):
         got = [swap(message, level[step][0]) for message, level in zip(sent, levels)]
-        return [keep(value, message, *level[step]) for value, message, level in zip(values, got, levels)]
-
-    def halve(values):
+        return [
+            keep(value, message, power, *level[step])
+            for value, message, power, level in zip(values, got, powers, levels)
+        ]
+
+    def halve(values, powers):
         value = jnp.stack(values)
-        for bit in rest[:-1]:
-            value = keep(value, swap(give(value, bit, 1), bit), bit, 1)
+        for bit, power in zip(rest[:-1], powers):
+            value = keep(value, swap(give(value, power, bit, 1), bit), power, bit, 1)
         return value
+
+    def total(value, got, power):
+        return (value + unpack(got, power)).astype(jnp.bfloat16)
 
     def gather(value, first=None):
         for bit in reversed([zbit] + rest[:-1]):
@@ -243,7 +266,7 @@
         return lax.dot_general(group, value, (((1,), (1,)), ((), ())), preferred_element_type=jnp.float32)
 
     blocks = train.reshape(examples * nblocks, width)
-    total = examples * nblocks
+    every = examples * nblocks
     middle = max(1, examples * 3 // 8) * nblocks
 
     def features(blocks, first, count, other):
@@ -259,37 +282,46 @@
     other_core, blocks = after((other_core, blocks), early)
     early = swap(early, ybit)
 
-    *full, high, low = product(other_core, left, [precond], other_kernel, OTHER_VMEM)
-    sent = [pack(value) for value in full]
+    high, low, power = load_columns(after(left, other_core), precond)
+    first_power = agree(power, 0, 0.0)
+    full = product(other_core, left, high, low)
+    sent = [pack(value, first_power) for value in full]
     got = [swap(value, 0) for value in sent]
     blocks = after(blocks, sent)
-    near = features(blocks, 0, total, 0)
+    near = features(blocks, 0, every, 0)
     sibling = swap(near, 0)
-    mine = product(after(core, sent), left, [high, low], mine_kernel, MINE_VMEM)
-    one = paths(mine[0], got[0])
-    sent = messages(one, 0)
-    two = paths(mine[1], after(got[1], sent))
-    one = exchange(one, sent, 0)
-    sent = messages(one, 1)
-    sent_two = after(messages(two, 0), (sent, sibling))
-    one = halve(exchange(one, sent, 1))
-    sent = pack(one)
+    power = after(first_power, sent)
+    powers = [[agree(power, level[0][0], 1.0) for level in levels]]
+    mine = product(after(core, sent), left, high, low)
+    one = paths(mine[0], got[0], first_power)
+    sent = messages(one, powers[0], 0)
+    power = agree(after(powers[0][0], sent), levels[0][1][0], 1.0)
+    powers.append([power] * PATHS)
+    rest_powers = []
+    for bit in rest:
+        power = agree(power, bit, 1.0)
+        rest_powers.append(power)
+    two = paths(mine[1], after(got[1], sent), first_power)
+    one = exchange(one, sent, powers[0], 0)
+    sent = after(messages(one, powers[1], 1), (rest_powers, early))
+    sent_two = after(messages(two, powers[0], 0), (sent, sibling))
+    one = halve(exchange(one, sent, powers[1], 1), rest_powers)
+    sent = pack(one, power)
     got_one = swap(sent, rest[-1])
-    two = exchange(two, sent_two, 0)
-    two = exchange(two, messages(two, 1), 1)
-    two = halve(two)
-    sent = pack(two)
-    one = (after(one, sent) + unpack(got_one)).astype(jnp.bfloat16)
+    two = exchange(two, sent_two, powers[0], 0)
+    two = halve(exchange(two, after(messages(two, powers[1], 1), sent), powers[1], 1), rest_powers)
+    one = total(one, got_one, power)
+    sent = after(pack(two, power), one)
     got_two = swap(sent, rest[-1])
     blocks, early = after((blocks, early), one)
-    late = swap(features(blocks, middle, total - middle, 1), ybit)
+    late = swap(features(blocks, middle, every - middle, 1), ybit)
     one = gather(one)
     groups = [
         jnp.concatenate([near, sibling], axis=0),
         jnp.concatenate([early, late, swap(early, 0), swap(late, 0)], axis=0),
     ]
     raws = [scores(group, one) for group in groups]
-    two = gather((two + unpack(got_two)).astype(jnp.bfloat16), raws)
+    two = gather(total(two, got_two, power), raws)
     raws = raws + [scores(group, two) for group in groups]
 
     ordered = in_slot_order(raws, slot_block).reshape(n, owned, 2 * CORES * examples, nq // CORES)

time: 85.2 us -> 99.6 us (1.17)
  waiting for transfers between devices: 44.1 us -> 55.3 us
  starting transfers between devices: 20.4 us -> 23.5 us
    ppermute x19 -> x24, waiting for transfers between devices: 31.5 us -> 42.6 us  [swap(): return lax.ppermute(value, 'rows', [(r, r ^ 1 << bit) for r in range(n)])]
    ppermute x19 -> x24, starting transfers between devices: 16.9 us -> 19.3 us  [swap(): return lax.ppermute(value, 'rows', [(r, r ^ 1 << bit) for r in range(n)])]
    pallas_call x2 -> x3, Pallas kernels: 6.03 us -> 5.98 us  [the longest x2 3.58 us: product(): pl.pallas_call(product_kernel, in_specs=[pl.BlockSpec(memory_space=pltpu....]
  transfers between devices with their start and end apart: 20 -> 25, of which waited for: 12 -> 12; matrix products, arithmetic and copies ran while one was open for 9% -> 8% of each run, Pallas kernels for 7% -> 6%
where the time goes in v15:
time: 99.6 us; the launch traced here: 99.3 us
  waiting for transfers between devices  55.3 us (56%)
  starting transfers between devices  23.5 us (24%)
  Pallas kernels  8.73 us (9%)
  other arithmetic  4.95 us (5%)
  matrix products  3.15 us (3%)
  local copies, waits for them, and re-layouts  3.13 us (3%)
    ppermute x24, waiting for transfers between devices, swap(): return lax.ppermute(value, 'rows', [(r, r ^ 1 << bit) for r in range(n)])  42.6 us
    ppermute x24, starting transfers between devices, swap(): return lax.ppermute(value, 'rows', [(r, r ^ 1 << bit) for r in range(n)])  19.3 us
    all_to_all x1, waiting for transfers between devices, shards(): lax.all_to_all(ordered, 'rows', split_axis=0, concat_axis=0, tiled=True)  12.8 us
    all_to_all x1, starting transfers between devices, shards(): lax.all_to_all(ordered, 'rows', split_axis=0, concat_axis=0, tiled=True)  4.23 us
    pallas_call x2, Pallas kernels, product(): pl.pallas_call(product_kernel, in_specs=[pl.BlockSpec(memory_space=pltpu....  3.58 us
    dot_general x4, matrix products, scores(): lax.dot_general(group, value, (((1,), (1,)), ((), ())), preferred_element...  2.89 us
    pallas_call x1, Pallas kernels, load_columns(): pl.pallas_call(load_kernel, in_specs=[in_vmem, pl.BlockSpec(memory_space=...  2.4 us
  transfers between devices with their start and end apart: 25, of which 12 were waited for; matrix products, arithmetic and copies ran while one was open for 8% of the time, Pallas kernels for 6%

profile of v15, /device:TPU:0, one launch (start us, length us, event | category | flops | bytes accessed | tf_op | source)
XLA Modules:
  0.0 99.3 jit_solution(5406735540098845017)
XLA Ops:
  0.0 1.3 %fusion.2 = (bf16[512,256]{1,0:T(8,128)(2,1)S(1)}, bf16[512,256]{1,0:T(8,128)(2,1)S(1)}) fusion(f32[512,256]{1,0:T(8,128)} %param.7), kind=kLoop, calls=%fused_computation.10 | loop fusion | flops 524288 | bytes 1048576 | tf_op jit(solution)/shard_map/convert_element_type | solution.py:277
  1.3 0.4 copy-done
  1.9 3.0 %collective-permute-start.9 = (bf16[96,2048]{1,0:T(8,128)(2,1)S(1)}, bf16[96,2048]{1,0:T(8,128)(2,1)S(1)}, u32[]{:S(2)}, u32[]{:S(2)}) collective-permute-start(bf16[96,2048]{1,0:T(8,128)(2,1)S(1)} %constant_dynamic-slice_fusion.2), channel_id=1, source_target_pairs={{0,2},{1,3},{2,0},{3,1},{4,6},{5,7},{6,4},{7,5},{8,10},{9,11},{10,... | collective-permute-start | bytes 1179656 | tf_op jit(solution)/shard_map/ppermute | solution.py:187
  5.0 2.4 %shard_map.73 = (bf16[256,4096]{1,0:T(8,128)(2,1)S(1)}, bf16[256,4096]{1,0:T(8,128)(2,1)S(1)}, f32[1,4096]{1,0:T(1,128)S(1)}) custom-call(bf16[512,768]{1,0:T(8,128)(2,1)S(1)} %pad_maximum_fusion.3.rows_ref, f32[256,4096]{1,0:T(8,128)} %columns_hbm.1), custom_call_target="tpu_custom_call" | custom-call | flops 4194304 | bytes 4194304 | tf_op jit(solution)/shard_map/pallas_call | solution.py:73
  7.5 1.8 %shard_map.74 = (f32[128,4096]{1,0:T(8,128)S(1)}, f32[128,4096]{1,0:T(8,128)S(1)}) custom-call(s32[1]{0:T(128)} %bitcast.1.core_ref, bf16[512,768]{1,0:T(8,128)(2,1)S(1)} %pad_maximum_fusion.3.rows_ref, bf16[256,4096]{1,0:T(8,128)(2,1)S(1)} %get-tuple-element.54.high_ref, bf16[256,4096]{1,0:T(8,128)(2,1)S(1)} %get-tuple-element.55.low_ref), custom_call_target="tpu_custom_call" | custom-call | flops 1610612736 | bytes 8388608 | tf_op jit(solution)/shard_map/pallas_call | solution.py:104
  9.4 0.4 multiply_convert_fusion
  9.7 1.6 %collective-permute-start.5 = (f32[1,4096]{1,0:T(1,128)S(1)}, f32[1,4096]{1,0:T(1,128)S(1)}, u32[]{:S(2)}, u32[]{:S(2)}) collective-permute-start(f32[1,4096]{1,0:T(1,128)S(1)} %get-tuple-element.65), channel_id=1, source_target_pairs={{0,4},{1,5},{2,6},{3,7},{4,0},{5,1},{6,2},{7,3},{8,12},{9,13},{10,... | collective-permute-start | bytes 49160 | tf_op jit(solution)/shard_map/ppermute | solution.py:187
  11.4 0.5 collective-permute-start.3
  11.9 0.5 collective-permute-start.2
  12.4 0.4 constant_dynamic-slice_fusion.1
  12.8 1.8 %shard_map.75 = (f32[128,4096]{1,0:T(8,128)S(1)}, f32[128,4096]{1,0:T(8,128)S(1)}) custom-call(s32[1]{0:T(128)} %bitcast.3.core_ref, bf16[512,768]{1,0:T(8,128)(2,1)S(1)} %pad_maximum_fusion.3.rows_ref, bf16[256,4096]{1,0:T(8,128)(2,1)S(1)} %get-tuple-element.54.high_ref, bf16[256,4096]{1,0:T(8,128)(2,1)S(1)} %get-tuple-element.55.low_ref), custom_call_target="tpu_custom_call" | custom-call | flops 1610612736 | bytes 8388608 | tf_op jit(solution)/shard_map/pallas_call | solution.py:104
  14.7 0.4 collective-permute-done.3
  15.2 0.8 collective-permute-done.2
  16.0 0.3 multiply_add_fusion.1
  16.7 1.6 %collective-permute-start.4 = (f16[64,2048]{1,0:T(8,128)(2,1)S(1)}, f16[64,2048]{1,0:T(8,128)(2,1)S(1)}, u32[]{:S(2)}, u32[]{:S(2)}) collective-permute-start(f16[64,2048]{1,0:T(8,128)(2,1)S(1)} %multiply_convert_fusion.7), channel_id=1, source_target_pairs={{0,2},{1,3},{2,0},{3,1},{4,6},{5,7},{6,4},{7,5},{8,10},{9,11},{10,... | collective-permute-start | bytes 786440 | tf_op jit(solution)/shard_map/ppermute | solution.py:187
  18.4 0.5 collective-permute-start.7
  18.9 0.3 multiply_add_fusion
  19.5 1.6 %collective-permute-start.6 = (f32[1,4096]{1,0:T(1,128)S(1)}, f32[1,4096]{1,0:T(1,128)S(1)}, u32[]{:S(2)}, u32[]{:S(2)}) collective-permute-start(f32[1,4096]{1,0:T(1,128)S(1)} %get-tuple-element.68), channel_id=1, source_target_pairs={{0,4},{1,5},{2,6},{3,7},{4,0},{5,1},{6,2},{7,3},{8,12},{9,13},{10,... | collective-permute-start | bytes 49160 | tf_op jit(solution)/shard_map/ppermute | solution.py:187
  21.4 5.5 %collective-permute-done.6 = f32[1,4096]{1,0:T(1,128)S(1)} collective-permute-done((f32[1,4096]{1,0:T(1,128)S(1)}, f32[1,4096]{1,0:T(1,128)S(1)}, u32[]{:S(2)}, u32[]{:S(2)}) %collective-permute-start.6) | collective-permute-done | bytes 16416 | tf_op jit(solution)/shard_map/ppermute | solution.py:187
  26.9 2.7 %collective-permute-start.8 = (f32[1,4096]{1,0:T(1,128)S(1)}, f32[1,4096]{1,0:T(1,128)S(1)}, u32[]{:S(2)}, u32[]{:S(2)}) collective-permute-start(f32[1,4096]{1,0:T(1,128)S(1)} %maximum_add_fusion.1), channel_id=1, source_target_pairs={{0,8},{1,9},{2,10},{3,11},{4,12},{5,13},{6,14},{7,15},{8,0},{9,1},... | collective-permute-start | bytes 49160 | tf_op jit(solution)/shard_map/ppermute | solution.py:187
  29.6 2.1 %collective-permute-done.8 = f32[1,4096]{1,0:T(1,128)S(1)} collective-permute-done((f32[1,4096]{1,0:T(1,128)S(1)}, f32[1,4096]{1,0:T(1,128)S(1)}, u32[]{:S(2)}, u32[]{:S(2)}) %collective-permute-start.8) | collective-permute-done | bytes 16416 | tf_op jit(solution)/shard_map/ppermute | solution.py:187
  31.8 0.2 multiply_add_fusion.5
  32.2 0.5 collective-permute-start.10
  32.7 0.3 collective-permute-start.11
  33.1 1.8 %collective-permute-start.18 = (f16[64,2048]{1,0:T(8,128)(2,1)S(1)}, f16[64,2048]{1,0:T(8,128)(2,1)S(1)}, u32[]{:S(2)}, u32[]{:S(2)}) collective-permute-start(f16[64,2048]{1,0:T(8,128)(2,1)S(1)} %multiply_convert_fusion.4), channel_id=1, source_target_pairs={{0,2},{1,3},{2,0},{3,1},{4,6},{5,7},{6,4},{7,5},{8,10},{9,11},{10,... | collective-permute-start | bytes 786440 | tf_op jit(solution)/shard_map/ppermute | solution.py:187
  34.8 1.6 %collective-permute-start.19 = (f16[32,4096]{1,0:T(8,128)(2,1)S(1)}, f16[32,4096]{1,0:T(8,128)(2,1)S(1)}, u32[]{:S(2)}, u32[]{:S(2)}) collective-permute-start(f16[32,4096]{1,0:T(8,128)(2,1)S(1)} %multiply_convert_fusion.3), channel_id=1, source_target_pairs={{0,4},{1,5},{2,6},{3,7},{4,0},{5,1},{6,2},{7,3},{8,12},{9,13},{10,... | collective-permute-start | bytes 786440 | tf_op jit(solution)/shard_map/ppermute | solution.py:187
  36.4 5.0 %collective-permute-done.10 = f16[32,2048]{1,0:T(8,128)(2,1)S(1)} collective-permute-done((f16[32,2048]{1,0:T(8,128)(2,1)S(1)}, f16[32,2048]{1,0:T(8,128)(2,1)S(1)}, u32[]{:S(2)}, u32[]{:S(2)}) %collective-permute-start.10) | collective-permute-done | bytes 131104 | tf_op jit(solution)/shard_map/ppermute | solution.py:187
  42.0 2.3 %collective-permute-done.19 = f16[32,4096]{1,0:T(8,128)(2,1)S(1)} collective-permute-done((f16[32,4096]{1,0:T(8,128)(2,1)S(1)}, f16[32,4096]{1,0:T(8,128)(2,1)S(1)}, u32[]{:S(2)}, u32[]{:S(2)}) %collective-permute-start.19) | collective-permute-done | bytes 262176 | tf_op jit(solution)/shard_map/ppermute | solution.py:187
  44.5 1.5 %collective-permute-start.20 = (f16[32,2048]{1,0:T(8,128)(2,1)S(1)}, f16[32,2048]{1,0:T(8,128)(2,1)S(1)}, u32[]{:S(2)}, u32[]{:S(2)}) collective-permute-start(f16[32,2048]{1,0:T(8,128)(2,1)S(1)} %get-tuple-element.77), channel_id=1, source_target_pairs={{0,4},{1,5},{2,6},{3,7},{4,0},{5,1},{6,2},{7,3},{8,12},{9,13},{10,... | collective-permute-start | bytes 393224 | tf_op jit(solution)/shard_map/ppermute | solution.py:187
  46.0 0.4 collective-permute-start.21
  46.5 5.8 %collective-permute-done.12 = f16[2,32,2048]{2,1,0:T(8,128)(2,1)S(1)} collective-permute-done((f16[2,32,2048]{2,1,0:T(8,128)(2,1)S(1)}, f16[2,32,2048]{2,1,0:T(8,128)(2,1)S(1)}, u32[]{:S(2)}, u32[]{:S(2)}) %collective-permute-start.12) | collective-permute-done | bytes 262176 | tf_op jit(solution)/shard_map/ppermute | solution.py:187
  52.4 3.1 %collective-permute-done.20 = f16[32,2048]{1,0:T(8,128)(2,1)S(1)} collective-permute-done((f16[32,2048]{1,0:T(8,128)(2,1)S(1)}, f16[32,2048]{1,0:T(8,128)(2,1)S(1)}, u32[]{:S(2)}, u32[]{:S(2)}) %collective-permute-start.20) | collective-permute-done | bytes 131104 | tf_op jit(solution)/shard_map/ppermute | solution.py:187
  55.9 0.3 constant_dynamic-slice_fusion.3
  56.2 0.5 collective-permute-start.14
  56.8 9.3 %collective-permute-done.22 = f16[2,32,2048]{2,1,0:T(8,128)(2,1)S(1)} collective-permute-done((f16[2,32,2048]{2,1,0:T(8,128)(2,1)S(1)}, f16[2,32,2048]{2,1,0:T(8,128)(2,1)S(1)}, u32[]{:S(2)}, u32[]{:S(2)}) %collective-permute-start.22) | collective-permute-done | bytes 262176 | tf_op jit(solution)/shard_map/ppermute | solution.py:187
  66.3 7.1 %collective-permute-done.14 = bf16[160,2048]{1,0:T(8,128)(2,1)S(1)} collective-permute-done((bf16[160,2048]{1,0:T(8,128)(2,1)S(1)}, bf16[160,2048]{1,0:T(8,128)(2,1)S(1)}, u32[]{:S(2)}, u32[]{:S(2)}) %collective-permute-start.14) | collective-permute-done | bytes 655392 | tf_op jit(solution)/shard_map/ppermute | solution.py:187
  73.4 0.7 fusion.1.refs_0_
  74.3 1.2 %collective-permute-done.16 = bf16[160,2048]{1,0:T(8,128)(2,1)S(1)} collective-permute-done((bf16[160,2048]{1,0:T(8,128)(2,1)S(1)}, bf16[160,2048]{1,0:T(8,128)(2,1)S(1)}, u32[]{:S(2)}, u32[]{:S(2)}) %collective-permute-start.16) | collective-permute-done | bytes 655392 | tf_op jit(solution)/shard_map/ppermute | solution.py:187
  75.6 0.7 fusion.12.refs_1_
  76.4 0.7 fusion.13.refs_3_
  77.1 0.7 fusion.refs_2_
  77.9 1.9 %shard_map.76 = bf16[16,64,256]{2,1,0:T(8,128)(2,1)} custom-call(s32[16]{0:T(128)S(1)} %copy-done.1, f32[512,128]{1,0:T(8,128)S(1)} %fusion.1.refs_0_, f32[512,128]{1,0:T(8,128)S(1)} %fusion.12.refs_1_, f32[512,128]{1,0:T(8,128)S(1)} %fusion.refs_2_, f32[512,128]{1,0:T(8,128)S(1)} %fusion.13.refs_3_), custom_call_target="tpu_custom_call" | custom-call | flops 65536 | bytes 1572864 | tf_op jit(solution)/shard_map/pallas_call | solution.py:136
  79.8 4.2 %all-to-all-start = ((bf16[16,1,64,256]{3,2,1,0:T(8,128)(2,1)}), bf16[16,1,64,256]{3,2,1,0:T(8,128)(2,1)S(1)}, u32[]{:S(2)}, u32[]{:S(2)}) async-start(bf16[16,1,64,256]{3,2,1,0:T(8,128)(2,1)} %bitcast.20), calls=%async_computation | async-start | bytes 1048576 | tf_op jit(solution)/shard_map/all_to_all | solution.py:328
  84.1 0.6 dynamic_slice.79
  84.8 0.3 fusion.3
  85.1 0.6 constant_dynamic-slice_fusion.allowed_ref
  85.7 12.8 %all-to-all-done = bf16[16,1,64,256]{3,2,1,0:T(8,128)(2,1)S(1)} async-done(((bf16[16,1,64,256]{3,2,1,0:T(8,128)(2,1)}), bf16[16,1,64,256]{3,2,1,0:T(8,128)(2,1)S(1)}, u32[]{:S(2)}, u32[]{:S(2)}) %all-to-all-start) | async-done | bytes 524320 | tf_op jit(solution)/shard_map/all_to_all | solution.py:328
  98.5 0.9 shard_map.77
  (67 shorter events, 3.9 us)
Async XLA Ops:
  0.0 1.7 %copy-start = (bf16[16,16,4096]{2,1,0:T(8,128)(2,1)S(1)}, bf16[16,16,4096]{2,1,0:T(8,128)(2,1)}, u32[]{:S(2)}) copy-start(bf16[16,16,4096]{2,1,0:T(8,128)(2,1)} %param.9) | copy-start | bytes 6291460
  1.9 30.3 %collective-permute-start.9 = (bf16[96,2048]{1,0:T(8,128)(2,1)S(1)}, bf16[96,2048]{1,0:T(8,128)(2,1)S(1)}, u32[]{:S(2)}, u32[]{:S(2)}) collective-permute-start(bf16[96,2048]{1,0:T(8,128)(2,1)S(1)} %constant_dynamic-slice_fusion.2), channel_id=1, source_target_pairs={{0,2},{1,3},{2,0},{3,1},{4,6},{5,7},{6,4},{7,5},{8,10},{9,11},{10,... | collective-permute-start | bytes 1179656 | tf_op jit(solution)/shard_map/ppermute | solution.py:187
  7.4 1.9 %collective-permute-start = (f32[1,4096]{1,0:T(1,128)S(1)}, f32[1,4096]{1,0:T(1,128)S(1)}, u32[]{:S(2)}, u32[]{:S(2)}) collective-permute-start(f32[1,4096]{1,0:T(1,128)S(1)} %get-tuple-element.57), channel_id=1, source_target_pairs={{0,1},{1,0},{2,3},{3,2},{4,5},{5,4},{6,7},{7,6},{8,9},{9,8},{10,11... | collective-permute-start | bytes 49160 | tf_op jit(solution)/shard_map/ppermute | solution.py:187
  9.7 4.9 %collective-permute-start.5 = (f32[1,4096]{1,0:T(1,128)S(1)}, f32[1,4096]{1,0:T(1,128)S(1)}, u32[]{:S(2)}, u32[]{:S(2)}) collective-permute-start(f32[1,4096]{1,0:T(1,128)S(1)} %get-tuple-element.65), channel_id=1, source_target_pairs={{0,4},{1,5},{2,6},{3,7},{4,0},{5,1},{6,2},{7,3},{8,12},{9,13},{10,... | collective-permute-start | bytes 49160 | tf_op jit(solution)/shard_map/ppermute | solution.py:187
  11.4 3.7 %collective-permute-start.3 = (f32[1,4096]{1,0:T(1,128)S(1)}, f32[1,4096]{1,0:T(1,128)S(1)}, u32[]{:S(2)}, u32[]{:S(2)}) collective-permute-start(f32[1,4096]{1,0:T(1,128)S(1)} %get-tuple-element.65), channel_id=1, source_target_pairs={{0,2},{1,3},{2,0},{3,1},{4,6},{5,7},{6,4},{7,5},{8,10},{9,11},{10,... | collective-permute-start | bytes 49160 | tf_op jit(solution)/shard_map/ppermute | solution.py:187
  11.9 7.0 %collective-permute-start.17 = (f16[128,4096]{1,0:T(8,128)(2,1)S(1)}, f16[128,4096]{1,0:T(8,128)(2,1)S(1)}, u32[]{:S(2)}, u32[]{:S(2)}) collective-permute-start(f16[128,4096]{1,0:T(8,128)(2,1)S(1)} %get-tuple-element.115), channel_id=1, source_target_pairs={{0,1},{1,0},{2,3},{3,2},{4,5},{5,4},{6,7},{7,6},{8,9},{9,8},{10,11... | collective-permute-start | bytes 3145736 | tf_op jit(solution)/shard_map/ppermute | solution.py:187
  11.9 4.2 %collective-permute-start.2 = (f16[128,4096]{1,0:T(8,128)(2,1)S(1)}, f16[128,4096]{1,0:T(8,128)(2,1)S(1)}, u32[]{:S(2)}, u32[]{:S(2)}) collective-permute-start(f16[128,4096]{1,0:T(8,128)(2,1)S(1)} %get-tuple-element.116), channel_id=1, source_target_pairs={{0,1},{1,0},{2,3},{3,2},{4,5},{5,4},{6,7},{7,6},{8,9},{9,8},{10,11... | collective-permute-start | bytes 3145736 | tf_op jit(solution)/shard_map/ppermute | solution.py:187
  14.6 18.4 %collective-permute-start.1 = (bf16[256,2048]{1,0:T(8,128)(2,1)S(1)}, bf16[256,2048]{1,0:T(8,128)(2,1)S(1)}, u32[]{:S(2)}, u32[]{:S(2)}) collective-permute-start(bf16[256,2048]{1,0:T(8,128)(2,1)S(1)} %constant_dynamic-slice_fusion.1), channel_id=1, source_target_pairs={{0,1},{1,0},{2,3},{3,2},{4,5},{5,4},{6,7},{7,6},{8,9},{9,8},{10,11... | collective-permute-start | bytes 3145736 | tf_op jit(solution)/shard_map/ppermute | solution.py:187
  16.7 15.1 %collective-permute-start.4 = (f16[64,2048]{1,0:T(8,128)(2,1)S(1)}, f16[64,2048]{1,0:T(8,128)(2,1)S(1)}, u32[]{:S(2)}, u32[]{:S(2)}) collective-permute-start(f16[64,2048]{1,0:T(8,128)(2,1)S(1)} %multiply_convert_fusion.7), channel_id=1, source_target_pairs={{0,2},{1,3},{2,0},{3,1},{4,6},{5,7},{6,4},{7,5},{8,10},{9,11},{10,... | collective-permute-start | bytes 786440 | tf_op jit(solution)/shard_map/ppermute | solution.py:187
  18.4 13.3 %collective-permute-start.7 = (f16[32,4096]{1,0:T(8,128)(2,1)S(1)}, f16[32,4096]{1,0:T(8,128)(2,1)S(1)}, u32[]{:S(2)}, u32[]{:S(2)}) collective-permute-start(f16[32,4096]{1,0:T(8,128)(2,1)S(1)} %multiply_convert_fusion.6), channel_id=1, source_target_pairs={{0,4},{1,5},{2,6},{3,7},{4,0},{5,1},{6,2},{7,3},{8,12},{9,13},{10,... | collective-permute-start | bytes 786440 | tf_op jit(solution)/shard_map/ppermute | solution.py:187
  19.5 7.4 %collective-permute-start.6 = (f32[1,4096]{1,0:T(1,128)S(1)}, f32[1,4096]{1,0:T(1,128)S(1)}, u32[]{:S(2)}, u32[]{:S(2)}) collective-permute-start(f32[1,4096]{1,0:T(1,128)S(1)} %get-tuple-element.68), channel_id=1, source_target_pairs={{0,4},{1,5},{2,6},{3,7},{4,0},{5,1},{6,2},{7,3},{8,12},{9,13},{10,... | collective-permute-start | bytes 49160 | tf_op jit(solution)/shard_map/ppermute | solution.py:187
  26.9 4.8 %collective-permute-start.8 = (f32[1,4096]{1,0:T(1,128)S(1)}, f32[1,4096]{1,0:T(1,128)S(1)}, u32[]{:S(2)}, u32[]{:S(2)}) collective-permute-start(f32[1,4096]{1,0:T(1,128)S(1)} %maximum_add_fusion.1), channel_id=1, source_target_pairs={{0,8},{1,9},{2,10},{3,11},{4,12},{5,13},{6,14},{7,15},{8,0},{9,1},... | collective-permute-start | bytes 49160 | tf_op jit(solution)/shard_map/ppermute | solution.py:187
  32.2 9.2 %collective-permute-start.10 = (f16[32,2048]{1,0:T(8,128)(2,1)S(1)}, f16[32,2048]{1,0:T(8,128)(2,1)S(1)}, u32[]{:S(2)}, u32[]{:S(2)}) collective-permute-start(f16[32,2048]{1,0:T(8,128)(2,1)S(1)} %get-tuple-element.69), channel_id=1, source_target_pairs={{0,4},{1,5},{2,6},{3,7},{4,0},{5,1},{6,2},{7,3},{8,12},{9,13},{10,... | collective-permute-start | bytes 393224 | tf_op jit(solution)/shard_map/ppermute | solution.py:187
  32.7 8.7 %collective-permute-start.11 = (f16[32,2048]{1,0:T(8,128)(2,1)S(1)}, f16[32,2048]{1,0:T(8,128)(2,1)S(1)}, u32[]{:S(2)}, u32[]{:S(2)}) collective-permute-start(f16[32,2048]{1,0:T(8,128)(2,1)S(1)} %get-tuple-element.70), channel_id=1, source_target_pairs={{0,2},{1,3},{2,0},{3,1},{4,6},{5,7},{6,4},{7,5},{8,10},{9,11},{10,... | collective-permute-start | bytes 393224 | tf_op jit(solution)/shard_map/ppermute | solution.py:187
  33.1 8.7 %collective-permute-start.18 = (f16[64,2048]{1,0:T(8,128)(2,1)S(1)}, f16[64,2048]{1,0:T(8,128)(2,1)S(1)}, u32[]{:S(2)}, u32[]{:S(2)}) collective-permute-start(f16[64,2048]{1,0:T(8,128)(2,1)S(1)} %multiply_convert_fusion.4), channel_id=1, source_target_pairs={{0,2},{1,3},{2,0},{3,1},{4,6},{5,7},{6,4},{7,5},{8,10},{9,11},{10,... | collective-permute-start | bytes 786440 | tf_op jit(solution)/shard_map/ppermute | solution.py:187
  34.8 9.4 %collective-permute-start.19 = (f16[32,4096]{1,0:T(8,128)(2,1)S(1)}, f16[32,4096]{1,0:T(8,128)(2,1)S(1)}, u32[]{:S(2)}, u32[]{:S(2)}) collective-permute-start(f16[32,4096]{1,0:T(8,128)(2,1)S(1)} %multiply_convert_fusion.3), channel_id=1, source_target_pairs={{0,4},{1,5},{2,6},{3,7},{4,0},{5,1},{6,2},{7,3},{8,12},{9,13},{10,... | collective-permute-start | bytes 786440 | tf_op jit(solution)/shard_map/ppermute | solution.py:187
  41.6 10.6 %collective-permute-start.12 = (f16[2,32,2048]{2,1,0:T(8,128)(2,1)S(1)}, f16[2,32,2048]{2,1,0:T(8,128)(2,1)S(1)}, u32[]{:S(2)}, u32[]{:S(2)}) collective-permute-start(f16[2,32,2048]{2,1,0:T(8,128)(2,1)S(1)} %multiply_convert_fusion.5), channel_id=1, source_target_pairs={{0,8},{1,9},{2,10},{3,11},{4,12},{5,13},{6,14},{7,15},{8,0},{9,1},... | collective-permute-start | bytes 786440 | tf_op jit(solution)/shard_map/ppermute | solution.py:187
  44.5 11.1 %collective-permute-start.20 = (f16[32,2048]{1,0:T(8,128)(2,1)S(1)}, f16[32,2048]{1,0:T(8,128)(2,1)S(1)}, u32[]{:S(2)}, u32[]{:S(2)}) collective-permute-start(f16[32,2048]{1,0:T(8,128)(2,1)S(1)} %get-tuple-element.77), channel_id=1, source_target_pairs={{0,4},{1,5},{2,6},{3,7},{4,0},{5,1},{6,2},{7,3},{8,12},{9,13},{10,... | collective-permute-start | bytes 393224 | tf_op jit(solution)/shard_map/ppermute | solution.py:187
  46.0 9.5 %collective-permute-start.21 = (f16[32,2048]{1,0:T(8,128)(2,1)S(1)}, f16[32,2048]{1,0:T(8,128)(2,1)S(1)}, u32[]{:S(2)}, u32[]{:S(2)}) collective-permute-start(f16[32,2048]{1,0:T(8,128)(2,1)S(1)} %get-tuple-element.78), channel_id=1, source_target_pairs={{0,2},{1,3},{2,0},{3,1},{4,6},{5,7},{6,4},{7,5},{8,10},{9,11},{10,... | collective-permute-start | bytes 393224 | tf_op jit(solution)/shard_map/ppermute | solution.py:187
  52.3 13.9 %collective-permute-start.13 = (bf16[2,32,2048]{2,1,0:T(8,128)(2,1)S(1)}, bf16[2,32,2048]{2,1,0:T(8,128)(2,1)S(1)}, u32[]{:S(2)}, u32[]{:S(2)}) collective-permute-start(bf16[2,32,2048]{2,1,0:T(8,128)(2,1)S(1)} %add_convert_fusion.1), channel_id=1, source_target_pairs={{0,4},{1,5},{2,6},{3,7},{4,0},{5,1},{6,2},{7,3},{8,12},{9,13},{10,... | collective-permute-start | bytes 786440 | tf_op jit(solution)/shard_map/ppermute | solution.py:187
  55.8 10.3 %collective-permute-start.22 = (f16[2,32,2048]{2,1,0:T(8,128)(2,1)S(1)}, f16[2,32,2048]{2,1,0:T(8,128)(2,1)S(1)}, u32[]{:S(2)}, u32[]{:S(2)}) collective-permute-start(f16[2,32,2048]{2,1,0:T(8,128)(2,1)S(1)} %multiply_convert_fusion.2), channel_id=1, source_target_pairs={{0,8},{1,9},{2,10},{3,11},{4,12},{5,13},{6,14},{7,15},{8,0},{9,1},... | collective-permute-start | bytes 786440 | tf_op jit(solution)/shard_map/ppermute | solution.py:187
  55.9 18.4 %collective-permute-start.15 = (bf16[96,2048]{1,0:T(8,128)(2,1)S(1)}, bf16[96,2048]{1,0:T(8,128)(2,1)S(1)}, u32[]{:S(2)}, u32[]{:S(2)}) collective-permute-start(bf16[96,2048]{1,0:T(8,128)(2,1)S(1)} %collective-permute-done.9), channel_id=1, source_target_pairs={{0,1},{1,0},{2,3},{3,2},{4,5},{5,4},{6,7},{7,6},{8,9},{9,8},{10,11... | collective-permute-start | bytes 1179656 | tf_op jit(solution)/shard_map/ppermute | solution.py:187
  56.2 17.2 %collective-permute-start.14 = (bf16[160,2048]{1,0:T(8,128)(2,1)S(1)}, bf16[160,2048]{1,0:T(8,128)(2,1)S(1)}, u32[]{:S(2)}, u32[]{:S(2)}) collective-permute-start(bf16[160,2048]{1,0:T(8,128)(2,1)S(1)} %constant_dynamic-slice_fusion.3), channel_id=1, source_target_pairs={{0,2},{1,3},{2,0},{3,1},{4,6},{5,7},{6,4},{7,5},{8,10},{9,11},{10,... | collective-permute-start | bytes 1966088 | tf_op jit(solution)/shard_map/ppermute | solution.py:187
  66.1 10.2 %collective-permute-start.23 = (bf16[2,32,2048]{2,1,0:T(8,128)(2,1)S(1)}, bf16[2,32,2048]{2,1,0:T(8,128)(2,1)S(1)}, u32[]{:S(2)}, u32[]{:S(2)}) collective-permute-start(bf16[2,32,2048]{2,1,0:T(8,128)(2,1)S(1)} %add_convert_fusion), channel_id=1, source_target_pairs={{0,4},{1,5},{2,6},{3,7},{4,0},{5,1},{6,2},{7,3},{8,12},{9,13},{10,... | collective-permute-start | bytes 786440 | tf_op jit(solution)/shard_map/ppermute | solution.py:187
  73.4 2.1 %collective-permute-start.16 = (bf16[160,2048]{1,0:T(8,128)(2,1)S(1)}, bf16[160,2048]{1,0:T(8,128)(2,1)S(1)}, u32[]{:S(2)}, u32[]{:S(2)}) collective-permute-start(bf16[160,2048]{1,0:T(8,128)(2,1)S(1)} %collective-permute-done.14), channel_id=1, source_target_pairs={{0,1},{1,0},{2,3},{3,2},{4,5},{5,4},{6,7},{7,6},{8,9},{9,8},{10,11... | collective-permute-start | bytes 1966088 | tf_op jit(solution)/shard_map/ppermute | solution.py:187
  77.1 0.7 copy-start.1
  77.9 6.2 %copy-start.2 = (s32[8,12]{1,0:T(8,128)S(1)}, s32[8,12]{1,0:T(8,128)}, u32[]{:S(2)}) copy-start(s32[8,12]{1,0:T(8,128)} %param.11) | copy-start | bytes 1156
  77.9 6.8 %copy-start.3 = (s32[8]{0:T(128)S(1)}, s32[8]{0:T(128)}, u32[]{:S(2)}) copy-start(s32[8]{0:T(128)} %param.12) | copy-start | bytes 100
  77.9 6.9 %copy-start.4 = (s32[512]{0:T(512)S(1)}, s32[512]{0:T(512)}, u32[]{:S(2)}) copy-start(s32[512]{0:T(512)} %param.10) | copy-start | bytes 6148
  79.8 18.7 %all-to-all-start = ((bf16[16,1,64,256]{3,2,1,0:T(8,128)(2,1)}), bf16[16,1,64,256]{3,2,1,0:T(8,128)(2,1)S(1)}, u32[]{:S(2)}, u32[]{:S(2)}) async-start(bf16[16,1,64,256]{3,2,1,0:T(8,128)(2,1)} %bitcast.20), calls=%async_computation | async-start | bytes 1048576 | tf_op jit(solution)/shard_map/all_to_all | solution.py:328

commit v16 on v14

--- a/solution.py
+++ b/solution.py
@@ -8,7 +8,8 @@
 CORES = 2
 CHUNKS = 2
 PATHS = 2
-UNIT = 4.0
+UNIT = 2.0 ** 18
+LEAST = 2.0 ** -100
 LANES = 128
 OTHER_VMEM = 44
 MINE_VMEM = 16
@@ -187,10 +188,12 @@
     core, other_core, first_slot, offsets, first_half = scalars
 
     def pack(value):
-        return (value * UNIT).astype(jnp.float16)
+        value = value * UNIT
+        return (value * lax.rsqrt(jnp.abs(value) + LEAST)).astype(jnp.float16)
 
     def unpack(value):
-        return value.astype(jnp.float32) * (1.0 / UNIT)
+        value = value.astype(jnp.float32)
+        return value * jnp.abs(value) * (1.0 / UNIT)
 
     def part(value, bit, axis, other=0):
         shape = list(value.shape)

time: 85.2 us -> 86.2 us (1.012)
  other arithmetic: 4.85 us -> 6.08 us
    convert_element_type x12, other arithmetic: 1.48 us -> 2.4 us  [pack(): return (value * lax.rsqrt(jnp.abs(value) + LEAST)).astype(jnp.float16)]
  transfers between devices with their start and end apart: 20 -> 20, of which waited for: 12 -> 12; matrix products, arithmetic and copies ran while one was open for 9% -> 11% of each run, Pallas kernels for 7% -> 7%
where the time goes in v16:
time: 86.2 us; the launch traced here: 85.9 us
  waiting for transfers between devices  43.6 us (51%)
  starting transfers between devices  20.6 us (24%)
  Pallas kernels  8.78 us (10%)
  other arithmetic  6.08 us (7%)
  matrix products  3.34 us (4%)
  local copies, waits for them, and re-layouts  3.11 us (4%)
    ppermute x19, waiting for transfers between devices, swap(): return lax.ppermute(value, 'rows', [(r, r ^ 1 << bit) for r in range(n)])  30.9 us
    ppermute x19, starting transfers between devices, swap(): return lax.ppermute(value, 'rows', [(r, r ^ 1 << bit) for r in range(n)])  17 us
    all_to_all x1, waiting for transfers between devices, shards(): lax.all_to_all(ordered, 'rows', split_axis=0, concat_axis=0, tiled=True)  12.7 us
    pallas_call x2, Pallas kernels, product(): pl.pallas_call(kernel, in_specs=[pl.BlockSpec(memory_space=pltpu.SMEM), i...  6.04 us
    all_to_all x1, starting transfers between devices, shards(): lax.all_to_all(ordered, 'rows', split_axis=0, concat_axis=0, tiled=True)  3.57 us
    dot_general x4, matrix products, scores(): lax.dot_general(group, value, (((1,), (1,)), ((), ())), preferred_element...  3.08 us
    convert_element_type x12, other arithmetic, pack(): return (value * lax.rsqrt(jnp.abs(value) + LEAST)).astype(jnp.float16)  2.4 us
    pallas_call x1, Pallas kernels, in_slot_order(): pl.pallas_call(order_kernel, in_specs=[pl.BlockSpec(memory_space=pltpu.SM...  1.88 us
  transfers between devices with their start and end apart: 20, of which 12 were waited for; matrix products, arithmetic and copies ran while one was open for 11% of the time, Pallas kernels for 7%

profile of v16, /device:TPU:0, one launch (start us, length us, event | category | flops | bytes accessed | tf_op | source)
XLA Modules:
  0.0 85.9 jit_solution(9526177591174804263)
XLA Ops:
  0.0 1.3 %fusion.6 = (bf16[512,256]{1,0:T(8,128)(2,1)S(1)}, bf16[512,256]{1,0:T(8,128)(2,1)S(1)}) fusion(f32[512,256]{1,0:T(8,128)} %param.7), kind=kLoop, calls=%fused_computation.20 | loop fusion | flops 524288 | bytes 1048576 | tf_op jit(solution)/shard_map/convert_element_type | solution.py:257
  1.3 0.4 copy-done
  1.9 3.0 %collective-permute-start.13 = (bf16[96,2048]{1,0:T(8,128)(2,1)S(1)}, bf16[96,2048]{1,0:T(8,128)(2,1)S(1)}, u32[]{:S(2)}, u32[]{:S(2)}) collective-permute-start(bf16[96,2048]{1,0:T(8,128)(2,1)S(1)} %constant_dynamic-slice_fusion.2), channel_id=1, source_target_pairs={{0,2},{1,3},{2,0},{3,1},{4,6},{5,7},{6,4},{7,5},{8,10},{9,11},{10,... | collective-permute-start | bytes 1179656 | tf_op jit(solution)/shard_map/ppermute | solution.py:174
  5.0 4.3 %shard_map.73 = (f32[128,4096]{1,0:T(8,128)S(1)}, f32[128,4096]{1,0:T(8,128)S(1)}, bf16[256,4096]{1,0:T(8,128)(2,1)S(1)}, bf16[256,4096]{1,0:T(8,128)(2,1)S(1)}) custom-call(s32[1]{0:T(128)} %bitcast.1.core_ref, bf16[512,768]{1,0:T(8,128)(2,1)S(1)} %pad_maximum_fusion.3.rows_ref, f32[256,4096]{1,0:T(8,128)} %columns_hbm.1), custom_call_target="tpu_custom_call" | custom-call | flops 1610612736 | bytes 8388608 | tf_op jit(solution)/shard_map/pallas_call | solution.py:90
  9.2 0.4 multiply_convert_fusion.1
  9.8 0.4 multiply_convert_fusion
  10.2 0.6 collective-permute-start.6
  10.8 0.4 constant_dynamic-slice_fusion.1
  11.3 1.8 %shard_map.74 = (f32[128,4096]{1,0:T(8,128)S(1)}, f32[128,4096]{1,0:T(8,128)S(1)}) custom-call(s32[1]{0:T(128)} %bitcast.2.core_ref, bf16[512,768]{1,0:T(8,128)(2,1)S(1)} %pad_maximum_fusion.3.rows_ref, bf16[256,4096]{1,0:T(8,128)(2,1)S(1)} %get-tuple-element.52.high_ref, bf16[256,4096]{1,0:T(8,128)(2,1)S(1)} %get-tuple-element.53.low_ref), custom_call_target="tpu_custom_call" | custom-call | flops 1610612736 | bytes 8388608 | tf_op jit(solution)/shard_map/pallas_call | solution.py:90
  13.1 0.4 fusion.1
  13.7 0.2 multiply_convert_fusion.7
  14.2 2.1 %collective-permute-start.4 = (f16[32,4096]{1,0:T(8,128)(2,1)S(1)}, f16[32,4096]{1,0:T(8,128)(2,1)S(1)}, u32[]{:S(2)}, u32[]{:S(2)}) collective-permute-start(f16[32,4096]{1,0:T(8,128)(2,1)S(1)} %multiply_convert_fusion.6), channel_id=1, source_target_pairs={{0,4},{1,5},{2,6},{3,7},{4,0},{5,1},{6,2},{7,3},{8,12},{9,13},{10,... | collective-permute-start | bytes 786440 | tf_op jit(solution)/shard_map/ppermute | solution.py:174
  16.3 0.4 fusion.3
  17.0 0.2 multiply_convert_fusion.5
  17.2 5.5 %collective-permute-done.2 = f16[64,2048]{1,0:T(8,128)(2,1)S(1)} collective-permute-done((f16[64,2048]{1,0:T(8,128)(2,1)S(1)}, f16[64,2048]{1,0:T(8,128)(2,1)S(1)}, u32[]{:S(2)}, u32[]{:S(2)}) %collective-permute-start.2) | collective-permute-done | bytes 262176 | tf_op jit(solution)/shard_map/ppermute | solution.py:174
  23.0 1.6 %collective-permute-start.3 = (f16[32,2048]{1,0:T(8,128)(2,1)S(1)}, f16[32,2048]{1,0:T(8,128)(2,1)S(1)}, u32[]{:S(2)}, u32[]{:S(2)}) collective-permute-start(f16[32,2048]{1,0:T(8,128)(2,1)S(1)} %multiply_convert_fusion.11), channel_id=1, source_target_pairs={{0,4},{1,5},{2,6},{3,7},{4,0},{5,1},{6,2},{7,3},{8,12},{9,13},{10,... | collective-permute-start | bytes 393224 | tf_op jit(solution)/shard_map/ppermute | solution.py:174
  24.9 0.6 collective-permute-start.5
  25.5 1.5 %collective-permute-start.7 = (f16[64,2048]{1,0:T(8,128)(2,1)S(1)}, f16[64,2048]{1,0:T(8,128)(2,1)S(1)}, u32[]{:S(2)}, u32[]{:S(2)}) collective-permute-start(f16[64,2048]{1,0:T(8,128)(2,1)S(1)} %multiply_convert_fusion.5), channel_id=1, source_target_pairs={{0,2},{1,3},{2,0},{3,1},{4,6},{5,7},{6,4},{7,5},{8,10},{9,11},{10,... | collective-permute-start | bytes 786440 | tf_op jit(solution)/shard_map/ppermute | solution.py:174
  27.0 0.5 collective-permute-start.9
  27.5 0.7 collective-permute-done.3
  28.3 3.2 %collective-permute-done.5 = f16[32,2048]{1,0:T(8,128)(2,1)S(1)} collective-permute-done((f16[32,2048]{1,0:T(8,128)(2,1)S(1)}, f16[32,2048]{1,0:T(8,128)(2,1)S(1)}, u32[]{:S(2)}, u32[]{:S(2)}) %collective-permute-start.5) | collective-permute-done | bytes 131104 | tf_op jit(solution)/shard_map/ppermute | solution.py:174
  31.7 2.6 %collective-permute-start.11 = (f16[2,32,2048]{2,1,0:T(8,128)(2,1)S(1)}, f16[2,32,2048]{2,1,0:T(8,128)(2,1)S(1)}, u32[]{:S(2)}, u32[]{:S(2)}) collective-permute-start(f16[2,32,2048]{2,1,0:T(8,128)(2,1)S(1)} %get-tuple-element.86), channel_id=1, source_target_pairs={{0,8},{1,9},{2,10},{3,11},{4,12},{5,13},{6,14},{7,15},{8,0},{9,1},... | collective-permute-start | bytes 786440 | tf_op jit(solution)/shard_map/ppermute | solution.py:174
  34.4 1.1 %collective-permute-done.7 = f16[64,2048]{1,0:T(8,128)(2,1)S(1)} collective-permute-done((f16[64,2048]{1,0:T(8,128)(2,1)S(1)}, f16[64,2048]{1,0:T(8,128)(2,1)S(1)}, u32[]{:S(2)}, u32[]{:S(2)}) %collective-permute-start.7) | collective-permute-done | bytes 262176 | tf_op jit(solution)/shard_map/ppermute | solution.py:174
  35.4 0.2 fusion.12
  35.7 0.5 collective-permute-start.8
  36.3 1.8 %collective-permute-done.9 = f16[32,4096]{1,0:T(8,128)(2,1)S(1)} collective-permute-done((f16[32,4096]{1,0:T(8,128)(2,1)S(1)}, f16[32,4096]{1,0:T(8,128)(2,1)S(1)}, u32[]{:S(2)}, u32[]{:S(2)}) %collective-permute-start.9) | collective-permute-done | bytes 262176 | tf_op jit(solution)/shard_map/ppermute | solution.py:174
  38.4 0.6 collective-permute-start.10
  39.0 3.0 %collective-permute-done.8 = f16[32,2048]{1,0:T(8,128)(2,1)S(1)} collective-permute-done((f16[32,2048]{1,0:T(8,128)(2,1)S(1)}, f16[32,2048]{1,0:T(8,128)(2,1)S(1)}, u32[]{:S(2)}, u32[]{:S(2)}) %collective-permute-start.8) | collective-permute-done | bytes 131104 | tf_op jit(solution)/shard_map/ppermute | solution.py:174
  42.0 1.4 %collective-permute-done.10 = f16[32,2048]{1,0:T(8,128)(2,1)S(1)} collective-permute-done((f16[32,2048]{1,0:T(8,128)(2,1)S(1)}, f16[32,2048]{1,0:T(8,128)(2,1)S(1)}, u32[]{:S(2)}, u32[]{:S(2)}) %collective-permute-start.10) | collective-permute-done | bytes 131104 | tf_op jit(solution)/shard_map/ppermute | solution.py:174
  43.7 1.9 %collective-permute-start.17 = (f16[2,32,2048]{2,1,0:T(8,128)(2,1)S(1)}, f16[2,32,2048]{2,1,0:T(8,128)(2,1)S(1)}, u32[]{:S(2)}, u32[]{:S(2)}) collective-permute-start(f16[2,32,2048]{2,1,0:T(8,128)(2,1)S(1)} %multiply_convert_fusion.3), channel_id=1, source_target_pairs={{0,8},{1,9},{2,10},{3,11},{4,12},{5,13},{6,14},{7,15},{8,0},{9,1},... | collective-permute-start | bytes 786440 | tf_op jit(solution)/shard_map/ppermute | solution.py:174
  45.7 0.6 collective-permute-start.12
  46.3 0.3 constant_dynamic-slice_fusion.3
  46.6 0.6 collective-permute-start.14
  47.2 8.6 %collective-permute-done.17 = f16[2,32,2048]{2,1,0:T(8,128)(2,1)S(1)} collective-permute-done((f16[2,32,2048]{2,1,0:T(8,128)(2,1)S(1)}, f16[2,32,2048]{2,1,0:T(8,128)(2,1)S(1)}, u32[]{:S(2)}, u32[]{:S(2)}) %collective-permute-start.17) | collective-permute-done | bytes 262176 | tf_op jit(solution)/shard_map/ppermute | solution.py:174
  55.9 1.0 %collective-permute-done.12 = bf16[2,32,2048]{2,1,0:T(8,128)(2,1)S(1)} collective-permute-done((bf16[2,32,2048]{2,1,0:T(8,128)(2,1)S(1)}, bf16[2,32,2048]{2,1,0:T(8,128)(2,1)S(1)}, u32[]{:S(2)}, u32[]{:S(2)}) %collective-permute-start.12) | collective-permute-done | bytes 262176 | tf_op jit(solution)/shard_map/ppermute | solution.py:174
  57.0 3.4 %collective-permute-done.14 = bf16[160,2048]{1,0:T(8,128)(2,1)S(1)} collective-permute-done((bf16[160,2048]{1,0:T(8,128)(2,1)S(1)}, bf16[160,2048]{1,0:T(8,128)(2,1)S(1)}, u32[]{:S(2)}, u32[]{:S(2)}) %collective-permute-start.14) | collective-permute-done | bytes 655392 | tf_op jit(solution)/shard_map/ppermute | solution.py:174
  60.4 0.7 fusion.5.refs_0_
  61.3 1.3 %collective-permute-done.16 = bf16[160,2048]{1,0:T(8,128)(2,1)S(1)} collective-permute-done((bf16[160,2048]{1,0:T(8,128)(2,1)S(1)}, bf16[160,2048]{1,0:T(8,128)(2,1)S(1)}, u32[]{:S(2)}, u32[]{:S(2)}) %collective-permute-start.16) | collective-permute-done | bytes 655392 | tf_op jit(solution)/shard_map/ppermute | solution.py:174
  62.6 0.9 %fusion.42.refs_1_ = f32[512,128]{1,0:T(8,128)S(1)} fusion(bf16[512,2048]{1,0:T(8,128)(2,1)S(1)} %constant_dynamic-update-slice_fusion, bf16[128,2048]{1,0:T(8,128)(2,1)S(1)} %bitcast.30), kind=kOutput, calls=%fused_computation.85 | convolution fusion | flops 268435456 | bytes 2883584 | tf_op jit(solution)/shard_map/dot_general | solution.py:246
  63.6 0.7 fusion.43.refs_3_
  64.4 0.7 fusion.4.refs_2_
  65.2 1.9 %shard_map.75 = bf16[16,64,256]{2,1,0:T(8,128)(2,1)} custom-call(s32[16]{0:T(128)S(1)} %copy-done.1, f32[512,128]{1,0:T(8,128)S(1)} %fusion.5.refs_0_, f32[512,128]{1,0:T(8,128)S(1)} %fusion.42.refs_1_, f32[512,128]{1,0:T(8,128)S(1)} %fusion.4.refs_2_, f32[512,128]{1,0:T(8,128)S(1)} %fusion.43.refs_3_), custom_call_target="tpu_custom_call" | custom-call | flops 65536 | bytes 1572864 | tf_op jit(solution)/shard_map/pallas_call | solution.py:123
  67.0 3.6 %all-to-all-start = ((bf16[16,1,64,256]{3,2,1,0:T(8,128)(2,1)}), bf16[16,1,64,256]{3,2,1,0:T(8,128)(2,1)S(1)}, u32[]{:S(2)}, u32[]{:S(2)}) async-start(bf16[16,1,64,256]{3,2,1,0:T(8,128)(2,1)} %bitcast.10), calls=%async_computation | async-start | bytes 1048576 | tf_op jit(solution)/shard_map/all_to_all | solution.py:299
  70.7 0.6 dynamic_slice.79
  71.4 0.3 fusion.33
  71.7 0.6 constant_dynamic-slice_fusion.allowed_ref
  72.4 12.7 %all-to-all-done = bf16[16,1,64,256]{3,2,1,0:T(8,128)(2,1)S(1)} async-done(((bf16[16,1,64,256]{3,2,1,0:T(8,128)(2,1)}), bf16[16,1,64,256]{3,2,1,0:T(8,128)(2,1)S(1)}, u32[]{:S(2)}, u32[]{:S(2)}) %all-to-all-start) | async-done | bytes 524320 | tf_op jit(solution)/shard_map/all_to_all | solution.py:299
  85.0 0.9 %shard_map.76 = f32[1024,128]{1,0:T(8,128)} custom-call(bf16[16,1,4,16,256]{4,3,2,1,0:T(8,128)(2,1)S(1)} %bitcast.28, f32[1,512]{1,0:T(1,128)S(1)} %constant_dynamic-slice_fusion.allowed_ref), custom_call_target="tpu_custom_call" | custom-call | flops 262144 | bytes 1048576 | tf_op jit(solution)/shard_map/pallas_call | solution.py:152
  (53 shorter events, 3.6 us)
Async XLA Ops:
  0.0 1.7 %copy-start = (bf16[16,16,4096]{2,1,0:T(8,128)(2,1)S(1)}, bf16[16,16,4096]{2,1,0:T(8,128)(2,1)}, u32[]{:S(2)}) copy-start(bf16[16,16,4096]{2,1,0:T(8,128)(2,1)} %param.9) | copy-start | bytes 6291460
  1.9 44.4 %collective-permute-start.13 = (bf16[96,2048]{1,0:T(8,128)(2,1)S(1)}, bf16[96,2048]{1,0:T(8,128)(2,1)S(1)}, u32[]{:S(2)}, u32[]{:S(2)}) collective-permute-start(bf16[96,2048]{1,0:T(8,128)(2,1)S(1)} %constant_dynamic-slice_fusion.2), channel_id=1, source_target_pairs={{0,2},{1,3},{2,0},{3,1},{4,6},{5,7},{6,4},{7,5},{8,10},{9,11},{10,... | collective-permute-start | bytes 1179656 | tf_op jit(solution)/shard_map/ppermute | solution.py:174
  9.7 3.4 %collective-permute-start.1 = (f16[128,4096]{1,0:T(8,128)(2,1)S(1)}, f16[128,4096]{1,0:T(8,128)(2,1)S(1)}, u32[]{:S(2)}, u32[]{:S(2)}) collective-permute-start(f16[128,4096]{1,0:T(8,128)(2,1)S(1)} %multiply_convert_fusion.1), channel_id=1, source_target_pairs={{0,1},{1,0},{2,3},{3,2},{4,5},{5,4},{6,7},{7,6},{8,9},{9,8},{10,11... | collective-permute-start | bytes 3145736 | tf_op jit(solution)/shard_map/ppermute | solution.py:174
  10.2 6.1 %collective-permute-start.6 = (f16[128,4096]{1,0:T(8,128)(2,1)S(1)}, f16[128,4096]{1,0:T(8,128)(2,1)S(1)}, u32[]{:S(2)}, u32[]{:S(2)}) collective-permute-start(f16[128,4096]{1,0:T(8,128)(2,1)S(1)} %multiply_convert_fusion), channel_id=1, source_target_pairs={{0,1},{1,0},{2,3},{3,2},{4,5},{5,4},{6,7},{7,6},{8,9},{9,8},{10,11... | collective-permute-start | bytes 3145736 | tf_op jit(solution)/shard_map/ppermute | solution.py:174
  11.2 14.3 %collective-permute-start = (bf16[256,2048]{1,0:T(8,128)(2,1)S(1)}, bf16[256,2048]{1,0:T(8,128)(2,1)S(1)}, u32[]{:S(2)}, u32[]{:S(2)}) collective-permute-start(bf16[256,2048]{1,0:T(8,128)(2,1)S(1)} %constant_dynamic-slice_fusion.1), channel_id=1, source_target_pairs={{0,1},{1,0},{2,3},{3,2},{4,5},{5,4},{6,7},{7,6},{8,9},{9,8},{10,11... | collective-permute-start | bytes 3145736 | tf_op jit(solution)/shard_map/ppermute | solution.py:174
  13.9 8.8 %collective-permute-start.2 = (f16[64,2048]{1,0:T(8,128)(2,1)S(1)}, f16[64,2048]{1,0:T(8,128)(2,1)S(1)}, u32[]{:S(2)}, u32[]{:S(2)}) collective-permute-start(f16[64,2048]{1,0:T(8,128)(2,1)S(1)} %multiply_convert_fusion.7), channel_id=1, source_target_pairs={{0,2},{1,3},{2,0},{3,1},{4,6},{5,7},{6,4},{7,5},{8,10},{9,11},{10,... | collective-permute-start | bytes 786440 | tf_op jit(solution)/shard_map/ppermute | solution.py:174
  14.2 10.5 %collective-permute-start.4 = (f16[32,4096]{1,0:T(8,128)(2,1)S(1)}, f16[32,4096]{1,0:T(8,128)(2,1)S(1)}, u32[]{:S(2)}, u32[]{:S(2)}) collective-permute-start(f16[32,4096]{1,0:T(8,128)(2,1)S(1)} %multiply_convert_fusion.6), channel_id=1, source_target_pairs={{0,4},{1,5},{2,6},{3,7},{4,0},{5,1},{6,2},{7,3},{8,12},{9,13},{10,... | collective-permute-start | bytes 786440 | tf_op jit(solution)/shard_map/ppermute | solution.py:174
  23.0 5.2 %collective-permute-start.3 = (f16[32,2048]{1,0:T(8,128)(2,1)S(1)}, f16[32,2048]{1,0:T(8,128)(2,1)S(1)}, u32[]{:S(2)}, u32[]{:S(2)}) collective-permute-start(f16[32,2048]{1,0:T(8,128)(2,1)S(1)} %multiply_convert_fusion.11), channel_id=1, source_target_pairs={{0,4},{1,5},{2,6},{3,7},{4,0},{5,1},{6,2},{7,3},{8,12},{9,13},{10,... | collective-permute-start | bytes 393224 | tf_op jit(solution)/shard_map/ppermute | solution.py:174
  24.9 6.5 %collective-permute-start.5 = (f16[32,2048]{1,0:T(8,128)(2,1)S(1)}, f16[32,2048]{1,0:T(8,128)(2,1)S(1)}, u32[]{:S(2)}, u32[]{:S(2)}) collective-permute-start(f16[32,2048]{1,0:T(8,128)(2,1)S(1)} %multiply_convert_fusion.10), channel_id=1, source_target_pairs={{0,2},{1,3},{2,0},{3,1},{4,6},{5,7},{6,4},{7,5},{8,10},{9,11},{10,... | collective-permute-start | bytes 393224 | tf_op jit(solution)/shard_map/ppermute | solution.py:174
  25.5 9.9 %collective-permute-start.7 = (f16[64,2048]{1,0:T(8,128)(2,1)S(1)}, f16[64,2048]{1,0:T(8,128)(2,1)S(1)}, u32[]{:S(2)}, u32[]{:S(2)}) collective-permute-start(f16[64,2048]{1,0:T(8,128)(2,1)S(1)} %multiply_convert_fusion.5), channel_id=1, source_target_pairs={{0,2},{1,3},{2,0},{3,1},{4,6},{5,7},{6,4},{7,5},{8,10},{9,11},{10,... | collective-permute-start | bytes 786440 | tf_op jit(solution)/shard_map/ppermute | solution.py:174
  27.0 11.1 %collective-permute-start.9 = (f16[32,4096]{1,0:T(8,128)(2,1)S(1)}, f16[32,4096]{1,0:T(8,128)(2,1)S(1)}, u32[]{:S(2)}, u32[]{:S(2)}) collective-permute-start(f16[32,4096]{1,0:T(8,128)(2,1)S(1)} %multiply_convert_fusion.4), channel_id=1, source_target_pairs={{0,4},{1,5},{2,6},{3,7},{4,0},{5,1},{6,2},{7,3},{8,12},{9,13},{10,... | collective-permute-start | bytes 786440 | tf_op jit(solution)/shard_map/ppermute | solution.py:174
  31.7 13.9 %collective-permute-start.11 = (f16[2,32,2048]{2,1,0:T(8,128)(2,1)S(1)}, f16[2,32,2048]{2,1,0:T(8,128)(2,1)S(1)}, u32[]{:S(2)}, u32[]{:S(2)}) collective-permute-start(f16[2,32,2048]{2,1,0:T(8,128)(2,1)S(1)} %get-tuple-element.86), channel_id=1, source_target_pairs={{0,8},{1,9},{2,10},{3,11},{4,12},{5,13},{6,14},{7,15},{8,0},{9,1},... | collective-permute-start | bytes 786440 | tf_op jit(solution)/shard_map/ppermute | solution.py:174
  35.7 6.2 %collective-permute-start.8 = (f16[32,2048]{1,0:T(8,128)(2,1)S(1)}, f16[32,2048]{1,0:T(8,128)(2,1)S(1)}, u32[]{:S(2)}, u32[]{:S(2)}) collective-permute-start(f16[32,2048]{1,0:T(8,128)(2,1)S(1)} %multiply_convert_fusion.9), channel_id=1, source_target_pairs={{0,4},{1,5},{2,6},{3,7},{4,0},{5,1},{6,2},{7,3},{8,12},{9,13},{10,... | collective-permute-start | bytes 393224 | tf_op jit(solution)/shard_map/ppermute | solution.py:174
  38.4 5.0 %collective-permute-start.10 = (f16[32,2048]{1,0:T(8,128)(2,1)S(1)}, f16[32,2048]{1,0:T(8,128)(2,1)S(1)}, u32[]{:S(2)}, u32[]{:S(2)}) collective-permute-start(f16[32,2048]{1,0:T(8,128)(2,1)S(1)} %multiply_convert_fusion.8), channel_id=1, source_target_pairs={{0,2},{1,3},{2,0},{3,1},{4,6},{5,7},{6,4},{7,5},{8,10},{9,11},{10,... | collective-permute-start | bytes 393224 | tf_op jit(solution)/shard_map/ppermute | solution.py:174
  43.7 12.0 %collective-permute-start.17 = (f16[2,32,2048]{2,1,0:T(8,128)(2,1)S(1)}, f16[2,32,2048]{2,1,0:T(8,128)(2,1)S(1)}, u32[]{:S(2)}, u32[]{:S(2)}) collective-permute-start(f16[2,32,2048]{2,1,0:T(8,128)(2,1)S(1)} %multiply_convert_fusion.3), channel_id=1, source_target_pairs={{0,8},{1,9},{2,10},{3,11},{4,12},{5,13},{6,14},{7,15},{8,0},{9,1},... | collective-permute-start | bytes 786440 | tf_op jit(solution)/shard_map/ppermute | solution.py:174
  45.7 11.2 %collective-permute-start.12 = (bf16[2,32,2048]{2,1,0:T(8,128)(2,1)S(1)}, bf16[2,32,2048]{2,1,0:T(8,128)(2,1)S(1)}, u32[]{:S(2)}, u32[]{:S(2)}) collective-permute-start(bf16[2,32,2048]{2,1,0:T(8,128)(2,1)S(1)} %fusion.17), channel_id=1, source_target_pairs={{0,4},{1,5},{2,6},{3,7},{4,0},{5,1},{6,2},{7,3},{8,12},{9,13},{10,... | collective-permute-start | bytes 786440 | tf_op jit(solution)/shard_map/ppermute | solution.py:174
  46.6 13.9 %collective-permute-start.14 = (bf16[160,2048]{1,0:T(8,128)(2,1)S(1)}, bf16[160,2048]{1,0:T(8,128)(2,1)S(1)}, u32[]{:S(2)}, u32[]{:S(2)}) collective-permute-start(bf16[160,2048]{1,0:T(8,128)(2,1)S(1)} %constant_dynamic-slice_fusion.3), channel_id=1, source_target_pairs={{0,2},{1,3},{2,0},{3,1},{4,6},{5,7},{6,4},{7,5},{8,10},{9,11},{10,... | collective-permute-start | bytes 1966088 | tf_op jit(solution)/shard_map/ppermute | solution.py:174
  47.1 14.1 %collective-permute-start.15 = (bf16[96,2048]{1,0:T(8,128)(2,1)S(1)}, bf16[96,2048]{1,0:T(8,128)(2,1)S(1)}, u32[]{:S(2)}, u32[]{:S(2)}) collective-permute-start(bf16[96,2048]{1,0:T(8,128)(2,1)S(1)} %collective-permute-done.13), channel_id=1, source_target_pairs={{0,1},{1,0},{2,3},{3,2},{4,5},{5,4},{6,7},{7,6},{8,9},{9,8},{10,11... | collective-permute-start | bytes 1179656 | tf_op jit(solution)/shard_map/ppermute | solution.py:174
  55.8 7.7 %collective-permute-start.18 = (bf16[2,32,2048]{2,1,0:T(8,128)(2,1)S(1)}, bf16[2,32,2048]{2,1,0:T(8,128)(2,1)S(1)}, u32[]{:S(2)}, u32[]{:S(2)}) collective-permute-start(bf16[2,32,2048]{2,1,0:T(8,128)(2,1)S(1)} %fusion.20), channel_id=1, source_target_pairs={{0,4},{1,5},{2,6},{3,7},{4,0},{5,1},{6,2},{7,3},{8,12},{9,13},{10,... | collective-permute-start | bytes 786440 | tf_op jit(solution)/shard_map/ppermute | solution.py:174
  60.4 2.1 %collective-permute-start.16 = (bf16[160,2048]{1,0:T(8,128)(2,1)S(1)}, bf16[160,2048]{1,0:T(8,128)(2,1)S(1)}, u32[]{:S(2)}, u32[]{:S(2)}) collective-permute-start(bf16[160,2048]{1,0:T(8,128)(2,1)S(1)} %collective-permute-done.14), channel_id=1, source_target_pairs={{0,1},{1,0},{2,3},{3,2},{4,5},{5,4},{6,7},{7,6},{8,9},{9,8},{10,11... | collective-permute-start | bytes 1966088 | tf_op jit(solution)/shard_map/ppermute | solution.py:174
  64.3 0.8 copy-start.1
  65.1 5.5 %copy-start.2 = (s32[8,12]{1,0:T(8,128)S(1)}, s32[8,12]{1,0:T(8,128)}, u32[]{:S(2)}) copy-start(s32[8,12]{1,0:T(8,128)} %param.11) | copy-start | bytes 1156
  65.1 6.2 %copy-start.3 = (s32[8]{0:T(128)S(1)}, s32[8]{0:T(128)}, u32[]{:S(2)}) copy-start(s32[8]{0:T(128)} %param.12) | copy-start | bytes 100
  65.1 6.3 %copy-start.4 = (s32[512]{0:T(512)S(1)}, s32[512]{0:T(512)}, u32[]{:S(2)}) copy-start(s32[512]{0:T(512)} %param.10) | copy-start | bytes 6148
  67.0 18.0 %all-to-all-start = ((bf16[16,1,64,256]{3,2,1,0:T(8,128)(2,1)}), bf16[16,1,64,256]{3,2,1,0:T(8,128)(2,1)S(1)}, u32[]{:S(2)}, u32[]{:S(2)}) async-start(bf16[16,1,64,256]{3,2,1,0:T(8,128)(2,1)} %bitcast.10), calls=%async_computation | async-start | bytes 1048576 | tf_op jit(solution)/shard_map/all_to_all | solution.py:299

commit v17 on v16

--- a/solution.py
+++ b/solution.py
@@ -246,7 +246,7 @@
         return lax.dot_general(group, value, (((1,), (1,)), ((), ())), preferred_element_type=jnp.float32)
 
     blocks = train.reshape(examples * nblocks, width)
-    total = examples * nblocks
+    every = examples * nblocks
     middle = max(1, examples * 3 // 8) * nblocks
 
     def features(blocks, first, count, other):
@@ -266,7 +266,7 @@
     sent = [pack(value) for value in full]
     got = [swap(value, 0) for value in sent]
     blocks = after(blocks, sent)
-    near = features(blocks, 0, total, 0)
+    near = features(blocks, 0, every, 0)
     sibling = swap(near, 0)
     mine = product(after(core, sent), left, [high, low], mine_kernel, MINE_VMEM)
     one = paths(mine[0], got[0])
@@ -280,12 +280,12 @@
     got_one = swap(sent, rest[-1])
     two = exchange(two, sent_two, 0)
     two = exchange(two, messages(two, 1), 1)
+    late = swap(features(after(blocks, two[0]), middle, every - middle, 1), ybit)
     two = halve(two)
     sent = pack(two)
     one = (after(one, sent) + unpack(got_one)).astype(jnp.bfloat16)
     got_two = swap(sent, rest[-1])
-    blocks, early = after((blocks, early), one)
-    late = swap(features(blocks, middle, total - middle, 1), ybit)
+    early = after(early, one)
     one = gather(one)
     groups = [
         jnp.concatenate([near, sibling], axis=0),

time: 86.2 us -> 85.9 us (level)
  no operation moved by 1% of the time
where the time goes in v17:
time: 85.9 us; the launch traced here: 85.7 us
  waiting for transfers between devices  43.4 us (51%)
  starting transfers between devices  20.6 us (24%)
  Pallas kernels  8.78 us (10%)
  other arithmetic  6.05 us (7%)
  matrix products  3.34 us (4%)
  local copies, waits for them, and re-layouts  3.11 us (4%)
    ppermute x19, waiting for transfers between devices, swap(): return lax.ppermute(value, 'rows', [(r, r ^ 1 << bit) for r in range(n)])  30.7 us
    ppermute x19, starting transfers between devices, swap(): return lax.ppermute(value, 'rows', [(r, r ^ 1 << bit) for r in range(n)])  17 us
    all_to_all x1, waiting for transfers between devices, shards(): lax.all_to_all(ordered, 'rows', split_axis=0, concat_axis=0, tiled=True)  12.7 us
    pallas_call x2, Pallas kernels, product(): pl.pallas_call(kernel, in_specs=[pl.BlockSpec(memory_space=pltpu.SMEM), i...  6.04 us
    all_to_all x1, starting transfers between devices, shards(): lax.all_to_all(ordered, 'rows', split_axis=0, concat_axis=0, tiled=True)  3.57 us
    dot_general x4, matrix products, scores(): lax.dot_general(group, value, (((1,), (1,)), ((), ())), preferred_element...  3.08 us
    convert_element_type x12, other arithmetic, pack(): return (value * lax.rsqrt(jnp.abs(value) + LEAST)).astype(jnp.float16)  2.4 us
    pallas_call x1, Pallas kernels, in_slot_order(): pl.pallas_call(order_kernel, in_specs=[pl.BlockSpec(memory_space=pltpu.SM...  1.88 us
  transfers between devices with their start and end apart: 20, of which 12 were waited for; matrix products, arithmetic and copies ran while one was open for 11% of the time, Pallas kernels for 7%

profile of v17, /device:TPU:0, one launch (start us, length us, event | category | flops | bytes accessed | tf_op | source)
XLA Modules:
  0.0 85.7 jit_solution(18363430220460193716)
XLA Ops:
  0.0 1.3 %fusion.6 = (bf16[512,256]{1,0:T(8,128)(2,1)S(1)}, bf16[512,256]{1,0:T(8,128)(2,1)S(1)}) fusion(f32[512,256]{1,0:T(8,128)} %param.7), kind=kLoop, calls=%fused_computation.20 | loop fusion | flops 524288 | bytes 1048576 | tf_op jit(solution)/shard_map/convert_element_type | solution.py:257
  1.3 0.4 copy-done
  1.9 3.0 %collective-permute-start.13 = (bf16[96,2048]{1,0:T(8,128)(2,1)S(1)}, bf16[96,2048]{1,0:T(8,128)(2,1)S(1)}, u32[]{:S(2)}, u32[]{:S(2)}) collective-permute-start(bf16[96,2048]{1,0:T(8,128)(2,1)S(1)} %constant_dynamic-slice_fusion.2), channel_id=1, source_target_pairs={{0,2},{1,3},{2,0},{3,1},{4,6},{5,7},{6,4},{7,5},{8,10},{9,11},{10,... | collective-permute-start | bytes 1179656 | tf_op jit(solution)/shard_map/ppermute | solution.py:174
  5.0 4.3 %shard_map.73 = (f32[128,4096]{1,0:T(8,128)S(1)}, f32[128,4096]{1,0:T(8,128)S(1)}, bf16[256,4096]{1,0:T(8,128)(2,1)S(1)}, bf16[256,4096]{1,0:T(8,128)(2,1)S(1)}) custom-call(s32[1]{0:T(128)} %bitcast.1.core_ref, bf16[512,768]{1,0:T(8,128)(2,1)S(1)} %pad_maximum_fusion.3.rows_ref, f32[256,4096]{1,0:T(8,128)} %columns_hbm.1), custom_call_target="tpu_custom_call" | custom-call | flops 1610612736 | bytes 8388608 | tf_op jit(solution)/shard_map/pallas_call | solution.py:90
  9.2 0.4 multiply_convert_fusion.1
  9.8 0.4 multiply_convert_fusion
  10.2 0.6 collective-permute-start.6
  10.8 0.4 constant_dynamic-slice_fusion.1
  11.3 1.8 %shard_map.74 = (f32[128,4096]{1,0:T(8,128)S(1)}, f32[128,4096]{1,0:T(8,128)S(1)}) custom-call(s32[1]{0:T(128)} %bitcast.2.core_ref, bf16[512,768]{1,0:T(8,128)(2,1)S(1)} %pad_maximum_fusion.3.rows_ref, bf16[256,4096]{1,0:T(8,128)(2,1)S(1)} %get-tuple-element.52.high_ref, bf16[256,4096]{1,0:T(8,128)(2,1)S(1)} %get-tuple-element.53.low_ref), custom_call_target="tpu_custom_call" | custom-call | flops 1610612736 | bytes 8388608 | tf_op jit(solution)/shard_map/pallas_call | solution.py:90
  13.1 0.4 fusion.1
  13.7 0.2 multiply_convert_fusion.7
  14.2 2.1 %collective-permute-start.4 = (f16[32,4096]{1,0:T(8,128)(2,1)S(1)}, f16[32,4096]{1,0:T(8,128)(2,1)S(1)}, u32[]{:S(2)}, u32[]{:S(2)}) collective-permute-start(f16[32,4096]{1,0:T(8,128)(2,1)S(1)} %multiply_convert_fusion.6), channel_id=1, source_target_pairs={{0,4},{1,5},{2,6},{3,7},{4,0},{5,1},{6,2},{7,3},{8,12},{9,13},{10,... | collective-permute-start | bytes 786440 | tf_op jit(solution)/shard_map/ppermute | solution.py:174
  16.3 0.4 fusion.3
  17.0 0.2 multiply_convert_fusion.5
  17.2 5.5 %collective-permute-done.2 = f16[64,2048]{1,0:T(8,128)(2,1)S(1)} collective-permute-done((f16[64,2048]{1,0:T(8,128)(2,1)S(1)}, f16[64,2048]{1,0:T(8,128)(2,1)S(1)}, u32[]{:S(2)}, u32[]{:S(2)}) %collective-permute-start.2) | collective-permute-done | bytes 262176 | tf_op jit(solution)/shard_map/ppermute | solution.py:174
  23.0 1.6 %collective-permute-start.3 = (f16[32,2048]{1,0:T(8,128)(2,1)S(1)}, f16[32,2048]{1,0:T(8,128)(2,1)S(1)}, u32[]{:S(2)}, u32[]{:S(2)}) collective-permute-start(f16[32,2048]{1,0:T(8,128)(2,1)S(1)} %multiply_convert_fusion.11), channel_id=1, source_target_pairs={{0,4},{1,5},{2,6},{3,7},{4,0},{5,1},{6,2},{7,3},{8,12},{9,13},{10,... | collective-permute-start | bytes 393224 | tf_op jit(solution)/shard_map/ppermute | solution.py:174
  24.9 0.6 collective-permute-start.5
  25.5 1.5 %collective-permute-start.7 = (f16[64,2048]{1,0:T(8,128)(2,1)S(1)}, f16[64,2048]{1,0:T(8,128)(2,1)S(1)}, u32[]{:S(2)}, u32[]{:S(2)}) collective-permute-start(f16[64,2048]{1,0:T(8,128)(2,1)S(1)} %multiply_convert_fusion.5), channel_id=1, source_target_pairs={{0,2},{1,3},{2,0},{3,1},{4,6},{5,7},{6,4},{7,5},{8,10},{9,11},{10,... | collective-permute-start | bytes 786440 | tf_op jit(solution)/shard_map/ppermute | solution.py:174
  27.0 0.5 collective-permute-start.9
  27.5 0.7 collective-permute-done.3
  28.2 3.2 %collective-permute-done.5 = f16[32,2048]{1,0:T(8,128)(2,1)S(1)} collective-permute-done((f16[32,2048]{1,0:T(8,128)(2,1)S(1)}, f16[32,2048]{1,0:T(8,128)(2,1)S(1)}, u32[]{:S(2)}, u32[]{:S(2)}) %collective-permute-start.5) | collective-permute-done | bytes 131104 | tf_op jit(solution)/shard_map/ppermute | solution.py:174
  31.7 2.6 %collective-permute-start.11 = (f16[2,32,2048]{2,1,0:T(8,128)(2,1)S(1)}, f16[2,32,2048]{2,1,0:T(8,128)(2,1)S(1)}, u32[]{:S(2)}, u32[]{:S(2)}) collective-permute-start(f16[2,32,2048]{2,1,0:T(8,128)(2,1)S(1)} %get-tuple-element.86), channel_id=1, source_target_pairs={{0,8},{1,9},{2,10},{3,11},{4,12},{5,13},{6,14},{7,15},{8,0},{9,1},... | collective-permute-start | bytes 786440 | tf_op jit(solution)/shard_map/ppermute | solution.py:174
  34.4 1.1 %collective-permute-done.7 = f16[64,2048]{1,0:T(8,128)(2,1)S(1)} collective-permute-done((f16[64,2048]{1,0:T(8,128)(2,1)S(1)}, f16[64,2048]{1,0:T(8,128)(2,1)S(1)}, u32[]{:S(2)}, u32[]{:S(2)}) %collective-permute-start.7) | collective-permute-done | bytes 262176 | tf_op jit(solution)/shard_map/ppermute | solution.py:174
  35.4 0.2 fusion.12
  35.7 0.5 collective-permute-start.8
  36.3 1.8 %collective-permute-done.9 = f16[32,4096]{1,0:T(8,128)(2,1)S(1)} collective-permute-done((f16[32,4096]{1,0:T(8,128)(2,1)S(1)}, f16[32,4096]{1,0:T(8,128)(2,1)S(1)}, u32[]{:S(2)}, u32[]{:S(2)}) %collective-permute-start.9) | collective-permute-done | bytes 262176 | tf_op jit(solution)/shard_map/ppermute | solution.py:174
  38.4 0.6 collective-permute-start.10
  39.0 3.0 %collective-permute-done.8 = f16[32,2048]{1,0:T(8,128)(2,1)S(1)} collective-permute-done((f16[32,2048]{1,0:T(8,128)(2,1)S(1)}, f16[32,2048]{1,0:T(8,128)(2,1)S(1)}, u32[]{:S(2)}, u32[]{:S(2)}) %collective-permute-start.8) | collective-permute-done | bytes 131104 | tf_op jit(solution)/shard_map/ppermute | solution.py:174
  42.0 1.4 %collective-permute-done.10 = f16[32,2048]{1,0:T(8,128)(2,1)S(1)} collective-permute-done((f16[32,2048]{1,0:T(8,128)(2,1)S(1)}, f16[32,2048]{1,0:T(8,128)(2,1)S(1)}, u32[]{:S(2)}, u32[]{:S(2)}) %collective-permute-start.10) | collective-permute-done | bytes 131104 | tf_op jit(solution)/shard_map/ppermute | solution.py:174
  43.7 1.9 %collective-permute-start.17 = (f16[2,32,2048]{2,1,0:T(8,128)(2,1)S(1)}, f16[2,32,2048]{2,1,0:T(8,128)(2,1)S(1)}, u32[]{:S(2)}, u32[]{:S(2)}) collective-permute-start(f16[2,32,2048]{2,1,0:T(8,128)(2,1)S(1)} %multiply_convert_fusion.3), channel_id=1, source_target_pairs={{0,8},{1,9},{2,10},{3,11},{4,12},{5,13},{6,14},{7,15},{8,0},{9,1},... | collective-permute-start | bytes 786440 | tf_op jit(solution)/shard_map/ppermute | solution.py:174
  45.6 0.3 constant_dynamic-slice_fusion.3
  45.8 0.6 collective-permute-start.14
  46.5 0.6 collective-permute-start.12
  47.1 8.6 %collective-permute-done.17 = f16[2,32,2048]{2,1,0:T(8,128)(2,1)S(1)} collective-permute-done((f16[2,32,2048]{2,1,0:T(8,128)(2,1)S(1)}, f16[2,32,2048]{2,1,0:T(8,128)(2,1)S(1)}, u32[]{:S(2)}, u32[]{:S(2)}) %collective-permute-start.17) | collective-permute-done | bytes 262176 | tf_op jit(solution)/shard_map/ppermute | solution.py:174
  55.9 1.6 %collective-permute-done.12 = bf16[2,32,2048]{2,1,0:T(8,128)(2,1)S(1)} collective-permute-done((bf16[2,32,2048]{2,1,0:T(8,128)(2,1)S(1)}, bf16[2,32,2048]{2,1,0:T(8,128)(2,1)S(1)}, u32[]{:S(2)}, u32[]{:S(2)}) %collective-permute-start.12) | collective-permute-done | bytes 262176 | tf_op jit(solution)/shard_map/ppermute | solution.py:174
  57.6 2.6 %collective-permute-done.14 = bf16[160,2048]{1,0:T(8,128)(2,1)S(1)} collective-permute-done((bf16[160,2048]{1,0:T(8,128)(2,1)S(1)}, bf16[160,2048]{1,0:T(8,128)(2,1)S(1)}, u32[]{:S(2)}, u32[]{:S(2)}) %collective-permute-start.14) | collective-permute-done | bytes 655392 | tf_op jit(solution)/shard_map/ppermute | solution.py:174
  60.2 0.7 fusion.5.refs_0_
  61.0 1.3 %collective-permute-done.16 = bf16[160,2048]{1,0:T(8,128)(2,1)S(1)} collective-permute-done((bf16[160,2048]{1,0:T(8,128)(2,1)S(1)}, bf16[160,2048]{1,0:T(8,128)(2,1)S(1)}, u32[]{:S(2)}, u32[]{:S(2)}) %collective-permute-start.16) | collective-permute-done | bytes 655392 | tf_op jit(solution)/shard_map/ppermute | solution.py:174
  62.4 0.9 %fusion.41.refs_1_ = f32[512,128]{1,0:T(8,128)S(1)} fusion(bf16[512,2048]{1,0:T(8,128)(2,1)S(1)} %constant_dynamic-update-slice_fusion, bf16[128,2048]{1,0:T(8,128)(2,1)S(1)} %bitcast.31), kind=kOutput, calls=%fused_computation.84 | convolution fusion | flops 268435456 | bytes 2883584 | tf_op jit(solution)/shard_map/dot_general | solution.py:246
  63.4 0.7 fusion.42.refs_3_
  64.1 0.7 fusion.4.refs_2_
  64.9 1.9 %shard_map.75 = bf16[16,64,256]{2,1,0:T(8,128)(2,1)} custom-call(s32[16]{0:T(128)S(1)} %copy-done.1, f32[512,128]{1,0:T(8,128)S(1)} %fusion.5.refs_0_, f32[512,128]{1,0:T(8,128)S(1)} %fusion.41.refs_1_, f32[512,128]{1,0:T(8,128)S(1)} %fusion.4.refs_2_, f32[512,128]{1,0:T(8,128)S(1)} %fusion.42.refs_3_), custom_call_target="tpu_custom_call" | custom-call | flops 65536 | bytes 1572864 | tf_op jit(solution)/shard_map/pallas_call | solution.py:123
  66.8 3.6 %all-to-all-start = ((bf16[16,1,64,256]{3,2,1,0:T(8,128)(2,1)}), bf16[16,1,64,256]{3,2,1,0:T(8,128)(2,1)S(1)}, u32[]{:S(2)}, u32[]{:S(2)}) async-start(bf16[16,1,64,256]{3,2,1,0:T(8,128)(2,1)} %bitcast.10), calls=%async_computation | async-start | bytes 1048576 | tf_op jit(solution)/shard_map/all_to_all | solution.py:299
  70.5 0.6 dynamic_slice.79
  71.2 0.3 fusion.32
  71.5 0.6 constant_dynamic-slice_fusion.allowed_ref
  72.1 12.7 %all-to-all-done = bf16[16,1,64,256]{3,2,1,0:T(8,128)(2,1)S(1)} async-done(((bf16[16,1,64,256]{3,2,1,0:T(8,128)(2,1)}), bf16[16,1,64,256]{3,2,1,0:T(8,128)(2,1)S(1)}, u32[]{:S(2)}, u32[]{:S(2)}) %all-to-all-start) | async-done | bytes 524320 | tf_op jit(solution)/shard_map/all_to_all | solution.py:299
  84.8 0.9 %shard_map.76 = f32[1024,128]{1,0:T(8,128)} custom-call(bf16[16,1,4,16,256]{4,3,2,1,0:T(8,128)(2,1)S(1)} %bitcast.27, f32[1,512]{1,0:T(1,128)S(1)} %constant_dynamic-slice_fusion.allowed_ref), custom_call_target="tpu_custom_call" | custom-call | flops 262144 | bytes 1048576 | tf_op jit(solution)/shard_map/pallas_call | solution.py:152
  (53 shorter events, 3.6 us)
Async XLA Ops:
  0.0 1.7 %copy-start = (bf16[16,16,4096]{2,1,0:T(8,128)(2,1)S(1)}, bf16[16,16,4096]{2,1,0:T(8,128)(2,1)}, u32[]{:S(2)}) copy-start(bf16[16,16,4096]{2,1,0:T(8,128)(2,1)} %param.9) | copy-start | bytes 6291460
  1.9 45.2 %collective-permute-start.13 = (bf16[96,2048]{1,0:T(8,128)(2,1)S(1)}, bf16[96,2048]{1,0:T(8,128)(2,1)S(1)}, u32[]{:S(2)}, u32[]{:S(2)}) collective-permute-start(bf16[96,2048]{1,0:T(8,128)(2,1)S(1)} %constant_dynamic-slice_fusion.2), channel_id=1, source_target_pairs={{0,2},{1,3},{2,0},{3,1},{4,6},{5,7},{6,4},{7,5},{8,10},{9,11},{10,... | collective-permute-start | bytes 1179656 | tf_op jit(solution)/shard_map/ppermute | solution.py:174
  9.7 3.4 %collective-permute-start.1 = (f16[128,4096]{1,0:T(8,128)(2,1)S(1)}, f16[128,4096]{1,0:T(8,128)(2,1)S(1)}, u32[]{:S(2)}, u32[]{:S(2)}) collective-permute-start(f16[128,4096]{1,0:T(8,128)(2,1)S(1)} %multiply_convert_fusion.1), channel_id=1, source_target_pairs={{0,1},{1,0},{2,3},{3,2},{4,5},{5,4},{6,7},{7,6},{8,9},{9,8},{10,11... | collective-permute-start | bytes 3145736 | tf_op jit(solution)/shard_map/ppermute | solution.py:174
  10.2 6.1 %collective-permute-start.6 = (f16[128,4096]{1,0:T(8,128)(2,1)S(1)}, f16[128,4096]{1,0:T(8,128)(2,1)S(1)}, u32[]{:S(2)}, u32[]{:S(2)}) collective-permute-start(f16[128,4096]{1,0:T(8,128)(2,1)S(1)} %multiply_convert_fusion), channel_id=1, source_target_pairs={{0,1},{1,0},{2,3},{3,2},{4,5},{5,4},{6,7},{7,6},{8,9},{9,8},{10,11... | collective-permute-start | bytes 3145736 | tf_op jit(solution)/shard_map/ppermute | solution.py:174
  11.2 14.3 %collective-permute-start = (bf16[256,2048]{1,0:T(8,128)(2,1)S(1)}, bf16[256,2048]{1,0:T(8,128)(2,1)S(1)}, u32[]{:S(2)}, u32[]{:S(2)}) collective-permute-start(bf16[256,2048]{1,0:T(8,128)(2,1)S(1)} %constant_dynamic-slice_fusion.1), channel_id=1, source_target_pairs={{0,1},{1,0},{2,3},{3,2},{4,5},{5,4},{6,7},{7,6},{8,9},{9,8},{10,11... | collective-permute-start | bytes 3145736 | tf_op jit(solution)/shard_map/ppermute | solution.py:174
  13.9 8.8 %collective-permute-start.2 = (f16[64,2048]{1,0:T(8,128)(2,1)S(1)}, f16[64,2048]{1,0:T(8,128)(2,1)S(1)}, u32[]{:S(2)}, u32[]{:S(2)}) collective-permute-start(f16[64,2048]{1,0:T(8,128)(2,1)S(1)} %multiply_convert_fusion.7), channel_id=1, source_target_pairs={{0,2},{1,3},{2,0},{3,1},{4,6},{5,7},{6,4},{7,5},{8,10},{9,11},{10,... | collective-permute-start | bytes 786440 | tf_op jit(solution)/shard_map/ppermute | solution.py:174
  14.2 10.5 %collective-permute-start.4 = (f16[32,4096]{1,0:T(8,128)(2,1)S(1)}, f16[32,4096]{1,0:T(8,128)(2,1)S(1)}, u32[]{:S(2)}, u32[]{:S(2)}) collective-permute-start(f16[32,4096]{1,0:T(8,128)(2,1)S(1)} %multiply_convert_fusion.6), channel_id=1, source_target_pairs={{0,4},{1,5},{2,6},{3,7},{4,0},{5,1},{6,2},{7,3},{8,12},{9,13},{10,... | collective-permute-start | bytes 786440 | tf_op jit(solution)/shard_map/ppermute | solution.py:174
  23.0 5.2 %collective-permute-start.3 = (f16[32,2048]{1,0:T(8,128)(2,1)S(1)}, f16[32,2048]{1,0:T(8,128)(2,1)S(1)}, u32[]{:S(2)}, u32[]{:S(2)}) collective-permute-start(f16[32,2048]{1,0:T(8,128)(2,1)S(1)} %multiply_convert_fusion.11), channel_id=1, source_target_pairs={{0,4},{1,5},{2,6},{3,7},{4,0},{5,1},{6,2},{7,3},{8,12},{9,13},{10,... | collective-permute-start | bytes 393224 | tf_op jit(solution)/shard_map/ppermute | solution.py:174
  24.9 6.5 %collective-permute-start.5 = (f16[32,2048]{1,0:T(8,128)(2,1)S(1)}, f16[32,2048]{1,0:T(8,128)(2,1)S(1)}, u32[]{:S(2)}, u32[]{:S(2)}) collective-permute-start(f16[32,2048]{1,0:T(8,128)(2,1)S(1)} %multiply_convert_fusion.10), channel_id=1, source_target_pairs={{0,2},{1,3},{2,0},{3,1},{4,6},{5,7},{6,4},{7,5},{8,10},{9,11},{10,... | collective-permute-start | bytes 393224 | tf_op jit(solution)/shard_map/ppermute | solution.py:174
  25.5 9.9 %collective-permute-start.7 = (f16[64,2048]{1,0:T(8,128)(2,1)S(1)}, f16[64,2048]{1,0:T(8,128)(2,1)S(1)}, u32[]{:S(2)}, u32[]{:S(2)}) collective-permute-start(f16[64,2048]{1,0:T(8,128)(2,1)S(1)} %multiply_convert_fusion.5), channel_id=1, source_target_pairs={{0,2},{1,3},{2,0},{3,1},{4,6},{5,7},{6,4},{7,5},{8,10},{9,11},{10,... | collective-permute-start | bytes 786440 | tf_op jit(solution)/shard_map/ppermute | solution.py:174
  27.0 11.1 %collective-permute-start.9 = (f16[32,4096]{1,0:T(8,128)(2,1)S(1)}, f16[32,4096]{1,0:T(8,128)(2,1)S(1)}, u32[]{:S(2)}, u32[]{:S(2)}) collective-permute-start(f16[32,4096]{1,0:T(8,128)(2,1)S(1)} %multiply_convert_fusion.4), channel_id=1, source_target_pairs={{0,4},{1,5},{2,6},{3,7},{4,0},{5,1},{6,2},{7,3},{8,12},{9,13},{10,... | collective-permute-start | bytes 786440 | tf_op jit(solution)/shard_map/ppermute | solution.py:174
  31.7 14.7 %collective-permute-start.11 = (f16[2,32,2048]{2,1,0:T(8,128)(2,1)S(1)}, f16[2,32,2048]{2,1,0:T(8,128)(2,1)S(1)}, u32[]{:S(2)}, u32[]{:S(2)}) collective-permute-start(f16[2,32,2048]{2,1,0:T(8,128)(2,1)S(1)} %get-tuple-element.86), channel_id=1, source_target_pairs={{0,8},{1,9},{2,10},{3,11},{4,12},{5,13},{6,14},{7,15},{8,0},{9,1},... | collective-permute-start | bytes 786440 | tf_op jit(solution)/shard_map/ppermute | solution.py:174
  35.7 6.2 %collective-permute-start.8 = (f16[32,2048]{1,0:T(8,128)(2,1)S(1)}, f16[32,2048]{1,0:T(8,128)(2,1)S(1)}, u32[]{:S(2)}, u32[]{:S(2)}) collective-permute-start(f16[32,2048]{1,0:T(8,128)(2,1)S(1)} %multiply_convert_fusion.9), channel_id=1, source_target_pairs={{0,4},{1,5},{2,6},{3,7},{4,0},{5,1},{6,2},{7,3},{8,12},{9,13},{10,... | collective-permute-start | bytes 393224 | tf_op jit(solution)/shard_map/ppermute | solution.py:174
  38.4 5.0 %collective-permute-start.10 = (f16[32,2048]{1,0:T(8,128)(2,1)S(1)}, f16[32,2048]{1,0:T(8,128)(2,1)S(1)}, u32[]{:S(2)}, u32[]{:S(2)}) collective-permute-start(f16[32,2048]{1,0:T(8,128)(2,1)S(1)} %multiply_convert_fusion.8), channel_id=1, source_target_pairs={{0,2},{1,3},{2,0},{3,1},{4,6},{5,7},{6,4},{7,5},{8,10},{9,11},{10,... | collective-permute-start | bytes 393224 | tf_op jit(solution)/shard_map/ppermute | solution.py:174
  43.7 12.0 %collective-permute-start.17 = (f16[2,32,2048]{2,1,0:T(8,128)(2,1)S(1)}, f16[2,32,2048]{2,1,0:T(8,128)(2,1)S(1)}, u32[]{:S(2)}, u32[]{:S(2)}) collective-permute-start(f16[2,32,2048]{2,1,0:T(8,128)(2,1)S(1)} %multiply_convert_fusion.3), channel_id=1, source_target_pairs={{0,8},{1,9},{2,10},{3,11},{4,12},{5,13},{6,14},{7,15},{8,0},{9,1},... | collective-permute-start | bytes 786440 | tf_op jit(solution)/shard_map/ppermute | solution.py:174
  45.8 14.4 %collective-permute-start.14 = (bf16[160,2048]{1,0:T(8,128)(2,1)S(1)}, bf16[160,2048]{1,0:T(8,128)(2,1)S(1)}, u32[]{:S(2)}, u32[]{:S(2)}) collective-permute-start(bf16[160,2048]{1,0:T(8,128)(2,1)S(1)} %constant_dynamic-slice_fusion.3), channel_id=1, source_target_pairs={{0,2},{1,3},{2,0},{3,1},{4,6},{5,7},{6,4},{7,5},{8,10},{9,11},{10,... | collective-permute-start | bytes 1966088 | tf_op jit(solution)/shard_map/ppermute | solution.py:174
  46.5 10.9 %collective-permute-start.12 = (bf16[2,32,2048]{2,1,0:T(8,128)(2,1)S(1)}, bf16[2,32,2048]{2,1,0:T(8,128)(2,1)S(1)}, u32[]{:S(2)}, u32[]{:S(2)}) collective-permute-start(bf16[2,32,2048]{2,1,0:T(8,128)(2,1)S(1)} %fusion.17), channel_id=1, source_target_pairs={{0,4},{1,5},{2,6},{3,7},{4,0},{5,1},{6,2},{7,3},{8,12},{9,13},{10,... | collective-permute-start | bytes 786440 | tf_op jit(solution)/shard_map/ppermute | solution.py:174
  47.1 13.9 %collective-permute-start.15 = (bf16[96,2048]{1,0:T(8,128)(2,1)S(1)}, bf16[96,2048]{1,0:T(8,128)(2,1)S(1)}, u32[]{:S(2)}, u32[]{:S(2)}) collective-permute-start(bf16[96,2048]{1,0:T(8,128)(2,1)S(1)} %collective-permute-done.13), channel_id=1, source_target_pairs={{0,1},{1,0},{2,3},{3,2},{4,5},{5,4},{6,7},{7,6},{8,9},{9,8},{10,11... | collective-permute-start | bytes 1179656 | tf_op jit(solution)/shard_map/ppermute | solution.py:174
  55.8 7.4 %collective-permute-start.18 = (bf16[2,32,2048]{2,1,0:T(8,128)(2,1)S(1)}, bf16[2,32,2048]{2,1,0:T(8,128)(2,1)S(1)}, u32[]{:S(2)}, u32[]{:S(2)}) collective-permute-start(bf16[2,32,2048]{2,1,0:T(8,128)(2,1)S(1)} %fusion.20), channel_id=1, source_target_pairs={{0,4},{1,5},{2,6},{3,7},{4,0},{5,1},{6,2},{7,3},{8,12},{9,13},{10,... | collective-permute-start | bytes 786440 | tf_op jit(solution)/shard_map/ppermute | solution.py:174
  60.2 2.1 %collective-permute-start.16 = (bf16[160,2048]{1,0:T(8,128)(2,1)S(1)}, bf16[160,2048]{1,0:T(8,128)(2,1)S(1)}, u32[]{:S(2)}, u32[]{:S(2)}) collective-permute-start(bf16[160,2048]{1,0:T(8,128)(2,1)S(1)} %collective-permute-done.14), channel_id=1, source_target_pairs={{0,1},{1,0},{2,3},{3,2},{4,5},{5,4},{6,7},{7,6},{8,9},{9,8},{10,11... | collective-permute-start | bytes 1966088 | tf_op jit(solution)/shard_map/ppermute | solution.py:174
  64.1 0.8 copy-start.1
  64.9 5.5 %copy-start.2 = (s32[8,12]{1,0:T(8,128)S(1)}, s32[8,12]{1,0:T(8,128)}, u32[]{:S(2)}) copy-start(s32[8,12]{1,0:T(8,128)} %param.11) | copy-start | bytes 1156
  64.9 6.2 %copy-start.3 = (s32[8]{0:T(128)S(1)}, s32[8]{0:T(128)}, u32[]{:S(2)}) copy-start(s32[8]{0:T(128)} %param.12) | copy-start | bytes 100
  64.9 6.3 %copy-start.4 = (s32[512]{0:T(512)S(1)}, s32[512]{0:T(512)}, u32[]{:S(2)}) copy-start(s32[512]{0:T(512)} %param.10) | copy-start | bytes 6148
  66.8 18.0 %all-to-all-start = ((bf16[16,1,64,256]{3,2,1,0:T(8,128)(2,1)}), bf16[16,1,64,256]{3,2,1,0:T(8,128)(2,1)S(1)}, u32[]{:S(2)}, u32[]{:S(2)}) async-start(bf16[16,1,64,256]{3,2,1,0:T(8,128)(2,1)} %bitcast.10), calls=%async_computation | async-start | bytes 1048576 | tf_op jit(solution)/shard_map/all_to_all | solution.py:299

commit v18 on v17

--- a/solution.py
+++ b/solution.py
@@ -72,12 +72,11 @@
         multiply(left, high_ref[:, columns], low_ref[:, columns], outs, columns)
 
 
-def product(core, rows, columns, kernel, vmem):
+def product(core, rows, columns, kernel, vmem, pieces):
     nrows = rows.shape[0]
     depth, width = columns[0].shape
     block = min(512, width)
-    part = nrows // CORES // CHUNKS
-    out = [jax.ShapeDtypeStruct((part, width), jnp.float32)] * CHUNKS
+    out = [jax.ShapeDtypeStruct((nrows // CORES // pieces, width), jnp.float32)] * pieces
     in_vmem = pl.BlockSpec(memory_space=pltpu.VMEM)
     operand, scratch = in_vmem, []
     if kernel is other_kernel:
@@ -103,28 +102,41 @@
 
 
 def order_kernel(slots_ref, *refs):
-    raws, out_ref = refs[:-1], refs[-1]
+    raws, (out_hbm, staged_ref, sems) = refs[:-3], refs[-3:]
     nblocks = slots_ref.shape[0]
     groups = len(raws) // CHUNKS
-    for slot in range(nblocks):
-        for i, raw_ref in enumerate(raws):
-            examples, width = raw_ref.shape[0] // nblocks, raw_ref.shape[1]
-            chunk, group = divmod(i, groups)
-            rows = pl.ds(slots_ref[slot], examples, stride=nblocks)
-            out_ref[
-                slot, group * examples:(group + 1) * examples, chunk * width:(chunk + 1) * width
-            ] = raw_ref[rows, :].astype(out_ref.dtype)
+    parts = sems.shape[0]
+    size = nblocks // parts
+
+    def send(part):
+        slots = pl.ds(part * size, size)
+        return pltpu.make_async_copy(staged_ref.at[slots], out_hbm.at[slots], sems.at[part])
+
+    for part in range(parts):
+        for slot in range(part * size, (part + 1) * size):
+            for i, raw_ref in enumerate(raws):
+                examples, width = raw_ref.shape[0] // nblocks, raw_ref.shape[1]
+                chunk, group = divmod(i, groups)
+                rows = pl.ds(slots_ref[slot], examples, stride=nblocks)
+                staged_ref[
+                    slot, group * examples:(group + 1) * examples, chunk * width:(chunk + 1) * width
+                ] = raw_ref[rows, :].astype(staged_ref.dtype)
+        send(part).start()
+    for part in range(parts):
+        send(part).wait()
 
 
 def in_slot_order(raws, slots):
     nblocks = slots.shape[0]
     rows, width = raws[0].shape
     groups = len(raws) // CHUNKS
+    shape = (nblocks, groups * rows // nblocks, CHUNKS * width)
     return pl.pallas_call(
         order_kernel,
         in_specs=[pl.BlockSpec(memory_space=pltpu.SMEM)] + [pl.BlockSpec(memory_space=pltpu.VMEM)] * len(raws),
-        out_specs=pl.BlockSpec(memory_space=pltpu.VMEM),
-        out_shape=jax.ShapeDtypeStruct((nblocks, groups * rows // nblocks, CHUNKS * width), jnp.bfloat16),
+        out_specs=pl.BlockSpec(memory_space=pltpu.HBM),
+        out_shape=jax.ShapeDtypeStruct(shape, jnp.bfloat16),
+        scratch_shapes=[pltpu.VMEM(shape, jnp.bfloat16), pltpu.SemaphoreType.DMA((4,))],
         compiler_params=pltpu.CompilerParams(vmem_limit_bytes=4 * 1024 * 1024),
         cost_estimate=pl.CostEstimate(
             flops=rows * width, bytes_accessed=6 * len(raws) * rows * width, transcendentals=0
@@ -215,9 +227,8 @@
     def after(value, first):
         return lax.optimization_barrier((value, first))[0]
 
-    def paths(value, other):
-        value = value + unpack(other)
-        return [value[i * rows:(i + 1) * rows] for i in range(PATHS)]
+    def paths(values, other):
+        return [value + unpack(other[i * rows:(i + 1) * rows]) for i, value in enumerate(values)]
 
     levels = ((ybit, 1), (zbit, 0)), ((zbit, 0), (ybit, 1))
 
@@ -262,19 +273,20 @@
     other_core, blocks = after((other_core, blocks), early)
     early = swap(early, ybit)
 
-    *full, high, low = product(other_core, left, [precond], other_kernel, OTHER_VMEM)
-    sent = [pack(value) for value in full]
-    got = [swap(value, 0) for value in sent]
+    *full, high, low = product(other_core, left, [precond], other_kernel, OTHER_VMEM, CHUNKS)
+    sent = pack(full[0])
+    got = swap(sent, 0)
+    mine = product(after(core, sent), left, [high, low], mine_kernel, MINE_VMEM, CHUNKS * PATHS)
+    one = paths(mine[:PATHS], got)
+    sent = messages(one, 0)
+    got = swap(pack(after(full[1], mine[0])), 0)
+    two = paths(mine[PATHS:], after(got, sent))
     blocks = after(blocks, sent)
     near = features(blocks, 0, every, 0)
     sibling = swap(near, 0)
-    mine = product(after(core, sent), left, [high, low], mine_kernel, MINE_VMEM)
-    one = paths(mine[0], got[0])
-    sent = messages(one, 0)
-    two = paths(mine[1], after(got[1], sent))
     one = exchange(one, sent, 0)
     sent = messages(one, 1)
-    sent_two = after(messages(two, 0), (sent, sibling))
+    sent_two = after(messages(two, 0), (sent, early))
     one = halve(exchange(one, sent, 1))
     sent = pack(one)
     got_one = swap(sent, rest[-1])

time: 85.9 us -> 85.4 us (level)
  waiting for transfers between devices: 43.4 us -> 36.5 us
  starting transfers between devices: 20.6 us -> 27.3 us
    ppermute x19, waiting for transfers between devices: 30.7 us -> 23.8 us  [swap(): return lax.ppermute(value, 'rows', [(r, r ^ 1 << bit) for r in range(n)])]
    ppermute x19, starting transfers between devices: 17 us -> 22.1 us  [swap(): return lax.ppermute(value, 'rows', [(r, r ^ 1 << bit) for r in range(n)])]
    all_to_all x1, starting transfers between devices: 3.57 us -> 5.24 us  [shards(): lax.all_to_all(ordered, 'rows', split_axis=0, concat_axis=0, tiled=True)]
  transfers between devices with their start and end apart: 20 -> 20, of which waited for: 12 -> 12; matrix products, arithmetic and copies ran while one was open for 11% -> 10% of each run, Pallas kernels for 7% -> 7%
where the time goes in v18:
time: 85.4 us; the launch traced here: 85.1 us
  waiting for transfers between devices  36.5 us (43%)
  starting transfers between devices  27.3 us (32%)
  Pallas kernels  8.69 us (10%)
  other arithmetic  6.05 us (7%)
  matrix products  3.34 us (4%)
  local copies, waits for them, and re-layouts  2.78 us (3%)
    ppermute x19, waiting for transfers between devices, swap(): return lax.ppermute(value, 'rows', [(r, r ^ 1 << bit) for r in range(n)])  23.8 us
    ppermute x19, starting transfers between devices, swap(): return lax.ppermute(value, 'rows', [(r, r ^ 1 << bit) for r in range(n)])  22.1 us
    all_to_all x1, waiting for transfers between devices, shards(): lax.all_to_all(ordered, 'rows', split_axis=0, concat_axis=0, tiled=True)  12.7 us
    pallas_call x2, Pallas kernels, product(): pl.pallas_call(kernel, in_specs=[pl.BlockSpec(memory_space=pltpu.SMEM), i...  6.05 us
    all_to_all x1, starting transfers between devices, shards(): lax.all_to_all(ordered, 'rows', split_axis=0, concat_axis=0, tiled=True)  5.24 us
    dot_general x4, matrix products, scores(): lax.dot_general(group, value, (((1,), (1,)), ((), ())), preferred_element...  3.07 us
    convert_element_type x12, other arithmetic, pack(): return (value * lax.rsqrt(jnp.abs(value) + LEAST)).astype(jnp.float16)  2.4 us
    pallas_call x1, Pallas kernels, in_slot_order(): pl.pallas_call(order_kernel, in_specs=[pl.BlockSpec(memory_space=pltpu.SM...  1.78 us
  transfers between devices with their start and end apart: 20, of which 12 were waited for; matrix products, arithmetic and copies ran while one was open for 10% of the time, Pallas kernels for 7%

profile of v18, /device:TPU:0, one launch (start us, length us, event | category | flops | bytes accessed | tf_op | source)
XLA Modules:
  0.0 85.1 jit_solution(15409186452256042049)
XLA Ops:
  0.0 1.3 %fusion.10 = (bf16[512,256]{1,0:T(8,128)(2,1)S(1)}, bf16[512,256]{1,0:T(8,128)(2,1)S(1)}) fusion(f32[512,256]{1,0:T(8,128)} %param.7), kind=kLoop, calls=%fused_computation.26 | loop fusion | flops 524288 | bytes 1048576 | tf_op jit(solution)/shard_map/convert_element_type | solution.py:268
  1.3 0.4 copy-done
  1.9 3.0 %collective-permute-start.7 = (bf16[96,2048]{1,0:T(8,128)(2,1)S(1)}, bf16[96,2048]{1,0:T(8,128)(2,1)S(1)}, u32[]{:S(2)}, u32[]{:S(2)}) collective-permute-start(bf16[96,2048]{1,0:T(8,128)(2,1)S(1)} %constant_dynamic-slice_fusion.2), channel_id=1, source_target_pairs={{0,2},{1,3},{2,0},{3,1},{4,6},{5,7},{6,4},{7,5},{8,10},{9,11},{10,... | collective-permute-start | bytes 1179656 | tf_op jit(solution)/shard_map/ppermute | solution.py:186
  5.0 4.3 %shard_map.73 = (f32[128,4096]{1,0:T(8,128)S(1)}, f32[128,4096]{1,0:T(8,128)S(1)}, bf16[256,4096]{1,0:T(8,128)(2,1)S(1)}, bf16[256,4096]{1,0:T(8,128)(2,1)S(1)}) custom-call(s32[1]{0:T(128)} %bitcast.1.core_ref, bf16[512,768]{1,0:T(8,128)(2,1)S(1)} %pad_maximum_fusion.3.rows_ref, f32[256,4096]{1,0:T(8,128)} %columns_hbm.1), custom_call_target="tpu_custom_call" | custom-call | flops 1610612736 | bytes 8388608 | tf_op jit(solution)/shard_map/pallas_call | solution.py:89
  9.2 0.4 multiply_convert_fusion.1
  9.8 1.8 %shard_map.74 = (f32[64,4096]{1,0:T(8,128)S(1)}, f32[64,4096]{1,0:T(8,128)S(1)}, f32[64,4096]{1,0:T(8,128)S(1)}, f32[64,4096]{1,0:T(8,128)S(1)}) custom-call(s32[1]{0:T(128)} %bitcast.2.core_ref, bf16[512,768]{1,0:T(8,128)(2,1)S(1)} %pad_maximum_fusion.3.rows_ref, bf16[256,4096]{1,0:T(8,128)(2,1)S(1)} %get-tuple-element.51.high_ref, ...), custom_call_target="tpu_custom_call" | custom-call | flops 1610612736 | bytes 8388608 | tf_op jit(solution)/shard_map/pallas_call | solution.py:89
  11.6 0.4 multiply_convert_fusion
  12.0 0.6 collective-permute-start.6
  12.6 0.4 fusion.3
  12.9 0.2 multiply_convert_fusion.7
  13.4 2.1 %collective-permute-start.4 = (f16[32,4096]{1,0:T(8,128)(2,1)S(1)}, f16[32,4096]{1,0:T(8,128)(2,1)S(1)}, u32[]{:S(2)}, u32[]{:S(2)}) collective-permute-start(f16[32,4096]{1,0:T(8,128)(2,1)S(1)} %multiply_convert_fusion.6), channel_id=1, source_target_pairs={{0,4},{1,5},{2,6},{3,7},{4,0},{5,1},{6,2},{7,3},{8,12},{9,13},{10,... | collective-permute-start | bytes 786440 | tf_op jit(solution)/shard_map/ppermute | solution.py:186
  15.5 0.4 fusion.9
  16.1 0.4 constant_dynamic-slice_fusion.1
  16.6 0.2 multiply_convert_fusion.5
  16.8 4.7 %collective-permute-done.2 = f16[64,2048]{1,0:T(8,128)(2,1)S(1)} collective-permute-done((f16[64,2048]{1,0:T(8,128)(2,1)S(1)}, f16[64,2048]{1,0:T(8,128)(2,1)S(1)}, u32[]{:S(2)}, u32[]{:S(2)}) %collective-permute-start.2) | collective-permute-done | bytes 262176 | tf_op jit(solution)/shard_map/ppermute | solution.py:186
  21.8 1.6 %collective-permute-start.3 = (f16[32,2048]{1,0:T(8,128)(2,1)S(1)}, f16[32,2048]{1,0:T(8,128)(2,1)S(1)}, u32[]{:S(2)}, u32[]{:S(2)}) collective-permute-start(f16[32,2048]{1,0:T(8,128)(2,1)S(1)} %multiply_convert_fusion.11), channel_id=1, source_target_pairs={{0,4},{1,5},{2,6},{3,7},{4,0},{5,1},{6,2},{7,3},{8,12},{9,13},{10,... | collective-permute-start | bytes 393224 | tf_op jit(solution)/shard_map/ppermute | solution.py:186
  23.7 0.6 collective-permute-start.5
  24.3 1.5 %collective-permute-start.8 = (f16[64,2048]{1,0:T(8,128)(2,1)S(1)}, f16[64,2048]{1,0:T(8,128)(2,1)S(1)}, u32[]{:S(2)}, u32[]{:S(2)}) collective-permute-start(f16[64,2048]{1,0:T(8,128)(2,1)S(1)} %multiply_convert_fusion.5), channel_id=1, source_target_pairs={{0,2},{1,3},{2,0},{3,1},{4,6},{5,7},{6,4},{7,5},{8,10},{9,11},{10,... | collective-permute-start | bytes 786440 | tf_op jit(solution)/shard_map/ppermute | solution.py:186
  25.8 0.5 collective-permute-start.10
  26.3 0.8 collective-permute-done.3
  27.2 3.1 %collective-permute-done.5 = f16[32,2048]{1,0:T(8,128)(2,1)S(1)} collective-permute-done((f16[32,2048]{1,0:T(8,128)(2,1)S(1)}, f16[32,2048]{1,0:T(8,128)(2,1)S(1)}, u32[]{:S(2)}, u32[]{:S(2)}) %collective-permute-start.5) | collective-permute-done | bytes 131104 | tf_op jit(solution)/shard_map/ppermute | solution.py:186
  30.5 2.6 %collective-permute-start.12 = (f16[2,32,2048]{2,1,0:T(8,128)(2,1)S(1)}, f16[2,32,2048]{2,1,0:T(8,128)(2,1)S(1)}, u32[]{:S(2)}, u32[]{:S(2)}) collective-permute-start(f16[2,32,2048]{2,1,0:T(8,128)(2,1)S(1)} %get-tuple-element.92), channel_id=1, source_target_pairs={{0,8},{1,9},{2,10},{3,11},{4,12},{5,13},{6,14},{7,15},{8,0},{9,1},... | collective-permute-start | bytes 786440 | tf_op jit(solution)/shard_map/ppermute | solution.py:186
  33.1 0.5 collective-permute-done.8
  33.7 0.2 fusion.16
  34.0 0.5 collective-permute-start.9
  34.5 1.4 %collective-permute-done.10 = f16[32,4096]{1,0:T(8,128)(2,1)S(1)} collective-permute-done((f16[32,4096]{1,0:T(8,128)(2,1)S(1)}, f16[32,4096]{1,0:T(8,128)(2,1)S(1)}, u32[]{:S(2)}, u32[]{:S(2)}) %collective-permute-start.10) | collective-permute-done | bytes 262176 | tf_op jit(solution)/shard_map/ppermute | solution.py:186
  36.2 0.3 collective-permute-start.11
  36.5 3.9 %collective-permute-done.9 = f16[32,2048]{1,0:T(8,128)(2,1)S(1)} collective-permute-done((f16[32,2048]{1,0:T(8,128)(2,1)S(1)}, f16[32,2048]{1,0:T(8,128)(2,1)S(1)}, u32[]{:S(2)}, u32[]{:S(2)}) %collective-permute-start.9) | collective-permute-done | bytes 131104 | tf_op jit(solution)/shard_map/ppermute | solution.py:186
  40.5 0.7 collective-permute-done.11
  41.5 3.2 %collective-permute-start.17 = (f16[2,32,2048]{2,1,0:T(8,128)(2,1)S(1)}, f16[2,32,2048]{2,1,0:T(8,128)(2,1)S(1)}, u32[]{:S(2)}, u32[]{:S(2)}) collective-permute-start(f16[2,32,2048]{2,1,0:T(8,128)(2,1)S(1)} %multiply_convert_fusion.3), channel_id=1, source_target_pairs={{0,8},{1,9},{2,10},{3,11},{4,12},{5,13},{6,14},{7,15},{8,0},{9,1},... | collective-permute-start | bytes 786440 | tf_op jit(solution)/shard_map/ppermute | solution.py:186
  44.7 0.3 constant_dynamic-slice_fusion.3
  45.2 4.4 %collective-permute-start.13 = (bf16[2,32,2048]{2,1,0:T(8,128)(2,1)S(1)}, bf16[2,32,2048]{2,1,0:T(8,128)(2,1)S(1)}, u32[]{:S(2)}, u32[]{:S(2)}) collective-permute-start(bf16[2,32,2048]{2,1,0:T(8,128)(2,1)S(1)} %fusion.21), channel_id=1, source_target_pairs={{0,4},{1,5},{2,6},{3,7},{4,0},{5,1},{6,2},{7,3},{8,12},{9,13},{10,... | collective-permute-start | bytes 786440 | tf_op jit(solution)/shard_map/ppermute | solution.py:186
  49.7 3.9 %collective-permute-done.17 = f16[2,32,2048]{2,1,0:T(8,128)(2,1)S(1)} collective-permute-done((f16[2,32,2048]{2,1,0:T(8,128)(2,1)S(1)}, f16[2,32,2048]{2,1,0:T(8,128)(2,1)S(1)}, u32[]{:S(2)}, u32[]{:S(2)}) %collective-permute-start.17) | collective-permute-done | bytes 262176 | tf_op jit(solution)/shard_map/ppermute | solution.py:186
  53.7 0.7 collective-permute-start.18
  54.4 1.8 %collective-permute-done.13 = bf16[2,32,2048]{2,1,0:T(8,128)(2,1)S(1)} collective-permute-done((bf16[2,32,2048]{2,1,0:T(8,128)(2,1)S(1)}, bf16[2,32,2048]{2,1,0:T(8,128)(2,1)S(1)}, u32[]{:S(2)}, u32[]{:S(2)}) %collective-permute-start.13) | collective-permute-done | bytes 262176 | tf_op jit(solution)/shard_map/ppermute | solution.py:186
  56.4 1.7 %collective-permute-done.14 = bf16[160,2048]{1,0:T(8,128)(2,1)S(1)} collective-permute-done((bf16[160,2048]{1,0:T(8,128)(2,1)S(1)}, bf16[160,2048]{1,0:T(8,128)(2,1)S(1)}, u32[]{:S(2)}, u32[]{:S(2)}) %collective-permute-start.14) | collective-permute-done | bytes 655392 | tf_op jit(solution)/shard_map/ppermute | solution.py:186
  58.1 0.7 fusion.1.refs_0_
  58.9 1.3 %collective-permute-done.16 = bf16[160,2048]{1,0:T(8,128)(2,1)S(1)} collective-permute-done((bf16[160,2048]{1,0:T(8,128)(2,1)S(1)}, bf16[160,2048]{1,0:T(8,128)(2,1)S(1)}, u32[]{:S(2)}, u32[]{:S(2)}) %collective-permute-start.16) | collective-permute-done | bytes 655392 | tf_op jit(solution)/shard_map/ppermute | solution.py:186
  60.2 0.9 %fusion.43.refs_1_ = f32[512,128]{1,0:T(8,128)S(1)} fusion(bf16[512,2048]{1,0:T(8,128)(2,1)S(1)} %constant_dynamic-update-slice_fusion, bf16[128,2048]{1,0:T(8,128)(2,1)S(1)} %bitcast.31), kind=kOutput, calls=%fused_computation.88 | convolution fusion | flops 268435456 | bytes 2883584 | tf_op jit(solution)/shard_map/dot_general | solution.py:257
  61.2 0.7 fusion.44.refs_3_
  61.9 0.7 fusion.refs_2_
  62.7 1.8 %shard_map.75 = bf16[16,64,256]{2,1,0:T(8,128)(2,1)} custom-call(s32[16]{0:T(128)S(1)} %copy-done.1, f32[512,128]{1,0:T(8,128)S(1)} %fusion.1.refs_0_, f32[512,128]{1,0:T(8,128)S(1)} %fusion.43.refs_1_, f32[512,128]{1,0:T(8,128)S(1)} %fusion.refs_2_, f32[512,128]{1,0:T(8,128)S(1)} %fusion.44.refs_3_), custom_call_target="tpu_custom_call" | custom-call | flops 65536 | bytes 1572864 | tf_op jit(solution)/shard_map/pallas_call | solution.py:134
  64.5 5.2 %all-to-all-start = ((bf16[16,1,64,256]{3,2,1,0:T(8,128)(2,1)}), bf16[16,1,64,256]{3,2,1,0:T(8,128)(2,1)S(1)}, u32[]{:S(2)}, u32[]{:S(2)}) async-start(bf16[16,1,64,256]{3,2,1,0:T(8,128)(2,1)} %bitcast.10), calls=%async_computation | async-start | bytes 1048576 | tf_op jit(solution)/shard_map/all_to_all | solution.py:311
  69.9 0.6 dynamic_slice.79
  70.6 0.3 fusion.36
  70.9 0.6 constant_dynamic-slice_fusion.allowed_ref
  71.5 12.7 %all-to-all-done = bf16[16,1,64,256]{3,2,1,0:T(8,128)(2,1)S(1)} async-done(((bf16[16,1,64,256]{3,2,1,0:T(8,128)(2,1)}), bf16[16,1,64,256]{3,2,1,0:T(8,128)(2,1)S(1)}, u32[]{:S(2)}, u32[]{:S(2)}) %all-to-all-start) | async-done | bytes 524320 | tf_op jit(solution)/shard_map/all_to_all | solution.py:311
  84.2 0.9 %shard_map.76 = f32[1024,128]{1,0:T(8,128)} custom-call(bf16[16,1,4,16,256]{4,3,2,1,0:T(8,128)(2,1)S(1)} %bitcast.27, f32[1,512]{1,0:T(1,128)S(1)} %constant_dynamic-slice_fusion.allowed_ref), custom_call_target="tpu_custom_call" | custom-call | flops 262144 | bytes 1048576 | tf_op jit(solution)/shard_map/pallas_call | solution.py:164
  (51 shorter events, 3.3 us)
Async XLA Ops:
  0.0 1.7 %copy-start = (bf16[16,16,4096]{2,1,0:T(8,128)(2,1)S(1)}, bf16[16,16,4096]{2,1,0:T(8,128)(2,1)}, u32[]{:S(2)}) copy-start(bf16[16,16,4096]{2,1,0:T(8,128)(2,1)} %param.9) | copy-start | bytes 6291460
  1.9 22.4 %collective-permute-start.7 = (bf16[96,2048]{1,0:T(8,128)(2,1)S(1)}, bf16[96,2048]{1,0:T(8,128)(2,1)S(1)}, u32[]{:S(2)}, u32[]{:S(2)}) collective-permute-start(bf16[96,2048]{1,0:T(8,128)(2,1)S(1)} %constant_dynamic-slice_fusion.2), channel_id=1, source_target_pairs={{0,2},{1,3},{2,0},{3,1},{4,6},{5,7},{6,4},{7,5},{8,10},{9,11},{10,... | collective-permute-start | bytes 1179656 | tf_op jit(solution)/shard_map/ppermute | solution.py:186
  9.7 2.9 %collective-permute-start = (f16[128,4096]{1,0:T(8,128)(2,1)S(1)}, f16[128,4096]{1,0:T(8,128)(2,1)S(1)}, u32[]{:S(2)}, u32[]{:S(2)}) collective-permute-start(f16[128,4096]{1,0:T(8,128)(2,1)S(1)} %multiply_convert_fusion.1), channel_id=1, source_target_pairs={{0,1},{1,0},{2,3},{3,2},{4,5},{5,4},{6,7},{7,6},{8,9},{9,8},{10,11... | collective-permute-start | bytes 3145736 | tf_op jit(solution)/shard_map/ppermute | solution.py:186
  12.0 3.5 %collective-permute-start.6 = (f16[128,4096]{1,0:T(8,128)(2,1)S(1)}, f16[128,4096]{1,0:T(8,128)(2,1)S(1)}, u32[]{:S(2)}, u32[]{:S(2)}) collective-permute-start(f16[128,4096]{1,0:T(8,128)(2,1)S(1)} %multiply_convert_fusion), channel_id=1, source_target_pairs={{0,1},{1,0},{2,3},{3,2},{4,5},{5,4},{6,7},{7,6},{8,9},{9,8},{10,11... | collective-permute-start | bytes 3145736 | tf_op jit(solution)/shard_map/ppermute | solution.py:186
  13.2 8.3 %collective-permute-start.2 = (f16[64,2048]{1,0:T(8,128)(2,1)S(1)}, f16[64,2048]{1,0:T(8,128)(2,1)S(1)}, u32[]{:S(2)}, u32[]{:S(2)}) collective-permute-start(f16[64,2048]{1,0:T(8,128)(2,1)S(1)} %multiply_convert_fusion.7), channel_id=1, source_target_pairs={{0,2},{1,3},{2,0},{3,1},{4,6},{5,7},{6,4},{7,5},{8,10},{9,11},{10,... | collective-permute-start | bytes 786440 | tf_op jit(solution)/shard_map/ppermute | solution.py:186
  13.4 10.0 %collective-permute-start.4 = (f16[32,4096]{1,0:T(8,128)(2,1)S(1)}, f16[32,4096]{1,0:T(8,128)(2,1)S(1)}, u32[]{:S(2)}, u32[]{:S(2)}) collective-permute-start(f16[32,4096]{1,0:T(8,128)(2,1)S(1)} %multiply_convert_fusion.6), channel_id=1, source_target_pairs={{0,4},{1,5},{2,6},{3,7},{4,0},{5,1},{6,2},{7,3},{8,12},{9,13},{10,... | collective-permute-start | bytes 786440 | tf_op jit(solution)/shard_map/ppermute | solution.py:186
  16.5 41.6 %collective-permute-start.1 = (bf16[256,2048]{1,0:T(8,128)(2,1)S(1)}, bf16[256,2048]{1,0:T(8,128)(2,1)S(1)}, u32[]{:S(2)}, u32[]{:S(2)}) collective-permute-start(bf16[256,2048]{1,0:T(8,128)(2,1)S(1)} %constant_dynamic-slice_fusion.1), channel_id=1, source_target_pairs={{0,1},{1,0},{2,3},{3,2},{4,5},{5,4},{6,7},{7,6},{8,9},{9,8},{10,11... | collective-permute-start | bytes 3145736 | tf_op jit(solution)/shard_map/ppermute | solution.py:186
  21.8 5.3 %collective-permute-start.3 = (f16[32,2048]{1,0:T(8,128)(2,1)S(1)}, f16[32,2048]{1,0:T(8,128)(2,1)S(1)}, u32[]{:S(2)}, u32[]{:S(2)}) collective-permute-start(f16[32,2048]{1,0:T(8,128)(2,1)S(1)} %multiply_convert_fusion.11), channel_id=1, source_target_pairs={{0,4},{1,5},{2,6},{3,7},{4,0},{5,1},{6,2},{7,3},{8,12},{9,13},{10,... | collective-permute-start | bytes 393224 | tf_op jit(solution)/shard_map/ppermute | solution.py:186
  23.7 6.5 %collective-permute-start.5 = (f16[32,2048]{1,0:T(8,128)(2,1)S(1)}, f16[32,2048]{1,0:T(8,128)(2,1)S(1)}, u32[]{:S(2)}, u32[]{:S(2)}) collective-permute-start(f16[32,2048]{1,0:T(8,128)(2,1)S(1)} %multiply_convert_fusion.10), channel_id=1, source_target_pairs={{0,2},{1,3},{2,0},{3,1},{4,6},{5,7},{6,4},{7,5},{8,10},{9,11},{10,... | collective-permute-start | bytes 393224 | tf_op jit(solution)/shard_map/ppermute | solution.py:186
  24.3 9.4 %collective-permute-start.8 = (f16[64,2048]{1,0:T(8,128)(2,1)S(1)}, f16[64,2048]{1,0:T(8,128)(2,1)S(1)}, u32[]{:S(2)}, u32[]{:S(2)}) collective-permute-start(f16[64,2048]{1,0:T(8,128)(2,1)S(1)} %multiply_convert_fusion.5), channel_id=1, source_target_pairs={{0,2},{1,3},{2,0},{3,1},{4,6},{5,7},{6,4},{7,5},{8,10},{9,11},{10,... | collective-permute-start | bytes 786440 | tf_op jit(solution)/shard_map/ppermute | solution.py:186
  25.8 10.1 %collective-permute-start.10 = (f16[32,4096]{1,0:T(8,128)(2,1)S(1)}, f16[32,4096]{1,0:T(8,128)(2,1)S(1)}, u32[]{:S(2)}, u32[]{:S(2)}) collective-permute-start(f16[32,4096]{1,0:T(8,128)(2,1)S(1)} %multiply_convert_fusion.4), channel_id=1, source_target_pairs={{0,4},{1,5},{2,6},{3,7},{4,0},{5,1},{6,2},{7,3},{8,12},{9,13},{10,... | collective-permute-start | bytes 786440 | tf_op jit(solution)/shard_map/ppermute | solution.py:186
  30.5 14.6 %collective-permute-start.12 = (f16[2,32,2048]{2,1,0:T(8,128)(2,1)S(1)}, f16[2,32,2048]{2,1,0:T(8,128)(2,1)S(1)}, u32[]{:S(2)}, u32[]{:S(2)}) collective-permute-start(f16[2,32,2048]{2,1,0:T(8,128)(2,1)S(1)} %get-tuple-element.92), channel_id=1, source_target_pairs={{0,8},{1,9},{2,10},{3,11},{4,12},{5,13},{6,14},{7,15},{8,0},{9,1},... | collective-permute-start | bytes 786440 | tf_op jit(solution)/shard_map/ppermute | solution.py:186
  34.0 6.4 %collective-permute-start.9 = (f16[32,2048]{1,0:T(8,128)(2,1)S(1)}, f16[32,2048]{1,0:T(8,128)(2,1)S(1)}, u32[]{:S(2)}, u32[]{:S(2)}) collective-permute-start(f16[32,2048]{1,0:T(8,128)(2,1)S(1)} %multiply_convert_fusion.9), channel_id=1, source_target_pairs={{0,4},{1,5},{2,6},{3,7},{4,0},{5,1},{6,2},{7,3},{8,12},{9,13},{10,... | collective-permute-start | bytes 393224 | tf_op jit(solution)/shard_map/ppermute | solution.py:186
  36.2 5.0 %collective-permute-start.11 = (f16[32,2048]{1,0:T(8,128)(2,1)S(1)}, f16[32,2048]{1,0:T(8,128)(2,1)S(1)}, u32[]{:S(2)}, u32[]{:S(2)}) collective-permute-start(f16[32,2048]{1,0:T(8,128)(2,1)S(1)} %multiply_convert_fusion.8), channel_id=1, source_target_pairs={{0,2},{1,3},{2,0},{3,1},{4,6},{5,7},{6,4},{7,5},{8,10},{9,11},{10,... | collective-permute-start | bytes 393224 | tf_op jit(solution)/shard_map/ppermute | solution.py:186
  41.5 12.1 %collective-permute-start.17 = (f16[2,32,2048]{2,1,0:T(8,128)(2,1)S(1)}, f16[2,32,2048]{2,1,0:T(8,128)(2,1)S(1)}, u32[]{:S(2)}, u32[]{:S(2)}) collective-permute-start(f16[2,32,2048]{2,1,0:T(8,128)(2,1)S(1)} %multiply_convert_fusion.3), channel_id=1, source_target_pairs={{0,8},{1,9},{2,10},{3,11},{4,12},{5,13},{6,14},{7,15},{8,0},{9,1},... | collective-permute-start | bytes 786440 | tf_op jit(solution)/shard_map/ppermute | solution.py:186
  45.0 13.1 %collective-permute-start.14 = (bf16[160,2048]{1,0:T(8,128)(2,1)S(1)}, bf16[160,2048]{1,0:T(8,128)(2,1)S(1)}, u32[]{:S(2)}, u32[]{:S(2)}) collective-permute-start(bf16[160,2048]{1,0:T(8,128)(2,1)S(1)} %constant_dynamic-slice_fusion.3), channel_id=1, source_target_pairs={{0,2},{1,3},{2,0},{3,1},{4,6},{5,7},{6,4},{7,5},{8,10},{9,11},{10,... | collective-permute-start | bytes 1966088 | tf_op jit(solution)/shard_map/ppermute | solution.py:186
  45.2 11.1 %collective-permute-start.13 = (bf16[2,32,2048]{2,1,0:T(8,128)(2,1)S(1)}, bf16[2,32,2048]{2,1,0:T(8,128)(2,1)S(1)}, u32[]{:S(2)}, u32[]{:S(2)}) collective-permute-start(bf16[2,32,2048]{2,1,0:T(8,128)(2,1)S(1)} %fusion.21), channel_id=1, source_target_pairs={{0,4},{1,5},{2,6},{3,7},{4,0},{5,1},{6,2},{7,3},{8,12},{9,13},{10,... | collective-permute-start | bytes 786440 | tf_op jit(solution)/shard_map/ppermute | solution.py:186
  49.6 9.2 %collective-permute-start.15 = (bf16[96,2048]{1,0:T(8,128)(2,1)S(1)}, bf16[96,2048]{1,0:T(8,128)(2,1)S(1)}, u32[]{:S(2)}, u32[]{:S(2)}) collective-permute-start(bf16[96,2048]{1,0:T(8,128)(2,1)S(1)} %collective-permute-done.7), channel_id=1, source_target_pairs={{0,1},{1,0},{2,3},{3,2},{4,5},{5,4},{6,7},{7,6},{8,9},{9,8},{10,11... | collective-permute-start | bytes 1179656 | tf_op jit(solution)/shard_map/ppermute | solution.py:186
  53.7 7.4 %collective-permute-start.18 = (bf16[2,32,2048]{2,1,0:T(8,128)(2,1)S(1)}, bf16[2,32,2048]{2,1,0:T(8,128)(2,1)S(1)}, u32[]{:S(2)}, u32[]{:S(2)}) collective-permute-start(bf16[2,32,2048]{2,1,0:T(8,128)(2,1)S(1)} %fusion.24), channel_id=1, source_target_pairs={{0,4},{1,5},{2,6},{3,7},{4,0},{5,1},{6,2},{7,3},{8,12},{9,13},{10,... | collective-permute-start | bytes 786440 | tf_op jit(solution)/shard_map/ppermute | solution.py:186
  58.0 2.1 %collective-permute-start.16 = (bf16[160,2048]{1,0:T(8,128)(2,1)S(1)}, bf16[160,2048]{1,0:T(8,128)(2,1)S(1)}, u32[]{:S(2)}, u32[]{:S(2)}) collective-permute-start(bf16[160,2048]{1,0:T(8,128)(2,1)S(1)} %collective-permute-done.14), channel_id=1, source_target_pairs={{0,1},{1,0},{2,3},{3,2},{4,5},{5,4},{6,7},{7,6},{8,9},{9,8},{10,11... | collective-permute-start | bytes 1966088 | tf_op jit(solution)/shard_map/ppermute | solution.py:186
  61.9 0.8 copy-start.1
  62.7 7.1 %copy-start.2 = (s32[8,12]{1,0:T(8,128)S(1)}, s32[8,12]{1,0:T(8,128)}, u32[]{:S(2)}) copy-start(s32[8,12]{1,0:T(8,128)} %param.11) | copy-start | bytes 1156
  62.7 7.8 %copy-start.3 = (s32[8]{0:T(128)S(1)}, s32[8]{0:T(128)}, u32[]{:S(2)}) copy-start(s32[8]{0:T(128)} %param.12) | copy-start | bytes 100
  62.7 7.9 %copy-start.4 = (s32[512]{0:T(512)S(1)}, s32[512]{0:T(512)}, u32[]{:S(2)}) copy-start(s32[512]{0:T(512)} %param.10) | copy-start | bytes 6148
  64.5 19.7 %all-to-all-start = ((bf16[16,1,64,256]{3,2,1,0:T(8,128)(2,1)}), bf16[16,1,64,256]{3,2,1,0:T(8,128)(2,1)S(1)}, u32[]{:S(2)}, u32[]{:S(2)}) async-start(bf16[16,1,64,256]{3,2,1,0:T(8,128)(2,1)} %bitcast.10), calls=%async_computation | async-start | bytes 1048576 | tf_op jit(solution)/shard_map/all_to_all | solution.py:311

commit v19 on v18

--- a/solution.py
+++ b/solution.py
@@ -258,7 +258,7 @@
 
     blocks = train.reshape(examples * nblocks, width)
     every = examples * nblocks
-    middle = max(1, examples * 3 // 8) * nblocks
+    middle = max(1, examples * 7 // 16) * nblocks
 
     def features(blocks, first, count, other):
         start = offsets[ybit, width // 2][other]

time: 85.4 us -> 85.7 us (level)
  starting transfers between devices: 27.3 us -> 28.8 us
  waiting for transfers between devices: 36.5 us -> 35.4 us
    ppermute x19, starting transfers between devices: 22.1 us -> 23.2 us  [swap(): return lax.ppermute(value, 'rows', [(r, r ^ 1 << bit) for r in range(n)])]
    ppermute x19, waiting for transfers between devices: 23.8 us -> 22.7 us  [swap(): return lax.ppermute(value, 'rows', [(r, r ^ 1 << bit) for r in range(n)])]
where the time goes in v19:
time: 85.7 us; the launch traced here: 85.5 us
  waiting for transfers between devices  35.4 us (41%)
  starting transfers between devices  28.8 us (34%)
  Pallas kernels  8.67 us (10%)
  other arithmetic  6.04 us (7%)
  matrix products  3.34 us (4%)
  local copies, waits for them, and re-layouts  2.77 us (3%)
    ppermute x19, starting transfers between devices, swap(): return lax.ppermute(value, 'rows', [(r, r ^ 1 << bit) for r in range(n)])  23.2 us
    ppermute x19, waiting for transfers between devices, swap(): return lax.ppermute(value, 'rows', [(r, r ^ 1 << bit) for r in range(n)])  22.7 us
    all_to_all x1, waiting for transfers between devices, shards(): lax.all_to_all(ordered, 'rows', split_axis=0, concat_axis=0, tiled=True)  12.7 us
    pallas_call x2, Pallas kernels, product(): pl.pallas_call(kernel, in_specs=[pl.BlockSpec(memory_space=pltpu.SMEM), i...  6.03 us
    all_to_all x1, starting transfers between devices, shards(): lax.all_to_all(ordered, 'rows', split_axis=0, concat_axis=0, tiled=True)  5.58 us
    dot_general x4, matrix products, scores(): lax.dot_general(group, value, (((1,), (1,)), ((), ())), preferred_element...  3.08 us
    convert_element_type x12, other arithmetic, pack(): return (value * lax.rsqrt(jnp.abs(value) + LEAST)).astype(jnp.float16)  2.39 us
    pallas_call x1, Pallas kernels, in_slot_order(): pl.pallas_call(order_kernel, in_specs=[pl.BlockSpec(memory_space=pltpu.SM...  1.78 us
  transfers between devices with their start and end apart: 20, of which 12 were waited for; matrix products, arithmetic and copies ran while one was open for 10% of the time, Pallas kernels for 7%

profile of v19, /device:TPU:0, one launch (start us, length us, event | category | flops | bytes accessed | tf_op | source)
XLA Modules:
  0.0 85.5 jit_solution(413529377004193154)
XLA Ops:
  0.0 1.3 %fusion.10 = (bf16[512,256]{1,0:T(8,128)(2,1)S(1)}, bf16[512,256]{1,0:T(8,128)(2,1)S(1)}) fusion(f32[512,256]{1,0:T(8,128)} %param.7), kind=kLoop, calls=%fused_computation.26 | loop fusion | flops 524288 | bytes 1048576 | tf_op jit(solution)/shard_map/convert_element_type | solution.py:268
  1.3 0.4 copy-done
  1.9 3.0 %collective-permute-start.7 = (bf16[112,2048]{1,0:T(8,128)(2,1)S(1)}, bf16[112,2048]{1,0:T(8,128)(2,1)S(1)}, u32[]{:S(2)}, u32[]{:S(2)}) collective-permute-start(bf16[112,2048]{1,0:T(8,128)(2,1)S(1)} %constant_dynamic-slice_fusion.2), channel_id=1, source_target_pairs={{0,2},{1,3},{2,0},{3,1},{4,6},{5,7},{6,4},{7,5},{8,10},{9,11},{10,... | collective-permute-start | bytes 1376264 | tf_op jit(solution)/shard_map/ppermute | solution.py:186
  5.0 4.2 %shard_map.73 = (f32[128,4096]{1,0:T(8,128)S(1)}, f32[128,4096]{1,0:T(8,128)S(1)}, bf16[256,4096]{1,0:T(8,128)(2,1)S(1)}, bf16[256,4096]{1,0:T(8,128)(2,1)S(1)}) custom-call(s32[1]{0:T(128)} %bitcast.1.core_ref, bf16[512,768]{1,0:T(8,128)(2,1)S(1)} %pad_maximum_fusion.3.rows_ref, f32[256,4096]{1,0:T(8,128)} %columns_hbm.1), custom_call_target="tpu_custom_call" | custom-call | flops 1610612736 | bytes 8388608 | tf_op jit(solution)/shard_map/pallas_call | solution.py:89
  9.2 0.4 multiply_convert_fusion.1
  9.8 1.8 %shard_map.74 = (f32[64,4096]{1,0:T(8,128)S(1)}, f32[64,4096]{1,0:T(8,128)S(1)}, f32[64,4096]{1,0:T(8,128)S(1)}, f32[64,4096]{1,0:T(8,128)S(1)}) custom-call(s32[1]{0:T(128)} %bitcast.2.core_ref, bf16[512,768]{1,0:T(8,128)(2,1)S(1)} %pad_maximum_fusion.3.rows_ref, bf16[256,4096]{1,0:T(8,128)(2,1)S(1)} %get-tuple-element.51.high_ref, ...), custom_call_target="tpu_custom_call" | custom-call | flops 1610612736 | bytes 8388608 | tf_op jit(solution)/shard_map/pallas_call | solution.py:89
  11.6 0.4 multiply_convert_fusion
  12.0 0.6 collective-permute-start.6
  12.6 0.4 fusion.3
  13.0 0.2 multiply_convert_fusion.7
  13.4 2.1 %collective-permute-start.4 = (f16[32,4096]{1,0:T(8,128)(2,1)S(1)}, f16[32,4096]{1,0:T(8,128)(2,1)S(1)}, u32[]{:S(2)}, u32[]{:S(2)}) collective-permute-start(f16[32,4096]{1,0:T(8,128)(2,1)S(1)} %multiply_convert_fusion.6), channel_id=1, source_target_pairs={{0,4},{1,5},{2,6},{3,7},{4,0},{5,1},{6,2},{7,3},{8,12},{9,13},{10,... | collective-permute-start | bytes 786440 | tf_op jit(solution)/shard_map/ppermute | solution.py:186
  15.5 0.4 fusion.9
  16.1 0.4 constant_dynamic-slice_fusion.1
  16.6 0.2 multiply_convert_fusion.5
  16.8 4.7 %collective-permute-done.2 = f16[64,2048]{1,0:T(8,128)(2,1)S(1)} collective-permute-done((f16[64,2048]{1,0:T(8,128)(2,1)S(1)}, f16[64,2048]{1,0:T(8,128)(2,1)S(1)}, u32[]{:S(2)}, u32[]{:S(2)}) %collective-permute-start.2) | collective-permute-done | bytes 262176 | tf_op jit(solution)/shard_map/ppermute | solution.py:186
  21.8 1.6 %collective-permute-start.3 = (f16[32,2048]{1,0:T(8,128)(2,1)S(1)}, f16[32,2048]{1,0:T(8,128)(2,1)S(1)}, u32[]{:S(2)}, u32[]{:S(2)}) collective-permute-start(f16[32,2048]{1,0:T(8,128)(2,1)S(1)} %multiply_convert_fusion.11), channel_id=1, source_target_pairs={{0,4},{1,5},{2,6},{3,7},{4,0},{5,1},{6,2},{7,3},{8,12},{9,13},{10,... | collective-permute-start | bytes 393224 | tf_op jit(solution)/shard_map/ppermute | solution.py:186
  23.7 1.4 %collective-permute-start.5 = (f16[32,2048]{1,0:T(8,128)(2,1)S(1)}, f16[32,2048]{1,0:T(8,128)(2,1)S(1)}, u32[]{:S(2)}, u32[]{:S(2)}) collective-permute-start(f16[32,2048]{1,0:T(8,128)(2,1)S(1)} %multiply_convert_fusion.10), channel_id=1, source_target_pairs={{0,2},{1,3},{2,0},{3,1},{4,6},{5,7},{6,4},{7,5},{8,10},{9,11},{10,... | collective-permute-start | bytes 393224 | tf_op jit(solution)/shard_map/ppermute | solution.py:186
  25.2 0.6 collective-permute-start.8
  25.8 0.4 collective-permute-start.10
  26.3 0.8 collective-permute-done.3
  27.2 3.0 %collective-permute-done.5 = f16[32,2048]{1,0:T(8,128)(2,1)S(1)} collective-permute-done((f16[32,2048]{1,0:T(8,128)(2,1)S(1)}, f16[32,2048]{1,0:T(8,128)(2,1)S(1)}, u32[]{:S(2)}, u32[]{:S(2)}) %collective-permute-start.5) | collective-permute-done | bytes 131104 | tf_op jit(solution)/shard_map/ppermute | solution.py:186
  30.5 2.7 %collective-permute-start.12 = (f16[2,32,2048]{2,1,0:T(8,128)(2,1)S(1)}, f16[2,32,2048]{2,1,0:T(8,128)(2,1)S(1)}, u32[]{:S(2)}, u32[]{:S(2)}) collective-permute-start(f16[2,32,2048]{2,1,0:T(8,128)(2,1)S(1)} %get-tuple-element.92), channel_id=1, source_target_pairs={{0,8},{1,9},{2,10},{3,11},{4,12},{5,13},{6,14},{7,15},{8,0},{9,1},... | collective-permute-start | bytes 786440 | tf_op jit(solution)/shard_map/ppermute | solution.py:186
  33.2 0.5 collective-permute-done.8
  34.0 0.5 collective-permute-start.9
  34.5 1.3 %collective-permute-done.10 = f16[32,4096]{1,0:T(8,128)(2,1)S(1)} collective-permute-done((f16[32,4096]{1,0:T(8,128)(2,1)S(1)}, f16[32,4096]{1,0:T(8,128)(2,1)S(1)}, u32[]{:S(2)}, u32[]{:S(2)}) %collective-permute-start.10) | collective-permute-done | bytes 262176 | tf_op jit(solution)/shard_map/ppermute | solution.py:186
  36.1 1.2 %collective-permute-start.11 = (f16[32,2048]{1,0:T(8,128)(2,1)S(1)}, f16[32,2048]{1,0:T(8,128)(2,1)S(1)}, u32[]{:S(2)}, u32[]{:S(2)}) collective-permute-start(f16[32,2048]{1,0:T(8,128)(2,1)S(1)} %multiply_convert_fusion.8), channel_id=1, source_target_pairs={{0,2},{1,3},{2,0},{3,1},{4,6},{5,7},{6,4},{7,5},{8,10},{9,11},{10,... | collective-permute-start | bytes 393224 | tf_op jit(solution)/shard_map/ppermute | solution.py:186
  37.3 3.1 %collective-permute-done.9 = f16[32,2048]{1,0:T(8,128)(2,1)S(1)} collective-permute-done((f16[32,2048]{1,0:T(8,128)(2,1)S(1)}, f16[32,2048]{1,0:T(8,128)(2,1)S(1)}, u32[]{:S(2)}, u32[]{:S(2)}) %collective-permute-start.9) | collective-permute-done | bytes 131104 | tf_op jit(solution)/shard_map/ppermute | solution.py:186
  40.5 0.6 collective-permute-done.11
  41.4 3.6 %collective-permute-start.17 = (f16[2,32,2048]{2,1,0:T(8,128)(2,1)S(1)}, f16[2,32,2048]{2,1,0:T(8,128)(2,1)S(1)}, u32[]{:S(2)}, u32[]{:S(2)}) collective-permute-start(f16[2,32,2048]{2,1,0:T(8,128)(2,1)S(1)} %multiply_convert_fusion.3), channel_id=1, source_target_pairs={{0,8},{1,9},{2,10},{3,11},{4,12},{5,13},{6,14},{7,15},{8,0},{9,1},... | collective-permute-start | bytes 786440 | tf_op jit(solution)/shard_map/ppermute | solution.py:186
  45.0 0.2 constant_dynamic-slice_fusion.3
  45.2 0.5 collective-permute-start.14
  45.8 3.9 %collective-permute-start.13 = (bf16[2,32,2048]{2,1,0:T(8,128)(2,1)S(1)}, bf16[2,32,2048]{2,1,0:T(8,128)(2,1)S(1)}, u32[]{:S(2)}, u32[]{:S(2)}) collective-permute-start(bf16[2,32,2048]{2,1,0:T(8,128)(2,1)S(1)} %fusion.21), channel_id=1, source_target_pairs={{0,4},{1,5},{2,6},{3,7},{4,0},{5,1},{6,2},{7,3},{8,12},{9,13},{10,... | collective-permute-start | bytes 786440 | tf_op jit(solution)/shard_map/ppermute | solution.py:186
  49.7 3.8 %collective-permute-done.17 = f16[2,32,2048]{2,1,0:T(8,128)(2,1)S(1)} collective-permute-done((f16[2,32,2048]{2,1,0:T(8,128)(2,1)S(1)}, f16[2,32,2048]{2,1,0:T(8,128)(2,1)S(1)}, u32[]{:S(2)}, u32[]{:S(2)}) %collective-permute-start.17) | collective-permute-done | bytes 262176 | tf_op jit(solution)/shard_map/ppermute | solution.py:186
  53.7 0.7 collective-permute-start.18
  54.4 2.9 %collective-permute-done.13 = bf16[2,32,2048]{2,1,0:T(8,128)(2,1)S(1)} collective-permute-done((bf16[2,32,2048]{2,1,0:T(8,128)(2,1)S(1)}, bf16[2,32,2048]{2,1,0:T(8,128)(2,1)S(1)}, u32[]{:S(2)}, u32[]{:S(2)}) %collective-permute-start.13) | collective-permute-done | bytes 262176 | tf_op jit(solution)/shard_map/ppermute | solution.py:186
  57.5 0.7 fusion.1.refs_0_
  58.4 1.2 %collective-permute-done.16 = bf16[144,2048]{1,0:T(8,128)(2,1)S(1)} collective-permute-done((bf16[144,2048]{1,0:T(8,128)(2,1)S(1)}, bf16[144,2048]{1,0:T(8,128)(2,1)S(1)}, u32[]{:S(2)}, u32[]{:S(2)}) %collective-permute-start.16) | collective-permute-done | bytes 589856 | tf_op jit(solution)/shard_map/ppermute | solution.py:186
  59.6 0.9 %fusion.43.refs_1_ = f32[512,128]{1,0:T(8,128)S(1)} fusion(bf16[512,2048]{1,0:T(8,128)(2,1)S(1)} %constant_dynamic-update-slice_fusion, bf16[128,2048]{1,0:T(8,128)(2,1)S(1)} %bitcast.31), kind=kOutput, calls=%fused_computation.88 | convolution fusion | flops 268435456 | bytes 2883584 | tf_op jit(solution)/shard_map/dot_general | solution.py:257
  60.5 0.7 collective-permute-done.18
  61.2 0.7 fusion.44.refs_3_
  62.0 0.7 fusion.refs_2_
  62.8 1.8 %shard_map.75 = bf16[16,64,256]{2,1,0:T(8,128)(2,1)} custom-call(s32[16]{0:T(128)S(1)} %copy-done.1, f32[512,128]{1,0:T(8,128)S(1)} %fusion.1.refs_0_, f32[512,128]{1,0:T(8,128)S(1)} %fusion.43.refs_1_, f32[512,128]{1,0:T(8,128)S(1)} %fusion.refs_2_, f32[512,128]{1,0:T(8,128)S(1)} %fusion.44.refs_3_), custom_call_target="tpu_custom_call" | custom-call | flops 65536 | bytes 1572864 | tf_op jit(solution)/shard_map/pallas_call | solution.py:134
  64.5 5.6 %all-to-all-start = ((bf16[16,1,64,256]{3,2,1,0:T(8,128)(2,1)}), bf16[16,1,64,256]{3,2,1,0:T(8,128)(2,1)S(1)}, u32[]{:S(2)}, u32[]{:S(2)}) async-start(bf16[16,1,64,256]{3,2,1,0:T(8,128)(2,1)} %bitcast.10), calls=%async_computation | async-start | bytes 1048576 | tf_op jit(solution)/shard_map/all_to_all | solution.py:311
  70.2 0.6 dynamic_slice.79
  71.0 0.3 fusion.36
  71.2 0.6 constant_dynamic-slice_fusion.allowed_ref
  71.9 12.7 %all-to-all-done = bf16[16,1,64,256]{3,2,1,0:T(8,128)(2,1)S(1)} async-done(((bf16[16,1,64,256]{3,2,1,0:T(8,128)(2,1)}), bf16[16,1,64,256]{3,2,1,0:T(8,128)(2,1)S(1)}, u32[]{:S(2)}, u32[]{:S(2)}) %all-to-all-start) | async-done | bytes 524320 | tf_op jit(solution)/shard_map/all_to_all | solution.py:311
  84.6 0.9 %shard_map.76 = f32[1024,128]{1,0:T(8,128)} custom-call(bf16[16,1,4,16,256]{4,3,2,1,0:T(8,128)(2,1)S(1)} %bitcast.27, f32[1,512]{1,0:T(1,128)S(1)} %constant_dynamic-slice_fusion.allowed_ref), custom_call_target="tpu_custom_call" | custom-call | flops 262144 | bytes 1048576 | tf_op jit(solution)/shard_map/pallas_call | solution.py:164
  (51 shorter events, 3.5 us)
Async XLA Ops:
  0.0 1.7 %copy-start = (bf16[16,16,4096]{2,1,0:T(8,128)(2,1)S(1)}, bf16[16,16,4096]{2,1,0:T(8,128)(2,1)}, u32[]{:S(2)}) copy-start(bf16[16,16,4096]{2,1,0:T(8,128)(2,1)} %param.9) | copy-start | bytes 6291460
  1.9 23.2 %collective-permute-start.7 = (bf16[112,2048]{1,0:T(8,128)(2,1)S(1)}, bf16[112,2048]{1,0:T(8,128)(2,1)S(1)}, u32[]{:S(2)}, u32[]{:S(2)}) collective-permute-start(bf16[112,2048]{1,0:T(8,128)(2,1)S(1)} %constant_dynamic-slice_fusion.2), channel_id=1, source_target_pairs={{0,2},{1,3},{2,0},{3,1},{4,6},{5,7},{6,4},{7,5},{8,10},{9,11},{10,... | collective-permute-start | bytes 1376264 | tf_op jit(solution)/shard_map/ppermute | solution.py:186
  9.7 2.9 %collective-permute-start = (f16[128,4096]{1,0:T(8,128)(2,1)S(1)}, f16[128,4096]{1,0:T(8,128)(2,1)S(1)}, u32[]{:S(2)}, u32[]{:S(2)}) collective-permute-start(f16[128,4096]{1,0:T(8,128)(2,1)S(1)} %multiply_convert_fusion.1), channel_id=1, source_target_pairs={{0,1},{1,0},{2,3},{3,2},{4,5},{5,4},{6,7},{7,6},{8,9},{9,8},{10,11... | collective-permute-start | bytes 3145736 | tf_op jit(solution)/shard_map/ppermute | solution.py:186
  12.0 3.5 %collective-permute-start.6 = (f16[128,4096]{1,0:T(8,128)(2,1)S(1)}, f16[128,4096]{1,0:T(8,128)(2,1)S(1)}, u32[]{:S(2)}, u32[]{:S(2)}) collective-permute-start(f16[128,4096]{1,0:T(8,128)(2,1)S(1)} %multiply_convert_fusion), channel_id=1, source_target_pairs={{0,1},{1,0},{2,3},{3,2},{4,5},{5,4},{6,7},{7,6},{8,9},{9,8},{10,11... | collective-permute-start | bytes 3145736 | tf_op jit(solution)/shard_map/ppermute | solution.py:186
  13.2 8.3 %collective-permute-start.2 = (f16[64,2048]{1,0:T(8,128)(2,1)S(1)}, f16[64,2048]{1,0:T(8,128)(2,1)S(1)}, u32[]{:S(2)}, u32[]{:S(2)}) collective-permute-start(f16[64,2048]{1,0:T(8,128)(2,1)S(1)} %multiply_convert_fusion.7), channel_id=1, source_target_pairs={{0,2},{1,3},{2,0},{3,1},{4,6},{5,7},{6,4},{7,5},{8,10},{9,11},{10,... | collective-permute-start | bytes 786440 | tf_op jit(solution)/shard_map/ppermute | solution.py:186
  13.4 10.0 %collective-permute-start.4 = (f16[32,4096]{1,0:T(8,128)(2,1)S(1)}, f16[32,4096]{1,0:T(8,128)(2,1)S(1)}, u32[]{:S(2)}, u32[]{:S(2)}) collective-permute-start(f16[32,4096]{1,0:T(8,128)(2,1)S(1)} %multiply_convert_fusion.6), channel_id=1, source_target_pairs={{0,4},{1,5},{2,6},{3,7},{4,0},{5,1},{6,2},{7,3},{8,12},{9,13},{10,... | collective-permute-start | bytes 786440 | tf_op jit(solution)/shard_map/ppermute | solution.py:186
  16.5 41.0 %collective-permute-start.1 = (bf16[256,2048]{1,0:T(8,128)(2,1)S(1)}, bf16[256,2048]{1,0:T(8,128)(2,1)S(1)}, u32[]{:S(2)}, u32[]{:S(2)}) collective-permute-start(bf16[256,2048]{1,0:T(8,128)(2,1)S(1)} %constant_dynamic-slice_fusion.1), channel_id=1, source_target_pairs={{0,1},{1,0},{2,3},{3,2},{4,5},{5,4},{6,7},{7,6},{8,9},{9,8},{10,11... | collective-permute-start | bytes 3145736 | tf_op jit(solution)/shard_map/ppermute | solution.py:186
  21.8 5.3 %collective-permute-start.3 = (f16[32,2048]{1,0:T(8,128)(2,1)S(1)}, f16[32,2048]{1,0:T(8,128)(2,1)S(1)}, u32[]{:S(2)}, u32[]{:S(2)}) collective-permute-start(f16[32,2048]{1,0:T(8,128)(2,1)S(1)} %multiply_convert_fusion.11), channel_id=1, source_target_pairs={{0,4},{1,5},{2,6},{3,7},{4,0},{5,1},{6,2},{7,3},{8,12},{9,13},{10,... | collective-permute-start | bytes 393224 | tf_op jit(solution)/shard_map/ppermute | solution.py:186
  23.7 6.5 %collective-permute-start.5 = (f16[32,2048]{1,0:T(8,128)(2,1)S(1)}, f16[32,2048]{1,0:T(8,128)(2,1)S(1)}, u32[]{:S(2)}, u32[]{:S(2)}) collective-permute-start(f16[32,2048]{1,0:T(8,128)(2,1)S(1)} %multiply_convert_fusion.10), channel_id=1, source_target_pairs={{0,2},{1,3},{2,0},{3,1},{4,6},{5,7},{6,4},{7,5},{8,10},{9,11},{10,... | collective-permute-start | bytes 393224 | tf_op jit(solution)/shard_map/ppermute | solution.py:186
  25.2 8.5 %collective-permute-start.8 = (f16[64,2048]{1,0:T(8,128)(2,1)S(1)}, f16[64,2048]{1,0:T(8,128)(2,1)S(1)}, u32[]{:S(2)}, u32[]{:S(2)}) collective-permute-start(f16[64,2048]{1,0:T(8,128)(2,1)S(1)} %multiply_convert_fusion.5), channel_id=1, source_target_pairs={{0,2},{1,3},{2,0},{3,1},{4,6},{5,7},{6,4},{7,5},{8,10},{9,11},{10,... | collective-permute-start | bytes 786440 | tf_op jit(solution)/shard_map/ppermute | solution.py:186
  25.8 10.0 %collective-permute-start.10 = (f16[32,4096]{1,0:T(8,128)(2,1)S(1)}, f16[32,4096]{1,0:T(8,128)(2,1)S(1)}, u32[]{:S(2)}, u32[]{:S(2)}) collective-permute-start(f16[32,4096]{1,0:T(8,128)(2,1)S(1)} %multiply_convert_fusion.4), channel_id=1, source_target_pairs={{0,4},{1,5},{2,6},{3,7},{4,0},{5,1},{6,2},{7,3},{8,12},{9,13},{10,... | collective-permute-start | bytes 786440 | tf_op jit(solution)/shard_map/ppermute | solution.py:186
  30.5 15.2 %collective-permute-start.12 = (f16[2,32,2048]{2,1,0:T(8,128)(2,1)S(1)}, f16[2,32,2048]{2,1,0:T(8,128)(2,1)S(1)}, u32[]{:S(2)}, u32[]{:S(2)}) collective-permute-start(f16[2,32,2048]{2,1,0:T(8,128)(2,1)S(1)} %get-tuple-element.92), channel_id=1, source_target_pairs={{0,8},{1,9},{2,10},{3,11},{4,12},{5,13},{6,14},{7,15},{8,0},{9,1},... | collective-permute-start | bytes 786440 | tf_op jit(solution)/shard_map/ppermute | solution.py:186
  34.0 6.4 %collective-permute-start.9 = (f16[32,2048]{1,0:T(8,128)(2,1)S(1)}, f16[32,2048]{1,0:T(8,128)(2,1)S(1)}, u32[]{:S(2)}, u32[]{:S(2)}) collective-permute-start(f16[32,2048]{1,0:T(8,128)(2,1)S(1)} %multiply_convert_fusion.9), channel_id=1, source_target_pairs={{0,4},{1,5},{2,6},{3,7},{4,0},{5,1},{6,2},{7,3},{8,12},{9,13},{10,... | collective-permute-start | bytes 393224 | tf_op jit(solution)/shard_map/ppermute | solution.py:186
  36.1 5.0 %collective-permute-start.11 = (f16[32,2048]{1,0:T(8,128)(2,1)S(1)}, f16[32,2048]{1,0:T(8,128)(2,1)S(1)}, u32[]{:S(2)}, u32[]{:S(2)}) collective-permute-start(f16[32,2048]{1,0:T(8,128)(2,1)S(1)} %multiply_convert_fusion.8), channel_id=1, source_target_pairs={{0,2},{1,3},{2,0},{3,1},{4,6},{5,7},{6,4},{7,5},{8,10},{9,11},{10,... | collective-permute-start | bytes 393224 | tf_op jit(solution)/shard_map/ppermute | solution.py:186
  41.4 12.2 %collective-permute-start.17 = (f16[2,32,2048]{2,1,0:T(8,128)(2,1)S(1)}, f16[2,32,2048]{2,1,0:T(8,128)(2,1)S(1)}, u32[]{:S(2)}, u32[]{:S(2)}) collective-permute-start(f16[2,32,2048]{2,1,0:T(8,128)(2,1)S(1)} %multiply_convert_fusion.3), channel_id=1, source_target_pairs={{0,8},{1,9},{2,10},{3,11},{4,12},{5,13},{6,14},{7,15},{8,0},{9,1},... | collective-permute-start | bytes 786440 | tf_op jit(solution)/shard_map/ppermute | solution.py:186
  45.2 12.2 %collective-permute-start.14 = (bf16[144,2048]{1,0:T(8,128)(2,1)S(1)}, bf16[144,2048]{1,0:T(8,128)(2,1)S(1)}, u32[]{:S(2)}, u32[]{:S(2)}) collective-permute-start(bf16[144,2048]{1,0:T(8,128)(2,1)S(1)} %constant_dynamic-slice_fusion.3), channel_id=1, source_target_pairs={{0,2},{1,3},{2,0},{3,1},{4,6},{5,7},{6,4},{7,5},{8,10},{9,11},{10,... | collective-permute-start | bytes 1769480 | tf_op jit(solution)/shard_map/ppermute | solution.py:186
  45.8 11.5 %collective-permute-start.13 = (bf16[2,32,2048]{2,1,0:T(8,128)(2,1)S(1)}, bf16[2,32,2048]{2,1,0:T(8,128)(2,1)S(1)}, u32[]{:S(2)}, u32[]{:S(2)}) collective-permute-start(bf16[2,32,2048]{2,1,0:T(8,128)(2,1)S(1)} %fusion.21), channel_id=1, source_target_pairs={{0,4},{1,5},{2,6},{3,7},{4,0},{5,1},{6,2},{7,3},{8,12},{9,13},{10,... | collective-permute-start | bytes 786440 | tf_op jit(solution)/shard_map/ppermute | solution.py:186
  49.7 8.6 %collective-permute-start.15 = (bf16[112,2048]{1,0:T(8,128)(2,1)S(1)}, bf16[112,2048]{1,0:T(8,128)(2,1)S(1)}, u32[]{:S(2)}, u32[]{:S(2)}) collective-permute-start(bf16[112,2048]{1,0:T(8,128)(2,1)S(1)} %collective-permute-done.7), channel_id=1, source_target_pairs={{0,1},{1,0},{2,3},{3,2},{4,5},{5,4},{6,7},{7,6},{8,9},{9,8},{10,11... | collective-permute-start | bytes 1376264 | tf_op jit(solution)/shard_map/ppermute | solution.py:186
  53.7 7.4 %collective-permute-start.18 = (bf16[2,32,2048]{2,1,0:T(8,128)(2,1)S(1)}, bf16[2,32,2048]{2,1,0:T(8,128)(2,1)S(1)}, u32[]{:S(2)}, u32[]{:S(2)}) collective-permute-start(bf16[2,32,2048]{2,1,0:T(8,128)(2,1)S(1)} %fusion.24), channel_id=1, source_target_pairs={{0,4},{1,5},{2,6},{3,7},{4,0},{5,1},{6,2},{7,3},{8,12},{9,13},{10,... | collective-permute-start | bytes 786440 | tf_op jit(solution)/shard_map/ppermute | solution.py:186
  57.4 2.1 %collective-permute-start.16 = (bf16[144,2048]{1,0:T(8,128)(2,1)S(1)}, bf16[144,2048]{1,0:T(8,128)(2,1)S(1)}, u32[]{:S(2)}, u32[]{:S(2)}) collective-permute-start(bf16[144,2048]{1,0:T(8,128)(2,1)S(1)} %collective-permute-done.14), channel_id=1, source_target_pairs={{0,1},{1,0},{2,3},{3,2},{4,5},{5,4},{6,7},{7,6},{8,9},{9,8},{10,11... | collective-permute-start | bytes 1769480 | tf_op jit(solution)/shard_map/ppermute | solution.py:186
  61.9 0.8 copy-start.1
  62.7 7.4 %copy-start.2 = (s32[8,12]{1,0:T(8,128)S(1)}, s32[8,12]{1,0:T(8,128)}, u32[]{:S(2)}) copy-start(s32[8,12]{1,0:T(8,128)} %param.11) | copy-start | bytes 1156
  62.7 8.1 %copy-start.3 = (s32[8]{0:T(128)S(1)}, s32[8]{0:T(128)}, u32[]{:S(2)}) copy-start(s32[8]{0:T(128)} %param.12) | copy-start | bytes 100
  62.7 8.2 %copy-start.4 = (s32[512]{0:T(512)S(1)}, s32[512]{0:T(512)}, u32[]{:S(2)}) copy-start(s32[512]{0:T(512)} %param.10) | copy-start | bytes 6148
  64.5 20.1 %all-to-all-start = ((bf16[16,1,64,256]{3,2,1,0:T(8,128)(2,1)}), bf16[16,1,64,256]{3,2,1,0:T(8,128)(2,1)S(1)}, u32[]{:S(2)}, u32[]{:S(2)}) async-start(bf16[16,1,64,256]{3,2,1,0:T(8,128)(2,1)} %bitcast.10), calls=%async_computation | async-start | bytes 1048576 | tf_op jit(solution)/shard_map/all_to_all | solution.py:311

commit v20 on v19

--- a/solution.py
+++ b/solution.py
@@ -104,7 +104,6 @@
 def order_kernel(slots_ref, *refs):
     raws, (out_hbm, staged_ref, sems) = refs[:-3], refs[-3:]
     nblocks = slots_ref.shape[0]
-    groups = len(raws) // CHUNKS
     parts = sems.shape[0]
     size = nblocks // parts
 
@@ -114,13 +113,12 @@
 
     for part in range(parts):
         for slot in range(part * size, (part + 1) * size):
-            for i, raw_ref in enumerate(raws):
-                examples, width = raw_ref.shape[0] // nblocks, raw_ref.shape[1]
-                chunk, group = divmod(i, groups)
+            for group, raw_ref in enumerate(raws):
+                examples = raw_ref.shape[0] // nblocks
                 rows = pl.ds(slots_ref[slot], examples, stride=nblocks)
-                staged_ref[
-                    slot, group * examples:(group + 1) * examples, chunk * width:(chunk + 1) * width
-                ] = raw_ref[rows, :].astype(staged_ref.dtype)
+                staged_ref[slot, group * examples:(group + 1) * examples, :] = (
+                    raw_ref[rows, :].astype(staged_ref.dtype)
+                )
         send(part).start()
     for part in range(parts):
         send(part).wait()
@@ -129,8 +127,7 @@
 def in_slot_order(raws, slots):
     nblocks = slots.shape[0]
     rows, width = raws[0].shape
-    groups = len(raws) // CHUNKS
-    shape = (nblocks, groups * rows // nblocks, CHUNKS * width)
+    shape = (nblocks, len(raws) * rows // nblocks, width)
     return pl.pallas_call(
         order_kernel,
         in_specs=[pl.BlockSpec(memory_space=pltpu.SMEM)] + [pl.BlockSpec(memory_space=pltpu.VMEM)] * len(raws),
@@ -144,30 +141,38 @@
     )(slots, *raws)
 
 
-def finish_kernel(got_ref, allowed_ref, out_ref):
-    n, owned, quad, examples, half = got_ref.shape
-    parts = half // LANES
-    per_row = owned * CORES * parts
+def finish_kernel(allowed_ref, *refs):
+    got, out_ref = refs[:-1], refs[-1]
+    n, owned, quad, examples, width = got[0].shape
+    parts = width // LANES
+    per_row = owned * CORES * len(got) * parts
     for device in range(n):
         for core in range(CORES):
             sources = [(device & ~3) | (y << 1) | core for y in range(quad // CORES)]
             for slot in range(owned):
-                scores = sum(got_ref[s, slot, s ^ device].astype(jnp.float32) for s in sources)
-                scores = scores * allowed_ref[slot:slot + 1, core * half:(core + 1) * half]
-                for i in range(parts):
-                    first = device * examples * per_row + (slot * CORES + core) * parts + i
-                    out_ref[pl.ds(first, examples, stride=per_row), :] = scores[:, i * LANES:(i + 1) * LANES]
+                for chunk, got_ref in enumerate(got):
+                    scores = sum(got_ref[s, slot, s ^ device].astype(jnp.float32) for s in sources)
+                    for i in range(parts):
+                        place = (core * len(got) + chunk) * parts + i
+                        allowed = allowed_ref[slot:slot + 1, place * LANES:(place + 1) * LANES]
+                        first = device * examples * per_row + slot * CORES * len(got) * parts + place
+                        out_ref[pl.ds(first, examples, stride=per_row), :] = (
+                            scores[:, i * LANES:(i + 1) * LANES] * allowed
+                        )
 
 
 def finish(got, allowed):
-    n, owned, _, examples, half = got.shape
+    n, owned, _, examples, width = got[0].shape
+    nq = allowed.shape[1]
     flat = pl.pallas_call(
         finish_kernel,
-        out_shape=jax.ShapeDtypeStruct((n * examples * owned * CORES * half // LANES, LANES), jnp.float32),
+        out_shape=jax.ShapeDtypeStruct((n * examples * owned * nq // LANES, LANES), jnp.float32),
         compiler_params=pltpu.CompilerParams(vmem_limit_bytes=4 * 1024 * 1024),
-        cost_estimate=pl.CostEstimate(flops=got.size, bytes_accessed=4 * got.size, transcendentals=0),
-    )(got, allowed)
-    return flat.reshape(n * examples, owned, CORES * half)
+        cost_estimate=pl.CostEstimate(
+            flops=len(got) * got[0].size, bytes_accessed=4 * len(got) * got[0].size, transcendentals=0
+        ),
+    )(allowed, *got)
+    return flat.reshape(n * examples, owned, nq)
 
 
 def shards(queries, precond, train, query_cluster, cand_blocks, cand_count, slot_block):
@@ -303,19 +308,22 @@
         jnp.concatenate([near, sibling], axis=0),
         jnp.concatenate([early, late, swap(early, 0), swap(late, 0)], axis=0),
     ]
-    raws = [scores(group, one) for group in groups]
-    two = gather((two + unpack(got_two)).astype(jnp.bfloat16), raws)
-    raws = raws + [scores(group, two) for group in groups]
-
-    ordered = in_slot_order(raws, slot_block).reshape(n, owned, 2 * CORES * examples, nq // CORES)
-    got = lax.all_to_all(ordered, "rows", split_axis=0, concat_axis=0, tiled=True)
+    def deliver(value):
+        ordered = in_slot_order([scores(group, value) for group in groups], slot_block)
+        ordered = ordered.reshape(n, owned, 2 * CORES * examples, value.shape[0])
+        return ordered, lax.all_to_all(ordered, "rows", split_axis=0, concat_axis=0, tiled=True)
+
+    ordered, got_one = deliver(one)
+    two = gather((two + unpack(got_two)).astype(jnp.bfloat16), ordered)
+    ordered, got_two = deliver(two)
 
     lists = (query_cluster, cand_blocks, cand_count, slot_block, first_slot)
     query_cluster, cand_blocks, cand_count, slot_block, first_slot = after(lists, ordered)
     allowed = listed_mask(query_cluster, cand_blocks, cand_count, nblocks)
     slots = lax.dynamic_slice(slot_block, (first_slot,), (owned,), allow_negative_indices=False)
     own_allowed = jnp.take(allowed, slots, axis=0, mode="clip")
-    return finish(got.reshape(n, owned, 2 * CORES, examples, nq // CORES), own_allowed)
+    got = [value.reshape(n, owned, 2 * CORES, examples, -1) for value in (got_one, got_two)]
+    return finish(got, own_allowed)
 
 
 def solution(mesh):

time: 85.7 us -> 106 us (1.24)
  waiting for transfers between devices: 35.4 us -> 54.9 us
  starting transfers between devices: 28.8 us -> 26.8 us
  matrix products: 3.34 us -> 4.99 us
  Pallas kernels: 8.67 us -> 9.85 us
    ppermute x19, waiting for transfers between devices: 22.7 us -> 41.1 us  [swap(): return lax.ppermute(value, 'rows', [(r, r ^ 1 << bit) for r in range(n)])]
    ppermute x19, starting transfers between devices: 23.2 us -> 17.3 us  [swap(): return lax.ppermute(value, 'rows', [(r, r ^ 1 << bit) for r in range(n)])]
    all_to_all x1 -> x2, starting transfers between devices: 5.58 us -> 9.46 us  [deliver(): lax.all_to_all(ordered, 'rows', split_axis=0, concat_axis=0, tiled=True)]
    dot_general x4, matrix products: 3.08 us -> 4.73 us  [scores(): lax.dot_general(group, value, (((1,), (1,)), ((), ())), preferred_element...]
    pallas_call x1 -> x2, Pallas kernels: 1.78 us -> 2.95 us  [in_slot_order(): pl.pallas_call(order_kernel, in_specs=[pl.BlockSpec(memory_space=pltpu.SM...]
    all_to_all x1 -> x2, waiting for transfers between devices: 12.7 us -> 13.7 us  [deliver(): lax.all_to_all(ordered, 'rows', split_axis=0, concat_axis=0, tiled=True)]
  transfers between devices with their start and end apart: 20 -> 21, of which waited for: 12 -> 13; matrix products, arithmetic and copies ran while one was open for 10% -> 11% of each run, Pallas kernels for 7% -> 7%
where the time goes in v20:
time: 106 us
  waiting for transfers between devices  54.9 us (52%)
  starting transfers between devices  26.8 us (25%)
  Pallas kernels  9.85 us (9%)
  other arithmetic  6.01 us (6%)
  matrix products  4.99 us (5%)
  local copies, waits for them, and re-layouts  2.94 us (3%)
    ppermute x19, waiting for transfers between devices, swap(): return lax.ppermute(value, 'rows', [(r, r ^ 1 << bit) for r in range(n)])  41.1 us
    ppermute x19, starting transfers between devices, swap(): return lax.ppermute(value, 'rows', [(r, r ^ 1 << bit) for r in range(n)])  17.3 us
    all_to_all x2, waiting for transfers between devices, deliver(): lax.all_to_all(ordered, 'rows', split_axis=0, concat_axis=0, tiled=True)  13.7 us
    all_to_all x2, starting transfers between devices, deliver(): lax.all_to_all(ordered, 'rows', split_axis=0, concat_axis=0, tiled=True)  9.46 us
    pallas_call x2, Pallas kernels, product(): pl.pallas_call(kernel, in_specs=[pl.BlockSpec(memory_space=pltpu.SMEM), i...  6.04 us
    dot_general x4, matrix products, scores(): lax.dot_general(group, value, (((1,), (1,)), ((), ())), preferred_element...  4.73 us
    pallas_call x2, Pallas kernels, in_slot_order(): pl.pallas_call(order_kernel, in_specs=[pl.BlockSpec(memory_space=pltpu.SM...  2.95 us
    convert_element_type x12, other arithmetic, pack(): return (value * lax.rsqrt(jnp.abs(value) + LEAST)).astype(jnp.float16)  2.4 us
  transfers between devices with their start and end apart: 21, of which 13 were waited for; matrix products, arithmetic and copies ran while one was open for 11% of the time, Pallas kernels for 7%

profile of v20, /device:TPU:0, one launch (start us, length us, event | category | flops | bytes accessed | tf_op | source)
XLA Modules:
  0.0 105.9 jit_solution(106922240932462138)
XLA Ops:
  0.0 1.3 %fusion.10 = (bf16[512,256]{1,0:T(8,128)(2,1)S(1)}, bf16[512,256]{1,0:T(8,128)(2,1)S(1)}) fusion(f32[512,256]{1,0:T(8,128)} %param.7), kind=kLoop, calls=%fused_computation.26 | loop fusion | flops 524288 | bytes 1048576 | tf_op jit(solution)/shard_map/convert_element_type | solution.py:273
  1.3 0.4 copy-done
  1.9 3.0 %collective-permute-start.5 = (bf16[112,2048]{1,0:T(8,128)(2,1)S(1)}, bf16[112,2048]{1,0:T(8,128)(2,1)S(1)}, u32[]{:S(2)}, u32[]{:S(2)}) collective-permute-start(bf16[112,2048]{1,0:T(8,128)(2,1)S(1)} %constant_dynamic-slice_fusion.2), channel_id=1, source_target_pairs={{0,2},{1,3},{2,0},{3,1},{4,6},{5,7},{6,4},{7,5},{8,10},{9,11},{10,... | collective-permute-start | bytes 1376264 | tf_op jit(solution)/shard_map/ppermute | solution.py:191
  5.0 4.2 %shard_map.73 = (f32[128,4096]{1,0:T(8,128)S(1)}, f32[128,4096]{1,0:T(8,128)S(1)}, bf16[256,4096]{1,0:T(8,128)(2,1)S(1)}, bf16[256,4096]{1,0:T(8,128)(2,1)S(1)}) custom-call(s32[1]{0:T(128)} %bitcast.1.core_ref, bf16[512,768]{1,0:T(8,128)(2,1)S(1)} %pad_maximum_fusion.3.rows_ref, f32[256,4096]{1,0:T(8,128)} %columns_hbm.1), custom_call_target="tpu_custom_call" | custom-call | flops 1610612736 | bytes 8388608 | tf_op jit(solution)/shard_map/pallas_call | solution.py:89
  9.2 0.4 multiply_convert_fusion.1
  9.8 1.8 %shard_map.74 = (f32[64,4096]{1,0:T(8,128)S(1)}, f32[64,4096]{1,0:T(8,128)S(1)}, f32[64,4096]{1,0:T(8,128)S(1)}, f32[64,4096]{1,0:T(8,128)S(1)}) custom-call(s32[1]{0:T(128)} %bitcast.2.core_ref, bf16[512,768]{1,0:T(8,128)(2,1)S(1)} %pad_maximum_fusion.3.rows_ref, bf16[256,4096]{1,0:T(8,128)(2,1)S(1)} %get-tuple-element.52.high_ref, ...), custom_call_target="tpu_custom_call" | custom-call | flops 1610612736 | bytes 8388608 | tf_op jit(solution)/shard_map/pallas_call | solution.py:89
  11.6 0.4 multiply_convert_fusion
  12.0 0.6 collective-permute-start.2
  12.6 0.4 fusion.3
  13.4 2.1 %collective-permute-start.4 = (f16[32,4096]{1,0:T(8,128)(2,1)S(1)}, f16[32,4096]{1,0:T(8,128)(2,1)S(1)}, u32[]{:S(2)}, u32[]{:S(2)}) collective-permute-start(f16[32,4096]{1,0:T(8,128)(2,1)S(1)} %multiply_convert_fusion.6), channel_id=1, source_target_pairs={{0,4},{1,5},{2,6},{3,7},{4,0},{5,1},{6,2},{7,3},{8,12},{9,13},{10,... | collective-permute-start | bytes 786440 | tf_op jit(solution)/shard_map/ppermute | solution.py:191
  15.5 0.4 fusion.9
  16.1 0.4 constant_dynamic-slice_fusion.1
  16.8 4.7 %collective-permute-done.3 = f16[64,2048]{1,0:T(8,128)(2,1)S(1)} collective-permute-done((f16[64,2048]{1,0:T(8,128)(2,1)S(1)}, f16[64,2048]{1,0:T(8,128)(2,1)S(1)}, u32[]{:S(2)}, u32[]{:S(2)}) %collective-permute-start.3) | collective-permute-done | bytes 262176 | tf_op jit(solution)/shard_map/ppermute | solution.py:191
  21.8 1.6 %collective-permute-start.12 = (f16[32,2048]{1,0:T(8,128)(2,1)S(1)}, f16[32,2048]{1,0:T(8,128)(2,1)S(1)}, u32[]{:S(2)}, u32[]{:S(2)}) collective-permute-start(f16[32,2048]{1,0:T(8,128)(2,1)S(1)} %multiply_convert_fusion.11), channel_id=1, source_target_pairs={{0,4},{1,5},{2,6},{3,7},{4,0},{5,1},{6,2},{7,3},{8,12},{9,13},{10,... | collective-permute-start | bytes 393224 | tf_op jit(solution)/shard_map/ppermute | solution.py:191
  23.7 1.4 %collective-permute-start.13 = (f16[32,2048]{1,0:T(8,128)(2,1)S(1)}, f16[32,2048]{1,0:T(8,128)(2,1)S(1)}, u32[]{:S(2)}, u32[]{:S(2)}) collective-permute-start(f16[32,2048]{1,0:T(8,128)(2,1)S(1)} %multiply_convert_fusion.10), channel_id=1, source_target_pairs={{0,2},{1,3},{2,0},{3,1},{4,6},{5,7},{6,4},{7,5},{8,10},{9,11},{10,... | collective-permute-start | bytes 393224 | tf_op jit(solution)/shard_map/ppermute | solution.py:191
  25.2 0.6 collective-permute-start.6
  25.8 0.5 collective-permute-start.8
  26.3 0.8 collective-permute-done.12
  27.2 3.0 %collective-permute-done.13 = f16[32,2048]{1,0:T(8,128)(2,1)S(1)} collective-permute-done((f16[32,2048]{1,0:T(8,128)(2,1)S(1)}, f16[32,2048]{1,0:T(8,128)(2,1)S(1)}, u32[]{:S(2)}, u32[]{:S(2)}) %collective-permute-start.13) | collective-permute-done | bytes 131104 | tf_op jit(solution)/shard_map/ppermute | solution.py:191
  30.4 3.3 %collective-permute-done.6 = f16[64,2048]{1,0:T(8,128)(2,1)S(1)} collective-permute-done((f16[64,2048]{1,0:T(8,128)(2,1)S(1)}, f16[64,2048]{1,0:T(8,128)(2,1)S(1)}, u32[]{:S(2)}, u32[]{:S(2)}) %collective-permute-start.6) | collective-permute-done | bytes 262176 | tf_op jit(solution)/shard_map/ppermute | solution.py:191
  34.0 0.5 collective-permute-start.7
  34.8 1.4 %collective-permute-start.9 = (f16[32,2048]{1,0:T(8,128)(2,1)S(1)}, f16[32,2048]{1,0:T(8,128)(2,1)S(1)}, u32[]{:S(2)}, u32[]{:S(2)}) collective-permute-start(f16[32,2048]{1,0:T(8,128)(2,1)S(1)} %multiply_convert_fusion.8), channel_id=1, source_target_pairs={{0,2},{1,3},{2,0},{3,1},{4,6},{5,7},{6,4},{7,5},{8,10},{9,11},{10,... | collective-permute-start | bytes 393224 | tf_op jit(solution)/shard_map/ppermute | solution.py:191
  36.2 2.8 %collective-permute-done.7 = f16[32,2048]{1,0:T(8,128)(2,1)S(1)} collective-permute-done((f16[32,2048]{1,0:T(8,128)(2,1)S(1)}, f16[32,2048]{1,0:T(8,128)(2,1)S(1)}, u32[]{:S(2)}, u32[]{:S(2)}) %collective-permute-start.7) | collective-permute-done | bytes 131104 | tf_op jit(solution)/shard_map/ppermute | solution.py:191
  39.1 0.8 collective-permute-done.9
  40.1 2.6 %collective-permute-start.10 = (f16[2,32,2048]{2,1,0:T(8,128)(2,1)S(1)}, f16[2,32,2048]{2,1,0:T(8,128)(2,1)S(1)}, u32[]{:S(2)}, u32[]{:S(2)}) collective-permute-start(f16[2,32,2048]{2,1,0:T(8,128)(2,1)S(1)} %multiply_convert_fusion.3), channel_id=1, source_target_pairs={{0,8},{1,9},{2,10},{3,11},{4,12},{5,13},{6,14},{7,15},{8,0},{9,1},... | collective-permute-start | bytes 786440 | tf_op jit(solution)/shard_map/ppermute | solution.py:191
  42.9 0.4 collective-permute-start.14
  43.6 1.4 %collective-permute-start.16 = (bf16[144,2048]{1,0:T(8,128)(2,1)S(1)}, bf16[144,2048]{1,0:T(8,128)(2,1)S(1)}, u32[]{:S(2)}, u32[]{:S(2)}) collective-permute-start(bf16[144,2048]{1,0:T(8,128)(2,1)S(1)} %constant_dynamic-slice_fusion.3), channel_id=1, source_target_pairs={{0,2},{1,3},{2,0},{3,1},{4,6},{5,7},{6,4},{7,5},{8,10},{9,11},{10,... | collective-permute-start | bytes 1769480 | tf_op jit(solution)/shard_map/ppermute | solution.py:191
  45.0 13.6 %collective-permute-done.10 = f16[2,32,2048]{2,1,0:T(8,128)(2,1)S(1)} collective-permute-done((f16[2,32,2048]{2,1,0:T(8,128)(2,1)S(1)}, f16[2,32,2048]{2,1,0:T(8,128)(2,1)S(1)}, u32[]{:S(2)}, u32[]{:S(2)}) %collective-permute-start.10) | collective-permute-done | bytes 262176 | tf_op jit(solution)/shard_map/ppermute | solution.py:191
  58.7 4.1 %collective-permute-done.14 = f16[2,32,2048]{2,1,0:T(8,128)(2,1)S(1)} collective-permute-done((f16[2,32,2048]{2,1,0:T(8,128)(2,1)S(1)}, f16[2,32,2048]{2,1,0:T(8,128)(2,1)S(1)}, u32[]{:S(2)}, u32[]{:S(2)}) %collective-permute-start.14) | collective-permute-done | bytes 262176 | tf_op jit(solution)/shard_map/ppermute | solution.py:191
  62.9 0.7 collective-permute-start.15
  63.6 4.8 %collective-permute-done.11 = bf16[2,32,2048]{2,1,0:T(8,128)(2,1)S(1)} collective-permute-done((bf16[2,32,2048]{2,1,0:T(8,128)(2,1)S(1)}, bf16[2,32,2048]{2,1,0:T(8,128)(2,1)S(1)}, u32[]{:S(2)}, u32[]{:S(2)}) %collective-permute-start.11) | collective-permute-done | bytes 262176 | tf_op jit(solution)/shard_map/ppermute | solution.py:191
  68.7 0.7 fusion.refs_0_
  69.4 0.2 copy-done.7
  69.7 0.9 collective-permute-done.18
  70.7 0.9 fusion.44.refs_1_
  71.6 2.4 %collective-permute-done.15 = bf16[2,32,2048]{2,1,0:T(8,128)(2,1)S(1)} collective-permute-done((bf16[2,32,2048]{2,1,0:T(8,128)(2,1)S(1)}, bf16[2,32,2048]{2,1,0:T(8,128)(2,1)S(1)}, u32[]{:S(2)}, u32[]{:S(2)}) %collective-permute-start.15) | collective-permute-done | bytes 262176 | tf_op jit(solution)/shard_map/ppermute | solution.py:191
  74.1 1.5 %shard_map.76 = bf16[16,64,128]{2,1,0:T(8,128)(2,1)} custom-call(s32[16]{0:T(128)S(1)} %copy-done.1, f32[512,128]{1,0:T(8,128)S(1)} %fusion.refs_0_, f32[512,128]{1,0:T(8,128)S(1)} %fusion.44.refs_1_), custom_call_target="tpu_custom_call" | custom-call | flops 65536 | bytes 786432 | tf_op jit(solution)/shard_map/pallas_call | solution.py:131
  75.6 5.9 %all-to-all-start.1 = ((bf16[16,1,64,128]{3,2,1,0:T(8,128)(2,1)}), bf16[16,1,64,128]{3,2,1,0:T(8,128)(2,1)S(1)}, u32[]{:S(2)}, u32[]{:S(2)}) async-start(bf16[16,1,64,128]{3,2,1,0:T(8,128)(2,1)} %bitcast.14), calls=%async_computation.1 | async-start | bytes 524288 | tf_op jit(solution)/shard_map/all_to_all | solution.py:314
  81.5 2.4 %fusion.1.refs_0_ = f32[512,128]{1,0:T(8,128)S(1)} fusion(bf16[128,2048]{1,0:T(8,128)(2,1)S(1)} %bitcast.37, bf16[256,2048]{1,0:T(8,128)(2,1)} %copy-done.7, bf16[256,2048]{1,0:T(8,128)(2,1)} %copy-done.4), kind=kOutput, calls=%fused_computation.8 | convolution fusion | flops 272629760 | bytes 2883584 | tf_op jit(solution)/shard_map/dot_general | solution.py:262
  84.0 0.7 fusion.43.refs_1_
  84.7 1.5 %shard_map.75 = bf16[16,64,128]{2,1,0:T(8,128)(2,1)} custom-call(s32[16]{0:T(128)S(1)} %copy-done.1, f32[512,128]{1,0:T(8,128)S(1)} %fusion.1.refs_0_, f32[512,128]{1,0:T(8,128)S(1)} %fusion.43.refs_1_), custom_call_target="tpu_custom_call" | custom-call | flops 65536 | bytes 786432 | tf_op jit(solution)/shard_map/pallas_call | solution.py:131
  86.2 5.4 %all-to-all-done.1 = bf16[16,1,64,128]{3,2,1,0:T(8,128)(2,1)S(1)} async-done(((bf16[16,1,64,128]{3,2,1,0:T(8,128)(2,1)}), bf16[16,1,64,128]{3,2,1,0:T(8,128)(2,1)S(1)}, u32[]{:S(2)}, u32[]{:S(2)}) %all-to-all-start.1) | async-done | bytes 262176 | tf_op jit(solution)/shard_map/all_to_all | solution.py:314
  91.5 3.5 %all-to-all-start = ((bf16[16,1,64,128]{3,2,1,0:T(8,128)(2,1)}), bf16[16,1,64,128]{3,2,1,0:T(8,128)(2,1)S(1)}, u32[]{:S(2)}, u32[]{:S(2)}) async-start(bf16[16,1,64,128]{3,2,1,0:T(8,128)(2,1)} %bitcast.12), calls=%async_computation | async-start | bytes 524288 | tf_op jit(solution)/shard_map/all_to_all | solution.py:314
  95.2 0.6 dynamic_slice.79
  95.9 0.3 fusion.36
  96.1 0.6 constant_dynamic-slice_fusion.allowed_ref
  96.7 8.4 %all-to-all-done = bf16[16,1,64,128]{3,2,1,0:T(8,128)(2,1)S(1)} async-done(((bf16[16,1,64,128]{3,2,1,0:T(8,128)(2,1)}), bf16[16,1,64,128]{3,2,1,0:T(8,128)(2,1)S(1)}, u32[]{:S(2)}, u32[]{:S(2)}) %all-to-all-start) | async-done | bytes 262176 | tf_op jit(solution)/shard_map/all_to_all | solution.py:314
  105.1 0.9 shard_map.77
  (62 shorter events, 4.2 us)
Async XLA Ops:
  0.0 1.7 %copy-start = (bf16[16,16,4096]{2,1,0:T(8,128)(2,1)S(1)}, bf16[16,16,4096]{2,1,0:T(8,128)(2,1)}, u32[]{:S(2)}) copy-start(bf16[16,16,4096]{2,1,0:T(8,128)(2,1)} %param.9) | copy-start | bytes 6291460
  1.9 23.2 %collective-permute-start.5 = (bf16[112,2048]{1,0:T(8,128)(2,1)S(1)}, bf16[112,2048]{1,0:T(8,128)(2,1)S(1)}, u32[]{:S(2)}, u32[]{:S(2)}) collective-permute-start(bf16[112,2048]{1,0:T(8,128)(2,1)S(1)} %constant_dynamic-slice_fusion.2), channel_id=1, source_target_pairs={{0,2},{1,3},{2,0},{3,1},{4,6},{5,7},{6,4},{7,5},{8,10},{9,11},{10,... | collective-permute-start | bytes 1376264 | tf_op jit(solution)/shard_map/ppermute | solution.py:191
  9.7 2.9 %collective-permute-start = (f16[128,4096]{1,0:T(8,128)(2,1)S(1)}, f16[128,4096]{1,0:T(8,128)(2,1)S(1)}, u32[]{:S(2)}, u32[]{:S(2)}) collective-permute-start(f16[128,4096]{1,0:T(8,128)(2,1)S(1)} %multiply_convert_fusion.1), channel_id=1, source_target_pairs={{0,1},{1,0},{2,3},{3,2},{4,5},{5,4},{6,7},{7,6},{8,9},{9,8},{10,11... | collective-permute-start | bytes 3145736 | tf_op jit(solution)/shard_map/ppermute | solution.py:191
  12.0 3.5 %collective-permute-start.2 = (f16[128,4096]{1,0:T(8,128)(2,1)S(1)}, f16[128,4096]{1,0:T(8,128)(2,1)S(1)}, u32[]{:S(2)}, u32[]{:S(2)}) collective-permute-start(f16[128,4096]{1,0:T(8,128)(2,1)S(1)} %multiply_convert_fusion), channel_id=1, source_target_pairs={{0,1},{1,0},{2,3},{3,2},{4,5},{5,4},{6,7},{7,6},{8,9},{9,8},{10,11... | collective-permute-start | bytes 3145736 | tf_op jit(solution)/shard_map/ppermute | solution.py:191
  13.2 8.3 %collective-permute-start.3 = (f16[64,2048]{1,0:T(8,128)(2,1)S(1)}, f16[64,2048]{1,0:T(8,128)(2,1)S(1)}, u32[]{:S(2)}, u32[]{:S(2)}) collective-permute-start(f16[64,2048]{1,0:T(8,128)(2,1)S(1)} %multiply_convert_fusion.7), channel_id=1, source_target_pairs={{0,2},{1,3},{2,0},{3,1},{4,6},{5,7},{6,4},{7,5},{8,10},{9,11},{10,... | collective-permute-start | bytes 786440 | tf_op jit(solution)/shard_map/ppermute | solution.py:191
  13.4 10.0 %collective-permute-start.4 = (f16[32,4096]{1,0:T(8,128)(2,1)S(1)}, f16[32,4096]{1,0:T(8,128)(2,1)S(1)}, u32[]{:S(2)}, u32[]{:S(2)}) collective-permute-start(f16[32,4096]{1,0:T(8,128)(2,1)S(1)} %multiply_convert_fusion.6), channel_id=1, source_target_pairs={{0,4},{1,5},{2,6},{3,7},{4,0},{5,1},{6,2},{7,3},{8,12},{9,13},{10,... | collective-permute-start | bytes 786440 | tf_op jit(solution)/shard_map/ppermute | solution.py:191
  16.5 52.1 %copy-start.4 = (bf16[256,2048]{1,0:T(8,128)(2,1)}, bf16[256,2048]{1,0:T(8,128)(2,1)S(1)}, u32[]{:S(2)}) copy-start(bf16[256,2048]{1,0:T(8,128)(2,1)S(1)} %constant_dynamic-slice_fusion.1) | copy-start | bytes 3145732
  16.5 52.1 %collective-permute-start.1 = (bf16[256,2048]{1,0:T(8,128)(2,1)S(1)}, bf16[256,2048]{1,0:T(8,128)(2,1)S(1)}, u32[]{:S(2)}, u32[]{:S(2)}) collective-permute-start(bf16[256,2048]{1,0:T(8,128)(2,1)S(1)} %constant_dynamic-slice_fusion.1), channel_id=1, source_target_pairs={{0,1},{1,0},{2,3},{3,2},{4,5},{5,4},{6,7},{7,6},{8,9},{9,8},{10,11... | collective-permute-start | bytes 3145736 | tf_op jit(solution)/shard_map/ppermute | solution.py:191
  21.8 5.3 %collective-permute-start.12 = (f16[32,2048]{1,0:T(8,128)(2,1)S(1)}, f16[32,2048]{1,0:T(8,128)(2,1)S(1)}, u32[]{:S(2)}, u32[]{:S(2)}) collective-permute-start(f16[32,2048]{1,0:T(8,128)(2,1)S(1)} %multiply_convert_fusion.11), channel_id=1, source_target_pairs={{0,4},{1,5},{2,6},{3,7},{4,0},{5,1},{6,2},{7,3},{8,12},{9,13},{10,... | collective-permute-start | bytes 393224 | tf_op jit(solution)/shard_map/ppermute | solution.py:191
  23.7 6.5 %collective-permute-start.13 = (f16[32,2048]{1,0:T(8,128)(2,1)S(1)}, f16[32,2048]{1,0:T(8,128)(2,1)S(1)}, u32[]{:S(2)}, u32[]{:S(2)}) collective-permute-start(f16[32,2048]{1,0:T(8,128)(2,1)S(1)} %multiply_convert_fusion.10), channel_id=1, source_target_pairs={{0,2},{1,3},{2,0},{3,1},{4,6},{5,7},{6,4},{7,5},{8,10},{9,11},{10,... | collective-permute-start | bytes 393224 | tf_op jit(solution)/shard_map/ppermute | solution.py:191
  25.2 8.5 %collective-permute-start.6 = (f16[64,2048]{1,0:T(8,128)(2,1)S(1)}, f16[64,2048]{1,0:T(8,128)(2,1)S(1)}, u32[]{:S(2)}, u32[]{:S(2)}) collective-permute-start(f16[64,2048]{1,0:T(8,128)(2,1)S(1)} %multiply_convert_fusion.5), channel_id=1, source_target_pairs={{0,2},{1,3},{2,0},{3,1},{4,6},{5,7},{6,4},{7,5},{8,10},{9,11},{10,... | collective-permute-start | bytes 786440 | tf_op jit(solution)/shard_map/ppermute | solution.py:191
  25.8 8.7 %collective-permute-start.8 = (f16[32,4096]{1,0:T(8,128)(2,1)S(1)}, f16[32,4096]{1,0:T(8,128)(2,1)S(1)}, u32[]{:S(2)}, u32[]{:S(2)}) collective-permute-start(f16[32,4096]{1,0:T(8,128)(2,1)S(1)} %multiply_convert_fusion.4), channel_id=1, source_target_pairs={{0,4},{1,5},{2,6},{3,7},{4,0},{5,1},{6,2},{7,3},{8,12},{9,13},{10,... | collective-permute-start | bytes 786440 | tf_op jit(solution)/shard_map/ppermute | solution.py:191
  34.0 5.0 %collective-permute-start.7 = (f16[32,2048]{1,0:T(8,128)(2,1)S(1)}, f16[32,2048]{1,0:T(8,128)(2,1)S(1)}, u32[]{:S(2)}, u32[]{:S(2)}) collective-permute-start(f16[32,2048]{1,0:T(8,128)(2,1)S(1)} %multiply_convert_fusion.9), channel_id=1, source_target_pairs={{0,4},{1,5},{2,6},{3,7},{4,0},{5,1},{6,2},{7,3},{8,12},{9,13},{10,... | collective-permute-start | bytes 393224 | tf_op jit(solution)/shard_map/ppermute | solution.py:191
  34.8 5.0 %collective-permute-start.9 = (f16[32,2048]{1,0:T(8,128)(2,1)S(1)}, f16[32,2048]{1,0:T(8,128)(2,1)S(1)}, u32[]{:S(2)}, u32[]{:S(2)}) collective-permute-start(f16[32,2048]{1,0:T(8,128)(2,1)S(1)} %multiply_convert_fusion.8), channel_id=1, source_target_pairs={{0,2},{1,3},{2,0},{3,1},{4,6},{5,7},{6,4},{7,5},{8,10},{9,11},{10,... | collective-permute-start | bytes 393224 | tf_op jit(solution)/shard_map/ppermute | solution.py:191
  40.1 18.4 %collective-permute-start.10 = (f16[2,32,2048]{2,1,0:T(8,128)(2,1)S(1)}, f16[2,32,2048]{2,1,0:T(8,128)(2,1)S(1)}, u32[]{:S(2)}, u32[]{:S(2)}) collective-permute-start(f16[2,32,2048]{2,1,0:T(8,128)(2,1)S(1)} %multiply_convert_fusion.3), channel_id=1, source_target_pairs={{0,8},{1,9},{2,10},{3,11},{4,12},{5,13},{6,14},{7,15},{8,0},{9,1},... | collective-permute-start | bytes 786440 | tf_op jit(solution)/shard_map/ppermute | solution.py:191
  42.9 19.9 %collective-permute-start.14 = (f16[2,32,2048]{2,1,0:T(8,128)(2,1)S(1)}, f16[2,32,2048]{2,1,0:T(8,128)(2,1)S(1)}, u32[]{:S(2)}, u32[]{:S(2)}) collective-permute-start(f16[2,32,2048]{2,1,0:T(8,128)(2,1)S(1)} %get-tuple-element.92), channel_id=1, source_target_pairs={{0,8},{1,9},{2,10},{3,11},{4,12},{5,13},{6,14},{7,15},{8,0},{9,1},... | collective-permute-start | bytes 786440 | tf_op jit(solution)/shard_map/ppermute | solution.py:191
  43.6 25.0 %collective-permute-start.16 = (bf16[144,2048]{1,0:T(8,128)(2,1)S(1)}, bf16[144,2048]{1,0:T(8,128)(2,1)S(1)}, u32[]{:S(2)}, u32[]{:S(2)}) collective-permute-start(bf16[144,2048]{1,0:T(8,128)(2,1)S(1)} %constant_dynamic-slice_fusion.3), channel_id=1, source_target_pairs={{0,2},{1,3},{2,0},{3,1},{4,6},{5,7},{6,4},{7,5},{8,10},{9,11},{10,... | collective-permute-start | bytes 1769480 | tf_op jit(solution)/shard_map/ppermute | solution.py:191
  58.7 9.8 %collective-permute-start.11 = (bf16[2,32,2048]{2,1,0:T(8,128)(2,1)S(1)}, bf16[2,32,2048]{2,1,0:T(8,128)(2,1)S(1)}, u32[]{:S(2)}, u32[]{:S(2)}) collective-permute-start(bf16[2,32,2048]{2,1,0:T(8,128)(2,1)S(1)} %fusion.21), channel_id=1, source_target_pairs={{0,4},{1,5},{2,6},{3,7},{4,0},{5,1},{6,2},{7,3},{8,12},{9,13},{10,... | collective-permute-start | bytes 786440 | tf_op jit(solution)/shard_map/ppermute | solution.py:191
  62.9 11.0 %collective-permute-start.15 = (bf16[2,32,2048]{2,1,0:T(8,128)(2,1)S(1)}, bf16[2,32,2048]{2,1,0:T(8,128)(2,1)S(1)}, u32[]{:S(2)}, u32[]{:S(2)}) collective-permute-start(bf16[2,32,2048]{2,1,0:T(8,128)(2,1)S(1)} %fusion.24), channel_id=1, source_target_pairs={{0,4},{1,5},{2,6},{3,7},{4,0},{5,1},{6,2},{7,3},{8,12},{9,13},{10,... | collective-permute-start | bytes 786440 | tf_op jit(solution)/shard_map/ppermute | solution.py:191
  63.6 6.1 %collective-permute-start.17 = (bf16[112,2048]{1,0:T(8,128)(2,1)S(1)}, bf16[112,2048]{1,0:T(8,128)(2,1)S(1)}, u32[]{:S(2)}, u32[]{:S(2)}) collective-permute-start(bf16[112,2048]{1,0:T(8,128)(2,1)S(1)} %collective-permute-done.5), channel_id=1, source_target_pairs={{0,1},{1,0},{2,3},{3,2},{4,5},{5,4},{6,7},{7,6},{8,9},{9,8},{10,11... | collective-permute-start | bytes 1376264 | tf_op jit(solution)/shard_map/ppermute | solution.py:191
  68.5 2.1 %collective-permute-start.18 = (bf16[144,2048]{1,0:T(8,128)(2,1)S(1)}, bf16[144,2048]{1,0:T(8,128)(2,1)S(1)}, u32[]{:S(2)}, u32[]{:S(2)}) collective-permute-start(bf16[144,2048]{1,0:T(8,128)(2,1)S(1)} %collective-permute-done.16), channel_id=1, source_target_pairs={{0,1},{1,0},{2,3},{3,2},{4,5},{5,4},{6,7},{7,6},{8,9},{9,8},{10,11... | collective-permute-start | bytes 1769480 | tf_op jit(solution)/shard_map/ppermute | solution.py:191
  68.6 1.0 copy-start.7
  70.7 4.9 %copy-start.2 = (bf16[512,2048]{1,0:T(8,128)(2,1)}, bf16[512,2048]{1,0:T(8,128)(2,1)S(1)}, u32[]{:S(2)}) copy-start(bf16[512,2048]{1,0:T(8,128)(2,1)S(1)} %constant_dynamic-update-slice_fusion) | copy-start | bytes 6291460
  70.7 3.4 %copy-start.1 = (s32[16]{0:T(128)S(1)}, s32[16]{0:T(128)}, u32[]{:S(2)}) copy-start(s32[16]{0:T(128)} %slots_ref.3) | copy-start | bytes 196
  75.6 16.0 %all-to-all-start.1 = ((bf16[16,1,64,128]{3,2,1,0:T(8,128)(2,1)}), bf16[16,1,64,128]{3,2,1,0:T(8,128)(2,1)S(1)}, u32[]{:S(2)}, u32[]{:S(2)}) async-start(bf16[16,1,64,128]{3,2,1,0:T(8,128)(2,1)} %bitcast.14), calls=%async_computation.1 | async-start | bytes 524288 | tf_op jit(solution)/shard_map/all_to_all | solution.py:314
  81.5 2.4 %copy-start.3 = (bf16[512,2048]{1,0:T(8,128)(2,1)S(1)}, bf16[512,2048]{1,0:T(8,128)(2,1)}, u32[]{:S(2)}) copy-start(bf16[512,2048]{1,0:T(8,128)(2,1)} %copy-done.2) | copy-start | bytes 6291460
  83.9 11.2 %copy-start.6 = (s32[8]{0:T(128)S(1)}, s32[8]{0:T(128)}, u32[]{:S(2)}) copy-start(s32[8]{0:T(128)} %param.12) | copy-start | bytes 100
  83.9 11.2 %copy-start.5 = (s32[8,12]{1,0:T(8,128)S(1)}, s32[8,12]{1,0:T(8,128)}, u32[]{:S(2)}) copy-start(s32[8,12]{1,0:T(8,128)} %param.11) | copy-start | bytes 1156
  83.9 11.9 %copy-start.8 = (s32[512]{0:T(512)S(1)}, s32[512]{0:T(512)}, u32[]{:S(2)}) copy-start(s32[512]{0:T(512)} %param.10) | copy-start | bytes 6148
  91.5 13.5 %all-to-all-start = ((bf16[16,1,64,128]{3,2,1,0:T(8,128)(2,1)}), bf16[16,1,64,128]{3,2,1,0:T(8,128)(2,1)S(1)}, u32[]{:S(2)}, u32[]{:S(2)}) async-start(bf16[16,1,64,128]{3,2,1,0:T(8,128)(2,1)} %bitcast.12), calls=%async_computation | async-start | bytes 524288 | tf_op jit(solution)/shard_map/all_to_all | solution.py:314

commit v21 on v18

--- a/solution.py
+++ b/solution.py
@@ -11,6 +11,7 @@
 UNIT = 2.0 ** 18
 LEAST = 2.0 ** -100
 LANES = 128
+AHEAD = 3
 OTHER_VMEM = 44
 MINE_VMEM = 16
 
@@ -51,11 +52,13 @@
             columns_hbm.at[:, i * block:(i + 1) * block], columns_ref.at[i], sems.at[i]
         )
 
-    for i in range(steps):
+    for i in range(min(AHEAD, steps)):
         load(i).start()
     left = rows_of(core_ref, rows_ref)
     for i in range(steps):
         load(i).wait()
+        if i + AHEAD < steps:
+            load(i + AHEAD).start()
         columns = slice(i * block, (i + 1) * block)
         high, low = split(columns_ref[i])
         high_ref[:, columns] = high

time: 85.4 us -> 85.6 us (level)
  no operation moved by 1% of the time
where the time goes in v21:
time: 85.6 us; the launch traced here: 85.3 us
  waiting for transfers between devices  36.2 us (42%)
  starting transfers between devices  27.8 us (32%)
  Pallas kernels  8.68 us (10%)
  other arithmetic  6.04 us (7%)
  matrix products  3.33 us (4%)
  local copies, waits for them, and re-layouts  2.78 us (3%)
    ppermute x19, waiting for transfers between devices, swap(): return lax.ppermute(value, 'rows', [(r, r ^ 1 << bit) for r in range(n)])  23.4 us
    ppermute x19, starting transfers between devices, swap(): return lax.ppermute(value, 'rows', [(r, r ^ 1 << bit) for r in range(n)])  22.4 us
    all_to_all x1, waiting for transfers between devices, shards(): lax.all_to_all(ordered, 'rows', split_axis=0, concat_axis=0, tiled=True)  12.7 us
    pallas_call x2, Pallas kernels, product(): pl.pallas_call(kernel, in_specs=[pl.BlockSpec(memory_space=pltpu.SMEM), i...  6.04 us
    all_to_all x1, starting transfers between devices, shards(): lax.all_to_all(ordered, 'rows', split_axis=0, concat_axis=0, tiled=True)  5.4 us
    dot_general x4, matrix products, scores(): lax.dot_general(group, value, (((1,), (1,)), ((), ())), preferred_element...  3.07 us
    convert_element_type x12, other arithmetic, pack(): return (value * lax.rsqrt(jnp.abs(value) + LEAST)).astype(jnp.float16)  2.39 us
    pallas_call x1, Pallas kernels, in_slot_order(): pl.pallas_call(order_kernel, in_specs=[pl.BlockSpec(memory_space=pltpu.SM...  1.78 us
  transfers between devices with their start and end apart: 20, of which 12 were waited for; matrix products, arithmetic and copies ran while one was open for 10% of the time, Pallas kernels for 7%

profile of v21, /device:TPU:0, one launch (start us, length us, event | category | flops | bytes accessed | tf_op | source)
XLA Modules:
  0.0 85.3 jit_solution(3772361018764479865)
XLA Ops:
  0.0 1.3 %fusion.10 = (bf16[512,256]{1,0:T(8,128)(2,1)S(1)}, bf16[512,256]{1,0:T(8,128)(2,1)S(1)}) fusion(f32[512,256]{1,0:T(8,128)} %param.7), kind=kLoop, calls=%fused_computation.26 | loop fusion | flops 524288 | bytes 1048576 | tf_op jit(solution)/shard_map/convert_element_type | solution.py:271
  1.3 0.4 copy-done
  1.9 3.0 %collective-permute-start.7 = (bf16[96,2048]{1,0:T(8,128)(2,1)S(1)}, bf16[96,2048]{1,0:T(8,128)(2,1)S(1)}, u32[]{:S(2)}, u32[]{:S(2)}) collective-permute-start(bf16[96,2048]{1,0:T(8,128)(2,1)S(1)} %constant_dynamic-slice_fusion.2), channel_id=1, source_target_pairs={{0,2},{1,3},{2,0},{3,1},{4,6},{5,7},{6,4},{7,5},{8,10},{9,11},{10,... | collective-permute-start | bytes 1179656 | tf_op jit(solution)/shard_map/ppermute | solution.py:189
  5.0 4.2 %shard_map.73 = (f32[128,4096]{1,0:T(8,128)S(1)}, f32[128,4096]{1,0:T(8,128)S(1)}, bf16[256,4096]{1,0:T(8,128)(2,1)S(1)}, bf16[256,4096]{1,0:T(8,128)(2,1)S(1)}) custom-call(s32[1]{0:T(128)} %bitcast.1.core_ref, bf16[512,768]{1,0:T(8,128)(2,1)S(1)} %pad_maximum_fusion.3.rows_ref, f32[256,4096]{1,0:T(8,128)} %columns_hbm.1), custom_call_target="tpu_custom_call" | custom-call | flops 1610612736 | bytes 8388608 | tf_op jit(solution)/shard_map/pallas_call | solution.py:92
  9.2 0.4 multiply_convert_fusion.1
  9.8 1.8 %shard_map.74 = (f32[64,4096]{1,0:T(8,128)S(1)}, f32[64,4096]{1,0:T(8,128)S(1)}, f32[64,4096]{1,0:T(8,128)S(1)}, f32[64,4096]{1,0:T(8,128)S(1)}) custom-call(s32[1]{0:T(128)} %bitcast.2.core_ref, bf16[512,768]{1,0:T(8,128)(2,1)S(1)} %pad_maximum_fusion.3.rows_ref, bf16[256,4096]{1,0:T(8,128)(2,1)S(1)} %get-tuple-element.51.high_ref, ...), custom_call_target="tpu_custom_call" | custom-call | flops 1610612736 | bytes 8388608 | tf_op jit(solution)/shard_map/pallas_call | solution.py:92
  11.6 0.4 multiply_convert_fusion
  12.0 0.6 collective-permute-start.6
  12.6 0.4 fusion.3
  12.9 0.2 multiply_convert_fusion.7
  13.4 2.1 %collective-permute-start.4 = (f16[32,4096]{1,0:T(8,128)(2,1)S(1)}, f16[32,4096]{1,0:T(8,128)(2,1)S(1)}, u32[]{:S(2)}, u32[]{:S(2)}) collective-permute-start(f16[32,4096]{1,0:T(8,128)(2,1)S(1)} %multiply_convert_fusion.6), channel_id=1, source_target_pairs={{0,4},{1,5},{2,6},{3,7},{4,0},{5,1},{6,2},{7,3},{8,12},{9,13},{10,... | collective-permute-start | bytes 786440 | tf_op jit(solution)/shard_map/ppermute | solution.py:189
  15.5 0.4 fusion.9
  16.1 0.4 constant_dynamic-slice_fusion.1
  16.6 0.2 multiply_convert_fusion.5
  16.8 4.7 %collective-permute-done.2 = f16[64,2048]{1,0:T(8,128)(2,1)S(1)} collective-permute-done((f16[64,2048]{1,0:T(8,128)(2,1)S(1)}, f16[64,2048]{1,0:T(8,128)(2,1)S(1)}, u32[]{:S(2)}, u32[]{:S(2)}) %collective-permute-start.2) | collective-permute-done | bytes 262176 | tf_op jit(solution)/shard_map/ppermute | solution.py:189
  21.8 1.7 %collective-permute-start.3 = (f16[32,2048]{1,0:T(8,128)(2,1)S(1)}, f16[32,2048]{1,0:T(8,128)(2,1)S(1)}, u32[]{:S(2)}, u32[]{:S(2)}) collective-permute-start(f16[32,2048]{1,0:T(8,128)(2,1)S(1)} %multiply_convert_fusion.11), channel_id=1, source_target_pairs={{0,4},{1,5},{2,6},{3,7},{4,0},{5,1},{6,2},{7,3},{8,12},{9,13},{10,... | collective-permute-start | bytes 393224 | tf_op jit(solution)/shard_map/ppermute | solution.py:189
  23.7 0.5 collective-permute-start.5
  24.3 1.6 %collective-permute-start.8 = (f16[64,2048]{1,0:T(8,128)(2,1)S(1)}, f16[64,2048]{1,0:T(8,128)(2,1)S(1)}, u32[]{:S(2)}, u32[]{:S(2)}) collective-permute-start(f16[64,2048]{1,0:T(8,128)(2,1)S(1)} %multiply_convert_fusion.5), channel_id=1, source_target_pairs={{0,2},{1,3},{2,0},{3,1},{4,6},{5,7},{6,4},{7,5},{8,10},{9,11},{10,... | collective-permute-start | bytes 786440 | tf_op jit(solution)/shard_map/ppermute | solution.py:189
  25.8 0.4 collective-permute-start.10
  26.3 0.9 %collective-permute-done.3 = f16[32,2048]{1,0:T(8,128)(2,1)S(1)} collective-permute-done((f16[32,2048]{1,0:T(8,128)(2,1)S(1)}, f16[32,2048]{1,0:T(8,128)(2,1)S(1)}, u32[]{:S(2)}, u32[]{:S(2)}) %collective-permute-start.3) | collective-permute-done | bytes 131104 | tf_op jit(solution)/shard_map/ppermute | solution.py:189
  27.2 3.0 %collective-permute-done.5 = f16[32,2048]{1,0:T(8,128)(2,1)S(1)} collective-permute-done((f16[32,2048]{1,0:T(8,128)(2,1)S(1)}, f16[32,2048]{1,0:T(8,128)(2,1)S(1)}, u32[]{:S(2)}, u32[]{:S(2)}) %collective-permute-start.5) | collective-permute-done | bytes 131104 | tf_op jit(solution)/shard_map/ppermute | solution.py:189
  30.5 2.6 %collective-permute-start.12 = (f16[2,32,2048]{2,1,0:T(8,128)(2,1)S(1)}, f16[2,32,2048]{2,1,0:T(8,128)(2,1)S(1)}, u32[]{:S(2)}, u32[]{:S(2)}) collective-permute-start(f16[2,32,2048]{2,1,0:T(8,128)(2,1)S(1)} %get-tuple-element.92), channel_id=1, source_target_pairs={{0,8},{1,9},{2,10},{3,11},{4,12},{5,13},{6,14},{7,15},{8,0},{9,1},... | collective-permute-start | bytes 786440 | tf_op jit(solution)/shard_map/ppermute | solution.py:189
  33.2 0.5 collective-permute-done.8
  33.7 0.2 fusion.16
  34.0 0.5 collective-permute-start.9
  34.5 1.2 %collective-permute-done.10 = f16[32,4096]{1,0:T(8,128)(2,1)S(1)} collective-permute-done((f16[32,4096]{1,0:T(8,128)(2,1)S(1)}, f16[32,4096]{1,0:T(8,128)(2,1)S(1)}, u32[]{:S(2)}, u32[]{:S(2)}) %collective-permute-start.10) | collective-permute-done | bytes 262176 | tf_op jit(solution)/shard_map/ppermute | solution.py:189
  36.0 0.5 collective-permute-start.11
  36.6 3.8 %collective-permute-done.9 = f16[32,2048]{1,0:T(8,128)(2,1)S(1)} collective-permute-done((f16[32,2048]{1,0:T(8,128)(2,1)S(1)}, f16[32,2048]{1,0:T(8,128)(2,1)S(1)}, u32[]{:S(2)}, u32[]{:S(2)}) %collective-permute-start.9) | collective-permute-done | bytes 131104 | tf_op jit(solution)/shard_map/ppermute | solution.py:189
  40.5 0.6 collective-permute-done.11
  41.3 3.5 %collective-permute-start.17 = (f16[2,32,2048]{2,1,0:T(8,128)(2,1)S(1)}, f16[2,32,2048]{2,1,0:T(8,128)(2,1)S(1)}, u32[]{:S(2)}, u32[]{:S(2)}) collective-permute-start(f16[2,32,2048]{2,1,0:T(8,128)(2,1)S(1)} %multiply_convert_fusion.3), channel_id=1, source_target_pairs={{0,8},{1,9},{2,10},{3,11},{4,12},{5,13},{6,14},{7,15},{8,0},{9,1},... | collective-permute-start | bytes 786440 | tf_op jit(solution)/shard_map/ppermute | solution.py:189
  44.9 0.3 constant_dynamic-slice_fusion.3
  45.4 4.3 %collective-permute-start.13 = (bf16[2,32,2048]{2,1,0:T(8,128)(2,1)S(1)}, bf16[2,32,2048]{2,1,0:T(8,128)(2,1)S(1)}, u32[]{:S(2)}, u32[]{:S(2)}) collective-permute-start(bf16[2,32,2048]{2,1,0:T(8,128)(2,1)S(1)} %fusion.21), channel_id=1, source_target_pairs={{0,4},{1,5},{2,6},{3,7},{4,0},{5,1},{6,2},{7,3},{8,12},{9,13},{10,... | collective-permute-start | bytes 786440 | tf_op jit(solution)/shard_map/ppermute | solution.py:189
  49.7 3.9 %collective-permute-done.17 = f16[2,32,2048]{2,1,0:T(8,128)(2,1)S(1)} collective-permute-done((f16[2,32,2048]{2,1,0:T(8,128)(2,1)S(1)}, f16[2,32,2048]{2,1,0:T(8,128)(2,1)S(1)}, u32[]{:S(2)}, u32[]{:S(2)}) %collective-permute-start.17) | collective-permute-done | bytes 262176 | tf_op jit(solution)/shard_map/ppermute | solution.py:189
  53.7 0.7 collective-permute-start.18
  54.4 1.9 %collective-permute-done.13 = bf16[2,32,2048]{2,1,0:T(8,128)(2,1)S(1)} collective-permute-done((bf16[2,32,2048]{2,1,0:T(8,128)(2,1)S(1)}, bf16[2,32,2048]{2,1,0:T(8,128)(2,1)S(1)}, u32[]{:S(2)}, u32[]{:S(2)}) %collective-permute-start.13) | collective-permute-done | bytes 262176 | tf_op jit(solution)/shard_map/ppermute | solution.py:189
  56.5 1.6 %collective-permute-done.14 = bf16[160,2048]{1,0:T(8,128)(2,1)S(1)} collective-permute-done((bf16[160,2048]{1,0:T(8,128)(2,1)S(1)}, bf16[160,2048]{1,0:T(8,128)(2,1)S(1)}, u32[]{:S(2)}, u32[]{:S(2)}) %collective-permute-start.14) | collective-permute-done | bytes 655392 | tf_op jit(solution)/shard_map/ppermute | solution.py:189
  58.1 0.7 fusion.1.refs_0_
  58.9 1.3 %collective-permute-done.16 = bf16[160,2048]{1,0:T(8,128)(2,1)S(1)} collective-permute-done((bf16[160,2048]{1,0:T(8,128)(2,1)S(1)}, bf16[160,2048]{1,0:T(8,128)(2,1)S(1)}, u32[]{:S(2)}, u32[]{:S(2)}) %collective-permute-start.16) | collective-permute-done | bytes 655392 | tf_op jit(solution)/shard_map/ppermute | solution.py:189
  60.2 0.9 %fusion.43.refs_1_ = f32[512,128]{1,0:T(8,128)S(1)} fusion(bf16[512,2048]{1,0:T(8,128)(2,1)S(1)} %constant_dynamic-update-slice_fusion, bf16[128,2048]{1,0:T(8,128)(2,1)S(1)} %bitcast.31), kind=kOutput, calls=%fused_computation.88 | convolution fusion | flops 268435456 | bytes 2883584 | tf_op jit(solution)/shard_map/dot_general | solution.py:260
  61.2 0.7 fusion.44.refs_3_
  61.9 0.7 fusion.refs_2_
  62.7 1.8 %shard_map.75 = bf16[16,64,256]{2,1,0:T(8,128)(2,1)} custom-call(s32[16]{0:T(128)S(1)} %copy-done.1, f32[512,128]{1,0:T(8,128)S(1)} %fusion.1.refs_0_, f32[512,128]{1,0:T(8,128)S(1)} %fusion.43.refs_1_, f32[512,128]{1,0:T(8,128)S(1)} %fusion.refs_2_, f32[512,128]{1,0:T(8,128)S(1)} %fusion.44.refs_3_), custom_call_target="tpu_custom_call" | custom-call | flops 65536 | bytes 1572864 | tf_op jit(solution)/shard_map/pallas_call | solution.py:137
  64.5 5.4 %all-to-all-start = ((bf16[16,1,64,256]{3,2,1,0:T(8,128)(2,1)}), bf16[16,1,64,256]{3,2,1,0:T(8,128)(2,1)S(1)}, u32[]{:S(2)}, u32[]{:S(2)}) async-start(bf16[16,1,64,256]{3,2,1,0:T(8,128)(2,1)} %bitcast.10), calls=%async_computation | async-start | bytes 1048576 | tf_op jit(solution)/shard_map/all_to_all | solution.py:314
  70.0 0.6 dynamic_slice.79
  70.8 0.3 fusion.36
  71.0 0.6 constant_dynamic-slice_fusion.allowed_ref
  71.7 12.7 %all-to-all-done = bf16[16,1,64,256]{3,2,1,0:T(8,128)(2,1)S(1)} async-done(((bf16[16,1,64,256]{3,2,1,0:T(8,128)(2,1)}), bf16[16,1,64,256]{3,2,1,0:T(8,128)(2,1)S(1)}, u32[]{:S(2)}, u32[]{:S(2)}) %all-to-all-start) | async-done | bytes 524320 | tf_op jit(solution)/shard_map/all_to_all | solution.py:314
  84.4 0.9 %shard_map.76 = f32[1024,128]{1,0:T(8,128)} custom-call(bf16[16,1,4,16,256]{4,3,2,1,0:T(8,128)(2,1)S(1)} %bitcast.27, f32[1,512]{1,0:T(1,128)S(1)} %constant_dynamic-slice_fusion.allowed_ref), custom_call_target="tpu_custom_call" | custom-call | flops 262144 | bytes 1048576 | tf_op jit(solution)/shard_map/pallas_call | solution.py:167
  (51 shorter events, 3.3 us)
Async XLA Ops:
  0.0 1.7 %copy-start = (bf16[16,16,4096]{2,1,0:T(8,128)(2,1)S(1)}, bf16[16,16,4096]{2,1,0:T(8,128)(2,1)}, u32[]{:S(2)}) copy-start(bf16[16,16,4096]{2,1,0:T(8,128)(2,1)} %param.9) | copy-start | bytes 6291460
  1.9 22.3 %collective-permute-start.7 = (bf16[96,2048]{1,0:T(8,128)(2,1)S(1)}, bf16[96,2048]{1,0:T(8,128)(2,1)S(1)}, u32[]{:S(2)}, u32[]{:S(2)}) collective-permute-start(bf16[96,2048]{1,0:T(8,128)(2,1)S(1)} %constant_dynamic-slice_fusion.2), channel_id=1, source_target_pairs={{0,2},{1,3},{2,0},{3,1},{4,6},{5,7},{6,4},{7,5},{8,10},{9,11},{10,... | collective-permute-start | bytes 1179656 | tf_op jit(solution)/shard_map/ppermute | solution.py:189
  9.7 2.9 %collective-permute-start = (f16[128,4096]{1,0:T(8,128)(2,1)S(1)}, f16[128,4096]{1,0:T(8,128)(2,1)S(1)}, u32[]{:S(2)}, u32[]{:S(2)}) collective-permute-start(f16[128,4096]{1,0:T(8,128)(2,1)S(1)} %multiply_convert_fusion.1), channel_id=1, source_target_pairs={{0,1},{1,0},{2,3},{3,2},{4,5},{5,4},{6,7},{7,6},{8,9},{9,8},{10,11... | collective-permute-start | bytes 3145736 | tf_op jit(solution)/shard_map/ppermute | solution.py:189
  12.0 3.5 %collective-permute-start.6 = (f16[128,4096]{1,0:T(8,128)(2,1)S(1)}, f16[128,4096]{1,0:T(8,128)(2,1)S(1)}, u32[]{:S(2)}, u32[]{:S(2)}) collective-permute-start(f16[128,4096]{1,0:T(8,128)(2,1)S(1)} %multiply_convert_fusion), channel_id=1, source_target_pairs={{0,1},{1,0},{2,3},{3,2},{4,5},{5,4},{6,7},{7,6},{8,9},{9,8},{10,11... | collective-permute-start | bytes 3145736 | tf_op jit(solution)/shard_map/ppermute | solution.py:189
  13.2 8.3 %collective-permute-start.2 = (f16[64,2048]{1,0:T(8,128)(2,1)S(1)}, f16[64,2048]{1,0:T(8,128)(2,1)S(1)}, u32[]{:S(2)}, u32[]{:S(2)}) collective-permute-start(f16[64,2048]{1,0:T(8,128)(2,1)S(1)} %multiply_convert_fusion.7), channel_id=1, source_target_pairs={{0,2},{1,3},{2,0},{3,1},{4,6},{5,7},{6,4},{7,5},{8,10},{9,11},{10,... | collective-permute-start | bytes 786440 | tf_op jit(solution)/shard_map/ppermute | solution.py:189
  13.4 10.0 %collective-permute-start.4 = (f16[32,4096]{1,0:T(8,128)(2,1)S(1)}, f16[32,4096]{1,0:T(8,128)(2,1)S(1)}, u32[]{:S(2)}, u32[]{:S(2)}) collective-permute-start(f16[32,4096]{1,0:T(8,128)(2,1)S(1)} %multiply_convert_fusion.6), channel_id=1, source_target_pairs={{0,4},{1,5},{2,6},{3,7},{4,0},{5,1},{6,2},{7,3},{8,12},{9,13},{10,... | collective-permute-start | bytes 786440 | tf_op jit(solution)/shard_map/ppermute | solution.py:189
  16.5 41.6 %collective-permute-start.1 = (bf16[256,2048]{1,0:T(8,128)(2,1)S(1)}, bf16[256,2048]{1,0:T(8,128)(2,1)S(1)}, u32[]{:S(2)}, u32[]{:S(2)}) collective-permute-start(bf16[256,2048]{1,0:T(8,128)(2,1)S(1)} %constant_dynamic-slice_fusion.1), channel_id=1, source_target_pairs={{0,1},{1,0},{2,3},{3,2},{4,5},{5,4},{6,7},{7,6},{8,9},{9,8},{10,11... | collective-permute-start | bytes 3145736 | tf_op jit(solution)/shard_map/ppermute | solution.py:189
  21.8 5.4 %collective-permute-start.3 = (f16[32,2048]{1,0:T(8,128)(2,1)S(1)}, f16[32,2048]{1,0:T(8,128)(2,1)S(1)}, u32[]{:S(2)}, u32[]{:S(2)}) collective-permute-start(f16[32,2048]{1,0:T(8,128)(2,1)S(1)} %multiply_convert_fusion.11), channel_id=1, source_target_pairs={{0,4},{1,5},{2,6},{3,7},{4,0},{5,1},{6,2},{7,3},{8,12},{9,13},{10,... | collective-permute-start | bytes 393224 | tf_op jit(solution)/shard_map/ppermute | solution.py:189
  23.7 6.5 %collective-permute-start.5 = (f16[32,2048]{1,0:T(8,128)(2,1)S(1)}, f16[32,2048]{1,0:T(8,128)(2,1)S(1)}, u32[]{:S(2)}, u32[]{:S(2)}) collective-permute-start(f16[32,2048]{1,0:T(8,128)(2,1)S(1)} %multiply_convert_fusion.10), channel_id=1, source_target_pairs={{0,2},{1,3},{2,0},{3,1},{4,6},{5,7},{6,4},{7,5},{8,10},{9,11},{10,... | collective-permute-start | bytes 393224 | tf_op jit(solution)/shard_map/ppermute | solution.py:189
  24.3 9.4 %collective-permute-start.8 = (f16[64,2048]{1,0:T(8,128)(2,1)S(1)}, f16[64,2048]{1,0:T(8,128)(2,1)S(1)}, u32[]{:S(2)}, u32[]{:S(2)}) collective-permute-start(f16[64,2048]{1,0:T(8,128)(2,1)S(1)} %multiply_convert_fusion.5), channel_id=1, source_target_pairs={{0,2},{1,3},{2,0},{3,1},{4,6},{5,7},{6,4},{7,5},{8,10},{9,11},{10,... | collective-permute-start | bytes 786440 | tf_op jit(solution)/shard_map/ppermute | solution.py:189
  25.8 9.9 %collective-permute-start.10 = (f16[32,4096]{1,0:T(8,128)(2,1)S(1)}, f16[32,4096]{1,0:T(8,128)(2,1)S(1)}, u32[]{:S(2)}, u32[]{:S(2)}) collective-permute-start(f16[32,4096]{1,0:T(8,128)(2,1)S(1)} %multiply_convert_fusion.4), channel_id=1, source_target_pairs={{0,4},{1,5},{2,6},{3,7},{4,0},{5,1},{6,2},{7,3},{8,12},{9,13},{10,... | collective-permute-start | bytes 786440 | tf_op jit(solution)/shard_map/ppermute | solution.py:189
  30.5 14.7 %collective-permute-start.12 = (f16[2,32,2048]{2,1,0:T(8,128)(2,1)S(1)}, f16[2,32,2048]{2,1,0:T(8,128)(2,1)S(1)}, u32[]{:S(2)}, u32[]{:S(2)}) collective-permute-start(f16[2,32,2048]{2,1,0:T(8,128)(2,1)S(1)} %get-tuple-element.92), channel_id=1, source_target_pairs={{0,8},{1,9},{2,10},{3,11},{4,12},{5,13},{6,14},{7,15},{8,0},{9,1},... | collective-permute-start | bytes 786440 | tf_op jit(solution)/shard_map/ppermute | solution.py:189
  34.0 6.4 %collective-permute-start.9 = (f16[32,2048]{1,0:T(8,128)(2,1)S(1)}, f16[32,2048]{1,0:T(8,128)(2,1)S(1)}, u32[]{:S(2)}, u32[]{:S(2)}) collective-permute-start(f16[32,2048]{1,0:T(8,128)(2,1)S(1)} %multiply_convert_fusion.9), channel_id=1, source_target_pairs={{0,4},{1,5},{2,6},{3,7},{4,0},{5,1},{6,2},{7,3},{8,12},{9,13},{10,... | collective-permute-start | bytes 393224 | tf_op jit(solution)/shard_map/ppermute | solution.py:189
  36.0 5.0 %collective-permute-start.11 = (f16[32,2048]{1,0:T(8,128)(2,1)S(1)}, f16[32,2048]{1,0:T(8,128)(2,1)S(1)}, u32[]{:S(2)}, u32[]{:S(2)}) collective-permute-start(f16[32,2048]{1,0:T(8,128)(2,1)S(1)} %multiply_convert_fusion.8), channel_id=1, source_target_pairs={{0,2},{1,3},{2,0},{3,1},{4,6},{5,7},{6,4},{7,5},{8,10},{9,11},{10,... | collective-permute-start | bytes 393224 | tf_op jit(solution)/shard_map/ppermute | solution.py:189
  41.3 12.2 %collective-permute-start.17 = (f16[2,32,2048]{2,1,0:T(8,128)(2,1)S(1)}, f16[2,32,2048]{2,1,0:T(8,128)(2,1)S(1)}, u32[]{:S(2)}, u32[]{:S(2)}) collective-permute-start(f16[2,32,2048]{2,1,0:T(8,128)(2,1)S(1)} %multiply_convert_fusion.3), channel_id=1, source_target_pairs={{0,8},{1,9},{2,10},{3,11},{4,12},{5,13},{6,14},{7,15},{8,0},{9,1},... | collective-permute-start | bytes 786440 | tf_op jit(solution)/shard_map/ppermute | solution.py:189
  45.2 12.9 %collective-permute-start.14 = (bf16[160,2048]{1,0:T(8,128)(2,1)S(1)}, bf16[160,2048]{1,0:T(8,128)(2,1)S(1)}, u32[]{:S(2)}, u32[]{:S(2)}) collective-permute-start(bf16[160,2048]{1,0:T(8,128)(2,1)S(1)} %constant_dynamic-slice_fusion.3), channel_id=1, source_target_pairs={{0,2},{1,3},{2,0},{3,1},{4,6},{5,7},{6,4},{7,5},{8,10},{9,11},{10,... | collective-permute-start | bytes 1966088 | tf_op jit(solution)/shard_map/ppermute | solution.py:189
  45.4 11.0 %collective-permute-start.13 = (bf16[2,32,2048]{2,1,0:T(8,128)(2,1)S(1)}, bf16[2,32,2048]{2,1,0:T(8,128)(2,1)S(1)}, u32[]{:S(2)}, u32[]{:S(2)}) collective-permute-start(bf16[2,32,2048]{2,1,0:T(8,128)(2,1)S(1)} %fusion.21), channel_id=1, source_target_pairs={{0,4},{1,5},{2,6},{3,7},{4,0},{5,1},{6,2},{7,3},{8,12},{9,13},{10,... | collective-permute-start | bytes 786440 | tf_op jit(solution)/shard_map/ppermute | solution.py:189
  49.7 9.1 %collective-permute-start.15 = (bf16[96,2048]{1,0:T(8,128)(2,1)S(1)}, bf16[96,2048]{1,0:T(8,128)(2,1)S(1)}, u32[]{:S(2)}, u32[]{:S(2)}) collective-permute-start(bf16[96,2048]{1,0:T(8,128)(2,1)S(1)} %collective-permute-done.7), channel_id=1, source_target_pairs={{0,1},{1,0},{2,3},{3,2},{4,5},{5,4},{6,7},{7,6},{8,9},{9,8},{10,11... | collective-permute-start | bytes 1179656 | tf_op jit(solution)/shard_map/ppermute | solution.py:189
  53.7 7.4 %collective-permute-start.18 = (bf16[2,32,2048]{2,1,0:T(8,128)(2,1)S(1)}, bf16[2,32,2048]{2,1,0:T(8,128)(2,1)S(1)}, u32[]{:S(2)}, u32[]{:S(2)}) collective-permute-start(bf16[2,32,2048]{2,1,0:T(8,128)(2,1)S(1)} %fusion.24), channel_id=1, source_target_pairs={{0,4},{1,5},{2,6},{3,7},{4,0},{5,1},{6,2},{7,3},{8,12},{9,13},{10,... | collective-permute-start | bytes 786440 | tf_op jit(solution)/shard_map/ppermute | solution.py:189
  58.0 2.1 %collective-permute-start.16 = (bf16[160,2048]{1,0:T(8,128)(2,1)S(1)}, bf16[160,2048]{1,0:T(8,128)(2,1)S(1)}, u32[]{:S(2)}, u32[]{:S(2)}) collective-permute-start(bf16[160,2048]{1,0:T(8,128)(2,1)S(1)} %collective-permute-done.14), channel_id=1, source_target_pairs={{0,1},{1,0},{2,3},{3,2},{4,5},{5,4},{6,7},{7,6},{8,9},{9,8},{10,11... | collective-permute-start | bytes 1966088 | tf_op jit(solution)/shard_map/ppermute | solution.py:189
  61.9 0.8 copy-start.1
  62.7 7.2 %copy-start.2 = (s32[8,12]{1,0:T(8,128)S(1)}, s32[8,12]{1,0:T(8,128)}, u32[]{:S(2)}) copy-start(s32[8,12]{1,0:T(8,128)} %param.11) | copy-start | bytes 1156
  62.7 7.9 %copy-start.3 = (s32[8]{0:T(128)S(1)}, s32[8]{0:T(128)}, u32[]{:S(2)}) copy-start(s32[8]{0:T(128)} %param.12) | copy-start | bytes 100
  62.7 8.0 %copy-start.4 = (s32[512]{0:T(512)S(1)}, s32[512]{0:T(512)}, u32[]{:S(2)}) copy-start(s32[512]{0:T(512)} %param.10) | copy-start | bytes 6148
  64.5 19.9 %all-to-all-start = ((bf16[16,1,64,256]{3,2,1,0:T(8,128)(2,1)}), bf16[16,1,64,256]{3,2,1,0:T(8,128)(2,1)S(1)}, u32[]{:S(2)}, u32[]{:S(2)}) async-start(bf16[16,1,64,256]{3,2,1,0:T(8,128)(2,1)} %bitcast.10), calls=%async_computation | async-start | bytes 1048576 | tf_op jit(solution)/shard_map/all_to_all | solution.py:314

commit v22 on v21

--- a/solution.py
+++ b/solution.py
@@ -11,7 +11,8 @@
 UNIT = 2.0 ** 18
 LEAST = 2.0 ** -100
 LANES = 128
-AHEAD = 3
+AHEAD = 6
+LOAD_COLUMNS = 256
 OTHER_VMEM = 44
 MINE_VMEM = 16
 
@@ -78,7 +79,7 @@
 def product(core, rows, columns, kernel, vmem, pieces):
     nrows = rows.shape[0]
     depth, width = columns[0].shape
-    block = min(512, width)
+    block = min(LOAD_COLUMNS, width)
     out = [jax.ShapeDtypeStruct((nrows // CORES // pieces, width), jnp.float32)] * pieces
     in_vmem = pl.BlockSpec(memory_space=pltpu.VMEM)
     operand, scratch = in_vmem, []

time: 85.6 us -> 88 us (1.028)
  Pallas kernels: 8.68 us -> 11.4 us
    pallas_call x2, Pallas kernels: 6.04 us -> 8.74 us  [product(): pl.pallas_call(kernel, in_specs=[pl.BlockSpec(memory_space=pltpu.SMEM), i...]
  transfers between devices with their start and end apart: 20 -> 20, of which waited for: 12 -> 12; matrix products, arithmetic and copies ran while one was open for 10% -> 10% of each run, Pallas kernels for 7% -> 10%
where the time goes in v22:
time: 88 us; the launch traced here: 87.7 us
  waiting for transfers between devices  36.1 us (41%)
  starting transfers between devices  27.6 us (31%)
  Pallas kernels  11.4 us (13%)
  other arithmetic  6.04 us (7%)
  matrix products  3.33 us (4%)
  local copies, waits for them, and re-layouts  2.78 us (3%)
    ppermute x19, waiting for transfers between devices, swap(): return lax.ppermute(value, 'rows', [(r, r ^ 1 << bit) for r in range(n)])  23.3 us
    ppermute x19, starting transfers between devices, swap(): return lax.ppermute(value, 'rows', [(r, r ^ 1 << bit) for r in range(n)])  22.3 us
    all_to_all x1, waiting for transfers between devices, shards(): lax.all_to_all(ordered, 'rows', split_axis=0, concat_axis=0, tiled=True)  12.7 us
    pallas_call x2, Pallas kernels, product(): pl.pallas_call(kernel, in_specs=[pl.BlockSpec(memory_space=pltpu.SMEM), i...  8.74 us
    all_to_all x1, starting transfers between devices, shards(): lax.all_to_all(ordered, 'rows', split_axis=0, concat_axis=0, tiled=True)  5.3 us
    dot_general x4, matrix products, scores(): lax.dot_general(group, value, (((1,), (1,)), ((), ())), preferred_element...  3.07 us
    convert_element_type x12, other arithmetic, pack(): return (value * lax.rsqrt(jnp.abs(value) + LEAST)).astype(jnp.float16)  2.39 us
    pallas_call x1, Pallas kernels, in_slot_order(): pl.pallas_call(order_kernel, in_specs=[pl.BlockSpec(memory_space=pltpu.SM...  1.78 us
  transfers between devices with their start and end apart: 20, of which 12 were waited for; matrix products, arithmetic and copies ran while one was open for 10% of the time, Pallas kernels for 10%

profile of v22, /device:TPU:0, one launch (start us, length us, event | category | flops | bytes accessed | tf_op | source)
XLA Modules:
  0.0 87.7 jit_solution(9338856664729040922)
XLA Ops:
  0.0 1.3 %fusion.10 = (bf16[512,256]{1,0:T(8,128)(2,1)S(1)}, bf16[512,256]{1,0:T(8,128)(2,1)S(1)}) fusion(f32[512,256]{1,0:T(8,128)} %param.7), kind=kLoop, calls=%fused_computation.26 | loop fusion | flops 524288 | bytes 1048576 | tf_op jit(solution)/shard_map/convert_element_type | solution.py:272
  1.3 0.4 copy-done
  1.9 3.0 %collective-permute-start.7 = (bf16[96,2048]{1,0:T(8,128)(2,1)S(1)}, bf16[96,2048]{1,0:T(8,128)(2,1)S(1)}, u32[]{:S(2)}, u32[]{:S(2)}) collective-permute-start(bf16[96,2048]{1,0:T(8,128)(2,1)S(1)} %constant_dynamic-slice_fusion.2), channel_id=1, source_target_pairs={{0,2},{1,3},{2,0},{3,1},{4,6},{5,7},{6,4},{7,5},{8,10},{9,11},{10,... | collective-permute-start | bytes 1179656 | tf_op jit(solution)/shard_map/ppermute | solution.py:190
  5.0 6.9 %shard_map.73 = (f32[128,4096]{1,0:T(8,128)S(1)}, f32[128,4096]{1,0:T(8,128)S(1)}, bf16[256,4096]{1,0:T(8,128)(2,1)S(1)}, bf16[256,4096]{1,0:T(8,128)(2,1)S(1)}) custom-call(s32[1]{0:T(128)} %bitcast.1.core_ref, bf16[512,768]{1,0:T(8,128)(2,1)S(1)} %pad_maximum_fusion.3.rows_ref, f32[256,4096]{1,0:T(8,128)} %columns_hbm.1), custom_call_target="tpu_custom_call" | custom-call | flops 1610612736 | bytes 8388608 | tf_op jit(solution)/shard_map/pallas_call | solution.py:93
  11.9 0.4 multiply_convert_fusion.1
  12.5 1.8 %shard_map.74 = (f32[64,4096]{1,0:T(8,128)S(1)}, f32[64,4096]{1,0:T(8,128)S(1)}, f32[64,4096]{1,0:T(8,128)S(1)}, f32[64,4096]{1,0:T(8,128)S(1)}) custom-call(s32[1]{0:T(128)} %bitcast.2.core_ref, bf16[512,768]{1,0:T(8,128)(2,1)S(1)} %pad_maximum_fusion.3.rows_ref, bf16[256,4096]{1,0:T(8,128)(2,1)S(1)} %get-tuple-element.51.high_ref, ...), custom_call_target="tpu_custom_call" | custom-call | flops 1610612736 | bytes 8388608 | tf_op jit(solution)/shard_map/pallas_call | solution.py:93
  14.3 0.4 multiply_convert_fusion
  14.7 0.6 collective-permute-start.6
  15.3 0.4 fusion.3
  15.6 0.2 multiply_convert_fusion.7
  16.1 2.1 %collective-permute-start.4 = (f16[32,4096]{1,0:T(8,128)(2,1)S(1)}, f16[32,4096]{1,0:T(8,128)(2,1)S(1)}, u32[]{:S(2)}, u32[]{:S(2)}) collective-permute-start(f16[32,4096]{1,0:T(8,128)(2,1)S(1)} %multiply_convert_fusion.6), channel_id=1, source_target_pairs={{0,4},{1,5},{2,6},{3,7},{4,0},{5,1},{6,2},{7,3},{8,12},{9,13},{10,... | collective-permute-start | bytes 786440 | tf_op jit(solution)/shard_map/ppermute | solution.py:190
  18.2 0.4 fusion.9
  18.8 0.4 constant_dynamic-slice_fusion.1
  19.3 0.2 multiply_convert_fusion.5
  19.5 4.7 %collective-permute-done.2 = f16[64,2048]{1,0:T(8,128)(2,1)S(1)} collective-permute-done((f16[64,2048]{1,0:T(8,128)(2,1)S(1)}, f16[64,2048]{1,0:T(8,128)(2,1)S(1)}, u32[]{:S(2)}, u32[]{:S(2)}) %collective-permute-start.2) | collective-permute-done | bytes 262176 | tf_op jit(solution)/shard_map/ppermute | solution.py:190
  24.5 1.6 %collective-permute-start.3 = (f16[32,2048]{1,0:T(8,128)(2,1)S(1)}, f16[32,2048]{1,0:T(8,128)(2,1)S(1)}, u32[]{:S(2)}, u32[]{:S(2)}) collective-permute-start(f16[32,2048]{1,0:T(8,128)(2,1)S(1)} %multiply_convert_fusion.11), channel_id=1, source_target_pairs={{0,4},{1,5},{2,6},{3,7},{4,0},{5,1},{6,2},{7,3},{8,12},{9,13},{10,... | collective-permute-start | bytes 393224 | tf_op jit(solution)/shard_map/ppermute | solution.py:190
  26.4 0.6 collective-permute-start.5
  27.0 1.5 %collective-permute-start.8 = (f16[64,2048]{1,0:T(8,128)(2,1)S(1)}, f16[64,2048]{1,0:T(8,128)(2,1)S(1)}, u32[]{:S(2)}, u32[]{:S(2)}) collective-permute-start(f16[64,2048]{1,0:T(8,128)(2,1)S(1)} %multiply_convert_fusion.5), channel_id=1, source_target_pairs={{0,2},{1,3},{2,0},{3,1},{4,6},{5,7},{6,4},{7,5},{8,10},{9,11},{10,... | collective-permute-start | bytes 786440 | tf_op jit(solution)/shard_map/ppermute | solution.py:190
  28.5 0.4 collective-permute-start.10
  29.0 0.8 collective-permute-done.3
  29.9 3.0 %collective-permute-done.5 = f16[32,2048]{1,0:T(8,128)(2,1)S(1)} collective-permute-done((f16[32,2048]{1,0:T(8,128)(2,1)S(1)}, f16[32,2048]{1,0:T(8,128)(2,1)S(1)}, u32[]{:S(2)}, u32[]{:S(2)}) %collective-permute-start.5) | collective-permute-done | bytes 131104 | tf_op jit(solution)/shard_map/ppermute | solution.py:190
  33.2 2.7 %collective-permute-start.12 = (f16[2,32,2048]{2,1,0:T(8,128)(2,1)S(1)}, f16[2,32,2048]{2,1,0:T(8,128)(2,1)S(1)}, u32[]{:S(2)}, u32[]{:S(2)}) collective-permute-start(f16[2,32,2048]{2,1,0:T(8,128)(2,1)S(1)} %get-tuple-element.92), channel_id=1, source_target_pairs={{0,8},{1,9},{2,10},{3,11},{4,12},{5,13},{6,14},{7,15},{8,0},{9,1},... | collective-permute-start | bytes 786440 | tf_op jit(solution)/shard_map/ppermute | solution.py:190
  35.9 0.5 collective-permute-done.8
  36.4 0.2 fusion.16
  36.7 0.5 collective-permute-start.9
  37.2 1.3 %collective-permute-done.10 = f16[32,4096]{1,0:T(8,128)(2,1)S(1)} collective-permute-done((f16[32,4096]{1,0:T(8,128)(2,1)S(1)}, f16[32,4096]{1,0:T(8,128)(2,1)S(1)}, u32[]{:S(2)}, u32[]{:S(2)}) %collective-permute-start.10) | collective-permute-done | bytes 262176 | tf_op jit(solution)/shard_map/ppermute | solution.py:190
  38.8 0.5 collective-permute-start.11
  39.3 3.8 %collective-permute-done.9 = f16[32,2048]{1,0:T(8,128)(2,1)S(1)} collective-permute-done((f16[32,2048]{1,0:T(8,128)(2,1)S(1)}, f16[32,2048]{1,0:T(8,128)(2,1)S(1)}, u32[]{:S(2)}, u32[]{:S(2)}) %collective-permute-start.9) | collective-permute-done | bytes 131104 | tf_op jit(solution)/shard_map/ppermute | solution.py:190
  43.2 0.7 collective-permute-done.11
  44.1 3.4 %collective-permute-start.17 = (f16[2,32,2048]{2,1,0:T(8,128)(2,1)S(1)}, f16[2,32,2048]{2,1,0:T(8,128)(2,1)S(1)}, u32[]{:S(2)}, u32[]{:S(2)}) collective-permute-start(f16[2,32,2048]{2,1,0:T(8,128)(2,1)S(1)} %multiply_convert_fusion.3), channel_id=1, source_target_pairs={{0,8},{1,9},{2,10},{3,11},{4,12},{5,13},{6,14},{7,15},{8,0},{9,1},... | collective-permute-start | bytes 786440 | tf_op jit(solution)/shard_map/ppermute | solution.py:190
  47.5 0.3 constant_dynamic-slice_fusion.3
  48.0 4.4 %collective-permute-start.13 = (bf16[2,32,2048]{2,1,0:T(8,128)(2,1)S(1)}, bf16[2,32,2048]{2,1,0:T(8,128)(2,1)S(1)}, u32[]{:S(2)}, u32[]{:S(2)}) collective-permute-start(bf16[2,32,2048]{2,1,0:T(8,128)(2,1)S(1)} %fusion.21), channel_id=1, source_target_pairs={{0,4},{1,5},{2,6},{3,7},{4,0},{5,1},{6,2},{7,3},{8,12},{9,13},{10,... | collective-permute-start | bytes 786440 | tf_op jit(solution)/shard_map/ppermute | solution.py:190
  52.4 3.9 %collective-permute-done.17 = f16[2,32,2048]{2,1,0:T(8,128)(2,1)S(1)} collective-permute-done((f16[2,32,2048]{2,1,0:T(8,128)(2,1)S(1)}, f16[2,32,2048]{2,1,0:T(8,128)(2,1)S(1)}, u32[]{:S(2)}, u32[]{:S(2)}) %collective-permute-start.17) | collective-permute-done | bytes 262176 | tf_op jit(solution)/shard_map/ppermute | solution.py:190
  56.4 0.7 collective-permute-start.18
  57.1 1.9 %collective-permute-done.13 = bf16[2,32,2048]{2,1,0:T(8,128)(2,1)S(1)} collective-permute-done((bf16[2,32,2048]{2,1,0:T(8,128)(2,1)S(1)}, bf16[2,32,2048]{2,1,0:T(8,128)(2,1)S(1)}, u32[]{:S(2)}, u32[]{:S(2)}) %collective-permute-start.13) | collective-permute-done | bytes 262176 | tf_op jit(solution)/shard_map/ppermute | solution.py:190
  59.1 1.6 %collective-permute-done.14 = bf16[160,2048]{1,0:T(8,128)(2,1)S(1)} collective-permute-done((bf16[160,2048]{1,0:T(8,128)(2,1)S(1)}, bf16[160,2048]{1,0:T(8,128)(2,1)S(1)}, u32[]{:S(2)}, u32[]{:S(2)}) %collective-permute-start.14) | collective-permute-done | bytes 655392 | tf_op jit(solution)/shard_map/ppermute | solution.py:190
  60.7 0.9 %fusion.1.refs_0_ = f32[512,128]{1,0:T(8,128)S(1)} fusion(bf16[128,2048]{1,0:T(8,128)(2,1)S(1)} %bitcast.30, bf16[256,2048]{1,0:T(8,128)(2,1)S(1)} %collective-permute-done.1, bf16[256,2048]{1,0:T(8,128)(2,1)S(1)} %constant_dynamic-slice_fusion.1), kind=kOutput, calls=%fused_computation.8 | convolution fusion | flops 272629760 | bytes 2883584 | tf_op jit(solution)/shard_map/dot_general | solution.py:261
  61.7 1.1 %collective-permute-done.16 = bf16[160,2048]{1,0:T(8,128)(2,1)S(1)} collective-permute-done((bf16[160,2048]{1,0:T(8,128)(2,1)S(1)}, bf16[160,2048]{1,0:T(8,128)(2,1)S(1)}, u32[]{:S(2)}, u32[]{:S(2)}) %collective-permute-start.16) | collective-permute-done | bytes 655392 | tf_op jit(solution)/shard_map/ppermute | solution.py:190
  62.9 0.7 fusion.43.refs_1_
  63.7 0.7 fusion.44.refs_3_
  64.5 0.7 fusion.refs_2_
  65.3 1.8 %shard_map.75 = bf16[16,64,256]{2,1,0:T(8,128)(2,1)} custom-call(s32[16]{0:T(128)S(1)} %copy-done.1, f32[512,128]{1,0:T(8,128)S(1)} %fusion.1.refs_0_, f32[512,128]{1,0:T(8,128)S(1)} %fusion.43.refs_1_, f32[512,128]{1,0:T(8,128)S(1)} %fusion.refs_2_, f32[512,128]{1,0:T(8,128)S(1)} %fusion.44.refs_3_), custom_call_target="tpu_custom_call" | custom-call | flops 65536 | bytes 1572864 | tf_op jit(solution)/shard_map/pallas_call | solution.py:138
  67.0 5.3 %all-to-all-start = ((bf16[16,1,64,256]{3,2,1,0:T(8,128)(2,1)}), bf16[16,1,64,256]{3,2,1,0:T(8,128)(2,1)S(1)}, u32[]{:S(2)}, u32[]{:S(2)}) async-start(bf16[16,1,64,256]{3,2,1,0:T(8,128)(2,1)} %bitcast.10), calls=%async_computation | async-start | bytes 1048576 | tf_op jit(solution)/shard_map/all_to_all | solution.py:315
  72.4 0.6 dynamic_slice.79
  73.2 0.3 fusion.36
  73.4 0.6 constant_dynamic-slice_fusion.allowed_ref
  74.1 12.7 %all-to-all-done = bf16[16,1,64,256]{3,2,1,0:T(8,128)(2,1)S(1)} async-done(((bf16[16,1,64,256]{3,2,1,0:T(8,128)(2,1)}), bf16[16,1,64,256]{3,2,1,0:T(8,128)(2,1)S(1)}, u32[]{:S(2)}, u32[]{:S(2)}) %all-to-all-start) | async-done | bytes 524320 | tf_op jit(solution)/shard_map/all_to_all | solution.py:315
  86.8 0.9 shard_map.76
  (51 shorter events, 3.3 us)
Async XLA Ops:
  0.0 1.7 %copy-start = (bf16[16,16,4096]{2,1,0:T(8,128)(2,1)S(1)}, bf16[16,16,4096]{2,1,0:T(8,128)(2,1)}, u32[]{:S(2)}) copy-start(bf16[16,16,4096]{2,1,0:T(8,128)(2,1)} %param.9) | copy-start | bytes 6291460
  1.9 25.1 %collective-permute-start.7 = (bf16[96,2048]{1,0:T(8,128)(2,1)S(1)}, bf16[96,2048]{1,0:T(8,128)(2,1)S(1)}, u32[]{:S(2)}, u32[]{:S(2)}) collective-permute-start(bf16[96,2048]{1,0:T(8,128)(2,1)S(1)} %constant_dynamic-slice_fusion.2), channel_id=1, source_target_pairs={{0,2},{1,3},{2,0},{3,1},{4,6},{5,7},{6,4},{7,5},{8,10},{9,11},{10,... | collective-permute-start | bytes 1179656 | tf_op jit(solution)/shard_map/ppermute | solution.py:190
  12.4 2.9 %collective-permute-start = (f16[128,4096]{1,0:T(8,128)(2,1)S(1)}, f16[128,4096]{1,0:T(8,128)(2,1)S(1)}, u32[]{:S(2)}, u32[]{:S(2)}) collective-permute-start(f16[128,4096]{1,0:T(8,128)(2,1)S(1)} %multiply_convert_fusion.1), channel_id=1, source_target_pairs={{0,1},{1,0},{2,3},{3,2},{4,5},{5,4},{6,7},{7,6},{8,9},{9,8},{10,11... | collective-permute-start | bytes 3145736 | tf_op jit(solution)/shard_map/ppermute | solution.py:190
  14.7 3.5 %collective-permute-start.6 = (f16[128,4096]{1,0:T(8,128)(2,1)S(1)}, f16[128,4096]{1,0:T(8,128)(2,1)S(1)}, u32[]{:S(2)}, u32[]{:S(2)}) collective-permute-start(f16[128,4096]{1,0:T(8,128)(2,1)S(1)} %multiply_convert_fusion), channel_id=1, source_target_pairs={{0,1},{1,0},{2,3},{3,2},{4,5},{5,4},{6,7},{7,6},{8,9},{9,8},{10,11... | collective-permute-start | bytes 3145736 | tf_op jit(solution)/shard_map/ppermute | solution.py:190
  15.9 8.3 %collective-permute-start.2 = (f16[64,2048]{1,0:T(8,128)(2,1)S(1)}, f16[64,2048]{1,0:T(8,128)(2,1)S(1)}, u32[]{:S(2)}, u32[]{:S(2)}) collective-permute-start(f16[64,2048]{1,0:T(8,128)(2,1)S(1)} %multiply_convert_fusion.7), channel_id=1, source_target_pairs={{0,2},{1,3},{2,0},{3,1},{4,6},{5,7},{6,4},{7,5},{8,10},{9,11},{10,... | collective-permute-start | bytes 786440 | tf_op jit(solution)/shard_map/ppermute | solution.py:190
  16.1 10.0 %collective-permute-start.4 = (f16[32,4096]{1,0:T(8,128)(2,1)S(1)}, f16[32,4096]{1,0:T(8,128)(2,1)S(1)}, u32[]{:S(2)}, u32[]{:S(2)}) collective-permute-start(f16[32,4096]{1,0:T(8,128)(2,1)S(1)} %multiply_convert_fusion.6), channel_id=1, source_target_pairs={{0,4},{1,5},{2,6},{3,7},{4,0},{5,1},{6,2},{7,3},{8,12},{9,13},{10,... | collective-permute-start | bytes 786440 | tf_op jit(solution)/shard_map/ppermute | solution.py:190
  19.2 41.5 %collective-permute-start.1 = (bf16[256,2048]{1,0:T(8,128)(2,1)S(1)}, bf16[256,2048]{1,0:T(8,128)(2,1)S(1)}, u32[]{:S(2)}, u32[]{:S(2)}) collective-permute-start(bf16[256,2048]{1,0:T(8,128)(2,1)S(1)} %constant_dynamic-slice_fusion.1), channel_id=1, source_target_pairs={{0,1},{1,0},{2,3},{3,2},{4,5},{5,4},{6,7},{7,6},{8,9},{9,8},{10,11... | collective-permute-start | bytes 3145736 | tf_op jit(solution)/shard_map/ppermute | solution.py:190
  24.5 5.3 %collective-permute-start.3 = (f16[32,2048]{1,0:T(8,128)(2,1)S(1)}, f16[32,2048]{1,0:T(8,128)(2,1)S(1)}, u32[]{:S(2)}, u32[]{:S(2)}) collective-permute-start(f16[32,2048]{1,0:T(8,128)(2,1)S(1)} %multiply_convert_fusion.11), channel_id=1, source_target_pairs={{0,4},{1,5},{2,6},{3,7},{4,0},{5,1},{6,2},{7,3},{8,12},{9,13},{10,... | collective-permute-start | bytes 393224 | tf_op jit(solution)/shard_map/ppermute | solution.py:190
  26.4 6.5 %collective-permute-start.5 = (f16[32,2048]{1,0:T(8,128)(2,1)S(1)}, f16[32,2048]{1,0:T(8,128)(2,1)S(1)}, u32[]{:S(2)}, u32[]{:S(2)}) collective-permute-start(f16[32,2048]{1,0:T(8,128)(2,1)S(1)} %multiply_convert_fusion.10), channel_id=1, source_target_pairs={{0,2},{1,3},{2,0},{3,1},{4,6},{5,7},{6,4},{7,5},{8,10},{9,11},{10,... | collective-permute-start | bytes 393224 | tf_op jit(solution)/shard_map/ppermute | solution.py:190
  27.0 9.4 %collective-permute-start.8 = (f16[64,2048]{1,0:T(8,128)(2,1)S(1)}, f16[64,2048]{1,0:T(8,128)(2,1)S(1)}, u32[]{:S(2)}, u32[]{:S(2)}) collective-permute-start(f16[64,2048]{1,0:T(8,128)(2,1)S(1)} %multiply_convert_fusion.5), channel_id=1, source_target_pairs={{0,2},{1,3},{2,0},{3,1},{4,6},{5,7},{6,4},{7,5},{8,10},{9,11},{10,... | collective-permute-start | bytes 786440 | tf_op jit(solution)/shard_map/ppermute | solution.py:190
  28.5 10.0 %collective-permute-start.10 = (f16[32,4096]{1,0:T(8,128)(2,1)S(1)}, f16[32,4096]{1,0:T(8,128)(2,1)S(1)}, u32[]{:S(2)}, u32[]{:S(2)}) collective-permute-start(f16[32,4096]{1,0:T(8,128)(2,1)S(1)} %multiply_convert_fusion.4), channel_id=1, source_target_pairs={{0,4},{1,5},{2,6},{3,7},{4,0},{5,1},{6,2},{7,3},{8,12},{9,13},{10,... | collective-permute-start | bytes 786440 | tf_op jit(solution)/shard_map/ppermute | solution.py:190
  33.2 14.7 %collective-permute-start.12 = (f16[2,32,2048]{2,1,0:T(8,128)(2,1)S(1)}, f16[2,32,2048]{2,1,0:T(8,128)(2,1)S(1)}, u32[]{:S(2)}, u32[]{:S(2)}) collective-permute-start(f16[2,32,2048]{2,1,0:T(8,128)(2,1)S(1)} %get-tuple-element.92), channel_id=1, source_target_pairs={{0,8},{1,9},{2,10},{3,11},{4,12},{5,13},{6,14},{7,15},{8,0},{9,1},... | collective-permute-start | bytes 786440 | tf_op jit(solution)/shard_map/ppermute | solution.py:190
  36.7 6.4 %collective-permute-start.9 = (f16[32,2048]{1,0:T(8,128)(2,1)S(1)}, f16[32,2048]{1,0:T(8,128)(2,1)S(1)}, u32[]{:S(2)}, u32[]{:S(2)}) collective-permute-start(f16[32,2048]{1,0:T(8,128)(2,1)S(1)} %multiply_convert_fusion.9), channel_id=1, source_target_pairs={{0,4},{1,5},{2,6},{3,7},{4,0},{5,1},{6,2},{7,3},{8,12},{9,13},{10,... | collective-permute-start | bytes 393224 | tf_op jit(solution)/shard_map/ppermute | solution.py:190
  38.8 5.0 %collective-permute-start.11 = (f16[32,2048]{1,0:T(8,128)(2,1)S(1)}, f16[32,2048]{1,0:T(8,128)(2,1)S(1)}, u32[]{:S(2)}, u32[]{:S(2)}) collective-permute-start(f16[32,2048]{1,0:T(8,128)(2,1)S(1)} %multiply_convert_fusion.8), channel_id=1, source_target_pairs={{0,2},{1,3},{2,0},{3,1},{4,6},{5,7},{6,4},{7,5},{8,10},{9,11},{10,... | collective-permute-start | bytes 393224 | tf_op jit(solution)/shard_map/ppermute | solution.py:190
  44.1 12.1 %collective-permute-start.17 = (f16[2,32,2048]{2,1,0:T(8,128)(2,1)S(1)}, f16[2,32,2048]{2,1,0:T(8,128)(2,1)S(1)}, u32[]{:S(2)}, u32[]{:S(2)}) collective-permute-start(f16[2,32,2048]{2,1,0:T(8,128)(2,1)S(1)} %multiply_convert_fusion.3), channel_id=1, source_target_pairs={{0,8},{1,9},{2,10},{3,11},{4,12},{5,13},{6,14},{7,15},{8,0},{9,1},... | collective-permute-start | bytes 786440 | tf_op jit(solution)/shard_map/ppermute | solution.py:190
  47.8 13.0 %collective-permute-start.14 = (bf16[160,2048]{1,0:T(8,128)(2,1)S(1)}, bf16[160,2048]{1,0:T(8,128)(2,1)S(1)}, u32[]{:S(2)}, u32[]{:S(2)}) collective-permute-start(bf16[160,2048]{1,0:T(8,128)(2,1)S(1)} %constant_dynamic-slice_fusion.3), channel_id=1, source_target_pairs={{0,2},{1,3},{2,0},{3,1},{4,6},{5,7},{6,4},{7,5},{8,10},{9,11},{10,... | collective-permute-start | bytes 1966088 | tf_op jit(solution)/shard_map/ppermute | solution.py:190
  48.0 11.0 %collective-permute-start.13 = (bf16[2,32,2048]{2,1,0:T(8,128)(2,1)S(1)}, bf16[2,32,2048]{2,1,0:T(8,128)(2,1)S(1)}, u32[]{:S(2)}, u32[]{:S(2)}) collective-permute-start(bf16[2,32,2048]{2,1,0:T(8,128)(2,1)S(1)} %fusion.21), channel_id=1, source_target_pairs={{0,4},{1,5},{2,6},{3,7},{4,0},{5,1},{6,2},{7,3},{8,12},{9,13},{10,... | collective-permute-start | bytes 786440 | tf_op jit(solution)/shard_map/ppermute | solution.py:190
  52.4 9.3 %collective-permute-start.15 = (bf16[96,2048]{1,0:T(8,128)(2,1)S(1)}, bf16[96,2048]{1,0:T(8,128)(2,1)S(1)}, u32[]{:S(2)}, u32[]{:S(2)}) collective-permute-start(bf16[96,2048]{1,0:T(8,128)(2,1)S(1)} %collective-permute-done.7), channel_id=1, source_target_pairs={{0,1},{1,0},{2,3},{3,2},{4,5},{5,4},{6,7},{7,6},{8,9},{9,8},{10,11... | collective-permute-start | bytes 1179656 | tf_op jit(solution)/shard_map/ppermute | solution.py:190
  56.4 7.2 %collective-permute-start.18 = (bf16[2,32,2048]{2,1,0:T(8,128)(2,1)S(1)}, bf16[2,32,2048]{2,1,0:T(8,128)(2,1)S(1)}, u32[]{:S(2)}, u32[]{:S(2)}) collective-permute-start(bf16[2,32,2048]{2,1,0:T(8,128)(2,1)S(1)} %fusion.24), channel_id=1, source_target_pairs={{0,4},{1,5},{2,6},{3,7},{4,0},{5,1},{6,2},{7,3},{8,12},{9,13},{10,... | collective-permute-start | bytes 786440 | tf_op jit(solution)/shard_map/ppermute | solution.py:190
  60.7 2.1 %collective-permute-start.16 = (bf16[160,2048]{1,0:T(8,128)(2,1)S(1)}, bf16[160,2048]{1,0:T(8,128)(2,1)S(1)}, u32[]{:S(2)}, u32[]{:S(2)}) collective-permute-start(bf16[160,2048]{1,0:T(8,128)(2,1)S(1)} %collective-permute-done.14), channel_id=1, source_target_pairs={{0,1},{1,0},{2,3},{3,2},{4,5},{5,4},{6,7},{7,6},{8,9},{9,8},{10,11... | collective-permute-start | bytes 1966088 | tf_op jit(solution)/shard_map/ppermute | solution.py:190
  64.4 0.8 copy-start.1
  65.2 7.1 %copy-start.2 = (s32[8,12]{1,0:T(8,128)S(1)}, s32[8,12]{1,0:T(8,128)}, u32[]{:S(2)}) copy-start(s32[8,12]{1,0:T(8,128)} %param.11) | copy-start | bytes 1156
  65.2 7.8 %copy-start.3 = (s32[8]{0:T(128)S(1)}, s32[8]{0:T(128)}, u32[]{:S(2)}) copy-start(s32[8]{0:T(128)} %param.12) | copy-start | bytes 100
  65.2 7.9 %copy-start.4 = (s32[512]{0:T(512)S(1)}, s32[512]{0:T(512)}, u32[]{:S(2)}) copy-start(s32[512]{0:T(512)} %param.10) | copy-start | bytes 6148
  67.0 19.8 %all-to-all-start = ((bf16[16,1,64,256]{3,2,1,0:T(8,128)(2,1)}), bf16[16,1,64,256]{3,2,1,0:T(8,128)(2,1)S(1)}, u32[]{:S(2)}, u32[]{:S(2)}) async-start(bf16[16,1,64,256]{3,2,1,0:T(8,128)(2,1)} %bitcast.10), calls=%async_computation | async-start | bytes 1048576 | tf_op jit(solution)/shard_map/all_to_all | solution.py:315

commit v23 on v18

--- a/solution.py
+++ b/solution.py
@@ -54,13 +54,20 @@
     for i in range(steps):
         load(i).start()
     left = rows_of(core_ref, rows_ref)
+
+    def take(i):
+        columns = slice(i * block, (i + 1) * block)
+        multiply(left, high_ref[:, columns], low_ref[:, columns], outs, columns)
+
     for i in range(steps):
         load(i).wait()
         columns = slice(i * block, (i + 1) * block)
         high, low = split(columns_ref[i])
         high_ref[:, columns] = high
         low_ref[:, columns] = low
-        multiply(left, high, low, outs, columns)
+        if i:
+            take(i - 1)
+    take(steps - 1)
 
 
 def mine_kernel(core_ref, rows_ref, high_ref, low_ref, *outs):

time: 85.4 us -> 86.1 us (level)
  transfers between devices with their start and end apart: 20 -> 20, of which waited for: 12 -> 12; matrix products, arithmetic and copies ran while one was open for 10% -> 10% of each run, Pallas kernels for 7% -> 8%
where the time goes in v23:
time: 86.1 us; the launch traced here: 85.8 us
  waiting for transfers between devices  36.5 us (42%)
  starting transfers between devices  27.4 us (32%)
  Pallas kernels  9.33 us (11%)
  other arithmetic  6.04 us (7%)
  matrix products  3.36 us (4%)
  local copies, waits for them, and re-layouts  2.78 us (3%)
    ppermute x19, waiting for transfers between devices, swap(): return lax.ppermute(value, 'rows', [(r, r ^ 1 << bit) for r in range(n)])  23.7 us
    ppermute x19, starting transfers between devices, swap(): return lax.ppermute(value, 'rows', [(r, r ^ 1 << bit) for r in range(n)])  22.2 us
    all_to_all x1, waiting for transfers between devices, shards(): lax.all_to_all(ordered, 'rows', split_axis=0, concat_axis=0, tiled=True)  12.7 us
    pallas_call x2, Pallas kernels, product(): pl.pallas_call(kernel, in_specs=[pl.BlockSpec(memory_space=pltpu.SMEM), i...  6.69 us
    all_to_all x1, starting transfers between devices, shards(): lax.all_to_all(ordered, 'rows', split_axis=0, concat_axis=0, tiled=True)  5.24 us
    dot_general x4, matrix products, scores(): lax.dot_general(group, value, (((1,), (1,)), ((), ())), preferred_element...  3.1 us
    convert_element_type x12, other arithmetic, pack(): return (value * lax.rsqrt(jnp.abs(value) + LEAST)).astype(jnp.float16)  2.39 us
    pallas_call x1, Pallas kernels, in_slot_order(): pl.pallas_call(order_kernel, in_specs=[pl.BlockSpec(memory_space=pltpu.SM...  1.78 us
  transfers between devices with their start and end apart: 20, of which 12 were waited for; matrix products, arithmetic and copies ran while one was open for 10% of the time, Pallas kernels for 8%

profile of v23, /device:TPU:0, one launch (start us, length us, event | category | flops | bytes accessed | tf_op | source)
XLA Modules:
  0.0 85.8 jit_solution(11936810071949894316)
XLA Ops:
  0.0 1.3 %fusion.10 = (bf16[512,256]{1,0:T(8,128)(2,1)S(1)}, bf16[512,256]{1,0:T(8,128)(2,1)S(1)}) fusion(f32[512,256]{1,0:T(8,128)} %param.7), kind=kLoop, calls=%fused_computation.26 | loop fusion | flops 524288 | bytes 1048576 | tf_op jit(solution)/shard_map/convert_element_type | solution.py:275
  1.3 0.4 copy-done
  1.9 3.0 %collective-permute-start.7 = (bf16[96,2048]{1,0:T(8,128)(2,1)S(1)}, bf16[96,2048]{1,0:T(8,128)(2,1)S(1)}, u32[]{:S(2)}, u32[]{:S(2)}) collective-permute-start(bf16[96,2048]{1,0:T(8,128)(2,1)S(1)} %constant_dynamic-slice_fusion.2), channel_id=1, source_target_pairs={{0,2},{1,3},{2,0},{3,1},{4,6},{5,7},{6,4},{7,5},{8,10},{9,11},{10,... | collective-permute-start | bytes 1179656 | tf_op jit(solution)/shard_map/ppermute | solution.py:193
  5.0 4.9 %shard_map.73 = (f32[128,4096]{1,0:T(8,128)S(1)}, f32[128,4096]{1,0:T(8,128)S(1)}, bf16[256,4096]{1,0:T(8,128)(2,1)S(1)}, bf16[256,4096]{1,0:T(8,128)(2,1)S(1)}) custom-call(s32[1]{0:T(128)} %bitcast.1.core_ref, bf16[512,768]{1,0:T(8,128)(2,1)S(1)} %pad_maximum_fusion.3.rows_ref, f32[256,4096]{1,0:T(8,128)} %columns_hbm.1), custom_call_target="tpu_custom_call" | custom-call | flops 1610612736 | bytes 8388608 | tf_op jit(solution)/shard_map/pallas_call | solution.py:96
  9.9 0.4 multiply_convert_fusion.1
  10.4 1.8 %shard_map.74 = (f32[64,4096]{1,0:T(8,128)S(1)}, f32[64,4096]{1,0:T(8,128)S(1)}, f32[64,4096]{1,0:T(8,128)S(1)}, f32[64,4096]{1,0:T(8,128)S(1)}) custom-call(s32[1]{0:T(128)} %bitcast.2.core_ref, bf16[512,768]{1,0:T(8,128)(2,1)S(1)} %pad_maximum_fusion.3.rows_ref, bf16[256,4096]{1,0:T(8,128)(2,1)S(1)} %get-tuple-element.51.high_ref, ...), custom_call_target="tpu_custom_call" | custom-call | flops 1610612736 | bytes 8388608 | tf_op jit(solution)/shard_map/pallas_call | solution.py:96
  12.2 0.4 multiply_convert_fusion
  12.7 0.6 collective-permute-start.6
  13.2 0.4 fusion.3
  13.6 0.2 multiply_convert_fusion.7
  14.1 2.1 %collective-permute-start.4 = (f16[32,4096]{1,0:T(8,128)(2,1)S(1)}, f16[32,4096]{1,0:T(8,128)(2,1)S(1)}, u32[]{:S(2)}, u32[]{:S(2)}) collective-permute-start(f16[32,4096]{1,0:T(8,128)(2,1)S(1)} %multiply_convert_fusion.6), channel_id=1, source_target_pairs={{0,4},{1,5},{2,6},{3,7},{4,0},{5,1},{6,2},{7,3},{8,12},{9,13},{10,... | collective-permute-start | bytes 786440 | tf_op jit(solution)/shard_map/ppermute | solution.py:193
  16.2 0.4 fusion.9
  16.7 0.4 constant_dynamic-slice_fusion.1
  17.2 0.2 multiply_convert_fusion.5
  17.5 4.7 %collective-permute-done.2 = f16[64,2048]{1,0:T(8,128)(2,1)S(1)} collective-permute-done((f16[64,2048]{1,0:T(8,128)(2,1)S(1)}, f16[64,2048]{1,0:T(8,128)(2,1)S(1)}, u32[]{:S(2)}, u32[]{:S(2)}) %collective-permute-start.2) | collective-permute-done | bytes 262176 | tf_op jit(solution)/shard_map/ppermute | solution.py:193
  22.4 1.6 %collective-permute-start.3 = (f16[32,2048]{1,0:T(8,128)(2,1)S(1)}, f16[32,2048]{1,0:T(8,128)(2,1)S(1)}, u32[]{:S(2)}, u32[]{:S(2)}) collective-permute-start(f16[32,2048]{1,0:T(8,128)(2,1)S(1)} %multiply_convert_fusion.11), channel_id=1, source_target_pairs={{0,4},{1,5},{2,6},{3,7},{4,0},{5,1},{6,2},{7,3},{8,12},{9,13},{10,... | collective-permute-start | bytes 393224 | tf_op jit(solution)/shard_map/ppermute | solution.py:193
  24.4 0.6 collective-permute-start.5
  24.9 1.5 %collective-permute-start.8 = (f16[64,2048]{1,0:T(8,128)(2,1)S(1)}, f16[64,2048]{1,0:T(8,128)(2,1)S(1)}, u32[]{:S(2)}, u32[]{:S(2)}) collective-permute-start(f16[64,2048]{1,0:T(8,128)(2,1)S(1)} %multiply_convert_fusion.5), channel_id=1, source_target_pairs={{0,2},{1,3},{2,0},{3,1},{4,6},{5,7},{6,4},{7,5},{8,10},{9,11},{10,... | collective-permute-start | bytes 786440 | tf_op jit(solution)/shard_map/ppermute | solution.py:193
  26.5 0.4 collective-permute-start.10
  26.9 0.8 collective-permute-done.3
  27.8 3.0 %collective-permute-done.5 = f16[32,2048]{1,0:T(8,128)(2,1)S(1)} collective-permute-done((f16[32,2048]{1,0:T(8,128)(2,1)S(1)}, f16[32,2048]{1,0:T(8,128)(2,1)S(1)}, u32[]{:S(2)}, u32[]{:S(2)}) %collective-permute-start.5) | collective-permute-done | bytes 131104 | tf_op jit(solution)/shard_map/ppermute | solution.py:193
  31.2 2.6 %collective-permute-start.12 = (f16[2,32,2048]{2,1,0:T(8,128)(2,1)S(1)}, f16[2,32,2048]{2,1,0:T(8,128)(2,1)S(1)}, u32[]{:S(2)}, u32[]{:S(2)}) collective-permute-start(f16[2,32,2048]{2,1,0:T(8,128)(2,1)S(1)} %get-tuple-element.92), channel_id=1, source_target_pairs={{0,8},{1,9},{2,10},{3,11},{4,12},{5,13},{6,14},{7,15},{8,0},{9,1},... | collective-permute-start | bytes 786440 | tf_op jit(solution)/shard_map/ppermute | solution.py:193
  33.8 0.6 collective-permute-done.8
  34.4 0.2 fusion.16
  34.7 0.5 collective-permute-start.9
  35.2 1.3 %collective-permute-done.10 = f16[32,4096]{1,0:T(8,128)(2,1)S(1)} collective-permute-done((f16[32,4096]{1,0:T(8,128)(2,1)S(1)}, f16[32,4096]{1,0:T(8,128)(2,1)S(1)}, u32[]{:S(2)}, u32[]{:S(2)}) %collective-permute-start.10) | collective-permute-done | bytes 262176 | tf_op jit(solution)/shard_map/ppermute | solution.py:193
  36.8 0.4 collective-permute-start.11
  37.2 3.8 %collective-permute-done.9 = f16[32,2048]{1,0:T(8,128)(2,1)S(1)} collective-permute-done((f16[32,2048]{1,0:T(8,128)(2,1)S(1)}, f16[32,2048]{1,0:T(8,128)(2,1)S(1)}, u32[]{:S(2)}, u32[]{:S(2)}) %collective-permute-start.9) | collective-permute-done | bytes 131104 | tf_op jit(solution)/shard_map/ppermute | solution.py:193
  41.1 0.7 collective-permute-done.11
  42.1 3.2 %collective-permute-start.17 = (f16[2,32,2048]{2,1,0:T(8,128)(2,1)S(1)}, f16[2,32,2048]{2,1,0:T(8,128)(2,1)S(1)}, u32[]{:S(2)}, u32[]{:S(2)}) collective-permute-start(f16[2,32,2048]{2,1,0:T(8,128)(2,1)S(1)} %multiply_convert_fusion.3), channel_id=1, source_target_pairs={{0,8},{1,9},{2,10},{3,11},{4,12},{5,13},{6,14},{7,15},{8,0},{9,1},... | collective-permute-start | bytes 786440 | tf_op jit(solution)/shard_map/ppermute | solution.py:193
  45.3 0.3 constant_dynamic-slice_fusion.3
  45.8 4.4 %collective-permute-start.13 = (bf16[2,32,2048]{2,1,0:T(8,128)(2,1)S(1)}, bf16[2,32,2048]{2,1,0:T(8,128)(2,1)S(1)}, u32[]{:S(2)}, u32[]{:S(2)}) collective-permute-start(bf16[2,32,2048]{2,1,0:T(8,128)(2,1)S(1)} %fusion.21), channel_id=1, source_target_pairs={{0,4},{1,5},{2,6},{3,7},{4,0},{5,1},{6,2},{7,3},{8,12},{9,13},{10,... | collective-permute-start | bytes 786440 | tf_op jit(solution)/shard_map/ppermute | solution.py:193
  50.3 4.0 %collective-permute-done.17 = f16[2,32,2048]{2,1,0:T(8,128)(2,1)S(1)} collective-permute-done((f16[2,32,2048]{2,1,0:T(8,128)(2,1)S(1)}, f16[2,32,2048]{2,1,0:T(8,128)(2,1)S(1)}, u32[]{:S(2)}, u32[]{:S(2)}) %collective-permute-start.17) | collective-permute-done | bytes 262176 | tf_op jit(solution)/shard_map/ppermute | solution.py:193
  54.4 0.7 collective-permute-start.18
  55.1 1.8 %collective-permute-done.13 = bf16[2,32,2048]{2,1,0:T(8,128)(2,1)S(1)} collective-permute-done((bf16[2,32,2048]{2,1,0:T(8,128)(2,1)S(1)}, bf16[2,32,2048]{2,1,0:T(8,128)(2,1)S(1)}, u32[]{:S(2)}, u32[]{:S(2)}) %collective-permute-start.13) | collective-permute-done | bytes 262176 | tf_op jit(solution)/shard_map/ppermute | solution.py:193
  57.0 1.7 %collective-permute-done.14 = bf16[160,2048]{1,0:T(8,128)(2,1)S(1)} collective-permute-done((bf16[160,2048]{1,0:T(8,128)(2,1)S(1)}, bf16[160,2048]{1,0:T(8,128)(2,1)S(1)}, u32[]{:S(2)}, u32[]{:S(2)}) %collective-permute-start.14) | collective-permute-done | bytes 655392 | tf_op jit(solution)/shard_map/ppermute | solution.py:193
  58.7 0.7 fusion.1.refs_0_
  59.5 1.3 %collective-permute-done.16 = bf16[160,2048]{1,0:T(8,128)(2,1)S(1)} collective-permute-done((bf16[160,2048]{1,0:T(8,128)(2,1)S(1)}, bf16[160,2048]{1,0:T(8,128)(2,1)S(1)}, u32[]{:S(2)}, u32[]{:S(2)}) %collective-permute-start.16) | collective-permute-done | bytes 655392 | tf_op jit(solution)/shard_map/ppermute | solution.py:193
  60.9 0.9 %fusion.43.refs_1_ = f32[512,128]{1,0:T(8,128)S(1)} fusion(bf16[512,2048]{1,0:T(8,128)(2,1)S(1)} %constant_dynamic-update-slice_fusion, bf16[128,2048]{1,0:T(8,128)(2,1)S(1)} %bitcast.31), kind=kOutput, calls=%fused_computation.88 | convolution fusion | flops 268435456 | bytes 2883584 | tf_op jit(solution)/shard_map/dot_general | solution.py:264
  61.9 0.7 fusion.44.refs_3_
  62.6 0.7 fusion.refs_2_
  63.4 1.8 %shard_map.75 = bf16[16,64,256]{2,1,0:T(8,128)(2,1)} custom-call(s32[16]{0:T(128)S(1)} %copy-done.1, f32[512,128]{1,0:T(8,128)S(1)} %fusion.1.refs_0_, f32[512,128]{1,0:T(8,128)S(1)} %fusion.43.refs_1_, f32[512,128]{1,0:T(8,128)S(1)} %fusion.refs_2_, f32[512,128]{1,0:T(8,128)S(1)} %fusion.44.refs_3_), custom_call_target="tpu_custom_call" | custom-call | flops 65536 | bytes 1572864 | tf_op jit(solution)/shard_map/pallas_call | solution.py:141
  65.2 5.2 %all-to-all-start = ((bf16[16,1,64,256]{3,2,1,0:T(8,128)(2,1)}), bf16[16,1,64,256]{3,2,1,0:T(8,128)(2,1)S(1)}, u32[]{:S(2)}, u32[]{:S(2)}) async-start(bf16[16,1,64,256]{3,2,1,0:T(8,128)(2,1)} %bitcast.10), calls=%async_computation | async-start | bytes 1048576 | tf_op jit(solution)/shard_map/all_to_all | solution.py:318
  70.6 0.6 dynamic_slice.79
  71.3 0.3 fusion.36
  71.6 0.6 constant_dynamic-slice_fusion.allowed_ref
  72.2 12.7 %all-to-all-done = bf16[16,1,64,256]{3,2,1,0:T(8,128)(2,1)S(1)} async-done(((bf16[16,1,64,256]{3,2,1,0:T(8,128)(2,1)}), bf16[16,1,64,256]{3,2,1,0:T(8,128)(2,1)S(1)}, u32[]{:S(2)}, u32[]{:S(2)}) %all-to-all-start) | async-done | bytes 524320 | tf_op jit(solution)/shard_map/all_to_all | solution.py:318
  84.9 0.9 %shard_map.76 = f32[1024,128]{1,0:T(8,128)} custom-call(bf16[16,1,4,16,256]{4,3,2,1,0:T(8,128)(2,1)S(1)} %bitcast.27, f32[1,512]{1,0:T(1,128)S(1)} %constant_dynamic-slice_fusion.allowed_ref), custom_call_target="tpu_custom_call" | custom-call | flops 262144 | bytes 1048576 | tf_op jit(solution)/shard_map/pallas_call | solution.py:171
  (51 shorter events, 3.3 us)
Async XLA Ops:
  0.0 1.7 %copy-start = (bf16[16,16,4096]{2,1,0:T(8,128)(2,1)S(1)}, bf16[16,16,4096]{2,1,0:T(8,128)(2,1)}, u32[]{:S(2)}) copy-start(bf16[16,16,4096]{2,1,0:T(8,128)(2,1)} %param.9) | copy-start | bytes 6291460
  1.9 23.0 %collective-permute-start.7 = (bf16[96,2048]{1,0:T(8,128)(2,1)S(1)}, bf16[96,2048]{1,0:T(8,128)(2,1)S(1)}, u32[]{:S(2)}, u32[]{:S(2)}) collective-permute-start(bf16[96,2048]{1,0:T(8,128)(2,1)S(1)} %constant_dynamic-slice_fusion.2), channel_id=1, source_target_pairs={{0,2},{1,3},{2,0},{3,1},{4,6},{5,7},{6,4},{7,5},{8,10},{9,11},{10,... | collective-permute-start | bytes 1179656 | tf_op jit(solution)/shard_map/ppermute | solution.py:193
  10.3 2.9 %collective-permute-start = (f16[128,4096]{1,0:T(8,128)(2,1)S(1)}, f16[128,4096]{1,0:T(8,128)(2,1)S(1)}, u32[]{:S(2)}, u32[]{:S(2)}) collective-permute-start(f16[128,4096]{1,0:T(8,128)(2,1)S(1)} %multiply_convert_fusion.1), channel_id=1, source_target_pairs={{0,1},{1,0},{2,3},{3,2},{4,5},{5,4},{6,7},{7,6},{8,9},{9,8},{10,11... | collective-permute-start | bytes 3145736 | tf_op jit(solution)/shard_map/ppermute | solution.py:193
  12.7 3.5 %collective-permute-start.6 = (f16[128,4096]{1,0:T(8,128)(2,1)S(1)}, f16[128,4096]{1,0:T(8,128)(2,1)S(1)}, u32[]{:S(2)}, u32[]{:S(2)}) collective-permute-start(f16[128,4096]{1,0:T(8,128)(2,1)S(1)} %multiply_convert_fusion), channel_id=1, source_target_pairs={{0,1},{1,0},{2,3},{3,2},{4,5},{5,4},{6,7},{7,6},{8,9},{9,8},{10,11... | collective-permute-start | bytes 3145736 | tf_op jit(solution)/shard_map/ppermute | solution.py:193
  13.8 8.3 %collective-permute-start.2 = (f16[64,2048]{1,0:T(8,128)(2,1)S(1)}, f16[64,2048]{1,0:T(8,128)(2,1)S(1)}, u32[]{:S(2)}, u32[]{:S(2)}) collective-permute-start(f16[64,2048]{1,0:T(8,128)(2,1)S(1)} %multiply_convert_fusion.7), channel_id=1, source_target_pairs={{0,2},{1,3},{2,0},{3,1},{4,6},{5,7},{6,4},{7,5},{8,10},{9,11},{10,... | collective-permute-start | bytes 786440 | tf_op jit(solution)/shard_map/ppermute | solution.py:193
  14.1 10.0 %collective-permute-start.4 = (f16[32,4096]{1,0:T(8,128)(2,1)S(1)}, f16[32,4096]{1,0:T(8,128)(2,1)S(1)}, u32[]{:S(2)}, u32[]{:S(2)}) collective-permute-start(f16[32,4096]{1,0:T(8,128)(2,1)S(1)} %multiply_convert_fusion.6), channel_id=1, source_target_pairs={{0,4},{1,5},{2,6},{3,7},{4,0},{5,1},{6,2},{7,3},{8,12},{9,13},{10,... | collective-permute-start | bytes 786440 | tf_op jit(solution)/shard_map/ppermute | solution.py:193
  17.2 41.6 %collective-permute-start.1 = (bf16[256,2048]{1,0:T(8,128)(2,1)S(1)}, bf16[256,2048]{1,0:T(8,128)(2,1)S(1)}, u32[]{:S(2)}, u32[]{:S(2)}) collective-permute-start(bf16[256,2048]{1,0:T(8,128)(2,1)S(1)} %constant_dynamic-slice_fusion.1), channel_id=1, source_target_pairs={{0,1},{1,0},{2,3},{3,2},{4,5},{5,4},{6,7},{7,6},{8,9},{9,8},{10,11... | collective-permute-start | bytes 3145736 | tf_op jit(solution)/shard_map/ppermute | solution.py:193
  22.4 5.3 %collective-permute-start.3 = (f16[32,2048]{1,0:T(8,128)(2,1)S(1)}, f16[32,2048]{1,0:T(8,128)(2,1)S(1)}, u32[]{:S(2)}, u32[]{:S(2)}) collective-permute-start(f16[32,2048]{1,0:T(8,128)(2,1)S(1)} %multiply_convert_fusion.11), channel_id=1, source_target_pairs={{0,4},{1,5},{2,6},{3,7},{4,0},{5,1},{6,2},{7,3},{8,12},{9,13},{10,... | collective-permute-start | bytes 393224 | tf_op jit(solution)/shard_map/ppermute | solution.py:193
  24.4 6.5 %collective-permute-start.5 = (f16[32,2048]{1,0:T(8,128)(2,1)S(1)}, f16[32,2048]{1,0:T(8,128)(2,1)S(1)}, u32[]{:S(2)}, u32[]{:S(2)}) collective-permute-start(f16[32,2048]{1,0:T(8,128)(2,1)S(1)} %multiply_convert_fusion.10), channel_id=1, source_target_pairs={{0,2},{1,3},{2,0},{3,1},{4,6},{5,7},{6,4},{7,5},{8,10},{9,11},{10,... | collective-permute-start | bytes 393224 | tf_op jit(solution)/shard_map/ppermute | solution.py:193
  24.9 9.4 %collective-permute-start.8 = (f16[64,2048]{1,0:T(8,128)(2,1)S(1)}, f16[64,2048]{1,0:T(8,128)(2,1)S(1)}, u32[]{:S(2)}, u32[]{:S(2)}) collective-permute-start(f16[64,2048]{1,0:T(8,128)(2,1)S(1)} %multiply_convert_fusion.5), channel_id=1, source_target_pairs={{0,2},{1,3},{2,0},{3,1},{4,6},{5,7},{6,4},{7,5},{8,10},{9,11},{10,... | collective-permute-start | bytes 786440 | tf_op jit(solution)/shard_map/ppermute | solution.py:193
  26.5 10.0 %collective-permute-start.10 = (f16[32,4096]{1,0:T(8,128)(2,1)S(1)}, f16[32,4096]{1,0:T(8,128)(2,1)S(1)}, u32[]{:S(2)}, u32[]{:S(2)}) collective-permute-start(f16[32,4096]{1,0:T(8,128)(2,1)S(1)} %multiply_convert_fusion.4), channel_id=1, source_target_pairs={{0,4},{1,5},{2,6},{3,7},{4,0},{5,1},{6,2},{7,3},{8,12},{9,13},{10,... | collective-permute-start | bytes 786440 | tf_op jit(solution)/shard_map/ppermute | solution.py:193
  31.2 14.5 %collective-permute-start.12 = (f16[2,32,2048]{2,1,0:T(8,128)(2,1)S(1)}, f16[2,32,2048]{2,1,0:T(8,128)(2,1)S(1)}, u32[]{:S(2)}, u32[]{:S(2)}) collective-permute-start(f16[2,32,2048]{2,1,0:T(8,128)(2,1)S(1)} %get-tuple-element.92), channel_id=1, source_target_pairs={{0,8},{1,9},{2,10},{3,11},{4,12},{5,13},{6,14},{7,15},{8,0},{9,1},... | collective-permute-start | bytes 786440 | tf_op jit(solution)/shard_map/ppermute | solution.py:193
  34.7 6.4 %collective-permute-start.9 = (f16[32,2048]{1,0:T(8,128)(2,1)S(1)}, f16[32,2048]{1,0:T(8,128)(2,1)S(1)}, u32[]{:S(2)}, u32[]{:S(2)}) collective-permute-start(f16[32,2048]{1,0:T(8,128)(2,1)S(1)} %multiply_convert_fusion.9), channel_id=1, source_target_pairs={{0,4},{1,5},{2,6},{3,7},{4,0},{5,1},{6,2},{7,3},{8,12},{9,13},{10,... | collective-permute-start | bytes 393224 | tf_op jit(solution)/shard_map/ppermute | solution.py:193
  36.8 5.0 %collective-permute-start.11 = (f16[32,2048]{1,0:T(8,128)(2,1)S(1)}, f16[32,2048]{1,0:T(8,128)(2,1)S(1)}, u32[]{:S(2)}, u32[]{:S(2)}) collective-permute-start(f16[32,2048]{1,0:T(8,128)(2,1)S(1)} %multiply_convert_fusion.8), channel_id=1, source_target_pairs={{0,2},{1,3},{2,0},{3,1},{4,6},{5,7},{6,4},{7,5},{8,10},{9,11},{10,... | collective-permute-start | bytes 393224 | tf_op jit(solution)/shard_map/ppermute | solution.py:193
  42.1 12.2 %collective-permute-start.17 = (f16[2,32,2048]{2,1,0:T(8,128)(2,1)S(1)}, f16[2,32,2048]{2,1,0:T(8,128)(2,1)S(1)}, u32[]{:S(2)}, u32[]{:S(2)}) collective-permute-start(f16[2,32,2048]{2,1,0:T(8,128)(2,1)S(1)} %multiply_convert_fusion.3), channel_id=1, source_target_pairs={{0,8},{1,9},{2,10},{3,11},{4,12},{5,13},{6,14},{7,15},{8,0},{9,1},... | collective-permute-start | bytes 786440 | tf_op jit(solution)/shard_map/ppermute | solution.py:193
  45.6 13.1 %collective-permute-start.14 = (bf16[160,2048]{1,0:T(8,128)(2,1)S(1)}, bf16[160,2048]{1,0:T(8,128)(2,1)S(1)}, u32[]{:S(2)}, u32[]{:S(2)}) collective-permute-start(bf16[160,2048]{1,0:T(8,128)(2,1)S(1)} %constant_dynamic-slice_fusion.3), channel_id=1, source_target_pairs={{0,2},{1,3},{2,0},{3,1},{4,6},{5,7},{6,4},{7,5},{8,10},{9,11},{10,... | collective-permute-start | bytes 1966088 | tf_op jit(solution)/shard_map/ppermute | solution.py:193
  45.8 11.1 %collective-permute-start.13 = (bf16[2,32,2048]{2,1,0:T(8,128)(2,1)S(1)}, bf16[2,32,2048]{2,1,0:T(8,128)(2,1)S(1)}, u32[]{:S(2)}, u32[]{:S(2)}) collective-permute-start(bf16[2,32,2048]{2,1,0:T(8,128)(2,1)S(1)} %fusion.21), channel_id=1, source_target_pairs={{0,4},{1,5},{2,6},{3,7},{4,0},{5,1},{6,2},{7,3},{8,12},{9,13},{10,... | collective-permute-start | bytes 786440 | tf_op jit(solution)/shard_map/ppermute | solution.py:193
  50.2 9.3 %collective-permute-start.15 = (bf16[96,2048]{1,0:T(8,128)(2,1)S(1)}, bf16[96,2048]{1,0:T(8,128)(2,1)S(1)}, u32[]{:S(2)}, u32[]{:S(2)}) collective-permute-start(bf16[96,2048]{1,0:T(8,128)(2,1)S(1)} %collective-permute-done.7), channel_id=1, source_target_pairs={{0,1},{1,0},{2,3},{3,2},{4,5},{5,4},{6,7},{7,6},{8,9},{9,8},{10,11... | collective-permute-start | bytes 1179656 | tf_op jit(solution)/shard_map/ppermute | solution.py:193
  54.4 7.4 %collective-permute-start.18 = (bf16[2,32,2048]{2,1,0:T(8,128)(2,1)S(1)}, bf16[2,32,2048]{2,1,0:T(8,128)(2,1)S(1)}, u32[]{:S(2)}, u32[]{:S(2)}) collective-permute-start(bf16[2,32,2048]{2,1,0:T(8,128)(2,1)S(1)} %fusion.24), channel_id=1, source_target_pairs={{0,4},{1,5},{2,6},{3,7},{4,0},{5,1},{6,2},{7,3},{8,12},{9,13},{10,... | collective-permute-start | bytes 786440 | tf_op jit(solution)/shard_map/ppermute | solution.py:193
  58.7 2.1 %collective-permute-start.16 = (bf16[160,2048]{1,0:T(8,128)(2,1)S(1)}, bf16[160,2048]{1,0:T(8,128)(2,1)S(1)}, u32[]{:S(2)}, u32[]{:S(2)}) collective-permute-start(bf16[160,2048]{1,0:T(8,128)(2,1)S(1)} %collective-permute-done.14), channel_id=1, source_target_pairs={{0,1},{1,0},{2,3},{3,2},{4,5},{5,4},{6,7},{7,6},{8,9},{9,8},{10,11... | collective-permute-start | bytes 1966088 | tf_op jit(solution)/shard_map/ppermute | solution.py:193
  62.6 0.8 copy-start.1
  63.4 7.1 %copy-start.2 = (s32[8,12]{1,0:T(8,128)S(1)}, s32[8,12]{1,0:T(8,128)}, u32[]{:S(2)}) copy-start(s32[8,12]{1,0:T(8,128)} %param.11) | copy-start | bytes 1156
  63.4 7.8 %copy-start.3 = (s32[8]{0:T(128)S(1)}, s32[8]{0:T(128)}, u32[]{:S(2)}) copy-start(s32[8]{0:T(128)} %param.12) | copy-start | bytes 100
  63.4 7.9 %copy-start.4 = (s32[512]{0:T(512)S(1)}, s32[512]{0:T(512)}, u32[]{:S(2)}) copy-start(s32[512]{0:T(512)} %param.10) | copy-start | bytes 6148
  65.2 19.7 %all-to-all-start = ((bf16[16,1,64,256]{3,2,1,0:T(8,128)(2,1)}), bf16[16,1,64,256]{3,2,1,0:T(8,128)(2,1)S(1)}, u32[]{:S(2)}, u32[]{:S(2)}) async-start(bf16[16,1,64,256]{3,2,1,0:T(8,128)(2,1)} %bitcast.10), calls=%async_computation | async-start | bytes 1048576 | tf_op jit(solution)/shard_map/all_to_all | solution.py:318

commit v24 on v18

--- a/solution.py
+++ b/solution.py
@@ -64,7 +64,11 @@
 
 
 def mine_kernel(core_ref, rows_ref, high_ref, low_ref, *outs):
-    left = rows_of(core_ref, rows_ref)
+    chunks = len(outs) // PATHS
+    half = rows_ref.shape[0] // CORES
+    count = half // CHUNKS * chunks
+    first = core_ref[0] * half + core_ref[1] * (half // CHUNKS)
+    left = rows_ref[pl.ds(pl.multiple_of(first, half // CHUNKS), count), :]
     width = high_ref.shape[1]
     block = min(512, width)
     for i in range(width // block):
@@ -76,7 +80,8 @@
     nrows = rows.shape[0]
     depth, width = columns[0].shape
     block = min(512, width)
-    out = [jax.ShapeDtypeStruct((nrows // CORES // pieces, width), jnp.float32)] * pieces
+    whole = CHUNKS if kernel is other_kernel else CHUNKS * PATHS
+    out = [jax.ShapeDtypeStruct((nrows // CORES // whole, width), jnp.float32)] * pieces
     in_vmem = pl.BlockSpec(memory_space=pltpu.VMEM)
     operand, scratch = in_vmem, []
     if kernel is other_kernel:
@@ -98,7 +103,7 @@
             bytes_accessed=4 * width * depth + 2 * width * nrows,
             transcendentals=0,
         ),
-    )(core.reshape(1), rows, *columns)
+    )(core, rows, *columns)
 
 
 def order_kernel(slots_ref, *refs):
@@ -195,9 +200,10 @@
         first_half[bit] = side == 0
     owned = nblocks // n
     first_slot = me * owned
-    scalars = (core, 1 - core, first_slot, offsets, first_half)
+    starts = [jnp.stack([core, jnp.int32(chunk)]) for chunk in range(CHUNKS)]
+    scalars = (starts, 1 - core, first_slot, offsets, first_half)
     scalars, queries, train = lax.optimization_barrier((scalars, queries, train))
-    core, other_core, first_slot, offsets, first_half = scalars
+    starts, other_core, first_slot, offsets, first_half = scalars
 
     def pack(value):
         value = value * UNIT
@@ -273,14 +279,15 @@
     other_core, blocks = after((other_core, blocks), early)
     early = swap(early, ybit)
 
-    *full, high, low = product(other_core, left, [precond], other_kernel, OTHER_VMEM, CHUNKS)
+    *full, high, low = product(other_core.reshape(1), left, [precond], other_kernel, OTHER_VMEM, CHUNKS)
     sent = pack(full[0])
     got = swap(sent, 0)
-    mine = product(after(core, sent), left, [high, low], mine_kernel, MINE_VMEM, CHUNKS * PATHS)
-    one = paths(mine[:PATHS], got)
+    mine = product(after(starts[0], sent), left, [high, low], mine_kernel, MINE_VMEM, PATHS)
+    one = paths(mine, got)
     sent = messages(one, 0)
     got = swap(pack(after(full[1], mine[0])), 0)
-    two = paths(mine[PATHS:], after(got, sent))
+    mine = product(after(starts[1], sent), left, [high, low], mine_kernel, MINE_VMEM, PATHS)
+    two = paths(mine, got)
     blocks = after(blocks, sent)
     near = features(blocks, 0, every, 0)
     sibling = swap(near, 0)

time: 85.4 us -> 84 us (0.984)
  starting transfers between devices: 27.3 us -> 25.1 us
  Pallas kernels: 8.69 us -> 9.98 us
    all_to_all x1, starting transfers between devices: 5.24 us -> 3.77 us  [shards(): lax.all_to_all(ordered, 'rows', split_axis=0, concat_axis=0, tiled=True)]
    pallas_call x2 -> x3, Pallas kernels: 6.05 us -> 7.33 us  [product(): pl.pallas_call(kernel, in_specs=[pl.BlockSpec(memory_space=pltpu.SMEM), i...]
  transfers between devices with their start and end apart: 20 -> 20, of which waited for: 12 -> 13; matrix products, arithmetic and copies ran while one was open for 10% -> 11% of each run, Pallas kernels for 7% -> 9%
where the time goes in v24:
time: 84 us; the launch traced here: 83.7 us
  waiting for transfers between devices  35.9 us (43%)
  starting transfers between devices  25.1 us (30%)
  Pallas kernels  9.98 us (12%)
  other arithmetic  6.14 us (7%)
  matrix products  3.31 us (4%)
  local copies, waits for them, and re-layouts  2.86 us (3%)
    ppermute x19, waiting for transfers between devices, swap(): return lax.ppermute(value, 'rows', [(r, r ^ 1 << bit) for r in range(n)])  23.3 us
    ppermute x19, starting transfers between devices, swap(): return lax.ppermute(value, 'rows', [(r, r ^ 1 << bit) for r in range(n)])  21.4 us
    all_to_all x1, waiting for transfers between devices, shards(): lax.all_to_all(ordered, 'rows', split_axis=0, concat_axis=0, tiled=True)  12.6 us
    pallas_call x3, Pallas kernels, product(): pl.pallas_call(kernel, in_specs=[pl.BlockSpec(memory_space=pltpu.SMEM), i...  7.33 us
    all_to_all x1, starting transfers between devices, shards(): lax.all_to_all(ordered, 'rows', split_axis=0, concat_axis=0, tiled=True)  3.77 us
    dot_general x4, matrix products, scores(): lax.dot_general(group, value, (((1,), (1,)), ((), ())), preferred_element...  3.04 us
    convert_element_type x12, other arithmetic, pack(): return (value * lax.rsqrt(jnp.abs(value) + LEAST)).astype(jnp.float16)  2.4 us
    pallas_call x1, Pallas kernels, in_slot_order(): pl.pallas_call(order_kernel, in_specs=[pl.BlockSpec(memory_space=pltpu.SM...  1.78 us
  transfers between devices with their start and end apart: 20, of which 13 were waited for; matrix products, arithmetic and copies ran while one was open for 11% of the time, Pallas kernels for 9%

profile of v24, /device:TPU:0, one launch (start us, length us, event | category | flops | bytes accessed | tf_op | source)
XLA Modules:
  0.0 83.7 jit_solution(6996152181979747062)
XLA Ops:
  0.1 1.2 %fusion.10 = (bf16[512,256]{1,0:T(8,128)(2,1)S(1)}, bf16[512,256]{1,0:T(8,128)(2,1)S(1)}) fusion(f32[512,256]{1,0:T(8,128)} %param.7), kind=kLoop, calls=%fused_computation.26 | loop fusion | flops 524288 | bytes 1048576 | tf_op jit(solution)/shard_map/convert_element_type | solution.py:274
  1.4 0.4 copy-done
  1.9 3.0 %collective-permute-start.7 = (bf16[96,2048]{1,0:T(8,128)(2,1)S(1)}, bf16[96,2048]{1,0:T(8,128)(2,1)S(1)}, u32[]{:S(2)}, u32[]{:S(2)}) collective-permute-start(bf16[96,2048]{1,0:T(8,128)(2,1)S(1)} %constant_dynamic-slice_fusion.2), channel_id=1, source_target_pairs={{0,2},{1,3},{2,0},{3,1},{4,6},{5,7},{6,4},{7,5},{8,10},{9,11},{10,... | collective-permute-start | bytes 1179656 | tf_op jit(solution)/shard_map/ppermute | solution.py:191
  5.0 4.2 %shard_map.73 = (f32[128,4096]{1,0:T(8,128)S(1)}, f32[128,4096]{1,0:T(8,128)S(1)}, bf16[256,4096]{1,0:T(8,128)(2,1)S(1)}, bf16[256,4096]{1,0:T(8,128)(2,1)S(1)}) custom-call(s32[1]{0:T(128)} %bitcast.2.core_ref, bf16[512,768]{1,0:T(8,128)(2,1)S(1)} %pad_maximum_fusion.3.rows_ref, f32[256,4096]{1,0:T(8,128)} %columns_hbm.1), custom_call_target="tpu_custom_call" | custom-call | flops 1610612736 | bytes 8388608 | tf_op jit(solution)/shard_map/pallas_call | solution.py:94
  9.2 0.4 multiply_convert_fusion.1
  9.7 1.5 %shard_map.74 = (f32[64,4096]{1,0:T(8,128)S(1)}, f32[64,4096]{1,0:T(8,128)S(1)}) custom-call(s32[2]{0:T(128)S(1)} %get-tuple-element.51.core_ref, bf16[512,768]{1,0:T(8,128)(2,1)S(1)} %pad_maximum_fusion.3.rows_ref, bf16[256,4096]{1,0:T(8,128)(2,1)S(1)} %get-tuple-element.52.high_ref, bf16[256,4096]{1,0:T(8,128)(2,1)S(1)} %get-tuple-element.53.low_ref), custom_call_target="tpu_custom_call" | custom-call | flops 1610612736 | bytes 8388608 | tf_op jit(solution)/shard_map/pallas_call | solution.py:94
  11.3 0.4 multiply_convert_fusion
  11.8 0.6 collective-permute-start.6
  12.4 0.4 fusion.3
  12.8 0.2 multiply_convert_fusion.7
  13.3 2.1 %collective-permute-start.4 = (f16[32,4096]{1,0:T(8,128)(2,1)S(1)}, f16[32,4096]{1,0:T(8,128)(2,1)S(1)}, u32[]{:S(2)}, u32[]{:S(2)}) collective-permute-start(f16[32,4096]{1,0:T(8,128)(2,1)S(1)} %multiply_convert_fusion.6), channel_id=1, source_target_pairs={{0,4},{1,5},{2,6},{3,7},{4,0},{5,1},{6,2},{7,3},{8,12},{9,13},{10,... | collective-permute-start | bytes 786440 | tf_op jit(solution)/shard_map/ppermute | solution.py:191
  15.4 1.5 %shard_map.75 = (f32[64,4096]{1,0:T(8,128)S(1)}, f32[64,4096]{1,0:T(8,128)S(1)}) custom-call(s32[2]{0:T(128)S(1)} %get-tuple-element.62.core_ref, bf16[512,768]{1,0:T(8,128)(2,1)S(1)} %pad_maximum_fusion.3.rows_ref, bf16[256,4096]{1,0:T(8,128)(2,1)S(1)} %get-tuple-element.52.high_ref, bf16[256,4096]{1,0:T(8,128)(2,1)S(1)} %get-tuple-element.53.low_ref), custom_call_target="tpu_custom_call" | custom-call | flops 1610612736 | bytes 8388608 | tf_op jit(solution)/shard_map/pallas_call | solution.py:94
  17.0 0.4 fusion.9
  17.5 0.4 constant_dynamic-slice_fusion.1
  18.2 3.2 %collective-permute-done.2 = f16[64,2048]{1,0:T(8,128)(2,1)S(1)} collective-permute-done((f16[64,2048]{1,0:T(8,128)(2,1)S(1)}, f16[64,2048]{1,0:T(8,128)(2,1)S(1)}, u32[]{:S(2)}, u32[]{:S(2)}) %collective-permute-start.2) | collective-permute-done | bytes 262176 | tf_op jit(solution)/shard_map/ppermute | solution.py:191
  21.8 1.6 %collective-permute-start.3 = (f16[32,2048]{1,0:T(8,128)(2,1)S(1)}, f16[32,2048]{1,0:T(8,128)(2,1)S(1)}, u32[]{:S(2)}, u32[]{:S(2)}) collective-permute-start(f16[32,2048]{1,0:T(8,128)(2,1)S(1)} %multiply_convert_fusion.11), channel_id=1, source_target_pairs={{0,4},{1,5},{2,6},{3,7},{4,0},{5,1},{6,2},{7,3},{8,12},{9,13},{10,... | collective-permute-start | bytes 393224 | tf_op jit(solution)/shard_map/ppermute | solution.py:191
  23.7 0.6 collective-permute-start.5
  24.3 1.5 %collective-permute-start.8 = (f16[64,2048]{1,0:T(8,128)(2,1)S(1)}, f16[64,2048]{1,0:T(8,128)(2,1)S(1)}, u32[]{:S(2)}, u32[]{:S(2)}) collective-permute-start(f16[64,2048]{1,0:T(8,128)(2,1)S(1)} %multiply_convert_fusion.5), channel_id=1, source_target_pairs={{0,2},{1,3},{2,0},{3,1},{4,6},{5,7},{6,4},{7,5},{8,10},{9,11},{10,... | collective-permute-start | bytes 786440 | tf_op jit(solution)/shard_map/ppermute | solution.py:191
  25.8 0.5 collective-permute-start.10
  26.3 0.8 collective-permute-done.3
  27.1 3.1 %collective-permute-done.5 = f16[32,2048]{1,0:T(8,128)(2,1)S(1)} collective-permute-done((f16[32,2048]{1,0:T(8,128)(2,1)S(1)}, f16[32,2048]{1,0:T(8,128)(2,1)S(1)}, u32[]{:S(2)}, u32[]{:S(2)}) %collective-permute-start.5) | collective-permute-done | bytes 131104 | tf_op jit(solution)/shard_map/ppermute | solution.py:191
  30.5 2.7 %collective-permute-start.12 = (f16[2,32,2048]{2,1,0:T(8,128)(2,1)S(1)}, f16[2,32,2048]{2,1,0:T(8,128)(2,1)S(1)}, u32[]{:S(2)}, u32[]{:S(2)}) collective-permute-start(f16[2,32,2048]{2,1,0:T(8,128)(2,1)S(1)} %get-tuple-element.94), channel_id=1, source_target_pairs={{0,8},{1,9},{2,10},{3,11},{4,12},{5,13},{6,14},{7,15},{8,0},{9,1},... | collective-permute-start | bytes 786440 | tf_op jit(solution)/shard_map/ppermute | solution.py:191
  33.1 0.7 collective-permute-done.8
  34.1 0.5 collective-permute-start.9
  34.7 0.9 %collective-permute-done.10 = f16[32,4096]{1,0:T(8,128)(2,1)S(1)} collective-permute-done((f16[32,4096]{1,0:T(8,128)(2,1)S(1)}, f16[32,4096]{1,0:T(8,128)(2,1)S(1)}, u32[]{:S(2)}, u32[]{:S(2)}) %collective-permute-start.10) | collective-permute-done | bytes 262176 | tf_op jit(solution)/shard_map/ppermute | solution.py:191
  35.9 0.8 collective-permute-start.11
  36.7 3.8 %collective-permute-done.9 = f16[32,2048]{1,0:T(8,128)(2,1)S(1)} collective-permute-done((f16[32,2048]{1,0:T(8,128)(2,1)S(1)}, f16[32,2048]{1,0:T(8,128)(2,1)S(1)}, u32[]{:S(2)}, u32[]{:S(2)}) %collective-permute-start.9) | collective-permute-done | bytes 131104 | tf_op jit(solution)/shard_map/ppermute | solution.py:191
  40.5 0.4 collective-permute-done.11
  41.2 2.8 %collective-permute-start.17 = (f16[2,32,2048]{2,1,0:T(8,128)(2,1)S(1)}, f16[2,32,2048]{2,1,0:T(8,128)(2,1)S(1)}, u32[]{:S(2)}, u32[]{:S(2)}) collective-permute-start(f16[2,32,2048]{2,1,0:T(8,128)(2,1)S(1)} %multiply_convert_fusion.3), channel_id=1, source_target_pairs={{0,8},{1,9},{2,10},{3,11},{4,12},{5,13},{6,14},{7,15},{8,0},{9,1},... | collective-permute-start | bytes 786440 | tf_op jit(solution)/shard_map/ppermute | solution.py:191
  44.0 0.3 constant_dynamic-slice_fusion.3
  44.3 0.5 collective-permute-start.14
  44.9 3.5 %collective-permute-start.13 = (bf16[2,32,2048]{2,1,0:T(8,128)(2,1)S(1)}, bf16[2,32,2048]{2,1,0:T(8,128)(2,1)S(1)}, u32[]{:S(2)}, u32[]{:S(2)}) collective-permute-start(bf16[2,32,2048]{2,1,0:T(8,128)(2,1)S(1)} %fusion.21), channel_id=1, source_target_pairs={{0,4},{1,5},{2,6},{3,7},{4,0},{5,1},{6,2},{7,3},{8,12},{9,13},{10,... | collective-permute-start | bytes 786440 | tf_op jit(solution)/shard_map/ppermute | solution.py:191
  48.4 5.3 %collective-permute-done.17 = f16[2,32,2048]{2,1,0:T(8,128)(2,1)S(1)} collective-permute-done((f16[2,32,2048]{2,1,0:T(8,128)(2,1)S(1)}, f16[2,32,2048]{2,1,0:T(8,128)(2,1)S(1)}, u32[]{:S(2)}, u32[]{:S(2)}) %collective-permute-start.17) | collective-permute-done | bytes 262176 | tf_op jit(solution)/shard_map/ppermute | solution.py:191
  53.8 0.5 collective-permute-start.18
  54.3 0.5 collective-permute-done.13
  54.9 3.3 %collective-permute-done.14 = bf16[160,2048]{1,0:T(8,128)(2,1)S(1)} collective-permute-done((bf16[160,2048]{1,0:T(8,128)(2,1)S(1)}, bf16[160,2048]{1,0:T(8,128)(2,1)S(1)}, u32[]{:S(2)}, u32[]{:S(2)}) %collective-permute-start.14) | collective-permute-done | bytes 655392 | tf_op jit(solution)/shard_map/ppermute | solution.py:191
  58.2 0.7 fusion.1.refs_0_
  59.0 1.3 %collective-permute-done.16 = bf16[160,2048]{1,0:T(8,128)(2,1)S(1)} collective-permute-done((bf16[160,2048]{1,0:T(8,128)(2,1)S(1)}, bf16[160,2048]{1,0:T(8,128)(2,1)S(1)}, u32[]{:S(2)}, u32[]{:S(2)}) %collective-permute-start.16) | collective-permute-done | bytes 655392 | tf_op jit(solution)/shard_map/ppermute | solution.py:191
  60.3 0.9 %fusion.43.refs_1_ = f32[512,128]{1,0:T(8,128)S(1)} fusion(bf16[512,2048]{1,0:T(8,128)(2,1)S(1)} %constant_dynamic-update-slice_fusion, bf16[128,2048]{1,0:T(8,128)(2,1)S(1)} %bitcast.31), kind=kOutput, calls=%fused_computation.90 | convolution fusion | flops 268435456 | bytes 2883584 | tf_op jit(solution)/shard_map/dot_general | solution.py:263
  61.4 0.7 fusion.44.refs_3_
  62.1 0.7 fusion.refs_2_
  62.9 1.8 %shard_map.76 = bf16[16,64,256]{2,1,0:T(8,128)(2,1)} custom-call(s32[16]{0:T(128)S(1)} %copy-done.1, f32[512,128]{1,0:T(8,128)S(1)} %fusion.1.refs_0_, f32[512,128]{1,0:T(8,128)S(1)} %fusion.43.refs_1_, f32[512,128]{1,0:T(8,128)S(1)} %fusion.refs_2_, f32[512,128]{1,0:T(8,128)S(1)} %fusion.44.refs_3_), custom_call_target="tpu_custom_call" | custom-call | flops 65536 | bytes 1572864 | tf_op jit(solution)/shard_map/pallas_call | solution.py:139
  64.6 3.8 %all-to-all-start = ((bf16[16,1,64,256]{3,2,1,0:T(8,128)(2,1)}), bf16[16,1,64,256]{3,2,1,0:T(8,128)(2,1)S(1)}, u32[]{:S(2)}, u32[]{:S(2)}) async-start(bf16[16,1,64,256]{3,2,1,0:T(8,128)(2,1)} %bitcast.10), calls=%async_computation | async-start | bytes 1048576 | tf_op jit(solution)/shard_map/all_to_all | solution.py:318
  68.5 0.7 dynamic_slice.79
  69.3 0.3 fusion.36
  69.6 0.7 constant_dynamic-slice_fusion.allowed_ref
  70.3 12.6 %all-to-all-done = bf16[16,1,64,256]{3,2,1,0:T(8,128)(2,1)S(1)} async-done(((bf16[16,1,64,256]{3,2,1,0:T(8,128)(2,1)}), bf16[16,1,64,256]{3,2,1,0:T(8,128)(2,1)S(1)}, u32[]{:S(2)}, u32[]{:S(2)}) %all-to-all-start) | async-done | bytes 524320 | tf_op jit(solution)/shard_map/all_to_all | solution.py:318
  82.9 0.9 %shard_map.77 = f32[1024,128]{1,0:T(8,128)} custom-call(bf16[16,1,4,16,256]{4,3,2,1,0:T(8,128)(2,1)S(1)} %bitcast.27, f32[1,512]{1,0:T(1,128)S(1)} %constant_dynamic-slice_fusion.allowed_ref), custom_call_target="tpu_custom_call" | custom-call | flops 262144 | bytes 1048576 | tf_op jit(solution)/shard_map/pallas_call | solution.py:169
  (53 shorter events, 3.8 us)
Async XLA Ops:
  0.0 1.7 %copy-start = (bf16[16,16,4096]{2,1,0:T(8,128)(2,1)S(1)}, bf16[16,16,4096]{2,1,0:T(8,128)(2,1)}, u32[]{:S(2)}) copy-start(bf16[16,16,4096]{2,1,0:T(8,128)(2,1)} %param.9) | copy-start | bytes 6291460
  1.9 22.4 %collective-permute-start.7 = (bf16[96,2048]{1,0:T(8,128)(2,1)S(1)}, bf16[96,2048]{1,0:T(8,128)(2,1)S(1)}, u32[]{:S(2)}, u32[]{:S(2)}) collective-permute-start(bf16[96,2048]{1,0:T(8,128)(2,1)S(1)} %constant_dynamic-slice_fusion.2), channel_id=1, source_target_pairs={{0,2},{1,3},{2,0},{3,1},{4,6},{5,7},{6,4},{7,5},{8,10},{9,11},{10,... | collective-permute-start | bytes 1179656 | tf_op jit(solution)/shard_map/ppermute | solution.py:191
  9.7 2.7 %collective-permute-start = (f16[128,4096]{1,0:T(8,128)(2,1)S(1)}, f16[128,4096]{1,0:T(8,128)(2,1)S(1)}, u32[]{:S(2)}, u32[]{:S(2)}) collective-permute-start(f16[128,4096]{1,0:T(8,128)(2,1)S(1)} %multiply_convert_fusion.1), channel_id=1, source_target_pairs={{0,1},{1,0},{2,3},{3,2},{4,5},{5,4},{6,7},{7,6},{8,9},{9,8},{10,11... | collective-permute-start | bytes 3145736 | tf_op jit(solution)/shard_map/ppermute | solution.py:191
  11.8 5.2 %collective-permute-start.6 = (f16[128,4096]{1,0:T(8,128)(2,1)S(1)}, f16[128,4096]{1,0:T(8,128)(2,1)S(1)}, u32[]{:S(2)}, u32[]{:S(2)}) collective-permute-start(f16[128,4096]{1,0:T(8,128)(2,1)S(1)} %multiply_convert_fusion), channel_id=1, source_target_pairs={{0,1},{1,0},{2,3},{3,2},{4,5},{5,4},{6,7},{7,6},{8,9},{9,8},{10,11... | collective-permute-start | bytes 3145736 | tf_op jit(solution)/shard_map/ppermute | solution.py:191
  13.0 8.4 %collective-permute-start.2 = (f16[64,2048]{1,0:T(8,128)(2,1)S(1)}, f16[64,2048]{1,0:T(8,128)(2,1)S(1)}, u32[]{:S(2)}, u32[]{:S(2)}) collective-permute-start(f16[64,2048]{1,0:T(8,128)(2,1)S(1)} %multiply_convert_fusion.7), channel_id=1, source_target_pairs={{0,2},{1,3},{2,0},{3,1},{4,6},{5,7},{6,4},{7,5},{8,10},{9,11},{10,... | collective-permute-start | bytes 786440 | tf_op jit(solution)/shard_map/ppermute | solution.py:191
  13.3 10.1 %collective-permute-start.4 = (f16[32,4096]{1,0:T(8,128)(2,1)S(1)}, f16[32,4096]{1,0:T(8,128)(2,1)S(1)}, u32[]{:S(2)}, u32[]{:S(2)}) collective-permute-start(f16[32,4096]{1,0:T(8,128)(2,1)S(1)} %multiply_convert_fusion.6), channel_id=1, source_target_pairs={{0,4},{1,5},{2,6},{3,7},{4,0},{5,1},{6,2},{7,3},{8,12},{9,13},{10,... | collective-permute-start | bytes 786440 | tf_op jit(solution)/shard_map/ppermute | solution.py:191
  17.9 40.2 %collective-permute-start.1 = (bf16[256,2048]{1,0:T(8,128)(2,1)S(1)}, bf16[256,2048]{1,0:T(8,128)(2,1)S(1)}, u32[]{:S(2)}, u32[]{:S(2)}) collective-permute-start(bf16[256,2048]{1,0:T(8,128)(2,1)S(1)} %constant_dynamic-slice_fusion.1), channel_id=1, source_target_pairs={{0,1},{1,0},{2,3},{3,2},{4,5},{5,4},{6,7},{7,6},{8,9},{9,8},{10,11... | collective-permute-start | bytes 3145736 | tf_op jit(solution)/shard_map/ppermute | solution.py:191
  21.8 5.2 %collective-permute-start.3 = (f16[32,2048]{1,0:T(8,128)(2,1)S(1)}, f16[32,2048]{1,0:T(8,128)(2,1)S(1)}, u32[]{:S(2)}, u32[]{:S(2)}) collective-permute-start(f16[32,2048]{1,0:T(8,128)(2,1)S(1)} %multiply_convert_fusion.11), channel_id=1, source_target_pairs={{0,4},{1,5},{2,6},{3,7},{4,0},{5,1},{6,2},{7,3},{8,12},{9,13},{10,... | collective-permute-start | bytes 393224 | tf_op jit(solution)/shard_map/ppermute | solution.py:191
  23.7 6.5 %collective-permute-start.5 = (f16[32,2048]{1,0:T(8,128)(2,1)S(1)}, f16[32,2048]{1,0:T(8,128)(2,1)S(1)}, u32[]{:S(2)}, u32[]{:S(2)}) collective-permute-start(f16[32,2048]{1,0:T(8,128)(2,1)S(1)} %multiply_convert_fusion.10), channel_id=1, source_target_pairs={{0,2},{1,3},{2,0},{3,1},{4,6},{5,7},{6,4},{7,5},{8,10},{9,11},{10,... | collective-permute-start | bytes 393224 | tf_op jit(solution)/shard_map/ppermute | solution.py:191
  24.3 9.5 %collective-permute-start.8 = (f16[64,2048]{1,0:T(8,128)(2,1)S(1)}, f16[64,2048]{1,0:T(8,128)(2,1)S(1)}, u32[]{:S(2)}, u32[]{:S(2)}) collective-permute-start(f16[64,2048]{1,0:T(8,128)(2,1)S(1)} %multiply_convert_fusion.5), channel_id=1, source_target_pairs={{0,2},{1,3},{2,0},{3,1},{4,6},{5,7},{6,4},{7,5},{8,10},{9,11},{10,... | collective-permute-start | bytes 786440 | tf_op jit(solution)/shard_map/ppermute | solution.py:191
  25.8 9.8 %collective-permute-start.10 = (f16[32,4096]{1,0:T(8,128)(2,1)S(1)}, f16[32,4096]{1,0:T(8,128)(2,1)S(1)}, u32[]{:S(2)}, u32[]{:S(2)}) collective-permute-start(f16[32,4096]{1,0:T(8,128)(2,1)S(1)} %multiply_convert_fusion.4), channel_id=1, source_target_pairs={{0,4},{1,5},{2,6},{3,7},{4,0},{5,1},{6,2},{7,3},{8,12},{9,13},{10,... | collective-permute-start | bytes 786440 | tf_op jit(solution)/shard_map/ppermute | solution.py:191
  30.5 14.3 %collective-permute-start.12 = (f16[2,32,2048]{2,1,0:T(8,128)(2,1)S(1)}, f16[2,32,2048]{2,1,0:T(8,128)(2,1)S(1)}, u32[]{:S(2)}, u32[]{:S(2)}) collective-permute-start(f16[2,32,2048]{2,1,0:T(8,128)(2,1)S(1)} %get-tuple-element.94), channel_id=1, source_target_pairs={{0,8},{1,9},{2,10},{3,11},{4,12},{5,13},{6,14},{7,15},{8,0},{9,1},... | collective-permute-start | bytes 786440 | tf_op jit(solution)/shard_map/ppermute | solution.py:191
  34.1 6.3 %collective-permute-start.9 = (f16[32,2048]{1,0:T(8,128)(2,1)S(1)}, f16[32,2048]{1,0:T(8,128)(2,1)S(1)}, u32[]{:S(2)}, u32[]{:S(2)}) collective-permute-start(f16[32,2048]{1,0:T(8,128)(2,1)S(1)} %multiply_convert_fusion.9), channel_id=1, source_target_pairs={{0,4},{1,5},{2,6},{3,7},{4,0},{5,1},{6,2},{7,3},{8,12},{9,13},{10,... | collective-permute-start | bytes 393224 | tf_op jit(solution)/shard_map/ppermute | solution.py:191
  35.9 5.0 %collective-permute-start.11 = (f16[32,2048]{1,0:T(8,128)(2,1)S(1)}, f16[32,2048]{1,0:T(8,128)(2,1)S(1)}, u32[]{:S(2)}, u32[]{:S(2)}) collective-permute-start(f16[32,2048]{1,0:T(8,128)(2,1)S(1)} %multiply_convert_fusion.8), channel_id=1, source_target_pairs={{0,2},{1,3},{2,0},{3,1},{4,6},{5,7},{6,4},{7,5},{8,10},{9,11},{10,... | collective-permute-start | bytes 393224 | tf_op jit(solution)/shard_map/ppermute | solution.py:191
  41.2 12.5 %collective-permute-start.17 = (f16[2,32,2048]{2,1,0:T(8,128)(2,1)S(1)}, f16[2,32,2048]{2,1,0:T(8,128)(2,1)S(1)}, u32[]{:S(2)}, u32[]{:S(2)}) collective-permute-start(f16[2,32,2048]{2,1,0:T(8,128)(2,1)S(1)} %multiply_convert_fusion.3), channel_id=1, source_target_pairs={{0,8},{1,9},{2,10},{3,11},{4,12},{5,13},{6,14},{7,15},{8,0},{9,1},... | collective-permute-start | bytes 786440 | tf_op jit(solution)/shard_map/ppermute | solution.py:191
  44.3 13.9 %collective-permute-start.14 = (bf16[160,2048]{1,0:T(8,128)(2,1)S(1)}, bf16[160,2048]{1,0:T(8,128)(2,1)S(1)}, u32[]{:S(2)}, u32[]{:S(2)}) collective-permute-start(bf16[160,2048]{1,0:T(8,128)(2,1)S(1)} %constant_dynamic-slice_fusion.3), channel_id=1, source_target_pairs={{0,2},{1,3},{2,0},{3,1},{4,6},{5,7},{6,4},{7,5},{8,10},{9,11},{10,... | collective-permute-start | bytes 1966088 | tf_op jit(solution)/shard_map/ppermute | solution.py:191
  44.9 9.9 %collective-permute-start.13 = (bf16[2,32,2048]{2,1,0:T(8,128)(2,1)S(1)}, bf16[2,32,2048]{2,1,0:T(8,128)(2,1)S(1)}, u32[]{:S(2)}, u32[]{:S(2)}) collective-permute-start(bf16[2,32,2048]{2,1,0:T(8,128)(2,1)S(1)} %fusion.21), channel_id=1, source_target_pairs={{0,4},{1,5},{2,6},{3,7},{4,0},{5,1},{6,2},{7,3},{8,12},{9,13},{10,... | collective-permute-start | bytes 786440 | tf_op jit(solution)/shard_map/ppermute | solution.py:191
  48.3 10.6 %collective-permute-start.15 = (bf16[96,2048]{1,0:T(8,128)(2,1)S(1)}, bf16[96,2048]{1,0:T(8,128)(2,1)S(1)}, u32[]{:S(2)}, u32[]{:S(2)}) collective-permute-start(bf16[96,2048]{1,0:T(8,128)(2,1)S(1)} %collective-permute-done.7), channel_id=1, source_target_pairs={{0,1},{1,0},{2,3},{3,2},{4,5},{5,4},{6,7},{7,6},{8,9},{9,8},{10,11... | collective-permute-start | bytes 1179656 | tf_op jit(solution)/shard_map/ppermute | solution.py:191
  53.8 7.4 %collective-permute-start.18 = (bf16[2,32,2048]{2,1,0:T(8,128)(2,1)S(1)}, bf16[2,32,2048]{2,1,0:T(8,128)(2,1)S(1)}, u32[]{:S(2)}, u32[]{:S(2)}) collective-permute-start(bf16[2,32,2048]{2,1,0:T(8,128)(2,1)S(1)} %fusion.24), channel_id=1, source_target_pairs={{0,4},{1,5},{2,6},{3,7},{4,0},{5,1},{6,2},{7,3},{8,12},{9,13},{10,... | collective-permute-start | bytes 786440 | tf_op jit(solution)/shard_map/ppermute | solution.py:191
  58.2 2.1 %collective-permute-start.16 = (bf16[160,2048]{1,0:T(8,128)(2,1)S(1)}, bf16[160,2048]{1,0:T(8,128)(2,1)S(1)}, u32[]{:S(2)}, u32[]{:S(2)}) collective-permute-start(bf16[160,2048]{1,0:T(8,128)(2,1)S(1)} %collective-permute-done.14), channel_id=1, source_target_pairs={{0,1},{1,0},{2,3},{3,2},{4,5},{5,4},{6,7},{7,6},{8,9},{9,8},{10,11... | collective-permute-start | bytes 1966088 | tf_op jit(solution)/shard_map/ppermute | solution.py:191
  62.1 0.7 copy-start.1
  62.8 5.6 %copy-start.2 = (s32[8,12]{1,0:T(8,128)S(1)}, s32[8,12]{1,0:T(8,128)}, u32[]{:S(2)}) copy-start(s32[8,12]{1,0:T(8,128)} %param.11) | copy-start | bytes 1156
  62.8 6.3 %copy-start.3 = (s32[8]{0:T(128)S(1)}, s32[8]{0:T(128)}, u32[]{:S(2)}) copy-start(s32[8]{0:T(128)} %param.12) | copy-start | bytes 100
  62.8 6.4 %copy-start.4 = (s32[512]{0:T(512)S(1)}, s32[512]{0:T(512)}, u32[]{:S(2)}) copy-start(s32[512]{0:T(512)} %param.10) | copy-start | bytes 6148
  64.6 18.2 %all-to-all-start = ((bf16[16,1,64,256]{3,2,1,0:T(8,128)(2,1)}), bf16[16,1,64,256]{3,2,1,0:T(8,128)(2,1)S(1)}, u32[]{:S(2)}, u32[]{:S(2)}) async-start(bf16[16,1,64,256]{3,2,1,0:T(8,128)(2,1)} %bitcast.10), calls=%async_computation | async-start | bytes 1048576 | tf_op jit(solution)/shard_map/all_to_all | solution.py:318

commit v25 on v24

--- a/solution.py
+++ b/solution.py
@@ -264,7 +264,7 @@
 
     blocks = train.reshape(examples * nblocks, width)
     every = examples * nblocks
-    middle = max(1, examples * 3 // 8) * nblocks
+    middle = max(1, examples * 7 // 16) * nblocks
 
     def features(blocks, first, count, other):
         start = offsets[ybit, width // 2][other]

time: 84 us -> 85 us (1.012)
  starting transfers between devices: 25.1 us -> 27.9 us
  waiting for transfers between devices: 35.9 us -> 34.1 us
    ppermute x19, starting transfers between devices: 21.4 us -> 23.7 us  [swap(): return lax.ppermute(value, 'rows', [(r, r ^ 1 << bit) for r in range(n)])]
    ppermute x19, waiting for transfers between devices: 23.3 us -> 21.5 us  [swap(): return lax.ppermute(value, 'rows', [(r, r ^ 1 << bit) for r in range(n)])]
  transfers between devices with their start and end apart: 20 -> 20, of which waited for: 13 -> 13; matrix products, arithmetic and copies ran while one was open for 11% -> 10% of each run, Pallas kernels for 9% -> 9%
where the time goes in v25:
time: 85 us; the launch traced here: 84.7 us
  waiting for transfers between devices  34.1 us (40%)
  starting transfers between devices  27.9 us (33%)
  Pallas kernels  9.98 us (12%)
  other arithmetic  6.14 us (7%)
  matrix products  3.32 us (4%)
  local copies, waits for them, and re-layouts  2.84 us (3%)
    ppermute x19, starting transfers between devices, swap(): return lax.ppermute(value, 'rows', [(r, r ^ 1 << bit) for r in range(n)])  23.7 us
    ppermute x19, waiting for transfers between devices, swap(): return lax.ppermute(value, 'rows', [(r, r ^ 1 << bit) for r in range(n)])  21.5 us
    all_to_all x1, waiting for transfers between devices, shards(): lax.all_to_all(ordered, 'rows', split_axis=0, concat_axis=0, tiled=True)  12.6 us
    pallas_call x3, Pallas kernels, product(): pl.pallas_call(kernel, in_specs=[pl.BlockSpec(memory_space=pltpu.SMEM), i...  7.34 us
    all_to_all x1, starting transfers between devices, shards(): lax.all_to_all(ordered, 'rows', split_axis=0, concat_axis=0, tiled=True)  4.19 us
    dot_general x4, matrix products, scores(): lax.dot_general(group, value, (((1,), (1,)), ((), ())), preferred_element...  3.05 us
    convert_element_type x12, other arithmetic, pack(): return (value * lax.rsqrt(jnp.abs(value) + LEAST)).astype(jnp.float16)  2.4 us
    pallas_call x1, Pallas kernels, in_slot_order(): pl.pallas_call(order_kernel, in_specs=[pl.BlockSpec(memory_space=pltpu.SM...  1.78 us
  transfers between devices with their start and end apart: 20, of which 13 were waited for; matrix products, arithmetic and copies ran while one was open for 10% of the time, Pallas kernels for 9%

profile of v25, /device:TPU:0, one launch (start us, length us, event | category | flops | bytes accessed | tf_op | source)
XLA Modules:
  0.0 84.7 jit_solution(10769257925500791813)
XLA Ops:
  0.1 1.2 %fusion.10 = (bf16[512,256]{1,0:T(8,128)(2,1)S(1)}, bf16[512,256]{1,0:T(8,128)(2,1)S(1)}) fusion(f32[512,256]{1,0:T(8,128)} %param.7), kind=kLoop, calls=%fused_computation.26 | loop fusion | flops 524288 | bytes 1048576 | tf_op jit(solution)/shard_map/convert_element_type | solution.py:274
  1.4 0.4 copy-done
  1.9 3.0 %collective-permute-start.7 = (bf16[112,2048]{1,0:T(8,128)(2,1)S(1)}, bf16[112,2048]{1,0:T(8,128)(2,1)S(1)}, u32[]{:S(2)}, u32[]{:S(2)}) collective-permute-start(bf16[112,2048]{1,0:T(8,128)(2,1)S(1)} %constant_dynamic-slice_fusion.2), channel_id=1, source_target_pairs={{0,2},{1,3},{2,0},{3,1},{4,6},{5,7},{6,4},{7,5},{8,10},{9,11},{10,... | collective-permute-start | bytes 1376264 | tf_op jit(solution)/shard_map/ppermute | solution.py:191
  5.0 4.2 %shard_map.73 = (f32[128,4096]{1,0:T(8,128)S(1)}, f32[128,4096]{1,0:T(8,128)S(1)}, bf16[256,4096]{1,0:T(8,128)(2,1)S(1)}, bf16[256,4096]{1,0:T(8,128)(2,1)S(1)}) custom-call(s32[1]{0:T(128)} %bitcast.2.core_ref, bf16[512,768]{1,0:T(8,128)(2,1)S(1)} %pad_maximum_fusion.3.rows_ref, f32[256,4096]{1,0:T(8,128)} %columns_hbm.1), custom_call_target="tpu_custom_call" | custom-call | flops 1610612736 | bytes 8388608 | tf_op jit(solution)/shard_map/pallas_call | solution.py:94
  9.2 0.4 multiply_convert_fusion.1
  9.8 1.5 %shard_map.74 = (f32[64,4096]{1,0:T(8,128)S(1)}, f32[64,4096]{1,0:T(8,128)S(1)}) custom-call(s32[2]{0:T(128)S(1)} %get-tuple-element.51.core_ref, bf16[512,768]{1,0:T(8,128)(2,1)S(1)} %pad_maximum_fusion.3.rows_ref, bf16[256,4096]{1,0:T(8,128)(2,1)S(1)} %get-tuple-element.52.high_ref, bf16[256,4096]{1,0:T(8,128)(2,1)S(1)} %get-tuple-element.53.low_ref), custom_call_target="tpu_custom_call" | custom-call | flops 1610612736 | bytes 8388608 | tf_op jit(solution)/shard_map/pallas_call | solution.py:94
  11.3 0.4 multiply_convert_fusion
  11.8 0.6 collective-permute-start.6
  12.4 0.4 fusion.3
  12.8 0.2 multiply_convert_fusion.7
  13.3 2.1 %collective-permute-start.4 = (f16[32,4096]{1,0:T(8,128)(2,1)S(1)}, f16[32,4096]{1,0:T(8,128)(2,1)S(1)}, u32[]{:S(2)}, u32[]{:S(2)}) collective-permute-start(f16[32,4096]{1,0:T(8,128)(2,1)S(1)} %multiply_convert_fusion.6), channel_id=1, source_target_pairs={{0,4},{1,5},{2,6},{3,7},{4,0},{5,1},{6,2},{7,3},{8,12},{9,13},{10,... | collective-permute-start | bytes 786440 | tf_op jit(solution)/shard_map/ppermute | solution.py:191
  15.4 1.5 %shard_map.75 = (f32[64,4096]{1,0:T(8,128)S(1)}, f32[64,4096]{1,0:T(8,128)S(1)}) custom-call(s32[2]{0:T(128)S(1)} %get-tuple-element.62.core_ref, bf16[512,768]{1,0:T(8,128)(2,1)S(1)} %pad_maximum_fusion.3.rows_ref, bf16[256,4096]{1,0:T(8,128)(2,1)S(1)} %get-tuple-element.52.high_ref, bf16[256,4096]{1,0:T(8,128)(2,1)S(1)} %get-tuple-element.53.low_ref), custom_call_target="tpu_custom_call" | custom-call | flops 1610612736 | bytes 8388608 | tf_op jit(solution)/shard_map/pallas_call | solution.py:94
  17.0 0.4 fusion.9
  17.5 0.4 constant_dynamic-slice_fusion.1
  18.2 3.2 %collective-permute-done.2 = f16[64,2048]{1,0:T(8,128)(2,1)S(1)} collective-permute-done((f16[64,2048]{1,0:T(8,128)(2,1)S(1)}, f16[64,2048]{1,0:T(8,128)(2,1)S(1)}, u32[]{:S(2)}, u32[]{:S(2)}) %collective-permute-start.2) | collective-permute-done | bytes 262176 | tf_op jit(solution)/shard_map/ppermute | solution.py:191
  21.8 1.6 %collective-permute-start.3 = (f16[32,2048]{1,0:T(8,128)(2,1)S(1)}, f16[32,2048]{1,0:T(8,128)(2,1)S(1)}, u32[]{:S(2)}, u32[]{:S(2)}) collective-permute-start(f16[32,2048]{1,0:T(8,128)(2,1)S(1)} %multiply_convert_fusion.11), channel_id=1, source_target_pairs={{0,4},{1,5},{2,6},{3,7},{4,0},{5,1},{6,2},{7,3},{8,12},{9,13},{10,... | collective-permute-start | bytes 393224 | tf_op jit(solution)/shard_map/ppermute | solution.py:191
  23.7 1.5 %collective-permute-start.5 = (f16[32,2048]{1,0:T(8,128)(2,1)S(1)}, f16[32,2048]{1,0:T(8,128)(2,1)S(1)}, u32[]{:S(2)}, u32[]{:S(2)}) collective-permute-start(f16[32,2048]{1,0:T(8,128)(2,1)S(1)} %multiply_convert_fusion.10), channel_id=1, source_target_pairs={{0,2},{1,3},{2,0},{3,1},{4,6},{5,7},{6,4},{7,5},{8,10},{9,11},{10,... | collective-permute-start | bytes 393224 | tf_op jit(solution)/shard_map/ppermute | solution.py:191
  25.2 0.6 collective-permute-start.8
  25.8 0.5 collective-permute-start.10
  26.3 0.8 collective-permute-done.3
  27.1 3.1 %collective-permute-done.5 = f16[32,2048]{1,0:T(8,128)(2,1)S(1)} collective-permute-done((f16[32,2048]{1,0:T(8,128)(2,1)S(1)}, f16[32,2048]{1,0:T(8,128)(2,1)S(1)}, u32[]{:S(2)}, u32[]{:S(2)}) %collective-permute-start.5) | collective-permute-done | bytes 131104 | tf_op jit(solution)/shard_map/ppermute | solution.py:191
  30.5 2.7 %collective-permute-start.12 = (f16[2,32,2048]{2,1,0:T(8,128)(2,1)S(1)}, f16[2,32,2048]{2,1,0:T(8,128)(2,1)S(1)}, u32[]{:S(2)}, u32[]{:S(2)}) collective-permute-start(f16[2,32,2048]{2,1,0:T(8,128)(2,1)S(1)} %get-tuple-element.94), channel_id=1, source_target_pairs={{0,8},{1,9},{2,10},{3,11},{4,12},{5,13},{6,14},{7,15},{8,0},{9,1},... | collective-permute-start | bytes 786440 | tf_op jit(solution)/shard_map/ppermute | solution.py:191
  33.2 0.7 collective-permute-done.8
  34.1 0.5 collective-permute-start.9
  34.7 0.9 %collective-permute-done.10 = f16[32,4096]{1,0:T(8,128)(2,1)S(1)} collective-permute-done((f16[32,4096]{1,0:T(8,128)(2,1)S(1)}, f16[32,4096]{1,0:T(8,128)(2,1)S(1)}, u32[]{:S(2)}, u32[]{:S(2)}) %collective-permute-start.10) | collective-permute-done | bytes 262176 | tf_op jit(solution)/shard_map/ppermute | solution.py:191
  35.9 1.5 %collective-permute-start.11 = (f16[32,2048]{1,0:T(8,128)(2,1)S(1)}, f16[32,2048]{1,0:T(8,128)(2,1)S(1)}, u32[]{:S(2)}, u32[]{:S(2)}) collective-permute-start(f16[32,2048]{1,0:T(8,128)(2,1)S(1)} %multiply_convert_fusion.8), channel_id=1, source_target_pairs={{0,2},{1,3},{2,0},{3,1},{4,6},{5,7},{6,4},{7,5},{8,10},{9,11},{10,... | collective-permute-start | bytes 393224 | tf_op jit(solution)/shard_map/ppermute | solution.py:191
  37.4 3.1 %collective-permute-done.9 = f16[32,2048]{1,0:T(8,128)(2,1)S(1)} collective-permute-done((f16[32,2048]{1,0:T(8,128)(2,1)S(1)}, f16[32,2048]{1,0:T(8,128)(2,1)S(1)}, u32[]{:S(2)}, u32[]{:S(2)}) %collective-permute-start.9) | collective-permute-done | bytes 131104 | tf_op jit(solution)/shard_map/ppermute | solution.py:191
  40.5 0.4 collective-permute-done.11
  41.2 2.8 %collective-permute-start.17 = (f16[2,32,2048]{2,1,0:T(8,128)(2,1)S(1)}, f16[2,32,2048]{2,1,0:T(8,128)(2,1)S(1)}, u32[]{:S(2)}, u32[]{:S(2)}) collective-permute-start(f16[2,32,2048]{2,1,0:T(8,128)(2,1)S(1)} %multiply_convert_fusion.3), channel_id=1, source_target_pairs={{0,8},{1,9},{2,10},{3,11},{4,12},{5,13},{6,14},{7,15},{8,0},{9,1},... | collective-permute-start | bytes 786440 | tf_op jit(solution)/shard_map/ppermute | solution.py:191
  44.0 0.2 constant_dynamic-slice_fusion.3
  44.2 1.6 %collective-permute-start.14 = (bf16[144,2048]{1,0:T(8,128)(2,1)S(1)}, bf16[144,2048]{1,0:T(8,128)(2,1)S(1)}, u32[]{:S(2)}, u32[]{:S(2)}) collective-permute-start(bf16[144,2048]{1,0:T(8,128)(2,1)S(1)} %constant_dynamic-slice_fusion.3), channel_id=1, source_target_pairs={{0,2},{1,3},{2,0},{3,1},{4,6},{5,7},{6,4},{7,5},{8,10},{9,11},{10,... | collective-permute-start | bytes 1769480 | tf_op jit(solution)/shard_map/ppermute | solution.py:191
  45.9 4.0 %collective-permute-start.13 = (bf16[2,32,2048]{2,1,0:T(8,128)(2,1)S(1)}, bf16[2,32,2048]{2,1,0:T(8,128)(2,1)S(1)}, u32[]{:S(2)}, u32[]{:S(2)}) collective-permute-start(bf16[2,32,2048]{2,1,0:T(8,128)(2,1)S(1)} %fusion.21), channel_id=1, source_target_pairs={{0,4},{1,5},{2,6},{3,7},{4,0},{5,1},{6,2},{7,3},{8,12},{9,13},{10,... | collective-permute-start | bytes 786440 | tf_op jit(solution)/shard_map/ppermute | solution.py:191
  50.0 3.7 %collective-permute-done.17 = f16[2,32,2048]{2,1,0:T(8,128)(2,1)S(1)} collective-permute-done((f16[2,32,2048]{2,1,0:T(8,128)(2,1)S(1)}, f16[2,32,2048]{2,1,0:T(8,128)(2,1)S(1)}, u32[]{:S(2)}, u32[]{:S(2)}) %collective-permute-start.17) | collective-permute-done | bytes 262176 | tf_op jit(solution)/shard_map/ppermute | solution.py:191
  53.8 0.5 collective-permute-start.18
  54.3 2.4 %collective-permute-done.13 = bf16[2,32,2048]{2,1,0:T(8,128)(2,1)S(1)} collective-permute-done((bf16[2,32,2048]{2,1,0:T(8,128)(2,1)S(1)}, bf16[2,32,2048]{2,1,0:T(8,128)(2,1)S(1)}, u32[]{:S(2)}, u32[]{:S(2)}) %collective-permute-start.13) | collective-permute-done | bytes 262176 | tf_op jit(solution)/shard_map/ppermute | solution.py:191
  57.0 0.7 fusion.1.refs_0_
  57.8 1.2 %collective-permute-done.16 = bf16[144,2048]{1,0:T(8,128)(2,1)S(1)} collective-permute-done((bf16[144,2048]{1,0:T(8,128)(2,1)S(1)}, bf16[144,2048]{1,0:T(8,128)(2,1)S(1)}, u32[]{:S(2)}, u32[]{:S(2)}) %collective-permute-start.16) | collective-permute-done | bytes 589856 | tf_op jit(solution)/shard_map/ppermute | solution.py:191
  59.0 0.9 %fusion.43.refs_1_ = f32[512,128]{1,0:T(8,128)S(1)} fusion(bf16[512,2048]{1,0:T(8,128)(2,1)S(1)} %constant_dynamic-update-slice_fusion, bf16[128,2048]{1,0:T(8,128)(2,1)S(1)} %bitcast.31), kind=kOutput, calls=%fused_computation.90 | convolution fusion | flops 268435456 | bytes 2883584 | tf_op jit(solution)/shard_map/dot_general | solution.py:263
  59.9 1.9 %collective-permute-done.18 = bf16[2,32,2048]{2,1,0:T(8,128)(2,1)S(1)} collective-permute-done((bf16[2,32,2048]{2,1,0:T(8,128)(2,1)S(1)}, bf16[2,32,2048]{2,1,0:T(8,128)(2,1)S(1)}, u32[]{:S(2)}, u32[]{:S(2)}) %collective-permute-start.18) | collective-permute-done | bytes 262176 | tf_op jit(solution)/shard_map/ppermute | solution.py:191
  61.9 0.7 fusion.44.refs_3_
  62.6 0.7 fusion.refs_2_
  63.4 1.8 %shard_map.76 = bf16[16,64,256]{2,1,0:T(8,128)(2,1)} custom-call(s32[16]{0:T(128)S(1)} %copy-done.1, f32[512,128]{1,0:T(8,128)S(1)} %fusion.1.refs_0_, f32[512,128]{1,0:T(8,128)S(1)} %fusion.43.refs_1_, f32[512,128]{1,0:T(8,128)S(1)} %fusion.refs_2_, f32[512,128]{1,0:T(8,128)S(1)} %fusion.44.refs_3_), custom_call_target="tpu_custom_call" | custom-call | flops 65536 | bytes 1572864 | tf_op jit(solution)/shard_map/pallas_call | solution.py:139
  65.2 4.2 %all-to-all-start = ((bf16[16,1,64,256]{3,2,1,0:T(8,128)(2,1)}), bf16[16,1,64,256]{3,2,1,0:T(8,128)(2,1)S(1)}, u32[]{:S(2)}, u32[]{:S(2)}) async-start(bf16[16,1,64,256]{3,2,1,0:T(8,128)(2,1)} %bitcast.10), calls=%async_computation | async-start | bytes 1048576 | tf_op jit(solution)/shard_map/all_to_all | solution.py:318
  69.5 0.7 dynamic_slice.79
  70.3 0.3 fusion.36
  70.5 0.7 constant_dynamic-slice_fusion.allowed_ref
  71.2 12.6 %all-to-all-done = bf16[16,1,64,256]{3,2,1,0:T(8,128)(2,1)S(1)} async-done(((bf16[16,1,64,256]{3,2,1,0:T(8,128)(2,1)}), bf16[16,1,64,256]{3,2,1,0:T(8,128)(2,1)S(1)}, u32[]{:S(2)}, u32[]{:S(2)}) %all-to-all-start) | async-done | bytes 524320 | tf_op jit(solution)/shard_map/all_to_all | solution.py:318
  83.8 0.9 %shard_map.77 = f32[1024,128]{1,0:T(8,128)} custom-call(bf16[16,1,4,16,256]{4,3,2,1,0:T(8,128)(2,1)S(1)} %bitcast.27, f32[1,512]{1,0:T(1,128)S(1)} %constant_dynamic-slice_fusion.allowed_ref), custom_call_target="tpu_custom_call" | custom-call | flops 262144 | bytes 1048576 | tf_op jit(solution)/shard_map/pallas_call | solution.py:169
  (53 shorter events, 3.9 us)
Async XLA Ops:
  0.0 1.7 %copy-start = (bf16[16,16,4096]{2,1,0:T(8,128)(2,1)S(1)}, bf16[16,16,4096]{2,1,0:T(8,128)(2,1)}, u32[]{:S(2)}) copy-start(bf16[16,16,4096]{2,1,0:T(8,128)(2,1)} %param.9) | copy-start | bytes 6291460
  1.9 23.2 %collective-permute-start.7 = (bf16[112,2048]{1,0:T(8,128)(2,1)S(1)}, bf16[112,2048]{1,0:T(8,128)(2,1)S(1)}, u32[]{:S(2)}, u32[]{:S(2)}) collective-permute-start(bf16[112,2048]{1,0:T(8,128)(2,1)S(1)} %constant_dynamic-slice_fusion.2), channel_id=1, source_target_pairs={{0,2},{1,3},{2,0},{3,1},{4,6},{5,7},{6,4},{7,5},{8,10},{9,11},{10,... | collective-permute-start | bytes 1376264 | tf_op jit(solution)/shard_map/ppermute | solution.py:191
  9.7 2.7 %collective-permute-start = (f16[128,4096]{1,0:T(8,128)(2,1)S(1)}, f16[128,4096]{1,0:T(8,128)(2,1)S(1)}, u32[]{:S(2)}, u32[]{:S(2)}) collective-permute-start(f16[128,4096]{1,0:T(8,128)(2,1)S(1)} %multiply_convert_fusion.1), channel_id=1, source_target_pairs={{0,1},{1,0},{2,3},{3,2},{4,5},{5,4},{6,7},{7,6},{8,9},{9,8},{10,11... | collective-permute-start | bytes 3145736 | tf_op jit(solution)/shard_map/ppermute | solution.py:191
  11.8 5.2 %collective-permute-start.6 = (f16[128,4096]{1,0:T(8,128)(2,1)S(1)}, f16[128,4096]{1,0:T(8,128)(2,1)S(1)}, u32[]{:S(2)}, u32[]{:S(2)}) collective-permute-start(f16[128,4096]{1,0:T(8,128)(2,1)S(1)} %multiply_convert_fusion), channel_id=1, source_target_pairs={{0,1},{1,0},{2,3},{3,2},{4,5},{5,4},{6,7},{7,6},{8,9},{9,8},{10,11... | collective-permute-start | bytes 3145736 | tf_op jit(solution)/shard_map/ppermute | solution.py:191
  13.1 8.4 %collective-permute-start.2 = (f16[64,2048]{1,0:T(8,128)(2,1)S(1)}, f16[64,2048]{1,0:T(8,128)(2,1)S(1)}, u32[]{:S(2)}, u32[]{:S(2)}) collective-permute-start(f16[64,2048]{1,0:T(8,128)(2,1)S(1)} %multiply_convert_fusion.7), channel_id=1, source_target_pairs={{0,2},{1,3},{2,0},{3,1},{4,6},{5,7},{6,4},{7,5},{8,10},{9,11},{10,... | collective-permute-start | bytes 786440 | tf_op jit(solution)/shard_map/ppermute | solution.py:191
  13.3 10.1 %collective-permute-start.4 = (f16[32,4096]{1,0:T(8,128)(2,1)S(1)}, f16[32,4096]{1,0:T(8,128)(2,1)S(1)}, u32[]{:S(2)}, u32[]{:S(2)}) collective-permute-start(f16[32,4096]{1,0:T(8,128)(2,1)S(1)} %multiply_convert_fusion.6), channel_id=1, source_target_pairs={{0,4},{1,5},{2,6},{3,7},{4,0},{5,1},{6,2},{7,3},{8,12},{9,13},{10,... | collective-permute-start | bytes 786440 | tf_op jit(solution)/shard_map/ppermute | solution.py:191
  17.9 39.0 %collective-permute-start.1 = (bf16[256,2048]{1,0:T(8,128)(2,1)S(1)}, bf16[256,2048]{1,0:T(8,128)(2,1)S(1)}, u32[]{:S(2)}, u32[]{:S(2)}) collective-permute-start(bf16[256,2048]{1,0:T(8,128)(2,1)S(1)} %constant_dynamic-slice_fusion.1), channel_id=1, source_target_pairs={{0,1},{1,0},{2,3},{3,2},{4,5},{5,4},{6,7},{7,6},{8,9},{9,8},{10,11... | collective-permute-start | bytes 3145736 | tf_op jit(solution)/shard_map/ppermute | solution.py:191
  21.8 5.2 %collective-permute-start.3 = (f16[32,2048]{1,0:T(8,128)(2,1)S(1)}, f16[32,2048]{1,0:T(8,128)(2,1)S(1)}, u32[]{:S(2)}, u32[]{:S(2)}) collective-permute-start(f16[32,2048]{1,0:T(8,128)(2,1)S(1)} %multiply_convert_fusion.11), channel_id=1, source_target_pairs={{0,4},{1,5},{2,6},{3,7},{4,0},{5,1},{6,2},{7,3},{8,12},{9,13},{10,... | collective-permute-start | bytes 393224 | tf_op jit(solution)/shard_map/ppermute | solution.py:191
  23.7 6.5 %collective-permute-start.5 = (f16[32,2048]{1,0:T(8,128)(2,1)S(1)}, f16[32,2048]{1,0:T(8,128)(2,1)S(1)}, u32[]{:S(2)}, u32[]{:S(2)}) collective-permute-start(f16[32,2048]{1,0:T(8,128)(2,1)S(1)} %multiply_convert_fusion.10), channel_id=1, source_target_pairs={{0,2},{1,3},{2,0},{3,1},{4,6},{5,7},{6,4},{7,5},{8,10},{9,11},{10,... | collective-permute-start | bytes 393224 | tf_op jit(solution)/shard_map/ppermute | solution.py:191
  25.2 8.6 %collective-permute-start.8 = (f16[64,2048]{1,0:T(8,128)(2,1)S(1)}, f16[64,2048]{1,0:T(8,128)(2,1)S(1)}, u32[]{:S(2)}, u32[]{:S(2)}) collective-permute-start(f16[64,2048]{1,0:T(8,128)(2,1)S(1)} %multiply_convert_fusion.5), channel_id=1, source_target_pairs={{0,2},{1,3},{2,0},{3,1},{4,6},{5,7},{6,4},{7,5},{8,10},{9,11},{10,... | collective-permute-start | bytes 786440 | tf_op jit(solution)/shard_map/ppermute | solution.py:191
  25.8 9.8 %collective-permute-start.10 = (f16[32,4096]{1,0:T(8,128)(2,1)S(1)}, f16[32,4096]{1,0:T(8,128)(2,1)S(1)}, u32[]{:S(2)}, u32[]{:S(2)}) collective-permute-start(f16[32,4096]{1,0:T(8,128)(2,1)S(1)} %multiply_convert_fusion.4), channel_id=1, source_target_pairs={{0,4},{1,5},{2,6},{3,7},{4,0},{5,1},{6,2},{7,3},{8,12},{9,13},{10,... | collective-permute-start | bytes 786440 | tf_op jit(solution)/shard_map/ppermute | solution.py:191
  30.5 15.3 %collective-permute-start.12 = (f16[2,32,2048]{2,1,0:T(8,128)(2,1)S(1)}, f16[2,32,2048]{2,1,0:T(8,128)(2,1)S(1)}, u32[]{:S(2)}, u32[]{:S(2)}) collective-permute-start(f16[2,32,2048]{2,1,0:T(8,128)(2,1)S(1)} %get-tuple-element.94), channel_id=1, source_target_pairs={{0,8},{1,9},{2,10},{3,11},{4,12},{5,13},{6,14},{7,15},{8,0},{9,1},... | collective-permute-start | bytes 786440 | tf_op jit(solution)/shard_map/ppermute | solution.py:191
  34.1 6.3 %collective-permute-start.9 = (f16[32,2048]{1,0:T(8,128)(2,1)S(1)}, f16[32,2048]{1,0:T(8,128)(2,1)S(1)}, u32[]{:S(2)}, u32[]{:S(2)}) collective-permute-start(f16[32,2048]{1,0:T(8,128)(2,1)S(1)} %multiply_convert_fusion.9), channel_id=1, source_target_pairs={{0,4},{1,5},{2,6},{3,7},{4,0},{5,1},{6,2},{7,3},{8,12},{9,13},{10,... | collective-permute-start | bytes 393224 | tf_op jit(solution)/shard_map/ppermute | solution.py:191
  35.9 5.0 %collective-permute-start.11 = (f16[32,2048]{1,0:T(8,128)(2,1)S(1)}, f16[32,2048]{1,0:T(8,128)(2,1)S(1)}, u32[]{:S(2)}, u32[]{:S(2)}) collective-permute-start(f16[32,2048]{1,0:T(8,128)(2,1)S(1)} %multiply_convert_fusion.8), channel_id=1, source_target_pairs={{0,2},{1,3},{2,0},{3,1},{4,6},{5,7},{6,4},{7,5},{8,10},{9,11},{10,... | collective-permute-start | bytes 393224 | tf_op jit(solution)/shard_map/ppermute | solution.py:191
  41.2 12.5 %collective-permute-start.17 = (f16[2,32,2048]{2,1,0:T(8,128)(2,1)S(1)}, f16[2,32,2048]{2,1,0:T(8,128)(2,1)S(1)}, u32[]{:S(2)}, u32[]{:S(2)}) collective-permute-start(f16[2,32,2048]{2,1,0:T(8,128)(2,1)S(1)} %multiply_convert_fusion.3), channel_id=1, source_target_pairs={{0,8},{1,9},{2,10},{3,11},{4,12},{5,13},{6,14},{7,15},{8,0},{9,1},... | collective-permute-start | bytes 786440 | tf_op jit(solution)/shard_map/ppermute | solution.py:191
  44.2 12.6 %collective-permute-start.14 = (bf16[144,2048]{1,0:T(8,128)(2,1)S(1)}, bf16[144,2048]{1,0:T(8,128)(2,1)S(1)}, u32[]{:S(2)}, u32[]{:S(2)}) collective-permute-start(bf16[144,2048]{1,0:T(8,128)(2,1)S(1)} %constant_dynamic-slice_fusion.3), channel_id=1, source_target_pairs={{0,2},{1,3},{2,0},{3,1},{4,6},{5,7},{6,4},{7,5},{8,10},{9,11},{10,... | collective-permute-start | bytes 1769480 | tf_op jit(solution)/shard_map/ppermute | solution.py:191
  45.9 10.8 %collective-permute-start.13 = (bf16[2,32,2048]{2,1,0:T(8,128)(2,1)S(1)}, bf16[2,32,2048]{2,1,0:T(8,128)(2,1)S(1)}, u32[]{:S(2)}, u32[]{:S(2)}) collective-permute-start(bf16[2,32,2048]{2,1,0:T(8,128)(2,1)S(1)} %fusion.21), channel_id=1, source_target_pairs={{0,4},{1,5},{2,6},{3,7},{4,0},{5,1},{6,2},{7,3},{8,12},{9,13},{10,... | collective-permute-start | bytes 786440 | tf_op jit(solution)/shard_map/ppermute | solution.py:191
  49.9 7.8 %collective-permute-start.15 = (bf16[112,2048]{1,0:T(8,128)(2,1)S(1)}, bf16[112,2048]{1,0:T(8,128)(2,1)S(1)}, u32[]{:S(2)}, u32[]{:S(2)}) collective-permute-start(bf16[112,2048]{1,0:T(8,128)(2,1)S(1)} %collective-permute-done.7), channel_id=1, source_target_pairs={{0,1},{1,0},{2,3},{3,2},{4,5},{5,4},{6,7},{7,6},{8,9},{9,8},{10,11... | collective-permute-start | bytes 1376264 | tf_op jit(solution)/shard_map/ppermute | solution.py:191
  53.8 7.9 %collective-permute-start.18 = (bf16[2,32,2048]{2,1,0:T(8,128)(2,1)S(1)}, bf16[2,32,2048]{2,1,0:T(8,128)(2,1)S(1)}, u32[]{:S(2)}, u32[]{:S(2)}) collective-permute-start(bf16[2,32,2048]{2,1,0:T(8,128)(2,1)S(1)} %fusion.24), channel_id=1, source_target_pairs={{0,4},{1,5},{2,6},{3,7},{4,0},{5,1},{6,2},{7,3},{8,12},{9,13},{10,... | collective-permute-start | bytes 786440 | tf_op jit(solution)/shard_map/ppermute | solution.py:191
  56.9 2.1 %collective-permute-start.16 = (bf16[144,2048]{1,0:T(8,128)(2,1)S(1)}, bf16[144,2048]{1,0:T(8,128)(2,1)S(1)}, u32[]{:S(2)}, u32[]{:S(2)}) collective-permute-start(bf16[144,2048]{1,0:T(8,128)(2,1)S(1)} %collective-permute-done.14), channel_id=1, source_target_pairs={{0,1},{1,0},{2,3},{3,2},{4,5},{5,4},{6,7},{7,6},{8,9},{9,8},{10,11... | collective-permute-start | bytes 1769480 | tf_op jit(solution)/shard_map/ppermute | solution.py:191
  62.6 0.7 copy-start.1
  63.4 6.0 %copy-start.2 = (s32[8,12]{1,0:T(8,128)S(1)}, s32[8,12]{1,0:T(8,128)}, u32[]{:S(2)}) copy-start(s32[8,12]{1,0:T(8,128)} %param.11) | copy-start | bytes 1156
  63.4 6.8 %copy-start.3 = (s32[8]{0:T(128)S(1)}, s32[8]{0:T(128)}, u32[]{:S(2)}) copy-start(s32[8]{0:T(128)} %param.12) | copy-start | bytes 100
  63.4 6.9 %copy-start.4 = (s32[512]{0:T(512)S(1)}, s32[512]{0:T(512)}, u32[]{:S(2)}) copy-start(s32[512]{0:T(512)} %param.10) | copy-start | bytes 6148
  65.2 18.7 %all-to-all-start = ((bf16[16,1,64,256]{3,2,1,0:T(8,128)(2,1)}), bf16[16,1,64,256]{3,2,1,0:T(8,128)(2,1)S(1)}, u32[]{:S(2)}, u32[]{:S(2)}) async-start(bf16[16,1,64,256]{3,2,1,0:T(8,128)(2,1)} %bitcast.10), calls=%async_computation | async-start | bytes 1048576 | tf_op jit(solution)/shard_map/all_to_all | solution.py:318

commit v26 on v25

--- a/solution.py
+++ b/solution.py
@@ -264,7 +264,7 @@
 
     blocks = train.reshape(examples * nblocks, width)
     every = examples * nblocks
-    middle = max(1, examples * 7 // 16) * nblocks
+    middle = max(1, examples * 5 // 16) * nblocks
 
     def features(blocks, first, count, other):
         start = offsets[ybit, width // 2][other]

time: 85 us -> 85.3 us (level)
  waiting for transfers between devices: 34.1 us -> 37.3 us
  starting transfers between devices: 27.9 us -> 25 us
    ppermute x19, waiting for transfers between devices: 21.5 us -> 24.7 us  [swap(): return lax.ppermute(value, 'rows', [(r, r ^ 1 << bit) for r in range(n)])]
    ppermute x19, starting transfers between devices: 23.7 us -> 21.4 us  [swap(): return lax.ppermute(value, 'rows', [(r, r ^ 1 << bit) for r in range(n)])]
  transfers between devices with their start and end apart: 20 -> 20, of which waited for: 13 -> 12; matrix products, arithmetic and copies ran while one was open for 10% -> 10% of each run, Pallas kernels for 9% -> 9%
where the time goes in v26:
time: 85.3 us; the launch traced here: 85 us
  waiting for transfers between devices  37.3 us (44%)
  starting transfers between devices  25 us (29%)
  Pallas kernels  9.97 us (12%)
  other arithmetic  6.13 us (7%)
  matrix products  3.31 us (4%)
  local copies, waits for them, and re-layouts  2.88 us (3%)
    ppermute x19, waiting for transfers between devices, swap(): return lax.ppermute(value, 'rows', [(r, r ^ 1 << bit) for r in range(n)])  24.7 us
    ppermute x19, starting transfers between devices, swap(): return lax.ppermute(value, 'rows', [(r, r ^ 1 << bit) for r in range(n)])  21.4 us
    all_to_all x1, waiting for transfers between devices, shards(): lax.all_to_all(ordered, 'rows', split_axis=0, concat_axis=0, tiled=True)  12.6 us
    pallas_call x3, Pallas kernels, product(): pl.pallas_call(kernel, in_specs=[pl.BlockSpec(memory_space=pltpu.SMEM), i...  7.33 us
    all_to_all x1, starting transfers between devices, shards(): lax.all_to_all(ordered, 'rows', split_axis=0, concat_axis=0, tiled=True)  3.59 us
    dot_general x4, matrix products, scores(): lax.dot_general(group, value, (((1,), (1,)), ((), ())), preferred_element...  3.04 us
    convert_element_type x12, other arithmetic, pack(): return (value * lax.rsqrt(jnp.abs(value) + LEAST)).astype(jnp.float16)  2.39 us
    pallas_call x1, Pallas kernels, in_slot_order(): pl.pallas_call(order_kernel, in_specs=[pl.BlockSpec(memory_space=pltpu.SM...  1.78 us
  transfers between devices with their start and end apart: 20, of which 12 were waited for; matrix products, arithmetic and copies ran while one was open for 10% of the time, Pallas kernels for 9%

profile of v26, /device:TPU:0, one launch (start us, length us, event | category | flops | bytes accessed | tf_op | source)
XLA Modules:
  0.0 85.0 jit_solution(9630533547629198623)
XLA Ops:
  0.1 1.2 %fusion.10 = (bf16[512,256]{1,0:T(8,128)(2,1)S(1)}, bf16[512,256]{1,0:T(8,128)(2,1)S(1)}) fusion(f32[512,256]{1,0:T(8,128)} %param.7), kind=kLoop, calls=%fused_computation.26 | loop fusion | flops 524288 | bytes 1048576 | tf_op jit(solution)/shard_map/convert_element_type | solution.py:274
  1.4 0.4 copy-done
  1.9 3.0 %collective-permute-start.7 = (bf16[80,2048]{1,0:T(8,128)(2,1)S(1)}, bf16[80,2048]{1,0:T(8,128)(2,1)S(1)}, u32[]{:S(2)}, u32[]{:S(2)}) collective-permute-start(bf16[80,2048]{1,0:T(8,128)(2,1)S(1)} %constant_dynamic-slice_fusion.2), channel_id=1, source_target_pairs={{0,2},{1,3},{2,0},{3,1},{4,6},{5,7},{6,4},{7,5},{8,10},{9,11},{10,... | collective-permute-start | bytes 983048 | tf_op jit(solution)/shard_map/ppermute | solution.py:191
  4.9 4.2 %shard_map.73 = (f32[128,4096]{1,0:T(8,128)S(1)}, f32[128,4096]{1,0:T(8,128)S(1)}, bf16[256,4096]{1,0:T(8,128)(2,1)S(1)}, bf16[256,4096]{1,0:T(8,128)(2,1)S(1)}) custom-call(s32[1]{0:T(128)} %bitcast.2.core_ref, bf16[512,768]{1,0:T(8,128)(2,1)S(1)} %pad_maximum_fusion.3.rows_ref, f32[256,4096]{1,0:T(8,128)} %columns_hbm.1), custom_call_target="tpu_custom_call" | custom-call | flops 1610612736 | bytes 8388608 | tf_op jit(solution)/shard_map/pallas_call | solution.py:94
  9.2 0.4 multiply_convert_fusion.1
  9.7 1.5 %shard_map.74 = (f32[64,4096]{1,0:T(8,128)S(1)}, f32[64,4096]{1,0:T(8,128)S(1)}) custom-call(s32[2]{0:T(128)S(1)} %get-tuple-element.51.core_ref, bf16[512,768]{1,0:T(8,128)(2,1)S(1)} %pad_maximum_fusion.3.rows_ref, bf16[256,4096]{1,0:T(8,128)(2,1)S(1)} %get-tuple-element.52.high_ref, bf16[256,4096]{1,0:T(8,128)(2,1)S(1)} %get-tuple-element.53.low_ref), custom_call_target="tpu_custom_call" | custom-call | flops 1610612736 | bytes 8388608 | tf_op jit(solution)/shard_map/pallas_call | solution.py:94
  11.3 0.4 multiply_convert_fusion
  11.7 0.6 collective-permute-start.6
  12.4 0.4 fusion.3
  12.8 0.2 multiply_convert_fusion.7
  13.3 2.1 %collective-permute-start.4 = (f16[32,4096]{1,0:T(8,128)(2,1)S(1)}, f16[32,4096]{1,0:T(8,128)(2,1)S(1)}, u32[]{:S(2)}, u32[]{:S(2)}) collective-permute-start(f16[32,4096]{1,0:T(8,128)(2,1)S(1)} %multiply_convert_fusion.6), channel_id=1, source_target_pairs={{0,4},{1,5},{2,6},{3,7},{4,0},{5,1},{6,2},{7,3},{8,12},{9,13},{10,... | collective-permute-start | bytes 786440 | tf_op jit(solution)/shard_map/ppermute | solution.py:191
  15.4 1.5 %shard_map.75 = (f32[64,4096]{1,0:T(8,128)S(1)}, f32[64,4096]{1,0:T(8,128)S(1)}) custom-call(s32[2]{0:T(128)S(1)} %get-tuple-element.62.core_ref, bf16[512,768]{1,0:T(8,128)(2,1)S(1)} %pad_maximum_fusion.3.rows_ref, bf16[256,4096]{1,0:T(8,128)(2,1)S(1)} %get-tuple-element.52.high_ref, bf16[256,4096]{1,0:T(8,128)(2,1)S(1)} %get-tuple-element.53.low_ref), custom_call_target="tpu_custom_call" | custom-call | flops 1610612736 | bytes 8388608 | tf_op jit(solution)/shard_map/pallas_call | solution.py:94
  16.9 0.4 fusion.9
  17.5 0.4 constant_dynamic-slice_fusion.1
  18.0 0.2 multiply_convert_fusion.5
  18.2 3.2 %collective-permute-done.2 = f16[64,2048]{1,0:T(8,128)(2,1)S(1)} collective-permute-done((f16[64,2048]{1,0:T(8,128)(2,1)S(1)}, f16[64,2048]{1,0:T(8,128)(2,1)S(1)}, u32[]{:S(2)}, u32[]{:S(2)}) %collective-permute-start.2) | collective-permute-done | bytes 262176 | tf_op jit(solution)/shard_map/ppermute | solution.py:191
  21.7 1.6 %collective-permute-start.3 = (f16[32,2048]{1,0:T(8,128)(2,1)S(1)}, f16[32,2048]{1,0:T(8,128)(2,1)S(1)}, u32[]{:S(2)}, u32[]{:S(2)}) collective-permute-start(f16[32,2048]{1,0:T(8,128)(2,1)S(1)} %multiply_convert_fusion.11), channel_id=1, source_target_pairs={{0,4},{1,5},{2,6},{3,7},{4,0},{5,1},{6,2},{7,3},{8,12},{9,13},{10,... | collective-permute-start | bytes 393224 | tf_op jit(solution)/shard_map/ppermute | solution.py:191
  23.7 0.6 collective-permute-start.5
  24.3 1.5 %collective-permute-start.8 = (f16[64,2048]{1,0:T(8,128)(2,1)S(1)}, f16[64,2048]{1,0:T(8,128)(2,1)S(1)}, u32[]{:S(2)}, u32[]{:S(2)}) collective-permute-start(f16[64,2048]{1,0:T(8,128)(2,1)S(1)} %multiply_convert_fusion.5), channel_id=1, source_target_pairs={{0,2},{1,3},{2,0},{3,1},{4,6},{5,7},{6,4},{7,5},{8,10},{9,11},{10,... | collective-permute-start | bytes 786440 | tf_op jit(solution)/shard_map/ppermute | solution.py:191
  25.8 0.4 collective-permute-start.10
  26.2 0.7 collective-permute-done.3
  27.0 3.2 %collective-permute-done.5 = f16[32,2048]{1,0:T(8,128)(2,1)S(1)} collective-permute-done((f16[32,2048]{1,0:T(8,128)(2,1)S(1)}, f16[32,2048]{1,0:T(8,128)(2,1)S(1)}, u32[]{:S(2)}, u32[]{:S(2)}) %collective-permute-start.5) | collective-permute-done | bytes 131104 | tf_op jit(solution)/shard_map/ppermute | solution.py:191
  30.5 2.6 %collective-permute-start.12 = (f16[2,32,2048]{2,1,0:T(8,128)(2,1)S(1)}, f16[2,32,2048]{2,1,0:T(8,128)(2,1)S(1)}, u32[]{:S(2)}, u32[]{:S(2)}) collective-permute-start(f16[2,32,2048]{2,1,0:T(8,128)(2,1)S(1)} %get-tuple-element.94), channel_id=1, source_target_pairs={{0,8},{1,9},{2,10},{3,11},{4,12},{5,13},{6,14},{7,15},{8,0},{9,1},... | collective-permute-start | bytes 786440 | tf_op jit(solution)/shard_map/ppermute | solution.py:191
  33.1 0.7 collective-permute-done.8
  34.1 0.5 collective-permute-start.9
  34.6 0.9 %collective-permute-done.10 = f16[32,4096]{1,0:T(8,128)(2,1)S(1)} collective-permute-done((f16[32,4096]{1,0:T(8,128)(2,1)S(1)}, f16[32,4096]{1,0:T(8,128)(2,1)S(1)}, u32[]{:S(2)}, u32[]{:S(2)}) %collective-permute-start.10) | collective-permute-done | bytes 262176 | tf_op jit(solution)/shard_map/ppermute | solution.py:191
  35.8 0.8 collective-permute-start.11
  36.6 3.9 %collective-permute-done.9 = f16[32,2048]{1,0:T(8,128)(2,1)S(1)} collective-permute-done((f16[32,2048]{1,0:T(8,128)(2,1)S(1)}, f16[32,2048]{1,0:T(8,128)(2,1)S(1)}, u32[]{:S(2)}, u32[]{:S(2)}) %collective-permute-start.9) | collective-permute-done | bytes 131104 | tf_op jit(solution)/shard_map/ppermute | solution.py:191
  40.5 0.3 collective-permute-done.11
  41.1 2.9 %collective-permute-start.17 = (f16[2,32,2048]{2,1,0:T(8,128)(2,1)S(1)}, f16[2,32,2048]{2,1,0:T(8,128)(2,1)S(1)}, u32[]{:S(2)}, u32[]{:S(2)}) collective-permute-start(f16[2,32,2048]{2,1,0:T(8,128)(2,1)S(1)} %multiply_convert_fusion.3), channel_id=1, source_target_pairs={{0,8},{1,9},{2,10},{3,11},{4,12},{5,13},{6,14},{7,15},{8,0},{9,1},... | collective-permute-start | bytes 786440 | tf_op jit(solution)/shard_map/ppermute | solution.py:191
  44.0 0.3 constant_dynamic-slice_fusion.3
  44.3 0.4 collective-permute-start.14
  44.9 3.5 %collective-permute-start.13 = (bf16[2,32,2048]{2,1,0:T(8,128)(2,1)S(1)}, bf16[2,32,2048]{2,1,0:T(8,128)(2,1)S(1)}, u32[]{:S(2)}, u32[]{:S(2)}) collective-permute-start(bf16[2,32,2048]{2,1,0:T(8,128)(2,1)S(1)} %fusion.21), channel_id=1, source_target_pairs={{0,4},{1,5},{2,6},{3,7},{4,0},{5,1},{6,2},{7,3},{8,12},{9,13},{10,... | collective-permute-start | bytes 786440 | tf_op jit(solution)/shard_map/ppermute | solution.py:191
  48.4 5.2 %collective-permute-done.17 = f16[2,32,2048]{2,1,0:T(8,128)(2,1)S(1)} collective-permute-done((f16[2,32,2048]{2,1,0:T(8,128)(2,1)S(1)}, f16[2,32,2048]{2,1,0:T(8,128)(2,1)S(1)}, u32[]{:S(2)}, u32[]{:S(2)}) %collective-permute-start.17) | collective-permute-done | bytes 262176 | tf_op jit(solution)/shard_map/ppermute | solution.py:191
  53.8 0.5 collective-permute-start.18
  54.3 5.3 %collective-permute-done.14 = bf16[176,2048]{1,0:T(8,128)(2,1)S(1)} collective-permute-done((bf16[176,2048]{1,0:T(8,128)(2,1)S(1)}, bf16[176,2048]{1,0:T(8,128)(2,1)S(1)}, u32[]{:S(2)}, u32[]{:S(2)}) %collective-permute-start.14) | collective-permute-done | bytes 720928 | tf_op jit(solution)/shard_map/ppermute | solution.py:191
  59.7 0.7 fusion.1.refs_0_
  60.5 1.2 %collective-permute-done.16 = bf16[176,2048]{1,0:T(8,128)(2,1)S(1)} collective-permute-done((bf16[176,2048]{1,0:T(8,128)(2,1)S(1)}, bf16[176,2048]{1,0:T(8,128)(2,1)S(1)}, u32[]{:S(2)}, u32[]{:S(2)}) %collective-permute-start.16) | collective-permute-done | bytes 720928 | tf_op jit(solution)/shard_map/ppermute | solution.py:191
  61.8 0.9 %fusion.43.refs_1_ = f32[512,128]{1,0:T(8,128)S(1)} fusion(bf16[512,2048]{1,0:T(8,128)(2,1)S(1)} %constant_dynamic-update-slice_fusion, bf16[128,2048]{1,0:T(8,128)(2,1)S(1)} %bitcast.31), kind=kOutput, calls=%fused_computation.90 | convolution fusion | flops 268435456 | bytes 2883584 | tf_op jit(solution)/shard_map/dot_general | solution.py:263
  62.9 0.7 fusion.44.refs_3_
  63.6 0.7 fusion.refs_2_
  64.4 1.8 %shard_map.76 = bf16[16,64,256]{2,1,0:T(8,128)(2,1)} custom-call(s32[16]{0:T(128)S(1)} %copy-done.1, f32[512,128]{1,0:T(8,128)S(1)} %fusion.1.refs_0_, f32[512,128]{1,0:T(8,128)S(1)} %fusion.43.refs_1_, f32[512,128]{1,0:T(8,128)S(1)} %fusion.refs_2_, f32[512,128]{1,0:T(8,128)S(1)} %fusion.44.refs_3_), custom_call_target="tpu_custom_call" | custom-call | flops 65536 | bytes 1572864 | tf_op jit(solution)/shard_map/pallas_call | solution.py:139
  66.1 3.6 %all-to-all-start = ((bf16[16,1,64,256]{3,2,1,0:T(8,128)(2,1)}), bf16[16,1,64,256]{3,2,1,0:T(8,128)(2,1)S(1)}, u32[]{:S(2)}, u32[]{:S(2)}) async-start(bf16[16,1,64,256]{3,2,1,0:T(8,128)(2,1)} %bitcast.10), calls=%async_computation | async-start | bytes 1048576 | tf_op jit(solution)/shard_map/all_to_all | solution.py:318
  69.8 0.7 dynamic_slice.79
  70.6 0.3 fusion.36
  70.9 0.7 constant_dynamic-slice_fusion.allowed_ref
  71.6 12.6 %all-to-all-done = bf16[16,1,64,256]{3,2,1,0:T(8,128)(2,1)S(1)} async-done(((bf16[16,1,64,256]{3,2,1,0:T(8,128)(2,1)}), bf16[16,1,64,256]{3,2,1,0:T(8,128)(2,1)S(1)}, u32[]{:S(2)}, u32[]{:S(2)}) %all-to-all-start) | async-done | bytes 524320 | tf_op jit(solution)/shard_map/all_to_all | solution.py:318
  84.2 0.9 %shard_map.77 = f32[1024,128]{1,0:T(8,128)} custom-call(bf16[16,1,4,16,256]{4,3,2,1,0:T(8,128)(2,1)S(1)} %bitcast.27, f32[1,512]{1,0:T(1,128)S(1)} %constant_dynamic-slice_fusion.allowed_ref), custom_call_target="tpu_custom_call" | custom-call | flops 262144 | bytes 1048576 | tf_op jit(solution)/shard_map/pallas_call | solution.py:169
  (53 shorter events, 3.6 us)
Async XLA Ops:
  0.0 1.7 %copy-start = (bf16[16,16,4096]{2,1,0:T(8,128)(2,1)S(1)}, bf16[16,16,4096]{2,1,0:T(8,128)(2,1)}, u32[]{:S(2)}) copy-start(bf16[16,16,4096]{2,1,0:T(8,128)(2,1)} %param.9) | copy-start | bytes 6291460
  1.9 22.3 %collective-permute-start.7 = (bf16[80,2048]{1,0:T(8,128)(2,1)S(1)}, bf16[80,2048]{1,0:T(8,128)(2,1)S(1)}, u32[]{:S(2)}, u32[]{:S(2)}) collective-permute-start(bf16[80,2048]{1,0:T(8,128)(2,1)S(1)} %constant_dynamic-slice_fusion.2), channel_id=1, source_target_pairs={{0,2},{1,3},{2,0},{3,1},{4,6},{5,7},{6,4},{7,5},{8,10},{9,11},{10,... | collective-permute-start | bytes 983048 | tf_op jit(solution)/shard_map/ppermute | solution.py:191
  9.6 2.7 %collective-permute-start = (f16[128,4096]{1,0:T(8,128)(2,1)S(1)}, f16[128,4096]{1,0:T(8,128)(2,1)S(1)}, u32[]{:S(2)}, u32[]{:S(2)}) collective-permute-start(f16[128,4096]{1,0:T(8,128)(2,1)S(1)} %multiply_convert_fusion.1), channel_id=1, source_target_pairs={{0,1},{1,0},{2,3},{3,2},{4,5},{5,4},{6,7},{7,6},{8,9},{9,8},{10,11... | collective-permute-start | bytes 3145736 | tf_op jit(solution)/shard_map/ppermute | solution.py:191
  11.7 5.2 %collective-permute-start.6 = (f16[128,4096]{1,0:T(8,128)(2,1)S(1)}, f16[128,4096]{1,0:T(8,128)(2,1)S(1)}, u32[]{:S(2)}, u32[]{:S(2)}) collective-permute-start(f16[128,4096]{1,0:T(8,128)(2,1)S(1)} %multiply_convert_fusion), channel_id=1, source_target_pairs={{0,1},{1,0},{2,3},{3,2},{4,5},{5,4},{6,7},{7,6},{8,9},{9,8},{10,11... | collective-permute-start | bytes 3145736 | tf_op jit(solution)/shard_map/ppermute | solution.py:191
  13.0 8.4 %collective-permute-start.2 = (f16[64,2048]{1,0:T(8,128)(2,1)S(1)}, f16[64,2048]{1,0:T(8,128)(2,1)S(1)}, u32[]{:S(2)}, u32[]{:S(2)}) collective-permute-start(f16[64,2048]{1,0:T(8,128)(2,1)S(1)} %multiply_convert_fusion.7), channel_id=1, source_target_pairs={{0,2},{1,3},{2,0},{3,1},{4,6},{5,7},{6,4},{7,5},{8,10},{9,11},{10,... | collective-permute-start | bytes 786440 | tf_op jit(solution)/shard_map/ppermute | solution.py:191
  13.3 10.1 %collective-permute-start.4 = (f16[32,4096]{1,0:T(8,128)(2,1)S(1)}, f16[32,4096]{1,0:T(8,128)(2,1)S(1)}, u32[]{:S(2)}, u32[]{:S(2)}) collective-permute-start(f16[32,4096]{1,0:T(8,128)(2,1)S(1)} %multiply_convert_fusion.6), channel_id=1, source_target_pairs={{0,4},{1,5},{2,6},{3,7},{4,0},{5,1},{6,2},{7,3},{8,12},{9,13},{10,... | collective-permute-start | bytes 786440 | tf_op jit(solution)/shard_map/ppermute | solution.py:191
  17.9 41.8 %collective-permute-start.1 = (bf16[256,2048]{1,0:T(8,128)(2,1)S(1)}, bf16[256,2048]{1,0:T(8,128)(2,1)S(1)}, u32[]{:S(2)}, u32[]{:S(2)}) collective-permute-start(bf16[256,2048]{1,0:T(8,128)(2,1)S(1)} %constant_dynamic-slice_fusion.1), channel_id=1, source_target_pairs={{0,1},{1,0},{2,3},{3,2},{4,5},{5,4},{6,7},{7,6},{8,9},{9,8},{10,11... | collective-permute-start | bytes 3145736 | tf_op jit(solution)/shard_map/ppermute | solution.py:191
  21.7 5.2 %collective-permute-start.3 = (f16[32,2048]{1,0:T(8,128)(2,1)S(1)}, f16[32,2048]{1,0:T(8,128)(2,1)S(1)}, u32[]{:S(2)}, u32[]{:S(2)}) collective-permute-start(f16[32,2048]{1,0:T(8,128)(2,1)S(1)} %multiply_convert_fusion.11), channel_id=1, source_target_pairs={{0,4},{1,5},{2,6},{3,7},{4,0},{5,1},{6,2},{7,3},{8,12},{9,13},{10,... | collective-permute-start | bytes 393224 | tf_op jit(solution)/shard_map/ppermute | solution.py:191
  23.7 6.5 %collective-permute-start.5 = (f16[32,2048]{1,0:T(8,128)(2,1)S(1)}, f16[32,2048]{1,0:T(8,128)(2,1)S(1)}, u32[]{:S(2)}, u32[]{:S(2)}) collective-permute-start(f16[32,2048]{1,0:T(8,128)(2,1)S(1)} %multiply_convert_fusion.10), channel_id=1, source_target_pairs={{0,2},{1,3},{2,0},{3,1},{4,6},{5,7},{6,4},{7,5},{8,10},{9,11},{10,... | collective-permute-start | bytes 393224 | tf_op jit(solution)/shard_map/ppermute | solution.py:191
  24.3 9.5 %collective-permute-start.8 = (f16[64,2048]{1,0:T(8,128)(2,1)S(1)}, f16[64,2048]{1,0:T(8,128)(2,1)S(1)}, u32[]{:S(2)}, u32[]{:S(2)}) collective-permute-start(f16[64,2048]{1,0:T(8,128)(2,1)S(1)} %multiply_convert_fusion.5), channel_id=1, source_target_pairs={{0,2},{1,3},{2,0},{3,1},{4,6},{5,7},{6,4},{7,5},{8,10},{9,11},{10,... | collective-permute-start | bytes 786440 | tf_op jit(solution)/shard_map/ppermute | solution.py:191
  25.8 9.8 %collective-permute-start.10 = (f16[32,4096]{1,0:T(8,128)(2,1)S(1)}, f16[32,4096]{1,0:T(8,128)(2,1)S(1)}, u32[]{:S(2)}, u32[]{:S(2)}) collective-permute-start(f16[32,4096]{1,0:T(8,128)(2,1)S(1)} %multiply_convert_fusion.4), channel_id=1, source_target_pairs={{0,4},{1,5},{2,6},{3,7},{4,0},{5,1},{6,2},{7,3},{8,12},{9,13},{10,... | collective-permute-start | bytes 786440 | tf_op jit(solution)/shard_map/ppermute | solution.py:191
  30.5 14.3 %collective-permute-start.12 = (f16[2,32,2048]{2,1,0:T(8,128)(2,1)S(1)}, f16[2,32,2048]{2,1,0:T(8,128)(2,1)S(1)}, u32[]{:S(2)}, u32[]{:S(2)}) collective-permute-start(f16[2,32,2048]{2,1,0:T(8,128)(2,1)S(1)} %get-tuple-element.94), channel_id=1, source_target_pairs={{0,8},{1,9},{2,10},{3,11},{4,12},{5,13},{6,14},{7,15},{8,0},{9,1},... | collective-permute-start | bytes 786440 | tf_op jit(solution)/shard_map/ppermute | solution.py:191
  34.1 6.3 %collective-permute-start.9 = (f16[32,2048]{1,0:T(8,128)(2,1)S(1)}, f16[32,2048]{1,0:T(8,128)(2,1)S(1)}, u32[]{:S(2)}, u32[]{:S(2)}) collective-permute-start(f16[32,2048]{1,0:T(8,128)(2,1)S(1)} %multiply_convert_fusion.9), channel_id=1, source_target_pairs={{0,4},{1,5},{2,6},{3,7},{4,0},{5,1},{6,2},{7,3},{8,12},{9,13},{10,... | collective-permute-start | bytes 393224 | tf_op jit(solution)/shard_map/ppermute | solution.py:191
  35.8 5.0 %collective-permute-start.11 = (f16[32,2048]{1,0:T(8,128)(2,1)S(1)}, f16[32,2048]{1,0:T(8,128)(2,1)S(1)}, u32[]{:S(2)}, u32[]{:S(2)}) collective-permute-start(f16[32,2048]{1,0:T(8,128)(2,1)S(1)} %multiply_convert_fusion.8), channel_id=1, source_target_pairs={{0,2},{1,3},{2,0},{3,1},{4,6},{5,7},{6,4},{7,5},{8,10},{9,11},{10,... | collective-permute-start | bytes 393224 | tf_op jit(solution)/shard_map/ppermute | solution.py:191
  41.1 12.5 %collective-permute-start.17 = (f16[2,32,2048]{2,1,0:T(8,128)(2,1)S(1)}, f16[2,32,2048]{2,1,0:T(8,128)(2,1)S(1)}, u32[]{:S(2)}, u32[]{:S(2)}) collective-permute-start(f16[2,32,2048]{2,1,0:T(8,128)(2,1)S(1)} %multiply_convert_fusion.3), channel_id=1, source_target_pairs={{0,8},{1,9},{2,10},{3,11},{4,12},{5,13},{6,14},{7,15},{8,0},{9,1},... | collective-permute-start | bytes 786440 | tf_op jit(solution)/shard_map/ppermute | solution.py:191
  44.3 15.2 %collective-permute-start.14 = (bf16[176,2048]{1,0:T(8,128)(2,1)S(1)}, bf16[176,2048]{1,0:T(8,128)(2,1)S(1)}, u32[]{:S(2)}, u32[]{:S(2)}) collective-permute-start(bf16[176,2048]{1,0:T(8,128)(2,1)S(1)} %constant_dynamic-slice_fusion.3), channel_id=1, source_target_pairs={{0,2},{1,3},{2,0},{3,1},{4,6},{5,7},{6,4},{7,5},{8,10},{9,11},{10,... | collective-permute-start | bytes 2162696 | tf_op jit(solution)/shard_map/ppermute | solution.py:191
  44.9 14.7 %collective-permute-start.13 = (bf16[2,32,2048]{2,1,0:T(8,128)(2,1)S(1)}, bf16[2,32,2048]{2,1,0:T(8,128)(2,1)S(1)}, u32[]{:S(2)}, u32[]{:S(2)}) collective-permute-start(bf16[2,32,2048]{2,1,0:T(8,128)(2,1)S(1)} %fusion.21), channel_id=1, source_target_pairs={{0,4},{1,5},{2,6},{3,7},{4,0},{5,1},{6,2},{7,3},{8,12},{9,13},{10,... | collective-permute-start | bytes 786440 | tf_op jit(solution)/shard_map/ppermute | solution.py:191
  48.4 12.1 %collective-permute-start.15 = (bf16[80,2048]{1,0:T(8,128)(2,1)S(1)}, bf16[80,2048]{1,0:T(8,128)(2,1)S(1)}, u32[]{:S(2)}, u32[]{:S(2)}) collective-permute-start(bf16[80,2048]{1,0:T(8,128)(2,1)S(1)} %collective-permute-done.7), channel_id=1, source_target_pairs={{0,1},{1,0},{2,3},{3,2},{4,5},{5,4},{6,7},{7,6},{8,9},{9,8},{10,11... | collective-permute-start | bytes 983048 | tf_op jit(solution)/shard_map/ppermute | solution.py:191
  53.8 8.9 %collective-permute-start.18 = (bf16[2,32,2048]{2,1,0:T(8,128)(2,1)S(1)}, bf16[2,32,2048]{2,1,0:T(8,128)(2,1)S(1)}, u32[]{:S(2)}, u32[]{:S(2)}) collective-permute-start(bf16[2,32,2048]{2,1,0:T(8,128)(2,1)S(1)} %fusion.24), channel_id=1, source_target_pairs={{0,4},{1,5},{2,6},{3,7},{4,0},{5,1},{6,2},{7,3},{8,12},{9,13},{10,... | collective-permute-start | bytes 786440 | tf_op jit(solution)/shard_map/ppermute | solution.py:191
  59.6 2.2 %collective-permute-start.16 = (bf16[176,2048]{1,0:T(8,128)(2,1)S(1)}, bf16[176,2048]{1,0:T(8,128)(2,1)S(1)}, u32[]{:S(2)}, u32[]{:S(2)}) collective-permute-start(bf16[176,2048]{1,0:T(8,128)(2,1)S(1)} %collective-permute-done.14), channel_id=1, source_target_pairs={{0,1},{1,0},{2,3},{3,2},{4,5},{5,4},{6,7},{7,6},{8,9},{9,8},{10,11... | collective-permute-start | bytes 2162696 | tf_op jit(solution)/shard_map/ppermute | solution.py:191
  63.6 0.7 copy-start.1
  64.3 5.4 %copy-start.2 = (s32[8,12]{1,0:T(8,128)S(1)}, s32[8,12]{1,0:T(8,128)}, u32[]{:S(2)}) copy-start(s32[8,12]{1,0:T(8,128)} %param.11) | copy-start | bytes 1156
  64.3 6.2 %copy-start.3 = (s32[8]{0:T(128)S(1)}, s32[8]{0:T(128)}, u32[]{:S(2)}) copy-start(s32[8]{0:T(128)} %param.12) | copy-start | bytes 100
  64.3 6.3 %copy-start.4 = (s32[512]{0:T(512)S(1)}, s32[512]{0:T(512)}, u32[]{:S(2)}) copy-start(s32[512]{0:T(512)} %param.10) | copy-start | bytes 6148
  66.1 18.0 %all-to-all-start = ((bf16[16,1,64,256]{3,2,1,0:T(8,128)(2,1)}), bf16[16,1,64,256]{3,2,1,0:T(8,128)(2,1)S(1)}, u32[]{:S(2)}, u32[]{:S(2)}) async-start(bf16[16,1,64,256]{3,2,1,0:T(8,128)(2,1)} %bitcast.10), calls=%async_computation | async-start | bytes 1048576 | tf_op jit(solution)/shard_map/all_to_all | solution.py:318

commit v27 on v24

--- a/solution.py
+++ b/solution.py
@@ -285,14 +285,14 @@
     mine = product(after(starts[0], sent), left, [high, low], mine_kernel, MINE_VMEM, PATHS)
     one = paths(mine, got)
     sent = messages(one, 0)
-    got = swap(pack(after(full[1], mine[0])), 0)
+    got = swap(pack(after(full[1], sent)), 0)
     mine = product(after(starts[1], sent), left, [high, low], mine_kernel, MINE_VMEM, PATHS)
     two = paths(mine, got)
     blocks = after(blocks, sent)
     near = features(blocks, 0, every, 0)
     sibling = swap(near, 0)
     one = exchange(one, sent, 0)
-    sent = messages(one, 1)
+    sent = after(messages(one, 1), two)
     sent_two = after(messages(two, 0), (sent, early))
     one = halve(exchange(one, sent, 1))
     sent = pack(one)

time: 84 us -> 89.9 us (1.070)
  waiting for transfers between devices: 35.9 us -> 42 us
    ppermute x19, waiting for transfers between devices: 23.3 us -> 29.3 us  [swap(): return lax.ppermute(value, 'rows', [(r, r ^ 1 << bit) for r in range(n)])]
  transfers between devices with their start and end apart: 20 -> 20, of which waited for: 13 -> 14; matrix products, arithmetic and copies ran while one was open for 11% -> 9% of each run, Pallas kernels for 9% -> 3%
where the time goes in v27:
time: 89.9 us; the launch traced here: 89.7 us
  waiting for transfers between devices  42 us (47%)
  starting transfers between devices  25.1 us (28%)
  Pallas kernels  9.96 us (11%)
  other arithmetic  6.08 us (7%)
  matrix products  3.34 us (4%)
  local copies, waits for them, and re-layouts  2.85 us (3%)
    ppermute x19, waiting for transfers between devices, swap(): return lax.ppermute(value, 'rows', [(r, r ^ 1 << bit) for r in range(n)])  29.3 us
    ppermute x19, starting transfers between devices, swap(): return lax.ppermute(value, 'rows', [(r, r ^ 1 << bit) for r in range(n)])  20.7 us
    all_to_all x1, waiting for transfers between devices, shards(): lax.all_to_all(ordered, 'rows', split_axis=0, concat_axis=0, tiled=True)  12.6 us
    pallas_call x3, Pallas kernels, product(): pl.pallas_call(kernel, in_specs=[pl.BlockSpec(memory_space=pltpu.SMEM), i...  7.32 us
    all_to_all x1, starting transfers between devices, shards(): lax.all_to_all(ordered, 'rows', split_axis=0, concat_axis=0, tiled=True)  4.35 us
    dot_general x4, matrix products, scores(): lax.dot_general(group, value, (((1,), (1,)), ((), ())), preferred_element...  3.07 us
    convert_element_type x12, other arithmetic, pack(): return (value * lax.rsqrt(jnp.abs(value) + LEAST)).astype(jnp.float16)  2.39 us
  transfers between devices with their start and end apart: 20, of which 14 were waited for; matrix products, arithmetic and copies ran while one was open for 9% of the time, Pallas kernels for 3%

profile of v27, /device:TPU:0, one launch (start us, length us, event | category | flops | bytes accessed | tf_op | source)
XLA Modules:
  0.0 89.7 jit_solution(484921168430398549)
XLA Ops:
  0.1 1.2 %fusion.10 = (bf16[512,256]{1,0:T(8,128)(2,1)S(1)}, bf16[512,256]{1,0:T(8,128)(2,1)S(1)}) fusion(f32[512,256]{1,0:T(8,128)} %param.7), kind=kLoop, calls=%fused_computation.26 | loop fusion | flops 524288 | bytes 1048576 | tf_op jit(solution)/shard_map/convert_element_type | solution.py:274
  1.4 0.4 copy-done
  1.9 4.2 %shard_map.73 = (f32[128,4096]{1,0:T(8,128)S(1)}, f32[128,4096]{1,0:T(8,128)S(1)}, bf16[256,4096]{1,0:T(8,128)(2,1)S(1)}, bf16[256,4096]{1,0:T(8,128)(2,1)S(1)}) custom-call(s32[1]{0:T(128)} %bitcast.2.core_ref, bf16[512,768]{1,0:T(8,128)(2,1)S(1)} %pad_maximum_fusion.3.rows_ref, f32[256,4096]{1,0:T(8,128)} %columns_hbm.1), custom_call_target="tpu_custom_call" | custom-call | flops 1610612736 | bytes 8388608 | tf_op jit(solution)/shard_map/pallas_call | solution.py:94
  6.2 0.4 multiply_convert_fusion.1
  6.6 0.5 collective-permute-start
  7.2 2.6 %collective-permute-start.7 = (bf16[96,2048]{1,0:T(8,128)(2,1)S(1)}, bf16[96,2048]{1,0:T(8,128)(2,1)S(1)}, u32[]{:S(2)}, u32[]{:S(2)}) collective-permute-start(bf16[96,2048]{1,0:T(8,128)(2,1)S(1)} %constant_dynamic-slice_fusion.2), channel_id=1, source_target_pairs={{0,2},{1,3},{2,0},{3,1},{4,6},{5,7},{6,4},{7,5},{8,10},{9,11},{10,... | collective-permute-start | bytes 1179656 | tf_op jit(solution)/shard_map/ppermute | solution.py:191
  9.7 1.5 %shard_map.74 = (f32[64,4096]{1,0:T(8,128)S(1)}, f32[64,4096]{1,0:T(8,128)S(1)}) custom-call(s32[2]{0:T(128)S(1)} %get-tuple-element.53.core_ref, bf16[512,768]{1,0:T(8,128)(2,1)S(1)} %pad_maximum_fusion.3.rows_ref, bf16[256,4096]{1,0:T(8,128)(2,1)S(1)} %get-tuple-element.54.high_ref, bf16[256,4096]{1,0:T(8,128)(2,1)S(1)} %get-tuple-element.55.low_ref), custom_call_target="tpu_custom_call" | custom-call | flops 1610612736 | bytes 8388608 | tf_op jit(solution)/shard_map/pallas_call | solution.py:94
  11.3 0.4 fusion.5
  12.0 1.7 %collective-permute-start.3 = (f16[32,4096]{1,0:T(8,128)(2,1)S(1)}, f16[32,4096]{1,0:T(8,128)(2,1)S(1)}, u32[]{:S(2)}, u32[]{:S(2)}) collective-permute-start(f16[32,4096]{1,0:T(8,128)(2,1)S(1)} %multiply_convert_fusion.6), channel_id=1, source_target_pairs={{0,4},{1,5},{2,6},{3,7},{4,0},{5,1},{6,2},{7,3},{8,12},{9,13},{10,... | collective-permute-start | bytes 786440 | tf_op jit(solution)/shard_map/ppermute | solution.py:191
  13.7 1.0 %collective-permute-start.2 = (f16[64,2048]{1,0:T(8,128)(2,1)S(1)}, f16[64,2048]{1,0:T(8,128)(2,1)S(1)}, u32[]{:S(2)}, u32[]{:S(2)}) collective-permute-start(f16[64,2048]{1,0:T(8,128)(2,1)S(1)} %multiply_convert_fusion.7), channel_id=1, source_target_pairs={{0,2},{1,3},{2,0},{3,1},{4,6},{5,7},{6,4},{7,5},{8,10},{9,11},{10,... | collective-permute-start | bytes 786440 | tf_op jit(solution)/shard_map/ppermute | solution.py:191
  14.7 0.4 multiply_convert_fusion
  15.2 0.4 constant_dynamic-slice_fusion.1
  15.7 0.6 collective-permute-start.1
  16.2 1.5 %shard_map.75 = (f32[64,4096]{1,0:T(8,128)S(1)}, f32[64,4096]{1,0:T(8,128)S(1)}) custom-call(s32[2]{0:T(128)S(1)} %get-tuple-element.64.core_ref, bf16[512,768]{1,0:T(8,128)(2,1)S(1)} %pad_maximum_fusion.3.rows_ref, bf16[256,4096]{1,0:T(8,128)(2,1)S(1)} %get-tuple-element.54.high_ref, bf16[256,4096]{1,0:T(8,128)(2,1)S(1)} %get-tuple-element.55.low_ref), custom_call_target="tpu_custom_call" | custom-call | flops 1610612736 | bytes 8388608 | tf_op jit(solution)/shard_map/pallas_call | solution.py:94
  17.8 2.7 %collective-permute-done.3 = f16[32,4096]{1,0:T(8,128)(2,1)S(1)} collective-permute-done((f16[32,4096]{1,0:T(8,128)(2,1)S(1)}, f16[32,4096]{1,0:T(8,128)(2,1)S(1)}, u32[]{:S(2)}, u32[]{:S(2)}) %collective-permute-start.3) | collective-permute-done | bytes 262176 | tf_op jit(solution)/shard_map/ppermute | solution.py:191
  20.8 4.3 %collective-permute-done.2 = f16[64,2048]{1,0:T(8,128)(2,1)S(1)} collective-permute-done((f16[64,2048]{1,0:T(8,128)(2,1)S(1)}, f16[64,2048]{1,0:T(8,128)(2,1)S(1)}, u32[]{:S(2)}, u32[]{:S(2)}) %collective-permute-start.2) | collective-permute-done | bytes 262176 | tf_op jit(solution)/shard_map/ppermute | solution.py:191
  25.4 0.4 fusion.9
  25.9 1.9 %collective-permute-start.5 = (f16[32,2048]{1,0:T(8,128)(2,1)S(1)}, f16[32,2048]{1,0:T(8,128)(2,1)S(1)}, u32[]{:S(2)}, u32[]{:S(2)}) collective-permute-start(f16[32,2048]{1,0:T(8,128)(2,1)S(1)} %multiply_convert_fusion.11), channel_id=1, source_target_pairs={{0,4},{1,5},{2,6},{3,7},{4,0},{5,1},{6,2},{7,3},{8,12},{9,13},{10,... | collective-permute-start | bytes 393224 | tf_op jit(solution)/shard_map/ppermute | solution.py:191
  27.8 1.5 %collective-permute-start.6 = (f16[32,2048]{1,0:T(8,128)(2,1)S(1)}, f16[32,2048]{1,0:T(8,128)(2,1)S(1)}, u32[]{:S(2)}, u32[]{:S(2)}) collective-permute-start(f16[32,2048]{1,0:T(8,128)(2,1)S(1)} %multiply_convert_fusion.10), channel_id=1, source_target_pairs={{0,2},{1,3},{2,0},{3,1},{4,6},{5,7},{6,4},{7,5},{8,10},{9,11},{10,... | collective-permute-start | bytes 393224 | tf_op jit(solution)/shard_map/ppermute | solution.py:191
  29.5 0.6 collective-permute-start.8
  30.3 1.0 %collective-permute-done.5 = f16[32,2048]{1,0:T(8,128)(2,1)S(1)} collective-permute-done((f16[32,2048]{1,0:T(8,128)(2,1)S(1)}, f16[32,2048]{1,0:T(8,128)(2,1)S(1)}, u32[]{:S(2)}, u32[]{:S(2)}) %collective-permute-start.5) | collective-permute-done | bytes 131104 | tf_op jit(solution)/shard_map/ppermute | solution.py:191
  31.4 2.7 %collective-permute-done.6 = f16[32,2048]{1,0:T(8,128)(2,1)S(1)} collective-permute-done((f16[32,2048]{1,0:T(8,128)(2,1)S(1)}, f16[32,2048]{1,0:T(8,128)(2,1)S(1)}, u32[]{:S(2)}, u32[]{:S(2)}) %collective-permute-start.6) | collective-permute-done | bytes 131104 | tf_op jit(solution)/shard_map/ppermute | solution.py:191
  34.5 2.7 %collective-permute-start.12 = (f16[2,32,2048]{2,1,0:T(8,128)(2,1)S(1)}, f16[2,32,2048]{2,1,0:T(8,128)(2,1)S(1)}, u32[]{:S(2)}, u32[]{:S(2)}) collective-permute-start(f16[2,32,2048]{2,1,0:T(8,128)(2,1)S(1)} %get-tuple-element.98), channel_id=1, source_target_pairs={{0,8},{1,9},{2,10},{3,11},{4,12},{5,13},{6,14},{7,15},{8,0},{9,1},... | collective-permute-start | bytes 786440 | tf_op jit(solution)/shard_map/ppermute | solution.py:191
  37.1 1.2 %collective-permute-done.8 = f16[64,2048]{1,0:T(8,128)(2,1)S(1)} collective-permute-done((f16[64,2048]{1,0:T(8,128)(2,1)S(1)}, f16[64,2048]{1,0:T(8,128)(2,1)S(1)}, u32[]{:S(2)}, u32[]{:S(2)}) %collective-permute-start.8) | collective-permute-done | bytes 262176 | tf_op jit(solution)/shard_map/ppermute | solution.py:191
  38.6 0.3 collective-permute-start.9
  39.0 2.7 %collective-permute-done.10 = f16[32,4096]{1,0:T(8,128)(2,1)S(1)} collective-permute-done((f16[32,4096]{1,0:T(8,128)(2,1)S(1)}, f16[32,4096]{1,0:T(8,128)(2,1)S(1)}, u32[]{:S(2)}, u32[]{:S(2)}) %collective-permute-start.10) | collective-permute-done | bytes 262176 | tf_op jit(solution)/shard_map/ppermute | solution.py:191
  42.0 1.7 %collective-permute-start.11 = (f16[32,2048]{1,0:T(8,128)(2,1)S(1)}, f16[32,2048]{1,0:T(8,128)(2,1)S(1)}, u32[]{:S(2)}, u32[]{:S(2)}) collective-permute-start(f16[32,2048]{1,0:T(8,128)(2,1)S(1)} %multiply_convert_fusion.8), channel_id=1, source_target_pairs={{0,2},{1,3},{2,0},{3,1},{4,6},{5,7},{6,4},{7,5},{8,10},{9,11},{10,... | collective-permute-start | bytes 393224 | tf_op jit(solution)/shard_map/ppermute | solution.py:191
  43.7 1.7 %collective-permute-done.9 = f16[32,2048]{1,0:T(8,128)(2,1)S(1)} collective-permute-done((f16[32,2048]{1,0:T(8,128)(2,1)S(1)}, f16[32,2048]{1,0:T(8,128)(2,1)S(1)}, u32[]{:S(2)}, u32[]{:S(2)}) %collective-permute-start.9) | collective-permute-done | bytes 131104 | tf_op jit(solution)/shard_map/ppermute | solution.py:191
  45.5 1.5 %collective-permute-done.11 = f16[32,2048]{1,0:T(8,128)(2,1)S(1)} collective-permute-done((f16[32,2048]{1,0:T(8,128)(2,1)S(1)}, f16[32,2048]{1,0:T(8,128)(2,1)S(1)}, u32[]{:S(2)}, u32[]{:S(2)}) %collective-permute-start.11) | collective-permute-done | bytes 131104 | tf_op jit(solution)/shard_map/ppermute | solution.py:191
  47.3 1.4 %collective-permute-start.17 = (f16[2,32,2048]{2,1,0:T(8,128)(2,1)S(1)}, f16[2,32,2048]{2,1,0:T(8,128)(2,1)S(1)}, u32[]{:S(2)}, u32[]{:S(2)}) collective-permute-start(f16[2,32,2048]{2,1,0:T(8,128)(2,1)S(1)} %multiply_convert_fusion.3), channel_id=1, source_target_pairs={{0,8},{1,9},{2,10},{3,11},{4,12},{5,13},{6,14},{7,15},{8,0},{9,1},... | collective-permute-start | bytes 786440 | tf_op jit(solution)/shard_map/ppermute | solution.py:191
  48.7 0.3 constant_dynamic-slice_fusion.3
  48.9 1.6 %collective-permute-start.14 = (bf16[160,2048]{1,0:T(8,128)(2,1)S(1)}, bf16[160,2048]{1,0:T(8,128)(2,1)S(1)}, u32[]{:S(2)}, u32[]{:S(2)}) collective-permute-start(bf16[160,2048]{1,0:T(8,128)(2,1)S(1)} %constant_dynamic-slice_fusion.3), channel_id=1, source_target_pairs={{0,2},{1,3},{2,0},{3,1},{4,6},{5,7},{6,4},{7,5},{8,10},{9,11},{10,... | collective-permute-start | bytes 1966088 | tf_op jit(solution)/shard_map/ppermute | solution.py:191
  50.6 2.4 %collective-permute-start.13 = (bf16[2,32,2048]{2,1,0:T(8,128)(2,1)S(1)}, bf16[2,32,2048]{2,1,0:T(8,128)(2,1)S(1)}, u32[]{:S(2)}, u32[]{:S(2)}) collective-permute-start(bf16[2,32,2048]{2,1,0:T(8,128)(2,1)S(1)} %fusion.21), channel_id=1, source_target_pairs={{0,4},{1,5},{2,6},{3,7},{4,0},{5,1},{6,2},{7,3},{8,12},{9,13},{10,... | collective-permute-start | bytes 786440 | tf_op jit(solution)/shard_map/ppermute | solution.py:191
  53.1 5.7 %collective-permute-done.17 = f16[2,32,2048]{2,1,0:T(8,128)(2,1)S(1)} collective-permute-done((f16[2,32,2048]{2,1,0:T(8,128)(2,1)S(1)}, f16[2,32,2048]{2,1,0:T(8,128)(2,1)S(1)}, u32[]{:S(2)}, u32[]{:S(2)}) %collective-permute-start.17) | collective-permute-done | bytes 262176 | tf_op jit(solution)/shard_map/ppermute | solution.py:191
  58.9 2.9 %collective-permute-done.13 = bf16[2,32,2048]{2,1,0:T(8,128)(2,1)S(1)} collective-permute-done((bf16[2,32,2048]{2,1,0:T(8,128)(2,1)S(1)}, bf16[2,32,2048]{2,1,0:T(8,128)(2,1)S(1)}, u32[]{:S(2)}, u32[]{:S(2)}) %collective-permute-start.13) | collective-permute-done | bytes 262176 | tf_op jit(solution)/shard_map/ppermute | solution.py:191
  61.9 1.3 %collective-permute-done.14 = bf16[160,2048]{1,0:T(8,128)(2,1)S(1)} collective-permute-done((bf16[160,2048]{1,0:T(8,128)(2,1)S(1)}, bf16[160,2048]{1,0:T(8,128)(2,1)S(1)}, u32[]{:S(2)}, u32[]{:S(2)}) %collective-permute-start.14) | collective-permute-done | bytes 655392 | tf_op jit(solution)/shard_map/ppermute | solution.py:191
  63.2 0.7 fusion.1.refs_0_
  64.1 1.3 %collective-permute-done.16 = bf16[160,2048]{1,0:T(8,128)(2,1)S(1)} collective-permute-done((bf16[160,2048]{1,0:T(8,128)(2,1)S(1)}, bf16[160,2048]{1,0:T(8,128)(2,1)S(1)}, u32[]{:S(2)}, u32[]{:S(2)}) %collective-permute-start.16) | collective-permute-done | bytes 655392 | tf_op jit(solution)/shard_map/ppermute | solution.py:191
  65.4 0.9 %fusion.43.refs_1_ = f32[512,128]{1,0:T(8,128)S(1)} fusion(bf16[512,2048]{1,0:T(8,128)(2,1)S(1)} %constant_dynamic-update-slice_fusion, bf16[128,2048]{1,0:T(8,128)(2,1)S(1)} %bitcast.31), kind=kOutput, calls=%fused_computation.90 | convolution fusion | flops 268435456 | bytes 2883584 | tf_op jit(solution)/shard_map/dot_general | solution.py:263
  66.3 0.3 collective-permute-done.18
  66.7 0.7 fusion.44.refs_3_
  67.4 0.7 fusion.refs_2_
  68.2 1.8 %shard_map.76 = bf16[16,64,256]{2,1,0:T(8,128)(2,1)} custom-call(s32[16]{0:T(128)S(1)} %copy-done.1, f32[512,128]{1,0:T(8,128)S(1)} %fusion.1.refs_0_, f32[512,128]{1,0:T(8,128)S(1)} %fusion.43.refs_1_, f32[512,128]{1,0:T(8,128)S(1)} %fusion.refs_2_, f32[512,128]{1,0:T(8,128)S(1)} %fusion.44.refs_3_), custom_call_target="tpu_custom_call" | custom-call | flops 65536 | bytes 1572864 | tf_op jit(solution)/shard_map/pallas_call | solution.py:139
  70.0 4.3 %all-to-all-start = ((bf16[16,1,64,256]{3,2,1,0:T(8,128)(2,1)}), bf16[16,1,64,256]{3,2,1,0:T(8,128)(2,1)S(1)}, u32[]{:S(2)}, u32[]{:S(2)}) async-start(bf16[16,1,64,256]{3,2,1,0:T(8,128)(2,1)} %bitcast.10), calls=%async_computation | async-start | bytes 1048576 | tf_op jit(solution)/shard_map/all_to_all | solution.py:318
  74.4 0.7 dynamic_slice.79
  75.5 0.7 constant_dynamic-slice_fusion.allowed_ref
  76.2 12.6 %all-to-all-done = bf16[16,1,64,256]{3,2,1,0:T(8,128)(2,1)S(1)} async-done(((bf16[16,1,64,256]{3,2,1,0:T(8,128)(2,1)}), bf16[16,1,64,256]{3,2,1,0:T(8,128)(2,1)S(1)}, u32[]{:S(2)}, u32[]{:S(2)}) %all-to-all-start) | async-done | bytes 524320 | tf_op jit(solution)/shard_map/all_to_all | solution.py:318
  88.8 0.9 shard_map.77
  (53 shorter events, 4.3 us)
Async XLA Ops:
  0.0 1.7 %copy-start = (bf16[16,16,4096]{2,1,0:T(8,128)(2,1)S(1)}, bf16[16,16,4096]{2,1,0:T(8,128)(2,1)}, u32[]{:S(2)}) copy-start(bf16[16,16,4096]{2,1,0:T(8,128)(2,1)} %param.9) | copy-start | bytes 6291460
  6.6 4.7 %collective-permute-start = (f16[128,4096]{1,0:T(8,128)(2,1)S(1)}, f16[128,4096]{1,0:T(8,128)(2,1)S(1)}, u32[]{:S(2)}, u32[]{:S(2)}) collective-permute-start(f16[128,4096]{1,0:T(8,128)(2,1)S(1)} %multiply_convert_fusion.1), channel_id=1, source_target_pairs={{0,1},{1,0},{2,3},{3,2},{4,5},{5,4},{6,7},{7,6},{8,9},{9,8},{10,11... | collective-permute-start | bytes 3145736 | tf_op jit(solution)/shard_map/ppermute | solution.py:191
  7.2 22.4 %collective-permute-start.7 = (bf16[96,2048]{1,0:T(8,128)(2,1)S(1)}, bf16[96,2048]{1,0:T(8,128)(2,1)S(1)}, u32[]{:S(2)}, u32[]{:S(2)}) collective-permute-start(bf16[96,2048]{1,0:T(8,128)(2,1)S(1)} %constant_dynamic-slice_fusion.2), channel_id=1, source_target_pairs={{0,2},{1,3},{2,0},{3,1},{4,6},{5,7},{6,4},{7,5},{8,10},{9,11},{10,... | collective-permute-start | bytes 1179656 | tf_op jit(solution)/shard_map/ppermute | solution.py:191
  12.0 8.4 %collective-permute-start.3 = (f16[32,4096]{1,0:T(8,128)(2,1)S(1)}, f16[32,4096]{1,0:T(8,128)(2,1)S(1)}, u32[]{:S(2)}, u32[]{:S(2)}) collective-permute-start(f16[32,4096]{1,0:T(8,128)(2,1)S(1)} %multiply_convert_fusion.6), channel_id=1, source_target_pairs={{0,4},{1,5},{2,6},{3,7},{4,0},{5,1},{6,2},{7,3},{8,12},{9,13},{10,... | collective-permute-start | bytes 786440 | tf_op jit(solution)/shard_map/ppermute | solution.py:191
  13.7 11.4 %collective-permute-start.2 = (f16[64,2048]{1,0:T(8,128)(2,1)S(1)}, f16[64,2048]{1,0:T(8,128)(2,1)S(1)}, u32[]{:S(2)}, u32[]{:S(2)}) collective-permute-start(f16[64,2048]{1,0:T(8,128)(2,1)S(1)} %multiply_convert_fusion.7), channel_id=1, source_target_pairs={{0,2},{1,3},{2,0},{3,1},{4,6},{5,7},{6,4},{7,5},{8,10},{9,11},{10,... | collective-permute-start | bytes 786440 | tf_op jit(solution)/shard_map/ppermute | solution.py:191
  15.2 10.2 %collective-permute-start.4 = (f16[128,4096]{1,0:T(8,128)(2,1)S(1)}, f16[128,4096]{1,0:T(8,128)(2,1)S(1)}, u32[]{:S(2)}, u32[]{:S(2)}) collective-permute-start(f16[128,4096]{1,0:T(8,128)(2,1)S(1)} %multiply_convert_fusion), channel_id=1, source_target_pairs={{0,1},{1,0},{2,3},{3,2},{4,5},{5,4},{6,7},{7,6},{8,9},{9,8},{10,11... | collective-permute-start | bytes 3145736 | tf_op jit(solution)/shard_map/ppermute | solution.py:191
  15.7 47.6 %collective-permute-start.1 = (bf16[256,2048]{1,0:T(8,128)(2,1)S(1)}, bf16[256,2048]{1,0:T(8,128)(2,1)S(1)}, u32[]{:S(2)}, u32[]{:S(2)}) collective-permute-start(bf16[256,2048]{1,0:T(8,128)(2,1)S(1)} %constant_dynamic-slice_fusion.1), channel_id=1, source_target_pairs={{0,1},{1,0},{2,3},{3,2},{4,5},{5,4},{6,7},{7,6},{8,9},{9,8},{10,11... | collective-permute-start | bytes 3145736 | tf_op jit(solution)/shard_map/ppermute | solution.py:191
  25.9 5.5 %collective-permute-start.5 = (f16[32,2048]{1,0:T(8,128)(2,1)S(1)}, f16[32,2048]{1,0:T(8,128)(2,1)S(1)}, u32[]{:S(2)}, u32[]{:S(2)}) collective-permute-start(f16[32,2048]{1,0:T(8,128)(2,1)S(1)} %multiply_convert_fusion.11), channel_id=1, source_target_pairs={{0,4},{1,5},{2,6},{3,7},{4,0},{5,1},{6,2},{7,3},{8,12},{9,13},{10,... | collective-permute-start | bytes 393224 | tf_op jit(solution)/shard_map/ppermute | solution.py:191
  27.8 6.4 %collective-permute-start.6 = (f16[32,2048]{1,0:T(8,128)(2,1)S(1)}, f16[32,2048]{1,0:T(8,128)(2,1)S(1)}, u32[]{:S(2)}, u32[]{:S(2)}) collective-permute-start(f16[32,2048]{1,0:T(8,128)(2,1)S(1)} %multiply_convert_fusion.10), channel_id=1, source_target_pairs={{0,2},{1,3},{2,0},{3,1},{4,6},{5,7},{6,4},{7,5},{8,10},{9,11},{10,... | collective-permute-start | bytes 393224 | tf_op jit(solution)/shard_map/ppermute | solution.py:191
  29.5 8.8 %collective-permute-start.8 = (f16[64,2048]{1,0:T(8,128)(2,1)S(1)}, f16[64,2048]{1,0:T(8,128)(2,1)S(1)}, u32[]{:S(2)}, u32[]{:S(2)}) collective-permute-start(f16[64,2048]{1,0:T(8,128)(2,1)S(1)} %multiply_convert_fusion.5), channel_id=1, source_target_pairs={{0,2},{1,3},{2,0},{3,1},{4,6},{5,7},{6,4},{7,5},{8,10},{9,11},{10,... | collective-permute-start | bytes 786440 | tf_op jit(solution)/shard_map/ppermute | solution.py:191
  30.1 11.6 %collective-permute-start.10 = (f16[32,4096]{1,0:T(8,128)(2,1)S(1)}, f16[32,4096]{1,0:T(8,128)(2,1)S(1)}, u32[]{:S(2)}, u32[]{:S(2)}) collective-permute-start(f16[32,4096]{1,0:T(8,128)(2,1)S(1)} %multiply_convert_fusion.4), channel_id=1, source_target_pairs={{0,4},{1,5},{2,6},{3,7},{4,0},{5,1},{6,2},{7,3},{8,12},{9,13},{10,... | collective-permute-start | bytes 786440 | tf_op jit(solution)/shard_map/ppermute | solution.py:191
  34.5 16.0 %collective-permute-start.12 = (f16[2,32,2048]{2,1,0:T(8,128)(2,1)S(1)}, f16[2,32,2048]{2,1,0:T(8,128)(2,1)S(1)}, u32[]{:S(2)}, u32[]{:S(2)}) collective-permute-start(f16[2,32,2048]{2,1,0:T(8,128)(2,1)S(1)} %get-tuple-element.98), channel_id=1, source_target_pairs={{0,8},{1,9},{2,10},{3,11},{4,12},{5,13},{6,14},{7,15},{8,0},{9,1},... | collective-permute-start | bytes 786440 | tf_op jit(solution)/shard_map/ppermute | solution.py:191
  38.6 6.8 %collective-permute-start.9 = (f16[32,2048]{1,0:T(8,128)(2,1)S(1)}, f16[32,2048]{1,0:T(8,128)(2,1)S(1)}, u32[]{:S(2)}, u32[]{:S(2)}) collective-permute-start(f16[32,2048]{1,0:T(8,128)(2,1)S(1)} %multiply_convert_fusion.9), channel_id=1, source_target_pairs={{0,4},{1,5},{2,6},{3,7},{4,0},{5,1},{6,2},{7,3},{8,12},{9,13},{10,... | collective-permute-start | bytes 393224 | tf_op jit(solution)/shard_map/ppermute | solution.py:191
  42.0 5.0 %collective-permute-start.11 = (f16[32,2048]{1,0:T(8,128)(2,1)S(1)}, f16[32,2048]{1,0:T(8,128)(2,1)S(1)}, u32[]{:S(2)}, u32[]{:S(2)}) collective-permute-start(f16[32,2048]{1,0:T(8,128)(2,1)S(1)} %multiply_convert_fusion.8), channel_id=1, source_target_pairs={{0,2},{1,3},{2,0},{3,1},{4,6},{5,7},{6,4},{7,5},{8,10},{9,11},{10,... | collective-permute-start | bytes 393224 | tf_op jit(solution)/shard_map/ppermute | solution.py:191
  47.3 11.5 %collective-permute-start.17 = (f16[2,32,2048]{2,1,0:T(8,128)(2,1)S(1)}, f16[2,32,2048]{2,1,0:T(8,128)(2,1)S(1)}, u32[]{:S(2)}, u32[]{:S(2)}) collective-permute-start(f16[2,32,2048]{2,1,0:T(8,128)(2,1)S(1)} %multiply_convert_fusion.3), channel_id=1, source_target_pairs={{0,8},{1,9},{2,10},{3,11},{4,12},{5,13},{6,14},{7,15},{8,0},{9,1},... | collective-permute-start | bytes 786440 | tf_op jit(solution)/shard_map/ppermute | solution.py:191
  48.9 14.3 %collective-permute-start.14 = (bf16[160,2048]{1,0:T(8,128)(2,1)S(1)}, bf16[160,2048]{1,0:T(8,128)(2,1)S(1)}, u32[]{:S(2)}, u32[]{:S(2)}) collective-permute-start(bf16[160,2048]{1,0:T(8,128)(2,1)S(1)} %constant_dynamic-slice_fusion.3), channel_id=1, source_target_pairs={{0,2},{1,3},{2,0},{3,1},{4,6},{5,7},{6,4},{7,5},{8,10},{9,11},{10,... | collective-permute-start | bytes 1966088 | tf_op jit(solution)/shard_map/ppermute | solution.py:191
  50.6 11.2 %collective-permute-start.13 = (bf16[2,32,2048]{2,1,0:T(8,128)(2,1)S(1)}, bf16[2,32,2048]{2,1,0:T(8,128)(2,1)S(1)}, u32[]{:S(2)}, u32[]{:S(2)}) collective-permute-start(bf16[2,32,2048]{2,1,0:T(8,128)(2,1)S(1)} %fusion.21), channel_id=1, source_target_pairs={{0,4},{1,5},{2,6},{3,7},{4,0},{5,1},{6,2},{7,3},{8,12},{9,13},{10,... | collective-permute-start | bytes 786440 | tf_op jit(solution)/shard_map/ppermute | solution.py:191
  53.0 11.0 %collective-permute-start.15 = (bf16[96,2048]{1,0:T(8,128)(2,1)S(1)}, bf16[96,2048]{1,0:T(8,128)(2,1)S(1)}, u32[]{:S(2)}, u32[]{:S(2)}) collective-permute-start(bf16[96,2048]{1,0:T(8,128)(2,1)S(1)} %collective-permute-done.7), channel_id=1, source_target_pairs={{0,1},{1,0},{2,3},{3,2},{4,5},{5,4},{6,7},{7,6},{8,9},{9,8},{10,11... | collective-permute-start | bytes 1179656 | tf_op jit(solution)/shard_map/ppermute | solution.py:191
  58.8 7.7 %collective-permute-start.18 = (bf16[2,32,2048]{2,1,0:T(8,128)(2,1)S(1)}, bf16[2,32,2048]{2,1,0:T(8,128)(2,1)S(1)}, u32[]{:S(2)}, u32[]{:S(2)}) collective-permute-start(bf16[2,32,2048]{2,1,0:T(8,128)(2,1)S(1)} %fusion.24), channel_id=1, source_target_pairs={{0,4},{1,5},{2,6},{3,7},{4,0},{5,1},{6,2},{7,3},{8,12},{9,13},{10,... | collective-permute-start | bytes 786440 | tf_op jit(solution)/shard_map/ppermute | solution.py:191
  63.2 2.1 %collective-permute-start.16 = (bf16[160,2048]{1,0:T(8,128)(2,1)S(1)}, bf16[160,2048]{1,0:T(8,128)(2,1)S(1)}, u32[]{:S(2)}, u32[]{:S(2)}) collective-permute-start(bf16[160,2048]{1,0:T(8,128)(2,1)S(1)} %collective-permute-done.14), channel_id=1, source_target_pairs={{0,1},{1,0},{2,3},{3,2},{4,5},{5,4},{6,7},{7,6},{8,9},{9,8},{10,11... | collective-permute-start | bytes 1966088 | tf_op jit(solution)/shard_map/ppermute | solution.py:191
  67.4 0.8 copy-start.1
  68.2 6.2 %copy-start.2 = (s32[8,12]{1,0:T(8,128)S(1)}, s32[8,12]{1,0:T(8,128)}, u32[]{:S(2)}) copy-start(s32[8,12]{1,0:T(8,128)} %param.11) | copy-start | bytes 1156
  68.2 6.9 %copy-start.3 = (s32[8]{0:T(128)S(1)}, s32[8]{0:T(128)}, u32[]{:S(2)}) copy-start(s32[8]{0:T(128)} %param.12) | copy-start | bytes 100
  68.2 7.0 %copy-start.4 = (s32[512]{0:T(512)S(1)}, s32[512]{0:T(512)}, u32[]{:S(2)}) copy-start(s32[512]{0:T(512)} %param.10) | copy-start | bytes 6148
  70.0 18.8 %all-to-all-start = ((bf16[16,1,64,256]{3,2,1,0:T(8,128)(2,1)}), bf16[16,1,64,256]{3,2,1,0:T(8,128)(2,1)S(1)}, u32[]{:S(2)}, u32[]{:S(2)}) async-start(bf16[16,1,64,256]{3,2,1,0:T(8,128)(2,1)} %bitcast.10), calls=%async_computation | async-start | bytes 1048576 | tf_op jit(solution)/shard_map/all_to_all | solution.py:318
